TPU v7x, 512 devices: a whole 4x4x16 slice. The times are simulated.
512 devices in a mesh: seq: 16 (over y, x), bal: 32 (over z, core).
Axes of the slice: x: 4, y: 4, z: 16, core: 2. Of those that a mesh axis runs over, the one named last changes fastest.
Arguments:
- tokens: bfloat16 [24576, 3072], P(('bal', 'seq')), may hold values from -6 to 6
- qkv_weight: bfloat16 [3072, 16, 3, 128], P(None, 'seq'), may hold values from -0.109375 to 0.109375
- q_gain: float32 [16, 128], P('seq'), may hold values from 0.5 to 2
- k_gain: float32 [16, 128], P('seq'), may hold values from 0.5 to 2
- key_tiles: int32 [16, 192, 64], P('seq'), may hold values from 0 to 191, as said below
- key_counts: int32 [16, 192], P('seq'), may hold values from 1 to 64, as said below
Outputs:
- attended: bfloat16 [24576, 2048], P(('bal', 'seq'))
Inputs may be any that keep to these rules, and one draw needn't show every extreme that they name: Each row of key_tiles lists 64 distinct tiles; only the first key_counts entries of a row are attended. `key_counts`: every head has a query tile that attends all 64 listed tiles.
All inputs are finite; a program needn't handle non-finite values.
Results may differ from a plain program's by a relative error of at most 0.0079.
Values may be sent and summed in bfloat16 or wider, within the bound.
No kernel may reach another device: no remote copies, remote signals or barrier semaphores. Data moves between devices by JAX's collectives and lax.ppermute only.
A program may use at most 128 MiB of HBM per device.

v0:
```python
import jax
import jax.numpy as jnp
from jax import lax
from jax.sharding import PartitionSpec as P

TILE = 128


def normalize(values, gain):
    mean_square = jnp.mean(values * values, axis=-1, keepdims=True)
    return (values * lax.rsqrt(mean_square + 1e-06) * gain).astype(jnp.bfloat16)


def attend(query_tiles, first, pair_block, lists, counts, scale):
    slots = query_tiles.shape[0]
    row_count = query_tiles.shape[1]
    head_dim = query_tiles.shape[2]
    tile_rows = pair_block.shape[1]
    my_lists = lax.dynamic_slice_in_dim(lists, first, slots, 0)
    my_counts = lax.dynamic_slice_in_dim(counts, first, slots, 0)

    def one_slot(slot, out):
        query = lax.dynamic_index_in_dim(query_tiles, slot, 0, keepdims=False)
        row_list = lax.dynamic_index_in_dim(my_lists, slot, 0, keepdims=False)
        count = lax.dynamic_index_in_dim(my_counts, slot, 0, keepdims=False)

        def turn(step, carry):
            sums, acc = carry
            picks = lax.dynamic_slice_in_dim(row_list, step * 8, 8, 0)
            pairs = jnp.take(pair_block, picks, axis=0)
            keys = pairs[:, :, :head_dim].reshape(8 * tile_rows, head_dim)
            vals = pairs[:, :, head_dim:].reshape(8 * tile_rows, head_dim)
            scores = jnp.dot(query, keys.T, preferred_element_type=jnp.float32) * scale
            live = jnp.repeat(step * 8 + jnp.arange(8, dtype=jnp.int32) < count, tile_rows)
            weights = jnp.where(live[None, :], jnp.exp(scores), jnp.float32(0.0))
            sums = sums + jnp.sum(weights, axis=-1)
            acc = acc + jnp.dot(
                weights.astype(jnp.bfloat16), vals, preferred_element_type=jnp.float32
            )
            return (sums, acc)

        start = (
            jnp.zeros((row_count,), jnp.float32),
            jnp.zeros((row_count, head_dim), jnp.float32),
        )
        sums, acc = lax.fori_loop(0, (count + 7) // 8, turn, start)
        result = (acc / sums[:, None]).astype(jnp.bfloat16)
        return lax.dynamic_update_index_in_dim(out, result, slot, 0)

    empty = jnp.zeros((slots, row_count, head_dim), jnp.bfloat16)
    return lax.fori_loop(0, slots, one_slot, empty)


def on_device(tokens, qkv_weight, q_gain, k_gain, key_tiles, key_counts):
    width = tokens.shape[1]
    heads_here = qkv_weight.shape[1]
    head_dim = qkv_weight.shape[3]
    scale = head_dim ** (-0.5)
    n_bal = lax.axis_size("bal")
    me_bal = lax.axis_index("bal")
    flat_weight = qkv_weight.reshape(width, heads_here * 3 * head_dim)
    proj = jnp.dot(
        lax.all_gather(tokens, "seq", axis=0, tiled=True),
        flat_weight,
        preferred_element_type=jnp.float32,
    )
    rows = proj.shape[0]
    slots = rows // TILE
    total_tiles = slots * n_bal
    proj = jnp.transpose(proj.reshape(rows, heads_here, 3, head_dim), (1, 2, 0, 3))
    queries = normalize(proj[:, 0], q_gain[:, None, :])
    keys = normalize(proj[:, 1], k_gain[:, None, :])
    values = proj[:, 2].astype(jnp.bfloat16)
    all_keys, all_values = (
        lax.all_gather(keys, "bal", axis=1, tiled=True),
        lax.all_gather(values, "bal", axis=1, tiled=True),
    )
    pair_blocks = jnp.concatenate((all_keys, all_values), axis=-1).reshape(
        heads_here, total_tiles, TILE, 2 * head_dim
    )
    query_tiles = queries[0].reshape(slots, TILE, head_dim)
    results = [
        attend(query_tiles, me_bal * slots, pair_blocks[0], key_tiles[0], key_counts[0], scale)
    ]
    stacked = jnp.stack(results, axis=0).reshape(heads_here, rows, head_dim)
    local_rows = jnp.transpose(stacked, (1, 0, 2)).reshape(rows, heads_here * head_dim)
    return lax.all_to_all(local_rows, "seq", split_axis=0, concat_axis=1, tiled=True)


def solution(mesh):
    placed = (
        P(("bal", "seq"), None),
        P(None, "seq", None, None),
        P("seq", None),
        P("seq", None),
        P("seq", None, None),
        P("seq", None),
    )
    return jax.shard_map(
        on_device, mesh=mesh, in_specs=placed, out_specs=P(("bal", "seq"), None), check_vma=False
    )
```

profile of v0, /device:TPU:481, one launch (start us, length us, event | category | flops | bytes accessed | tf_op | source)
XLA Modules:
  0.0 528.9 jit_solution(8827958985436768932)
XLA Ops:
  6.5 0.7 all-gather.5.cloned.1.call-update
  7.3 2.8 copy.15
  10.2 68.6 %all-gather.5.cloned.1.call-done = bf16[768,3072]{1,0:T(8,128)(2,1)} async-done(((bf16[48,3072]{1,0:T(8,128)(2,1)}), bf16[768,3072]{1,0:T(8,128)(2,1)}) %all-gather.5.cloned.1.call-update) | async-done | bytes 4718608 | tf_op jit(solution)/shard_map/all_gather | solution.py:63
  78.8 4.5 fusion.7
  83.5 0.8 copy-done.1
  84.3 0.9 multiply_convert_fusion
  85.2 1.7 slice.33
  87.2 1.2 multiply_reduce_fusion.1
  88.6 72.8 %all-gather.7.cloned.1.call-done = bf16[1,24576,128]{2,1,0:T(8,128)(2,1)} async-done(((bf16[1,768,128]{2,1,0:T(8,128)(2,1)}), bf16[1,24576,128]{2,1,0:T(8,128)(2,1)}) %all-gather.7.cloned.1.call-update) | async-done | bytes 6291472 | tf_op jit(solution)/shard_map/all_gather | solution.py:75
  161.4 76.2 %all-gather.9.cloned.1.call-done = bf16[1,1,24576,128]{3,2,1,0:T(8,128)(2,1)} async-done(((bf16[1,1,768,128]{3,2,1,0:T(8,128)(2,1)}), bf16[1,1,24576,128]{3,2,1,0:T(8,128)(2,1)}) %all-gather.9.cloned.1.call-update) | async-done | bytes 6291472 | tf_op jit(solution)/shard_map/all_gather | solution.py:76
  237.6 10.5 %pad_maximum_fusion = bf16[1,24576,256]{2,1,0:T(8,128)(2,1)} fusion(bf16[1,24576,128]{2,1,0:T(8,128)(2,1)} %bitcast.81, bf16[1,24576,128]{2,1,0:T(8,128)(2,1)} %all-gather.7.cloned.1.call-done), kind=kLoop, calls=%fused_computation.17 | loop fusion | flops 25165824 | bytes 25165824 | tf_op jit(solution)/shard_map/concatenate | solution.py:78
  248.1 90.6 %while.56 = (s32[]{:T(128)}, bf16[6,128,128]{2,1,0:T(8,128)(2,1)S(1)}, s32[6]{0:T(128)S(1)}, s32[6,64]{1,0:T(8,128)S(1)}, bf16[6,128,128]{2,1,0:T(8,128)(2,1)S(1...) while((s32[]{:T(128)}, ...), condition=%wide.region_6.7_spmd, body=%wide.region_2.6_spmd.sunk | while | flops 67945552 | bytes 4598038 | solution.py:51
  248.1 0.6 dynamic_slice.63
  249.4 13.7 %while.57 = (s32[]{:T(128)}, f32[128]{0:T(128)S(1)}, f32[128,128]{1,0:T(8,128)S(1)}, s32[]{:T(128)}, s32[]{:T(128)}, /*index=5*/s32[64]{0:T(128)S(1)}, bf16[192,...) while((s32[]{:T(128)}, f32[128]{0:T(128)S(1)}, ...), condition=%wide.region_5.5_spmd, body=%wide.region_3.4_spmd.sunk | while | flops 67912768 | bytes 4366671 | solution.py:46
  249.4 0.7 compare_and_fusion.2
  250.2 5.2 gather_fusion
  255.6 0.3 fusion.32
  256.0 0.3 convolution_add_fusion.2
  256.3 0.7 compare_and_fusion.2
  257.0 5.2 gather_fusion
  262.5 0.3 fusion.32
  262.8 0.3 convolution_add_fusion.2
  263.2 0.6 dynamic_slice.63
  264.5 20.5 %while.57 = (s32[]{:T(128)}, f32[128]{0:T(128)S(1)}, f32[128,128]{1,0:T(8,128)S(1)}, s32[]{:T(128)}, s32[]{:T(128)}, /*index=5*/s32[64]{0:T(128)S(1)}, bf16[192,...) while((s32[]{:T(128)}, f32[128]{0:T(128)S(1)}, ...), condition=%wide.region_5.5_spmd, body=%wide.region_3.4_spmd.sunk | while | flops 67912768 | bytes 4366671 | solution.py:46
  264.5 0.7 compare_and_fusion.2
  265.3 5.2 gather_fusion
  270.7 0.3 fusion.32
  271.4 0.7 compare_and_fusion.2
  272.2 5.2 gather_fusion
  277.6 0.3 fusion.32
  278.2 0.7 compare_and_fusion.2
  279.0 5.2 gather_fusion
  284.4 0.3 fusion.32
  285.2 0.6 dynamic_slice.63
  286.5 13.7 %while.57 = (s32[]{:T(128)}, f32[128]{0:T(128)S(1)}, f32[128,128]{1,0:T(8,128)S(1)}, s32[]{:T(128)}, s32[]{:T(128)}, /*index=5*/s32[64]{0:T(128)S(1)}, bf16[192,...) while((s32[]{:T(128)}, f32[128]{0:T(128)S(1)}, ...), condition=%wide.region_5.5_spmd, body=%wide.region_3.4_spmd.sunk | while | flops 67912768 | bytes 4366671 | solution.py:46
  286.5 0.7 compare_and_fusion.2
  287.3 5.2 gather_fusion
  292.7 0.3 fusion.32
  293.3 0.7 compare_and_fusion.2
  294.1 5.2 gather_fusion
  299.5 0.3 fusion.32
  300.3 0.6 dynamic_slice.63
  301.6 6.8 %while.57 = (s32[]{:T(128)}, f32[128]{0:T(128)S(1)}, f32[128,128]{1,0:T(8,128)S(1)}, s32[]{:T(128)}, s32[]{:T(128)}, /*index=5*/s32[64]{0:T(128)S(1)}, bf16[192,...) while((s32[]{:T(128)}, f32[128]{0:T(128)S(1)}, ...), condition=%wide.region_5.5_spmd, body=%wide.region_3.4_spmd.sunk | while | flops 67912768 | bytes 4366671 | solution.py:46
  301.6 0.7 compare_and_fusion.2
  302.4 5.2 gather_fusion
  307.8 0.3 fusion.32
  308.5 0.6 dynamic_slice.63
  309.8 6.8 %while.57 = (s32[]{:T(128)}, f32[128]{0:T(128)S(1)}, f32[128,128]{1,0:T(8,128)S(1)}, s32[]{:T(128)}, s32[]{:T(128)}, /*index=5*/s32[64]{0:T(128)S(1)}, bf16[192,...) while((s32[]{:T(128)}, f32[128]{0:T(128)S(1)}, ...), condition=%wide.region_5.5_spmd, body=%wide.region_3.4_spmd.sunk | while | flops 67912768 | bytes 4366671 | solution.py:46
  309.9 0.7 compare_and_fusion.2
  310.6 5.2 gather_fusion
  316.1 0.3 fusion.32
  316.8 0.6 dynamic_slice.63
  318.1 20.5 %while.57 = (s32[]{:T(128)}, f32[128]{0:T(128)S(1)}, f32[128,128]{1,0:T(8,128)S(1)}, s32[]{:T(128)}, s32[]{:T(128)}, /*index=5*/s32[64]{0:T(128)S(1)}, bf16[192,...) while((s32[]{:T(128)}, f32[128]{0:T(128)S(1)}, ...), condition=%wide.region_5.5_spmd, body=%wide.region_3.4_spmd.sunk | while | flops 67912768 | bytes 4366671 | solution.py:46
  318.1 0.7 compare_and_fusion.2
  318.9 5.2 gather_fusion
  324.3 0.3 fusion.32
  325.0 0.7 compare_and_fusion.2
  325.7 5.2 gather_fusion
  331.2 0.3 fusion.32
  331.8 0.7 compare_and_fusion.2
  332.6 5.2 gather_fusion
  338.0 0.3 fusion.32
  338.8 182.9 %all_to_all.19 = bf16[16,48,128]{2,1,0:T(8,128)(2,1)S(1)} all-to-all(bf16[16,48,128]{2,1,0:T(8,128)(2,1)S(1)} %bitcast.83), channel_id=1, replica_groups=mesh['seq'=16,'bal'=32] {'seq'}, dimensions={0} | all-to-all | bytes 393216 | tf_op jit(solution)/shard_map/all_to_all | solution.py:87
  521.7 0.7 copy_bitcast_fusion
  (122 shorter events, 8.2 us)
Async XLA Ops:
  6.5 80.4 %copy-start = (s32[1,192,64]{1,2,0:T(8,128)S(1)}, s32[1,192,64]{1,2,0:T(8,128)}, u32[]{:S(2)}) copy-start(s32[1,192,64]{1,2,0:T(8,128)} %param.14) | copy-start | bytes 147460
  6.5 72.2 %all-gather.5.cloned.1.call-start = ((), (), s32[]{:S(2)}) async-start(), calls=%async_computation.1 | async-start | bytes 5013504 | tf_op jit(solution)/shard_map/all_gather | solution.py:63
  7.3 154.2 %all-gather.7.cloned.1.call-start = ((), (), s32[]{:S(2)}) async-start(), calls=%async_computation.2 | async-start | bytes 6488064 | tf_op jit(solution)/shard_map/all_gather | solution.py:75
  10.2 74.1 %copy-start.2 = (f32[1,128]{1,0:T(1,128)S(1)}, f32[1,128]{1,0:T(1,128)}, u32[]{:S(2)}) copy-start(f32[1,128]{1,0:T(1,128)} %param.13) | copy-start | bytes 1540
  10.2 76.9 %copy-start.4 = (s32[1,192]{1,0:T(1,128)S(1)}, s32[1,192]{1,0:T(1,128)}, u32[]{:S(2)}) copy-start(s32[1,192]{1,0:T(1,128)} %param.15) | copy-start | bytes 2308
  10.2 78.2 %copy-start.3 = (f32[1,128]{1,0:T(1,128)S(1)}, f32[1,128]{1,0:T(1,128)}, u32[]{:S(2)}) copy-start(f32[1,128]{1,0:T(1,128)} %param.12) | copy-start | bytes 1540
  83.3 1.0 copy-start.1
  85.2 152.5 %all-gather.9.cloned.1.call-start = ((), (), s32[]{:S(2)}) async-start(), calls=%async_computation.3 | async-start | bytes 6488064 | tf_op jit(solution)/shard_map/all_gather | solution.py:76
Sparse Core Ops, SparseCore 0:
  10.4 68.3 all-gather.4
  85.3 76.0 all-gather.6
  163.5 74.0 all-gather.8
where the time goes:
time: 531 us; the launch traced here: 529 us
  waiting for transfers between devices  218 us (41%)
  blocking collectives  183 us (34%)
  local copies, waits for them, and re-layouts  74.3 us (14%)
  other arithmetic  23.5 us (4%)
  between operations  13.2 us (2%)
  matrix products  11.7 us (2%)
    all_to_all x1, blocking collectives, on_device(): lax.all_to_all(local_rows, 'seq', split_axis=0, concat_axis=1, tiled=True)  183 us
    all_gather x1, waiting for transfers between devices, on_device(): lax.all_gather(values, 'bal', axis=1, tiled=True)  76.2 us
    all_gather x1, waiting for transfers between devices, on_device(): lax.all_gather(keys, 'bal', axis=1, tiled=True)  72.8 us
    all_gather x1, waiting for transfers between devices, on_device(): lax.all_gather(tokens, 'seq', axis=0, tiled=True)  68.6 us
    gather x12, local copies, waits for them, and re-layouts, turn(): pairs = jnp.take(pair_block, picks, axis=0)  61.9 us
  transfers between devices with their start and end apart: 3, of which 3 were waited for; matrix products, arithmetic and copies ran while one was open for 1% of the time, Pallas kernels for 0%

commit v1 on v0

v1 whole, which is shorter than its diff:
```python
import functools
import jax
import jax.numpy as jnp
from jax import lax
from jax.experimental import pallas as pl
from jax.experimental.pallas import tpu as pltpu
from jax.sharding import PartitionSpec as P

TILE = 128
HEAD = 128
PIECE = 48
GROUP = 8
LOG2E = 1.4426950408889634
MESH_AXES = ("seq", "bal")
VMEM = pl.BlockSpec(memory_space=pltpu.VMEM)
SMEM = pl.BlockSpec(memory_space=pltpu.SMEM)


def plane_perm(phase, shift):
    pairs = []
    for bal in range(32):
        for y in range(4):
            for x in range(4):
                along_x = (bal % 2 == 0) == (phase == 1)
                to_y = y if along_x else (y + shift) % 4
                to_x = (x + shift) % 4 if along_x else x
                pairs.append(((4 * y + x) * 32 + bal, (4 * to_y + to_x) * 32 + bal))
    return pairs


def send(block, phase, shift):
    return lax.ppermute(block, MESH_AXES, plane_perm(phase, shift))


def gather_tokens(tokens):
    before = send(tokens, 1, 1)
    after = send(tokens, 1, -1)
    across = send(tokens, 1, 2)
    line = jnp.concatenate((tokens, before, after, across), axis=0)
    line_before = send(line, 2, 1)
    line_after = send(line, 2, -1)
    half = line.shape[0] // 2
    across_low = send(line_before[:half], 2, 1)
    across_high = send(line_after[half:], 2, -1)
    return line, line_before, line_after, across_low, across_high


def project_kernel(place, line, before, after, low, high, weight, q_gain, k_gain, q_out, kv_out):
    first = place[0]
    second = place[1]
    first_step = place[2]
    second_step = place[3]

    def normalize(values, gain):
        mean_square = jnp.mean(values * values, axis=-1, keepdims=True)
        return (values * lax.rsqrt(mean_square + 1e-06) * gain).astype(jnp.bfloat16)

    def project(block, shift, pieces):
        proj = jnp.dot(block[...], weight[...], preferred_element_type=jnp.float32)
        query = normalize(proj[:, :HEAD], q_gain[...])
        key = normalize(proj[:, HEAD : 2 * HEAD], k_gain[...])
        value = proj[:, 2 * HEAD :].astype(jnp.bfloat16)
        for at, piece in enumerate(pieces):
            spot = ((first + piece) % 4) * first_step + ((second + shift) % 4) * second_step
            rows = pl.ds(pl.multiple_of(spot * PIECE, PIECE), PIECE)
            here = slice(at * PIECE, (at + 1) * PIECE)
            q_out[rows, :] = query[here]
            kv_out[rows, :HEAD] = key[here]
            kv_out[rows, HEAD:] = value[here]

    project(line, 0, (0, 3, 1, 2))
    project(before, 3, (0, 3, 1, 2))
    project(after, 1, (0, 3, 1, 2))
    project(low, 2, (0, 3))
    project(high, 2, (1, 2))


def project(blocks, weight, q_gain, k_gain, place):
    rows = 16 * PIECE
    return pl.pallas_call(
        project_kernel,
        out_shape=(
            jax.ShapeDtypeStruct((rows, HEAD), jnp.bfloat16),
            jax.ShapeDtypeStruct((rows, 2 * HEAD), jnp.bfloat16),
        ),
        in_specs=[SMEM] + [VMEM] * 8,
        out_specs=(VMEM, VMEM),
        compiler_params=pltpu.CompilerParams(vmem_limit_bytes=40 * 1024 * 1024),
        name="project",
    )(place, *blocks, weight, q_gain, k_gain)


def attend_kernel(scale, lists, counts, q, kv, out):
    ones = jnp.ones((GROUP * TILE, HEAD), jnp.bfloat16)

    def one_slot(slot, _):
        query = q[slot]
        count = counts[slot]

        def turn(step, acc):
            picks = [lists[slot, step * GROUP + at] for at in range(GROUP)]
            keys = jnp.concatenate([kv[pick, :, :HEAD] for pick in picks], axis=0)
            values = jnp.concatenate([kv[pick, :, HEAD:] for pick in picks], axis=0)
            scores = lax.dot_general(
                query, keys, (((1,), (1,)), ((), ())), preferred_element_type=jnp.float32
            )
            live = (count - step * GROUP) * TILE
            column = lax.broadcasted_iota(jnp.int32, scores.shape, 1)
            weights = jnp.where(column < live, jnp.exp2(scores * scale), 0.0)
            return acc + jnp.dot(
                weights.astype(jnp.bfloat16),
                jnp.concatenate((values, ones), axis=1),
                preferred_element_type=jnp.float32,
            )

        acc = lax.fori_loop(
            0, (count + GROUP - 1) // GROUP, turn, jnp.zeros((TILE, 2 * HEAD), jnp.float32)
        )
        out[slot] = (acc[:, :HEAD] / acc[:, HEAD:]).astype(jnp.bfloat16)
        return 0

    lax.fori_loop(0, q.shape[0], one_slot, 0)


def attend(q, kv, lists, counts):
    scale = HEAD ** (-0.5) * LOG2E
    return pl.pallas_call(
        functools.partial(attend_kernel, scale),
        out_shape=jax.ShapeDtypeStruct(q.shape, jnp.bfloat16),
        in_specs=[SMEM, SMEM, VMEM, VMEM],
        out_specs=VMEM,
        compiler_params=pltpu.CompilerParams(vmem_limit_bytes=48 * 1024 * 1024),
        name="attend",
    )(lists, counts, q, kv)


def on_device(tokens, qkv_weight, q_gain, k_gain, key_tiles, key_counts):
    me_seq = lax.axis_index("seq")
    me_bal = lax.axis_index("bal")
    y, x = me_seq // 4, me_seq % 4
    core = me_bal % 2
    place = jnp.where(
        core == 0, jnp.stack((x, y, 1 + 0 * x, 4 + 0 * x)), jnp.stack((y, x, 4 + 0 * x, 1 + 0 * x))
    ).astype(jnp.int32)
    weight = qkv_weight.reshape(qkv_weight.shape[0], 3 * HEAD)
    blocks = gather_tokens(tokens)
    queries, pairs = project(blocks, weight, q_gain, k_gain, place)
    slots = queries.shape[0] // TILE
    all_pairs = lax.all_gather(pairs, "bal", axis=0, tiled=True)
    lists = lax.dynamic_slice_in_dim(key_tiles[0], me_bal * slots, slots, 0)
    counts = lax.dynamic_slice_in_dim(key_counts[0], me_bal * slots, slots, 0)
    result = attend(
        queries.reshape(slots, TILE, HEAD),
        all_pairs.reshape(-1, TILE, 2 * HEAD),
        lists,
        counts,
    )
    return lax.all_to_all(
        result.reshape(slots * TILE, HEAD), "seq", split_axis=0, concat_axis=1, tiled=True
    )


def solution(mesh):
    placed = (
        P(("bal", "seq"), None),
        P(None, "seq", None, None),
        P("seq", None),
        P("seq", None),
        P("seq", None, None),
        P("seq", None),
    )
    return jax.shard_map(
        on_device, mesh=mesh, in_specs=placed, out_specs=P(("bal", "seq"), None), check_vma=False
    )
```

time: 531 us -> 198 us (0.37)
  the two profiles are of different devices: /device:TPU:481 before, /device:TPU:1 now
where the time goes in v1:
time: 198 us; the launch traced here: 197 us
  waiting for transfers between devices  113 us (57%)
  starting transfers between devices  24.3 us (12%)
  blocking collectives  16.5 us (8%)
  local copies, waits for them, and re-layouts  15.1 us (8%)
  Pallas kernels  14.4 us (7%)
  between operations  13.6 us (7%)
    all_gather x1, waiting for transfers between devices, on_device(): all_pairs = lax.all_gather(pairs, 'bal', axis=0, tiled=True)  93.6 us
    ppermute x7, starting transfers between devices, send(): return lax.ppermute(block, MESH_AXES, plane_perm(phase, shift))  24.3 us
    ppermute x7, waiting for transfers between devices, send(): return lax.ppermute(block, MESH_AXES, plane_perm(phase, shift))  19.2 us
    all_to_all x1, blocking collectives, on_device(): lax.all_to_all(result.reshape(slots * TILE, HEAD), 'seq', split_axis=0, c...  16.5 us
    pallas_call x1, Pallas kernels, attend(): pl.pallas_call(functools.partial(attend_kernel, scale), out_shape=jax.Sha...  9.7 us
    unnamed x26, local copies, waits for them, and re-layouts  9.38 us
    pallas_call x1, Pallas kernels, project(): pl.pallas_call(project_kernel, out_shape=(jax.ShapeDtypeStruct((rows, HEA...  4.73 us
  transfers between devices with their start and end apart: 8, of which 4 were waited for; matrix products, arithmetic and copies ran while one was open for 4% of the time, Pallas kernels for 0%

profile of v1, /device:TPU:1, one launch (start us, length us, event | category | flops | bytes accessed | tf_op | source)
XLA Modules:
  0.0 196.8 jit_solution(4388462261991374317)
XLA Ops:
  6.5 0.0 copy-start
  6.5 0.0 all-gather.2.cloned.1.call-start
  6.5 4.2 %collective-permute-start = (bf16[48,3072]{1,0:T(8,128)(2,1)}, bf16[48,3072]{1,0:T(8,128)(2,1)S(1)}, u32[]{:S(2)}, u32[]{:S(2)}) collective-permute-start(bf16[48,3072]{1,0:T(8,128)(2,1)} %param.6), channel_id=1, source_target_pairs={{0,32},{32,64},{64,96},{96,0},{128,160},{160,192},{192,224},{224,1... | collective-permute-start | bytes 884744 | tf_op jit(solution)/shard_map/ppermute | solution.py:32
  10.7 3.4 %collective-permute-start.1 = (bf16[48,3072]{1,0:T(8,128)(2,1)}, bf16[48,3072]{1,0:T(8,128)(2,1)S(1)}, u32[]{:S(2)}, u32[]{:S(2)}) collective-permute-start(bf16[48,3072]{1,0:T(8,128)(2,1)} %param.6), channel_id=1, source_target_pairs={{0,96},{32,0},{64,32},{96,64},{128,224},{160,128},{192,160},{224,1... | collective-permute-start | bytes 884744 | tf_op jit(solution)/shard_map/ppermute | solution.py:32
  14.1 3.5 %collective-permute-start.2 = (bf16[48,3072]{1,0:T(8,128)(2,1)}, bf16[48,3072]{1,0:T(8,128)(2,1)S(1)}, u32[]{:S(2)}, u32[]{:S(2)}) collective-permute-start(bf16[48,3072]{1,0:T(8,128)(2,1)} %param.6), channel_id=1, source_target_pairs={{0,64},{32,96},{64,0},{96,32},{128,192},{160,224},{192,128},{224,1... | collective-permute-start | bytes 884744 | tf_op jit(solution)/shard_map/ppermute | solution.py:32
  17.6 1.0 constant_dynamic-update-slice_fusion.3
  18.6 0.0 collective-permute-done
  18.7 0.0 collective-permute-done.1
  18.7 4.6 %collective-permute-done.2 = bf16[48,3072]{1,0:T(8,128)(2,1)S(1)} collective-permute-done((bf16[48,3072]{1,0:T(8,128)(2,1)}, bf16[48,3072]{1,0:T(8,128)(2,1)S(1)}, u32[]{:S(2)}, u32[]{:S(2)}) %collective-permute-start.2) | collective-permute-done | bytes 294944 | tf_op jit(solution)/shard_map/ppermute | solution.py:32
  23.3 0.0 copy-start.5
  23.3 0.0 copy-start.9
  23.3 3.4 %collective-permute-start.3 = (bf16[192,3072]{1,0:T(8,128)(2,1)S(1)}, bf16[192,3072]{1,0:T(8,128)(2,1)S(1)}, u32[]{:S(2)}, u32[]{:S(2)}) collective-permute-start(bf16[192,3072]{1,0:T(8,128)(2,1)S(1)} %constant_dynamic-update-slice_fusion.line), channel_id=1, source_target_pairs={{0,128},{32,160},{64,192},{96,224},{128,256},{160,288},{192,320},{... | collective-permute-start | bytes 3538952 | tf_op jit(solution)/shard_map/ppermute | solution.py:32
  26.7 3.4 %collective-permute-start.4 = (bf16[192,3072]{1,0:T(8,128)(2,1)S(1)}, bf16[192,3072]{1,0:T(8,128)(2,1)S(1)}, u32[]{:S(2)}, u32[]{:S(2)}) collective-permute-start(bf16[192,3072]{1,0:T(8,128)(2,1)S(1)} %constant_dynamic-update-slice_fusion.line), channel_id=1, source_target_pairs={{0,384},{32,416},{64,448},{96,480},{128,0},{160,32},{192,64},{224,... | collective-permute-start | bytes 3538952 | tf_op jit(solution)/shard_map/ppermute | solution.py:32
  30.1 13.1 %collective-permute-done.3.before = bf16[192,3072]{1,0:T(8,128)(2,1)S(1)} collective-permute-done((bf16[192,3072]{1,0:T(8,128)(2,1)S(1)}, bf16[192,3072]{1,0:T(8,128)(2,1)S(1)}, u32[]{:S(2)}, u32[]{:S(2)}) %collective-permute-start.3) | collective-permute-done | bytes 1179680 | tf_op jit(solution)/shard_map/ppermute | solution.py:32
  43.2 0.9 slice.8
  44.1 0.0 copy-start.1
  44.1 1.0 copy-done.1
  45.1 1.9 collective-permute-start.5
  47.0 0.0 collective-permute-done.4.after
  47.0 0.8 slice.9
  47.9 0.0 copy-done.5
  47.9 0.0 copy-start.3
  47.9 1.0 copy-done.3
  48.9 4.6 %collective-permute-start.6 = (bf16[96,3072]{1,0:T(8,128)(2,1)}, bf16[96,3072]{1,0:T(8,128)(2,1)}, u32[]{:S(2)}, u32[]{:S(2)}) collective-permute-start(bf16[96,3072]{1,0:T(8,128)(2,1)} %slice.9), channel_id=1, source_target_pairs={{0,384},{32,416},{64,448},{96,480},{128,0},{160,32},{192,64},{224,... | collective-permute-start | bytes 1769480 | tf_op jit(solution)/shard_map/ppermute | solution.py:32
  53.5 0.0 copy-done.9
  53.5 2.4 %copy.11 = bf16[3072,1,3,128]{0,3,2,1:T(8,128)(2,1)} copy(bf16[3072,1,3,128]{3,0,2,1:T(8,128)(2,1)S(1)} %copy-done.9) | data formatting | bytes 4718592 | tf_op args[1]
  55.9 0.0 copy-start.7
  55.9 0.0 copy-start.8
  56.0 3.0 %copy.12.weight = bf16[3072,384]{1,0:T(8,128)(2,1)S(1)} copy(bf16[3072,384]{0,1:T(8,128)(2,1)} %bitcast.19) | data formatting | bytes 4718592 | tf_op jit(solution)/shard_map/reshape | solution.py:145
  59.0 0.0 copy-start.10
  59.0 0.1 broadcast_select_fusion.place
  59.1 0.0 collective-permute-done.5.low
  59.1 1.5 collective-permute-done.6.high
  60.6 0.0 copy-done.7
  60.6 0.0 copy-done.8
  60.6 0.0 copy-start.2
  60.6 1.3 copy-done.2
  61.9 0.0 copy-start.4
  61.9 1.3 copy-done.4
  63.1 0.0 copy-start.6
  63.2 1.3 copy-done.6
  64.4 4.7 %project.1 = (bf16[768,128]{1,0:T(8,128)(2,1)S(1)}, bf16[768,256]{1,0:T(8,128)(2,1)}) custom-call(s32[4]{0:T(128)S(1)} %broadcast_select_fusion.place, bf16[192,3072]{1,0:T(8,128)(2,1)S(1)} %copy-done.6, bf16[192,3072]{1,0:T(8,128)(2,1)S(1)} %copy-done.2, bf16[192,3072]{1,0:T(8,128)(2,1)S(1)} %copy-done.4, bf16[96,3072]{1,0:T(8,128)(2,1)S(1)} %collective-permute-done.5.low, ...), custom_call_target="tpu_custom_call" | custom-call | tf_op jit(solution)/shard_map/project/pallas_call | solution.py:80
  69.1 0.0 all-gather.2.cloned.1.call-update
  69.2 0.0 copy-done
  69.2 0.1 constant_dynamic-slice_fusion
  69.3 0.1 copy.10
  69.3 0.0 copy-done.10
  69.3 0.1 dynamic-slice_bitcast_fusion.counts
  69.4 93.6 %all-gather.2.cloned.1.call-done = bf16[24576,256]{1,0:T(8,128)(2,1)} async-done(((bf16[768,256]{1,0:T(8,128)(2,1)}), bf16[24576,256]{1,0:T(8,128)(2,1)}) %all-gather.2.cloned.1.call-update) | async-done | bytes 12582928 | tf_op jit(solution)/shard_map/all_gather | solution.py:149
  163.0 9.7 %attend.1 = bf16[6,128,128]{2,1,0:T(8,128)(2,1)S(1)} custom-call(s32[6,64]{1,0:T(8,128)S(1)} %bitcast.17, s32[6]{0:T(128)S(1)} %dynamic-slice_bitcast_fusion.counts, bf16[6,128,128]{2,1,0:T(8,128)(2,1)S(1)} %bitcast.16, bf16[192,128,256]{2,1,0:T(8,128)(2,1)} %bitcast.18), custom_call_target="tpu_custom_call" | custom-call | tf_op jit(solution)/shard_map/attend/pallas_call | solution.py:127
  172.8 16.5 %all_to_all.19 = bf16[16,48,128]{2,1,0:T(8,128)(2,1)S(1)} all-to-all(bf16[16,48,128]{2,1,0:T(8,128)(2,1)S(1)} %bitcast.15), channel_id=1, replica_groups=mesh['seq'=16,'bal'=32] {'seq'}, dimensions={0} | all-to-all | bytes 393216 | tf_op jit(solution)/shard_map/all_to_all | solution.py:158
  189.3 0.7 copy_bitcast_fusion
  (3 shorter events, 0.1 us)
Async XLA Ops:
  6.5 62.6 %copy-start = (s32[1,192,64]{1,2,0:T(8,128)S(1)}, s32[1,192,64]{1,2,0:T(8,128)}, u32[]{:S(2)}) copy-start(s32[1,192,64]{1,2,0:T(8,128)} %param.10) | copy-start | bytes 147460
  6.5 156.5 %all-gather.2.cloned.1.call-start = ((), (), s32[]{:S(2)}) async-start(), calls=%async_computation.1 | async-start | bytes 12976128 | tf_op jit(solution)/shard_map/all_gather | solution.py:149
  6.5 12.1 %collective-permute-start = (bf16[48,3072]{1,0:T(8,128)(2,1)}, bf16[48,3072]{1,0:T(8,128)(2,1)S(1)}, u32[]{:S(2)}, u32[]{:S(2)}) collective-permute-start(bf16[48,3072]{1,0:T(8,128)(2,1)} %param.6), channel_id=1, source_target_pairs={{0,32},{32,64},{64,96},{96,0},{128,160},{160,192},{192,224},{224,1... | collective-permute-start | bytes 884744 | tf_op jit(solution)/shard_map/ppermute | solution.py:32
  10.7 8.0 %collective-permute-start.1 = (bf16[48,3072]{1,0:T(8,128)(2,1)}, bf16[48,3072]{1,0:T(8,128)(2,1)S(1)}, u32[]{:S(2)}, u32[]{:S(2)}) collective-permute-start(bf16[48,3072]{1,0:T(8,128)(2,1)} %param.6), channel_id=1, source_target_pairs={{0,96},{32,0},{64,32},{96,64},{128,224},{160,128},{192,160},{224,1... | collective-permute-start | bytes 884744 | tf_op jit(solution)/shard_map/ppermute | solution.py:32
  14.1 9.2 %collective-permute-start.2 = (bf16[48,3072]{1,0:T(8,128)(2,1)}, bf16[48,3072]{1,0:T(8,128)(2,1)S(1)}, u32[]{:S(2)}, u32[]{:S(2)}) collective-permute-start(bf16[48,3072]{1,0:T(8,128)(2,1)} %param.6), channel_id=1, source_target_pairs={{0,64},{32,96},{64,0},{96,32},{128,192},{160,224},{192,128},{224,1... | collective-permute-start | bytes 884744 | tf_op jit(solution)/shard_map/ppermute | solution.py:32
  23.3 24.6 %copy-start.5 = (bf16[192,3072]{1,0:T(8,128)(2,1)}, bf16[192,3072]{1,0:T(8,128)(2,1)S(1)}, u32[]{:S(2)}) copy-start(bf16[192,3072]{1,0:T(8,128)(2,1)S(1)} %constant_dynamic-update-slice_fusion.line) | copy-start | bytes 3538948
  23.3 30.2 %copy-start.9 = (bf16[3072,1,3,128]{3,0,2,1:T(8,128)(2,1)S(1)}, bf16[3072,1,3,128]{3,0,2,1:T(8,128)(2,1)}, u32[]{:S(2)}) copy-start(bf16[3072,1,3,128]{3,0,2,1:T(8,128)(2,1)} %param.7) | copy-start | bytes 7077892
  23.3 19.9 %collective-permute-start.3 = (bf16[192,3072]{1,0:T(8,128)(2,1)S(1)}, bf16[192,3072]{1,0:T(8,128)(2,1)S(1)}, u32[]{:S(2)}, u32[]{:S(2)}) collective-permute-start(bf16[192,3072]{1,0:T(8,128)(2,1)S(1)} %constant_dynamic-update-slice_fusion.line), channel_id=1, source_target_pairs={{0,128},{32,160},{64,192},{96,224},{128,256},{160,288},{192,320},{... | collective-permute-start | bytes 3538952 | tf_op jit(solution)/shard_map/ppermute | solution.py:32
  26.7 20.3 %collective-permute-start.4 = (bf16[192,3072]{1,0:T(8,128)(2,1)S(1)}, bf16[192,3072]{1,0:T(8,128)(2,1)S(1)}, u32[]{:S(2)}, u32[]{:S(2)}) collective-permute-start(bf16[192,3072]{1,0:T(8,128)(2,1)S(1)} %constant_dynamic-update-slice_fusion.line), channel_id=1, source_target_pairs={{0,384},{32,416},{64,448},{96,480},{128,0},{160,32},{192,64},{224,... | collective-permute-start | bytes 3538952 | tf_op jit(solution)/shard_map/ppermute | solution.py:32
  44.1 1.0 copy-start.1
  45.1 14.0 %collective-permute-start.5 = (bf16[96,3072]{1,0:T(8,128)(2,1)}, bf16[96,3072]{1,0:T(8,128)(2,1)S(1)}, u32[]{:S(2)}, u32[]{:S(2)}) collective-permute-start(bf16[96,3072]{1,0:T(8,128)(2,1)} %slice.8), channel_id=1, source_target_pairs={{0,128},{32,160},{64,192},{96,224},{128,256},{160,288},{192,320},{... | collective-permute-start | bytes 1769480 | tf_op jit(solution)/shard_map/ppermute | solution.py:32
  47.9 1.0 copy-start.3
  48.9 11.7 %collective-permute-start.6 = (bf16[96,3072]{1,0:T(8,128)(2,1)}, bf16[96,3072]{1,0:T(8,128)(2,1)}, u32[]{:S(2)}, u32[]{:S(2)}) collective-permute-start(bf16[96,3072]{1,0:T(8,128)(2,1)} %slice.9), channel_id=1, source_target_pairs={{0,384},{32,416},{64,448},{96,480},{128,0},{160,32},{192,64},{224,... | collective-permute-start | bytes 1769480 | tf_op jit(solution)/shard_map/ppermute | solution.py:32
  55.9 4.7 %copy-start.7 = (f32[1,128]{1,0:T(1,128)S(1)}, f32[1,128]{1,0:T(1,128)}, u32[]{:S(2)}) copy-start(f32[1,128]{1,0:T(1,128)} %q_gain.1) | copy-start | bytes 1540
  55.9 4.7 %copy-start.8 = (f32[1,128]{1,0:T(1,128)S(1)}, f32[1,128]{1,0:T(1,128)}, u32[]{:S(2)}) copy-start(f32[1,128]{1,0:T(1,128)} %k_gain.1) | copy-start | bytes 1540
  59.0 10.3 %copy-start.10 = (s32[1,192]{1,0:T(1,128)S(1)}, s32[1,192]{1,0:T(1,128)}, u32[]{:S(2)}) copy-start(s32[1,192]{1,0:T(1,128)} %param.11) | copy-start | bytes 2308
  60.6 1.3 copy-start.2
  61.9 1.3 copy-start.4
  63.1 1.3 copy-start.6
Sparse Core Ops, SparseCore 0:
  69.3 93.7 all-gather.1

commit v2 on v1

v2 whole, which is shorter than its diff:
```python
import functools
import jax
import jax.numpy as jnp
from jax import lax
from jax.experimental import pallas as pl
from jax.experimental.pallas import tpu as pltpu
from jax.sharding import PartitionSpec as P

TILE = 128
HEAD = 128
PIECE = 48
GROUP = 8
PLANES = 16
BLOCKS = 16
LOG2E = 1.4426950408889634
MESH_AXES = ("seq", "bal")
VMEM = pl.BlockSpec(memory_space=pltpu.VMEM)
SMEM = pl.BlockSpec(memory_space=pltpu.SMEM)


def plane_perm(phase, shift):
    pairs = []
    for bal in range(32):
        for y in range(4):
            for x in range(4):
                along_x = (bal % 2 == 0) == (phase == 1)
                to_y = y if along_x else (y + shift) % 4
                to_x = (x + shift) % 4 if along_x else x
                pairs.append(((4 * y + x) * 32 + bal, (4 * to_y + to_x) * 32 + bal))
    return pairs


def send(block, phase, shift):
    return lax.ppermute(block, MESH_AXES, plane_perm(phase, shift))


def swap_cores(block):
    return lax.ppermute(block, "bal", [(at, at ^ 1) for at in range(32)])


def pass_on(block):
    pairs = []
    for z in range(PLANES):
        pairs.append((2 * z, 2 * ((z + 1) % PLANES)))
        pairs.append((2 * z + 1, 2 * ((z - 1) % PLANES) + 1))
    return lax.ppermute(block, "bal", pairs)


def project_kernel(lines, place, *refs):
    first = place[0]
    second = place[1]
    first_step = place[2]
    second_step = place[3]
    count = sum(len(halves) for _, halves in lines)
    blocks = refs[:count]
    weight, q_gain, k_gain = refs[count : count + 3]
    q_out, kv_out = refs[-2:]
    if len(refs) > count + 5:
        carried = refs[count + 3]
        q_out[...] = carried[...]

    def normalize(values, gain):
        mean_square = jnp.mean(values * values, axis=-1, keepdims=True)
        return (values * lax.rsqrt(mean_square + 1e-06) * gain).astype(jnp.bfloat16)

    at_block = 0
    for at_line, (shift, halves) in enumerate(lines):
        for pieces in halves:
            proj = jnp.dot(
                blocks[at_block][...], weight[...], preferred_element_type=jnp.float32
            )
            at_block += 1
            query = normalize(proj[:, :HEAD], q_gain[...])
            key = normalize(proj[:, HEAD : 2 * HEAD], k_gain[...])
            value = proj[:, 2 * HEAD :].astype(jnp.bfloat16)
            for at, piece in enumerate(pieces):
                here = slice(at * PIECE, (at + 1) * PIECE)
                along = (first + piece) % 4
                spot = along * first_step + ((second + shift) % 4) * second_step
                rows = pl.ds(pl.multiple_of(spot * PIECE, PIECE), PIECE)
                q_out[rows, :] = query[here]
                rows = pl.ds(pl.multiple_of((at_line * 4 + along) * PIECE, PIECE), PIECE)
                kv_out[rows, :HEAD] = key[here]
                kv_out[rows, HEAD:] = value[here]


def project(lines, blocks, weight, q_gain, k_gain, place, carried=None):
    rows = 16 * PIECE
    more = () if carried is None else (carried,)
    return pl.pallas_call(
        functools.partial(project_kernel, lines),
        out_shape=(
            jax.ShapeDtypeStruct((rows, HEAD), jnp.bfloat16),
            jax.ShapeDtypeStruct((len(lines) * 4 * PIECE, 2 * HEAD), jnp.bfloat16),
        ),
        in_specs=[SMEM] + [VMEM] * (len(blocks) + 3 + len(more)),
        out_specs=(VMEM, VMEM),
        compiler_params=pltpu.CompilerParams(vmem_limit_bytes=32 * 1024 * 1024),
        name="project",
    )(place, *blocks, weight, q_gain, k_gain, *more)


def attend_kernel(scale, place, lists, counts, q, lines, *refs):
    pieces = refs[: BLOCKS]
    out, kv, ready = refs[BLOCKS:]
    second = place[1]
    core = place[4]
    plane = place[5]
    line_rows = 4 * PIECE

    def load(block):
        same = block <= PLANES // 2
        away = block if same else block - PLANES // 2
        from_plane = (plane + PLANES + away * (2 * core - 1)) % PLANES
        from_core = core if same else 1 - core
        bal = 2 * from_plane + from_core
        across = place[1] if same else place[0]
        along_step = jnp.where(from_core == 0, 1, 4)
        across_step = 5 - along_step
        for at_line, shift in enumerate((0, 3, 1, 2)):
            line_spot = ((across + shift) % 4) * across_step
            for along in range(4):
                spot = block * 16 + line_spot + along * along_step
                rows = pl.ds(pl.multiple_of(spot * PIECE, PIECE), PIECE)
                if at_line == 0:
                    start = bal * line_rows + along * PIECE
                    source = lines.at[pl.ds(pl.multiple_of(start, PIECE), PIECE), :]
                else:
                    start = (at_line - 1) * line_rows + along * PIECE
                    source = pieces[block].at[pl.ds(start, PIECE), :]
                pltpu.make_async_copy(source, kv.at[rows, :], ready).start()

    for block in range(BLOCKS):
        load(block)
    pltpu.make_async_copy(kv, kv, ready).wait()
    ones = jnp.ones((GROUP * TILE, HEAD), jnp.bfloat16)

    def one_slot(slot, _):
        query = q[slot]
        count = counts[slot]

        def turn(step, acc):
            picks = [
                pl.ds(pl.multiple_of(lists[slot, step * GROUP + at] * TILE, TILE), TILE)
                for at in range(GROUP)
            ]
            keys = jnp.concatenate([kv[pick, :HEAD] for pick in picks], axis=0)
            values = jnp.concatenate([kv[pick, HEAD:] for pick in picks], axis=0)
            scores = lax.dot_general(
                query, keys, (((1,), (1,)), ((), ())), preferred_element_type=jnp.float32
            )
            live = (count - step * GROUP) * TILE
            column = lax.broadcasted_iota(jnp.int32, scores.shape, 1)
            weights = jnp.where(column < live, jnp.exp2(scores * scale), 0.0)
            return acc + jnp.dot(
                weights.astype(jnp.bfloat16),
                jnp.concatenate((values, ones), axis=1),
                preferred_element_type=jnp.float32,
            )

        out[slot] = lax.fori_loop(
            0, (count + GROUP - 1) // GROUP, turn, jnp.zeros((TILE, 2 * HEAD), jnp.float32)
        )
        return 0

    lax.fori_loop(0, q.shape[0], one_slot, 0)


def attend(place, q, lines, pieces, lists, counts):
    scale = HEAD ** (-0.5) * LOG2E
    block_rows = 16 * PIECE
    return pl.pallas_call(
        functools.partial(attend_kernel, scale),
        out_shape=jax.ShapeDtypeStruct((q.shape[0], TILE, 2 * HEAD), jnp.float32),
        in_specs=[SMEM, SMEM, SMEM, VMEM] + [pl.BlockSpec(memory_space=pl.ANY)] * (1 + BLOCKS),
        out_specs=VMEM,
        scratch_shapes=[
            pltpu.VMEM((BLOCKS * block_rows, 2 * HEAD), jnp.bfloat16),
            pltpu.SemaphoreType.DMA,
        ],
        compiler_params=pltpu.CompilerParams(vmem_limit_bytes=32 * 1024 * 1024),
        name="attend",
    )(place, lists, counts, q, lines, *pieces)


def local_lists(key_tiles, key_counts, me_bal, slots):
    core, plane = me_bal % 2, me_bal // 2
    mine = jnp.stack((me_bal, me_bal ^ 1))
    tiles = key_tiles.reshape(2 * PLANES, slots, -1)[mine].reshape(2 * slots, -1)
    counts = key_counts.reshape(2 * PLANES, slots)[mine].reshape(2 * slots, 1)
    bal = tiles // slots
    away = ((bal // 2 - plane) * (2 * core - 1)) % PLANES
    same = bal % 2 == core
    half = PLANES // 2
    held = jnp.where(same, away <= half, (away >= 1) & (away < half))
    block = jnp.where(same, away, away + half)
    entries = jnp.arange(tiles.shape[1], dtype=jnp.int32)
    held = held & (entries[None, :] < counts)
    order = jnp.cumsum(held.astype(jnp.int32), axis=1) - 1
    picks = jnp.where(held, block * slots + tiles % slots, 0)
    placed = (order[:, :, None] == entries[None, None, :]) & held[:, :, None]
    lists = jnp.sum(jnp.where(placed, picks[:, :, None], 0), axis=1)
    return lists, jnp.sum(held.astype(jnp.int32), axis=1)


def on_device(tokens, qkv_weight, q_gain, k_gain, key_tiles, key_counts):
    me_seq = lax.axis_index("seq")
    me_bal = lax.axis_index("bal")
    y, x = me_seq // 4, me_seq % 4
    core = me_bal % 2
    place = jnp.stack(
        (
            jnp.where(core == 0, x, y),
            jnp.where(core == 0, y, x),
            jnp.where(core == 0, 1, 4),
            jnp.where(core == 0, 4, 1),
            core,
            me_bal // 2,
        )
    ).astype(jnp.int32)
    weight = qkv_weight.reshape(qkv_weight.shape[0], 3 * HEAD)
    slots = 16 * PIECE // TILE
    lists, counts = local_lists(key_tiles[0], key_counts[0], me_bal, slots)

    before = send(tokens, 1, 1)
    after = send(tokens, 1, -1)
    across = send(tokens, 1, 2)
    low = jnp.concatenate((tokens, before), axis=0)
    before_low = send(low, 2, 1)
    high = jnp.concatenate((after, across), axis=0)
    after_high = send(high, 2, -1)
    after_low = send(low, 2, -1)
    before_high = send(high, 2, 1)
    across_low = send(before_low, 2, 1)
    across_high = send(after_high, 2, -1)

    halves = ((0, 3), (1, 2))
    own_queries, own_line = project(
        ((0, halves),), (low, high), weight, q_gain, k_gain, place
    )
    lines = lax.all_gather(own_line, "bal", axis=0, tiled=True)
    queries, rest = project(
        ((3, halves), (1, halves), (2, halves)),
        (before_low, before_high, after_low, after_high, across_low, across_high),
        weight,
        q_gain,
        k_gain,
        place,
        own_queries,
    )
    same, other = [rest], []
    same.append(pass_on(rest))
    swapped = swap_cores(jnp.concatenate((rest.reshape(-1, HEAD), queries), axis=0))
    moving = swapped[: 2 * rest.shape[0]].reshape(rest.shape)
    other_queries = swapped[2 * rest.shape[0] :]
    for step in range(1, PLANES // 2):
        moving = pass_on(moving)
        other.append(moving)
        same.append(pass_on(same[-1]))

    both = jnp.concatenate((queries, other_queries), axis=0).reshape(2 * slots, TILE, HEAD)
    sums = attend(place, both, lines, same + other, lists, counts)
    sums = sums[:slots] + swap_cores(sums[slots:])
    result = (sums[:, :, :HEAD] / sums[:, :, HEAD:]).astype(jnp.bfloat16)
    return lax.all_to_all(
        result.reshape(slots * TILE, HEAD), "seq", split_axis=0, concat_axis=1, tiled=True
    )


def solution(mesh):
    placed = (
        P(("bal", "seq"), None),
        P(None, "seq", None, None),
        P("seq", None),
        P("seq", None),
        P("seq", None, None),
        P("seq", None),
    )
    return jax.shard_map(
        on_device, mesh=mesh, in_specs=placed, out_specs=P(("bal", "seq"), None), check_vma=False
    )
```

time: 198 us -> 207 us (1.045)
  waiting for transfers between devices: 113 us -> 24.2 us
  starting transfers between devices: 24.3 us -> 111 us
  Pallas kernels: 14.4 us -> 24 us
  blocking collectives: 16.5 us -> 10.9 us
  local copies, waits for them, and re-layouts: 15.1 us -> 19.4 us
    all_gather x1, waiting for transfers between devices: 93.6 us -> 0.01 us  [on_device(): lines = lax.all_gather(own_line, 'bal', axis=0, tiled=True)]
    ppermute x0 -> x17, starting transfers between devices: none -> 81.3 us  [the longest x15 65.2 us: pass_on(): return lax.ppermute(block, 'bal', pairs)]
    ppermute x0 -> x17, waiting for transfers between devices: none -> 14.2 us  [the longest x15 12.3 us: pass_on(): return lax.ppermute(block, 'bal', pairs)]
    pallas_call x1, Pallas kernels: 9.7 us -> 19.2 us  [attend(): pl.pallas_call(functools.partial(attend_kernel, scale), out_shape=jax.Sha...]
    ppermute x7 -> x9, waiting for transfers between devices: 19.2 us -> 9.94 us  [send(): return lax.ppermute(block, MESH_AXES, plane_perm(phase, shift))]
    all_to_all x1, blocking collectives: 16.5 us -> 10.9 us  [on_device(): lax.all_to_all(result.reshape(slots * TILE, HEAD), 'seq', split_axis=0, c...]
    ppermute x7 -> x9, starting transfers between devices: 24.3 us -> 29.8 us  [send(): return lax.ppermute(block, MESH_AXES, plane_perm(phase, shift))]
    unnamed x26 -> x29, local copies, waits for them, and re-layouts: 9.38 us -> 11 us
  transfers between devices with their start and end apart: 8 -> 27, of which waited for: 4 -> 11; matrix products, arithmetic and copies ran while one was open for 4% -> 7% of each run, Pallas kernels for 0% -> 2%
where the time goes in v2:
time: 207 us; the launch traced here: 206 us
  starting transfers between devices  111 us (54%)
  waiting for transfers between devices  24.2 us (12%)
  Pallas kernels  24 us (12%)
  local copies, waits for them, and re-layouts  19.4 us (9%)
  between operations  14 us (7%)
  blocking collectives  10.9 us (5%)
    ppermute x15, starting transfers between devices, pass_on(): return lax.ppermute(block, 'bal', pairs)  65.2 us
    ppermute x9, starting transfers between devices, send(): return lax.ppermute(block, MESH_AXES, plane_perm(phase, shift))  29.8 us
    pallas_call x1, Pallas kernels, attend(): pl.pallas_call(functools.partial(attend_kernel, scale), out_shape=jax.Sha...  19.2 us
    ppermute x2, starting transfers between devices, swap_cores(): return lax.ppermute(block, 'bal', [(at, at ^ 1) for at in range(32)])  16 us
    ppermute x15, waiting for transfers between devices, pass_on(): return lax.ppermute(block, 'bal', pairs)  12.3 us
    unnamed x29, local copies, waits for them, and re-layouts  11 us
    all_to_all x1, blocking collectives, on_device(): lax.all_to_all(result.reshape(slots * TILE, HEAD), 'seq', split_axis=0, c...  10.9 us
    ppermute x9, waiting for transfers between devices, send(): return lax.ppermute(block, MESH_AXES, plane_perm(phase, shift))  9.94 us
  transfers between devices with their start and end apart: 27, of which 11 were waited for; matrix products, arithmetic and copies ran while one was open for 7% of the time, Pallas kernels for 2%

profile of v2, /device:TPU:1, one launch (start us, length us, event | category | flops | bytes accessed | tf_op | source)
XLA Modules:
  0.0 205.5 jit_solution(9957963354190224239)
XLA Ops:
  6.5 4.0 %collective-permute-start = (bf16[48,3072]{1,0:T(8,128)(2,1)}, bf16[48,3072]{1,0:T(8,128)(2,1)}, u32[]{:S(2)}, u32[]{:S(2)}) collective-permute-start(bf16[48,3072]{1,0:T(8,128)(2,1)} %param.6), channel_id=1, source_target_pairs={{0,32},{32,64},{64,96},{96,0},{128,160},{160,192},{192,224},{224,1... | collective-permute-start | bytes 884744 | tf_op jit(solution)/shard_map/ppermute | solution.py:34
  10.6 4.5 %collective-permute-start.3 = (bf16[48,3072]{1,0:T(8,128)(2,1)}, bf16[48,3072]{1,0:T(8,128)(2,1)}, u32[]{:S(2)}, u32[]{:S(2)}) collective-permute-start(bf16[48,3072]{1,0:T(8,128)(2,1)} %param.6), channel_id=1, source_target_pairs={{0,64},{32,96},{64,0},{96,32},{128,192},{160,224},{192,128},{224,1... | collective-permute-start | bytes 884744 | tf_op jit(solution)/shard_map/ppermute | solution.py:34
  15.1 3.0 %collective-permute-start.2 = (bf16[48,3072]{1,0:T(8,128)(2,1)}, bf16[48,3072]{1,0:T(8,128)(2,1)}, u32[]{:S(2)}, u32[]{:S(2)}) collective-permute-start(bf16[48,3072]{1,0:T(8,128)(2,1)} %param.6), channel_id=1, source_target_pairs={{0,96},{32,0},{64,32},{96,64},{128,224},{160,128},{192,160},{224,1... | collective-permute-start | bytes 884744 | tf_op jit(solution)/shard_map/ppermute | solution.py:34
  18.2 4.3 %copy.15 = bf16[3072,1,3,128]{0,3,2,1:T(8,128)(2,1)} copy(bf16[3072,1,3,128]{3,0,2,1:T(8,128)(2,1)} %param.7) | data formatting | bytes 4718592 | tf_op args[1]
  22.5 3.0 %copy.17.refs_2_.refs_6_ = bf16[3072,384]{1,0:T(8,128)(2,1)S(1)} copy(bf16[3072,384]{0,1:T(8,128)(2,1)} %bitcast.20) | data formatting | bytes 4718592 | tf_op jit(solution)/shard_map/reshape | solution.py:221
  25.7 1.0 constant_dynamic-update-slice_fusion.3
  26.7 1.0 constant_dynamic-update-slice_fusion.2.refs_1_
  27.7 1.0 constant_dynamic-update-slice_fusion.refs_0_
  28.7 1.5 project.2
  30.2 0.7 copy-done.3
  30.9 0.6 copy-done.5
  31.5 3.1 %collective-permute-start.1 = (bf16[96,3072]{1,0:T(8,128)(2,1)S(1)}, bf16[96,3072]{1,0:T(8,128)(2,1)S(1)}, u32[]{:S(2)}, u32[]{:S(2)}) collective-permute-start(bf16[96,3072]{1,0:T(8,128)(2,1)S(1)} %constant_dynamic-update-slice_fusion.refs_0_), channel_id=1, source_target_pairs={{0,128},{32,160},{64,192},{96,224},{128,256},{160,288},{192,320},{... | collective-permute-start | bytes 1769480 | tf_op jit(solution)/shard_map/ppermute | solution.py:34
  34.7 3.4 %collective-permute-start.6 = (bf16[96,3072]{1,0:T(8,128)(2,1)S(1)}, bf16[96,3072]{1,0:T(8,128)(2,1)S(1)}, u32[]{:S(2)}, u32[]{:S(2)}) collective-permute-start(bf16[96,3072]{1,0:T(8,128)(2,1)S(1)} %constant_dynamic-update-slice_fusion.2.refs_1_), channel_id=1, source_target_pairs={{0,384},{32,416},{64,448},{96,480},{128,0},{160,32},{192,64},{224,... | collective-permute-start | bytes 1769480 | tf_op jit(solution)/shard_map/ppermute | solution.py:34
  38.0 3.2 %collective-permute-start.5 = (bf16[96,3072]{1,0:T(8,128)(2,1)S(1)}, bf16[96,3072]{1,0:T(8,128)(2,1)S(1)}, u32[]{:S(2)}, u32[]{:S(2)}) collective-permute-start(bf16[96,3072]{1,0:T(8,128)(2,1)S(1)} %constant_dynamic-update-slice_fusion.refs_0_), channel_id=1, source_target_pairs={{0,384},{32,416},{64,448},{96,480},{128,0},{160,32},{192,64},{224,... | collective-permute-start | bytes 1769480 | tf_op jit(solution)/shard_map/ppermute | solution.py:34
  41.2 2.1 %collective-permute-start.4 = (bf16[96,3072]{1,0:T(8,128)(2,1)S(1)}, bf16[96,3072]{1,0:T(8,128)(2,1)S(1)}, u32[]{:S(2)}, u32[]{:S(2)}) collective-permute-start(bf16[96,3072]{1,0:T(8,128)(2,1)S(1)} %constant_dynamic-update-slice_fusion.2.refs_1_), channel_id=1, source_target_pairs={{0,128},{32,160},{64,192},{96,224},{128,256},{160,288},{192,320},{... | collective-permute-start | bytes 1769480 | tf_op jit(solution)/shard_map/ppermute | solution.py:34
  43.3 0.3 collective-permute-done.1.refs_0_
  43.7 1.9 collective-permute-start.7
  45.6 4.6 %collective-permute-start.8 = (bf16[96,3072]{1,0:T(8,128)(2,1)S(1)}, bf16[96,3072]{1,0:T(8,128)(2,1)S(1)}, u32[]{:S(2)}, u32[]{:S(2)}) collective-permute-start(bf16[96,3072]{1,0:T(8,128)(2,1)S(1)} %collective-permute-done.6.refs_3_), channel_id=1, source_target_pairs={{0,384},{32,416},{64,448},{96,480},{128,0},{160,32},{192,64},{224,... | collective-permute-start | bytes 1769480 | tf_op jit(solution)/shard_map/ppermute | solution.py:34
  50.2 1.7 collective-permute-done.5.refs_2_
  51.9 1.5 collective-permute-done.4.refs_1_
  53.4 6.4 %collective-permute-done.7.refs_4_ = bf16[96,3072]{1,0:T(8,128)(2,1)S(1)} collective-permute-done((bf16[96,3072]{1,0:T(8,128)(2,1)S(1)}, bf16[96,3072]{1,0:T(8,128)(2,1)S(1)}, u32[]{:S(2)}, u32[]{:S(2)}) %collective-permute-start.7) | collective-permute-done | bytes 589856 | tf_op jit(solution)/shard_map/ppermute | solution.py:34
  59.8 0.9 copy-done.4
  60.7 3.2 %project.3 = (bf16[768,128]{1,0:T(8,128)(2,1)S(1)}, bf16[576,256]{1,0:T(8,128)(2,1)S(1)}) custom-call(s32[6]{0:T(128)S(1)} %stack.36.place, bf16[96,3072]{1,0:T(8,128)(2,1)S(1)} %collective-permute-done.1.refs_0_, bf16[96,3072]{1,0:T(8,128)(2,1)S(1)} %collective-permute-done.4.refs_1_, bf16[96,3072]{1,0:T(8,128)(2,1)S(1)} %collective-permute-done.5.refs_2_, ...), custom_call_target="tpu_custom_call" | custom-call | tf_op jit(solution)/shard_map/project/pallas_call | solution.py:90
  64.0 0.1 reshape.331
  64.1 6.3 %collective-permute-start.9 = (bf16[1920,128]{1,0:T(8,128)(2,1)S(1)}, bf16[1920,128]{1,0:T(8,128)(2,1)S(1)}, u32[]{:S(2)}, u32[]{:S(2)}) collective-permute-start(bf16[1920,128]{1,0:T(8,128)(2,1)S(1)} %pad_maximum_fusion), channel_id=1, source_target_pairs={{0,1},{1,0},{2,3},{3,2},{4,5},{5,4},{6,7},{7,6},{8,9},{9,8},{10,11... | collective-permute-start | bytes 1474568 | tf_op jit(solution)/shard_map/ppermute | solution.py:38
  70.4 10.0 %collective-permute-start.10 = (bf16[576,256]{1,0:T(8,128)(2,1)S(1)}, bf16[576,256]{1,0:T(8,128)(2,1)S(1)}, u32[]{:S(2)}, u32[]{:S(2)}) collective-permute-start(bf16[576,256]{1,0:T(8,128)(2,1)S(1)} %get-tuple-element.11.refs_0_), channel_id=1, source_target_pairs={{0,2},{1,31},{2,4},{3,1},{4,6},{5,3},{6,8},{7,5},{8,10},{9,7},{10,... | collective-permute-start | bytes 884744 | tf_op jit(solution)/shard_map/ppermute | solution.py:46
  80.4 5.1 %collective-permute-done.10.refs_1_ = bf16[576,256]{1,0:T(8,128)(2,1)S(1)} collective-permute-done((bf16[576,256]{1,0:T(8,128)(2,1)S(1)}, bf16[576,256]{1,0:T(8,128)(2,1)S(1)}, u32[]{:S(2)}, u32[]{:S(2)}) %collective-permute-start.10) | collective-permute-done | bytes 294944 | tf_op jit(solution)/shard_map/ppermute | solution.py:46
  85.5 5.3 %collective-permute-start.11 = (bf16[576,256]{1,0:T(8,128)(2,1)S(1)}, bf16[576,256]{1,0:T(8,128)(2,1)S(1)}, u32[]{:S(2)}, u32[]{:S(2)}) collective-permute-start(bf16[576,256]{1,0:T(8,128)(2,1)S(1)} %collective-permute-done.10.refs_1_), channel_id=1, source_target_pairs={{0,2},{1,31},{2,4},{3,1},{4,6},{5,3},{6,8},{7,5},{8,10},{9,7},{10,... | collective-permute-start | bytes 884744 | tf_op jit(solution)/shard_map/ppermute | solution.py:46
  90.8 0.1 reshape.333
  90.9 1.9 collective-permute-start.18
  92.9 3.0 %collective-permute-done.11.refs_2_ = bf16[576,256]{1,0:T(8,128)(2,1)S(1)} collective-permute-done((bf16[576,256]{1,0:T(8,128)(2,1)S(1)}, bf16[576,256]{1,0:T(8,128)(2,1)S(1)}, u32[]{:S(2)}, u32[]{:S(2)}) %collective-permute-start.11) | collective-permute-done | bytes 294944 | tf_op jit(solution)/shard_map/ppermute | solution.py:46
  95.9 5.3 %collective-permute-start.12 = (bf16[576,256]{1,0:T(8,128)(2,1)S(1)}, bf16[576,256]{1,0:T(8,128)(2,1)S(1)}, u32[]{:S(2)}, u32[]{:S(2)}) collective-permute-start(bf16[576,256]{1,0:T(8,128)(2,1)S(1)} %collective-permute-done.11.refs_2_), channel_id=1, source_target_pairs={{0,2},{1,31},{2,4},{3,1},{4,6},{5,3},{6,8},{7,5},{8,10},{9,7},{10,... | collective-permute-start | bytes 884744 | tf_op jit(solution)/shard_map/ppermute | solution.py:46
  101.2 3.7 %collective-permute-start.19 = (bf16[576,256]{1,0:T(8,128)(2,1)S(1)}, bf16[576,256]{1,0:T(8,128)(2,1)S(1)}, u32[]{:S(2)}, u32[]{:S(2)}) collective-permute-start(bf16[576,256]{1,0:T(8,128)(2,1)S(1)} %collective-permute-done.18.refs_9_), channel_id=1, source_target_pairs={{0,2},{1,31},{2,4},{3,1},{4,6},{5,3},{6,8},{7,5},{8,10},{9,7},{10,... | collective-permute-start | bytes 884744 | tf_op jit(solution)/shard_map/ppermute | solution.py:46
  104.9 0.4 collective-permute-done.12.refs_3_
  105.3 5.0 %collective-permute-start.13 = (bf16[576,256]{1,0:T(8,128)(2,1)S(1)}, bf16[576,256]{1,0:T(8,128)(2,1)S(1)}, u32[]{:S(2)}, u32[]{:S(2)}) collective-permute-start(bf16[576,256]{1,0:T(8,128)(2,1)S(1)} %collective-permute-done.12.refs_3_), channel_id=1, source_target_pairs={{0,2},{1,31},{2,4},{3,1},{4,6},{5,3},{6,8},{7,5},{8,10},{9,7},{10,... | collective-permute-start | bytes 884744 | tf_op jit(solution)/shard_map/ppermute | solution.py:46
  110.3 3.3 %collective-permute-start.20 = (bf16[576,256]{1,0:T(8,128)(2,1)S(1)}, bf16[576,256]{1,0:T(8,128)(2,1)S(1)}, u32[]{:S(2)}, u32[]{:S(2)}) collective-permute-start(bf16[576,256]{1,0:T(8,128)(2,1)S(1)} %collective-permute-done.19.refs_10_), channel_id=1, source_target_pairs={{0,2},{1,31},{2,4},{3,1},{4,6},{5,3},{6,8},{7,5},{8,10},{9,7},{10,... | collective-permute-start | bytes 884744 | tf_op jit(solution)/shard_map/ppermute | solution.py:46
  113.7 0.3 collective-permute-done.13.refs_4_
  114.0 5.0 %collective-permute-start.14 = (bf16[576,256]{1,0:T(8,128)(2,1)S(1)}, bf16[576,256]{1,0:T(8,128)(2,1)S(1)}, u32[]{:S(2)}, u32[]{:S(2)}) collective-permute-start(bf16[576,256]{1,0:T(8,128)(2,1)S(1)} %collective-permute-done.13.refs_4_), channel_id=1, source_target_pairs={{0,2},{1,31},{2,4},{3,1},{4,6},{5,3},{6,8},{7,5},{8,10},{9,7},{10,... | collective-permute-start | bytes 884744 | tf_op jit(solution)/shard_map/ppermute | solution.py:46
  119.0 3.3 %collective-permute-start.21 = (bf16[576,256]{1,0:T(8,128)(2,1)S(1)}, bf16[576,256]{1,0:T(8,128)(2,1)S(1)}, u32[]{:S(2)}, u32[]{:S(2)}) collective-permute-start(bf16[576,256]{1,0:T(8,128)(2,1)S(1)} %collective-permute-done.20.refs_11_), channel_id=1, source_target_pairs={{0,2},{1,31},{2,4},{3,1},{4,6},{5,3},{6,8},{7,5},{8,10},{9,7},{10,... | collective-permute-start | bytes 884744 | tf_op jit(solution)/shard_map/ppermute | solution.py:46
  122.3 0.5 broadcast.466
  122.8 0.7 reduce.4
  123.5 0.1 reshape_squeeze.7
  123.7 3.9 %collective-permute-start.15 = (bf16[576,256]{1,0:T(8,128)(2,1)S(1)}, bf16[576,256]{1,0:T(8,128)(2,1)}, u32[]{:S(2)}, u32[]{:S(2)}) collective-permute-start(bf16[576,256]{1,0:T(8,128)(2,1)S(1)} %collective-permute-done.14.refs_5_), channel_id=1, source_target_pairs={{0,2},{1,31},{2,4},{3,1},{4,6},{5,3},{6,8},{7,5},{8,10},{9,7},{10,... | collective-permute-start | bytes 884744 | tf_op jit(solution)/shard_map/ppermute | solution.py:46
  127.7 3.3 %collective-permute-start.22 = (bf16[576,256]{1,0:T(8,128)(2,1)S(1)}, bf16[576,256]{1,0:T(8,128)(2,1)}, u32[]{:S(2)}, u32[]{:S(2)}) collective-permute-start(bf16[576,256]{1,0:T(8,128)(2,1)S(1)} %collective-permute-done.21.refs_12_), channel_id=1, source_target_pairs={{0,2},{1,31},{2,4},{3,1},{4,6},{5,3},{6,8},{7,5},{8,10},{9,7},{10,... | collective-permute-start | bytes 884744 | tf_op jit(solution)/shard_map/ppermute | solution.py:46
  131.0 0.6 gather_fusion.1
  131.8 0.5 gather_fusion
  132.3 0.2 convert_reduce_fusion
  132.6 3.8 %collective-permute-start.16 = (bf16[576,256]{1,0:T(8,128)(2,1)}, bf16[576,256]{1,0:T(8,128)(2,1)}, u32[]{:S(2)}, u32[]{:S(2)}) collective-permute-start(bf16[576,256]{1,0:T(8,128)(2,1)} %collective-permute-done.15.refs_6_), channel_id=1, source_target_pairs={{0,2},{1,31},{2,4},{3,1},{4,6},{5,3},{6,8},{7,5},{8,10},{9,7},{10,... | collective-permute-start | bytes 884744 | tf_op jit(solution)/shard_map/ppermute | solution.py:46
  136.4 3.3 %collective-permute-start.23 = (bf16[576,256]{1,0:T(8,128)(2,1)}, bf16[576,256]{1,0:T(8,128)(2,1)}, u32[]{:S(2)}, u32[]{:S(2)}) collective-permute-start(bf16[576,256]{1,0:T(8,128)(2,1)} %collective-permute-done.22.refs_13_), channel_id=1, source_target_pairs={{0,2},{1,31},{2,4},{3,1},{4,6},{5,3},{6,8},{7,5},{8,10},{9,7},{10,... | collective-permute-start | bytes 884744 | tf_op jit(solution)/shard_map/ppermute | solution.py:46
  139.8 0.2 reduce_window_sum.11
  140.1 0.6 collective-permute-done.16.refs_7_
  140.7 4.7 %collective-permute-start.17 = (bf16[576,256]{1,0:T(8,128)(2,1)}, bf16[576,256]{1,0:T(8,128)(2,1)}, u32[]{:S(2)}, u32[]{:S(2)}) collective-permute-start(bf16[576,256]{1,0:T(8,128)(2,1)} %collective-permute-done.16.refs_7_), channel_id=1, source_target_pairs={{0,2},{1,31},{2,4},{3,1},{4,6},{5,3},{6,8},{7,5},{8,10},{9,7},{10,... | collective-permute-start | bytes 884744 | tf_op jit(solution)/shard_map/ppermute | solution.py:46
  145.4 3.3 %collective-permute-start.24 = (bf16[576,256]{1,0:T(8,128)(2,1)}, bf16[576,256]{1,0:T(8,128)(2,1)}, u32[]{:S(2)}, u32[]{:S(2)}) collective-permute-start(bf16[576,256]{1,0:T(8,128)(2,1)} %collective-permute-done.23.refs_14_), channel_id=1, source_target_pairs={{0,2},{1,31},{2,4},{3,1},{4,6},{5,3},{6,8},{7,5},{8,10},{9,7},{10,... | collective-permute-start | bytes 884744 | tf_op jit(solution)/shard_map/ppermute | solution.py:46
  148.7 0.5 select_reduce_fusion.lists
  149.3 0.9 slice.28
  150.3 2.9 %collective-permute-done.24.refs_15_ = bf16[576,256]{1,0:T(8,128)(2,1)} collective-permute-done((bf16[576,256]{1,0:T(8,128)(2,1)}, bf16[576,256]{1,0:T(8,128)(2,1)}, u32[]{:S(2)}, u32[]{:S(2)}) %collective-permute-start.24) | collective-permute-done | bytes 294944 | tf_op jit(solution)/shard_map/ppermute | solution.py:46
  153.2 1.9 copy-done
  155.1 1.0 copy-done.2
  156.1 19.2 %attend.1 = f32[12,128,256]{2,1,0:T(8,128)S(1)} custom-call(s32[6]{0:T(128)S(1)} %stack.36.place, s32[12,64]{1,0:T(8,128)S(1)} %select_reduce_fusion.lists, s32[12]{0:T(128)S(1)} %reduce_sum.22.counts, bf16[12,128,128]{2,1,0:T(8,128)(2,1)S(1)} %bitcast.19, bf16[6144,256]{1,0:T(8,128)(2,1)S(1)} %copy-done, bf16[576,256]{1,0:T(8,128)(2,1)S(1)} %get-tuple-element.11.refs_0_, ...), custom_call_target="tpu_custom_call" | custom-call | tf_op jit(solution)/shard_map/attend/pallas_call | solution.py:172
  175.3 9.7 %collective-permute-start.25 = (f32[6,128,256]{2,1,0:T(8,128)S(1)}, f32[6,128,256]{2,1,0:T(8,128)S(1)}, u32[]{:S(2)}, u32[]{:S(2)}) collective-permute-start(f32[6,128,256]{2,1,0:T(8,128)S(1)} %slice.31), channel_id=1, source_target_pairs={{0,1},{1,0},{2,3},{3,2},{4,5},{5,4},{6,7},{7,6},{8,9},{9,8},{10,11... | collective-permute-start | bytes 2359304 | tf_op jit(solution)/shard_map/ppermute | solution.py:38
  185.0 1.9 collective-permute-done.25
  186.9 0.1 slice_add_fusion
  187.1 10.9 %all_to_all.19 = bf16[16,48,128]{2,1,0:T(8,128)(2,1)S(1)} all-to-all(bf16[16,48,128]{2,1,0:T(8,128)(2,1)S(1)} %bitcast.21), channel_id=1, replica_groups=mesh['seq'=16,'bal'=32] {'seq'}, dimensions={0} | all-to-all | bytes 393216 | tf_op jit(solution)/shard_map/all_to_all | solution.py:265
  198.0 0.7 copy_bitcast_fusion
  (55 shorter events, 0.9 us)
Async XLA Ops:
  6.5 146.7 %all-gather.2.cloned.1.call-start = ((), (), s32[]{:S(2)}) async-start(), calls=%async_computation.1 | async-start | bytes 3244032 | tf_op jit(solution)/shard_map/all_gather | solution.py:241
  6.5 21.1 %collective-permute-start = (bf16[48,3072]{1,0:T(8,128)(2,1)}, bf16[48,3072]{1,0:T(8,128)(2,1)}, u32[]{:S(2)}, u32[]{:S(2)}) collective-permute-start(bf16[48,3072]{1,0:T(8,128)(2,1)} %param.6), channel_id=1, source_target_pairs={{0,32},{32,64},{64,96},{96,0},{128,160},{160,192},{192,224},{224,1... | collective-permute-start | bytes 884744 | tf_op jit(solution)/shard_map/ppermute | solution.py:34
  10.6 16.1 %collective-permute-start.3 = (bf16[48,3072]{1,0:T(8,128)(2,1)}, bf16[48,3072]{1,0:T(8,128)(2,1)}, u32[]{:S(2)}, u32[]{:S(2)}) collective-permute-start(bf16[48,3072]{1,0:T(8,128)(2,1)} %param.6), channel_id=1, source_target_pairs={{0,64},{32,96},{64,0},{96,32},{128,192},{160,224},{192,128},{224,1... | collective-permute-start | bytes 884744 | tf_op jit(solution)/shard_map/ppermute | solution.py:34
  15.1 10.5 %collective-permute-start.2 = (bf16[48,3072]{1,0:T(8,128)(2,1)}, bf16[48,3072]{1,0:T(8,128)(2,1)}, u32[]{:S(2)}, u32[]{:S(2)}) collective-permute-start(bf16[48,3072]{1,0:T(8,128)(2,1)} %param.6), channel_id=1, source_target_pairs={{0,96},{32,0},{64,32},{96,64},{128,224},{160,128},{192,160},{224,1... | collective-permute-start | bytes 884744 | tf_op jit(solution)/shard_map/ppermute | solution.py:34
  22.4 3.2 %copy-start.9 = (bf16[48,3072]{1,0:T(8,128)(2,1)S(1)}, bf16[48,3072]{1,0:T(8,128)(2,1)}, u32[]{:S(2)}) copy-start(bf16[48,3072]{1,0:T(8,128)(2,1)} %param.6) | copy-start | bytes 884740
  25.5 3.1 %copy-start.6 = (f32[1,128]{1,0:T(1,128)S(1)}, f32[1,128]{1,0:T(1,128)}, u32[]{:S(2)}) copy-start(f32[1,128]{1,0:T(1,128)} %refs_7_.1) | copy-start | bytes 1540
  25.5 3.1 %copy-start.7 = (f32[1,128]{1,0:T(1,128)S(1)}, f32[1,128]{1,0:T(1,128)}, u32[]{:S(2)}) copy-start(f32[1,128]{1,0:T(1,128)} %refs_8_.1) | copy-start | bytes 1540
  30.2 0.7 copy-start.3
  30.9 0.6 copy-start.5
  31.5 12.1 %collective-permute-start.1 = (bf16[96,3072]{1,0:T(8,128)(2,1)S(1)}, bf16[96,3072]{1,0:T(8,128)(2,1)S(1)}, u32[]{:S(2)}, u32[]{:S(2)}) collective-permute-start(bf16[96,3072]{1,0:T(8,128)(2,1)S(1)} %constant_dynamic-update-slice_fusion.refs_0_), channel_id=1, source_target_pairs={{0,128},{32,160},{64,192},{96,224},{128,256},{160,288},{192,320},{... | collective-permute-start | bytes 1769480 | tf_op jit(solution)/shard_map/ppermute | solution.py:34
  34.7 10.9 %collective-permute-start.6 = (bf16[96,3072]{1,0:T(8,128)(2,1)S(1)}, bf16[96,3072]{1,0:T(8,128)(2,1)S(1)}, u32[]{:S(2)}, u32[]{:S(2)}) collective-permute-start(bf16[96,3072]{1,0:T(8,128)(2,1)S(1)} %constant_dynamic-update-slice_fusion.2.refs_1_), channel_id=1, source_target_pairs={{0,384},{32,416},{64,448},{96,480},{128,0},{160,32},{192,64},{224,... | collective-permute-start | bytes 1769480 | tf_op jit(solution)/shard_map/ppermute | solution.py:34
  38.0 13.9 %collective-permute-start.5 = (bf16[96,3072]{1,0:T(8,128)(2,1)S(1)}, bf16[96,3072]{1,0:T(8,128)(2,1)S(1)}, u32[]{:S(2)}, u32[]{:S(2)}) collective-permute-start(bf16[96,3072]{1,0:T(8,128)(2,1)S(1)} %constant_dynamic-update-slice_fusion.refs_0_), channel_id=1, source_target_pairs={{0,384},{32,416},{64,448},{96,480},{128,0},{160,32},{192,64},{224,... | collective-permute-start | bytes 1769480 | tf_op jit(solution)/shard_map/ppermute | solution.py:34
  41.2 12.1 %collective-permute-start.4 = (bf16[96,3072]{1,0:T(8,128)(2,1)S(1)}, bf16[96,3072]{1,0:T(8,128)(2,1)S(1)}, u32[]{:S(2)}, u32[]{:S(2)}) collective-permute-start(bf16[96,3072]{1,0:T(8,128)(2,1)S(1)} %constant_dynamic-update-slice_fusion.2.refs_1_), channel_id=1, source_target_pairs={{0,128},{32,160},{64,192},{96,224},{128,256},{160,288},{192,320},{... | collective-permute-start | bytes 1769480 | tf_op jit(solution)/shard_map/ppermute | solution.py:34
  43.7 16.1 %collective-permute-start.7 = (bf16[96,3072]{1,0:T(8,128)(2,1)S(1)}, bf16[96,3072]{1,0:T(8,128)(2,1)S(1)}, u32[]{:S(2)}, u32[]{:S(2)}) collective-permute-start(bf16[96,3072]{1,0:T(8,128)(2,1)S(1)} %collective-permute-done.1.refs_0_), channel_id=1, source_target_pairs={{0,128},{32,160},{64,192},{96,224},{128,256},{160,288},{192,320},{... | collective-permute-start | bytes 1769480 | tf_op jit(solution)/shard_map/ppermute | solution.py:34
  45.6 14.2 %collective-permute-start.8 = (bf16[96,3072]{1,0:T(8,128)(2,1)S(1)}, bf16[96,3072]{1,0:T(8,128)(2,1)S(1)}, u32[]{:S(2)}, u32[]{:S(2)}) collective-permute-start(bf16[96,3072]{1,0:T(8,128)(2,1)S(1)} %collective-permute-done.6.refs_3_), channel_id=1, source_target_pairs={{0,384},{32,416},{64,448},{96,480},{128,0},{160,32},{192,64},{224,... | collective-permute-start | bytes 1769480 | tf_op jit(solution)/shard_map/ppermute | solution.py:34
  59.8 0.9 copy-start.4
  64.0 58.9 %copy-start.11 = (s32[1,192]{1,0:T(1,128)S(1)}, s32[1,192]{1,0:T(1,128)}, u32[]{:S(2)}) copy-start(s32[1,192]{1,0:T(1,128)} %param.11) | copy-start | bytes 2308
  64.0 67.7 %copy-start.10 = (s32[1,192,64]{1,2,0:T(8,128)S(1)}, s32[1,192,64]{1,2,0:T(8,128)}, u32[]{:S(2)}) copy-start(s32[1,192,64]{1,2,0:T(8,128)} %param.10) | copy-start | bytes 147460
  64.1 26.6 %collective-permute-start.9 = (bf16[1920,128]{1,0:T(8,128)(2,1)S(1)}, bf16[1920,128]{1,0:T(8,128)(2,1)S(1)}, u32[]{:S(2)}, u32[]{:S(2)}) collective-permute-start(bf16[1920,128]{1,0:T(8,128)(2,1)S(1)} %pad_maximum_fusion), channel_id=1, source_target_pairs={{0,1},{1,0},{2,3},{3,2},{4,5},{5,4},{6,7},{7,6},{8,9},{9,8},{10,11... | collective-permute-start | bytes 1474568 | tf_op jit(solution)/shard_map/ppermute | solution.py:38
  70.4 15.1 %collective-permute-start.10 = (bf16[576,256]{1,0:T(8,128)(2,1)S(1)}, bf16[576,256]{1,0:T(8,128)(2,1)S(1)}, u32[]{:S(2)}, u32[]{:S(2)}) collective-permute-start(bf16[576,256]{1,0:T(8,128)(2,1)S(1)} %get-tuple-element.11.refs_0_), channel_id=1, source_target_pairs={{0,2},{1,31},{2,4},{3,1},{4,6},{5,3},{6,8},{7,5},{8,10},{9,7},{10,... | collective-permute-start | bytes 884744 | tf_op jit(solution)/shard_map/ppermute | solution.py:46
  85.5 10.4 %collective-permute-start.11 = (bf16[576,256]{1,0:T(8,128)(2,1)S(1)}, bf16[576,256]{1,0:T(8,128)(2,1)S(1)}, u32[]{:S(2)}, u32[]{:S(2)}) collective-permute-start(bf16[576,256]{1,0:T(8,128)(2,1)S(1)} %collective-permute-done.10.refs_1_), channel_id=1, source_target_pairs={{0,2},{1,31},{2,4},{3,1},{4,6},{5,3},{6,8},{7,5},{8,10},{9,7},{10,... | collective-permute-start | bytes 884744 | tf_op jit(solution)/shard_map/ppermute | solution.py:46
  90.8 19.5 %copy-start.8 = (bf16[1920,128]{1,0:T(8,128)(2,1)}, bf16[1920,128]{1,0:T(8,128)(2,1)S(1)}, u32[]{:S(2)}) copy-start(bf16[1920,128]{1,0:T(8,128)(2,1)S(1)} %collective-permute-done.9) | copy-start | bytes 1474564
  90.9 10.2 %collective-permute-start.18 = (bf16[576,256]{1,0:T(8,128)(2,1)S(1)}, bf16[576,256]{1,0:T(8,128)(2,1)S(1)}, u32[]{:S(2)}, u32[]{:S(2)}) collective-permute-start(bf16[576,256]{1,0:T(8,128)(2,1)S(1)} %reshape.333), channel_id=1, source_target_pairs={{0,2},{1,31},{2,4},{3,1},{4,6},{5,3},{6,8},{7,5},{8,10},{9,7},{10,... | collective-permute-start | bytes 884744 | tf_op jit(solution)/shard_map/ppermute | solution.py:46
  95.9 9.4 %collective-permute-start.12 = (bf16[576,256]{1,0:T(8,128)(2,1)S(1)}, bf16[576,256]{1,0:T(8,128)(2,1)S(1)}, u32[]{:S(2)}, u32[]{:S(2)}) collective-permute-start(bf16[576,256]{1,0:T(8,128)(2,1)S(1)} %collective-permute-done.11.refs_2_), channel_id=1, source_target_pairs={{0,2},{1,31},{2,4},{3,1},{4,6},{5,3},{6,8},{7,5},{8,10},{9,7},{10,... | collective-permute-start | bytes 884744 | tf_op jit(solution)/shard_map/ppermute | solution.py:46
  101.2 9.2 %collective-permute-start.19 = (bf16[576,256]{1,0:T(8,128)(2,1)S(1)}, bf16[576,256]{1,0:T(8,128)(2,1)S(1)}, u32[]{:S(2)}, u32[]{:S(2)}) collective-permute-start(bf16[576,256]{1,0:T(8,128)(2,1)S(1)} %collective-permute-done.18.refs_9_), channel_id=1, source_target_pairs={{0,2},{1,31},{2,4},{3,1},{4,6},{5,3},{6,8},{7,5},{8,10},{9,7},{10,... | collective-permute-start | bytes 884744 | tf_op jit(solution)/shard_map/ppermute | solution.py:46
  105.3 8.7 %collective-permute-start.13 = (bf16[576,256]{1,0:T(8,128)(2,1)S(1)}, bf16[576,256]{1,0:T(8,128)(2,1)S(1)}, u32[]{:S(2)}, u32[]{:S(2)}) collective-permute-start(bf16[576,256]{1,0:T(8,128)(2,1)S(1)} %collective-permute-done.12.refs_3_), channel_id=1, source_target_pairs={{0,2},{1,31},{2,4},{3,1},{4,6},{5,3},{6,8},{7,5},{8,10},{9,7},{10,... | collective-permute-start | bytes 884744 | tf_op jit(solution)/shard_map/ppermute | solution.py:46
  110.3 8.6 %collective-permute-start.20 = (bf16[576,256]{1,0:T(8,128)(2,1)S(1)}, bf16[576,256]{1,0:T(8,128)(2,1)S(1)}, u32[]{:S(2)}, u32[]{:S(2)}) collective-permute-start(bf16[576,256]{1,0:T(8,128)(2,1)S(1)} %collective-permute-done.19.refs_10_), channel_id=1, source_target_pairs={{0,2},{1,31},{2,4},{3,1},{4,6},{5,3},{6,8},{7,5},{8,10},{9,7},{10,... | collective-permute-start | bytes 884744 | tf_op jit(solution)/shard_map/ppermute | solution.py:46
  114.0 9.7 %collective-permute-start.14 = (bf16[576,256]{1,0:T(8,128)(2,1)S(1)}, bf16[576,256]{1,0:T(8,128)(2,1)S(1)}, u32[]{:S(2)}, u32[]{:S(2)}) collective-permute-start(bf16[576,256]{1,0:T(8,128)(2,1)S(1)} %collective-permute-done.13.refs_4_), channel_id=1, source_target_pairs={{0,2},{1,31},{2,4},{3,1},{4,6},{5,3},{6,8},{7,5},{8,10},{9,7},{10,... | collective-permute-start | bytes 884744 | tf_op jit(solution)/shard_map/ppermute | solution.py:46
  119.0 8.7 %collective-permute-start.21 = (bf16[576,256]{1,0:T(8,128)(2,1)S(1)}, bf16[576,256]{1,0:T(8,128)(2,1)S(1)}, u32[]{:S(2)}, u32[]{:S(2)}) collective-permute-start(bf16[576,256]{1,0:T(8,128)(2,1)S(1)} %collective-permute-done.20.refs_11_), channel_id=1, source_target_pairs={{0,2},{1,31},{2,4},{3,1},{4,6},{5,3},{6,8},{7,5},{8,10},{9,7},{10,... | collective-permute-start | bytes 884744 | tf_op jit(solution)/shard_map/ppermute | solution.py:46
  123.7 8.9 %collective-permute-start.15 = (bf16[576,256]{1,0:T(8,128)(2,1)S(1)}, bf16[576,256]{1,0:T(8,128)(2,1)}, u32[]{:S(2)}, u32[]{:S(2)}) collective-permute-start(bf16[576,256]{1,0:T(8,128)(2,1)S(1)} %collective-permute-done.14.refs_5_), channel_id=1, source_target_pairs={{0,2},{1,31},{2,4},{3,1},{4,6},{5,3},{6,8},{7,5},{8,10},{9,7},{10,... | collective-permute-start | bytes 884744 | tf_op jit(solution)/shard_map/ppermute | solution.py:46
  127.7 21.7 %copy-start.1 = (bf16[576,256]{1,0:T(8,128)(2,1)}, bf16[576,256]{1,0:T(8,128)(2,1)S(1)}, u32[]{:S(2)}) copy-start(bf16[576,256]{1,0:T(8,128)(2,1)S(1)} %collective-permute-done.21.refs_12_) | copy-start | bytes 884740
  127.7 8.8 %collective-permute-start.22 = (bf16[576,256]{1,0:T(8,128)(2,1)S(1)}, bf16[576,256]{1,0:T(8,128)(2,1)}, u32[]{:S(2)}, u32[]{:S(2)}) collective-permute-start(bf16[576,256]{1,0:T(8,128)(2,1)S(1)} %collective-permute-done.21.refs_12_), channel_id=1, source_target_pairs={{0,2},{1,31},{2,4},{3,1},{4,6},{5,3},{6,8},{7,5},{8,10},{9,7},{10,... | collective-permute-start | bytes 884744 | tf_op jit(solution)/shard_map/ppermute | solution.py:46
  132.6 8.1 %collective-permute-start.16 = (bf16[576,256]{1,0:T(8,128)(2,1)}, bf16[576,256]{1,0:T(8,128)(2,1)}, u32[]{:S(2)}, u32[]{:S(2)}) collective-permute-start(bf16[576,256]{1,0:T(8,128)(2,1)} %collective-permute-done.15.refs_6_), channel_id=1, source_target_pairs={{0,2},{1,31},{2,4},{3,1},{4,6},{5,3},{6,8},{7,5},{8,10},{9,7},{10,... | collective-permute-start | bytes 884744 | tf_op jit(solution)/shard_map/ppermute | solution.py:46
  136.4 9.0 %collective-permute-start.23 = (bf16[576,256]{1,0:T(8,128)(2,1)}, bf16[576,256]{1,0:T(8,128)(2,1)}, u32[]{:S(2)}, u32[]{:S(2)}) collective-permute-start(bf16[576,256]{1,0:T(8,128)(2,1)} %collective-permute-done.22.refs_13_), channel_id=1, source_target_pairs={{0,2},{1,31},{2,4},{3,1},{4,6},{5,3},{6,8},{7,5},{8,10},{9,7},{10,... | collective-permute-start | bytes 884744 | tf_op jit(solution)/shard_map/ppermute | solution.py:46
  140.7 9.7 %collective-permute-start.17 = (bf16[576,256]{1,0:T(8,128)(2,1)}, bf16[576,256]{1,0:T(8,128)(2,1)}, u32[]{:S(2)}, u32[]{:S(2)}) collective-permute-start(bf16[576,256]{1,0:T(8,128)(2,1)} %collective-permute-done.16.refs_7_), channel_id=1, source_target_pairs={{0,2},{1,31},{2,4},{3,1},{4,6},{5,3},{6,8},{7,5},{8,10},{9,7},{10,... | collective-permute-start | bytes 884744 | tf_op jit(solution)/shard_map/ppermute | solution.py:46
  145.4 7.8 %collective-permute-start.24 = (bf16[576,256]{1,0:T(8,128)(2,1)}, bf16[576,256]{1,0:T(8,128)(2,1)}, u32[]{:S(2)}, u32[]{:S(2)}) collective-permute-start(bf16[576,256]{1,0:T(8,128)(2,1)} %collective-permute-done.23.refs_14_), channel_id=1, source_target_pairs={{0,2},{1,31},{2,4},{3,1},{4,6},{5,3},{6,8},{7,5},{8,10},{9,7},{10,... | collective-permute-start | bytes 884744 | tf_op jit(solution)/shard_map/ppermute | solution.py:46
  153.2 1.9 copy-start
  155.1 1.0 copy-start.2
  175.3 11.6 %collective-permute-start.25 = (f32[6,128,256]{2,1,0:T(8,128)S(1)}, f32[6,128,256]{2,1,0:T(8,128)S(1)}, u32[]{:S(2)}, u32[]{:S(2)}) collective-permute-start(f32[6,128,256]{2,1,0:T(8,128)S(1)} %slice.31), channel_id=1, source_target_pairs={{0,1},{1,0},{2,3},{3,2},{4,5},{5,4},{6,7},{7,6},{8,9},{9,8},{10,11... | collective-permute-start | bytes 2359304 | tf_op jit(solution)/shard_map/ppermute | solution.py:38
Sparse Core Ops, SparseCore 0:
  31.7 77.3 all-gather.1

commit v3 on v1

v3 whole, which is shorter than its diff:
```python
import functools
import jax
import jax.numpy as jnp
from jax import lax
from jax.experimental import pallas as pl
from jax.experimental.pallas import tpu as pltpu
from jax.sharding import PartitionSpec as P

TILE = 128
HEAD = 128
PIECE = 48
GROUP = 8
LOG2E = 1.4426950408889634
MESH_AXES = ("seq", "bal")
VMEM = pl.BlockSpec(memory_space=pltpu.VMEM)
SMEM = pl.BlockSpec(memory_space=pltpu.SMEM)


def plane_perm(phase, shift):
    pairs = []
    for bal in range(32):
        for y in range(4):
            for x in range(4):
                along_x = (bal % 2 == 0) == (phase == 1)
                to_y = y if along_x else (y + shift) % 4
                to_x = (x + shift) % 4 if along_x else x
                pairs.append(((4 * y + x) * 32 + bal, (4 * to_y + to_x) * 32 + bal))
    return pairs


def send(block, phase, shift):
    return lax.ppermute(block, MESH_AXES, plane_perm(phase, shift))


def project_kernel(lines, carry, place, *refs):
    first = place[0]
    second = place[1]
    first_step = place[2]
    second_step = place[3]
    count = sum(len(halves) for _, halves in lines)
    blocks = refs[:count]
    weight, q_gain, k_gain = refs[count : count + 3]
    q_out, kv_out = refs[-2:]
    if carry:
        q_out[...] = refs[count + 3][...]
        kv_out[...] = refs[count + 4][...]

    def normalize(values, gain):
        mean_square = jnp.mean(values * values, axis=-1, keepdims=True)
        return (values * lax.rsqrt(mean_square + 1e-06) * gain).astype(jnp.bfloat16)

    whole = jnp.concatenate([weight[at] for at in range(3)], axis=1)
    at_block = 0
    for shift, halves in lines:
        for pieces in halves:
            proj = jnp.dot(blocks[at_block][...], whole, preferred_element_type=jnp.float32)
            at_block += 1
            query = normalize(proj[:, :HEAD], q_gain[...])
            key = normalize(proj[:, HEAD : 2 * HEAD], k_gain[...])
            value = proj[:, 2 * HEAD :].astype(jnp.bfloat16)
            for at, piece in enumerate(pieces):
                here = slice(at * PIECE, (at + 1) * PIECE)
                spot = ((first + piece) % 4) * first_step + ((second + shift) % 4) * second_step
                rows = pl.ds(pl.multiple_of(spot * PIECE, PIECE), PIECE)
                q_out[rows, :] = query[here]
                kv_out[rows, :HEAD] = key[here]
                kv_out[rows, HEAD:] = value[here]


def project(lines, blocks, weight, q_gain, k_gain, place, carried=()):
    rows = 16 * PIECE
    return pl.pallas_call(
        functools.partial(project_kernel, lines, len(carried) > 0),
        out_shape=(
            jax.ShapeDtypeStruct((rows, HEAD), jnp.bfloat16),
            jax.ShapeDtypeStruct((rows, 2 * HEAD), jnp.bfloat16),
        ),
        in_specs=[SMEM] + [VMEM] * (len(blocks) + 3 + len(carried)),
        out_specs=(VMEM, VMEM),
        compiler_params=pltpu.CompilerParams(vmem_limit_bytes=32 * 1024 * 1024),
        name="project",
    )(place, *blocks, weight, q_gain, k_gain, *carried)


def attend_kernel(scale, lists, counts, q, kv, out, held, ready):
    ones = jnp.ones((GROUP * TILE, HEAD), jnp.bfloat16)
    slots = q.shape[0]

    def fetch(slot, step, buffer):
        for at in range(GROUP):
            pick = lists[slot, step * GROUP + at]
            pltpu.make_async_copy(kv.at[pick], held.at[buffer, at], ready.at[buffer]).start()

    fetch(0, 0, 0)

    def one_slot(slot, turns_before):
        query = q[slot]
        count = counts[slot]
        turns = (count + GROUP - 1) // GROUP

        def turn(step, acc):
            buffer = (turns_before + step) % 2
            last = step + 1 == turns
            next_slot = jnp.where(last, slot + 1, slot)
            next_step = jnp.where(last, 0, step + 1)

            @pl.when(next_slot < slots)
            def _():
                fetch(next_slot, next_step, 1 - buffer)

            pltpu.make_async_copy(held.at[buffer], held.at[buffer], ready.at[buffer]).wait()
            keys = held[buffer, :, :, :HEAD].reshape(GROUP * TILE, HEAD)
            values = held[buffer, :, :, HEAD:].reshape(GROUP * TILE, HEAD)
            scores = lax.dot_general(
                query, keys, (((1,), (1,)), ((), ())), preferred_element_type=jnp.float32
            )
            live = (count - step * GROUP) * TILE
            column = lax.broadcasted_iota(jnp.int32, scores.shape, 1)
            weights = jnp.where(column < live, jnp.exp2(scores * scale), 0.0)
            return acc + jnp.dot(
                weights.astype(jnp.bfloat16),
                jnp.concatenate((values, ones), axis=1),
                preferred_element_type=jnp.float32,
            )

        acc = lax.fori_loop(0, turns, turn, jnp.zeros((TILE, 2 * HEAD), jnp.float32))
        out[slot] = (acc[:, :HEAD] / acc[:, HEAD:]).astype(jnp.bfloat16)
        return turns_before + turns

    lax.fori_loop(0, slots, one_slot, 0)


def attend(q, kv, lists, counts):
    scale = HEAD ** (-0.5) * LOG2E
    return pl.pallas_call(
        functools.partial(attend_kernel, scale),
        out_shape=jax.ShapeDtypeStruct(q.shape, jnp.bfloat16),
        in_specs=[SMEM, SMEM, VMEM, pl.BlockSpec(memory_space=pl.ANY)],
        out_specs=VMEM,
        scratch_shapes=[
            pltpu.VMEM((2, GROUP, TILE, 2 * HEAD), jnp.bfloat16),
            pltpu.SemaphoreType.DMA((2,)),
        ],
        compiler_params=pltpu.CompilerParams(vmem_limit_bytes=56 * 1024 * 1024),
        name="attend",
    )(lists, counts, q, kv)


def on_device(tokens, qkv_weight, q_gain, k_gain, key_tiles, key_counts):
    me_seq = lax.axis_index("seq")
    me_bal = lax.axis_index("bal")
    y, x = me_seq // 4, me_seq % 4
    core = me_bal % 2
    place = jnp.stack(
        (
            jnp.where(core == 0, x, y),
            jnp.where(core == 0, y, x),
            jnp.where(core == 0, 1, 4),
            jnp.where(core == 0, 4, 1),
        )
    ).astype(jnp.int32)
    slots = 16 * PIECE // TILE
    lists = lax.dynamic_slice_in_dim(key_tiles[0], me_bal * slots, slots, 0)
    counts = lax.dynamic_slice_in_dim(key_counts[0], me_bal * slots, slots, 0)

    before = send(tokens, 1, 1)
    after = send(tokens, 1, -1)
    across = send(tokens, 1, 2)
    low = jnp.concatenate((tokens, before), axis=0)
    before_low = send(low, 2, 1)
    high = jnp.concatenate((after, across), axis=0)
    after_high = send(high, 2, -1)
    after_low = send(low, 2, -1)
    before_high = send(high, 2, 1)
    across_low = send(before_low, 2, 1)
    across_high = send(after_high, 2, -1)

    weight = jnp.transpose(qkv_weight[:, 0], (1, 0, 2))
    halves = ((0, 3), (1, 2))
    early = project(
        ((0, halves), (3, halves), (1, halves)),
        (low, high, before_low, before_high, after_low, after_high),
        weight,
        q_gain,
        k_gain,
        place,
    )
    queries, pairs = project(
        ((2, halves),), (across_low, across_high), weight, q_gain, k_gain, place, early
    )
    all_pairs = lax.all_gather(pairs, "bal", axis=0, tiled=True)
    result = attend(
        queries.reshape(slots, TILE, HEAD),
        all_pairs.reshape(-1, TILE, 2 * HEAD),
        lists,
        counts,
    )
    return lax.all_to_all(
        result.reshape(slots * TILE, HEAD), "seq", split_axis=0, concat_axis=1, tiled=True
    )


def solution(mesh):
    placed = (
        P(("bal", "seq"), None),
        P(None, "seq", None, None),
        P("seq", None),
        P("seq", None),
        P("seq", None, None),
        P("seq", None),
    )
    return jax.shard_map(
        on_device, mesh=mesh, in_specs=placed, out_specs=P(("bal", "seq"), None), check_vma=False
    )
```

time: 198 us -> 189 us (0.955)
  waiting for transfers between devices: 113 us -> 97.1 us
  Pallas kernels: 14.4 us -> 23.7 us
  local copies, waits for them, and re-layouts: 15.1 us -> 8.46 us
  starting transfers between devices: 24.3 us -> 28.5 us
    ppermute x7 -> x9, waiting for transfers between devices: 19.2 us -> 8.11 us  [send(): return lax.ppermute(block, MESH_AXES, plane_perm(phase, shift))]
    pallas_call x1, Pallas kernels: 9.7 us -> 17 us  [attend(): pl.pallas_call(functools.partial(attend_kernel, scale), out_shape=jax.Sha...]
    all_gather x1, waiting for transfers between devices: 93.6 us -> 89 us  [on_device(): all_pairs = lax.all_gather(pairs, 'bal', axis=0, tiled=True)]
    ppermute x7 -> x9, starting transfers between devices: 24.3 us -> 28.5 us  [send(): return lax.ppermute(block, MESH_AXES, plane_perm(phase, shift))]
    unnamed x26 -> x16, local copies, waits for them, and re-layouts: 9.38 us -> 6.33 us
    reshape x1 -> x0, local copies, waits for them, and re-layouts: 3.02 us -> none  [on_device(): weight = qkv_weight.reshape(qkv_weight.shape[0], 3 * HEAD)]
    pallas_call x1 -> x2, Pallas kernels: 4.73 us -> 6.73 us  [project(): pl.pallas_call(functools.partial(project_kernel, lines, len(carried) > 0)...]
  transfers between devices with their start and end apart: 8 -> 10, of which waited for: 4 -> 5; matrix products, arithmetic and copies ran while one was open for 4% -> 1% of each run, Pallas kernels for 0% -> 2%
where the time goes in v3:
time: 189 us; the launch traced here: 187 us
  waiting for transfers between devices  97.1 us (51%)
  starting transfers between devices  28.5 us (15%)
  Pallas kernels  23.7 us (13%)
  blocking collectives  15.9 us (8%)
  between operations  13.6 us (7%)
  local copies, waits for them, and re-layouts  8.46 us (4%)
    all_gather x1, waiting for transfers between devices, on_device(): all_pairs = lax.all_gather(pairs, 'bal', axis=0, tiled=True)  89 us
    ppermute x9, starting transfers between devices, send(): return lax.ppermute(block, MESH_AXES, plane_perm(phase, shift))  28.5 us
    pallas_call x1, Pallas kernels, attend(): pl.pallas_call(functools.partial(attend_kernel, scale), out_shape=jax.Sha...  17 us
    all_to_all x1, blocking collectives, on_device(): lax.all_to_all(result.reshape(slots * TILE, HEAD), 'seq', split_axis=0, c...  15.9 us
    ppermute x9, waiting for transfers between devices, send(): return lax.ppermute(block, MESH_AXES, plane_perm(phase, shift))  8.11 us
    pallas_call x2, Pallas kernels, project(): pl.pallas_call(functools.partial(project_kernel, lines, len(carried) > 0)...  6.73 us
    unnamed x16, local copies, waits for them, and re-layouts  6.33 us
  transfers between devices with their start and end apart: 10, of which 5 were waited for; matrix products, arithmetic and copies ran while one was open for 1% of the time, Pallas kernels for 2%

profile of v3, /device:TPU:1, one launch (start us, length us, event | category | flops | bytes accessed | tf_op | source)
XLA Modules:
  0.0 187.4 jit_solution(14982890827420044262)
XLA Ops:
  6.5 0.0 copy-start
  6.5 0.0 copy-start.6
  6.5 0.0 all-gather.2.cloned.1.call-start
  6.5 5.6 %collective-permute-start.3 = (bf16[48,3072]{1,0:T(8,128)(2,1)}, bf16[48,3072]{1,0:T(8,128)(2,1)S(1)}, u32[]{:S(2)}, u32[]{:S(2)}) collective-permute-start(bf16[48,3072]{1,0:T(8,128)(2,1)} %param.6), channel_id=1, source_target_pairs={{0,96},{32,0},{64,32},{96,64},{128,224},{160,128},{192,160},{224,1... | collective-permute-start | bytes 884744 | tf_op jit(solution)/shard_map/ppermute | solution.py:32
  12.1 2.3 %collective-permute-start.4 = (bf16[48,3072]{1,0:T(8,128)(2,1)}, bf16[48,3072]{1,0:T(8,128)(2,1)S(1)}, u32[]{:S(2)}, u32[]{:S(2)}) collective-permute-start(bf16[48,3072]{1,0:T(8,128)(2,1)} %param.6), channel_id=1, source_target_pairs={{0,64},{32,96},{64,0},{96,32},{128,192},{160,224},{192,128},{224,1... | collective-permute-start | bytes 884744 | tf_op jit(solution)/shard_map/ppermute | solution.py:32
  14.4 2.6 %collective-permute-start = (bf16[48,3072]{1,0:T(8,128)(2,1)}, bf16[48,3072]{1,0:T(8,128)(2,1)S(1)}, u32[]{:S(2)}, u32[]{:S(2)}) collective-permute-start(bf16[48,3072]{1,0:T(8,128)(2,1)} %param.6), channel_id=1, source_target_pairs={{0,32},{32,64},{64,96},{96,0},{128,160},{160,192},{192,224},{224,1... | collective-permute-start | bytes 884744 | tf_op jit(solution)/shard_map/ppermute | solution.py:32
  17.0 1.0 constant_dynamic-update-slice_fusion.1
  18.0 1.3 collective-permute-done.3
  19.3 2.1 %collective-permute-done.4 = bf16[48,3072]{1,0:T(8,128)(2,1)S(1)} collective-permute-done((bf16[48,3072]{1,0:T(8,128)(2,1)}, bf16[48,3072]{1,0:T(8,128)(2,1)S(1)}, u32[]{:S(2)}, u32[]{:S(2)}) %collective-permute-start.4) | collective-permute-done | bytes 294944 | tf_op jit(solution)/shard_map/ppermute | solution.py:32
  21.5 4.4 %collective-permute-start.5 = (bf16[96,3072]{1,0:T(8,128)(2,1)S(1)}, bf16[96,3072]{1,0:T(8,128)(2,1)S(1)}, u32[]{:S(2)}, u32[]{:S(2)}) collective-permute-start(bf16[96,3072]{1,0:T(8,128)(2,1)S(1)} %constant_dynamic-update-slice_fusion.2.refs_1_), channel_id=1, source_target_pairs={{0,384},{32,416},{64,448},{96,480},{128,0},{160,32},{192,64},{224,... | collective-permute-start | bytes 1769480 | tf_op jit(solution)/shard_map/ppermute | solution.py:32
  25.8 0.0 collective-permute-done
  25.9 1.9 %collective-permute-start.1 = (bf16[96,3072]{1,0:T(8,128)(2,1)S(1)}, bf16[96,3072]{1,0:T(8,128)(2,1)S(1)}, u32[]{:S(2)}, u32[]{:S(2)}) collective-permute-start(bf16[96,3072]{1,0:T(8,128)(2,1)S(1)} %constant_dynamic-update-slice_fusion.refs_0_), channel_id=1, source_target_pairs={{0,128},{32,160},{64,192},{96,224},{128,256},{160,288},{192,320},{... | collective-permute-start | bytes 1769480 | tf_op jit(solution)/shard_map/ppermute | solution.py:32
  27.8 2.9 %collective-permute-start.7 = (bf16[96,3072]{1,0:T(8,128)(2,1)S(1)}, bf16[96,3072]{1,0:T(8,128)(2,1)}, u32[]{:S(2)}, u32[]{:S(2)}) collective-permute-start(bf16[96,3072]{1,0:T(8,128)(2,1)S(1)} %constant_dynamic-update-slice_fusion.2.refs_1_), channel_id=1, source_target_pairs={{0,128},{32,160},{64,192},{96,224},{128,256},{160,288},{192,320},{... | collective-permute-start | bytes 1769480 | tf_op jit(solution)/shard_map/ppermute | solution.py:32
  30.8 3.6 %collective-permute-start.8 = (bf16[96,3072]{1,0:T(8,128)(2,1)S(1)}, bf16[96,3072]{1,0:T(8,128)(2,1)}, u32[]{:S(2)}, u32[]{:S(2)}) collective-permute-start(bf16[96,3072]{1,0:T(8,128)(2,1)S(1)} %constant_dynamic-update-slice_fusion.refs_0_), channel_id=1, source_target_pairs={{0,384},{32,416},{64,448},{96,480},{128,0},{160,32},{192,64},{224,... | collective-permute-start | bytes 1769480 | tf_op jit(solution)/shard_map/ppermute | solution.py:32
  34.3 0.0 collective-permute-done.5.refs_5_
  34.3 3.4 %collective-permute-start.6 = (bf16[96,3072]{1,0:T(8,128)(2,1)S(1)}, bf16[96,3072]{1,0:T(8,128)(2,1)S(1)}, u32[]{:S(2)}, u32[]{:S(2)}) collective-permute-start(bf16[96,3072]{1,0:T(8,128)(2,1)S(1)} %collective-permute-done.5.refs_5_), channel_id=1, source_target_pairs={{0,384},{32,416},{64,448},{96,480},{128,0},{160,32},{192,64},{224,... | collective-permute-start | bytes 1769480 | tf_op jit(solution)/shard_map/ppermute | solution.py:32
  37.7 0.3 collective-permute-done.1.refs_2_
  38.0 1.9 %collective-permute-start.2 = (bf16[96,3072]{1,0:T(8,128)(2,1)S(1)}, bf16[96,3072]{1,0:T(8,128)(2,1)}, u32[]{:S(2)}, u32[]{:S(2)}) collective-permute-start(bf16[96,3072]{1,0:T(8,128)(2,1)S(1)} %collective-permute-done.1.refs_2_), channel_id=1, source_target_pairs={{0,128},{32,160},{64,192},{96,224},{128,256},{160,288},{192,320},{... | collective-permute-start | bytes 1769480 | tf_op jit(solution)/shard_map/ppermute | solution.py:32
  40.0 0.1 pad_add_fusion.place
  40.1 4.4 %collective-permute-done.7.refs_3_ = bf16[96,3072]{1,0:T(8,128)(2,1)} collective-permute-done((bf16[96,3072]{1,0:T(8,128)(2,1)S(1)}, bf16[96,3072]{1,0:T(8,128)(2,1)}, u32[]{:S(2)}, u32[]{:S(2)}) %collective-permute-start.7) | collective-permute-done | bytes 589856 | tf_op jit(solution)/shard_map/ppermute | solution.py:32
  44.4 0.0 collective-permute-done.8.refs_4_
  44.4 0.0 copy-start.1
  44.4 1.7 copy-done.1
  46.1 0.0 copy-start.4
  46.1 0.7 copy-done.4
  46.8 0.0 copy-start.5
  46.8 0.7 copy-done.5
  47.4 3.8 %project.2 = (bf16[768,128]{1,0:T(8,128)(2,1)S(1)}, bf16[768,256]{1,0:T(8,128)(2,1)S(1)}) custom-call(s32[4]{0:T(128)S(1)} %pad_add_fusion.place, bf16[96,3072]{1,0:T(8,128)(2,1)S(1)} %constant_dynamic-update-slice_fusion.refs_0_, bf16[96,3072]{1,0:T(8,128)(2,1)S(1)} %constant_dynamic-update-slice_fusion.2.refs_1_, ...), custom_call_target="tpu_custom_call" | custom-call | tf_op jit(solution)/shard_map/project/pallas_call | solution.py:72
  51.3 0.0 collective-permute-done.6.refs_1_
  51.3 0.0 collective-permute-done.2.refs_0_
  51.3 0.0 copy-start.2
  51.3 1.7 copy-done.2
  53.0 2.9 %project.3 = (bf16[768,128]{1,0:T(8,128)(2,1)S(1)}, bf16[768,256]{1,0:T(8,128)(2,1)}) custom-call(s32[4]{0:T(128)S(1)} %pad_add_fusion.place, bf16[96,3072]{1,0:T(8,128)(2,1)} %collective-permute-done.2.refs_0_, bf16[96,3072]{1,0:T(8,128)(2,1)S(1)} %collective-permute-done.6.refs_1_, bf16[3,3072,128]{2,1,0:T(8,128)(2,1)S(1)} %bitcast.20, ...), custom_call_target="tpu_custom_call" | custom-call | tf_op jit(solution)/shard_map/project/pallas_call | solution.py:72
  55.9 0.0 copy-start.3
  55.9 0.7 copy-done.3
  56.5 0.0 all-gather.2.cloned.1.call-update
  56.6 0.0 copy-done
  56.6 0.1 constant_dynamic-slice_fusion
  56.7 0.7 copy.7
  57.3 0.0 copy-done.6
  57.3 0.6 dynamic-slice_bitcast_fusion.counts
  58.0 89.0 %all-gather.2.cloned.1.call-done = bf16[24576,256]{1,0:T(8,128)(2,1)} async-done(((bf16[768,256]{1,0:T(8,128)(2,1)}), bf16[24576,256]{1,0:T(8,128)(2,1)}) %all-gather.2.cloned.1.call-update) | async-done | bytes 12582928 | tf_op jit(solution)/shard_map/all_gather | solution.py:191
  146.9 17.0 %attend.1 = bf16[6,128,128]{2,1,0:T(8,128)(2,1)} custom-call(s32[6,64]{1,0:T(8,128)} %bitcast.24, s32[6]{0:T(128)} %dynamic-slice_bitcast_fusion.counts, bf16[6,128,128]{2,1,0:T(8,128)(2,1)} %bitcast.21, bf16[192,128,256]{2,1,0:T(8,128)(2,1)} %bitcast.22), custom_call_target="tpu_custom_call" | custom-call | tf_op jit(solution)/shard_map/attend/pallas_call | solution.py:135
  163.9 15.9 %all_to_all.19 = bf16[16,48,128]{2,1,0:T(8,128)(2,1)S(1)} all-to-all(bf16[16,48,128]{2,1,0:T(8,128)(2,1)} %bitcast.23), channel_id=1, replica_groups=mesh['seq'=16,'bal'=32] {'seq'}, dimensions={0} | all-to-all | bytes 393216 | tf_op jit(solution)/shard_map/all_to_all | solution.py:198
  179.8 0.7 copy_bitcast_fusion
  (3 shorter events, 0.1 us)
Async XLA Ops:
  6.5 50.0 %copy-start = (s32[1,192,64]{1,2,0:T(8,128)S(1)}, s32[1,192,64]{1,2,0:T(8,128)}, u32[]{:S(2)}) copy-start(s32[1,192,64]{1,2,0:T(8,128)} %param.10) | copy-start | bytes 147460
  6.5 50.8 %copy-start.6 = (s32[1,192]{1,0:T(1,128)S(1)}, s32[1,192]{1,0:T(1,128)}, u32[]{:S(2)}) copy-start(s32[1,192]{1,0:T(1,128)} %param.11) | copy-start | bytes 2308
  6.5 140.4 %all-gather.2.cloned.1.call-start = ((), (), s32[]{:S(2)}) async-start(), calls=%async_computation.1 | async-start | bytes 12976128 | tf_op jit(solution)/shard_map/all_gather | solution.py:191
  6.5 12.8 %collective-permute-start.3 = (bf16[48,3072]{1,0:T(8,128)(2,1)}, bf16[48,3072]{1,0:T(8,128)(2,1)S(1)}, u32[]{:S(2)}, u32[]{:S(2)}) collective-permute-start(bf16[48,3072]{1,0:T(8,128)(2,1)} %param.6), channel_id=1, source_target_pairs={{0,96},{32,0},{64,32},{96,64},{128,224},{160,128},{192,160},{224,1... | collective-permute-start | bytes 884744 | tf_op jit(solution)/shard_map/ppermute | solution.py:32
  12.1 9.3 %collective-permute-start.4 = (bf16[48,3072]{1,0:T(8,128)(2,1)}, bf16[48,3072]{1,0:T(8,128)(2,1)S(1)}, u32[]{:S(2)}, u32[]{:S(2)}) collective-permute-start(bf16[48,3072]{1,0:T(8,128)(2,1)} %param.6), channel_id=1, source_target_pairs={{0,64},{32,96},{64,0},{96,32},{128,192},{160,224},{192,128},{224,1... | collective-permute-start | bytes 884744 | tf_op jit(solution)/shard_map/ppermute | solution.py:32
  14.4 11.4 %collective-permute-start = (bf16[48,3072]{1,0:T(8,128)(2,1)}, bf16[48,3072]{1,0:T(8,128)(2,1)S(1)}, u32[]{:S(2)}, u32[]{:S(2)}) collective-permute-start(bf16[48,3072]{1,0:T(8,128)(2,1)} %param.6), channel_id=1, source_target_pairs={{0,32},{32,64},{64,96},{96,0},{128,160},{160,192},{192,224},{224,1... | collective-permute-start | bytes 884744 | tf_op jit(solution)/shard_map/ppermute | solution.py:32
  21.5 12.9 %collective-permute-start.5 = (bf16[96,3072]{1,0:T(8,128)(2,1)S(1)}, bf16[96,3072]{1,0:T(8,128)(2,1)S(1)}, u32[]{:S(2)}, u32[]{:S(2)}) collective-permute-start(bf16[96,3072]{1,0:T(8,128)(2,1)S(1)} %constant_dynamic-update-slice_fusion.2.refs_1_), channel_id=1, source_target_pairs={{0,384},{32,416},{64,448},{96,480},{128,0},{160,32},{192,64},{224,... | collective-permute-start | bytes 1769480 | tf_op jit(solution)/shard_map/ppermute | solution.py:32
  25.9 12.1 %collective-permute-start.1 = (bf16[96,3072]{1,0:T(8,128)(2,1)S(1)}, bf16[96,3072]{1,0:T(8,128)(2,1)S(1)}, u32[]{:S(2)}, u32[]{:S(2)}) collective-permute-start(bf16[96,3072]{1,0:T(8,128)(2,1)S(1)} %constant_dynamic-update-slice_fusion.refs_0_), channel_id=1, source_target_pairs={{0,128},{32,160},{64,192},{96,224},{128,256},{160,288},{192,320},{... | collective-permute-start | bytes 1769480 | tf_op jit(solution)/shard_map/ppermute | solution.py:32
  27.8 16.6 %collective-permute-start.7 = (bf16[96,3072]{1,0:T(8,128)(2,1)S(1)}, bf16[96,3072]{1,0:T(8,128)(2,1)}, u32[]{:S(2)}, u32[]{:S(2)}) collective-permute-start(bf16[96,3072]{1,0:T(8,128)(2,1)S(1)} %constant_dynamic-update-slice_fusion.2.refs_1_), channel_id=1, source_target_pairs={{0,128},{32,160},{64,192},{96,224},{128,256},{160,288},{192,320},{... | collective-permute-start | bytes 1769480 | tf_op jit(solution)/shard_map/ppermute | solution.py:32
  30.8 13.7 %collective-permute-start.8 = (bf16[96,3072]{1,0:T(8,128)(2,1)S(1)}, bf16[96,3072]{1,0:T(8,128)(2,1)}, u32[]{:S(2)}, u32[]{:S(2)}) collective-permute-start(bf16[96,3072]{1,0:T(8,128)(2,1)S(1)} %constant_dynamic-update-slice_fusion.refs_0_), channel_id=1, source_target_pairs={{0,384},{32,416},{64,448},{96,480},{128,0},{160,32},{192,64},{224,... | collective-permute-start | bytes 1769480 | tf_op jit(solution)/shard_map/ppermute | solution.py:32
  34.3 16.9 %collective-permute-start.6 = (bf16[96,3072]{1,0:T(8,128)(2,1)S(1)}, bf16[96,3072]{1,0:T(8,128)(2,1)S(1)}, u32[]{:S(2)}, u32[]{:S(2)}) collective-permute-start(bf16[96,3072]{1,0:T(8,128)(2,1)S(1)} %collective-permute-done.5.refs_5_), channel_id=1, source_target_pairs={{0,384},{32,416},{64,448},{96,480},{128,0},{160,32},{192,64},{224,... | collective-permute-start | bytes 1769480 | tf_op jit(solution)/shard_map/ppermute | solution.py:32
  38.0 13.3 %collective-permute-start.2 = (bf16[96,3072]{1,0:T(8,128)(2,1)S(1)}, bf16[96,3072]{1,0:T(8,128)(2,1)}, u32[]{:S(2)}, u32[]{:S(2)}) collective-permute-start(bf16[96,3072]{1,0:T(8,128)(2,1)S(1)} %collective-permute-done.1.refs_2_), channel_id=1, source_target_pairs={{0,128},{32,160},{64,192},{96,224},{128,256},{160,288},{192,320},{... | collective-permute-start | bytes 1769480 | tf_op jit(solution)/shard_map/ppermute | solution.py:32
  44.4 1.7 copy-start.1
  46.1 0.7 copy-start.4
  46.8 0.7 copy-start.5
  51.3 1.7 copy-start.2
  55.9 0.7 copy-start.3
Sparse Core Ops, SparseCore 0:
  56.7 90.1 all-gather.1

commit v4 on v3

v4 whole, which is shorter than its diff:
```python
import functools
import jax
import jax.numpy as jnp
from jax import lax
from jax.experimental import pallas as pl
from jax.experimental.pallas import tpu as pltpu
from jax.sharding import PartitionSpec as P

TILE = 128
HEAD = 128
PIECE = 48
GROUP = 8
BUFFERS = 8
LOG2E = 1.4426950408889634
MESH_AXES = ("seq", "bal")
VMEM = pl.BlockSpec(memory_space=pltpu.VMEM)
SMEM = pl.BlockSpec(memory_space=pltpu.SMEM)


def plane_perm(phase, shift):
    pairs = []
    for bal in range(32):
        for y in range(4):
            for x in range(4):
                along_x = (bal % 2 == 0) == (phase == 1)
                to_y = y if along_x else (y + shift) % 4
                to_x = (x + shift) % 4 if along_x else x
                pairs.append(((4 * y + x) * 32 + bal, (4 * to_y + to_x) * 32 + bal))
    return pairs


def send(block, phase, shift):
    return lax.ppermute(block, MESH_AXES, plane_perm(phase, shift))


def project_kernel(shares, place, *refs):
    count = len(shares)
    blocks = refs[:count]
    weight, q_gain, k_gain = refs[count : count + 3]
    q_out, kv_out, block_in, weight_in, gain_in, q_held, kv_held, arrive, leave = refs[-9:]
    first = place[0]
    second = place[1]
    first_step = place[2]
    second_step = place[3]
    half = 2 * PIECE

    copies = [
        pltpu.make_async_copy(weight, weight_in, arrive.at[count]),
        pltpu.make_async_copy(q_gain, gain_in.at[0], arrive.at[count + 1]),
        pltpu.make_async_copy(k_gain, gain_in.at[1], arrive.at[count + 2]),
    ]
    for at in range(count):
        copies.append(pltpu.make_async_copy(blocks[at], block_in.at[at], arrive.at[at]))
    for copy in copies:
        copy.start()
    for copy in copies[:3]:
        copy.wait()

    def normalize(values, gain):
        mean_square = jnp.mean(values * values, axis=-1, keepdims=True)
        return (values * lax.rsqrt(mean_square + 1e-06) * gain).astype(jnp.bfloat16)

    whole = jnp.concatenate([weight_in[at] for at in range(3)], axis=1)
    for at, (shift, pieces) in enumerate(shares):
        copies[3 + at].wait()
        proj = jnp.dot(block_in[at], whole, preferred_element_type=jnp.float32)
        here = slice(at * half, (at + 1) * half)
        q_held[here, :] = normalize(proj[:, :HEAD], gain_in[0])
        kv_held[here, :HEAD] = normalize(proj[:, HEAD : 2 * HEAD], gain_in[1])
        kv_held[here, HEAD:] = proj[:, 2 * HEAD :].astype(jnp.bfloat16)
        for order, piece in enumerate(pieces):
            spot = ((first + piece) % 4) * first_step + ((second + shift) % 4) * second_step
            rows = pl.ds(pl.multiple_of(spot * PIECE, PIECE), PIECE)
            source = pl.ds(at * half + order * PIECE, PIECE)
            pltpu.make_async_copy(q_held.at[source, :], q_out.at[rows, :], leave.at[0]).start()
            pltpu.make_async_copy(kv_held.at[source, :], kv_out.at[rows, :], leave.at[1]).start()
    pltpu.make_async_copy(q_held, q_held, leave.at[0]).wait()
    pltpu.make_async_copy(kv_held, kv_held, leave.at[1]).wait()


def project(shares, blocks, weight, q_gain, k_gain, place, begun=()):
    rows = 16 * PIECE
    count = len(blocks)
    done_rows = count * 2 * PIECE
    width = blocks[0].shape[1]
    anywhere = pl.BlockSpec(memory_space=pl.ANY)
    return pl.pallas_call(
        functools.partial(project_kernel, shares),
        out_shape=(
            jax.ShapeDtypeStruct((rows, HEAD), jnp.bfloat16),
            jax.ShapeDtypeStruct((rows, 2 * HEAD), jnp.bfloat16),
        ),
        in_specs=[SMEM] + [anywhere] * (count + 3 + len(begun)),
        out_specs=(anywhere, anywhere),
        scratch_shapes=[
            pltpu.VMEM((count, 2 * PIECE, width), jnp.bfloat16),
            pltpu.VMEM((3, width, HEAD), jnp.bfloat16),
            pltpu.VMEM((2, 1, HEAD), jnp.float32),
            pltpu.VMEM((done_rows, HEAD), jnp.bfloat16),
            pltpu.VMEM((done_rows, 2 * HEAD), jnp.bfloat16),
            pltpu.SemaphoreType.DMA((count + 3,)),
            pltpu.SemaphoreType.DMA((2,)),
        ],
        input_output_aliases={count + 4: 0, count + 5: 1} if begun else {},
        compiler_params=pltpu.CompilerParams(vmem_limit_bytes=56 * 1024 * 1024),
        name="project",
    )(place, *blocks, weight, q_gain, k_gain, *begun)


def attend_kernel(scale, lists, counts, q, kv, out, held, ready):
    ones = jnp.ones((GROUP * TILE, HEAD), jnp.bfloat16)
    slots = q.shape[0]

    def turns_of(slot):
        return (counts[slot] + GROUP - 1) // GROUP

    def fetch(ahead, buffer):
        slot, step = ahead

        @pl.when(slot < slots)
        def _():
            for at in range(GROUP):
                pick = lists[slot, step * GROUP + at]
                pltpu.make_async_copy(kv.at[pick], held.at[buffer, at], ready.at[buffer]).start()

        last = step + 1 >= turns_of(jnp.minimum(slot, slots - 1))
        return jnp.where(last, slot + 1, slot), jnp.where(last, 0, step + 1)

    ahead = (jnp.int32(0), jnp.int32(0))
    for buffer in range(BUFFERS - 1):
        ahead = fetch(ahead, buffer)

    def one_slot(slot, carry):
        query = q[slot]
        count = counts[slot]

        def turn(step, carry):
            acc, group, ahead = carry
            buffer = group % BUFFERS
            ahead = fetch(ahead, (group + BUFFERS - 1) % BUFFERS)
            pltpu.make_async_copy(held.at[buffer], held.at[buffer], ready.at[buffer]).wait()
            keys = held[buffer, :, :, :HEAD].reshape(GROUP * TILE, HEAD)
            values = held[buffer, :, :, HEAD:].reshape(GROUP * TILE, HEAD)
            scores = lax.dot_general(
                query, keys, (((1,), (1,)), ((), ())), preferred_element_type=jnp.float32
            )
            live = (count - step * GROUP) * TILE
            column = lax.broadcasted_iota(jnp.int32, scores.shape, 1)
            weights = jnp.where(column < live, jnp.exp2(scores * scale), 0.0)
            acc = acc + jnp.dot(
                weights.astype(jnp.bfloat16),
                jnp.concatenate((values, ones), axis=1),
                preferred_element_type=jnp.float32,
            )
            return acc, group + 1, ahead

        acc, group, ahead = lax.fori_loop(
            0, turns_of(slot), turn, (jnp.zeros((TILE, 2 * HEAD), jnp.float32), *carry)
        )
        out[slot] = (acc[:, :HEAD] / acc[:, HEAD:]).astype(jnp.bfloat16)
        return group, ahead

    lax.fori_loop(0, slots, one_slot, (jnp.int32(0), ahead))


def attend(q, kv, lists, counts):
    scale = HEAD ** (-0.5) * LOG2E
    return pl.pallas_call(
        functools.partial(attend_kernel, scale),
        out_shape=jax.ShapeDtypeStruct(q.shape, jnp.bfloat16),
        in_specs=[SMEM, SMEM, VMEM, pl.BlockSpec(memory_space=pl.ANY)],
        out_specs=VMEM,
        scratch_shapes=[
            pltpu.VMEM((BUFFERS, GROUP, TILE, 2 * HEAD), jnp.bfloat16),
            pltpu.SemaphoreType.DMA((BUFFERS,)),
        ],
        compiler_params=pltpu.CompilerParams(vmem_limit_bytes=56 * 1024 * 1024),
        name="attend",
    )(lists, counts, q, kv)


def on_device(tokens, qkv_weight, q_gain, k_gain, key_tiles, key_counts):
    me_seq = lax.axis_index("seq")
    me_bal = lax.axis_index("bal")
    y, x = me_seq // 4, me_seq % 4
    core = me_bal % 2
    place = jnp.stack(
        (
            jnp.where(core == 0, x, y),
            jnp.where(core == 0, y, x),
            jnp.where(core == 0, 1, 4),
            jnp.where(core == 0, 4, 1),
        )
    ).astype(jnp.int32)
    slots = 16 * PIECE // TILE
    lists = lax.dynamic_slice_in_dim(key_tiles[0], me_bal * slots, slots, 0)
    counts = lax.dynamic_slice_in_dim(key_counts[0], me_bal * slots, slots, 0)

    before = send(tokens, 1, 1)
    after = send(tokens, 1, -1)
    across = send(tokens, 1, 2)
    low = jnp.concatenate((tokens, before), axis=0)
    before_low = send(low, 2, 1)
    high = jnp.concatenate((after, across), axis=0)
    after_high = send(high, 2, -1)
    after_low = send(low, 2, -1)
    before_high = send(high, 2, 1)
    across_low = send(before_low, 2, 1)
    across_high = send(after_high, 2, -1)

    weight = jnp.transpose(qkv_weight[:, 0], (1, 0, 2))
    low_pieces, high_pieces = (0, 3), (1, 2)
    begun = project(
        ((0, low_pieces), (0, high_pieces), (3, low_pieces), (1, high_pieces)),
        (low, high, before_low, after_high),
        weight,
        q_gain,
        k_gain,
        place,
    )
    queries, pairs = project(
        ((1, low_pieces), (3, high_pieces), (2, low_pieces), (2, high_pieces)),
        (after_low, before_high, across_low, across_high),
        weight,
        q_gain,
        k_gain,
        place,
        begun,
    )
    all_pairs = lax.all_gather(pairs, "bal", axis=0, tiled=True)
    result = attend(
        queries.reshape(slots, TILE, HEAD),
        all_pairs.reshape(-1, TILE, 2 * HEAD),
        lists,
        counts,
    )
    return lax.all_to_all(
        result.reshape(slots * TILE, HEAD), "seq", split_axis=0, concat_axis=1, tiled=True
    )


def solution(mesh):
    placed = (
        P(("bal", "seq"), None),
        P(None, "seq", None, None),
        P("seq", None),
        P("seq", None),
        P("seq", None, None),
        P("seq", None),
    )
    return jax.shard_map(
        on_device, mesh=mesh, in_specs=placed, out_specs=P(("bal", "seq"), None), check_vma=False
    )
```

time: 189 us -> 183 us (0.968)
  local copies, waits for them, and re-layouts: 8.46 us -> 3.17 us
  Pallas kernels: 23.7 us -> 19.2 us
  blocking collectives: 15.9 us -> 19.9 us
    pallas_call x1, Pallas kernels: 17 us -> 7.44 us  [attend(): pl.pallas_call(functools.partial(attend_kernel, scale), out_shape=jax.Sha...]
    unnamed x16, local copies, waits for them, and re-layouts: 6.33 us -> 1.04 us
    pallas_call x2, Pallas kernels: 6.73 us -> 11.7 us  [project(): pl.pallas_call(functools.partial(project_kernel, shares), out_shape=(jax....]
    all_to_all x1, blocking collectives: 15.9 us -> 19.9 us  [on_device(): lax.all_to_all(result.reshape(slots * TILE, HEAD), 'seq', split_axis=0, c...]
  transfers between devices with their start and end apart: 10 -> 10, of which waited for: 5 -> 6; matrix products, arithmetic and copies ran while one was open for 1% -> 2% of each run, Pallas kernels for 2% -> 3%
where the time goes in v4:
time: 183 us
  waiting for transfers between devices  97.6 us (53%)
  starting transfers between devices  28.6 us (16%)
  blocking collectives  19.9 us (11%)
  Pallas kernels  19.2 us (10%)
  between operations  13.6 us (7%)
  local copies, waits for them, and re-layouts  3.17 us (2%)
    all_gather x1, waiting for transfers between devices, on_device(): all_pairs = lax.all_gather(pairs, 'bal', axis=0, tiled=True)  89.6 us
    ppermute x9, starting transfers between devices, send(): return lax.ppermute(block, MESH_AXES, plane_perm(phase, shift))  28.6 us
    all_to_all x1, blocking collectives, on_device(): lax.all_to_all(result.reshape(slots * TILE, HEAD), 'seq', split_axis=0, c...  19.9 us
    pallas_call x2, Pallas kernels, project(): pl.pallas_call(functools.partial(project_kernel, shares), out_shape=(jax....  11.7 us
    ppermute x9, waiting for transfers between devices, send(): return lax.ppermute(block, MESH_AXES, plane_perm(phase, shift))  7.91 us
    pallas_call x1, Pallas kernels, attend(): pl.pallas_call(functools.partial(attend_kernel, scale), out_shape=jax.Sha...  7.44 us
  transfers between devices with their start and end apart: 10, of which 6 were waited for; matrix products, arithmetic and copies ran while one was open for 2% of the time, Pallas kernels for 3%

profile of v4, /device:TPU:1, one launch (start us, length us, event | category | flops | bytes accessed | tf_op | source)
XLA Modules:
  0.0 182.7 jit_solution(4685662300399242581)
XLA Ops:
  6.5 0.0 copy-start
  6.5 0.0 copy-start.6
  6.5 0.0 all-gather.2.cloned.1.call-start
  6.5 5.6 %collective-permute-start.2 = (bf16[48,3072]{1,0:T(8,128)(2,1)}, bf16[48,3072]{1,0:T(8,128)(2,1)S(1)}, u32[]{:S(2)}, u32[]{:S(2)}) collective-permute-start(bf16[48,3072]{1,0:T(8,128)(2,1)} %param.6), channel_id=1, source_target_pairs={{0,96},{32,0},{64,32},{96,64},{128,224},{160,128},{192,160},{224,1... | collective-permute-start | bytes 884744 | tf_op jit(solution)/shard_map/ppermute | solution.py:33
  12.1 2.3 %collective-permute-start.3 = (bf16[48,3072]{1,0:T(8,128)(2,1)}, bf16[48,3072]{1,0:T(8,128)(2,1)S(1)}, u32[]{:S(2)}, u32[]{:S(2)}) collective-permute-start(bf16[48,3072]{1,0:T(8,128)(2,1)} %param.6), channel_id=1, source_target_pairs={{0,64},{32,96},{64,0},{96,32},{128,192},{160,224},{192,128},{224,1... | collective-permute-start | bytes 884744 | tf_op jit(solution)/shard_map/ppermute | solution.py:33
  14.4 2.6 %collective-permute-start = (bf16[48,3072]{1,0:T(8,128)(2,1)}, bf16[48,3072]{1,0:T(8,128)(2,1)S(1)}, u32[]{:S(2)}, u32[]{:S(2)}) collective-permute-start(bf16[48,3072]{1,0:T(8,128)(2,1)} %param.6), channel_id=1, source_target_pairs={{0,32},{32,64},{64,96},{96,0},{128,160},{160,192},{192,224},{224,1... | collective-permute-start | bytes 884744 | tf_op jit(solution)/shard_map/ppermute | solution.py:33
  17.0 1.0 constant_dynamic-update-slice_fusion.1
  18.0 1.3 collective-permute-done.2
  19.3 2.1 %collective-permute-done.3 = bf16[48,3072]{1,0:T(8,128)(2,1)S(1)} collective-permute-done((bf16[48,3072]{1,0:T(8,128)(2,1)}, bf16[48,3072]{1,0:T(8,128)(2,1)S(1)}, u32[]{:S(2)}, u32[]{:S(2)}) %collective-permute-start.3) | collective-permute-done | bytes 294944 | tf_op jit(solution)/shard_map/ppermute | solution.py:33
  21.5 0.0 copy-start.2
  21.5 4.4 %collective-permute-start.7 = (bf16[96,3072]{1,0:T(8,128)(2,1)S(1)}, bf16[96,3072]{1,0:T(8,128)(2,1)}, u32[]{:S(2)}, u32[]{:S(2)}) collective-permute-start(bf16[96,3072]{1,0:T(8,128)(2,1)S(1)} %constant_dynamic-update-slice_fusion.2.refs_1_), channel_id=1, source_target_pairs={{0,384},{32,416},{64,448},{96,480},{128,0},{160,32},{192,64},{224,... | collective-permute-start | bytes 1769480 | tf_op jit(solution)/shard_map/ppermute | solution.py:33
  25.9 0.0 collective-permute-done
  25.9 0.0 copy-start.1
  25.9 1.9 %collective-permute-start.5 = (bf16[96,3072]{1,0:T(8,128)(2,1)S(1)}, bf16[96,3072]{1,0:T(8,128)(2,1)}, u32[]{:S(2)}, u32[]{:S(2)}) collective-permute-start(bf16[96,3072]{1,0:T(8,128)(2,1)S(1)} %constant_dynamic-update-slice_fusion.refs_0_), channel_id=1, source_target_pairs={{0,128},{32,160},{64,192},{96,224},{128,256},{160,288},{192,320},{... | collective-permute-start | bytes 1769480 | tf_op jit(solution)/shard_map/ppermute | solution.py:33
  27.8 2.9 %collective-permute-start.4 = (bf16[96,3072]{1,0:T(8,128)(2,1)S(1)}, bf16[96,3072]{1,0:T(8,128)(2,1)S(1)}, u32[]{:S(2)}, u32[]{:S(2)}) collective-permute-start(bf16[96,3072]{1,0:T(8,128)(2,1)S(1)} %constant_dynamic-update-slice_fusion.2.refs_1_), channel_id=1, source_target_pairs={{0,128},{32,160},{64,192},{96,224},{128,256},{160,288},{192,320},{... | collective-permute-start | bytes 1769480 | tf_op jit(solution)/shard_map/ppermute | solution.py:33
  30.8 3.6 %collective-permute-start.1 = (bf16[96,3072]{1,0:T(8,128)(2,1)S(1)}, bf16[96,3072]{1,0:T(8,128)(2,1)S(1)}, u32[]{:S(2)}, u32[]{:S(2)}) collective-permute-start(bf16[96,3072]{1,0:T(8,128)(2,1)S(1)} %constant_dynamic-update-slice_fusion.refs_0_), channel_id=1, source_target_pairs={{0,384},{32,416},{64,448},{96,480},{128,0},{160,32},{192,64},{224,... | collective-permute-start | bytes 1769480 | tf_op jit(solution)/shard_map/ppermute | solution.py:33
  34.3 0.0 collective-permute-done.7.refs_3_
  34.4 3.4 %collective-permute-start.8 = (bf16[96,3072]{1,0:T(8,128)(2,1)}, bf16[96,3072]{1,0:T(8,128)(2,1)S(1)}, u32[]{:S(2)}, u32[]{:S(2)}) collective-permute-start(bf16[96,3072]{1,0:T(8,128)(2,1)} %collective-permute-done.7.refs_3_), channel_id=1, source_target_pairs={{0,384},{32,416},{64,448},{96,480},{128,0},{160,32},{192,64},{224,... | collective-permute-start | bytes 1769480 | tf_op jit(solution)/shard_map/ppermute | solution.py:33
  37.8 0.4 collective-permute-done.5.refs_2_
  38.1 1.9 %collective-permute-start.6 = (bf16[96,3072]{1,0:T(8,128)(2,1)}, bf16[96,3072]{1,0:T(8,128)(2,1)}, u32[]{:S(2)}, u32[]{:S(2)}) collective-permute-start(bf16[96,3072]{1,0:T(8,128)(2,1)} %collective-permute-done.5.refs_2_), channel_id=1, source_target_pairs={{0,128},{32,160},{64,192},{96,224},{128,256},{160,288},{192,320},{... | collective-permute-start | bytes 1769480 | tf_op jit(solution)/shard_map/ppermute | solution.py:33
  40.1 0.6 pad_add_fusion.place
  40.7 0.0 copy-done.2
  40.7 0.0 copy-done.1
  40.7 5.9 %project.2 = (bf16[768,128]{1,0:T(8,128)(2,1)}, bf16[768,256]{1,0:T(8,128)(2,1)}) custom-call(s32[4]{0:T(128)} %pad_add_fusion.place, bf16[96,3072]{1,0:T(8,128)(2,1)} %copy-done.1, bf16[96,3072]{1,0:T(8,128)(2,1)} %copy-done.2, bf16[96,3072]{1,0:T(8,128)(2,1)} %collective-permute-done.5.refs_2_, bf16[96,3072]{1,0:T(8,128)(2,1)} %collective-permute-done.7.refs_3_, ...), custom_call_target="tpu_custom_call" | custom-call | tf_op jit(solution)/shard_map/project/pallas_call | solution.py:87
  46.6 0.0 collective-permute-done.4.refs_1_
  46.6 0.0 copy-start.3
  46.6 0.0 collective-permute-done.1.refs_0_
  46.6 0.0 copy-start.4
  46.6 1.4 collective-permute-done.8.refs_3_
  48.0 0.0 copy-start.5
  48.0 2.8 %collective-permute-done.6.refs_2_ = bf16[96,3072]{1,0:T(8,128)(2,1)} collective-permute-done((bf16[96,3072]{1,0:T(8,128)(2,1)}, bf16[96,3072]{1,0:T(8,128)(2,1)}, u32[]{:S(2)}, u32[]{:S(2)}) %collective-permute-start.6) | collective-permute-done | bytes 589856 | tf_op jit(solution)/shard_map/ppermute | solution.py:33
  50.8 0.0 copy-done.3
  50.8 0.0 copy-done.4
  50.8 0.0 copy-done.5
  50.8 5.9 %project.3 = (bf16[768,128]{1,0:T(8,128)(2,1)}, bf16[768,256]{1,0:T(8,128)(2,1)}) custom-call(s32[4]{0:T(128)} %pad_add_fusion.place, bf16[96,3072]{1,0:T(8,128)(2,1)} %copy-done.4, bf16[96,3072]{1,0:T(8,128)(2,1)} %copy-done.3, bf16[96,3072]{1,0:T(8,128)(2,1)} %collective-permute-done.6.refs_2_, ...), custom_call_target="tpu_custom_call", output_to_operand_aliasing={{0}: (8, {}), {1}: (9, {})} | custom-call | tf_op jit(solution)/shard_map/project/pallas_call | solution.py:87
  56.7 0.0 all-gather.2.cloned.1.call-update
  56.7 0.0 copy-done
  56.7 0.1 constant_dynamic-slice_fusion
  56.8 0.7 copy.9
  57.5 0.0 copy-done.6
  57.5 0.6 dynamic-slice_bitcast_fusion.counts
  58.1 89.6 %all-gather.2.cloned.1.call-done = bf16[24576,256]{1,0:T(8,128)(2,1)} async-done(((bf16[768,256]{1,0:T(8,128)(2,1)}), bf16[24576,256]{1,0:T(8,128)(2,1)}) %all-gather.2.cloned.1.call-update) | async-done | bytes 12582928 | tf_op jit(solution)/shard_map/all_gather | solution.py:230
  147.8 7.4 %attend.1 = bf16[6,128,128]{2,1,0:T(8,128)(2,1)} custom-call(s32[6,64]{1,0:T(8,128)} %bitcast.24, s32[6]{0:T(128)} %dynamic-slice_bitcast_fusion.counts, bf16[6,128,128]{2,1,0:T(8,128)(2,1)} %bitcast.22, bf16[192,128,256]{2,1,0:T(8,128)(2,1)} %bitcast.19), custom_call_target="tpu_custom_call" | custom-call | tf_op jit(solution)/shard_map/attend/pallas_call | solution.py:168
  155.2 19.9 %all_to_all.19 = bf16[16,48,128]{2,1,0:T(8,128)(2,1)S(1)} all-to-all(bf16[16,48,128]{2,1,0:T(8,128)(2,1)} %bitcast.23), channel_id=1, replica_groups=mesh['seq'=16,'bal'=32] {'seq'}, dimensions={0} | all-to-all | bytes 393216 | tf_op jit(solution)/shard_map/all_to_all | solution.py:237
  175.1 0.7 copy_bitcast_fusion
  (3 shorter events, 0.1 us)
Async XLA Ops:
  6.5 50.2 %copy-start = (s32[1,192,64]{1,2,0:T(8,128)S(1)}, s32[1,192,64]{1,2,0:T(8,128)}, u32[]{:S(2)}) copy-start(s32[1,192,64]{1,2,0:T(8,128)} %param.10) | copy-start | bytes 147460
  6.5 50.9 %copy-start.6 = (s32[1,192]{1,0:T(1,128)S(1)}, s32[1,192]{1,0:T(1,128)}, u32[]{:S(2)}) copy-start(s32[1,192]{1,0:T(1,128)} %param.11) | copy-start | bytes 2308
  6.5 141.2 %all-gather.2.cloned.1.call-start = ((), (), s32[]{:S(2)}) async-start(), calls=%async_computation.1 | async-start | bytes 12976128 | tf_op jit(solution)/shard_map/all_gather | solution.py:230
  6.5 12.8 %collective-permute-start.2 = (bf16[48,3072]{1,0:T(8,128)(2,1)}, bf16[48,3072]{1,0:T(8,128)(2,1)S(1)}, u32[]{:S(2)}, u32[]{:S(2)}) collective-permute-start(bf16[48,3072]{1,0:T(8,128)(2,1)} %param.6), channel_id=1, source_target_pairs={{0,96},{32,0},{64,32},{96,64},{128,224},{160,128},{192,160},{224,1... | collective-permute-start | bytes 884744 | tf_op jit(solution)/shard_map/ppermute | solution.py:33
  12.1 9.3 %collective-permute-start.3 = (bf16[48,3072]{1,0:T(8,128)(2,1)}, bf16[48,3072]{1,0:T(8,128)(2,1)S(1)}, u32[]{:S(2)}, u32[]{:S(2)}) collective-permute-start(bf16[48,3072]{1,0:T(8,128)(2,1)} %param.6), channel_id=1, source_target_pairs={{0,64},{32,96},{64,0},{96,32},{128,192},{160,224},{192,128},{224,1... | collective-permute-start | bytes 884744 | tf_op jit(solution)/shard_map/ppermute | solution.py:33
  14.4 11.5 %collective-permute-start = (bf16[48,3072]{1,0:T(8,128)(2,1)}, bf16[48,3072]{1,0:T(8,128)(2,1)S(1)}, u32[]{:S(2)}, u32[]{:S(2)}) collective-permute-start(bf16[48,3072]{1,0:T(8,128)(2,1)} %param.6), channel_id=1, source_target_pairs={{0,32},{32,64},{64,96},{96,0},{128,160},{160,192},{192,224},{224,1... | collective-permute-start | bytes 884744 | tf_op jit(solution)/shard_map/ppermute | solution.py:33
  21.5 19.3 %copy-start.2 = (bf16[96,3072]{1,0:T(8,128)(2,1)}, bf16[96,3072]{1,0:T(8,128)(2,1)S(1)}, u32[]{:S(2)}) copy-start(bf16[96,3072]{1,0:T(8,128)(2,1)S(1)} %constant_dynamic-update-slice_fusion.2.refs_1_) | copy-start | bytes 1769476
  21.5 12.9 %collective-permute-start.7 = (bf16[96,3072]{1,0:T(8,128)(2,1)S(1)}, bf16[96,3072]{1,0:T(8,128)(2,1)}, u32[]{:S(2)}, u32[]{:S(2)}) collective-permute-start(bf16[96,3072]{1,0:T(8,128)(2,1)S(1)} %constant_dynamic-update-slice_fusion.2.refs_1_), channel_id=1, source_target_pairs={{0,384},{32,416},{64,448},{96,480},{128,0},{160,32},{192,64},{224,... | collective-permute-start | bytes 1769480 | tf_op jit(solution)/shard_map/ppermute | solution.py:33
  25.9 14.8 %copy-start.1 = (bf16[96,3072]{1,0:T(8,128)(2,1)}, bf16[96,3072]{1,0:T(8,128)(2,1)S(1)}, u32[]{:S(2)}) copy-start(bf16[96,3072]{1,0:T(8,128)(2,1)S(1)} %constant_dynamic-update-slice_fusion.refs_0_) | copy-start | bytes 1769476
  25.9 12.2 %collective-permute-start.5 = (bf16[96,3072]{1,0:T(8,128)(2,1)S(1)}, bf16[96,3072]{1,0:T(8,128)(2,1)}, u32[]{:S(2)}, u32[]{:S(2)}) collective-permute-start(bf16[96,3072]{1,0:T(8,128)(2,1)S(1)} %constant_dynamic-update-slice_fusion.refs_0_), channel_id=1, source_target_pairs={{0,128},{32,160},{64,192},{96,224},{128,256},{160,288},{192,320},{... | collective-permute-start | bytes 1769480 | tf_op jit(solution)/shard_map/ppermute | solution.py:33
  27.8 18.8 %collective-permute-start.4 = (bf16[96,3072]{1,0:T(8,128)(2,1)S(1)}, bf16[96,3072]{1,0:T(8,128)(2,1)S(1)}, u32[]{:S(2)}, u32[]{:S(2)}) collective-permute-start(bf16[96,3072]{1,0:T(8,128)(2,1)S(1)} %constant_dynamic-update-slice_fusion.2.refs_1_), channel_id=1, source_target_pairs={{0,128},{32,160},{64,192},{96,224},{128,256},{160,288},{192,320},{... | collective-permute-start | bytes 1769480 | tf_op jit(solution)/shard_map/ppermute | solution.py:33
  30.8 15.8 %collective-permute-start.1 = (bf16[96,3072]{1,0:T(8,128)(2,1)S(1)}, bf16[96,3072]{1,0:T(8,128)(2,1)S(1)}, u32[]{:S(2)}, u32[]{:S(2)}) collective-permute-start(bf16[96,3072]{1,0:T(8,128)(2,1)S(1)} %constant_dynamic-update-slice_fusion.refs_0_), channel_id=1, source_target_pairs={{0,384},{32,416},{64,448},{96,480},{128,0},{160,32},{192,64},{224,... | collective-permute-start | bytes 1769480 | tf_op jit(solution)/shard_map/ppermute | solution.py:33
  34.4 13.7 %collective-permute-start.8 = (bf16[96,3072]{1,0:T(8,128)(2,1)}, bf16[96,3072]{1,0:T(8,128)(2,1)S(1)}, u32[]{:S(2)}, u32[]{:S(2)}) collective-permute-start(bf16[96,3072]{1,0:T(8,128)(2,1)} %collective-permute-done.7.refs_3_), channel_id=1, source_target_pairs={{0,384},{32,416},{64,448},{96,480},{128,0},{160,32},{192,64},{224,... | collective-permute-start | bytes 1769480 | tf_op jit(solution)/shard_map/ppermute | solution.py:33
  38.1 12.6 %collective-permute-start.6 = (bf16[96,3072]{1,0:T(8,128)(2,1)}, bf16[96,3072]{1,0:T(8,128)(2,1)}, u32[]{:S(2)}, u32[]{:S(2)}) collective-permute-start(bf16[96,3072]{1,0:T(8,128)(2,1)} %collective-permute-done.5.refs_2_), channel_id=1, source_target_pairs={{0,128},{32,160},{64,192},{96,224},{128,256},{160,288},{192,320},{... | collective-permute-start | bytes 1769480 | tf_op jit(solution)/shard_map/ppermute | solution.py:33
  46.6 4.2 %copy-start.3 = (bf16[96,3072]{1,0:T(8,128)(2,1)}, bf16[96,3072]{1,0:T(8,128)(2,1)S(1)}, u32[]{:S(2)}) copy-start(bf16[96,3072]{1,0:T(8,128)(2,1)S(1)} %collective-permute-done.4.refs_1_) | copy-start | bytes 1769476
  46.6 4.2 %copy-start.4 = (bf16[96,3072]{1,0:T(8,128)(2,1)}, bf16[96,3072]{1,0:T(8,128)(2,1)S(1)}, u32[]{:S(2)}) copy-start(bf16[96,3072]{1,0:T(8,128)(2,1)S(1)} %collective-permute-done.1.refs_0_) | copy-start | bytes 1769476
  48.0 2.8 %copy-start.5 = (bf16[96,3072]{1,0:T(8,128)(2,1)}, bf16[96,3072]{1,0:T(8,128)(2,1)S(1)}, u32[]{:S(2)}) copy-start(bf16[96,3072]{1,0:T(8,128)(2,1)S(1)} %collective-permute-done.8.refs_3_) | copy-start | bytes 1769476
Sparse Core Ops, SparseCore 0:
  56.8 90.8 all-gather.1

commit v5 on v4

--- a/solution.py
+++ b/solution.py
@@ -61,19 +61,20 @@
         return (values * lax.rsqrt(mean_square + 1e-06) * gain).astype(jnp.bfloat16)
 
     whole = jnp.concatenate([weight_in[at] for at in range(3)], axis=1)
+    for copy in copies[3:]:
+        copy.wait()
+    rows = block_in[...].reshape(count * half, block_in.shape[2])
+    proj = jnp.dot(rows, whole, preferred_element_type=jnp.float32)
+    q_held[...] = normalize(proj[:, :HEAD], gain_in[0])
+    kv_held[:, :HEAD] = normalize(proj[:, HEAD : 2 * HEAD], gain_in[1])
+    kv_held[:, HEAD:] = proj[:, 2 * HEAD :].astype(jnp.bfloat16)
     for at, (shift, pieces) in enumerate(shares):
-        copies[3 + at].wait()
-        proj = jnp.dot(block_in[at], whole, preferred_element_type=jnp.float32)
-        here = slice(at * half, (at + 1) * half)
-        q_held[here, :] = normalize(proj[:, :HEAD], gain_in[0])
-        kv_held[here, :HEAD] = normalize(proj[:, HEAD : 2 * HEAD], gain_in[1])
-        kv_held[here, HEAD:] = proj[:, 2 * HEAD :].astype(jnp.bfloat16)
         for order, piece in enumerate(pieces):
             spot = ((first + piece) % 4) * first_step + ((second + shift) % 4) * second_step
-            rows = pl.ds(pl.multiple_of(spot * PIECE, PIECE), PIECE)
+            target = pl.ds(pl.multiple_of(spot * PIECE, PIECE), PIECE)
             source = pl.ds(at * half + order * PIECE, PIECE)
-            pltpu.make_async_copy(q_held.at[source, :], q_out.at[rows, :], leave.at[0]).start()
-            pltpu.make_async_copy(kv_held.at[source, :], kv_out.at[rows, :], leave.at[1]).start()
+            pltpu.make_async_copy(q_held.at[source, :], q_out.at[target, :], leave.at[0]).start()
+            pltpu.make_async_copy(kv_held.at[source, :], kv_out.at[target, :], leave.at[1]).start()
     pltpu.make_async_copy(q_held, q_held, leave.at[0]).wait()
     pltpu.make_async_copy(kv_held, kv_held, leave.at[1]).wait()
 
@@ -107,38 +108,30 @@
     )(place, *blocks, weight, q_gain, k_gain, *begun)
 
 
-def attend_kernel(scale, lists, counts, q, kv, out, held, ready):
+def attend_kernel(scale, picks, counts, q, kv, out, held, ready):
     ones = jnp.ones((GROUP * TILE, HEAD), jnp.bfloat16)
-    slots = q.shape[0]
-
-    def turns_of(slot):
-        return (counts[slot] + GROUP - 1) // GROUP
-
-    def fetch(ahead, buffer):
-        slot, step = ahead
-
-        @pl.when(slot < slots)
-        def _():
-            for at in range(GROUP):
-                pick = lists[slot, step * GROUP + at]
-                pltpu.make_async_copy(kv.at[pick], held.at[buffer, at], ready.at[buffer]).start()
-
-        last = step + 1 >= turns_of(jnp.minimum(slot, slots - 1))
-        return jnp.where(last, slot + 1, slot), jnp.where(last, 0, step + 1)
-
-    ahead = (jnp.int32(0), jnp.int32(0))
+
+    def fetch(group, buffer):
+        for at in range(GROUP):
+            pick = picks[group * GROUP + at]
+            pltpu.make_async_copy(kv.at[pick], held.at[buffer, at], ready.at[buffer]).start()
+
+    def arrive(buffer):
+        pltpu.make_async_copy(held.at[buffer], held.at[buffer], ready.at[buffer]).wait()
+
     for buffer in range(BUFFERS - 1):
-        ahead = fetch(ahead, buffer)
-
-    def one_slot(slot, carry):
+        fetch(buffer, buffer)
+
+    def one_slot(slot, group):
         query = q[slot]
         count = counts[slot]
-
-        def turn(step, carry):
-            acc, group, ahead = carry
-            buffer = group % BUFFERS
-            ahead = fetch(ahead, (group + BUFFERS - 1) % BUFFERS)
-            pltpu.make_async_copy(held.at[buffer], held.at[buffer], ready.at[buffer]).wait()
+        turns = (count + GROUP - 1) // GROUP
+
+        def turn(step, acc):
+            at = group + step
+            buffer = at % BUFFERS
+            fetch(at + BUFFERS - 1, (at + BUFFERS - 1) % BUFFERS)
+            arrive(buffer)
             keys = held[buffer, :, :, :HEAD].reshape(GROUP * TILE, HEAD)
             values = held[buffer, :, :, HEAD:].reshape(GROUP * TILE, HEAD)
             scores = lax.dot_general(
@@ -147,20 +140,33 @@
             live = (count - step * GROUP) * TILE
             column = lax.broadcasted_iota(jnp.int32, scores.shape, 1)
             weights = jnp.where(column < live, jnp.exp2(scores * scale), 0.0)
-            acc = acc + jnp.dot(
+            return acc + jnp.dot(
                 weights.astype(jnp.bfloat16),
                 jnp.concatenate((values, ones), axis=1),
                 preferred_element_type=jnp.float32,
             )
-            return acc, group + 1, ahead
-
-        acc, group, ahead = lax.fori_loop(
-            0, turns_of(slot), turn, (jnp.zeros((TILE, 2 * HEAD), jnp.float32), *carry)
-        )
+
+        acc = lax.fori_loop(0, turns, turn, jnp.zeros((TILE, 2 * HEAD), jnp.float32))
         out[slot] = (acc[:, :HEAD] / acc[:, HEAD:]).astype(jnp.bfloat16)
-        return group, ahead
-
-    lax.fori_loop(0, slots, one_slot, (jnp.int32(0), ahead))
+        return group + turns
+
+    groups = lax.fori_loop(0, q.shape[0], one_slot, jnp.int32(0))
+    for extra in range(BUFFERS - 1):
+        arrive((groups + extra) % BUFFERS)
+
+
+def flat_picks(lists, counts):
+    slots, listed = lists.shape
+    turns = (counts + GROUP - 1) // GROUP
+    ends = jnp.cumsum(turns)
+    room = slots * (listed // GROUP) + BUFFERS
+    group = jnp.arange(room, dtype=jnp.int32)
+    slot = jnp.sum((group[:, None] >= ends[None, :]).astype(jnp.int32), axis=1)
+    slot = jnp.minimum(slot, slots - 1)
+    step = jnp.clip(group - (ends - turns)[slot], 0, listed // GROUP - 1)
+    return lists.reshape(slots * (listed // GROUP), GROUP)[
+        slot * (listed // GROUP) + step
+    ].reshape(-1)
 
 
 def attend(q, kv, lists, counts):
@@ -176,7 +182,7 @@
         ],
         compiler_params=pltpu.CompilerParams(vmem_limit_bytes=56 * 1024 * 1024),
         name="attend",
-    )(lists, counts, q, kv)
+    )(flat_picks(lists, counts), counts, q, kv)
 
 
 def on_device(tokens, qkv_weight, q_gain, k_gain, key_tiles, key_counts):
@@ -218,9 +224,18 @@
         k_gain,
         place,
     )
+    begun = project(
+        ((1, low_pieces), (3, high_pieces)),
+        (after_low, before_high),
+        weight,
+        q_gain,
+        k_gain,
+        place,
+        begun,
+    )
     queries, pairs = project(
-        ((1, low_pieces), (3, high_pieces), (2, low_pieces), (2, high_pieces)),
-        (after_low, before_high, across_low, across_high),
+        ((2, low_pieces), (2, high_pieces)),
+        (across_low, across_high),
         weight,
         q_gain,
         k_gain,

time: 183 us -> 184 us (level)
  waiting for transfers between devices: 97.6 us -> 89.5 us
  other arithmetic: 0.61 us -> 5.31 us
  Pallas kernels: 19.2 us -> 22.3 us
  blocking collectives: 19.9 us -> 17.1 us
  local copies, waits for them, and re-layouts: 3.17 us -> 5.67 us
    ppermute x9, waiting for transfers between devices: 7.91 us -> 3.77 us  [send(): return lax.ppermute(block, MESH_AXES, plane_perm(phase, shift))]
    all_gather x1, waiting for transfers between devices: 89.6 us -> 85.7 us  [on_device(): all_pairs = lax.all_gather(pairs, 'bal', axis=0, tiled=True)]
    select_n x0 -> x2, other arithmetic: none -> 3.82 us  [the longest x1 3.74 us: flat_picks(): lists.reshape(slots * (listed // GROUP), GROUP)]
    all_to_all x1, blocking collectives: 19.9 us -> 17.1 us  [on_device(): lax.all_to_all(result.reshape(slots * TILE, HEAD), 'seq', split_axis=0, c...]
    pallas_call x2 -> x3, Pallas kernels: 11.7 us -> 13.7 us  [project(): pl.pallas_call(functools.partial(project_kernel, shares), out_shape=(jax....]
  transfers between devices with their start and end apart: 10 -> 10, of which waited for: 6 -> 4; matrix products, arithmetic and copies ran while one was open for 2% -> 5% of each run, Pallas kernels for 3% -> 5%
where the time goes in v5:
time: 184 us; the launch traced here: 182 us
  waiting for transfers between devices  89.5 us (49%)
  starting transfers between devices  28.6 us (16%)
  Pallas kernels  22.3 us (12%)
  blocking collectives  17.1 us (9%)
  between operations  13.7 us (7%)
  local copies, waits for them, and re-layouts  5.67 us (3%)
  other arithmetic  5.31 us (3%)
    all_gather x1, waiting for transfers between devices, on_device(): all_pairs = lax.all_gather(pairs, 'bal', axis=0, tiled=True)  85.7 us
    ppermute x9, starting transfers between devices, send(): return lax.ppermute(block, MESH_AXES, plane_perm(phase, shift))  28.6 us
    all_to_all x1, blocking collectives, on_device(): lax.all_to_all(result.reshape(slots * TILE, HEAD), 'seq', split_axis=0, c...  17.1 us
    pallas_call x3, Pallas kernels, project(): pl.pallas_call(functools.partial(project_kernel, shares), out_shape=(jax....  13.7 us
    pallas_call x1, Pallas kernels, attend(): pl.pallas_call(functools.partial(attend_kernel, scale), out_shape=jax.Sha...  8.65 us
    ppermute x9, waiting for transfers between devices, send(): return lax.ppermute(block, MESH_AXES, plane_perm(phase, shift))  3.77 us
    select_n x1, other arithmetic, flat_picks(): lists.reshape(slots * (listed // GROUP), GROUP)  3.74 us
  transfers between devices with their start and end apart: 10, of which 4 were waited for; matrix products, arithmetic and copies ran while one was open for 5% of the time, Pallas kernels for 5%

profile of v5, /device:TPU:1, one launch (start us, length us, event | category | flops | bytes accessed | tf_op | source)
XLA Modules:
  0.0 182.1 jit_solution(10372243749455727880)
XLA Ops:
  6.5 0.0 copy-start
  6.5 0.0 copy-start.6
  6.5 0.0 all-gather.2.cloned.1.call-start
  6.5 5.6 %collective-permute-start.3 = (bf16[48,3072]{1,0:T(8,128)(2,1)}, bf16[48,3072]{1,0:T(8,128)(2,1)S(1)}, u32[]{:S(2)}, u32[]{:S(2)}) collective-permute-start(bf16[48,3072]{1,0:T(8,128)(2,1)} %param.6), channel_id=1, source_target_pairs={{0,96},{32,0},{64,32},{96,64},{128,224},{160,128},{192,160},{224,1... | collective-permute-start | bytes 884744 | tf_op jit(solution)/shard_map/ppermute | solution.py:33
  12.1 2.3 %collective-permute-start.4 = (bf16[48,3072]{1,0:T(8,128)(2,1)}, bf16[48,3072]{1,0:T(8,128)(2,1)S(1)}, u32[]{:S(2)}, u32[]{:S(2)}) collective-permute-start(bf16[48,3072]{1,0:T(8,128)(2,1)} %param.6), channel_id=1, source_target_pairs={{0,64},{32,96},{64,0},{96,32},{128,192},{160,224},{192,128},{224,1... | collective-permute-start | bytes 884744 | tf_op jit(solution)/shard_map/ppermute | solution.py:33
  14.4 2.6 %collective-permute-start = (bf16[48,3072]{1,0:T(8,128)(2,1)}, bf16[48,3072]{1,0:T(8,128)(2,1)S(1)}, u32[]{:S(2)}, u32[]{:S(2)}) collective-permute-start(bf16[48,3072]{1,0:T(8,128)(2,1)} %param.6), channel_id=1, source_target_pairs={{0,32},{32,64},{64,96},{96,0},{128,160},{160,192},{192,224},{224,1... | collective-permute-start | bytes 884744 | tf_op jit(solution)/shard_map/ppermute | solution.py:33
  17.0 1.0 constant_dynamic-update-slice_fusion.1
  18.0 1.3 collective-permute-done.3
  19.3 2.1 %collective-permute-done.4 = bf16[48,3072]{1,0:T(8,128)(2,1)S(1)} collective-permute-done((bf16[48,3072]{1,0:T(8,128)(2,1)}, bf16[48,3072]{1,0:T(8,128)(2,1)S(1)}, u32[]{:S(2)}, u32[]{:S(2)}) %collective-permute-start.4) | collective-permute-done | bytes 294944 | tf_op jit(solution)/shard_map/ppermute | solution.py:33
  21.5 0.0 copy-start.2
  21.5 4.4 %collective-permute-start.5 = (bf16[96,3072]{1,0:T(8,128)(2,1)S(1)}, bf16[96,3072]{1,0:T(8,128)(2,1)}, u32[]{:S(2)}, u32[]{:S(2)}) collective-permute-start(bf16[96,3072]{1,0:T(8,128)(2,1)S(1)} %constant_dynamic-update-slice_fusion.2.refs_1_), channel_id=1, source_target_pairs={{0,384},{32,416},{64,448},{96,480},{128,0},{160,32},{192,64},{224,... | collective-permute-start | bytes 1769480 | tf_op jit(solution)/shard_map/ppermute | solution.py:33
  25.9 0.0 collective-permute-done
  25.9 0.0 copy-start.1
  25.9 1.9 %collective-permute-start.1 = (bf16[96,3072]{1,0:T(8,128)(2,1)S(1)}, bf16[96,3072]{1,0:T(8,128)(2,1)}, u32[]{:S(2)}, u32[]{:S(2)}) collective-permute-start(bf16[96,3072]{1,0:T(8,128)(2,1)S(1)} %constant_dynamic-update-slice_fusion.refs_0_), channel_id=1, source_target_pairs={{0,128},{32,160},{64,192},{96,224},{128,256},{160,288},{192,320},{... | collective-permute-start | bytes 1769480 | tf_op jit(solution)/shard_map/ppermute | solution.py:33
  27.8 2.9 %collective-permute-start.8 = (bf16[96,3072]{1,0:T(8,128)(2,1)S(1)}, bf16[96,3072]{1,0:T(8,128)(2,1)S(1)}, u32[]{:S(2)}, u32[]{:S(2)}) collective-permute-start(bf16[96,3072]{1,0:T(8,128)(2,1)S(1)} %constant_dynamic-update-slice_fusion.2.refs_1_), channel_id=1, source_target_pairs={{0,128},{32,160},{64,192},{96,224},{128,256},{160,288},{192,320},{... | collective-permute-start | bytes 1769480 | tf_op jit(solution)/shard_map/ppermute | solution.py:33
  30.8 3.6 %collective-permute-start.7 = (bf16[96,3072]{1,0:T(8,128)(2,1)S(1)}, bf16[96,3072]{1,0:T(8,128)(2,1)}, u32[]{:S(2)}, u32[]{:S(2)}) collective-permute-start(bf16[96,3072]{1,0:T(8,128)(2,1)S(1)} %constant_dynamic-update-slice_fusion.refs_0_), channel_id=1, source_target_pairs={{0,384},{32,416},{64,448},{96,480},{128,0},{160,32},{192,64},{224,... | collective-permute-start | bytes 1769480 | tf_op jit(solution)/shard_map/ppermute | solution.py:33
  34.3 0.0 collective-permute-done.5.refs_3_
  34.4 3.4 %collective-permute-start.6 = (bf16[96,3072]{1,0:T(8,128)(2,1)}, bf16[96,3072]{1,0:T(8,128)(2,1)S(1)}, u32[]{:S(2)}, u32[]{:S(2)}) collective-permute-start(bf16[96,3072]{1,0:T(8,128)(2,1)} %collective-permute-done.5.refs_3_), channel_id=1, source_target_pairs={{0,384},{32,416},{64,448},{96,480},{128,0},{160,32},{192,64},{224,... | collective-permute-start | bytes 1769480 | tf_op jit(solution)/shard_map/ppermute | solution.py:33
  37.8 0.4 collective-permute-done.1.refs_2_
  38.1 1.9 %collective-permute-start.2 = (bf16[96,3072]{1,0:T(8,128)(2,1)}, bf16[96,3072]{1,0:T(8,128)(2,1)S(1)}, u32[]{:S(2)}, u32[]{:S(2)}) collective-permute-start(bf16[96,3072]{1,0:T(8,128)(2,1)} %collective-permute-done.1.refs_2_), channel_id=1, source_target_pairs={{0,128},{32,160},{64,192},{96,224},{128,256},{160,288},{192,320},{... | collective-permute-start | bytes 1769480 | tf_op jit(solution)/shard_map/ppermute | solution.py:33
  40.1 0.6 pad_add_fusion.place
  40.7 0.0 copy-done.2
  40.7 0.0 copy-done.1
  40.7 5.2 %project.3 = (bf16[768,128]{1,0:T(8,128)(2,1)}, bf16[768,256]{1,0:T(8,128)(2,1)}) custom-call(s32[4]{0:T(128)} %pad_add_fusion.place, bf16[96,3072]{1,0:T(8,128)(2,1)} %copy-done.1, bf16[96,3072]{1,0:T(8,128)(2,1)} %copy-done.2, bf16[96,3072]{1,0:T(8,128)(2,1)} %collective-permute-done.1.refs_2_, bf16[96,3072]{1,0:T(8,128)(2,1)} %collective-permute-done.5.refs_3_, ...), custom_call_target="tpu_custom_call" | custom-call | tf_op jit(solution)/shard_map/project/pallas_call | solution.py:88
  45.9 0.0 collective-permute-done.8.refs_1_
  45.9 0.0 copy-start.4
  46.0 0.0 collective-permute-done.7.refs_0_
  46.0 0.8 copy-done.4
  46.8 4.2 %project.4 = (bf16[768,128]{1,0:T(8,128)(2,1)}, bf16[768,256]{1,0:T(8,128)(2,1)}) custom-call(s32[4]{0:T(128)} %pad_add_fusion.place, bf16[96,3072]{1,0:T(8,128)(2,1)} %collective-permute-done.7.refs_0_, bf16[96,3072]{1,0:T(8,128)(2,1)} %copy-done.4, bf16[3,3072,128]{2,1,0:T(8,128)(2,1)} %bitcast.47, ...), custom_call_target="tpu_custom_call", output_to_operand_aliasing={{0}: (6, {}), {1}: (7, {})} | custom-call | tf_op jit(solution)/shard_map/project/pallas_call | solution.py:88
  51.0 0.0 collective-permute-done.6.refs_1_
  51.0 0.0 copy-start.3
  51.0 0.0 collective-permute-done.2.refs_0_
  51.0 0.0 copy-start.5
  51.0 0.8 copy-done.3
  51.8 0.2 copy-done.5
  52.0 4.2 %project.5 = (bf16[768,128]{1,0:T(8,128)(2,1)}, bf16[768,256]{1,0:T(8,128)(2,1)}) custom-call(s32[4]{0:T(128)} %pad_add_fusion.place, bf16[96,3072]{1,0:T(8,128)(2,1)} %copy-done.5, bf16[96,3072]{1,0:T(8,128)(2,1)} %copy-done.3, bf16[3,3072,128]{2,1,0:T(8,128)(2,1)} %bitcast.48, f32[1,128]{1,0:T(1,128)} %refs_3_.3, ...), custom_call_target="tpu_custom_call", output_to_operand_aliasing={{0}: (6, {}), {1}: (7, {})} | custom-call | tf_op jit(solution)/shard_map/project/pallas_call | solution.py:88
  56.3 0.0 all-gather.2.cloned.1.call-update
  56.3 0.0 copy-done.6
  56.3 0.1 and_select_fusion.1
  56.4 0.2 reduce-window.8
  56.6 0.0 copy-done
  56.6 0.1 constant_dynamic-slice_fusion.1
  56.6 0.1 copy.15
  56.7 0.1 reshape.146
  56.8 0.6 fusion.3
  57.4 0.7 fusion.6
  58.1 0.1 convert_reduce_fusion
  58.2 3.7 %fusion.1 = s32[56]{0:T(128)S(1)} fusion(s32[56]{0:T(128)S(1)} %convert_reduce_fusion, s32[]{:T(128)} %bitcast.4, s32[]{:T(128)} %bitcast.5, s32[]{:T(128)} %bitcast.6, s32[]{:T(128)} %bitcast.7, s32[]{:T(128)} %bitcast.9, s32[]{:T(128)} %bitcast.8), kind=kLoop, calls=%fused_computation.25 | loop fusion | flops 1176 | bytes 472 | tf_op jit(solution)/shard_map/select_n | solution.py:167
  61.9 0.6 gather_fusion
  62.5 0.6 reshape.148.picks
  63.1 85.7 %all-gather.2.cloned.1.call-done = bf16[24576,256]{1,0:T(8,128)(2,1)} async-done(((bf16[768,256]{1,0:T(8,128)(2,1)}), bf16[24576,256]{1,0:T(8,128)(2,1)}) %all-gather.2.cloned.1.call-update) | async-done | bytes 12582928 | tf_op jit(solution)/shard_map/all_gather | solution.py:245
  148.9 8.7 %attend.1 = bf16[6,128,128]{2,1,0:T(8,128)(2,1)} custom-call(s32[448]{0:T(512)} %reshape.148.picks, s32[6]{0:T(128)} %get-tuple-element.18.counts, bf16[6,128,128]{2,1,0:T(8,128)(2,1)} %bitcast.50, bf16[192,128,256]{2,1,0:T(8,128)(2,1)} %bitcast.49), custom_call_target="tpu_custom_call" | custom-call | tf_op jit(solution)/shard_map/attend/pallas_call | solution.py:174
  157.5 17.1 %all_to_all.19 = bf16[16,48,128]{2,1,0:T(8,128)(2,1)S(1)} all-to-all(bf16[16,48,128]{2,1,0:T(8,128)(2,1)} %bitcast.51), channel_id=1, replica_groups=mesh['seq'=16,'bal'=32] {'seq'}, dimensions={0} | all-to-all | bytes 393216 | tf_op jit(solution)/shard_map/all_to_all | solution.py:252
  174.6 0.7 copy_bitcast_fusion
  (4 shorter events, 0.1 us)
Async XLA Ops:
  6.5 50.0 %copy-start = (s32[1,192,64]{1,2,0:T(8,128)S(1)}, s32[1,192,64]{1,2,0:T(8,128)}, u32[]{:S(2)}) copy-start(s32[1,192,64]{1,2,0:T(8,128)} %param.10) | copy-start | bytes 147460
  6.5 49.7 %copy-start.6 = (s32[1,192]{1,0:T(1,128)S(1)}, s32[1,192]{1,0:T(1,128)}, u32[]{:S(2)}) copy-start(s32[1,192]{1,0:T(1,128)} %param.11) | copy-start | bytes 2308
  6.5 142.3 %all-gather.2.cloned.1.call-start = ((), (), s32[]{:S(2)}) async-start(), calls=%async_computation.1 | async-start | bytes 12976128 | tf_op jit(solution)/shard_map/all_gather | solution.py:245
  6.5 12.8 %collective-permute-start.3 = (bf16[48,3072]{1,0:T(8,128)(2,1)}, bf16[48,3072]{1,0:T(8,128)(2,1)S(1)}, u32[]{:S(2)}, u32[]{:S(2)}) collective-permute-start(bf16[48,3072]{1,0:T(8,128)(2,1)} %param.6), channel_id=1, source_target_pairs={{0,96},{32,0},{64,32},{96,64},{128,224},{160,128},{192,160},{224,1... | collective-permute-start | bytes 884744 | tf_op jit(solution)/shard_map/ppermute | solution.py:33
  12.1 9.3 %collective-permute-start.4 = (bf16[48,3072]{1,0:T(8,128)(2,1)}, bf16[48,3072]{1,0:T(8,128)(2,1)S(1)}, u32[]{:S(2)}, u32[]{:S(2)}) collective-permute-start(bf16[48,3072]{1,0:T(8,128)(2,1)} %param.6), channel_id=1, source_target_pairs={{0,64},{32,96},{64,0},{96,32},{128,192},{160,224},{192,128},{224,1... | collective-permute-start | bytes 884744 | tf_op jit(solution)/shard_map/ppermute | solution.py:33
  14.4 11.5 %collective-permute-start = (bf16[48,3072]{1,0:T(8,128)(2,1)}, bf16[48,3072]{1,0:T(8,128)(2,1)S(1)}, u32[]{:S(2)}, u32[]{:S(2)}) collective-permute-start(bf16[48,3072]{1,0:T(8,128)(2,1)} %param.6), channel_id=1, source_target_pairs={{0,32},{32,64},{64,96},{96,0},{128,160},{160,192},{192,224},{224,1... | collective-permute-start | bytes 884744 | tf_op jit(solution)/shard_map/ppermute | solution.py:33
  21.5 19.2 %copy-start.2 = (bf16[96,3072]{1,0:T(8,128)(2,1)}, bf16[96,3072]{1,0:T(8,128)(2,1)S(1)}, u32[]{:S(2)}) copy-start(bf16[96,3072]{1,0:T(8,128)(2,1)S(1)} %constant_dynamic-update-slice_fusion.2.refs_1_) | copy-start | bytes 1769476
  21.5 12.9 %collective-permute-start.5 = (bf16[96,3072]{1,0:T(8,128)(2,1)S(1)}, bf16[96,3072]{1,0:T(8,128)(2,1)}, u32[]{:S(2)}, u32[]{:S(2)}) collective-permute-start(bf16[96,3072]{1,0:T(8,128)(2,1)S(1)} %constant_dynamic-update-slice_fusion.2.refs_1_), channel_id=1, source_target_pairs={{0,384},{32,416},{64,448},{96,480},{128,0},{160,32},{192,64},{224,... | collective-permute-start | bytes 1769480 | tf_op jit(solution)/shard_map/ppermute | solution.py:33
  25.9 14.8 %copy-start.1 = (bf16[96,3072]{1,0:T(8,128)(2,1)}, bf16[96,3072]{1,0:T(8,128)(2,1)S(1)}, u32[]{:S(2)}) copy-start(bf16[96,3072]{1,0:T(8,128)(2,1)S(1)} %constant_dynamic-update-slice_fusion.refs_0_) | copy-start | bytes 1769476
  25.9 12.2 %collective-permute-start.1 = (bf16[96,3072]{1,0:T(8,128)(2,1)S(1)}, bf16[96,3072]{1,0:T(8,128)(2,1)}, u32[]{:S(2)}, u32[]{:S(2)}) collective-permute-start(bf16[96,3072]{1,0:T(8,128)(2,1)S(1)} %constant_dynamic-update-slice_fusion.refs_0_), channel_id=1, source_target_pairs={{0,128},{32,160},{64,192},{96,224},{128,256},{160,288},{192,320},{... | collective-permute-start | bytes 1769480 | tf_op jit(solution)/shard_map/ppermute | solution.py:33
  27.8 18.1 %collective-permute-start.8 = (bf16[96,3072]{1,0:T(8,128)(2,1)S(1)}, bf16[96,3072]{1,0:T(8,128)(2,1)S(1)}, u32[]{:S(2)}, u32[]{:S(2)}) collective-permute-start(bf16[96,3072]{1,0:T(8,128)(2,1)S(1)} %constant_dynamic-update-slice_fusion.2.refs_1_), channel_id=1, source_target_pairs={{0,128},{32,160},{64,192},{96,224},{128,256},{160,288},{192,320},{... | collective-permute-start | bytes 1769480 | tf_op jit(solution)/shard_map/ppermute | solution.py:33
  30.8 15.2 %collective-permute-start.7 = (bf16[96,3072]{1,0:T(8,128)(2,1)S(1)}, bf16[96,3072]{1,0:T(8,128)(2,1)}, u32[]{:S(2)}, u32[]{:S(2)}) collective-permute-start(bf16[96,3072]{1,0:T(8,128)(2,1)S(1)} %constant_dynamic-update-slice_fusion.refs_0_), channel_id=1, source_target_pairs={{0,384},{32,416},{64,448},{96,480},{128,0},{160,32},{192,64},{224,... | collective-permute-start | bytes 1769480 | tf_op jit(solution)/shard_map/ppermute | solution.py:33
  34.4 16.6 %collective-permute-start.6 = (bf16[96,3072]{1,0:T(8,128)(2,1)}, bf16[96,3072]{1,0:T(8,128)(2,1)S(1)}, u32[]{:S(2)}, u32[]{:S(2)}) collective-permute-start(bf16[96,3072]{1,0:T(8,128)(2,1)} %collective-permute-done.5.refs_3_), channel_id=1, source_target_pairs={{0,384},{32,416},{64,448},{96,480},{128,0},{160,32},{192,64},{224,... | collective-permute-start | bytes 1769480 | tf_op jit(solution)/shard_map/ppermute | solution.py:33
  38.1 12.9 %collective-permute-start.2 = (bf16[96,3072]{1,0:T(8,128)(2,1)}, bf16[96,3072]{1,0:T(8,128)(2,1)S(1)}, u32[]{:S(2)}, u32[]{:S(2)}) collective-permute-start(bf16[96,3072]{1,0:T(8,128)(2,1)} %collective-permute-done.1.refs_2_), channel_id=1, source_target_pairs={{0,128},{32,160},{64,192},{96,224},{128,256},{160,288},{192,320},{... | collective-permute-start | bytes 1769480 | tf_op jit(solution)/shard_map/ppermute | solution.py:33
  45.9 0.8 copy-start.4
  51.0 0.8 copy-start.3
  51.0 1.0 copy-start.5
Sparse Core Ops, SparseCore 0:
  56.4 92.4 all-gather.1

commit v6 on v5

--- a/solution.py
+++ b/solution.py
@@ -10,7 +10,8 @@
 HEAD = 128
 PIECE = 48
 GROUP = 8
-BUFFERS = 8
+PLANES = 16
+BLOCKS = 16
 LOG2E = 1.4426950408889634
 MESH_AXES = ("seq", "bal")
 VMEM = pl.BlockSpec(memory_space=pltpu.VMEM)
@@ -31,6 +32,18 @@
 
 def send(block, phase, shift):
     return lax.ppermute(block, MESH_AXES, plane_perm(phase, shift))
+
+
+def swap_cores(block):
+    return lax.ppermute(block, "bal", [(at, at ^ 1) for at in range(32)])
+
+
+def pass_on(block):
+    pairs = []
+    for z in range(PLANES):
+        pairs.append((2 * z, 2 * ((z + 1) % PLANES)))
+        pairs.append((2 * z + 1, 2 * ((z - 1) % PLANES) + 1))
+    return lax.ppermute(block, "bal", pairs)
 
 
 def project_kernel(shares, place, *refs):
@@ -103,86 +116,116 @@
             pltpu.SemaphoreType.DMA((2,)),
         ],
         input_output_aliases={count + 4: 0, count + 5: 1} if begun else {},
-        compiler_params=pltpu.CompilerParams(vmem_limit_bytes=56 * 1024 * 1024),
+        compiler_params=pltpu.CompilerParams(vmem_limit_bytes=16 * 1024 * 1024),
         name="project",
     )(place, *blocks, weight, q_gain, k_gain, *begun)
 
 
-def attend_kernel(scale, picks, counts, q, kv, out, held, ready):
+def attend_kernel(scale, place, lists, counts, mine, other, *refs):
+    pieces = refs[:BLOCKS]
+    out_mine, out_other, kv, ready = refs[BLOCKS:]
     ones = jnp.ones((GROUP * TILE, HEAD), jnp.bfloat16)
-
-    def fetch(group, buffer):
-        for at in range(GROUP):
-            pick = picks[group * GROUP + at]
-            pltpu.make_async_copy(kv.at[pick], held.at[buffer, at], ready.at[buffer]).start()
-
-    def arrive(buffer):
-        pltpu.make_async_copy(held.at[buffer], held.at[buffer], ready.at[buffer]).wait()
-
-    for buffer in range(BUFFERS - 1):
-        fetch(buffer, buffer)
-
-    def one_slot(slot, group):
-        query = q[slot]
-        count = counts[slot]
-        turns = (count + GROUP - 1) // GROUP
-
-        def turn(step, acc):
-            at = group + step
-            buffer = at % BUFFERS
-            fetch(at + BUFFERS - 1, (at + BUFFERS - 1) % BUFFERS)
-            arrive(buffer)
-            keys = held[buffer, :, :, :HEAD].reshape(GROUP * TILE, HEAD)
-            values = held[buffer, :, :, HEAD:].reshape(GROUP * TILE, HEAD)
-            scores = lax.dot_general(
-                query, keys, (((1,), (1,)), ((), ())), preferred_element_type=jnp.float32
-            )
-            live = (count - step * GROUP) * TILE
-            column = lax.broadcasted_iota(jnp.int32, scores.shape, 1)
-            weights = jnp.where(column < live, jnp.exp2(scores * scale), 0.0)
-            return acc + jnp.dot(
-                weights.astype(jnp.bfloat16),
-                jnp.concatenate((values, ones), axis=1),
-                preferred_element_type=jnp.float32,
-            )
-
-        acc = lax.fori_loop(0, turns, turn, jnp.zeros((TILE, 2 * HEAD), jnp.float32))
-        out[slot] = (acc[:, :HEAD] / acc[:, HEAD:]).astype(jnp.bfloat16)
-        return group + turns
-
-    groups = lax.fori_loop(0, q.shape[0], one_slot, jnp.int32(0))
-    for extra in range(BUFFERS - 1):
-        arrive((groups + extra) % BUFFERS)
-
-
-def flat_picks(lists, counts):
-    slots, listed = lists.shape
-    turns = (counts + GROUP - 1) // GROUP
-    ends = jnp.cumsum(turns)
-    room = slots * (listed // GROUP) + BUFFERS
-    group = jnp.arange(room, dtype=jnp.int32)
-    slot = jnp.sum((group[:, None] >= ends[None, :]).astype(jnp.int32), axis=1)
-    slot = jnp.minimum(slot, slots - 1)
-    step = jnp.clip(group - (ends - turns)[slot], 0, listed // GROUP - 1)
-    return lists.reshape(slots * (listed // GROUP), GROUP)[
-        slot * (listed // GROUP) + step
-    ].reshape(-1)
-
-
-def attend(q, kv, lists, counts):
+    slots = mine.shape[0]
+    loads = [
+        pltpu.make_async_copy(pieces[at], kv.at[pl.ds(at * slots, slots)], ready.at[at])
+        for at in range(BLOCKS)
+    ]
+    for load in loads:
+        load.start()
+    for load in loads:
+        load.wait()
+
+    def attend_tiles(q, out, base):
+        def one_slot(slot, _):
+            query = q[slot]
+            count = counts[0, base + slot]
+
+            def turn(step, acc):
+                picks = [lists[base + slot, step * GROUP + at] for at in range(GROUP)]
+                keys = jnp.concatenate([kv[pick, :, :HEAD] for pick in picks], axis=0)
+                values = jnp.concatenate([kv[pick, :, HEAD:] for pick in picks], axis=0)
+                scores = lax.dot_general(
+                    query, keys, (((1,), (1,)), ((), ())), preferred_element_type=jnp.float32
+                )
+                live = (count - step * GROUP) * TILE
+                column = lax.broadcasted_iota(jnp.int32, scores.shape, 1)
+                weights = jnp.where(column < live, jnp.exp2(scores * scale), 0.0)
+                return acc + jnp.dot(
+                    weights.astype(jnp.bfloat16),
+                    jnp.concatenate((values, ones), axis=1),
+                    preferred_element_type=jnp.float32,
+                )
+
+            turns = (count + GROUP - 1) // GROUP
+            out[slot] = lax.fori_loop(0, turns, turn, jnp.zeros((TILE, 2 * HEAD), jnp.float32))
+            return 0
+
+        lax.fori_loop(0, slots, one_slot, 0)
+
+    attend_tiles(other, out_other, (1 - place[4]) * slots)
+    attend_tiles(mine, out_mine, place[4] * slots)
+
+
+def attend(place, mine, other, pieces, lists, counts):
     scale = HEAD ** (-0.5) * LOG2E
+    slots = mine.shape[0]
+    sums = jax.ShapeDtypeStruct((slots, TILE, 2 * HEAD), jnp.float32)
     return pl.pallas_call(
         functools.partial(attend_kernel, scale),
-        out_shape=jax.ShapeDtypeStruct(q.shape, jnp.bfloat16),
-        in_specs=[SMEM, SMEM, VMEM, pl.BlockSpec(memory_space=pl.ANY)],
-        out_specs=VMEM,
+        out_shape=(sums, sums),
+        in_specs=[SMEM, SMEM, SMEM, VMEM, VMEM] + [pl.BlockSpec(memory_space=pl.ANY)] * BLOCKS,
+        out_specs=(VMEM, VMEM),
         scratch_shapes=[
-            pltpu.VMEM((BUFFERS, GROUP, TILE, 2 * HEAD), jnp.bfloat16),
-            pltpu.SemaphoreType.DMA((BUFFERS,)),
+            pltpu.VMEM((BLOCKS * slots, TILE, 2 * HEAD), jnp.bfloat16),
+            pltpu.SemaphoreType.DMA((BLOCKS,)),
         ],
-        compiler_params=pltpu.CompilerParams(vmem_limit_bytes=56 * 1024 * 1024),
+        compiler_params=pltpu.CompilerParams(vmem_limit_bytes=24 * 1024 * 1024),
         name="attend",
-    )(flat_picks(lists, counts), counts, q, kv)
+    )(place, lists, counts, mine, other, *pieces)
+
+
+def list_kernel(slots, place, tiles, counts, lists_out, counts_out):
+    core = place[4]
+    plane = place[5]
+    half = PLANES // 2
+    listed, rows = tiles.shape
+    tile = tiles[...]
+    bal = (tile * (65536 // slots + 1)) >> 16
+    away = (((bal >> 1) - plane) * (2 * core - 1)) & (PLANES - 1)
+    same = (bal & 1) == core
+    entry = lax.broadcasted_iota(jnp.int32, (listed, rows), 0)
+    least = jnp.where(same, 0, 1)
+    most = jnp.where(same, half, half - 1)
+    inside = (away >= least) & (away <= most) & (entry < counts[...])
+    held = jnp.where(inside, 1.0, 0.0)
+    pick = jnp.where(same, away, away + half) * slots + tile - bal * slots
+    down = lax.broadcasted_iota(jnp.int32, (listed, listed), 0)
+    along = lax.broadcasted_iota(jnp.int32, (listed, listed), 1)
+    before = jnp.where(along < down, 1.0, 0.0)
+    order = jnp.dot(before, held, preferred_element_type=jnp.float32)
+    order = jnp.where(held > 0.0, order, -1.0).astype(jnp.int32)
+    counts_out[...] = jnp.sum(held, axis=0, keepdims=True).astype(jnp.int32)
+    for row in range(rows):
+        hit = order[:, row : row + 1] == along
+        placed = jnp.where(hit, pick[:, row : row + 1], 0)
+        lists_out[row : row + 1, :] = jnp.sum(placed, axis=0, keepdims=True)
+
+
+def local_lists(key_tiles, key_counts, place, slots):
+    rows, listed = 2 * slots, key_tiles.shape[1]
+    tiles = lax.dynamic_slice_in_dim(key_tiles.T, place[5] * rows, rows, 1)
+    counts = lax.dynamic_slice_in_dim(key_counts, place[5] * rows, rows, 1)
+    return pl.pallas_call(
+        functools.partial(list_kernel, slots),
+        out_shape=(
+            jax.ShapeDtypeStruct((rows, listed), jnp.int32),
+            jax.ShapeDtypeStruct((1, rows), jnp.int32),
+        ),
+        in_specs=[SMEM, VMEM, VMEM],
+        out_specs=(VMEM, VMEM),
+        compiler_params=pltpu.CompilerParams(vmem_limit_bytes=4 * 1024 * 1024),
+        name="lists",
+    )(place, tiles, counts)
 
 
 def on_device(tokens, qkv_weight, q_gain, k_gain, key_tiles, key_counts):
@@ -196,11 +239,12 @@
             jnp.where(core == 0, y, x),
             jnp.where(core == 0, 1, 4),
             jnp.where(core == 0, 4, 1),
+            core,
+            me_bal // 2,
         )
     ).astype(jnp.int32)
     slots = 16 * PIECE // TILE
-    lists = lax.dynamic_slice_in_dim(key_tiles[0], me_bal * slots, slots, 0)
-    counts = lax.dynamic_slice_in_dim(key_counts[0], me_bal * slots, slots, 0)
+    lists, counts = local_lists(key_tiles[0], key_counts, place, slots)
 
     before = send(tokens, 1, 1)
     after = send(tokens, 1, -1)
@@ -242,13 +286,23 @@
         place,
         begun,
     )
-    all_pairs = lax.all_gather(pairs, "bal", axis=0, tiled=True)
-    result = attend(
-        queries.reshape(slots, TILE, HEAD),
-        all_pairs.reshape(-1, TILE, 2 * HEAD),
-        lists,
-        counts,
-    )
+    same, other = [pairs, pass_on(pairs)], []
+    moving = swap_cores(pairs)
+    for step in range(1, PLANES // 2):
+        moving = pass_on(moving)
+        other.append(moving)
+        same.append(pass_on(same[-1]))
+        if step == 3:
+            queries, moving = lax.optimization_barrier((queries, moving))
+            other_queries = swap_cores(queries)
+
+    def tiles(block):
+        return block.reshape(slots, TILE, block.shape[1])
+
+    pieces = [tiles(block) for block in same + other]
+    kept, given = attend(place, tiles(queries), tiles(other_queries), pieces, lists, counts)
+    sums = kept + swap_cores(given)
+    result = (sums[:, :, :HEAD] / sums[:, :, HEAD:]).astype(jnp.bfloat16)
     return lax.all_to_all(
         result.reshape(slots * TILE, HEAD), "seq", split_axis=0, concat_axis=1, tiled=True
     )

time: 184 us -> 186 us (1.011)
  starting transfers between devices: 28.6 us -> 120 us
  waiting for transfers between devices: 89.5 us -> 14.2 us
  between operations: 13.7 us -> 0.5 us
  local copies, waits for them, and re-layouts: 5.67 us -> 11.8 us
  other arithmetic: 5.31 us -> 0.16 us
  blocking collectives: 17.1 us -> 13.8 us
  Pallas kernels: 22.3 us -> 24.2 us
    ppermute x0 -> x18, starting transfers between devices: none -> 89.4 us  [the longest x15 66.2 us: pass_on(): return lax.ppermute(block, 'bal', pairs)]
    all_gather x1 -> x0, waiting for transfers between devices: 85.7 us -> none  [on_device(): all_pairs = lax.all_gather(pairs, 'bal', axis=0, tiled=True)]
    ppermute x0 -> x18, waiting for transfers between devices: none -> 12.4 us  [the longest x15 10.5 us: pass_on(): return lax.ppermute(block, 'bal', pairs)]
    unnamed x16 -> x28, local copies, waits for them, and re-layouts: 2.84 us -> 9.43 us
    pallas_call x1 -> x2, Pallas kernels: 8.65 us -> 13.7 us  [the longest x1 12.8 us: attend(): pl.pallas_call(functools.partial(attend_kernel, scale), out_shape=(sums,...]
    select_n x2 -> x0, other arithmetic: 3.82 us -> none  [the longest x1 3.74 us: flat_picks(): lists.reshape(slots * (listed // GROUP), GROUP)]
    all_to_all x1, blocking collectives: 17.1 us -> 13.8 us  [on_device(): lax.all_to_all(result.reshape(slots * TILE, HEAD), 'seq', split_axis=0, c...]
    pallas_call x3, Pallas kernels: 13.7 us -> 10.5 us  [project(): pl.pallas_call(functools.partial(project_kernel, shares), out_shape=(jax....]
  transfers between devices with their start and end apart: 10 -> 27, of which waited for: 4 -> 8; matrix products, arithmetic and copies ran while one was open for 5% -> 2% of each run, Pallas kernels for 5% -> 4%
where the time goes in v6:
time: 186 us; the launch traced here: 185 us
  starting transfers between devices  120 us (65%)
  Pallas kernels  24.2 us (13%)
  waiting for transfers between devices  14.2 us (8%)
  blocking collectives  13.8 us (7%)
  local copies, waits for them, and re-layouts  11.8 us (6%)
    ppermute x15, starting transfers between devices, pass_on(): return lax.ppermute(block, 'bal', pairs)  66.2 us
    ppermute x9, starting transfers between devices, send(): return lax.ppermute(block, MESH_AXES, plane_perm(phase, shift))  30.7 us
    ppermute x3, starting transfers between devices, swap_cores(): return lax.ppermute(block, 'bal', [(at, at ^ 1) for at in range(32)])  23.2 us
    all_to_all x1, blocking collectives, on_device(): lax.all_to_all(result.reshape(slots * TILE, HEAD), 'seq', split_axis=0, c...  13.8 us
    pallas_call x1, Pallas kernels, attend(): pl.pallas_call(functools.partial(attend_kernel, scale), out_shape=(sums,...  12.8 us
    ppermute x15, waiting for transfers between devices, pass_on(): return lax.ppermute(block, 'bal', pairs)  10.5 us
    pallas_call x3, Pallas kernels, project(): pl.pallas_call(functools.partial(project_kernel, shares), out_shape=(jax....  10.5 us
    unnamed x28, local copies, waits for them, and re-layouts  9.43 us
  transfers between devices with their start and end apart: 27, of which 8 were waited for; matrix products, arithmetic and copies ran while one was open for 2% of the time, Pallas kernels for 4%

profile of v6, /device:TPU:1, one launch (start us, length us, event | category | flops | bytes accessed | tf_op | source)
XLA Modules:
  0.0 184.7 jit_solution(4801841368962574310)
XLA Ops:
  0.0 4.2 %collective-permute-start = (bf16[48,3072]{1,0:T(8,128)(2,1)}, bf16[48,3072]{1,0:T(8,128)(2,1)S(1)}, u32[]{:S(2)}, u32[]{:S(2)}) collective-permute-start(bf16[48,3072]{1,0:T(8,128)(2,1)} %param.6), channel_id=1, source_target_pairs={{0,32},{32,64},{64,96},{96,0},{128,160},{160,192},{192,224},{224,1... | collective-permute-start | bytes 884744 | tf_op jit(solution)/shard_map/ppermute | solution.py:34
  4.2 4.5 %collective-permute-start.4 = (bf16[48,3072]{1,0:T(8,128)(2,1)}, bf16[48,3072]{1,0:T(8,128)(2,1)S(1)}, u32[]{:S(2)}, u32[]{:S(2)}) collective-permute-start(bf16[48,3072]{1,0:T(8,128)(2,1)} %param.6), channel_id=1, source_target_pairs={{0,64},{32,96},{64,0},{96,32},{128,192},{160,224},{192,128},{224,1... | collective-permute-start | bytes 884744 | tf_op jit(solution)/shard_map/ppermute | solution.py:34
  8.7 3.0 %collective-permute-start.3 = (bf16[48,3072]{1,0:T(8,128)(2,1)}, bf16[48,3072]{1,0:T(8,128)(2,1)S(1)}, u32[]{:S(2)}, u32[]{:S(2)}) collective-permute-start(bf16[48,3072]{1,0:T(8,128)(2,1)} %param.6), channel_id=1, source_target_pairs={{0,96},{32,0},{64,32},{96,64},{128,224},{160,128},{192,160},{224,1... | collective-permute-start | bytes 884744 | tf_op jit(solution)/shard_map/ppermute | solution.py:34
  11.7 1.7 constant_dynamic-update-slice_fusion.1
  13.4 0.8 constant_dynamic-update-slice_fusion.refs_0_
  14.2 3.1 %collective-permute-start.1 = (bf16[96,3072]{1,0:T(8,128)(2,1)}, bf16[96,3072]{1,0:T(8,128)(2,1)}, u32[]{:S(2)}, u32[]{:S(2)}) collective-permute-start(bf16[96,3072]{1,0:T(8,128)(2,1)} %constant_dynamic-update-slice_fusion.refs_0_), channel_id=1, source_target_pairs={{0,128},{32,160},{64,192},{96,224},{128,256},{160,288},{192,320},{... | collective-permute-start | bytes 1769480 | tf_op jit(solution)/shard_map/ppermute | solution.py:34
  17.3 0.0 collective-permute-done.3
  17.3 0.7 constant_dynamic-update-slice_fusion.3
  18.1 0.7 constant_dynamic-update-slice_fusion.2.refs_1_
  18.8 3.8 %collective-permute-start.5 = (bf16[96,3072]{1,0:T(8,128)(2,1)}, bf16[96,3072]{1,0:T(8,128)(2,1)}, u32[]{:S(2)}, u32[]{:S(2)}) collective-permute-start(bf16[96,3072]{1,0:T(8,128)(2,1)} %constant_dynamic-update-slice_fusion.2.refs_1_), channel_id=1, source_target_pairs={{0,384},{32,416},{64,448},{96,480},{128,0},{160,32},{192,64},{224,... | collective-permute-start | bytes 1769480 | tf_op jit(solution)/shard_map/ppermute | solution.py:34
  22.6 2.8 %collective-permute-start.7 = (bf16[96,3072]{1,0:T(8,128)(2,1)}, bf16[96,3072]{1,0:T(8,128)(2,1)}, u32[]{:S(2)}, u32[]{:S(2)}) collective-permute-start(bf16[96,3072]{1,0:T(8,128)(2,1)} %constant_dynamic-update-slice_fusion.refs_0_), channel_id=1, source_target_pairs={{0,384},{32,416},{64,448},{96,480},{128,0},{160,32},{192,64},{224,... | collective-permute-start | bytes 1769480 | tf_op jit(solution)/shard_map/ppermute | solution.py:34
  25.3 2.5 %collective-permute-start.8 = (bf16[96,3072]{1,0:T(8,128)(2,1)}, bf16[96,3072]{1,0:T(8,128)(2,1)}, u32[]{:S(2)}, u32[]{:S(2)}) collective-permute-start(bf16[96,3072]{1,0:T(8,128)(2,1)} %constant_dynamic-update-slice_fusion.2.refs_1_), channel_id=1, source_target_pairs={{0,128},{32,160},{64,192},{96,224},{128,256},{160,288},{192,320},{... | collective-permute-start | bytes 1769480 | tf_op jit(solution)/shard_map/ppermute | solution.py:34
  27.9 1.9 %collective-permute-start.2 = (bf16[96,3072]{1,0:T(8,128)(2,1)}, bf16[96,3072]{1,0:T(8,128)(2,1)}, u32[]{:S(2)}, u32[]{:S(2)}) collective-permute-start(bf16[96,3072]{1,0:T(8,128)(2,1)} %collective-permute-done.1.refs_2_), channel_id=1, source_target_pairs={{0,128},{32,160},{64,192},{96,224},{128,256},{160,288},{192,320},{... | collective-permute-start | bytes 1769480 | tf_op jit(solution)/shard_map/ppermute | solution.py:34
  29.8 0.2 collective-permute-done.5.refs_3_
  30.0 5.0 %collective-permute-start.6 = (bf16[96,3072]{1,0:T(8,128)(2,1)}, bf16[96,3072]{1,0:T(8,128)(2,1)}, u32[]{:S(2)}, u32[]{:S(2)}) collective-permute-start(bf16[96,3072]{1,0:T(8,128)(2,1)} %collective-permute-done.5.refs_3_), channel_id=1, source_target_pairs={{0,384},{32,416},{64,448},{96,480},{128,0},{160,32},{192,64},{224,... | collective-permute-start | bytes 1769480 | tf_op jit(solution)/shard_map/ppermute | solution.py:34
  35.0 0.1 stack.27.place
  35.1 4.3 %project.3 = (bf16[768,128]{1,0:T(8,128)(2,1)S(1)}, bf16[768,256]{1,0:T(8,128)(2,1)S(1)}) custom-call(s32[6]{0:T(128)S(1)} %stack.27.place, bf16[96,3072]{1,0:T(8,128)(2,1)} %constant_dynamic-update-slice_fusion.refs_0_, bf16[96,3072]{1,0:T(8,128)(2,1)} %constant_dynamic-update-slice_fusion.2.refs_1_, bf16[96,3072]{1,0:T(8,128)(2,1)} %collective-permute-done.1.refs_2_, ...), custom_call_target="tpu_custom_call" | custom-call | tf_op jit(solution)/shard_map/project/pallas_call | solution.py:101
  39.4 0.0 collective-permute-done.7.refs_0_
  39.4 0.0 collective-permute-done.8.refs_1_
  39.5 3.1 %project.4 = (bf16[768,128]{1,0:T(8,128)(2,1)S(1)}, bf16[768,256]{1,0:T(8,128)(2,1)S(1)}) custom-call(s32[6]{0:T(128)S(1)} %stack.27.place, bf16[96,3072]{1,0:T(8,128)(2,1)} %collective-permute-done.7.refs_0_, bf16[96,3072]{1,0:T(8,128)(2,1)} %collective-permute-done.8.refs_1_, ...), custom_call_target="tpu_custom_call", output_to_operand_aliasing={{0}: (6, {}), {1}: (7, {})} | custom-call | tf_op jit(solution)/shard_map/project/pallas_call | solution.py:101
  42.6 0.0 copy-start.12
  42.6 1.5 collective-permute-done.2.refs_0_
  44.1 0.0 collective-permute-done.6.refs_1_
  44.1 3.1 %project.5 = (bf16[768,128]{1,0:T(8,128)(2,1)S(1)}, bf16[768,256]{1,0:T(8,128)(2,1)S(1)}) custom-call(s32[6]{0:T(128)S(1)} %stack.27.place, bf16[96,3072]{1,0:T(8,128)(2,1)} %collective-permute-done.2.refs_0_, bf16[96,3072]{1,0:T(8,128)(2,1)} %collective-permute-done.6.refs_1_, ...), custom_call_target="tpu_custom_call", output_to_operand_aliasing={{0}: (6, {}), {1}: (7, {})} | custom-call | tf_op jit(solution)/shard_map/project/pallas_call | solution.py:101
  47.2 8.9 %collective-permute-start.9 = (bf16[768,256]{1,0:T(8,128)(2,1)S(1)}, bf16[768,256]{1,0:T(8,128)(2,1)S(1)}, u32[]{:S(2)}, u32[]{:S(2)}) collective-permute-start(bf16[768,256]{1,0:T(8,128)(2,1)S(1)} %get-tuple-element.24), channel_id=1, source_target_pairs={{0,1},{1,0},{2,3},{3,2},{4,5},{5,4},{6,7},{7,6},{8,9},{9,8},{10,11... | collective-permute-start | bytes 1179656 | tf_op jit(solution)/shard_map/ppermute | solution.py:38
  56.1 7.5 %collective-permute-start.14 = (bf16[768,256]{1,0:T(8,128)(2,1)S(1)}, bf16[768,256]{1,0:T(8,128)(2,1)S(1)}, u32[]{:S(2)}, u32[]{:S(2)}) collective-permute-start(bf16[768,256]{1,0:T(8,128)(2,1)S(1)} %get-tuple-element.24), channel_id=1, source_target_pairs={{0,2},{1,31},{2,4},{3,1},{4,6},{5,3},{6,8},{7,5},{8,10},{9,7},{10,... | collective-permute-start | bytes 1179656 | tf_op jit(solution)/shard_map/ppermute | solution.py:46
  63.6 2.6 %collective-permute-start.10 = (bf16[768,256]{1,0:T(8,128)(2,1)S(1)}, bf16[768,256]{1,0:T(8,128)(2,1)S(1)}, u32[]{:S(2)}, u32[]{:S(2)}) collective-permute-start(bf16[768,256]{1,0:T(8,128)(2,1)S(1)} %collective-permute-done.9), channel_id=1, source_target_pairs={{0,2},{1,31},{2,4},{3,1},{4,6},{5,3},{6,8},{7,5},{8,10},{9,7},{10,... | collective-permute-start | bytes 1179656 | tf_op jit(solution)/shard_map/ppermute | solution.py:46
  66.2 2.0 %collective-permute-done.14 = bf16[768,256]{1,0:T(8,128)(2,1)S(1)} collective-permute-done((bf16[768,256]{1,0:T(8,128)(2,1)S(1)}, bf16[768,256]{1,0:T(8,128)(2,1)S(1)}, u32[]{:S(2)}, u32[]{:S(2)}) %collective-permute-start.14) | collective-permute-done | bytes 393248 | tf_op jit(solution)/shard_map/ppermute | solution.py:46
  68.2 5.0 %collective-permute-start.15 = (bf16[768,256]{1,0:T(8,128)(2,1)S(1)}, bf16[768,256]{1,0:T(8,128)(2,1)S(1)}, u32[]{:S(2)}, u32[]{:S(2)}) collective-permute-start(bf16[768,256]{1,0:T(8,128)(2,1)S(1)} %collective-permute-done.14), channel_id=1, source_target_pairs={{0,2},{1,31},{2,4},{3,1},{4,6},{5,3},{6,8},{7,5},{8,10},{9,7},{10,... | collective-permute-start | bytes 1179656 | tf_op jit(solution)/shard_map/ppermute | solution.py:46
  73.3 4.2 %collective-permute-start.11 = (bf16[768,256]{1,0:T(8,128)(2,1)S(1)}, bf16[768,256]{1,0:T(8,128)(2,1)S(1)}, u32[]{:S(2)}, u32[]{:S(2)}) collective-permute-start(bf16[768,256]{1,0:T(8,128)(2,1)S(1)} %collective-permute-done.10), channel_id=1, source_target_pairs={{0,2},{1,31},{2,4},{3,1},{4,6},{5,3},{6,8},{7,5},{8,10},{9,7},{10,... | collective-permute-start | bytes 1179656 | tf_op jit(solution)/shard_map/ppermute | solution.py:46
  77.5 0.5 collective-permute-done.15
  78.0 5.0 %collective-permute-start.16 = (bf16[768,256]{1,0:T(8,128)(2,1)S(1)}, bf16[768,256]{1,0:T(8,128)(2,1)S(1)}, u32[]{:S(2)}, u32[]{:S(2)}) collective-permute-start(bf16[768,256]{1,0:T(8,128)(2,1)S(1)} %collective-permute-done.15), channel_id=1, source_target_pairs={{0,2},{1,31},{2,4},{3,1},{4,6},{5,3},{6,8},{7,5},{8,10},{9,7},{10,... | collective-permute-start | bytes 1179656 | tf_op jit(solution)/shard_map/ppermute | solution.py:46
  83.0 4.2 %collective-permute-start.12 = (bf16[768,256]{1,0:T(8,128)(2,1)S(1)}, bf16[768,256]{1,0:T(8,128)(2,1)S(1)}, u32[]{:S(2)}, u32[]{:S(2)}) collective-permute-start(bf16[768,256]{1,0:T(8,128)(2,1)S(1)} %collective-permute-done.11), channel_id=1, source_target_pairs={{0,2},{1,31},{2,4},{3,1},{4,6},{5,3},{6,8},{7,5},{8,10},{9,7},{10,... | collective-permute-start | bytes 1179656 | tf_op jit(solution)/shard_map/ppermute | solution.py:46
  87.2 0.5 collective-permute-done.16
  87.7 5.0 %collective-permute-start.17 = (bf16[768,256]{1,0:T(8,128)(2,1)S(1)}, bf16[768,256]{1,0:T(8,128)(2,1)S(1)}, u32[]{:S(2)}, u32[]{:S(2)}) collective-permute-start(bf16[768,256]{1,0:T(8,128)(2,1)S(1)} %collective-permute-done.16), channel_id=1, source_target_pairs={{0,2},{1,31},{2,4},{3,1},{4,6},{5,3},{6,8},{7,5},{8,10},{9,7},{10,... | collective-permute-start | bytes 1179656 | tf_op jit(solution)/shard_map/ppermute | solution.py:46
  92.7 4.7 %collective-permute-done.17 = bf16[768,256]{1,0:T(8,128)(2,1)S(1)} collective-permute-done((bf16[768,256]{1,0:T(8,128)(2,1)S(1)}, bf16[768,256]{1,0:T(8,128)(2,1)S(1)}, u32[]{:S(2)}, u32[]{:S(2)}) %collective-permute-start.17) | collective-permute-done | bytes 393248 | tf_op jit(solution)/shard_map/ppermute | solution.py:46
  97.4 5.0 %collective-permute-start.18 = (bf16[768,256]{1,0:T(8,128)(2,1)S(1)}, bf16[768,256]{1,0:T(8,128)(2,1)S(1)}, u32[]{:S(2)}, u32[]{:S(2)}) collective-permute-start(bf16[768,256]{1,0:T(8,128)(2,1)S(1)} %collective-permute-done.17), channel_id=1, source_target_pairs={{0,2},{1,31},{2,4},{3,1},{4,6},{5,3},{6,8},{7,5},{8,10},{9,7},{10,... | collective-permute-start | bytes 1179656 | tf_op jit(solution)/shard_map/ppermute | solution.py:46
  102.4 1.9 %collective-permute-start.22 = (bf16[768,256]{1,0:T(8,128)(2,1)S(1)}, bf16[768,256]{1,0:T(8,128)(2,1)S(1)}, u32[]{:S(2)}, u32[]{:S(2)}) collective-permute-start(bf16[768,256]{1,0:T(8,128)(2,1)S(1)} %collective-permute-done.12), channel_id=1, source_target_pairs={{0,2},{1,31},{2,4},{3,1},{4,6},{5,3},{6,8},{7,5},{8,10},{9,7},{10,... | collective-permute-start | bytes 1179656 | tf_op jit(solution)/shard_map/ppermute | solution.py:46
  104.4 2.8 %collective-permute-done.18 = bf16[768,256]{1,0:T(8,128)(2,1)S(1)} collective-permute-done((bf16[768,256]{1,0:T(8,128)(2,1)S(1)}, bf16[768,256]{1,0:T(8,128)(2,1)S(1)}, u32[]{:S(2)}, u32[]{:S(2)}) %collective-permute-start.18) | collective-permute-done | bytes 393248 | tf_op jit(solution)/shard_map/ppermute | solution.py:46
  107.1 5.0 %collective-permute-start.19 = (bf16[768,256]{1,0:T(8,128)(2,1)S(1)}, bf16[768,256]{1,0:T(8,128)(2,1)S(1)}, u32[]{:S(2)}, u32[]{:S(2)}) collective-permute-start(bf16[768,256]{1,0:T(8,128)(2,1)S(1)} %collective-permute-done.18), channel_id=1, source_target_pairs={{0,2},{1,31},{2,4},{3,1},{4,6},{5,3},{6,8},{7,5},{8,10},{9,7},{10,... | collective-permute-start | bytes 1179656 | tf_op jit(solution)/shard_map/ppermute | solution.py:46
  112.2 0.7 copy-done.2
  112.9 3.5 %collective-permute-start.23 = (bf16[768,256]{1,0:T(8,128)(2,1)S(1)}, bf16[768,256]{1,0:T(8,128)(2,1)S(1)}, u32[]{:S(2)}, u32[]{:S(2)}) collective-permute-start(bf16[768,256]{1,0:T(8,128)(2,1)S(1)} %collective-permute-done.22), channel_id=1, source_target_pairs={{0,2},{1,31},{2,4},{3,1},{4,6},{5,3},{6,8},{7,5},{8,10},{9,7},{10,... | collective-permute-start | bytes 1179656 | tf_op jit(solution)/shard_map/ppermute | solution.py:46
  116.4 0.7 copy-done.4
  117.1 4.8 %collective-permute-start.20 = (bf16[768,256]{1,0:T(8,128)(2,1)S(1)}, bf16[768,256]{1,0:T(8,128)(2,1)}, u32[]{:S(2)}, u32[]{:S(2)}) collective-permute-start(bf16[768,256]{1,0:T(8,128)(2,1)S(1)} %collective-permute-done.19), channel_id=1, source_target_pairs={{0,2},{1,31},{2,4},{3,1},{4,6},{5,3},{6,8},{7,5},{8,10},{9,7},{10,... | collective-permute-start | bytes 1179656 | tf_op jit(solution)/shard_map/ppermute | solution.py:46
  121.9 0.7 copy-done.6
  122.6 3.4 %collective-permute-start.24 = (bf16[768,256]{1,0:T(8,128)(2,1)S(1)}, bf16[768,256]{1,0:T(8,128)(2,1)}, u32[]{:S(2)}, u32[]{:S(2)}) collective-permute-start(bf16[768,256]{1,0:T(8,128)(2,1)S(1)} %collective-permute-done.23), channel_id=1, source_target_pairs={{0,2},{1,31},{2,4},{3,1},{4,6},{5,3},{6,8},{7,5},{8,10},{9,7},{10,... | collective-permute-start | bytes 1179656 | tf_op jit(solution)/shard_map/ppermute | solution.py:46
  126.1 0.8 copy-done.8
  126.9 4.8 %collective-permute-start.21 = (bf16[768,256]{1,0:T(8,128)(2,1)}, bf16[768,256]{1,0:T(8,128)(2,1)}, u32[]{:S(2)}, u32[]{:S(2)}) collective-permute-start(bf16[768,256]{1,0:T(8,128)(2,1)} %collective-permute-done.20), channel_id=1, source_target_pairs={{0,2},{1,31},{2,4},{3,1},{4,6},{5,3},{6,8},{7,5},{8,10},{9,7},{10,... | collective-permute-start | bytes 1179656 | tf_op jit(solution)/shard_map/ppermute | solution.py:46
  131.7 4.2 %collective-permute-start.25 = (bf16[768,256]{1,0:T(8,128)(2,1)}, bf16[768,256]{1,0:T(8,128)(2,1)}, u32[]{:S(2)}, u32[]{:S(2)}) collective-permute-start(bf16[768,256]{1,0:T(8,128)(2,1)} %collective-permute-done.24), channel_id=1, source_target_pairs={{0,2},{1,31},{2,4},{3,1},{4,6},{5,3},{6,8},{7,5},{8,10},{9,7},{10,... | collective-permute-start | bytes 1179656 | tf_op jit(solution)/shard_map/ppermute | solution.py:46
  135.9 7.0 %collective-permute-start.13 = (bf16[768,128]{1,0:T(8,128)(2,1)S(1)}, bf16[768,128]{1,0:T(8,128)(2,1)S(1)}, u32[]{:S(2)}, u32[]{:S(2)}) collective-permute-start(bf16[768,128]{1,0:T(8,128)(2,1)S(1)} %get-tuple-element.25), channel_id=1, source_target_pairs={{0,1},{1,0},{2,3},{3,2},{4,5},{5,4},{6,7},{7,6},{8,9},{9,8},{10,11... | collective-permute-start | bytes 589832 | tf_op jit(solution)/shard_map/ppermute | solution.py:38
  143.0 0.1 constant_dynamic-slice_fusion.counts
  143.1 0.1 dynamic-slice_bitcast_fusion.tiles
  143.1 0.9 lists.1
  144.1 1.0 copy-done.3
  145.1 1.0 copy-done.5
  146.1 1.0 copy-done.7
  147.1 1.0 copy-done.9
  148.1 12.8 %attend.1 = (f32[6,128,256]{2,1,0:T(8,128)S(1)}, f32[6,128,256]{2,1,0:T(8,128)S(1)}) custom-call(s32[6]{0:T(128)S(1)} %stack.27.place, s32[12,64]{1,0:T(8,128)S(1)} %get-tuple-element.17.lists, s32[1,12]{1,0:T(1,128)S(1)} %get-tuple-element.18.counts, bf16[6,128,128]{2,1,0:T(8,128)(2,1)S(1)} %bitcast.42, bf16[6,128,128]{2,1,0:T(8,128)(2,1)S(1)} %bitcast.54, ...), custom_call_target="tpu_custom_call" | custom-call | tf_op jit(solution)/shard_map/attend/pallas_call | solution.py:173
  160.9 7.3 %collective-permute-start.26 = (f32[6,128,256]{2,1,0:T(8,128)S(1)}, f32[6,128,256]{2,1,0:T(8,128)S(1)}, u32[]{:S(2)}, u32[]{:S(2)}) collective-permute-start(f32[6,128,256]{2,1,0:T(8,128)S(1)} %get-tuple-element.28), channel_id=1, source_target_pairs={{0,1},{1,0},{2,3},{3,2},{4,5},{5,4},{6,7},{7,6},{8,9},{9,8},{10,11... | collective-permute-start | bytes 2359304 | tf_op jit(solution)/shard_map/ppermute | solution.py:38
  168.2 1.9 %collective-permute-done.26 = f32[6,128,256]{2,1,0:T(8,128)S(1)} collective-permute-done((f32[6,128,256]{2,1,0:T(8,128)S(1)}, f32[6,128,256]{2,1,0:T(8,128)S(1)}, u32[]{:S(2)}, u32[]{:S(2)}) %collective-permute-start.26) | collective-permute-done | bytes 786464 | tf_op jit(solution)/shard_map/ppermute | solution.py:38
  170.1 0.1 add.19
  170.2 0.1 fusion
  170.3 13.8 %all_to_all.19 = bf16[16,48,128]{2,1,0:T(8,128)(2,1)S(1)} all-to-all(bf16[16,48,128]{2,1,0:T(8,128)(2,1)S(1)} %bitcast.55), channel_id=1, replica_groups=mesh['seq'=16,'bal'=32] {'seq'}, dimensions={0} | all-to-all | bytes 393216 | tf_op jit(solution)/shard_map/all_to_all | solution.py:306
  184.1 0.7 copy_bitcast_fusion
  (32 shorter events, 0.1 us)
Async XLA Ops:
  0.0 143.1 %copy-start = (s32[1,192,64]{1,2,0:T(8,128)S(1)}, s32[1,192,64]{1,2,0:T(8,128)}, u32[]{:S(2)}) copy-start(s32[1,192,64]{1,2,0:T(8,128)} %param.10) | copy-start | bytes 147460
  0.0 35.1 %copy-start.11 = (f32[1,128]{1,0:T(1,128)S(1)}, f32[1,128]{1,0:T(1,128)}, u32[]{:S(2)}) copy-start(f32[1,128]{1,0:T(1,128)} %refs_4_.3) | copy-start | bytes 1540
  0.0 35.1 %copy-start.10 = (f32[1,128]{1,0:T(1,128)S(1)}, f32[1,128]{1,0:T(1,128)}, u32[]{:S(2)}) copy-start(f32[1,128]{1,0:T(1,128)} %refs_3_.3) | copy-start | bytes 1540
  0.0 35.1 %copy-start.1 = (bf16[3072,1,3,128]{3,0,2,1:T(8,128)(2,1)S(1)}, bf16[3072,1,3,128]{3,0,2,1:T(8,128)(2,1)}, u32[]{:S(2)}) copy-start(bf16[3072,1,3,128]{3,0,2,1:T(8,128)(2,1)} %param.7) | copy-start | bytes 7077892
  0.0 13.4 %collective-permute-start = (bf16[48,3072]{1,0:T(8,128)(2,1)}, bf16[48,3072]{1,0:T(8,128)(2,1)S(1)}, u32[]{:S(2)}, u32[]{:S(2)}) collective-permute-start(bf16[48,3072]{1,0:T(8,128)(2,1)} %param.6), channel_id=1, source_target_pairs={{0,32},{32,64},{64,96},{96,0},{128,160},{160,192},{192,224},{224,1... | collective-permute-start | bytes 884744 | tf_op jit(solution)/shard_map/ppermute | solution.py:34
  4.2 13.9 %collective-permute-start.4 = (bf16[48,3072]{1,0:T(8,128)(2,1)}, bf16[48,3072]{1,0:T(8,128)(2,1)S(1)}, u32[]{:S(2)}, u32[]{:S(2)}) collective-permute-start(bf16[48,3072]{1,0:T(8,128)(2,1)} %param.6), channel_id=1, source_target_pairs={{0,64},{32,96},{64,0},{96,32},{128,192},{160,224},{192,128},{224,1... | collective-permute-start | bytes 884744 | tf_op jit(solution)/shard_map/ppermute | solution.py:34
  8.7 8.6 %collective-permute-start.3 = (bf16[48,3072]{1,0:T(8,128)(2,1)}, bf16[48,3072]{1,0:T(8,128)(2,1)S(1)}, u32[]{:S(2)}, u32[]{:S(2)}) collective-permute-start(bf16[48,3072]{1,0:T(8,128)(2,1)} %param.6), channel_id=1, source_target_pairs={{0,96},{32,0},{64,32},{96,64},{128,224},{160,128},{192,160},{224,1... | collective-permute-start | bytes 884744 | tf_op jit(solution)/shard_map/ppermute | solution.py:34
  14.2 13.7 %collective-permute-start.1 = (bf16[96,3072]{1,0:T(8,128)(2,1)}, bf16[96,3072]{1,0:T(8,128)(2,1)}, u32[]{:S(2)}, u32[]{:S(2)}) collective-permute-start(bf16[96,3072]{1,0:T(8,128)(2,1)} %constant_dynamic-update-slice_fusion.refs_0_), channel_id=1, source_target_pairs={{0,128},{32,160},{64,192},{96,224},{128,256},{160,288},{192,320},{... | collective-permute-start | bytes 1769480 | tf_op jit(solution)/shard_map/ppermute | solution.py:34
  18.8 11.2 %collective-permute-start.5 = (bf16[96,3072]{1,0:T(8,128)(2,1)}, bf16[96,3072]{1,0:T(8,128)(2,1)}, u32[]{:S(2)}, u32[]{:S(2)}) collective-permute-start(bf16[96,3072]{1,0:T(8,128)(2,1)} %constant_dynamic-update-slice_fusion.2.refs_1_), channel_id=1, source_target_pairs={{0,384},{32,416},{64,448},{96,480},{128,0},{160,32},{192,64},{224,... | collective-permute-start | bytes 1769480 | tf_op jit(solution)/shard_map/ppermute | solution.py:34
  22.6 16.9 %collective-permute-start.7 = (bf16[96,3072]{1,0:T(8,128)(2,1)}, bf16[96,3072]{1,0:T(8,128)(2,1)}, u32[]{:S(2)}, u32[]{:S(2)}) collective-permute-start(bf16[96,3072]{1,0:T(8,128)(2,1)} %constant_dynamic-update-slice_fusion.refs_0_), channel_id=1, source_target_pairs={{0,384},{32,416},{64,448},{96,480},{128,0},{160,32},{192,64},{224,... | collective-permute-start | bytes 1769480 | tf_op jit(solution)/shard_map/ppermute | solution.py:34
  25.3 14.1 %collective-permute-start.8 = (bf16[96,3072]{1,0:T(8,128)(2,1)}, bf16[96,3072]{1,0:T(8,128)(2,1)}, u32[]{:S(2)}, u32[]{:S(2)}) collective-permute-start(bf16[96,3072]{1,0:T(8,128)(2,1)} %constant_dynamic-update-slice_fusion.2.refs_1_), channel_id=1, source_target_pairs={{0,128},{32,160},{64,192},{96,224},{128,256},{160,288},{192,320},{... | collective-permute-start | bytes 1769480 | tf_op jit(solution)/shard_map/ppermute | solution.py:34
  27.9 16.2 %collective-permute-start.2 = (bf16[96,3072]{1,0:T(8,128)(2,1)}, bf16[96,3072]{1,0:T(8,128)(2,1)}, u32[]{:S(2)}, u32[]{:S(2)}) collective-permute-start(bf16[96,3072]{1,0:T(8,128)(2,1)} %collective-permute-done.1.refs_2_), channel_id=1, source_target_pairs={{0,128},{32,160},{64,192},{96,224},{128,256},{160,288},{192,320},{... | collective-permute-start | bytes 1769480 | tf_op jit(solution)/shard_map/ppermute | solution.py:34
  30.0 14.1 %collective-permute-start.6 = (bf16[96,3072]{1,0:T(8,128)(2,1)}, bf16[96,3072]{1,0:T(8,128)(2,1)}, u32[]{:S(2)}, u32[]{:S(2)}) collective-permute-start(bf16[96,3072]{1,0:T(8,128)(2,1)} %collective-permute-done.5.refs_3_), channel_id=1, source_target_pairs={{0,384},{32,416},{64,448},{96,480},{128,0},{160,32},{192,64},{224,... | collective-permute-start | bytes 1769480 | tf_op jit(solution)/shard_map/ppermute | solution.py:34
  42.6 100.4 %copy-start.12 = (s32[1,192]{1,0:T(1,128)S(1)}, s32[1,192]{1,0:T(1,128)}, u32[]{:S(2)}) copy-start(s32[1,192]{1,0:T(1,128)} %param.11) | copy-start | bytes 2308
  47.2 16.3 %collective-permute-start.9 = (bf16[768,256]{1,0:T(8,128)(2,1)S(1)}, bf16[768,256]{1,0:T(8,128)(2,1)S(1)}, u32[]{:S(2)}, u32[]{:S(2)}) collective-permute-start(bf16[768,256]{1,0:T(8,128)(2,1)S(1)} %get-tuple-element.24), channel_id=1, source_target_pairs={{0,1},{1,0},{2,3},{3,2},{4,5},{5,4},{6,7},{7,6},{8,9},{9,8},{10,11... | collective-permute-start | bytes 1179656 | tf_op jit(solution)/shard_map/ppermute | solution.py:38
  56.1 12.2 %collective-permute-start.14 = (bf16[768,256]{1,0:T(8,128)(2,1)S(1)}, bf16[768,256]{1,0:T(8,128)(2,1)S(1)}, u32[]{:S(2)}, u32[]{:S(2)}) collective-permute-start(bf16[768,256]{1,0:T(8,128)(2,1)S(1)} %get-tuple-element.24), channel_id=1, source_target_pairs={{0,2},{1,31},{2,4},{3,1},{4,6},{5,3},{6,8},{7,5},{8,10},{9,7},{10,... | collective-permute-start | bytes 1179656 | tf_op jit(solution)/shard_map/ppermute | solution.py:46
  63.6 9.7 %collective-permute-start.10 = (bf16[768,256]{1,0:T(8,128)(2,1)S(1)}, bf16[768,256]{1,0:T(8,128)(2,1)S(1)}, u32[]{:S(2)}, u32[]{:S(2)}) collective-permute-start(bf16[768,256]{1,0:T(8,128)(2,1)S(1)} %collective-permute-done.9), channel_id=1, source_target_pairs={{0,2},{1,31},{2,4},{3,1},{4,6},{5,3},{6,8},{7,5},{8,10},{9,7},{10,... | collective-permute-start | bytes 1179656 | tf_op jit(solution)/shard_map/ppermute | solution.py:46
  68.2 9.7 %collective-permute-start.15 = (bf16[768,256]{1,0:T(8,128)(2,1)S(1)}, bf16[768,256]{1,0:T(8,128)(2,1)S(1)}, u32[]{:S(2)}, u32[]{:S(2)}) collective-permute-start(bf16[768,256]{1,0:T(8,128)(2,1)S(1)} %collective-permute-done.14), channel_id=1, source_target_pairs={{0,2},{1,31},{2,4},{3,1},{4,6},{5,3},{6,8},{7,5},{8,10},{9,7},{10,... | collective-permute-start | bytes 1179656 | tf_op jit(solution)/shard_map/ppermute | solution.py:46
  73.3 9.7 %collective-permute-start.11 = (bf16[768,256]{1,0:T(8,128)(2,1)S(1)}, bf16[768,256]{1,0:T(8,128)(2,1)S(1)}, u32[]{:S(2)}, u32[]{:S(2)}) collective-permute-start(bf16[768,256]{1,0:T(8,128)(2,1)S(1)} %collective-permute-done.10), channel_id=1, source_target_pairs={{0,2},{1,31},{2,4},{3,1},{4,6},{5,3},{6,8},{7,5},{8,10},{9,7},{10,... | collective-permute-start | bytes 1179656 | tf_op jit(solution)/shard_map/ppermute | solution.py:46
  78.0 9.7 %collective-permute-start.16 = (bf16[768,256]{1,0:T(8,128)(2,1)S(1)}, bf16[768,256]{1,0:T(8,128)(2,1)S(1)}, u32[]{:S(2)}, u32[]{:S(2)}) collective-permute-start(bf16[768,256]{1,0:T(8,128)(2,1)S(1)} %collective-permute-done.15), channel_id=1, source_target_pairs={{0,2},{1,31},{2,4},{3,1},{4,6},{5,3},{6,8},{7,5},{8,10},{9,7},{10,... | collective-permute-start | bytes 1179656 | tf_op jit(solution)/shard_map/ppermute | solution.py:46
  83.0 9.7 %collective-permute-start.12 = (bf16[768,256]{1,0:T(8,128)(2,1)S(1)}, bf16[768,256]{1,0:T(8,128)(2,1)S(1)}, u32[]{:S(2)}, u32[]{:S(2)}) collective-permute-start(bf16[768,256]{1,0:T(8,128)(2,1)S(1)} %collective-permute-done.11), channel_id=1, source_target_pairs={{0,2},{1,31},{2,4},{3,1},{4,6},{5,3},{6,8},{7,5},{8,10},{9,7},{10,... | collective-permute-start | bytes 1179656 | tf_op jit(solution)/shard_map/ppermute | solution.py:46
  87.7 9.7 %collective-permute-start.17 = (bf16[768,256]{1,0:T(8,128)(2,1)S(1)}, bf16[768,256]{1,0:T(8,128)(2,1)S(1)}, u32[]{:S(2)}, u32[]{:S(2)}) collective-permute-start(bf16[768,256]{1,0:T(8,128)(2,1)S(1)} %collective-permute-done.16), channel_id=1, source_target_pairs={{0,2},{1,31},{2,4},{3,1},{4,6},{5,3},{6,8},{7,5},{8,10},{9,7},{10,... | collective-permute-start | bytes 1179656 | tf_op jit(solution)/shard_map/ppermute | solution.py:46
  97.4 9.7 %collective-permute-start.18 = (bf16[768,256]{1,0:T(8,128)(2,1)S(1)}, bf16[768,256]{1,0:T(8,128)(2,1)S(1)}, u32[]{:S(2)}, u32[]{:S(2)}) collective-permute-start(bf16[768,256]{1,0:T(8,128)(2,1)S(1)} %collective-permute-done.17), channel_id=1, source_target_pairs={{0,2},{1,31},{2,4},{3,1},{4,6},{5,3},{6,8},{7,5},{8,10},{9,7},{10,... | collective-permute-start | bytes 1179656 | tf_op jit(solution)/shard_map/ppermute | solution.py:46
  102.4 10.5 %collective-permute-start.22 = (bf16[768,256]{1,0:T(8,128)(2,1)S(1)}, bf16[768,256]{1,0:T(8,128)(2,1)S(1)}, u32[]{:S(2)}, u32[]{:S(2)}) collective-permute-start(bf16[768,256]{1,0:T(8,128)(2,1)S(1)} %collective-permute-done.12), channel_id=1, source_target_pairs={{0,2},{1,31},{2,4},{3,1},{4,6},{5,3},{6,8},{7,5},{8,10},{9,7},{10,... | collective-permute-start | bytes 1179656 | tf_op jit(solution)/shard_map/ppermute | solution.py:46
  107.1 10.0 %collective-permute-start.19 = (bf16[768,256]{1,0:T(8,128)(2,1)S(1)}, bf16[768,256]{1,0:T(8,128)(2,1)S(1)}, u32[]{:S(2)}, u32[]{:S(2)}) collective-permute-start(bf16[768,256]{1,0:T(8,128)(2,1)S(1)} %collective-permute-done.18), channel_id=1, source_target_pairs={{0,2},{1,31},{2,4},{3,1},{4,6},{5,3},{6,8},{7,5},{8,10},{9,7},{10,... | collective-permute-start | bytes 1179656 | tf_op jit(solution)/shard_map/ppermute | solution.py:46
  112.1 0.7 copy-start.2
  112.9 9.7 %collective-permute-start.23 = (bf16[768,256]{1,0:T(8,128)(2,1)S(1)}, bf16[768,256]{1,0:T(8,128)(2,1)S(1)}, u32[]{:S(2)}, u32[]{:S(2)}) collective-permute-start(bf16[768,256]{1,0:T(8,128)(2,1)S(1)} %collective-permute-done.22), channel_id=1, source_target_pairs={{0,2},{1,31},{2,4},{3,1},{4,6},{5,3},{6,8},{7,5},{8,10},{9,7},{10,... | collective-permute-start | bytes 1179656 | tf_op jit(solution)/shard_map/ppermute | solution.py:46
  116.4 0.7 copy-start.4
  117.1 9.8 %collective-permute-start.20 = (bf16[768,256]{1,0:T(8,128)(2,1)S(1)}, bf16[768,256]{1,0:T(8,128)(2,1)}, u32[]{:S(2)}, u32[]{:S(2)}) collective-permute-start(bf16[768,256]{1,0:T(8,128)(2,1)S(1)} %collective-permute-done.19), channel_id=1, source_target_pairs={{0,2},{1,31},{2,4},{3,1},{4,6},{5,3},{6,8},{7,5},{8,10},{9,7},{10,... | collective-permute-start | bytes 1179656 | tf_op jit(solution)/shard_map/ppermute | solution.py:46
  121.9 0.8 copy-start.6
  122.6 9.1 %collective-permute-start.24 = (bf16[768,256]{1,0:T(8,128)(2,1)S(1)}, bf16[768,256]{1,0:T(8,128)(2,1)}, u32[]{:S(2)}, u32[]{:S(2)}) collective-permute-start(bf16[768,256]{1,0:T(8,128)(2,1)S(1)} %collective-permute-done.23), channel_id=1, source_target_pairs={{0,2},{1,31},{2,4},{3,1},{4,6},{5,3},{6,8},{7,5},{8,10},{9,7},{10,... | collective-permute-start | bytes 1179656 | tf_op jit(solution)/shard_map/ppermute | solution.py:46
  126.1 0.8 copy-start.8
  126.9 17.2 %collective-permute-start.21 = (bf16[768,256]{1,0:T(8,128)(2,1)}, bf16[768,256]{1,0:T(8,128)(2,1)}, u32[]{:S(2)}, u32[]{:S(2)}) collective-permute-start(bf16[768,256]{1,0:T(8,128)(2,1)} %collective-permute-done.20), channel_id=1, source_target_pairs={{0,2},{1,31},{2,4},{3,1},{4,6},{5,3},{6,8},{7,5},{8,10},{9,7},{10,... | collective-permute-start | bytes 1179656 | tf_op jit(solution)/shard_map/ppermute | solution.py:46
  131.7 12.4 %collective-permute-start.25 = (bf16[768,256]{1,0:T(8,128)(2,1)}, bf16[768,256]{1,0:T(8,128)(2,1)}, u32[]{:S(2)}, u32[]{:S(2)}) collective-permute-start(bf16[768,256]{1,0:T(8,128)(2,1)} %collective-permute-done.24), channel_id=1, source_target_pairs={{0,2},{1,31},{2,4},{3,1},{4,6},{5,3},{6,8},{7,5},{8,10},{9,7},{10,... | collective-permute-start | bytes 1179656 | tf_op jit(solution)/shard_map/ppermute | solution.py:46
  135.9 8.1 %collective-permute-start.13 = (bf16[768,128]{1,0:T(8,128)(2,1)S(1)}, bf16[768,128]{1,0:T(8,128)(2,1)S(1)}, u32[]{:S(2)}, u32[]{:S(2)}) collective-permute-start(bf16[768,128]{1,0:T(8,128)(2,1)S(1)} %get-tuple-element.25), channel_id=1, source_target_pairs={{0,1},{1,0},{2,3},{3,2},{4,5},{5,4},{6,7},{7,6},{8,9},{9,8},{10,11... | collective-permute-start | bytes 589832 | tf_op jit(solution)/shard_map/ppermute | solution.py:38
  144.1 1.0 copy-start.3
  145.1 1.0 copy-start.5
  146.1 1.0 copy-start.7
  147.1 1.0 copy-start.9
  160.9 9.2 %collective-permute-start.26 = (f32[6,128,256]{2,1,0:T(8,128)S(1)}, f32[6,128,256]{2,1,0:T(8,128)S(1)}, u32[]{:S(2)}, u32[]{:S(2)}) collective-permute-start(f32[6,128,256]{2,1,0:T(8,128)S(1)} %get-tuple-element.28), channel_id=1, source_target_pairs={{0,1},{1,0},{2,3},{3,2},{4,5},{5,4},{6,7},{7,6},{8,9},{9,8},{10,11... | collective-permute-start | bytes 2359304 | tf_op jit(solution)/shard_map/ppermute | solution.py:38

commit v7 on v6

v7 whole, which is shorter than its diff:
```python
import functools
import jax
import jax.numpy as jnp
from jax import lax
from jax.experimental import pallas as pl
from jax.experimental.pallas import tpu as pltpu
from jax.sharding import PartitionSpec as P

TILE = 128
HEAD = 128
PIECE = 48
PLANES = 16
UNROLL = 4
CALLS = ((0, 3),) + tuple((step, step + 1) for step in range(3, 9))
LOG2E = 1.4426950408889634
MESH_AXES = ("seq", "bal")
VMEM = pl.BlockSpec(memory_space=pltpu.VMEM)
SMEM = pl.BlockSpec(memory_space=pltpu.SMEM)


def plane_perm(phase, shift):
    pairs = []
    for bal in range(32):
        for y in range(4):
            for x in range(4):
                along_x = (bal % 2 == 0) == (phase == 1)
                to_y = y if along_x else (y + shift) % 4
                to_x = (x + shift) % 4 if along_x else x
                pairs.append(((4 * y + x) * 32 + bal, (4 * to_y + to_x) * 32 + bal))
    return pairs


def send(block, phase, shift):
    return lax.ppermute(block, MESH_AXES, plane_perm(phase, shift))


def swap_cores(block):
    return lax.ppermute(block, "bal", [(at, at ^ 1) for at in range(32)])


def pass_on(block, cores):
    pairs = []
    for z in range(PLANES):
        if 0 in cores:
            pairs.append((2 * z, 2 * ((z + 1) % PLANES)))
        if 1 in cores:
            pairs.append((2 * z + 1, 2 * ((z - 1) % PLANES) + 1))
    return lax.ppermute(block, "bal", pairs)


def project_kernel(shares, place, *refs):
    count = len(shares)
    blocks = refs[:count]
    weight, q_gain, k_gain = refs[count : count + 3]
    q_out, kv_out, rows_in, weight_in, gain_in, q_held, kv_held, arrive, leave = refs[-9:]
    first = place[0]
    second = place[1]
    first_step = place[2]
    second_step = place[3]

    copies = [
        pltpu.make_async_copy(weight, weight_in, arrive.at[count]),
        pltpu.make_async_copy(q_gain, gain_in.at[0], arrive.at[count + 1]),
        pltpu.make_async_copy(k_gain, gain_in.at[1], arrive.at[count + 2]),
    ]
    targets = []
    row = 0
    for at, (shift, pieces) in enumerate(shares):
        here = rows_in.at[pl.ds(row, len(pieces) * PIECE), :]
        copies.append(pltpu.make_async_copy(blocks[at], here, arrive.at[at]))
        for piece in pieces:
            spot = ((first + piece) % 4) * first_step + ((second + shift) % 4) * second_step
            target = pl.ds(pl.multiple_of(spot * PIECE, PIECE), PIECE)
            targets.append((pl.ds(row, PIECE), target))
            row += PIECE
    for copy in copies:
        copy.start()
    for copy in copies:
        copy.wait()

    def normalize(values, gain):
        mean_square = jnp.mean(values * values, axis=-1, keepdims=True)
        return (values * lax.rsqrt(mean_square + 1e-06) * gain).astype(jnp.bfloat16)

    whole = jnp.concatenate([weight_in[at] for at in range(3)], axis=1)
    proj = jnp.dot(rows_in[...], whole, preferred_element_type=jnp.float32)
    q_held[...] = normalize(proj[:, :HEAD], gain_in[0])
    kv_held[:, :HEAD] = normalize(proj[:, HEAD : 2 * HEAD], gain_in[1])
    kv_held[:, HEAD:] = proj[:, 2 * HEAD :].astype(jnp.bfloat16)
    for source, target in targets:
        pltpu.make_async_copy(q_held.at[source, :], q_out.at[target, :], leave.at[0]).start()
        pltpu.make_async_copy(kv_held.at[source, :], kv_out.at[target, :], leave.at[1]).start()
    pltpu.make_async_copy(q_held, q_held, leave.at[0]).wait()
    pltpu.make_async_copy(kv_held, kv_held, leave.at[1]).wait()


def project(shares, blocks, weight, q_gain, k_gain, place, begun=()):
    rows = 16 * PIECE
    count = len(blocks)
    rows_here = sum(len(pieces) for _, pieces in shares) * PIECE
    width = blocks[0].shape[1]
    anywhere = pl.BlockSpec(memory_space=pl.ANY)
    return pl.pallas_call(
        functools.partial(project_kernel, shares),
        out_shape=(
            jax.ShapeDtypeStruct((rows, HEAD), jnp.bfloat16),
            jax.ShapeDtypeStruct((rows, 2 * HEAD), jnp.bfloat16),
        ),
        in_specs=[SMEM] + [anywhere] * (count + 3 + len(begun)),
        out_specs=(anywhere, anywhere),
        scratch_shapes=[
            pltpu.VMEM((rows_here, width), jnp.bfloat16),
            pltpu.VMEM((3, width, HEAD), jnp.bfloat16),
            pltpu.VMEM((2, 1, HEAD), jnp.float32),
            pltpu.VMEM((rows_here, HEAD), jnp.bfloat16),
            pltpu.VMEM((rows_here, 2 * HEAD), jnp.bfloat16),
            pltpu.SemaphoreType.DMA((count + 3,)),
            pltpu.SemaphoreType.DMA((2,)),
        ],
        input_output_aliases={count + 4: 0, count + 5: 1} if begun else {},
        compiler_params=pltpu.CompilerParams(vmem_limit_bytes=16 * 1024 * 1024),
        name="project",
    )(place, *blocks, weight, q_gain, k_gain, *begun)


def attend_kernel(scale, first_call, last_call, call, blocks, place, pairs, counts, q, *refs):
    pieces = refs[:blocks]
    kv = refs[-1]
    slots = pieces[0].shape[0]
    rows = q.shape[0]
    if last_call:
        sums_in, kept, given, sums = refs[blocks : blocks + 4]
    elif first_call:
        sums = refs[blocks]
    else:
        sums_in, sums = refs[blocks : blocks + 2]
    for at in range(blocks):
        kv[at * slots : (at + 1) * slots] = pieces[at][...]
    if first_call:
        sums[...] = jnp.zeros_like(sums)
    else:
        sums[...] = sums_in[...]
    ones = jnp.ones((TILE, HEAD), jnp.bfloat16)

    def turn(step, _):
        for at in range(UNROLL):
            pair = pairs[call, step * UNROLL + at]
            row = pair >> 7
            tile = pair & 127
            scores = lax.dot_general(
                q[jnp.minimum(row, rows - 1)],
                kv[tile, :, :HEAD],
                (((1,), (1,)), ((), ())),
                preferred_element_type=jnp.float32,
            )
            weights = jnp.exp2(scores * scale).astype(jnp.bfloat16)
            values = jnp.concatenate((kv[tile, :, HEAD:], ones), axis=1)
            sums[row] += jnp.dot(weights, values, preferred_element_type=jnp.float32)
        return 0

    lax.fori_loop(0, (counts[0, call] + UNROLL - 1) // UNROLL, turn, 0)
    if last_call:
        core = place[4]
        for at in range(slots):
            kept[at] = sums[core * slots + at]
            given[at] = sums[(1 - core) * slots + at]


def attend(call, calls, place, pairs, counts, q, pieces, sums=None):
    scale = HEAD ** (-0.5) * LOG2E
    first_call, last_call = call == 0, call == calls - 1
    blocks, slots, rows = len(pieces), pieces[0].shape[0], q.shape[0]
    whole = jax.ShapeDtypeStruct((rows + 1, TILE, 2 * HEAD), jnp.float32)
    half = jax.ShapeDtypeStruct((slots, TILE, 2 * HEAD), jnp.float32)
    scratch = [pltpu.VMEM((blocks * slots, TILE, 2 * HEAD), jnp.bfloat16)]
    if last_call:
        scratch.insert(0, pltpu.VMEM(whole.shape, whole.dtype))
    more = () if first_call else (sums,)
    return pl.pallas_call(
        functools.partial(attend_kernel, scale, first_call, last_call, call, blocks),
        out_shape=(half, half) if last_call else whole,
        in_specs=[SMEM] * 3 + [VMEM] * (1 + blocks + len(more)),
        out_specs=(VMEM, VMEM) if last_call else VMEM,
        scratch_shapes=scratch,
        input_output_aliases={} if first_call or last_call else {4 + blocks: 0},
        compiler_params=pltpu.CompilerParams(vmem_limit_bytes=16 * 1024 * 1024),
        cost_estimate=pl.CostEstimate(
            flops=blocks * 10**9, bytes_accessed=blocks * 10**6, transcendentals=0
        ),
        name="attend",
    )(place, pairs, counts, q, *pieces, *more)


def list_kernel(slots, calls, place, tiles, counts, pairs_out, counts_out):
    core = place[4]
    plane = place[5]
    listed, rows = tiles.shape
    room = pairs_out.shape[1]
    tile = tiles[...]
    bal = (tile * (65536 // slots + 1)) >> 16
    away = (((bal >> 1) - plane) * (2 * core - 1)) & (PLANES - 1)
    same = (bal & 1) == core
    entry = lax.broadcasted_iota(jnp.int32, (listed, rows), 0)
    column = lax.broadcasted_iota(jnp.int32, (listed, rows), 1)
    least = jnp.where(same, 0, 1)
    most = PLANES // 2 - 1 + core
    inside = (away >= least) & (away <= most) & (entry < counts[...])
    down = lax.broadcasted_iota(jnp.int32, (listed, listed), 0)
    along = lax.broadcasted_iota(jnp.int32, (listed, listed), 1)
    before = jnp.where(along < down, 1.0, 0.0)
    down = lax.broadcasted_iota(jnp.int32, (rows, rows), 0)
    along = lax.broadcasted_iota(jnp.int32, (rows, rows), 1)
    ahead = jnp.where(down < along, 1.0, 0.0)
    spot = lax.broadcasted_iota(jnp.int32, (listed, room), 1)
    nothing = rows * TILE
    totals = []
    for call, (start, stop) in enumerate(calls):
        here = inside & (away >= start) & (away < stop)
        held = jnp.where(here, 1.0, 0.0)
        total = jnp.sum(held, axis=0, keepdims=True)
        order = jnp.dot(before, held, preferred_element_type=jnp.float32)
        order = order + jnp.dot(
            jnp.broadcast_to(total, (8, rows)), ahead, preferred_element_type=jnp.float32
        )[:1]
        order = jnp.where(held > 0.0, order, -1.0).astype(jnp.int32)
        skip = stop - start - max(start, 1)
        block = jnp.where(same, away - start, away + skip)
        pair = column * TILE + block * slots + tile - bal * slots - nothing
        placed = jnp.zeros((1, room), jnp.int32)
        for row in range(rows):
            hit = order[:, row : row + 1] == spot
            placed += jnp.sum(jnp.where(hit, pair[:, row : row + 1], 0), axis=0, keepdims=True)
        pairs_out[call : call + 1, :] = placed + nothing
        totals.append(jnp.sum(total, axis=1, keepdims=True).astype(jnp.int32))
    counts_out[...] = jnp.concatenate(totals, axis=1)


def list_pairs(calls, key_tiles, key_counts, place, slots):
    rows = 2 * slots
    tiles = lax.dynamic_slice_in_dim(key_tiles.T, place[5] * rows, rows, 1)
    counts = lax.dynamic_slice_in_dim(key_counts, place[5] * rows, rows, 1)
    most = max(2 * stop - start - max(start, 1) for start, stop in calls) * slots
    room = -(-rows * most // TILE) * TILE
    return pl.pallas_call(
        functools.partial(list_kernel, slots, calls),
        out_shape=(
            jax.ShapeDtypeStruct((len(calls), room), jnp.int32),
            jax.ShapeDtypeStruct((1, len(calls)), jnp.int32),
        ),
        in_specs=[SMEM, VMEM, VMEM],
        out_specs=(VMEM, VMEM),
        compiler_params=pltpu.CompilerParams(vmem_limit_bytes=4 * 1024 * 1024),
        name="lists",
    )(place, tiles, counts)


def on_device(tokens, qkv_weight, q_gain, k_gain, key_tiles, key_counts):
    me_seq = lax.axis_index("seq")
    me_bal = lax.axis_index("bal")
    y, x = me_seq // 4, me_seq % 4
    core = me_bal % 2
    place = jnp.stack(
        (
            jnp.where(core == 0, x, y),
            jnp.where(core == 0, y, x),
            jnp.where(core == 0, 1, 4),
            jnp.where(core == 0, 4, 1),
            core,
            me_bal // 2,
        )
    ).astype(jnp.int32)
    slots = 16 * PIECE // TILE
    pairs, counts = list_pairs(CALLS, key_tiles[0], key_counts, place, slots)

    before = send(tokens, 1, 1)
    after = send(tokens, 1, -1)
    across = send(tokens, 1, 2)
    low = jnp.concatenate((tokens, before), axis=0)
    before_low = send(low, 2, 1)
    high = jnp.concatenate((after, across), axis=0)
    after_high = send(high, 2, -1)
    after_low = send(low, 2, -1)
    before_high = send(high, 2, 1)
    across_low = send(before_low, 2, 1)
    across_high = send(after_high, 2, -1)

    weight = jnp.transpose(qkv_weight[:, 0], (1, 0, 2))
    low_pieces, high_pieces = (0, 3), (1, 2)
    begun = project(
        ((0, (0,)), (0, (3,)), (0, (1,)), (0, (2,)), (3, low_pieces), (1, high_pieces)),
        (tokens, before, after, across, before_low, after_high),
        weight,
        q_gain,
        k_gain,
        place,
    )
    begun = project(
        ((1, low_pieces), (3, high_pieces)),
        (after_low, before_high),
        weight,
        q_gain,
        k_gain,
        place,
        begun,
    )
    queries, keys_values = project(
        ((2, low_pieces), (2, high_pieces)),
        (across_low, across_high),
        weight,
        q_gain,
        k_gain,
        place,
        begun,
    )
    def tiles(block):
        return block.reshape(-1, TILE, block.shape[1])

    same, other, sums = [keys_values], [swap_cores(keys_values)], None
    for step in range(1, PLANES // 2 + 1):
        cores = (0, 1) if step < PLANES // 2 else (1,)
        same.append(pass_on(same[-1], cores))
        other.append(pass_on(other[-1], cores))
        if sums is not None:
            same[-1], sums = lax.optimization_barrier((same[-1], sums))
        if step == 1:
            queries, other[1] = lax.optimization_barrier((queries, other[1]))
            other_queries = swap_cores(queries)
        if step == 2:
            low_queries = jnp.where(core == 0, queries, other_queries)
            high_queries = jnp.where(core == 0, other_queries, queries)
            chip_queries = tiles(jnp.concatenate((low_queries, high_queries), axis=0))
            other[2], chip_queries = lax.optimization_barrier((other[2], chip_queries))
        call = step - CALLS[0][1] + 1
        if call >= 0:
            start, stop = CALLS[call]
            blocks = [tiles(block) for block in same[start:stop] + other[max(start, 1) : stop]]
            sums = attend(call, len(CALLS), place, pairs, counts, chip_queries, blocks, sums)
    kept, given = sums
    sums = kept + swap_cores(given)
    result = (sums[:, :, :HEAD] / sums[:, :, HEAD:]).astype(jnp.bfloat16)
    return lax.all_to_all(
        result.reshape(slots * TILE, HEAD), "seq", split_axis=0, concat_axis=1, tiled=True
    )


def solution(mesh):
    placed = (
        P(("bal", "seq"), None),
        P(None, "seq", None, None),
        P("seq", None),
        P("seq", None),
        P("seq", None, None),
        P("seq", None),
    )
    return jax.shard_map(
        on_device, mesh=mesh, in_specs=placed, out_specs=P(("bal", "seq"), None), check_vma=False
    )
```

time: 186 us -> 184 us (0.989)
  Pallas kernels: 24.2 us -> 41.9 us
  starting transfers between devices: 120 us -> 104 us
  local copies, waits for them, and re-layouts: 11.8 us -> 7.84 us
  blocking collectives: 13.8 us -> 16.5 us
  waiting for transfers between devices: 14.2 us -> 12.1 us
    pallas_call x2 -> x8, Pallas kernels: 13.7 us -> 31.5 us  [the longest x7 28.8 us: attend(): pl.pallas_call(functools.partial(attend_kernel, scale, first_call, last_c...]
    ppermute x3, starting transfers between devices: 23.2 us -> 10.3 us  [swap_cores(): return lax.ppermute(block, 'bal', [(at, at ^ 1) for at in range(32)])]
    unnamed x28 -> x22, local copies, waits for them, and re-layouts: 9.43 us -> 5.34 us
    ppermute x15 -> x16, waiting for transfers between devices: 10.5 us -> 6.93 us  [pass_on(): return lax.ppermute(block, 'bal', pairs)]
    all_to_all x1, blocking collectives: 13.8 us -> 16.5 us  [on_device(): lax.all_to_all(result.reshape(slots * TILE, HEAD), 'seq', split_axis=0, c...]
    ppermute x9, starting transfers between devices: 30.7 us -> 28.5 us  [send(): return lax.ppermute(block, MESH_AXES, plane_perm(phase, shift))]
    ppermute x15 -> x16, starting transfers between devices: 66.2 us -> 64.9 us  [pass_on(): return lax.ppermute(block, 'bal', pairs)]
  transfers between devices with their start and end apart: 27 -> 28, of which waited for: 8 -> 10; matrix products, arithmetic and copies ran while one was open for 2% -> 2% of each run, Pallas kernels for 4% -> 19%
where the time goes in v7:
time: 184 us; the launch traced here: 183 us
  starting transfers between devices  104 us (57%)
  Pallas kernels  41.9 us (23%)
  blocking collectives  16.5 us (9%)
  waiting for transfers between devices  12.1 us (7%)
  local copies, waits for them, and re-layouts  7.84 us (4%)
    ppermute x16, starting transfers between devices, pass_on(): return lax.ppermute(block, 'bal', pairs)  64.9 us
    pallas_call x7, Pallas kernels, attend(): pl.pallas_call(functools.partial(attend_kernel, scale, first_call, last_c...  28.8 us
    ppermute x9, starting transfers between devices, send(): return lax.ppermute(block, MESH_AXES, plane_perm(phase, shift))  28.5 us
    all_to_all x1, blocking collectives, on_device(): lax.all_to_all(result.reshape(slots * TILE, HEAD), 'seq', split_axis=0, c...  16.5 us
    pallas_call x3, Pallas kernels, project(): pl.pallas_call(functools.partial(project_kernel, shares), out_shape=(jax....  10.4 us
    ppermute x3, starting transfers between devices, swap_cores(): return lax.ppermute(block, 'bal', [(at, at ^ 1) for at in range(32)])  10.3 us
    ppermute x16, waiting for transfers between devices, pass_on(): return lax.ppermute(block, 'bal', pairs)  6.93 us
    unnamed x22, local copies, waits for them, and re-layouts  5.34 us
  transfers between devices with their start and end apart: 28, of which 10 were waited for; matrix products, arithmetic and copies ran while one was open for 2% of the time, Pallas kernels for 19%

profile of v7, /device:TPU:1, one launch (start us, length us, event | category | flops | bytes accessed | tf_op | source)
XLA Modules:
  0.0 182.9 jit_solution(12125286614583700187)
XLA Ops:
  0.0 5.6 %collective-permute-start.3 = (bf16[48,3072]{1,0:T(8,128)(2,1)}, bf16[48,3072]{1,0:T(8,128)(2,1)S(1)}, u32[]{:S(2)}, u32[]{:S(2)}) collective-permute-start(bf16[48,3072]{1,0:T(8,128)(2,1)} %refs_0_.1), channel_id=1, source_target_pairs={{0,96},{32,0},{64,32},{96,64},{128,224},{160,128},{192,160},{224,1... | collective-permute-start | bytes 884744 | tf_op jit(solution)/shard_map/ppermute | solution.py:34
  5.6 2.3 %collective-permute-start.4 = (bf16[48,3072]{1,0:T(8,128)(2,1)}, bf16[48,3072]{1,0:T(8,128)(2,1)S(1)}, u32[]{:S(2)}, u32[]{:S(2)}) collective-permute-start(bf16[48,3072]{1,0:T(8,128)(2,1)} %refs_0_.1), channel_id=1, source_target_pairs={{0,64},{32,96},{64,0},{96,32},{128,192},{160,224},{192,128},{224,1... | collective-permute-start | bytes 884744 | tf_op jit(solution)/shard_map/ppermute | solution.py:34
  7.9 2.6 %collective-permute-start = (bf16[48,3072]{1,0:T(8,128)(2,1)}, bf16[48,3072]{1,0:T(8,128)(2,1)S(1)}, u32[]{:S(2)}, u32[]{:S(2)}) collective-permute-start(bf16[48,3072]{1,0:T(8,128)(2,1)} %refs_0_.1), channel_id=1, source_target_pairs={{0,32},{32,64},{64,96},{96,0},{128,160},{160,192},{192,224},{224,1... | collective-permute-start | bytes 884744 | tf_op jit(solution)/shard_map/ppermute | solution.py:34
  10.5 1.7 constant_dynamic-update-slice_fusion.1
  12.2 0.6 collective-permute-done.3.refs_2_
  12.8 0.7 constant_dynamic-update-slice_fusion.3
  13.5 1.4 collective-permute-done.4.refs_3_
  14.9 0.8 constant_dynamic-update-slice_fusion.2
  15.7 4.4 %collective-permute-start.5 = (bf16[96,3072]{1,0:T(8,128)(2,1)}, bf16[96,3072]{1,0:T(8,128)(2,1)}, u32[]{:S(2)}, u32[]{:S(2)}) collective-permute-start(bf16[96,3072]{1,0:T(8,128)(2,1)} %constant_dynamic-update-slice_fusion.2), channel_id=1, source_target_pairs={{0,384},{32,416},{64,448},{96,480},{128,0},{160,32},{192,64},{224,... | collective-permute-start | bytes 1769480 | tf_op jit(solution)/shard_map/ppermute | solution.py:34
  20.1 0.8 constant_dynamic-update-slice_fusion
  20.9 1.9 %collective-permute-start.1 = (bf16[96,3072]{1,0:T(8,128)(2,1)}, bf16[96,3072]{1,0:T(8,128)(2,1)}, u32[]{:S(2)}, u32[]{:S(2)}) collective-permute-start(bf16[96,3072]{1,0:T(8,128)(2,1)} %constant_dynamic-update-slice_fusion), channel_id=1, source_target_pairs={{0,128},{32,160},{64,192},{96,224},{128,256},{160,288},{192,320},{... | collective-permute-start | bytes 1769480 | tf_op jit(solution)/shard_map/ppermute | solution.py:34
  22.8 2.2 %collective-permute-start.8 = (bf16[96,3072]{1,0:T(8,128)(2,1)}, bf16[96,3072]{1,0:T(8,128)(2,1)}, u32[]{:S(2)}, u32[]{:S(2)}) collective-permute-start(bf16[96,3072]{1,0:T(8,128)(2,1)} %constant_dynamic-update-slice_fusion.2), channel_id=1, source_target_pairs={{0,128},{32,160},{64,192},{96,224},{128,256},{160,288},{192,320},{... | collective-permute-start | bytes 1769480 | tf_op jit(solution)/shard_map/ppermute | solution.py:34
  25.0 4.3 %collective-permute-start.7 = (bf16[96,3072]{1,0:T(8,128)(2,1)}, bf16[96,3072]{1,0:T(8,128)(2,1)}, u32[]{:S(2)}, u32[]{:S(2)}) collective-permute-start(bf16[96,3072]{1,0:T(8,128)(2,1)} %constant_dynamic-update-slice_fusion), channel_id=1, source_target_pairs={{0,384},{32,416},{64,448},{96,480},{128,0},{160,32},{192,64},{224,... | collective-permute-start | bytes 1769480 | tf_op jit(solution)/shard_map/ppermute | solution.py:34
  29.3 3.4 %collective-permute-start.6 = (bf16[96,3072]{1,0:T(8,128)(2,1)}, bf16[96,3072]{1,0:T(8,128)(2,1)}, u32[]{:S(2)}, u32[]{:S(2)}) collective-permute-start(bf16[96,3072]{1,0:T(8,128)(2,1)} %collective-permute-done.5.refs_5_), channel_id=1, source_target_pairs={{0,384},{32,416},{64,448},{96,480},{128,0},{160,32},{192,64},{224,... | collective-permute-start | bytes 1769480 | tf_op jit(solution)/shard_map/ppermute | solution.py:34
  32.7 0.6 collective-permute-done.1.refs_4_
  33.3 1.9 %collective-permute-start.2 = (bf16[96,3072]{1,0:T(8,128)(2,1)}, bf16[96,3072]{1,0:T(8,128)(2,1)}, u32[]{:S(2)}, u32[]{:S(2)}) collective-permute-start(bf16[96,3072]{1,0:T(8,128)(2,1)} %collective-permute-done.1.refs_4_), channel_id=1, source_target_pairs={{0,128},{32,160},{64,192},{96,224},{128,256},{160,288},{192,320},{... | collective-permute-start | bytes 1769480 | tf_op jit(solution)/shard_map/ppermute | solution.py:34
  35.3 0.1 stack.27.place
  35.4 0.0 copy-start.2
  35.4 1.0 copy-done.2
  36.4 1.0 copy-done.4
  37.3 1.0 copy-done.6
  38.3 4.2 %project.3 = (bf16[768,128]{1,0:T(8,128)(2,1)S(1)}, bf16[768,256]{1,0:T(8,128)(2,1)S(1)}) custom-call(s32[6]{0:T(128)S(1)} %stack.27.place, bf16[48,3072]{1,0:T(8,128)(2,1)S(1)} %copy-done.2, bf16[48,3072]{1,0:T(8,128)(2,1)S(1)} %copy-done.6, bf16[48,3072]{1,0:T(8,128)(2,1)S(1)} %collective-permute-done.3.refs_2_, bf16[48,3072]{1,0:T(8,128)(2,1)S(1)} %copy-done.4, ...), custom_call_target="tpu_custom_call" | custom-call | tf_op jit(solution)/shard_map/project/pallas_call | solution.py:103
  42.5 3.1 %project.4 = (bf16[768,128]{1,0:T(8,128)(2,1)S(1)}, bf16[768,256]{1,0:T(8,128)(2,1)S(1)}) custom-call(s32[6]{0:T(128)S(1)} %stack.27.place, bf16[96,3072]{1,0:T(8,128)(2,1)} %collective-permute-done.7.refs_0_, bf16[96,3072]{1,0:T(8,128)(2,1)} %collective-permute-done.8.refs_1_, ...), custom_call_target="tpu_custom_call", output_to_operand_aliasing={{0}: (6, {}), {1}: (7, {})} | custom-call | tf_op jit(solution)/shard_map/project/pallas_call | solution.py:103
  45.6 0.3 collective-permute-done.2.refs_0_
  46.0 3.1 %project.5 = (bf16[768,128]{1,0:T(8,128)(2,1)S(1)}, bf16[768,256]{1,0:T(8,128)(2,1)S(1)}) custom-call(s32[6]{0:T(128)S(1)} %stack.27.place, bf16[96,3072]{1,0:T(8,128)(2,1)} %collective-permute-done.2.refs_0_, bf16[96,3072]{1,0:T(8,128)(2,1)} %collective-permute-done.6.refs_1_, ...), custom_call_target="tpu_custom_call", output_to_operand_aliasing={{0}: (6, {}), {1}: (7, {})} | custom-call | tf_op jit(solution)/shard_map/project/pallas_call | solution.py:103
  49.1 6.0 %collective-permute-start.9 = (bf16[768,256]{1,0:T(8,128)(2,1)S(1)}, bf16[768,256]{1,0:T(8,128)(2,1)S(1)}, u32[]{:S(2)}, u32[]{:S(2)}) collective-permute-start(bf16[768,256]{1,0:T(8,128)(2,1)S(1)} %get-tuple-element.38), channel_id=1, source_target_pairs={{0,1},{1,0},{2,3},{3,2},{4,5},{5,4},{6,7},{7,6},{8,9},{9,8},{10,11... | collective-permute-start | bytes 1179656 | tf_op jit(solution)/shard_map/ppermute | solution.py:38
  55.1 10.9 %collective-permute-start.13 = (bf16[768,256]{1,0:T(8,128)(2,1)S(1)}, bf16[768,256]{1,0:T(8,128)(2,1)S(1)}, u32[]{:S(2)}, u32[]{:S(2)}) collective-permute-start(bf16[768,256]{1,0:T(8,128)(2,1)S(1)} %get-tuple-element.38), channel_id=1, source_target_pairs={{0,2},{1,31},{2,4},{3,1},{4,6},{5,3},{6,8},{7,5},{8,10},{9,7},{10,... | collective-permute-start | bytes 1179656 | tf_op jit(solution)/shard_map/ppermute | solution.py:48
  66.0 2.6 %collective-permute-start.10 = (bf16[768,256]{1,0:T(8,128)(2,1)S(1)}, bf16[768,256]{1,0:T(8,128)(2,1)S(1)}, u32[]{:S(2)}, u32[]{:S(2)}) collective-permute-start(bf16[768,256]{1,0:T(8,128)(2,1)S(1)} %collective-permute-done.9), channel_id=1, source_target_pairs={{0,2},{1,31},{2,4},{3,1},{4,6},{5,3},{6,8},{7,5},{8,10},{9,7},{10,... | collective-permute-start | bytes 1179656 | tf_op jit(solution)/shard_map/ppermute | solution.py:48
  68.6 2.0 %collective-permute-done.13 = bf16[768,256]{1,0:T(8,128)(2,1)S(1)} collective-permute-done((bf16[768,256]{1,0:T(8,128)(2,1)S(1)}, bf16[768,256]{1,0:T(8,128)(2,1)S(1)}, u32[]{:S(2)}, u32[]{:S(2)}) %collective-permute-start.13) | collective-permute-done | bytes 393248 | tf_op jit(solution)/shard_map/ppermute | solution.py:48
  70.7 5.0 %collective-permute-start.14 = (bf16[768,256]{1,0:T(8,128)(2,1)S(1)}, bf16[768,256]{1,0:T(8,128)(2,1)S(1)}, u32[]{:S(2)}, u32[]{:S(2)}) collective-permute-start(bf16[768,256]{1,0:T(8,128)(2,1)S(1)} %collective-permute-done.13), channel_id=1, source_target_pairs={{0,2},{1,31},{2,4},{3,1},{4,6},{5,3},{6,8},{7,5},{8,10},{9,7},{10,... | collective-permute-start | bytes 1179656 | tf_op jit(solution)/shard_map/ppermute | solution.py:48
  75.7 2.4 %collective-permute-start.12 = (bf16[768,128]{1,0:T(8,128)(2,1)S(1)}, bf16[768,128]{1,0:T(8,128)(2,1)S(1)}, u32[]{:S(2)}, u32[]{:S(2)}) collective-permute-start(bf16[768,128]{1,0:T(8,128)(2,1)S(1)} %get-tuple-element.40), channel_id=1, source_target_pairs={{0,1},{1,0},{2,3},{3,2},{4,5},{5,4},{6,7},{7,6},{8,9},{9,8},{10,11... | collective-permute-start | bytes 589832 | tf_op jit(solution)/shard_map/ppermute | solution.py:38
  78.1 0.1 constant_dynamic-slice_fusion.counts
  78.2 0.1 dynamic-slice_bitcast_fusion.tiles
  78.3 2.8 %lists.1 = (s32[7,384]{1,0:T(8,128)S(1)}, s32[1,7]{1,0:T(1,128)S(1)}) custom-call(s32[6]{0:T(128)S(1)} %stack.27.place, s32[64,12]{1,0:T(8,128)S(1)} %dynamic-slice_bitcast_fusion.tiles, s32[1,12]{1,0:T(1,128)S(1)} %constant_dynamic-slice_fusion.counts), custom_call_target="tpu_custom_call" | custom-call | tf_op jit(solution)/shard_map/lists/pallas_call | solution.py:244
  81.1 3.7 %collective-permute-start.11 = (bf16[768,256]{1,0:T(8,128)(2,1)S(1)}, bf16[768,256]{1,0:T(8,128)(2,1)S(1)}, u32[]{:S(2)}, u32[]{:S(2)}) collective-permute-start(bf16[768,256]{1,0:T(8,128)(2,1)S(1)} %collective-permute-done.10), channel_id=1, source_target_pairs={{0,2},{1,31},{2,4},{3,1},{4,6},{5,3},{6,8},{7,5},{8,10},{9,7},{10,... | collective-permute-start | bytes 1179656 | tf_op jit(solution)/shard_map/ppermute | solution.py:48
  84.8 2.6 %collective-permute-start.15 = (bf16[768,256]{1,0:T(8,128)(2,1)S(1)}, bf16[768,256]{1,0:T(8,128)(2,1)S(1)}, u32[]{:S(2)}, u32[]{:S(2)}) collective-permute-start(bf16[768,256]{1,0:T(8,128)(2,1)S(1)} %collective-permute-done.14), channel_id=1, source_target_pairs={{0,2},{1,31},{2,4},{3,1},{4,6},{5,3},{6,8},{7,5},{8,10},{9,7},{10,... | collective-permute-start | bytes 1179656 | tf_op jit(solution)/shard_map/ppermute | solution.py:48
  87.4 2.4 %collective-permute-done.11 = bf16[768,256]{1,0:T(8,128)(2,1)S(1)} collective-permute-done((bf16[768,256]{1,0:T(8,128)(2,1)S(1)}, bf16[768,256]{1,0:T(8,128)(2,1)S(1)}, u32[]{:S(2)}, u32[]{:S(2)}) %collective-permute-start.11) | collective-permute-done | bytes 393248 | tf_op jit(solution)/shard_map/ppermute | solution.py:48
  89.9 4.6 %collective-permute-start.17 = (bf16[768,256]{1,0:T(8,128)(2,1)S(1)}, bf16[768,256]{1,0:T(8,128)(2,1)S(1)}, u32[]{:S(2)}, u32[]{:S(2)}) collective-permute-start(bf16[768,256]{1,0:T(8,128)(2,1)S(1)} %collective-permute-done.11), channel_id=1, source_target_pairs={{0,2},{1,31},{2,4},{3,1},{4,6},{5,3},{6,8},{7,5},{8,10},{9,7},{10,... | collective-permute-start | bytes 1179656 | tf_op jit(solution)/shard_map/ppermute | solution.py:48
  94.5 6.4 %attend.7.refs_2_ = f32[13,128,256]{2,1,0:T(8,128)S(1)} custom-call(s32[6]{0:T(128)S(1)} %stack.27.place, s32[7,384]{1,0:T(8,128)S(1)} %get-tuple-element.31.pairs, s32[1,7]{1,0:T(1,128)S(1)} %get-tuple-element.32.counts, bf16[12,128,128]{2,1,0:T(8,128)(2,1)S(1)} %bitcast.42, bf16[6,128,256]{2,1,0:T(8,128)(2,1)S(1)} %bitcast.41, ...), custom_call_target="tpu_custom_call" | custom-call | flops 5000000000 | bytes 5000000 | tf_op jit(solution)/shard_map/attend/pallas_call | solution.py:179
  100.9 1.9 %collective-permute-start.16 = (bf16[768,256]{1,0:T(8,128)(2,1)S(1)}, bf16[768,256]{1,0:T(8,128)(2,1)S(1)}, u32[]{:S(2)}, u32[]{:S(2)}) collective-permute-start(bf16[768,256]{1,0:T(8,128)(2,1)S(1)} %collective-permute-done.15), channel_id=1, source_target_pairs={{0,2},{1,31},{2,4},{3,1},{4,6},{5,3},{6,8},{7,5},{8,10},{9,7},{10,... | collective-permute-start | bytes 1179656 | tf_op jit(solution)/shard_map/ppermute | solution.py:48
  102.8 6.2 %collective-permute-start.19 = (bf16[768,256]{1,0:T(8,128)(2,1)S(1)}, bf16[768,256]{1,0:T(8,128)(2,1)S(1)}, u32[]{:S(2)}, u32[]{:S(2)}) collective-permute-start(bf16[768,256]{1,0:T(8,128)(2,1)S(1)} %collective-permute-done.17), channel_id=1, source_target_pairs={{0,2},{1,31},{2,4},{3,1},{4,6},{5,3},{6,8},{7,5},{8,10},{9,7},{10,... | collective-permute-start | bytes 1179656 | tf_op jit(solution)/shard_map/ppermute | solution.py:48
  109.1 2.6 %attend.8.refs_2_ = f32[13,128,256]{2,1,0:T(8,128)S(1)} custom-call(s32[6]{0:T(128)S(1)} %stack.27.place, s32[7,384]{1,0:T(8,128)S(1)} %get-tuple-element.31.pairs, s32[1,7]{1,0:T(1,128)S(1)} %get-tuple-element.32.counts, bf16[12,128,128]{2,1,0:T(8,128)(2,1)S(1)} %bitcast.43, bf16[6,128,256]{2,1,0:T(8,128)(2,1)S(1)} %bitcast.52, ...), custom_call_target="tpu_custom_call", output_to_operand_aliasing={{}: (6, {})} | custom-call | flops 2000000000 | bytes 2000000 | tf_op jit(solution)/shard_map/attend/pallas_call | solution.py:179
  111.7 3.5 %collective-permute-start.18 = (bf16[768,256]{1,0:T(8,128)(2,1)S(1)}, bf16[768,256]{1,0:T(8,128)(2,1)S(1)}, u32[]{:S(2)}, u32[]{:S(2)}) collective-permute-start(bf16[768,256]{1,0:T(8,128)(2,1)S(1)} %collective-permute-done.16), channel_id=1, source_target_pairs={{0,2},{1,31},{2,4},{3,1},{4,6},{5,3},{6,8},{7,5},{8,10},{9,7},{10,... | collective-permute-start | bytes 1179656 | tf_op jit(solution)/shard_map/ppermute | solution.py:48
  115.2 4.8 %collective-permute-start.21 = (bf16[768,256]{1,0:T(8,128)(2,1)S(1)}, bf16[768,256]{1,0:T(8,128)(2,1)S(1)}, u32[]{:S(2)}, u32[]{:S(2)}) collective-permute-start(bf16[768,256]{1,0:T(8,128)(2,1)S(1)} %collective-permute-done.19), channel_id=1, source_target_pairs={{0,2},{1,31},{2,4},{3,1},{4,6},{5,3},{6,8},{7,5},{8,10},{9,7},{10,... | collective-permute-start | bytes 1179656 | tf_op jit(solution)/shard_map/ppermute | solution.py:48
  119.9 5.7 %attend.9.refs_2_ = f32[13,128,256]{2,1,0:T(8,128)S(1)} custom-call(s32[6]{0:T(128)S(1)} %stack.27.place, s32[7,384]{1,0:T(8,128)S(1)} %get-tuple-element.31.pairs, s32[1,7]{1,0:T(1,128)S(1)} %get-tuple-element.32.counts, bf16[12,128,128]{2,1,0:T(8,128)(2,1)S(1)} %bitcast.44, bf16[6,128,256]{2,1,0:T(8,128)(2,1)S(1)} %bitcast.55, ...), custom_call_target="tpu_custom_call", output_to_operand_aliasing={{}: (6, {})} | custom-call | flops 2000000000 | bytes 2000000 | tf_op jit(solution)/shard_map/attend/pallas_call | solution.py:179
  125.6 1.9 %collective-permute-start.20 = (bf16[768,256]{1,0:T(8,128)(2,1)S(1)}, bf16[768,256]{1,0:T(8,128)(2,1)S(1)}, u32[]{:S(2)}, u32[]{:S(2)}) collective-permute-start(bf16[768,256]{1,0:T(8,128)(2,1)S(1)} %collective-permute-done.18), channel_id=1, source_target_pairs={{0,2},{1,31},{2,4},{3,1},{4,6},{5,3},{6,8},{7,5},{8,10},{9,7},{10,... | collective-permute-start | bytes 1179656 | tf_op jit(solution)/shard_map/ppermute | solution.py:48
  127.6 2.2 %collective-permute-start.23 = (bf16[768,256]{1,0:T(8,128)(2,1)S(1)}, bf16[768,256]{1,0:T(8,128)(2,1)S(1)}, u32[]{:S(2)}, u32[]{:S(2)}) collective-permute-start(bf16[768,256]{1,0:T(8,128)(2,1)S(1)} %collective-permute-done.21), channel_id=1, source_target_pairs={{0,2},{1,31},{2,4},{3,1},{4,6},{5,3},{6,8},{7,5},{8,10},{9,7},{10,... | collective-permute-start | bytes 1179656 | tf_op jit(solution)/shard_map/ppermute | solution.py:48
  129.7 3.3 %attend.10.refs_2_ = f32[13,128,256]{2,1,0:T(8,128)S(1)} custom-call(s32[6]{0:T(128)S(1)} %stack.27.place, s32[7,384]{1,0:T(8,128)S(1)} %get-tuple-element.31.pairs, s32[1,7]{1,0:T(1,128)S(1)} %get-tuple-element.32.counts, bf16[12,128,128]{2,1,0:T(8,128)(2,1)S(1)} %bitcast.45, bf16[6,128,256]{2,1,0:T(8,128)(2,1)S(1)} %bitcast.57, ...), custom_call_target="tpu_custom_call", output_to_operand_aliasing={{}: (6, {})} | custom-call | flops 2000000000 | bytes 2000000 | tf_op jit(solution)/shard_map/attend/pallas_call | solution.py:179
  133.1 1.4 collective-permute-done.20
  134.4 3.4 %collective-permute-start.22 = (bf16[768,256]{1,0:T(8,128)(2,1)S(1)}, bf16[768,256]{1,0:T(8,128)(2,1)S(1)}, u32[]{:S(2)}, u32[]{:S(2)}) collective-permute-start(bf16[768,256]{1,0:T(8,128)(2,1)S(1)} %collective-permute-done.20), channel_id=1, source_target_pairs={{0,2},{1,31},{2,4},{3,1},{4,6},{5,3},{6,8},{7,5},{8,10},{9,7},{10,... | collective-permute-start | bytes 1179656 | tf_op jit(solution)/shard_map/ppermute | solution.py:48
  137.9 0.5 collective-permute-done.23
  138.4 3.1 %collective-permute-start.25 = (bf16[768,256]{1,0:T(8,128)(2,1)S(1)}, bf16[768,256]{1,0:T(8,128)(2,1)S(1)}, u32[]{:S(2)}, u32[]{:S(2)}) collective-permute-start(bf16[768,256]{1,0:T(8,128)(2,1)S(1)} %collective-permute-done.23), channel_id=1, source_target_pairs={{0,2},{1,31},{2,4},{3,1},{4,6},{5,3},{6,8},{7,5},{8,10},{9,7},{10,... | collective-permute-start | bytes 1179656 | tf_op jit(solution)/shard_map/ppermute | solution.py:48
  141.5 3.3 %attend.11.refs_2_ = f32[13,128,256]{2,1,0:T(8,128)S(1)} custom-call(s32[6]{0:T(128)S(1)} %stack.27.place, s32[7,384]{1,0:T(8,128)S(1)} %get-tuple-element.31.pairs, s32[1,7]{1,0:T(1,128)S(1)} %get-tuple-element.32.counts, bf16[12,128,128]{2,1,0:T(8,128)(2,1)S(1)} %bitcast.46, bf16[6,128,256]{2,1,0:T(8,128)(2,1)S(1)} %bitcast.59, ...), custom_call_target="tpu_custom_call", output_to_operand_aliasing={{}: (6, {})} | custom-call | flops 2000000000 | bytes 2000000 | tf_op jit(solution)/shard_map/attend/pallas_call | solution.py:179
  144.9 3.5 %collective-permute-start.24 = (bf16[768,256]{1,0:T(8,128)(2,1)S(1)}, bf16[768,256]{1,0:T(8,128)(2,1)S(1)}, u32[]{:S(2)}, u32[]{:S(2)}) collective-permute-start(bf16[768,256]{1,0:T(8,128)(2,1)S(1)} %collective-permute-done.22), channel_id=1, source_target_pairs={{1,31},{3,1},{5,3},{7,5},{9,7},{11,9},{13,11},{15,13},{17,15},{19,... | collective-permute-start | bytes 1179656 | tf_op jit(solution)/shard_map/ppermute | solution.py:48
  148.3 5.0 %collective-permute-start.26 = (bf16[768,256]{1,0:T(8,128)(2,1)S(1)}, bf16[768,256]{1,0:T(8,128)(2,1)S(1)}, u32[]{:S(2)}, u32[]{:S(2)}) collective-permute-start(bf16[768,256]{1,0:T(8,128)(2,1)S(1)} %collective-permute-done.25), channel_id=1, source_target_pairs={{1,31},{3,1},{5,3},{7,5},{9,7},{11,9},{13,11},{15,13},{17,15},{19,... | collective-permute-start | bytes 1179656 | tf_op jit(solution)/shard_map/ppermute | solution.py:48
  153.4 4.1 %attend.12.refs_2_ = f32[13,128,256]{2,1,0:T(8,128)S(1)} custom-call(s32[6]{0:T(128)S(1)} %stack.27.place, s32[7,384]{1,0:T(8,128)S(1)} %get-tuple-element.31.pairs, s32[1,7]{1,0:T(1,128)S(1)} %get-tuple-element.32.counts, bf16[12,128,128]{2,1,0:T(8,128)(2,1)S(1)} %bitcast.47, bf16[6,128,256]{2,1,0:T(8,128)(2,1)S(1)} %bitcast.61, ...), custom_call_target="tpu_custom_call", output_to_operand_aliasing={{}: (6, {})} | custom-call | flops 2000000000 | bytes 2000000 | tf_op jit(solution)/shard_map/attend/pallas_call | solution.py:179
  157.5 0.6 collective-permute-done.26
  158.1 3.3 %attend.13 = (f32[6,128,256]{2,1,0:T(8,128)S(1)}, f32[6,128,256]{2,1,0:T(8,128)S(1)}) custom-call(s32[6]{0:T(128)S(1)} %stack.27.place, s32[7,384]{1,0:T(8,128)S(1)} %get-tuple-element.31.pairs, s32[1,7]{1,0:T(1,128)S(1)} %get-tuple-element.32.counts, bf16[12,128,128]{2,1,0:T(8,128)(2,1)S(1)} %bitcast.48, bf16[6,128,256]{2,1,0:T(8,128)(2,1)S(1)} %bitcast.62, ...), custom_call_target="tpu_custom_call" | custom-call | flops 2000000000 | bytes 2000000 | tf_op jit(solution)/shard_map/attend/pallas_call | solution.py:179
  161.4 1.9 %collective-permute-start.27 = (f32[6,128,256]{2,1,0:T(8,128)S(1)}, f32[6,128,256]{2,1,0:T(8,128)S(1)}, u32[]{:S(2)}, u32[]{:S(2)}) collective-permute-start(f32[6,128,256]{2,1,0:T(8,128)S(1)} %get-tuple-element.56), channel_id=1, source_target_pairs={{0,1},{1,0},{2,3},{3,2},{4,5},{5,4},{6,7},{7,6},{8,9},{9,8},{10,11... | collective-permute-start | bytes 2359304 | tf_op jit(solution)/shard_map/ppermute | solution.py:38
  163.3 2.3 %collective-permute-done.27 = f32[6,128,256]{2,1,0:T(8,128)S(1)} collective-permute-done((f32[6,128,256]{2,1,0:T(8,128)S(1)}, f32[6,128,256]{2,1,0:T(8,128)S(1)}, u32[]{:S(2)}, u32[]{:S(2)}) %collective-permute-start.27) | collective-permute-done | bytes 786464 | tf_op jit(solution)/shard_map/ppermute | solution.py:38
  165.6 0.1 add.19
  165.7 0.1 fusion
  165.8 16.5 %all_to_all.19 = bf16[16,48,128]{2,1,0:T(8,128)(2,1)S(1)} all-to-all(bf16[16,48,128]{2,1,0:T(8,128)(2,1)S(1)} %bitcast.65), channel_id=1, replica_groups=mesh['seq'=16,'bal'=32] {'seq'}, dimensions={0} | all-to-all | bytes 393216 | tf_op jit(solution)/shard_map/all_to_all | solution.py:341
  182.2 0.7 copy_bitcast_fusion
  (36 shorter events, 0.1 us)
Async XLA Ops:
  0.0 78.2 %copy-start = (s32[1,192,64]{1,2,0:T(8,128)S(1)}, s32[1,192,64]{1,2,0:T(8,128)}, u32[]{:S(2)}) copy-start(s32[1,192,64]{1,2,0:T(8,128)} %param.10) | copy-start | bytes 147460
  0.0 35.4 %copy-start.1 = (bf16[3072,1,3,128]{3,0,2,1:T(8,128)(2,1)S(1)}, bf16[3072,1,3,128]{3,0,2,1:T(8,128)(2,1)}, u32[]{:S(2)}) copy-start(bf16[3072,1,3,128]{3,0,2,1:T(8,128)(2,1)} %param.7) | copy-start | bytes 7077892
  0.0 35.4 %copy-start.7 = (f32[1,128]{1,0:T(1,128)S(1)}, f32[1,128]{1,0:T(1,128)}, u32[]{:S(2)}) copy-start(f32[1,128]{1,0:T(1,128)} %refs_3_.3) | copy-start | bytes 1540
  0.0 35.4 %copy-start.8 = (f32[1,128]{1,0:T(1,128)S(1)}, f32[1,128]{1,0:T(1,128)}, u32[]{:S(2)}) copy-start(f32[1,128]{1,0:T(1,128)} %refs_4_.3) | copy-start | bytes 1540
  0.0 12.8 %collective-permute-start.3 = (bf16[48,3072]{1,0:T(8,128)(2,1)}, bf16[48,3072]{1,0:T(8,128)(2,1)S(1)}, u32[]{:S(2)}, u32[]{:S(2)}) collective-permute-start(bf16[48,3072]{1,0:T(8,128)(2,1)} %refs_0_.1), channel_id=1, source_target_pairs={{0,96},{32,0},{64,32},{96,64},{128,224},{160,128},{192,160},{224,1... | collective-permute-start | bytes 884744 | tf_op jit(solution)/shard_map/ppermute | solution.py:34
  5.6 9.3 %collective-permute-start.4 = (bf16[48,3072]{1,0:T(8,128)(2,1)}, bf16[48,3072]{1,0:T(8,128)(2,1)S(1)}, u32[]{:S(2)}, u32[]{:S(2)}) collective-permute-start(bf16[48,3072]{1,0:T(8,128)(2,1)} %refs_0_.1), channel_id=1, source_target_pairs={{0,64},{32,96},{64,0},{96,32},{128,192},{160,224},{192,128},{224,1... | collective-permute-start | bytes 884744 | tf_op jit(solution)/shard_map/ppermute | solution.py:34
  7.9 12.2 %collective-permute-start = (bf16[48,3072]{1,0:T(8,128)(2,1)}, bf16[48,3072]{1,0:T(8,128)(2,1)S(1)}, u32[]{:S(2)}, u32[]{:S(2)}) collective-permute-start(bf16[48,3072]{1,0:T(8,128)(2,1)} %refs_0_.1), channel_id=1, source_target_pairs={{0,32},{32,64},{64,96},{96,0},{128,160},{160,192},{192,224},{224,1... | collective-permute-start | bytes 884744 | tf_op jit(solution)/shard_map/ppermute | solution.py:34
  14.9 20.5 %copy-start.3 = (bf16[48,3072]{1,0:T(8,128)(2,1)}, bf16[48,3072]{1,0:T(8,128)(2,1)S(1)}, u32[]{:S(2)}) copy-start(bf16[48,3072]{1,0:T(8,128)(2,1)S(1)} %collective-permute-done.4.refs_3_) | copy-start | bytes 884740
  15.7 13.6 %collective-permute-start.5 = (bf16[96,3072]{1,0:T(8,128)(2,1)}, bf16[96,3072]{1,0:T(8,128)(2,1)}, u32[]{:S(2)}, u32[]{:S(2)}) collective-permute-start(bf16[96,3072]{1,0:T(8,128)(2,1)} %constant_dynamic-update-slice_fusion.2), channel_id=1, source_target_pairs={{0,384},{32,416},{64,448},{96,480},{128,0},{160,32},{192,64},{224,... | collective-permute-start | bytes 1769480 | tf_op jit(solution)/shard_map/ppermute | solution.py:34
  20.1 15.3 %copy-start.5 = (bf16[48,3072]{1,0:T(8,128)(2,1)}, bf16[48,3072]{1,0:T(8,128)(2,1)S(1)}, u32[]{:S(2)}) copy-start(bf16[48,3072]{1,0:T(8,128)(2,1)S(1)} %collective-permute-done.refs_1_) | copy-start | bytes 884740
  20.9 12.4 %collective-permute-start.1 = (bf16[96,3072]{1,0:T(8,128)(2,1)}, bf16[96,3072]{1,0:T(8,128)(2,1)}, u32[]{:S(2)}, u32[]{:S(2)}) collective-permute-start(bf16[96,3072]{1,0:T(8,128)(2,1)} %constant_dynamic-update-slice_fusion), channel_id=1, source_target_pairs={{0,128},{32,160},{64,192},{96,224},{128,256},{160,288},{192,320},{... | collective-permute-start | bytes 1769480 | tf_op jit(solution)/shard_map/ppermute | solution.py:34
  22.8 19.7 %collective-permute-start.8 = (bf16[96,3072]{1,0:T(8,128)(2,1)}, bf16[96,3072]{1,0:T(8,128)(2,1)}, u32[]{:S(2)}, u32[]{:S(2)}) collective-permute-start(bf16[96,3072]{1,0:T(8,128)(2,1)} %constant_dynamic-update-slice_fusion.2), channel_id=1, source_target_pairs={{0,128},{32,160},{64,192},{96,224},{128,256},{160,288},{192,320},{... | collective-permute-start | bytes 1769480 | tf_op jit(solution)/shard_map/ppermute | solution.py:34
  25.0 17.5 %collective-permute-start.7 = (bf16[96,3072]{1,0:T(8,128)(2,1)}, bf16[96,3072]{1,0:T(8,128)(2,1)}, u32[]{:S(2)}, u32[]{:S(2)}) collective-permute-start(bf16[96,3072]{1,0:T(8,128)(2,1)} %constant_dynamic-update-slice_fusion), channel_id=1, source_target_pairs={{0,384},{32,416},{64,448},{96,480},{128,0},{160,32},{192,64},{224,... | collective-permute-start | bytes 1769480 | tf_op jit(solution)/shard_map/ppermute | solution.py:34
  29.3 16.3 %collective-permute-start.6 = (bf16[96,3072]{1,0:T(8,128)(2,1)}, bf16[96,3072]{1,0:T(8,128)(2,1)}, u32[]{:S(2)}, u32[]{:S(2)}) collective-permute-start(bf16[96,3072]{1,0:T(8,128)(2,1)} %collective-permute-done.5.refs_5_), channel_id=1, source_target_pairs={{0,384},{32,416},{64,448},{96,480},{128,0},{160,32},{192,64},{224,... | collective-permute-start | bytes 1769480 | tf_op jit(solution)/shard_map/ppermute | solution.py:34
  33.3 12.6 %collective-permute-start.2 = (bf16[96,3072]{1,0:T(8,128)(2,1)}, bf16[96,3072]{1,0:T(8,128)(2,1)}, u32[]{:S(2)}, u32[]{:S(2)}) collective-permute-start(bf16[96,3072]{1,0:T(8,128)(2,1)} %collective-permute-done.1.refs_4_), channel_id=1, source_target_pairs={{0,128},{32,160},{64,192},{96,224},{128,256},{160,288},{192,320},{... | collective-permute-start | bytes 1769480 | tf_op jit(solution)/shard_map/ppermute | solution.py:34
  35.4 1.0 copy-start.2
  36.4 1.0 copy-start.4
  37.3 1.0 copy-start.6
  46.0 32.2 %copy-start.9 = (s32[1,192]{1,0:T(1,128)S(1)}, s32[1,192]{1,0:T(1,128)}, u32[]{:S(2)}) copy-start(s32[1,192]{1,0:T(1,128)} %param.11) | copy-start | bytes 2308
  49.1 16.9 %collective-permute-start.9 = (bf16[768,256]{1,0:T(8,128)(2,1)S(1)}, bf16[768,256]{1,0:T(8,128)(2,1)S(1)}, u32[]{:S(2)}, u32[]{:S(2)}) collective-permute-start(bf16[768,256]{1,0:T(8,128)(2,1)S(1)} %get-tuple-element.38), channel_id=1, source_target_pairs={{0,1},{1,0},{2,3},{3,2},{4,5},{5,4},{6,7},{7,6},{8,9},{9,8},{10,11... | collective-permute-start | bytes 1179656 | tf_op jit(solution)/shard_map/ppermute | solution.py:38
  55.1 15.6 %collective-permute-start.13 = (bf16[768,256]{1,0:T(8,128)(2,1)S(1)}, bf16[768,256]{1,0:T(8,128)(2,1)S(1)}, u32[]{:S(2)}, u32[]{:S(2)}) collective-permute-start(bf16[768,256]{1,0:T(8,128)(2,1)S(1)} %get-tuple-element.38), channel_id=1, source_target_pairs={{0,2},{1,31},{2,4},{3,1},{4,6},{5,3},{6,8},{7,5},{8,10},{9,7},{10,... | collective-permute-start | bytes 1179656 | tf_op jit(solution)/shard_map/ppermute | solution.py:48
  66.0 9.7 %collective-permute-start.10 = (bf16[768,256]{1,0:T(8,128)(2,1)S(1)}, bf16[768,256]{1,0:T(8,128)(2,1)S(1)}, u32[]{:S(2)}, u32[]{:S(2)}) collective-permute-start(bf16[768,256]{1,0:T(8,128)(2,1)S(1)} %collective-permute-done.9), channel_id=1, source_target_pairs={{0,2},{1,31},{2,4},{3,1},{4,6},{5,3},{6,8},{7,5},{8,10},{9,7},{10,... | collective-permute-start | bytes 1179656 | tf_op jit(solution)/shard_map/ppermute | solution.py:48
  70.7 14.1 %collective-permute-start.14 = (bf16[768,256]{1,0:T(8,128)(2,1)S(1)}, bf16[768,256]{1,0:T(8,128)(2,1)S(1)}, u32[]{:S(2)}, u32[]{:S(2)}) collective-permute-start(bf16[768,256]{1,0:T(8,128)(2,1)S(1)} %collective-permute-done.13), channel_id=1, source_target_pairs={{0,2},{1,31},{2,4},{3,1},{4,6},{5,3},{6,8},{7,5},{8,10},{9,7},{10,... | collective-permute-start | bytes 1179656 | tf_op jit(solution)/shard_map/ppermute | solution.py:48
  75.7 11.6 %collective-permute-start.12 = (bf16[768,128]{1,0:T(8,128)(2,1)S(1)}, bf16[768,128]{1,0:T(8,128)(2,1)S(1)}, u32[]{:S(2)}, u32[]{:S(2)}) collective-permute-start(bf16[768,128]{1,0:T(8,128)(2,1)S(1)} %get-tuple-element.40), channel_id=1, source_target_pairs={{0,1},{1,0},{2,3},{3,2},{4,5},{5,4},{6,7},{7,6},{8,9},{9,8},{10,11... | collective-permute-start | bytes 589832 | tf_op jit(solution)/shard_map/ppermute | solution.py:38
  81.1 8.8 %collective-permute-start.11 = (bf16[768,256]{1,0:T(8,128)(2,1)S(1)}, bf16[768,256]{1,0:T(8,128)(2,1)S(1)}, u32[]{:S(2)}, u32[]{:S(2)}) collective-permute-start(bf16[768,256]{1,0:T(8,128)(2,1)S(1)} %collective-permute-done.10), channel_id=1, source_target_pairs={{0,2},{1,31},{2,4},{3,1},{4,6},{5,3},{6,8},{7,5},{8,10},{9,7},{10,... | collective-permute-start | bytes 1179656 | tf_op jit(solution)/shard_map/ppermute | solution.py:48
  84.8 16.1 %collective-permute-start.15 = (bf16[768,256]{1,0:T(8,128)(2,1)S(1)}, bf16[768,256]{1,0:T(8,128)(2,1)S(1)}, u32[]{:S(2)}, u32[]{:S(2)}) collective-permute-start(bf16[768,256]{1,0:T(8,128)(2,1)S(1)} %collective-permute-done.14), channel_id=1, source_target_pairs={{0,2},{1,31},{2,4},{3,1},{4,6},{5,3},{6,8},{7,5},{8,10},{9,7},{10,... | collective-permute-start | bytes 1179656 | tf_op jit(solution)/shard_map/ppermute | solution.py:48
  89.9 13.0 %collective-permute-start.17 = (bf16[768,256]{1,0:T(8,128)(2,1)S(1)}, bf16[768,256]{1,0:T(8,128)(2,1)S(1)}, u32[]{:S(2)}, u32[]{:S(2)}) collective-permute-start(bf16[768,256]{1,0:T(8,128)(2,1)S(1)} %collective-permute-done.11), channel_id=1, source_target_pairs={{0,2},{1,31},{2,4},{3,1},{4,6},{5,3},{6,8},{7,5},{8,10},{9,7},{10,... | collective-permute-start | bytes 1179656 | tf_op jit(solution)/shard_map/ppermute | solution.py:48
  100.9 10.8 %collective-permute-start.16 = (bf16[768,256]{1,0:T(8,128)(2,1)S(1)}, bf16[768,256]{1,0:T(8,128)(2,1)S(1)}, u32[]{:S(2)}, u32[]{:S(2)}) collective-permute-start(bf16[768,256]{1,0:T(8,128)(2,1)S(1)} %collective-permute-done.15), channel_id=1, source_target_pairs={{0,2},{1,31},{2,4},{3,1},{4,6},{5,3},{6,8},{7,5},{8,10},{9,7},{10,... | collective-permute-start | bytes 1179656 | tf_op jit(solution)/shard_map/ppermute | solution.py:48
  102.8 12.3 %collective-permute-start.19 = (bf16[768,256]{1,0:T(8,128)(2,1)S(1)}, bf16[768,256]{1,0:T(8,128)(2,1)S(1)}, u32[]{:S(2)}, u32[]{:S(2)}) collective-permute-start(bf16[768,256]{1,0:T(8,128)(2,1)S(1)} %collective-permute-done.17), channel_id=1, source_target_pairs={{0,2},{1,31},{2,4},{3,1},{4,6},{5,3},{6,8},{7,5},{8,10},{9,7},{10,... | collective-permute-start | bytes 1179656 | tf_op jit(solution)/shard_map/ppermute | solution.py:48
  111.7 13.9 %collective-permute-start.18 = (bf16[768,256]{1,0:T(8,128)(2,1)S(1)}, bf16[768,256]{1,0:T(8,128)(2,1)S(1)}, u32[]{:S(2)}, u32[]{:S(2)}) collective-permute-start(bf16[768,256]{1,0:T(8,128)(2,1)S(1)} %collective-permute-done.16), channel_id=1, source_target_pairs={{0,2},{1,31},{2,4},{3,1},{4,6},{5,3},{6,8},{7,5},{8,10},{9,7},{10,... | collective-permute-start | bytes 1179656 | tf_op jit(solution)/shard_map/ppermute | solution.py:48
  115.2 12.4 %collective-permute-start.21 = (bf16[768,256]{1,0:T(8,128)(2,1)S(1)}, bf16[768,256]{1,0:T(8,128)(2,1)S(1)}, u32[]{:S(2)}, u32[]{:S(2)}) collective-permute-start(bf16[768,256]{1,0:T(8,128)(2,1)S(1)} %collective-permute-done.19), channel_id=1, source_target_pairs={{0,2},{1,31},{2,4},{3,1},{4,6},{5,3},{6,8},{7,5},{8,10},{9,7},{10,... | collective-permute-start | bytes 1179656 | tf_op jit(solution)/shard_map/ppermute | solution.py:48
  125.6 8.8 %collective-permute-start.20 = (bf16[768,256]{1,0:T(8,128)(2,1)S(1)}, bf16[768,256]{1,0:T(8,128)(2,1)S(1)}, u32[]{:S(2)}, u32[]{:S(2)}) collective-permute-start(bf16[768,256]{1,0:T(8,128)(2,1)S(1)} %collective-permute-done.18), channel_id=1, source_target_pairs={{0,2},{1,31},{2,4},{3,1},{4,6},{5,3},{6,8},{7,5},{8,10},{9,7},{10,... | collective-permute-start | bytes 1179656 | tf_op jit(solution)/shard_map/ppermute | solution.py:48
  127.6 10.8 %collective-permute-start.23 = (bf16[768,256]{1,0:T(8,128)(2,1)S(1)}, bf16[768,256]{1,0:T(8,128)(2,1)S(1)}, u32[]{:S(2)}, u32[]{:S(2)}) collective-permute-start(bf16[768,256]{1,0:T(8,128)(2,1)S(1)} %collective-permute-done.21), channel_id=1, source_target_pairs={{0,2},{1,31},{2,4},{3,1},{4,6},{5,3},{6,8},{7,5},{8,10},{9,7},{10,... | collective-permute-start | bytes 1179656 | tf_op jit(solution)/shard_map/ppermute | solution.py:48
  134.4 10.4 %collective-permute-start.22 = (bf16[768,256]{1,0:T(8,128)(2,1)S(1)}, bf16[768,256]{1,0:T(8,128)(2,1)S(1)}, u32[]{:S(2)}, u32[]{:S(2)}) collective-permute-start(bf16[768,256]{1,0:T(8,128)(2,1)S(1)} %collective-permute-done.20), channel_id=1, source_target_pairs={{0,2},{1,31},{2,4},{3,1},{4,6},{5,3},{6,8},{7,5},{8,10},{9,7},{10,... | collective-permute-start | bytes 1179656 | tf_op jit(solution)/shard_map/ppermute | solution.py:48
  138.4 10.0 %collective-permute-start.25 = (bf16[768,256]{1,0:T(8,128)(2,1)S(1)}, bf16[768,256]{1,0:T(8,128)(2,1)S(1)}, u32[]{:S(2)}, u32[]{:S(2)}) collective-permute-start(bf16[768,256]{1,0:T(8,128)(2,1)S(1)} %collective-permute-done.23), channel_id=1, source_target_pairs={{0,2},{1,31},{2,4},{3,1},{4,6},{5,3},{6,8},{7,5},{8,10},{9,7},{10,... | collective-permute-start | bytes 1179656 | tf_op jit(solution)/shard_map/ppermute | solution.py:48
  144.9 12.6 %collective-permute-start.24 = (bf16[768,256]{1,0:T(8,128)(2,1)S(1)}, bf16[768,256]{1,0:T(8,128)(2,1)S(1)}, u32[]{:S(2)}, u32[]{:S(2)}) collective-permute-start(bf16[768,256]{1,0:T(8,128)(2,1)S(1)} %collective-permute-done.22), channel_id=1, source_target_pairs={{1,31},{3,1},{5,3},{7,5},{9,7},{11,9},{13,11},{15,13},{17,15},{19,... | collective-permute-start | bytes 1179656 | tf_op jit(solution)/shard_map/ppermute | solution.py:48
  148.3 9.7 %collective-permute-start.26 = (bf16[768,256]{1,0:T(8,128)(2,1)S(1)}, bf16[768,256]{1,0:T(8,128)(2,1)S(1)}, u32[]{:S(2)}, u32[]{:S(2)}) collective-permute-start(bf16[768,256]{1,0:T(8,128)(2,1)S(1)} %collective-permute-done.25), channel_id=1, source_target_pairs={{1,31},{3,1},{5,3},{7,5},{9,7},{11,9},{13,11},{15,13},{17,15},{19,... | collective-permute-start | bytes 1179656 | tf_op jit(solution)/shard_map/ppermute | solution.py:48
  161.4 4.2 %collective-permute-start.27 = (f32[6,128,256]{2,1,0:T(8,128)S(1)}, f32[6,128,256]{2,1,0:T(8,128)S(1)}, u32[]{:S(2)}, u32[]{:S(2)}) collective-permute-start(f32[6,128,256]{2,1,0:T(8,128)S(1)} %get-tuple-element.56), channel_id=1, source_target_pairs={{0,1},{1,0},{2,3},{3,2},{4,5},{5,4},{6,7},{7,6},{8,9},{9,8},{10,11... | collective-permute-start | bytes 2359304 | tf_op jit(solution)/shard_map/ppermute | solution.py:38

commit v8 on v7

--- a/solution.py
+++ b/solution.py
@@ -10,7 +10,7 @@
 HEAD = 128
 PIECE = 48
 PLANES = 16
-UNROLL = 4
+UNROLL = 8
 CALLS = ((0, 3),) + tuple((step, step + 1) for step in range(3, 9))
 LOG2E = 1.4426950408889634
 MESH_AXES = ("seq", "bal")
@@ -52,44 +52,31 @@
     count = len(shares)
     blocks = refs[:count]
     weight, q_gain, k_gain = refs[count : count + 3]
-    q_out, kv_out, rows_in, weight_in, gain_in, q_held, kv_held, arrive, leave = refs[-9:]
+    q_out, kv_out, q_held, kv_held, leave = refs[-5:]
     first = place[0]
     second = place[1]
     first_step = place[2]
     second_step = place[3]
 
-    copies = [
-        pltpu.make_async_copy(weight, weight_in, arrive.at[count]),
-        pltpu.make_async_copy(q_gain, gain_in.at[0], arrive.at[count + 1]),
-        pltpu.make_async_copy(k_gain, gain_in.at[1], arrive.at[count + 2]),
-    ]
-    targets = []
+    def normalize(values, gain):
+        mean_square = jnp.mean(values * values, axis=-1, keepdims=True)
+        return (values * lax.rsqrt(mean_square + 1e-06) * gain).astype(jnp.bfloat16)
+
+    rows = jnp.concatenate([block[...] for block in blocks], axis=0)
+    whole = jnp.concatenate([weight[at] for at in range(3)], axis=1)
+    proj = jnp.dot(rows, whole, preferred_element_type=jnp.float32)
+    q_held[...] = normalize(proj[:, :HEAD], q_gain[...])
+    kv_held[:, :HEAD] = normalize(proj[:, HEAD : 2 * HEAD], k_gain[...])
+    kv_held[:, HEAD:] = proj[:, 2 * HEAD :].astype(jnp.bfloat16)
     row = 0
-    for at, (shift, pieces) in enumerate(shares):
-        here = rows_in.at[pl.ds(row, len(pieces) * PIECE), :]
-        copies.append(pltpu.make_async_copy(blocks[at], here, arrive.at[at]))
+    for shift, pieces in shares:
         for piece in pieces:
             spot = ((first + piece) % 4) * first_step + ((second + shift) % 4) * second_step
             target = pl.ds(pl.multiple_of(spot * PIECE, PIECE), PIECE)
-            targets.append((pl.ds(row, PIECE), target))
+            source = pl.ds(row, PIECE)
+            pltpu.make_async_copy(q_held.at[source, :], q_out.at[target, :], leave.at[0]).start()
+            pltpu.make_async_copy(kv_held.at[source, :], kv_out.at[target, :], leave.at[1]).start()
             row += PIECE
-    for copy in copies:
-        copy.start()
-    for copy in copies:
-        copy.wait()
-
-    def normalize(values, gain):
-        mean_square = jnp.mean(values * values, axis=-1, keepdims=True)
-        return (values * lax.rsqrt(mean_square + 1e-06) * gain).astype(jnp.bfloat16)
-
-    whole = jnp.concatenate([weight_in[at] for at in range(3)], axis=1)
-    proj = jnp.dot(rows_in[...], whole, preferred_element_type=jnp.float32)
-    q_held[...] = normalize(proj[:, :HEAD], gain_in[0])
-    kv_held[:, :HEAD] = normalize(proj[:, HEAD : 2 * HEAD], gain_in[1])
-    kv_held[:, HEAD:] = proj[:, 2 * HEAD :].astype(jnp.bfloat16)
-    for source, target in targets:
-        pltpu.make_async_copy(q_held.at[source, :], q_out.at[target, :], leave.at[0]).start()
-        pltpu.make_async_copy(kv_held.at[source, :], kv_out.at[target, :], leave.at[1]).start()
     pltpu.make_async_copy(q_held, q_held, leave.at[0]).wait()
     pltpu.make_async_copy(kv_held, kv_held, leave.at[1]).wait()
 
@@ -98,7 +85,6 @@
     rows = 16 * PIECE
     count = len(blocks)
     rows_here = sum(len(pieces) for _, pieces in shares) * PIECE
-    width = blocks[0].shape[1]
     anywhere = pl.BlockSpec(memory_space=pl.ANY)
     return pl.pallas_call(
         functools.partial(project_kernel, shares),
@@ -106,19 +92,15 @@
             jax.ShapeDtypeStruct((rows, HEAD), jnp.bfloat16),
             jax.ShapeDtypeStruct((rows, 2 * HEAD), jnp.bfloat16),
         ),
-        in_specs=[SMEM] + [anywhere] * (count + 3 + len(begun)),
+        in_specs=[SMEM] + [VMEM] * (count + 3) + [anywhere] * len(begun),
         out_specs=(anywhere, anywhere),
         scratch_shapes=[
-            pltpu.VMEM((rows_here, width), jnp.bfloat16),
-            pltpu.VMEM((3, width, HEAD), jnp.bfloat16),
-            pltpu.VMEM((2, 1, HEAD), jnp.float32),
             pltpu.VMEM((rows_here, HEAD), jnp.bfloat16),
             pltpu.VMEM((rows_here, 2 * HEAD), jnp.bfloat16),
-            pltpu.SemaphoreType.DMA((count + 3,)),
             pltpu.SemaphoreType.DMA((2,)),
         ],
         input_output_aliases={count + 4: 0, count + 5: 1} if begun else {},
-        compiler_params=pltpu.CompilerParams(vmem_limit_bytes=16 * 1024 * 1024),
+        compiler_params=pltpu.CompilerParams(vmem_limit_bytes=20 * 1024 * 1024),
         name="project",
     )(place, *blocks, weight, q_gain, k_gain, *begun)
 
@@ -143,19 +125,25 @@
     ones = jnp.ones((TILE, HEAD), jnp.bfloat16)
 
     def turn(step, _):
+        rows_here, scores, products = [], [], []
         for at in range(UNROLL):
             pair = pairs[call, step * UNROLL + at]
-            row = pair >> 7
-            tile = pair & 127
-            scores = lax.dot_general(
-                q[jnp.minimum(row, rows - 1)],
-                kv[tile, :, :HEAD],
-                (((1,), (1,)), ((), ())),
-                preferred_element_type=jnp.float32,
+            rows_here.append((pair >> 7, pair & 127))
+        for row, tile in rows_here:
+            scores.append(
+                lax.dot_general(
+                    q[jnp.minimum(row, rows - 1)],
+                    kv[tile, :, :HEAD],
+                    (((1,), (1,)), ((), ())),
+                    preferred_element_type=jnp.float32,
+                )
             )
-            weights = jnp.exp2(scores * scale).astype(jnp.bfloat16)
+        for (row, tile), score in zip(rows_here, scores):
+            weights = jnp.exp2(score * scale).astype(jnp.bfloat16)
             values = jnp.concatenate((kv[tile, :, HEAD:], ones), axis=1)
-            sums[row] += jnp.dot(weights, values, preferred_element_type=jnp.float32)
+            products.append(jnp.dot(weights, values, preferred_element_type=jnp.float32))
+        for (row, _), product in zip(rows_here, products):
+            sums[row] += product
         return 0
 
     lax.fori_loop(0, (counts[0, call] + UNROLL - 1) // UNROLL, turn, 0)
@@ -191,11 +179,15 @@
     )(place, pairs, counts, q, *pieces, *more)
 
 
+def call_room(start, stop, slots):
+    pairs = 2 * slots * (2 * stop - start - max(start, 1)) * slots
+    return -(-pairs // TILE) * TILE
+
+
 def list_kernel(slots, calls, place, tiles, counts, pairs_out, counts_out):
     core = place[4]
     plane = place[5]
     listed, rows = tiles.shape
-    room = pairs_out.shape[1]
     tile = tiles[...]
     bal = (tile * (65536 // slots + 1)) >> 16
     away = (((bal >> 1) - plane) * (2 * core - 1)) & (PLANES - 1)
@@ -211,7 +203,6 @@
     down = lax.broadcasted_iota(jnp.int32, (rows, rows), 0)
     along = lax.broadcasted_iota(jnp.int32, (rows, rows), 1)
     ahead = jnp.where(down < along, 1.0, 0.0)
-    spot = lax.broadcasted_iota(jnp.int32, (listed, room), 1)
     nothing = rows * TILE
     totals = []
     for call, (start, stop) in enumerate(calls):
@@ -226,11 +217,13 @@
         skip = stop - start - max(start, 1)
         block = jnp.where(same, away - start, away + skip)
         pair = column * TILE + block * slots + tile - bal * slots - nothing
+        room = call_room(start, stop, slots)
+        spot = lax.broadcasted_iota(jnp.int32, (listed, room), 1)
         placed = jnp.zeros((1, room), jnp.int32)
         for row in range(rows):
             hit = order[:, row : row + 1] == spot
             placed += jnp.sum(jnp.where(hit, pair[:, row : row + 1], 0), axis=0, keepdims=True)
-        pairs_out[call : call + 1, :] = placed + nothing
+        pairs_out[call : call + 1, :room] = placed + nothing
         totals.append(jnp.sum(total, axis=1, keepdims=True).astype(jnp.int32))
     counts_out[...] = jnp.concatenate(totals, axis=1)
 
@@ -239,8 +232,7 @@
     rows = 2 * slots
     tiles = lax.dynamic_slice_in_dim(key_tiles.T, place[5] * rows, rows, 1)
     counts = lax.dynamic_slice_in_dim(key_counts, place[5] * rows, rows, 1)
-    most = max(2 * stop - start - max(start, 1) for start, stop in calls) * slots
-    room = -(-rows * most // TILE) * TILE
+    room = max(call_room(start, stop, slots) for start, stop in calls)
     return pl.pallas_call(
         functools.partial(list_kernel, slots, calls),
         out_shape=(
@@ -303,6 +295,7 @@
         place,
         begun,
     )
+    begun, (pairs, counts) = lax.optimization_barrier((begun, (pairs, counts)))
     queries, keys_values = project(
         ((2, low_pieces), (2, high_pieces)),
         (across_low, across_high),

time: 184 us -> 165 us (0.90)
  Pallas kernels: 41.9 us -> 21.4 us
  starting transfers between devices: 104 us -> 110 us
  blocking collectives: 16.5 us -> 13.5 us
  local copies, waits for them, and re-layouts: 7.84 us -> 5.82 us
    pallas_call x7, Pallas kernels: 28.8 us -> 10.9 us  [attend(): pl.pallas_call(functools.partial(attend_kernel, scale, first_call, last_c...]
    ppermute x16, starting transfers between devices: 64.9 us -> 71 us  [pass_on(): return lax.ppermute(block, 'bal', pairs)]
    all_to_all x1, blocking collectives: 16.5 us -> 13.5 us  [on_device(): lax.all_to_all(result.reshape(slots * TILE, HEAD), 'seq', split_axis=0, c...]
    pallas_call x3, Pallas kernels: 10.4 us -> 7.88 us  [project(): pl.pallas_call(functools.partial(project_kernel, shares), out_shape=(jax....]
    unnamed x22 -> x14, local copies, waits for them, and re-layouts: 5.34 us -> 3.42 us
  transfers between devices with their start and end apart: 28 -> 28, of which waited for: 10 -> 8; matrix products, arithmetic and copies ran while one was open for 2% -> 3% of each run, Pallas kernels for 19% -> 11%
where the time goes in v8:
time: 165 us; the launch traced here: 164 us
  starting transfers between devices  110 us (67%)
  Pallas kernels  21.4 us (13%)
  blocking collectives  13.5 us (8%)
  waiting for transfers between devices  12.6 us (8%)
  local copies, waits for them, and re-layouts  5.82 us (4%)
    ppermute x16, starting transfers between devices, pass_on(): return lax.ppermute(block, 'bal', pairs)  71 us
    ppermute x9, starting transfers between devices, send(): return lax.ppermute(block, MESH_AXES, plane_perm(phase, shift))  28.5 us
    all_to_all x1, blocking collectives, on_device(): lax.all_to_all(result.reshape(slots * TILE, HEAD), 'seq', split_axis=0, c...  13.5 us
    pallas_call x7, Pallas kernels, attend(): pl.pallas_call(functools.partial(attend_kernel, scale, first_call, last_c...  10.9 us
    ppermute x3, starting transfers between devices, swap_cores(): return lax.ppermute(block, 'bal', [(at, at ^ 1) for at in range(32)])  10.4 us
    pallas_call x3, Pallas kernels, project(): pl.pallas_call(functools.partial(project_kernel, shares), out_shape=(jax....  7.88 us
    ppermute x16, waiting for transfers between devices, pass_on(): return lax.ppermute(block, 'bal', pairs)  6.71 us
    ppermute x9, waiting for transfers between devices, send(): return lax.ppermute(block, MESH_AXES, plane_perm(phase, shift))  3.88 us
  transfers between devices with their start and end apart: 28, of which 8 were waited for; matrix products, arithmetic and copies ran while one was open for 3% of the time, Pallas kernels for 11%

profile of v8, /device:TPU:1, one launch (start us, length us, event | category | flops | bytes accessed | tf_op | source)
XLA Modules:
  0.0 164.0 jit_solution(11864389469963318875)
XLA Ops:
  0.0 5.6 %collective-permute-start.2 = (bf16[48,3072]{1,0:T(8,128)(2,1)}, bf16[48,3072]{1,0:T(8,128)(2,1)S(1)}, u32[]{:S(2)}, u32[]{:S(2)}) collective-permute-start(bf16[48,3072]{1,0:T(8,128)(2,1)} %refs_0_.1), channel_id=1, source_target_pairs={{0,96},{32,0},{64,32},{96,64},{128,224},{160,128},{192,160},{224,1... | collective-permute-start | bytes 884744 | tf_op jit(solution)/shard_map/ppermute | solution.py:34
  5.6 2.3 %collective-permute-start.3 = (bf16[48,3072]{1,0:T(8,128)(2,1)}, bf16[48,3072]{1,0:T(8,128)(2,1)S(1)}, u32[]{:S(2)}, u32[]{:S(2)}) collective-permute-start(bf16[48,3072]{1,0:T(8,128)(2,1)} %refs_0_.1), channel_id=1, source_target_pairs={{0,64},{32,96},{64,0},{96,32},{128,192},{160,224},{192,128},{224,1... | collective-permute-start | bytes 884744 | tf_op jit(solution)/shard_map/ppermute | solution.py:34
  7.9 2.6 %collective-permute-start = (bf16[48,3072]{1,0:T(8,128)(2,1)}, bf16[48,3072]{1,0:T(8,128)(2,1)S(1)}, u32[]{:S(2)}, u32[]{:S(2)}) collective-permute-start(bf16[48,3072]{1,0:T(8,128)(2,1)} %refs_0_.1), channel_id=1, source_target_pairs={{0,32},{32,64},{64,96},{96,0},{128,160},{160,192},{192,224},{224,1... | collective-permute-start | bytes 884744 | tf_op jit(solution)/shard_map/ppermute | solution.py:34
  10.5 1.7 %constant_dynamic-update-slice_fusion.1 = bf16[96,3072]{1,0:T(8,128)(2,1)} fusion(bf16[48,3072]{1,0:T(8,128)(2,1)} %refs_0_.1), kind=kLoop, calls=%fused_computation.8 | loop fusion | bytes 589824
  12.2 0.6 collective-permute-done.2.refs_2_
  12.8 0.7 constant_dynamic-update-slice_fusion.3
  13.5 1.4 collective-permute-done.3.refs_3_
  14.9 0.7 constant_dynamic-update-slice_fusion.2
  15.7 4.4 %collective-permute-start.6 = (bf16[96,3072]{1,0:T(8,128)(2,1)}, bf16[96,3072]{1,0:T(8,128)(2,1)}, u32[]{:S(2)}, u32[]{:S(2)}) collective-permute-start(bf16[96,3072]{1,0:T(8,128)(2,1)} %constant_dynamic-update-slice_fusion.2), channel_id=1, source_target_pairs={{0,384},{32,416},{64,448},{96,480},{128,0},{160,32},{192,64},{224,... | collective-permute-start | bytes 1769480 | tf_op jit(solution)/shard_map/ppermute | solution.py:34
  20.0 0.0 collective-permute-done.refs_1_
  20.1 0.7 constant_dynamic-update-slice_fusion
  20.8 1.9 %collective-permute-start.5 = (bf16[96,3072]{1,0:T(8,128)(2,1)}, bf16[96,3072]{1,0:T(8,128)(2,1)}, u32[]{:S(2)}, u32[]{:S(2)}) collective-permute-start(bf16[96,3072]{1,0:T(8,128)(2,1)} %constant_dynamic-update-slice_fusion), channel_id=1, source_target_pairs={{0,128},{32,160},{64,192},{96,224},{128,256},{160,288},{192,320},{... | collective-permute-start | bytes 1769480 | tf_op jit(solution)/shard_map/ppermute | solution.py:34
  22.7 2.2 %collective-permute-start.4 = (bf16[96,3072]{1,0:T(8,128)(2,1)}, bf16[96,3072]{1,0:T(8,128)(2,1)}, u32[]{:S(2)}, u32[]{:S(2)}) collective-permute-start(bf16[96,3072]{1,0:T(8,128)(2,1)} %constant_dynamic-update-slice_fusion.2), channel_id=1, source_target_pairs={{0,128},{32,160},{64,192},{96,224},{128,256},{160,288},{192,320},{... | collective-permute-start | bytes 1769480 | tf_op jit(solution)/shard_map/ppermute | solution.py:34
  25.0 4.2 %collective-permute-start.1 = (bf16[96,3072]{1,0:T(8,128)(2,1)}, bf16[96,3072]{1,0:T(8,128)(2,1)}, u32[]{:S(2)}, u32[]{:S(2)}) collective-permute-start(bf16[96,3072]{1,0:T(8,128)(2,1)} %constant_dynamic-update-slice_fusion), channel_id=1, source_target_pairs={{0,384},{32,416},{64,448},{96,480},{128,0},{160,32},{192,64},{224,... | collective-permute-start | bytes 1769480 | tf_op jit(solution)/shard_map/ppermute | solution.py:34
  29.2 0.0 collective-permute-done.6.refs_5_
  29.2 3.4 %collective-permute-start.8 = (bf16[96,3072]{1,0:T(8,128)(2,1)}, bf16[96,3072]{1,0:T(8,128)(2,1)}, u32[]{:S(2)}, u32[]{:S(2)}) collective-permute-start(bf16[96,3072]{1,0:T(8,128)(2,1)} %collective-permute-done.6.refs_5_), channel_id=1, source_target_pairs={{0,384},{32,416},{64,448},{96,480},{128,0},{160,32},{192,64},{224,... | collective-permute-start | bytes 1769480 | tf_op jit(solution)/shard_map/ppermute | solution.py:34
  32.6 0.6 collective-permute-done.5.refs_4_
  33.2 1.9 %collective-permute-start.7 = (bf16[96,3072]{1,0:T(8,128)(2,1)}, bf16[96,3072]{1,0:T(8,128)(2,1)}, u32[]{:S(2)}, u32[]{:S(2)}) collective-permute-start(bf16[96,3072]{1,0:T(8,128)(2,1)} %collective-permute-done.5.refs_4_), channel_id=1, source_target_pairs={{0,128},{32,160},{64,192},{96,224},{128,256},{160,288},{192,320},{... | collective-permute-start | bytes 1769480 | tf_op jit(solution)/shard_map/ppermute | solution.py:34
  35.2 0.1 stack.27.place
  35.3 0.1 constant_dynamic-slice_fusion.counts
  35.4 0.1 dynamic-slice_bitcast_fusion.tiles
  35.5 2.6 %lists.1 = (s32[7,384]{1,0:T(8,128)S(1)}, s32[1,7]{1,0:T(1,128)S(1)}) custom-call(s32[6]{0:T(128)S(1)} %stack.27.place, s32[64,12]{1,0:T(8,128)S(1)} %dynamic-slice_bitcast_fusion.tiles, s32[1,12]{1,0:T(1,128)S(1)} %constant_dynamic-slice_fusion.counts), custom_call_target="tpu_custom_call" | custom-call | tf_op jit(solution)/shard_map/lists/pallas_call | solution.py:236
  38.1 0.0 copy-start.2
  38.1 1.0 copy-done.2
  39.0 3.2 %project.3 = (bf16[768,128]{1,0:T(8,128)(2,1)S(1)}, bf16[768,256]{1,0:T(8,128)(2,1)S(1)}) custom-call(s32[6]{0:T(128)S(1)} %stack.27.place, bf16[48,3072]{1,0:T(8,128)(2,1)S(1)} %copy-done.2, bf16[48,3072]{1,0:T(8,128)(2,1)S(1)} %collective-permute-done.refs_1_, bf16[48,3072]{1,0:T(8,128)(2,1)S(1)} %collective-permute-done.2.refs_2_, ...), custom_call_target="tpu_custom_call" | custom-call | tf_op jit(solution)/shard_map/project/pallas_call | solution.py:89
  42.2 0.0 collective-permute-done.4.refs_1_
  42.2 2.4 %project.4 = (bf16[768,128]{1,0:T(8,128)(2,1)S(1)}, bf16[768,256]{1,0:T(8,128)(2,1)S(1)}) custom-call(s32[6]{0:T(128)S(1)} %stack.27.place, bf16[96,3072]{1,0:T(8,128)(2,1)} %collective-permute-done.1.refs_0_, bf16[96,3072]{1,0:T(8,128)(2,1)} %collective-permute-done.4.refs_1_, ...), custom_call_target="tpu_custom_call", output_to_operand_aliasing={{0}: (6, {}), {1}: (7, {})} | custom-call | tf_op jit(solution)/shard_map/project/pallas_call | solution.py:89
  44.6 1.3 collective-permute-done.7.refs_0_
  45.9 2.4 %project.5 = (bf16[768,128]{1,0:T(8,128)(2,1)S(1)}, bf16[768,256]{1,0:T(8,128)(2,1)S(1)}) custom-call(s32[6]{0:T(128)S(1)} %stack.27.place, bf16[96,3072]{1,0:T(8,128)(2,1)} %collective-permute-done.7.refs_0_, bf16[96,3072]{1,0:T(8,128)(2,1)} %collective-permute-done.8.refs_1_, ...), custom_call_target="tpu_custom_call", output_to_operand_aliasing={{0}: (6, {}), {1}: (7, {})} | custom-call | tf_op jit(solution)/shard_map/project/pallas_call | solution.py:89
  48.2 5.8 %collective-permute-start.9 = (bf16[768,256]{1,0:T(8,128)(2,1)S(1)}, bf16[768,256]{1,0:T(8,128)(2,1)S(1)}, u32[]{:S(2)}, u32[]{:S(2)}) collective-permute-start(bf16[768,256]{1,0:T(8,128)(2,1)S(1)} %get-tuple-element.46), channel_id=1, source_target_pairs={{0,1},{1,0},{2,3},{3,2},{4,5},{5,4},{6,7},{7,6},{8,9},{9,8},{10,11... | collective-permute-start | bytes 1179656 | tf_op jit(solution)/shard_map/ppermute | solution.py:38
  54.1 11.1 %collective-permute-start.13 = (bf16[768,256]{1,0:T(8,128)(2,1)S(1)}, bf16[768,256]{1,0:T(8,128)(2,1)S(1)}, u32[]{:S(2)}, u32[]{:S(2)}) collective-permute-start(bf16[768,256]{1,0:T(8,128)(2,1)S(1)} %get-tuple-element.46), channel_id=1, source_target_pairs={{0,2},{1,31},{2,4},{3,1},{4,6},{5,3},{6,8},{7,5},{8,10},{9,7},{10,... | collective-permute-start | bytes 1179656 | tf_op jit(solution)/shard_map/ppermute | solution.py:48
  65.2 2.6 %collective-permute-start.10 = (bf16[768,256]{1,0:T(8,128)(2,1)S(1)}, bf16[768,256]{1,0:T(8,128)(2,1)S(1)}, u32[]{:S(2)}, u32[]{:S(2)}) collective-permute-start(bf16[768,256]{1,0:T(8,128)(2,1)S(1)} %collective-permute-done.9), channel_id=1, source_target_pairs={{0,2},{1,31},{2,4},{3,1},{4,6},{5,3},{6,8},{7,5},{8,10},{9,7},{10,... | collective-permute-start | bytes 1179656 | tf_op jit(solution)/shard_map/ppermute | solution.py:48
  67.8 2.0 %collective-permute-done.13 = bf16[768,256]{1,0:T(8,128)(2,1)S(1)} collective-permute-done((bf16[768,256]{1,0:T(8,128)(2,1)S(1)}, bf16[768,256]{1,0:T(8,128)(2,1)S(1)}, u32[]{:S(2)}, u32[]{:S(2)}) %collective-permute-start.13) | collective-permute-done | bytes 393248 | tf_op jit(solution)/shard_map/ppermute | solution.py:48
  69.8 5.0 %collective-permute-start.14 = (bf16[768,256]{1,0:T(8,128)(2,1)S(1)}, bf16[768,256]{1,0:T(8,128)(2,1)S(1)}, u32[]{:S(2)}, u32[]{:S(2)}) collective-permute-start(bf16[768,256]{1,0:T(8,128)(2,1)S(1)} %collective-permute-done.13), channel_id=1, source_target_pairs={{0,2},{1,31},{2,4},{3,1},{4,6},{5,3},{6,8},{7,5},{8,10},{9,7},{10,... | collective-permute-start | bytes 1179656 | tf_op jit(solution)/shard_map/ppermute | solution.py:48
  74.9 0.0 collective-permute-done.10
  74.9 2.4 %collective-permute-start.12 = (bf16[768,128]{1,0:T(8,128)(2,1)S(1)}, bf16[768,128]{1,0:T(8,128)(2,1)S(1)}, u32[]{:S(2)}, u32[]{:S(2)}) collective-permute-start(bf16[768,128]{1,0:T(8,128)(2,1)S(1)} %get-tuple-element.48), channel_id=1, source_target_pairs={{0,1},{1,0},{2,3},{3,2},{4,5},{5,4},{6,7},{7,6},{8,9},{9,8},{10,11... | collective-permute-start | bytes 589832 | tf_op jit(solution)/shard_map/ppermute | solution.py:38
  77.3 3.7 %collective-permute-start.11 = (bf16[768,256]{1,0:T(8,128)(2,1)S(1)}, bf16[768,256]{1,0:T(8,128)(2,1)S(1)}, u32[]{:S(2)}, u32[]{:S(2)}) collective-permute-start(bf16[768,256]{1,0:T(8,128)(2,1)S(1)} %collective-permute-done.10), channel_id=1, source_target_pairs={{0,2},{1,31},{2,4},{3,1},{4,6},{5,3},{6,8},{7,5},{8,10},{9,7},{10,... | collective-permute-start | bytes 1179656 | tf_op jit(solution)/shard_map/ppermute | solution.py:48
  81.0 3.6 %collective-permute-start.15 = (bf16[768,256]{1,0:T(8,128)(2,1)S(1)}, bf16[768,256]{1,0:T(8,128)(2,1)S(1)}, u32[]{:S(2)}, u32[]{:S(2)}) collective-permute-start(bf16[768,256]{1,0:T(8,128)(2,1)S(1)} %collective-permute-done.14), channel_id=1, source_target_pairs={{0,2},{1,31},{2,4},{3,1},{4,6},{5,3},{6,8},{7,5},{8,10},{9,7},{10,... | collective-permute-start | bytes 1179656 | tf_op jit(solution)/shard_map/ppermute | solution.py:48
  84.7 1.4 collective-permute-done.11
  86.1 4.6 %collective-permute-start.17 = (bf16[768,256]{1,0:T(8,128)(2,1)S(1)}, bf16[768,256]{1,0:T(8,128)(2,1)S(1)}, u32[]{:S(2)}, u32[]{:S(2)}) collective-permute-start(bf16[768,256]{1,0:T(8,128)(2,1)S(1)} %collective-permute-done.11), channel_id=1, source_target_pairs={{0,2},{1,31},{2,4},{3,1},{4,6},{5,3},{6,8},{7,5},{8,10},{9,7},{10,... | collective-permute-start | bytes 1179656 | tf_op jit(solution)/shard_map/ppermute | solution.py:48
  90.7 1.9 %attend.7.refs_2_ = f32[13,128,256]{2,1,0:T(8,128)S(1)} custom-call(s32[6]{0:T(128)S(1)} %stack.27.place, s32[7,384]{1,0:T(8,128)S(1)} %get-tuple-element.41.pairs, s32[1,7]{1,0:T(1,128)S(1)} %get-tuple-element.42.counts, bf16[12,128,128]{2,1,0:T(8,128)(2,1)S(1)} %bitcast.42, bf16[6,128,256]{2,1,0:T(8,128)(2,1)S(1)} %bitcast.41, ...), custom_call_target="tpu_custom_call" | custom-call | flops 5000000000 | bytes 5000000 | tf_op jit(solution)/shard_map/attend/pallas_call | solution.py:167
  92.7 3.4 %collective-permute-start.16 = (bf16[768,256]{1,0:T(8,128)(2,1)S(1)}, bf16[768,256]{1,0:T(8,128)(2,1)S(1)}, u32[]{:S(2)}, u32[]{:S(2)}) collective-permute-start(bf16[768,256]{1,0:T(8,128)(2,1)S(1)} %collective-permute-done.15), channel_id=1, source_target_pairs={{0,2},{1,31},{2,4},{3,1},{4,6},{5,3},{6,8},{7,5},{8,10},{9,7},{10,... | collective-permute-start | bytes 1179656 | tf_op jit(solution)/shard_map/ppermute | solution.py:48
  96.1 4.4 %collective-permute-start.19 = (bf16[768,256]{1,0:T(8,128)(2,1)S(1)}, bf16[768,256]{1,0:T(8,128)(2,1)S(1)}, u32[]{:S(2)}, u32[]{:S(2)}) collective-permute-start(bf16[768,256]{1,0:T(8,128)(2,1)S(1)} %collective-permute-done.17), channel_id=1, source_target_pairs={{0,2},{1,31},{2,4},{3,1},{4,6},{5,3},{6,8},{7,5},{8,10},{9,7},{10,... | collective-permute-start | bytes 1179656 | tf_op jit(solution)/shard_map/ppermute | solution.py:48
  100.5 1.5 attend.8.refs_2_
  102.0 3.8 %collective-permute-start.18 = (bf16[768,256]{1,0:T(8,128)(2,1)S(1)}, bf16[768,256]{1,0:T(8,128)(2,1)S(1)}, u32[]{:S(2)}, u32[]{:S(2)}) collective-permute-start(bf16[768,256]{1,0:T(8,128)(2,1)S(1)} %collective-permute-done.16), channel_id=1, source_target_pairs={{0,2},{1,31},{2,4},{3,1},{4,6},{5,3},{6,8},{7,5},{8,10},{9,7},{10,... | collective-permute-start | bytes 1179656 | tf_op jit(solution)/shard_map/ppermute | solution.py:48
  105.8 4.4 %collective-permute-start.21 = (bf16[768,256]{1,0:T(8,128)(2,1)S(1)}, bf16[768,256]{1,0:T(8,128)(2,1)S(1)}, u32[]{:S(2)}, u32[]{:S(2)}) collective-permute-start(bf16[768,256]{1,0:T(8,128)(2,1)S(1)} %collective-permute-done.19), channel_id=1, source_target_pairs={{0,2},{1,31},{2,4},{3,1},{4,6},{5,3},{6,8},{7,5},{8,10},{9,7},{10,... | collective-permute-start | bytes 1179656 | tf_op jit(solution)/shard_map/ppermute | solution.py:48
  110.2 1.5 attend.9.refs_2_
  111.7 3.8 %collective-permute-start.20 = (bf16[768,256]{1,0:T(8,128)(2,1)S(1)}, bf16[768,256]{1,0:T(8,128)(2,1)S(1)}, u32[]{:S(2)}, u32[]{:S(2)}) collective-permute-start(bf16[768,256]{1,0:T(8,128)(2,1)S(1)} %collective-permute-done.18), channel_id=1, source_target_pairs={{0,2},{1,31},{2,4},{3,1},{4,6},{5,3},{6,8},{7,5},{8,10},{9,7},{10,... | collective-permute-start | bytes 1179656 | tf_op jit(solution)/shard_map/ppermute | solution.py:48
  115.5 4.4 %collective-permute-start.23 = (bf16[768,256]{1,0:T(8,128)(2,1)S(1)}, bf16[768,256]{1,0:T(8,128)(2,1)S(1)}, u32[]{:S(2)}, u32[]{:S(2)}) collective-permute-start(bf16[768,256]{1,0:T(8,128)(2,1)S(1)} %collective-permute-done.21), channel_id=1, source_target_pairs={{0,2},{1,31},{2,4},{3,1},{4,6},{5,3},{6,8},{7,5},{8,10},{9,7},{10,... | collective-permute-start | bytes 1179656 | tf_op jit(solution)/shard_map/ppermute | solution.py:48
  119.9 1.5 attend.10.refs_2_
  121.4 3.8 %collective-permute-start.22 = (bf16[768,256]{1,0:T(8,128)(2,1)S(1)}, bf16[768,256]{1,0:T(8,128)(2,1)S(1)}, u32[]{:S(2)}, u32[]{:S(2)}) collective-permute-start(bf16[768,256]{1,0:T(8,128)(2,1)S(1)} %collective-permute-done.20), channel_id=1, source_target_pairs={{0,2},{1,31},{2,4},{3,1},{4,6},{5,3},{6,8},{7,5},{8,10},{9,7},{10,... | collective-permute-start | bytes 1179656 | tf_op jit(solution)/shard_map/ppermute | solution.py:48
  125.2 4.4 %collective-permute-start.25 = (bf16[768,256]{1,0:T(8,128)(2,1)S(1)}, bf16[768,256]{1,0:T(8,128)(2,1)S(1)}, u32[]{:S(2)}, u32[]{:S(2)}) collective-permute-start(bf16[768,256]{1,0:T(8,128)(2,1)S(1)} %collective-permute-done.23), channel_id=1, source_target_pairs={{0,2},{1,31},{2,4},{3,1},{4,6},{5,3},{6,8},{7,5},{8,10},{9,7},{10,... | collective-permute-start | bytes 1179656 | tf_op jit(solution)/shard_map/ppermute | solution.py:48
  129.6 1.5 attend.11.refs_2_
  131.1 3.8 %collective-permute-start.24 = (bf16[768,256]{1,0:T(8,128)(2,1)S(1)}, bf16[768,256]{1,0:T(8,128)(2,1)S(1)}, u32[]{:S(2)}, u32[]{:S(2)}) collective-permute-start(bf16[768,256]{1,0:T(8,128)(2,1)S(1)} %collective-permute-done.22), channel_id=1, source_target_pairs={{1,31},{3,1},{5,3},{7,5},{9,7},{11,9},{13,11},{15,13},{17,15},{19,... | collective-permute-start | bytes 1179656 | tf_op jit(solution)/shard_map/ppermute | solution.py:48
  135.0 4.4 %collective-permute-start.26 = (bf16[768,256]{1,0:T(8,128)(2,1)S(1)}, bf16[768,256]{1,0:T(8,128)(2,1)S(1)}, u32[]{:S(2)}, u32[]{:S(2)}) collective-permute-start(bf16[768,256]{1,0:T(8,128)(2,1)S(1)} %collective-permute-done.25), channel_id=1, source_target_pairs={{1,31},{3,1},{5,3},{7,5},{9,7},{11,9},{13,11},{15,13},{17,15},{19,... | collective-permute-start | bytes 1179656 | tf_op jit(solution)/shard_map/ppermute | solution.py:48
  139.3 1.5 attend.12.refs_2_
  140.8 3.2 %collective-permute-done.26 = bf16[768,256]{1,0:T(8,128)(2,1)S(1)} collective-permute-done((bf16[768,256]{1,0:T(8,128)(2,1)S(1)}, bf16[768,256]{1,0:T(8,128)(2,1)S(1)}, u32[]{:S(2)}, u32[]{:S(2)}) %collective-permute-start.26) | collective-permute-done | bytes 393248 | tf_op jit(solution)/shard_map/ppermute | solution.py:48
  144.0 1.5 attend.13
  145.5 2.1 %collective-permute-start.27 = (f32[6,128,256]{2,1,0:T(8,128)S(1)}, f32[6,128,256]{2,1,0:T(8,128)S(1)}, u32[]{:S(2)}, u32[]{:S(2)}) collective-permute-start(f32[6,128,256]{2,1,0:T(8,128)S(1)} %get-tuple-element.64), channel_id=1, source_target_pairs={{0,1},{1,0},{2,3},{3,2},{4,5},{5,4},{6,7},{7,6},{8,9},{9,8},{10,11... | collective-permute-start | bytes 2359304 | tf_op jit(solution)/shard_map/ppermute | solution.py:38
  147.7 2.0 %collective-permute-done.27 = f32[6,128,256]{2,1,0:T(8,128)S(1)} collective-permute-done((f32[6,128,256]{2,1,0:T(8,128)S(1)}, f32[6,128,256]{2,1,0:T(8,128)S(1)}, u32[]{:S(2)}, u32[]{:S(2)}) %collective-permute-start.27) | collective-permute-done | bytes 786464 | tf_op jit(solution)/shard_map/ppermute | solution.py:38
  149.7 0.1 add.19
  149.8 0.1 fusion
  149.9 13.5 %all_to_all.19 = bf16[16,48,128]{2,1,0:T(8,128)(2,1)S(1)} all-to-all(bf16[16,48,128]{2,1,0:T(8,128)(2,1)S(1)} %bitcast.65), channel_id=1, replica_groups=mesh['seq'=16,'bal'=32] {'seq'}, dimensions={0} | all-to-all | bytes 393216 | tf_op jit(solution)/shard_map/all_to_all | solution.py:334
  163.4 0.7 copy_bitcast_fusion
  (28 shorter events, 0.1 us)
Async XLA Ops:
  0.0 35.4 %copy-start = (s32[1,192,64]{1,2,0:T(8,128)S(1)}, s32[1,192,64]{1,2,0:T(8,128)}, u32[]{:S(2)}) copy-start(s32[1,192,64]{1,2,0:T(8,128)} %param.10) | copy-start | bytes 147460
  0.0 35.3 %copy-start.5 = (s32[1,192]{1,0:T(1,128)S(1)}, s32[1,192]{1,0:T(1,128)}, u32[]{:S(2)}) copy-start(s32[1,192]{1,0:T(1,128)} %param.11) | copy-start | bytes 2308
  0.0 38.1 %copy-start.1 = (bf16[3072,1,3,128]{3,0,2,1:T(8,128)(2,1)S(1)}, bf16[3072,1,3,128]{3,0,2,1:T(8,128)(2,1)}, u32[]{:S(2)}) copy-start(bf16[3072,1,3,128]{3,0,2,1:T(8,128)(2,1)} %param.7) | copy-start | bytes 7077892
  0.0 38.0 %copy-start.3 = (f32[1,128]{1,0:T(1,128)S(1)}, f32[1,128]{1,0:T(1,128)}, u32[]{:S(2)}) copy-start(f32[1,128]{1,0:T(1,128)} %refs_3_.3) | copy-start | bytes 1540
  0.0 38.0 %copy-start.4 = (f32[1,128]{1,0:T(1,128)S(1)}, f32[1,128]{1,0:T(1,128)}, u32[]{:S(2)}) copy-start(f32[1,128]{1,0:T(1,128)} %refs_4_.3) | copy-start | bytes 1540
  0.0 12.8 %collective-permute-start.2 = (bf16[48,3072]{1,0:T(8,128)(2,1)}, bf16[48,3072]{1,0:T(8,128)(2,1)S(1)}, u32[]{:S(2)}, u32[]{:S(2)}) collective-permute-start(bf16[48,3072]{1,0:T(8,128)(2,1)} %refs_0_.1), channel_id=1, source_target_pairs={{0,96},{32,0},{64,32},{96,64},{128,224},{160,128},{192,160},{224,1... | collective-permute-start | bytes 884744 | tf_op jit(solution)/shard_map/ppermute | solution.py:34
  5.6 9.3 %collective-permute-start.3 = (bf16[48,3072]{1,0:T(8,128)(2,1)}, bf16[48,3072]{1,0:T(8,128)(2,1)S(1)}, u32[]{:S(2)}, u32[]{:S(2)}) collective-permute-start(bf16[48,3072]{1,0:T(8,128)(2,1)} %refs_0_.1), channel_id=1, source_target_pairs={{0,64},{32,96},{64,0},{96,32},{128,192},{160,224},{192,128},{224,1... | collective-permute-start | bytes 884744 | tf_op jit(solution)/shard_map/ppermute | solution.py:34
  7.9 12.1 %collective-permute-start = (bf16[48,3072]{1,0:T(8,128)(2,1)}, bf16[48,3072]{1,0:T(8,128)(2,1)S(1)}, u32[]{:S(2)}, u32[]{:S(2)}) collective-permute-start(bf16[48,3072]{1,0:T(8,128)(2,1)} %refs_0_.1), channel_id=1, source_target_pairs={{0,32},{32,64},{64,96},{96,0},{128,160},{160,192},{192,224},{224,1... | collective-permute-start | bytes 884744 | tf_op jit(solution)/shard_map/ppermute | solution.py:34
  15.7 13.6 %collective-permute-start.6 = (bf16[96,3072]{1,0:T(8,128)(2,1)}, bf16[96,3072]{1,0:T(8,128)(2,1)}, u32[]{:S(2)}, u32[]{:S(2)}) collective-permute-start(bf16[96,3072]{1,0:T(8,128)(2,1)} %constant_dynamic-update-slice_fusion.2), channel_id=1, source_target_pairs={{0,384},{32,416},{64,448},{96,480},{128,0},{160,32},{192,64},{224,... | collective-permute-start | bytes 1769480 | tf_op jit(solution)/shard_map/ppermute | solution.py:34
  20.8 12.4 %collective-permute-start.5 = (bf16[96,3072]{1,0:T(8,128)(2,1)}, bf16[96,3072]{1,0:T(8,128)(2,1)}, u32[]{:S(2)}, u32[]{:S(2)}) collective-permute-start(bf16[96,3072]{1,0:T(8,128)(2,1)} %constant_dynamic-update-slice_fusion), channel_id=1, source_target_pairs={{0,128},{32,160},{64,192},{96,224},{128,256},{160,288},{192,320},{... | collective-permute-start | bytes 1769480 | tf_op jit(solution)/shard_map/ppermute | solution.py:34
  22.7 19.5 %collective-permute-start.4 = (bf16[96,3072]{1,0:T(8,128)(2,1)}, bf16[96,3072]{1,0:T(8,128)(2,1)}, u32[]{:S(2)}, u32[]{:S(2)}) collective-permute-start(bf16[96,3072]{1,0:T(8,128)(2,1)} %constant_dynamic-update-slice_fusion.2), channel_id=1, source_target_pairs={{0,128},{32,160},{64,192},{96,224},{128,256},{160,288},{192,320},{... | collective-permute-start | bytes 1769480 | tf_op jit(solution)/shard_map/ppermute | solution.py:34
  25.0 17.3 %collective-permute-start.1 = (bf16[96,3072]{1,0:T(8,128)(2,1)}, bf16[96,3072]{1,0:T(8,128)(2,1)}, u32[]{:S(2)}, u32[]{:S(2)}) collective-permute-start(bf16[96,3072]{1,0:T(8,128)(2,1)} %constant_dynamic-update-slice_fusion), channel_id=1, source_target_pairs={{0,384},{32,416},{64,448},{96,480},{128,0},{160,32},{192,64},{224,... | collective-permute-start | bytes 1769480 | tf_op jit(solution)/shard_map/ppermute | solution.py:34
  29.2 15.4 %collective-permute-start.8 = (bf16[96,3072]{1,0:T(8,128)(2,1)}, bf16[96,3072]{1,0:T(8,128)(2,1)}, u32[]{:S(2)}, u32[]{:S(2)}) collective-permute-start(bf16[96,3072]{1,0:T(8,128)(2,1)} %collective-permute-done.6.refs_5_), channel_id=1, source_target_pairs={{0,384},{32,416},{64,448},{96,480},{128,0},{160,32},{192,64},{224,... | collective-permute-start | bytes 1769480 | tf_op jit(solution)/shard_map/ppermute | solution.py:34
  33.2 12.6 %collective-permute-start.7 = (bf16[96,3072]{1,0:T(8,128)(2,1)}, bf16[96,3072]{1,0:T(8,128)(2,1)}, u32[]{:S(2)}, u32[]{:S(2)}) collective-permute-start(bf16[96,3072]{1,0:T(8,128)(2,1)} %collective-permute-done.5.refs_4_), channel_id=1, source_target_pairs={{0,128},{32,160},{64,192},{96,224},{128,256},{160,288},{192,320},{... | collective-permute-start | bytes 1769480 | tf_op jit(solution)/shard_map/ppermute | solution.py:34
  38.1 1.0 copy-start.2
  48.2 16.9 %collective-permute-start.9 = (bf16[768,256]{1,0:T(8,128)(2,1)S(1)}, bf16[768,256]{1,0:T(8,128)(2,1)S(1)}, u32[]{:S(2)}, u32[]{:S(2)}) collective-permute-start(bf16[768,256]{1,0:T(8,128)(2,1)S(1)} %get-tuple-element.46), channel_id=1, source_target_pairs={{0,1},{1,0},{2,3},{3,2},{4,5},{5,4},{6,7},{7,6},{8,9},{9,8},{10,11... | collective-permute-start | bytes 1179656 | tf_op jit(solution)/shard_map/ppermute | solution.py:38
  54.1 15.8 %collective-permute-start.13 = (bf16[768,256]{1,0:T(8,128)(2,1)S(1)}, bf16[768,256]{1,0:T(8,128)(2,1)S(1)}, u32[]{:S(2)}, u32[]{:S(2)}) collective-permute-start(bf16[768,256]{1,0:T(8,128)(2,1)S(1)} %get-tuple-element.46), channel_id=1, source_target_pairs={{0,2},{1,31},{2,4},{3,1},{4,6},{5,3},{6,8},{7,5},{8,10},{9,7},{10,... | collective-permute-start | bytes 1179656 | tf_op jit(solution)/shard_map/ppermute | solution.py:48
  65.2 9.7 %collective-permute-start.10 = (bf16[768,256]{1,0:T(8,128)(2,1)S(1)}, bf16[768,256]{1,0:T(8,128)(2,1)S(1)}, u32[]{:S(2)}, u32[]{:S(2)}) collective-permute-start(bf16[768,256]{1,0:T(8,128)(2,1)S(1)} %collective-permute-done.9), channel_id=1, source_target_pairs={{0,2},{1,31},{2,4},{3,1},{4,6},{5,3},{6,8},{7,5},{8,10},{9,7},{10,... | collective-permute-start | bytes 1179656 | tf_op jit(solution)/shard_map/ppermute | solution.py:48
  69.8 11.2 %collective-permute-start.14 = (bf16[768,256]{1,0:T(8,128)(2,1)S(1)}, bf16[768,256]{1,0:T(8,128)(2,1)S(1)}, u32[]{:S(2)}, u32[]{:S(2)}) collective-permute-start(bf16[768,256]{1,0:T(8,128)(2,1)S(1)} %collective-permute-done.13), channel_id=1, source_target_pairs={{0,2},{1,31},{2,4},{3,1},{4,6},{5,3},{6,8},{7,5},{8,10},{9,7},{10,... | collective-permute-start | bytes 1179656 | tf_op jit(solution)/shard_map/ppermute | solution.py:48
  74.9 9.7 %collective-permute-start.12 = (bf16[768,128]{1,0:T(8,128)(2,1)S(1)}, bf16[768,128]{1,0:T(8,128)(2,1)S(1)}, u32[]{:S(2)}, u32[]{:S(2)}) collective-permute-start(bf16[768,128]{1,0:T(8,128)(2,1)S(1)} %get-tuple-element.48), channel_id=1, source_target_pairs={{0,1},{1,0},{2,3},{3,2},{4,5},{5,4},{6,7},{7,6},{8,9},{9,8},{10,11... | collective-permute-start | bytes 589832 | tf_op jit(solution)/shard_map/ppermute | solution.py:38
  77.3 8.8 %collective-permute-start.11 = (bf16[768,256]{1,0:T(8,128)(2,1)S(1)}, bf16[768,256]{1,0:T(8,128)(2,1)S(1)}, u32[]{:S(2)}, u32[]{:S(2)}) collective-permute-start(bf16[768,256]{1,0:T(8,128)(2,1)S(1)} %collective-permute-done.10), channel_id=1, source_target_pairs={{0,2},{1,31},{2,4},{3,1},{4,6},{5,3},{6,8},{7,5},{8,10},{9,7},{10,... | collective-permute-start | bytes 1179656 | tf_op jit(solution)/shard_map/ppermute | solution.py:48
  81.0 11.7 %collective-permute-start.15 = (bf16[768,256]{1,0:T(8,128)(2,1)S(1)}, bf16[768,256]{1,0:T(8,128)(2,1)S(1)}, u32[]{:S(2)}, u32[]{:S(2)}) collective-permute-start(bf16[768,256]{1,0:T(8,128)(2,1)S(1)} %collective-permute-done.14), channel_id=1, source_target_pairs={{0,2},{1,31},{2,4},{3,1},{4,6},{5,3},{6,8},{7,5},{8,10},{9,7},{10,... | collective-permute-start | bytes 1179656 | tf_op jit(solution)/shard_map/ppermute | solution.py:48
  86.1 9.9 %collective-permute-start.17 = (bf16[768,256]{1,0:T(8,128)(2,1)S(1)}, bf16[768,256]{1,0:T(8,128)(2,1)S(1)}, u32[]{:S(2)}, u32[]{:S(2)}) collective-permute-start(bf16[768,256]{1,0:T(8,128)(2,1)S(1)} %collective-permute-done.11), channel_id=1, source_target_pairs={{0,2},{1,31},{2,4},{3,1},{4,6},{5,3},{6,8},{7,5},{8,10},{9,7},{10,... | collective-permute-start | bytes 1179656 | tf_op jit(solution)/shard_map/ppermute | solution.py:48
  92.7 9.3 %collective-permute-start.16 = (bf16[768,256]{1,0:T(8,128)(2,1)S(1)}, bf16[768,256]{1,0:T(8,128)(2,1)S(1)}, u32[]{:S(2)}, u32[]{:S(2)}) collective-permute-start(bf16[768,256]{1,0:T(8,128)(2,1)S(1)} %collective-permute-done.15), channel_id=1, source_target_pairs={{0,2},{1,31},{2,4},{3,1},{4,6},{5,3},{6,8},{7,5},{8,10},{9,7},{10,... | collective-permute-start | bytes 1179656 | tf_op jit(solution)/shard_map/ppermute | solution.py:48
  96.1 9.7 %collective-permute-start.19 = (bf16[768,256]{1,0:T(8,128)(2,1)S(1)}, bf16[768,256]{1,0:T(8,128)(2,1)S(1)}, u32[]{:S(2)}, u32[]{:S(2)}) collective-permute-start(bf16[768,256]{1,0:T(8,128)(2,1)S(1)} %collective-permute-done.17), channel_id=1, source_target_pairs={{0,2},{1,31},{2,4},{3,1},{4,6},{5,3},{6,8},{7,5},{8,10},{9,7},{10,... | collective-permute-start | bytes 1179656 | tf_op jit(solution)/shard_map/ppermute | solution.py:48
  102.0 9.7 %collective-permute-start.18 = (bf16[768,256]{1,0:T(8,128)(2,1)S(1)}, bf16[768,256]{1,0:T(8,128)(2,1)S(1)}, u32[]{:S(2)}, u32[]{:S(2)}) collective-permute-start(bf16[768,256]{1,0:T(8,128)(2,1)S(1)} %collective-permute-done.16), channel_id=1, source_target_pairs={{0,2},{1,31},{2,4},{3,1},{4,6},{5,3},{6,8},{7,5},{8,10},{9,7},{10,... | collective-permute-start | bytes 1179656 | tf_op jit(solution)/shard_map/ppermute | solution.py:48
  105.8 9.7 %collective-permute-start.21 = (bf16[768,256]{1,0:T(8,128)(2,1)S(1)}, bf16[768,256]{1,0:T(8,128)(2,1)S(1)}, u32[]{:S(2)}, u32[]{:S(2)}) collective-permute-start(bf16[768,256]{1,0:T(8,128)(2,1)S(1)} %collective-permute-done.19), channel_id=1, source_target_pairs={{0,2},{1,31},{2,4},{3,1},{4,6},{5,3},{6,8},{7,5},{8,10},{9,7},{10,... | collective-permute-start | bytes 1179656 | tf_op jit(solution)/shard_map/ppermute | solution.py:48
  111.7 9.7 %collective-permute-start.20 = (bf16[768,256]{1,0:T(8,128)(2,1)S(1)}, bf16[768,256]{1,0:T(8,128)(2,1)S(1)}, u32[]{:S(2)}, u32[]{:S(2)}) collective-permute-start(bf16[768,256]{1,0:T(8,128)(2,1)S(1)} %collective-permute-done.18), channel_id=1, source_target_pairs={{0,2},{1,31},{2,4},{3,1},{4,6},{5,3},{6,8},{7,5},{8,10},{9,7},{10,... | collective-permute-start | bytes 1179656 | tf_op jit(solution)/shard_map/ppermute | solution.py:48
  115.5 9.7 %collective-permute-start.23 = (bf16[768,256]{1,0:T(8,128)(2,1)S(1)}, bf16[768,256]{1,0:T(8,128)(2,1)S(1)}, u32[]{:S(2)}, u32[]{:S(2)}) collective-permute-start(bf16[768,256]{1,0:T(8,128)(2,1)S(1)} %collective-permute-done.21), channel_id=1, source_target_pairs={{0,2},{1,31},{2,4},{3,1},{4,6},{5,3},{6,8},{7,5},{8,10},{9,7},{10,... | collective-permute-start | bytes 1179656 | tf_op jit(solution)/shard_map/ppermute | solution.py:48
  121.4 9.7 %collective-permute-start.22 = (bf16[768,256]{1,0:T(8,128)(2,1)S(1)}, bf16[768,256]{1,0:T(8,128)(2,1)S(1)}, u32[]{:S(2)}, u32[]{:S(2)}) collective-permute-start(bf16[768,256]{1,0:T(8,128)(2,1)S(1)} %collective-permute-done.20), channel_id=1, source_target_pairs={{0,2},{1,31},{2,4},{3,1},{4,6},{5,3},{6,8},{7,5},{8,10},{9,7},{10,... | collective-permute-start | bytes 1179656 | tf_op jit(solution)/shard_map/ppermute | solution.py:48
  125.2 9.7 %collective-permute-start.25 = (bf16[768,256]{1,0:T(8,128)(2,1)S(1)}, bf16[768,256]{1,0:T(8,128)(2,1)S(1)}, u32[]{:S(2)}, u32[]{:S(2)}) collective-permute-start(bf16[768,256]{1,0:T(8,128)(2,1)S(1)} %collective-permute-done.23), channel_id=1, source_target_pairs={{0,2},{1,31},{2,4},{3,1},{4,6},{5,3},{6,8},{7,5},{8,10},{9,7},{10,... | collective-permute-start | bytes 1179656 | tf_op jit(solution)/shard_map/ppermute | solution.py:48
  131.1 9.7 %collective-permute-start.24 = (bf16[768,256]{1,0:T(8,128)(2,1)S(1)}, bf16[768,256]{1,0:T(8,128)(2,1)S(1)}, u32[]{:S(2)}, u32[]{:S(2)}) collective-permute-start(bf16[768,256]{1,0:T(8,128)(2,1)S(1)} %collective-permute-done.22), channel_id=1, source_target_pairs={{1,31},{3,1},{5,3},{7,5},{9,7},{11,9},{13,11},{15,13},{17,15},{19,... | collective-permute-start | bytes 1179656 | tf_op jit(solution)/shard_map/ppermute | solution.py:48
  135.0 9.1 %collective-permute-start.26 = (bf16[768,256]{1,0:T(8,128)(2,1)S(1)}, bf16[768,256]{1,0:T(8,128)(2,1)S(1)}, u32[]{:S(2)}, u32[]{:S(2)}) collective-permute-start(bf16[768,256]{1,0:T(8,128)(2,1)S(1)} %collective-permute-done.25), channel_id=1, source_target_pairs={{1,31},{3,1},{5,3},{7,5},{9,7},{11,9},{13,11},{15,13},{17,15},{19,... | collective-permute-start | bytes 1179656 | tf_op jit(solution)/shard_map/ppermute | solution.py:48
  145.5 4.2 %collective-permute-start.27 = (f32[6,128,256]{2,1,0:T(8,128)S(1)}, f32[6,128,256]{2,1,0:T(8,128)S(1)}, u32[]{:S(2)}, u32[]{:S(2)}) collective-permute-start(f32[6,128,256]{2,1,0:T(8,128)S(1)} %get-tuple-element.64), channel_id=1, source_target_pairs={{0,1},{1,0},{2,3},{3,2},{4,5},{5,4},{6,7},{7,6},{8,9},{9,8},{10,11... | collective-permute-start | bytes 2359304 | tf_op jit(solution)/shard_map/ppermute | solution.py:38

commit v9 on v8

--- a/solution.py
+++ b/solution.py
@@ -34,6 +34,32 @@
     return lax.ppermute(block, MESH_AXES, plane_perm(phase, shift))
 
 
+def join_kernel(upper, lower, out, done):
+    rows = upper.shape[0]
+    copies = [
+        pltpu.make_async_copy(upper, out.at[pl.ds(0, rows), :], done.at[0]),
+        pltpu.make_async_copy(lower, out.at[pl.ds(rows, rows), :], done.at[1]),
+    ]
+    for copy in copies:
+        copy.start()
+    for copy in copies:
+        copy.wait()
+
+
+def join(upper, lower):
+    rows, width = upper.shape
+    anywhere = pl.BlockSpec(memory_space=pl.ANY)
+    return pl.pallas_call(
+        join_kernel,
+        out_shape=jax.ShapeDtypeStruct((2 * rows, width), upper.dtype),
+        in_specs=[anywhere, anywhere],
+        out_specs=anywhere,
+        scratch_shapes=[pltpu.SemaphoreType.DMA((2,))],
+        compiler_params=pltpu.CompilerParams(vmem_limit_bytes=1024 * 1024),
+        name="join",
+    )(upper, lower)
+
+
 def swap_cores(block):
     return lax.ppermute(block, "bal", [(at, at ^ 1) for at in range(32)])
 
@@ -51,7 +77,7 @@
 def project_kernel(shares, place, *refs):
     count = len(shares)
     blocks = refs[:count]
-    weight, q_gain, k_gain = refs[count : count + 3]
+    weight, gains = refs[count : count + 2]
     q_out, kv_out, q_held, kv_held, leave = refs[-5:]
     first = place[0]
     second = place[1]
@@ -65,8 +91,8 @@
     rows = jnp.concatenate([block[...] for block in blocks], axis=0)
     whole = jnp.concatenate([weight[at] for at in range(3)], axis=1)
     proj = jnp.dot(rows, whole, preferred_element_type=jnp.float32)
-    q_held[...] = normalize(proj[:, :HEAD], q_gain[...])
-    kv_held[:, :HEAD] = normalize(proj[:, HEAD : 2 * HEAD], k_gain[...])
+    q_held[...] = normalize(proj[:, :HEAD], gains[0:1, :])
+    kv_held[:, :HEAD] = normalize(proj[:, HEAD : 2 * HEAD], gains[1:2, :])
     kv_held[:, HEAD:] = proj[:, 2 * HEAD :].astype(jnp.bfloat16)
     row = 0
     for shift, pieces in shares:
@@ -81,7 +107,7 @@
     pltpu.make_async_copy(kv_held, kv_held, leave.at[1]).wait()
 
 
-def project(shares, blocks, weight, q_gain, k_gain, place, begun=()):
+def project(shares, blocks, weight, gains, place, begun=()):
     rows = 16 * PIECE
     count = len(blocks)
     rows_here = sum(len(pieces) for _, pieces in shares) * PIECE
@@ -92,17 +118,17 @@
             jax.ShapeDtypeStruct((rows, HEAD), jnp.bfloat16),
             jax.ShapeDtypeStruct((rows, 2 * HEAD), jnp.bfloat16),
         ),
-        in_specs=[SMEM] + [VMEM] * (count + 3) + [anywhere] * len(begun),
+        in_specs=[SMEM] + [VMEM] * (count + 2) + [anywhere] * len(begun),
         out_specs=(anywhere, anywhere),
         scratch_shapes=[
             pltpu.VMEM((rows_here, HEAD), jnp.bfloat16),
             pltpu.VMEM((rows_here, 2 * HEAD), jnp.bfloat16),
             pltpu.SemaphoreType.DMA((2,)),
         ],
-        input_output_aliases={count + 4: 0, count + 5: 1} if begun else {},
+        input_output_aliases={count + 3: 0, count + 4: 1} if begun else {},
         compiler_params=pltpu.CompilerParams(vmem_limit_bytes=20 * 1024 * 1024),
         name="project",
-    )(place, *blocks, weight, q_gain, k_gain, *begun)
+    )(place, *blocks, weight, gains, *begun)
 
 
 def attend_kernel(scale, first_call, last_call, call, blocks, place, pairs, counts, q, *refs):
@@ -262,46 +288,41 @@
         )
     ).astype(jnp.int32)
     slots = 16 * PIECE // TILE
-    pairs, counts = list_pairs(CALLS, key_tiles[0], key_counts, place, slots)
-
     before = send(tokens, 1, 1)
     after = send(tokens, 1, -1)
     across = send(tokens, 1, 2)
-    low = jnp.concatenate((tokens, before), axis=0)
+    low = join(tokens, before)
     before_low = send(low, 2, 1)
-    high = jnp.concatenate((after, across), axis=0)
+    high = join(after, across)
     after_high = send(high, 2, -1)
     after_low = send(low, 2, -1)
     before_high = send(high, 2, 1)
     across_low = send(before_low, 2, 1)
     across_high = send(after_high, 2, -1)
 
+    gains = jnp.concatenate((q_gain, k_gain), axis=0)
     weight = jnp.transpose(qkv_weight[:, 0], (1, 0, 2))
     low_pieces, high_pieces = (0, 3), (1, 2)
     begun = project(
-        ((0, (0,)), (0, (3,)), (0, (1,)), (0, (2,)), (3, low_pieces), (1, high_pieces)),
-        (tokens, before, after, across, before_low, after_high),
+        ((0, low_pieces), (0, high_pieces), (3, low_pieces), (1, high_pieces)),
+        (low, high, before_low, after_high),
         weight,
-        q_gain,
-        k_gain,
+        gains,
         place,
     )
     begun = project(
         ((1, low_pieces), (3, high_pieces)),
         (after_low, before_high),
         weight,
-        q_gain,
-        k_gain,
+        gains,
         place,
         begun,
     )
-    begun, (pairs, counts) = lax.optimization_barrier((begun, (pairs, counts)))
     queries, keys_values = project(
         ((2, low_pieces), (2, high_pieces)),
         (across_low, across_high),
         weight,
-        q_gain,
-        k_gain,
+        gains,
         place,
         begun,
     )
@@ -316,6 +337,9 @@
         if sums is not None:
             same[-1], sums = lax.optimization_barrier((same[-1], sums))
         if step == 1:
+            key_tiles, other[0] = lax.optimization_barrier((key_tiles, other[0]))
+            pairs, counts = list_pairs(CALLS, key_tiles[0], key_counts, place, slots)
+            same[1], pairs, counts = lax.optimization_barrier((same[1], pairs, counts))
             queries, other[1] = lax.optimization_barrier((queries, other[1]))
             other_queries = swap_cores(queries)
         if step == 2:

time: 165 us -> 165 us (level)
  Pallas kernels: 21.4 us -> 27.9 us
  local copies, waits for them, and re-layouts: 5.82 us -> 1.9 us
  blocking collectives: 13.5 us -> 10.5 us
  starting transfers between devices: 110 us -> 107 us
  waiting for transfers between devices: 12.6 us -> 15.4 us
    ppermute x9, waiting for transfers between devices: 3.88 us -> 8.39 us  [send(): return lax.ppermute(block, MESH_AXES, plane_perm(phase, shift))]
    pallas_call x7, Pallas kernels: 10.9 us -> 15 us  [attend(): pl.pallas_call(functools.partial(attend_kernel, scale, first_call, last_c...]
    ppermute x16, starting transfers between devices: 71 us -> 67.6 us  [pass_on(): return lax.ppermute(block, 'bal', pairs)]
    all_to_all x1, blocking collectives: 13.5 us -> 10.5 us  [on_device(): lax.all_to_all(result.reshape(slots * TILE, HEAD), 'seq', split_axis=0, c...]
    unnamed x14 -> x8, local copies, waits for them, and re-layouts: 3.42 us -> 0.97 us
    ppermute x16, waiting for transfers between devices: 6.71 us -> 4.78 us  [pass_on(): return lax.ppermute(block, 'bal', pairs)]
  transfers between devices with their start and end apart: 28 -> 28, of which waited for: 8 -> 9; matrix products, arithmetic and copies ran while one was open for 3% -> 1% of each run, Pallas kernels for 11% -> 14%
where the time goes in v9:
time: 165 us; the launch traced here: 164 us
  starting transfers between devices  107 us (65%)
  Pallas kernels  27.9 us (17%)
  waiting for transfers between devices  15.4 us (9%)
  blocking collectives  10.5 us (6%)
  local copies, waits for them, and re-layouts  1.9 us (1%)
    ppermute x16, starting transfers between devices, pass_on(): return lax.ppermute(block, 'bal', pairs)  67.6 us
    ppermute x9, starting transfers between devices, send(): return lax.ppermute(block, MESH_AXES, plane_perm(phase, shift))  28.5 us
    pallas_call x7, Pallas kernels, attend(): pl.pallas_call(functools.partial(attend_kernel, scale, first_call, last_c...  15 us
    ppermute x3, starting transfers between devices, swap_cores(): return lax.ppermute(block, 'bal', [(at, at ^ 1) for at in range(32)])  10.7 us
    all_to_all x1, blocking collectives, on_device(): lax.all_to_all(result.reshape(slots * TILE, HEAD), 'seq', split_axis=0, c...  10.5 us
    pallas_call x3, Pallas kernels, project(): pl.pallas_call(functools.partial(project_kernel, shares), out_shape=(jax....  9.37 us
    ppermute x9, waiting for transfers between devices, send(): return lax.ppermute(block, MESH_AXES, plane_perm(phase, shift))  8.39 us
    ppermute x16, waiting for transfers between devices, pass_on(): return lax.ppermute(block, 'bal', pairs)  4.78 us
  transfers between devices with their start and end apart: 28, of which 9 were waited for; matrix products, arithmetic and copies ran while one was open for 1% of the time, Pallas kernels for 14%

profile of v9, /device:TPU:1, one launch (start us, length us, event | category | flops | bytes accessed | tf_op | source)
XLA Modules:
  0.0 164.1 jit_solution(15125931410999587022)
XLA Ops:
  0.0 5.6 %collective-permute-start.3 = (bf16[48,3072]{1,0:T(8,128)(2,1)}, bf16[48,3072]{1,0:T(8,128)(2,1)S(1)}, u32[]{:S(2)}, u32[]{:S(2)}) collective-permute-start(bf16[48,3072]{1,0:T(8,128)(2,1)} %upper.1), channel_id=1, source_target_pairs={{0,96},{32,0},{64,32},{96,64},{128,224},{160,128},{192,160},{224,1... | collective-permute-start | bytes 884744 | tf_op jit(solution)/shard_map/ppermute | solution.py:34
  5.6 2.3 %collective-permute-start.4 = (bf16[48,3072]{1,0:T(8,128)(2,1)}, bf16[48,3072]{1,0:T(8,128)(2,1)S(1)}, u32[]{:S(2)}, u32[]{:S(2)}) collective-permute-start(bf16[48,3072]{1,0:T(8,128)(2,1)} %upper.1), channel_id=1, source_target_pairs={{0,64},{32,96},{64,0},{96,32},{128,192},{160,224},{192,128},{224,1... | collective-permute-start | bytes 884744 | tf_op jit(solution)/shard_map/ppermute | solution.py:34
  7.9 2.6 %collective-permute-start = (bf16[48,3072]{1,0:T(8,128)(2,1)}, bf16[48,3072]{1,0:T(8,128)(2,1)S(1)}, u32[]{:S(2)}, u32[]{:S(2)}) collective-permute-start(bf16[48,3072]{1,0:T(8,128)(2,1)} %upper.1), channel_id=1, source_target_pairs={{0,32},{32,64},{64,96},{96,0},{128,160},{160,192},{192,224},{224,1... | collective-permute-start | bytes 884744 | tf_op jit(solution)/shard_map/ppermute | solution.py:34
  10.5 2.3 %collective-permute-done.3.upper = bf16[48,3072]{1,0:T(8,128)(2,1)S(1)} collective-permute-done((bf16[48,3072]{1,0:T(8,128)(2,1)}, bf16[48,3072]{1,0:T(8,128)(2,1)S(1)}, u32[]{:S(2)}, u32[]{:S(2)}) %collective-permute-start.3) | collective-permute-done | bytes 294944 | tf_op jit(solution)/shard_map/ppermute | solution.py:34
  12.8 2.1 %collective-permute-done.4.lower = bf16[48,3072]{1,0:T(8,128)(2,1)S(1)} collective-permute-done((bf16[48,3072]{1,0:T(8,128)(2,1)}, bf16[48,3072]{1,0:T(8,128)(2,1)S(1)}, u32[]{:S(2)}, u32[]{:S(2)}) %collective-permute-start.4) | collective-permute-done | bytes 294944 | tf_op jit(solution)/shard_map/ppermute | solution.py:34
  14.9 0.1 join.3.refs_1_
  15.0 4.4 %collective-permute-start.5 = (bf16[96,3072]{1,0:T(8,128)(2,1)S(1)}, bf16[96,3072]{1,0:T(8,128)(2,1)}, u32[]{:S(2)}, u32[]{:S(2)}) collective-permute-start(bf16[96,3072]{1,0:T(8,128)(2,1)S(1)} %join.3.refs_1_), channel_id=1, source_target_pairs={{0,384},{32,416},{64,448},{96,480},{128,0},{160,32},{192,64},{224,... | collective-permute-start | bytes 1769480 | tf_op jit(solution)/shard_map/ppermute | solution.py:34
  19.4 0.0 collective-permute-done.lower
  19.4 0.0 copy-start.2
  19.5 1.0 copy-done.2
  20.4 0.8 join.2.refs_0_
  21.3 1.9 %collective-permute-start.1 = (bf16[96,3072]{1,0:T(8,128)(2,1)}, bf16[96,3072]{1,0:T(8,128)(2,1)}, u32[]{:S(2)}, u32[]{:S(2)}) collective-permute-start(bf16[96,3072]{1,0:T(8,128)(2,1)} %join.2.refs_0_), channel_id=1, source_target_pairs={{0,128},{32,160},{64,192},{96,224},{128,256},{160,288},{192,320},{... | collective-permute-start | bytes 1769480 | tf_op jit(solution)/shard_map/ppermute | solution.py:34
  23.2 2.8 %collective-permute-start.8 = (bf16[96,3072]{1,0:T(8,128)(2,1)S(1)}, bf16[96,3072]{1,0:T(8,128)(2,1)}, u32[]{:S(2)}, u32[]{:S(2)}) collective-permute-start(bf16[96,3072]{1,0:T(8,128)(2,1)S(1)} %join.3.refs_1_), channel_id=1, source_target_pairs={{0,128},{32,160},{64,192},{96,224},{128,256},{160,288},{192,320},{... | collective-permute-start | bytes 1769480 | tf_op jit(solution)/shard_map/ppermute | solution.py:34
  26.0 3.7 %collective-permute-start.7 = (bf16[96,3072]{1,0:T(8,128)(2,1)}, bf16[96,3072]{1,0:T(8,128)(2,1)}, u32[]{:S(2)}, u32[]{:S(2)}) collective-permute-start(bf16[96,3072]{1,0:T(8,128)(2,1)} %join.2.refs_0_), channel_id=1, source_target_pairs={{0,384},{32,416},{64,448},{96,480},{128,0},{160,32},{192,64},{224,... | collective-permute-start | bytes 1769480 | tf_op jit(solution)/shard_map/ppermute | solution.py:34
  29.7 0.0 collective-permute-done.5.refs_3_
  29.7 3.4 %collective-permute-start.6 = (bf16[96,3072]{1,0:T(8,128)(2,1)}, bf16[96,3072]{1,0:T(8,128)(2,1)}, u32[]{:S(2)}, u32[]{:S(2)}) collective-permute-start(bf16[96,3072]{1,0:T(8,128)(2,1)} %collective-permute-done.5.refs_3_), channel_id=1, source_target_pairs={{0,384},{32,416},{64,448},{96,480},{128,0},{160,32},{192,64},{224,... | collective-permute-start | bytes 1769480 | tf_op jit(solution)/shard_map/ppermute | solution.py:34
  33.1 0.6 collective-permute-done.1.refs_2_
  33.7 1.9 %collective-permute-start.2 = (bf16[96,3072]{1,0:T(8,128)(2,1)}, bf16[96,3072]{1,0:T(8,128)(2,1)}, u32[]{:S(2)}, u32[]{:S(2)}) collective-permute-start(bf16[96,3072]{1,0:T(8,128)(2,1)} %collective-permute-done.1.refs_2_), channel_id=1, source_target_pairs={{0,128},{32,160},{64,192},{96,224},{128,256},{160,288},{192,320},{... | collective-permute-start | bytes 1769480 | tf_op jit(solution)/shard_map/ppermute | solution.py:34
  35.7 0.1 stack.27.place
  35.8 0.7 pad_maximum_fusion.1.refs_5_.refs_3_
  36.4 3.7 %project.3 = (bf16[768,128]{1,0:T(8,128)(2,1)S(1)}, bf16[768,256]{1,0:T(8,128)(2,1)}) custom-call(s32[6]{0:T(128)S(1)} %stack.27.place, bf16[96,3072]{1,0:T(8,128)(2,1)} %join.2.refs_0_, bf16[96,3072]{1,0:T(8,128)(2,1)S(1)} %join.3.refs_1_, bf16[96,3072]{1,0:T(8,128)(2,1)} %collective-permute-done.1.refs_2_, ...), custom_call_target="tpu_custom_call" | custom-call | tf_op jit(solution)/shard_map/project/pallas_call | solution.py:115
  40.2 0.0 collective-permute-done.7.refs_0_
  40.2 2.8 %project.4 = (bf16[768,128]{1,0:T(8,128)(2,1)S(1)}, bf16[768,256]{1,0:T(8,128)(2,1)}) custom-call(s32[6]{0:T(128)S(1)} %stack.27.place, bf16[96,3072]{1,0:T(8,128)(2,1)} %collective-permute-done.7.refs_0_, bf16[96,3072]{1,0:T(8,128)(2,1)} %collective-permute-done.8.refs_1_, ...), custom_call_target="tpu_custom_call", output_to_operand_aliasing={{0}: (5, {}), {1}: (6, {})} | custom-call | tf_op jit(solution)/shard_map/project/pallas_call | solution.py:115
  43.0 0.6 collective-permute-done.6.refs_1_
  43.6 2.8 %collective-permute-done.2.refs_0_ = bf16[96,3072]{1,0:T(8,128)(2,1)} collective-permute-done((bf16[96,3072]{1,0:T(8,128)(2,1)}, bf16[96,3072]{1,0:T(8,128)(2,1)}, u32[]{:S(2)}, u32[]{:S(2)}) %collective-permute-start.2) | collective-permute-done | bytes 589856 | tf_op jit(solution)/shard_map/ppermute | solution.py:34
  46.3 2.8 %project.5 = (bf16[768,128]{1,0:T(8,128)(2,1)S(1)}, bf16[768,256]{1,0:T(8,128)(2,1)}) custom-call(s32[6]{0:T(128)S(1)} %stack.27.place, bf16[96,3072]{1,0:T(8,128)(2,1)} %collective-permute-done.2.refs_0_, bf16[96,3072]{1,0:T(8,128)(2,1)} %collective-permute-done.6.refs_1_, ...), custom_call_target="tpu_custom_call", output_to_operand_aliasing={{0}: (5, {}), {1}: (6, {})} | custom-call | tf_op jit(solution)/shard_map/project/pallas_call | solution.py:115
  49.2 6.4 %collective-permute-start.10 = (bf16[768,256]{1,0:T(8,128)(2,1)}, bf16[768,256]{1,0:T(8,128)(2,1)S(1)}, u32[]{:S(2)}, u32[]{:S(2)}) collective-permute-start(bf16[768,256]{1,0:T(8,128)(2,1)} %get-tuple-element.39), channel_id=1, source_target_pairs={{0,1},{1,0},{2,3},{3,2},{4,5},{5,4},{6,7},{7,6},{8,9},{9,8},{10,11... | collective-permute-start | bytes 1179656 | tf_op jit(solution)/shard_map/ppermute | solution.py:64
  55.6 10.5 %collective-permute-start.9 = (bf16[768,256]{1,0:T(8,128)(2,1)}, bf16[768,256]{1,0:T(8,128)(2,1)S(1)}, u32[]{:S(2)}, u32[]{:S(2)}) collective-permute-start(bf16[768,256]{1,0:T(8,128)(2,1)} %get-tuple-element.39), channel_id=1, source_target_pairs={{0,2},{1,31},{2,4},{3,1},{4,6},{5,3},{6,8},{7,5},{8,10},{9,7},{10,... | collective-permute-start | bytes 1179656 | tf_op jit(solution)/shard_map/ppermute | solution.py:74
  66.1 2.6 %collective-permute-start.11 = (bf16[768,256]{1,0:T(8,128)(2,1)S(1)}, bf16[768,256]{1,0:T(8,128)(2,1)S(1)}, u32[]{:S(2)}, u32[]{:S(2)}) collective-permute-start(bf16[768,256]{1,0:T(8,128)(2,1)S(1)} %collective-permute-done.10), channel_id=1, source_target_pairs={{0,2},{1,31},{2,4},{3,1},{4,6},{5,3},{6,8},{7,5},{8,10},{9,7},{10,... | collective-permute-start | bytes 1179656 | tf_op jit(solution)/shard_map/ppermute | solution.py:74
  68.8 0.1 constant_dynamic-slice_fusion.counts
  68.9 0.1 dynamic-slice_bitcast_fusion.tiles
  68.9 2.6 %lists.1 = (s32[7,384]{1,0:T(8,128)S(1)}, s32[1,7]{1,0:T(1,128)S(1)}) custom-call(s32[6]{0:T(128)S(1)} %stack.27.place, s32[64,12]{1,0:T(8,128)S(1)} %dynamic-slice_bitcast_fusion.tiles, s32[1,12]{1,0:T(1,128)S(1)} %constant_dynamic-slice_fusion.counts), custom_call_target="tpu_custom_call" | custom-call | tf_op jit(solution)/shard_map/lists/pallas_call | solution.py:262
  71.5 4.5 %collective-permute-start.14 = (bf16[768,256]{1,0:T(8,128)(2,1)S(1)}, bf16[768,256]{1,0:T(8,128)(2,1)S(1)}, u32[]{:S(2)}, u32[]{:S(2)}) collective-permute-start(bf16[768,256]{1,0:T(8,128)(2,1)S(1)} %collective-permute-done.9), channel_id=1, source_target_pairs={{0,2},{1,31},{2,4},{3,1},{4,6},{5,3},{6,8},{7,5},{8,10},{9,7},{10,... | collective-permute-start | bytes 1179656 | tf_op jit(solution)/shard_map/ppermute | solution.py:74
  76.1 2.4 %collective-permute-start.13 = (bf16[768,128]{1,0:T(8,128)(2,1)S(1)}, bf16[768,128]{1,0:T(8,128)(2,1)S(1)}, u32[]{:S(2)}, u32[]{:S(2)}) collective-permute-start(bf16[768,128]{1,0:T(8,128)(2,1)S(1)} %get-tuple-element.47), channel_id=1, source_target_pairs={{0,1},{1,0},{2,3},{3,2},{4,5},{5,4},{6,7},{7,6},{8,9},{9,8},{10,11... | collective-permute-start | bytes 589832 | tf_op jit(solution)/shard_map/ppermute | solution.py:64
  78.5 3.7 %collective-permute-start.12 = (bf16[768,256]{1,0:T(8,128)(2,1)S(1)}, bf16[768,256]{1,0:T(8,128)(2,1)S(1)}, u32[]{:S(2)}, u32[]{:S(2)}) collective-permute-start(bf16[768,256]{1,0:T(8,128)(2,1)S(1)} %collective-permute-done.11), channel_id=1, source_target_pairs={{0,2},{1,31},{2,4},{3,1},{4,6},{5,3},{6,8},{7,5},{8,10},{9,7},{10,... | collective-permute-start | bytes 1179656 | tf_op jit(solution)/shard_map/ppermute | solution.py:74
  82.2 3.6 %collective-permute-start.15 = (bf16[768,256]{1,0:T(8,128)(2,1)S(1)}, bf16[768,256]{1,0:T(8,128)(2,1)S(1)}, u32[]{:S(2)}, u32[]{:S(2)}) collective-permute-start(bf16[768,256]{1,0:T(8,128)(2,1)S(1)} %collective-permute-done.14), channel_id=1, source_target_pairs={{0,2},{1,31},{2,4},{3,1},{4,6},{5,3},{6,8},{7,5},{8,10},{9,7},{10,... | collective-permute-start | bytes 1179656 | tf_op jit(solution)/shard_map/ppermute | solution.py:74
  85.8 0.1 broadcast_select_fusion.1
  85.9 1.4 collective-permute-done.12
  87.3 4.6 %collective-permute-start.17 = (bf16[768,256]{1,0:T(8,128)(2,1)S(1)}, bf16[768,256]{1,0:T(8,128)(2,1)S(1)}, u32[]{:S(2)}, u32[]{:S(2)}) collective-permute-start(bf16[768,256]{1,0:T(8,128)(2,1)S(1)} %collective-permute-done.12), channel_id=1, source_target_pairs={{0,2},{1,31},{2,4},{3,1},{4,6},{5,3},{6,8},{7,5},{8,10},{9,7},{10,... | collective-permute-start | bytes 1179656 | tf_op jit(solution)/shard_map/ppermute | solution.py:74
  91.9 3.2 %attend.7.refs_2_ = f32[13,128,256]{2,1,0:T(8,128)S(1)} custom-call(s32[6]{0:T(128)S(1)} %stack.27.place, s32[7,384]{1,0:T(8,128)S(1)} %get-tuple-element.43.pairs, s32[1,7]{1,0:T(1,128)S(1)} %get-tuple-element.44.counts, bf16[12,128,128]{2,1,0:T(8,128)(2,1)S(1)} %bitcast.41, bf16[6,128,256]{2,1,0:T(8,128)(2,1)} %bitcast.12.refs_0_, ...), custom_call_target="tpu_custom_call" | custom-call | flops 5000000000 | bytes 5000000 | tf_op jit(solution)/shard_map/attend/pallas_call | solution.py:193
  95.1 3.4 %collective-permute-start.16 = (bf16[768,256]{1,0:T(8,128)(2,1)S(1)}, bf16[768,256]{1,0:T(8,128)(2,1)S(1)}, u32[]{:S(2)}, u32[]{:S(2)}) collective-permute-start(bf16[768,256]{1,0:T(8,128)(2,1)S(1)} %collective-permute-done.15), channel_id=1, source_target_pairs={{0,2},{1,31},{2,4},{3,1},{4,6},{5,3},{6,8},{7,5},{8,10},{9,7},{10,... | collective-permute-start | bytes 1179656 | tf_op jit(solution)/shard_map/ppermute | solution.py:74
  98.5 3.1 %collective-permute-start.19 = (bf16[768,256]{1,0:T(8,128)(2,1)S(1)}, bf16[768,256]{1,0:T(8,128)(2,1)S(1)}, u32[]{:S(2)}, u32[]{:S(2)}) collective-permute-start(bf16[768,256]{1,0:T(8,128)(2,1)S(1)} %collective-permute-done.17), channel_id=1, source_target_pairs={{0,2},{1,31},{2,4},{3,1},{4,6},{5,3},{6,8},{7,5},{8,10},{9,7},{10,... | collective-permute-start | bytes 1179656 | tf_op jit(solution)/shard_map/ppermute | solution.py:74
  101.6 2.0 %attend.8.refs_2_ = f32[13,128,256]{2,1,0:T(8,128)S(1)} custom-call(s32[6]{0:T(128)S(1)} %stack.27.place, s32[7,384]{1,0:T(8,128)S(1)} %get-tuple-element.43.pairs, s32[1,7]{1,0:T(1,128)S(1)} %get-tuple-element.44.counts, bf16[12,128,128]{2,1,0:T(8,128)(2,1)S(1)} %bitcast.42, bf16[6,128,256]{2,1,0:T(8,128)(2,1)S(1)} %bitcast.51, ...), custom_call_target="tpu_custom_call", output_to_operand_aliasing={{}: (6, {})} | custom-call | flops 2000000000 | bytes 2000000 | tf_op jit(solution)/shard_map/attend/pallas_call | solution.py:193
  103.6 0.3 collective-permute-done.16
  103.9 4.3 %collective-permute-start.18 = (bf16[768,256]{1,0:T(8,128)(2,1)S(1)}, bf16[768,256]{1,0:T(8,128)(2,1)S(1)}, u32[]{:S(2)}, u32[]{:S(2)}) collective-permute-start(bf16[768,256]{1,0:T(8,128)(2,1)S(1)} %collective-permute-done.16), channel_id=1, source_target_pairs={{0,2},{1,31},{2,4},{3,1},{4,6},{5,3},{6,8},{7,5},{8,10},{9,7},{10,... | collective-permute-start | bytes 1179656 | tf_op jit(solution)/shard_map/ppermute | solution.py:74
  108.2 4.2 %collective-permute-start.21 = (bf16[768,256]{1,0:T(8,128)(2,1)S(1)}, bf16[768,256]{1,0:T(8,128)(2,1)S(1)}, u32[]{:S(2)}, u32[]{:S(2)}) collective-permute-start(bf16[768,256]{1,0:T(8,128)(2,1)S(1)} %collective-permute-done.19), channel_id=1, source_target_pairs={{0,2},{1,31},{2,4},{3,1},{4,6},{5,3},{6,8},{7,5},{8,10},{9,7},{10,... | collective-permute-start | bytes 1179656 | tf_op jit(solution)/shard_map/ppermute | solution.py:74
  112.4 2.0 %attend.9.refs_2_ = f32[13,128,256]{2,1,0:T(8,128)S(1)} custom-call(s32[6]{0:T(128)S(1)} %stack.27.place, s32[7,384]{1,0:T(8,128)S(1)} %get-tuple-element.43.pairs, s32[1,7]{1,0:T(1,128)S(1)} %get-tuple-element.44.counts, bf16[12,128,128]{2,1,0:T(8,128)(2,1)S(1)} %bitcast.43, bf16[6,128,256]{2,1,0:T(8,128)(2,1)S(1)} %bitcast.54, ...), custom_call_target="tpu_custom_call", output_to_operand_aliasing={{}: (6, {})} | custom-call | flops 2000000000 | bytes 2000000 | tf_op jit(solution)/shard_map/attend/pallas_call | solution.py:193
  114.4 3.5 %collective-permute-start.20 = (bf16[768,256]{1,0:T(8,128)(2,1)S(1)}, bf16[768,256]{1,0:T(8,128)(2,1)S(1)}, u32[]{:S(2)}, u32[]{:S(2)}) collective-permute-start(bf16[768,256]{1,0:T(8,128)(2,1)S(1)} %collective-permute-done.18), channel_id=1, source_target_pairs={{0,2},{1,31},{2,4},{3,1},{4,6},{5,3},{6,8},{7,5},{8,10},{9,7},{10,... | collective-permute-start | bytes 1179656 | tf_op jit(solution)/shard_map/ppermute | solution.py:74
  117.9 4.2 %collective-permute-start.23 = (bf16[768,256]{1,0:T(8,128)(2,1)S(1)}, bf16[768,256]{1,0:T(8,128)(2,1)S(1)}, u32[]{:S(2)}, u32[]{:S(2)}) collective-permute-start(bf16[768,256]{1,0:T(8,128)(2,1)S(1)} %collective-permute-done.21), channel_id=1, source_target_pairs={{0,2},{1,31},{2,4},{3,1},{4,6},{5,3},{6,8},{7,5},{8,10},{9,7},{10,... | collective-permute-start | bytes 1179656 | tf_op jit(solution)/shard_map/ppermute | solution.py:74
  122.1 2.0 %attend.10.refs_2_ = f32[13,128,256]{2,1,0:T(8,128)S(1)} custom-call(s32[6]{0:T(128)S(1)} %stack.27.place, s32[7,384]{1,0:T(8,128)S(1)} %get-tuple-element.43.pairs, s32[1,7]{1,0:T(1,128)S(1)} %get-tuple-element.44.counts, bf16[12,128,128]{2,1,0:T(8,128)(2,1)S(1)} %bitcast.44, bf16[6,128,256]{2,1,0:T(8,128)(2,1)S(1)} %bitcast.56, ...), custom_call_target="tpu_custom_call", output_to_operand_aliasing={{}: (6, {})} | custom-call | flops 2000000000 | bytes 2000000 | tf_op jit(solution)/shard_map/attend/pallas_call | solution.py:193
  124.1 3.5 %collective-permute-start.22 = (bf16[768,256]{1,0:T(8,128)(2,1)S(1)}, bf16[768,256]{1,0:T(8,128)(2,1)S(1)}, u32[]{:S(2)}, u32[]{:S(2)}) collective-permute-start(bf16[768,256]{1,0:T(8,128)(2,1)S(1)} %collective-permute-done.20), channel_id=1, source_target_pairs={{0,2},{1,31},{2,4},{3,1},{4,6},{5,3},{6,8},{7,5},{8,10},{9,7},{10,... | collective-permute-start | bytes 1179656 | tf_op jit(solution)/shard_map/ppermute | solution.py:74
  127.6 4.2 %collective-permute-start.25 = (bf16[768,256]{1,0:T(8,128)(2,1)S(1)}, bf16[768,256]{1,0:T(8,128)(2,1)S(1)}, u32[]{:S(2)}, u32[]{:S(2)}) collective-permute-start(bf16[768,256]{1,0:T(8,128)(2,1)S(1)} %collective-permute-done.23), channel_id=1, source_target_pairs={{0,2},{1,31},{2,4},{3,1},{4,6},{5,3},{6,8},{7,5},{8,10},{9,7},{10,... | collective-permute-start | bytes 1179656 | tf_op jit(solution)/shard_map/ppermute | solution.py:74
  131.8 2.0 %attend.11.refs_2_ = f32[13,128,256]{2,1,0:T(8,128)S(1)} custom-call(s32[6]{0:T(128)S(1)} %stack.27.place, s32[7,384]{1,0:T(8,128)S(1)} %get-tuple-element.43.pairs, s32[1,7]{1,0:T(1,128)S(1)} %get-tuple-element.44.counts, bf16[12,128,128]{2,1,0:T(8,128)(2,1)S(1)} %bitcast.45, bf16[6,128,256]{2,1,0:T(8,128)(2,1)S(1)} %bitcast.58, ...), custom_call_target="tpu_custom_call", output_to_operand_aliasing={{}: (6, {})} | custom-call | flops 2000000000 | bytes 2000000 | tf_op jit(solution)/shard_map/attend/pallas_call | solution.py:193
  133.8 3.5 %collective-permute-start.24 = (bf16[768,256]{1,0:T(8,128)(2,1)S(1)}, bf16[768,256]{1,0:T(8,128)(2,1)S(1)}, u32[]{:S(2)}, u32[]{:S(2)}) collective-permute-start(bf16[768,256]{1,0:T(8,128)(2,1)S(1)} %collective-permute-done.22), channel_id=1, source_target_pairs={{1,31},{3,1},{5,3},{7,5},{9,7},{11,9},{13,11},{15,13},{17,15},{19,... | collective-permute-start | bytes 1179656 | tf_op jit(solution)/shard_map/ppermute | solution.py:74
  137.4 4.2 %collective-permute-start.26 = (bf16[768,256]{1,0:T(8,128)(2,1)S(1)}, bf16[768,256]{1,0:T(8,128)(2,1)S(1)}, u32[]{:S(2)}, u32[]{:S(2)}) collective-permute-start(bf16[768,256]{1,0:T(8,128)(2,1)S(1)} %collective-permute-done.25), channel_id=1, source_target_pairs={{1,31},{3,1},{5,3},{7,5},{9,7},{11,9},{13,11},{15,13},{17,15},{19,... | collective-permute-start | bytes 1179656 | tf_op jit(solution)/shard_map/ppermute | solution.py:74
  141.6 2.0 %attend.12.refs_2_ = f32[13,128,256]{2,1,0:T(8,128)S(1)} custom-call(s32[6]{0:T(128)S(1)} %stack.27.place, s32[7,384]{1,0:T(8,128)S(1)} %get-tuple-element.43.pairs, s32[1,7]{1,0:T(1,128)S(1)} %get-tuple-element.44.counts, bf16[12,128,128]{2,1,0:T(8,128)(2,1)S(1)} %bitcast.46, bf16[6,128,256]{2,1,0:T(8,128)(2,1)S(1)} %bitcast.60, ...), custom_call_target="tpu_custom_call", output_to_operand_aliasing={{}: (6, {})} | custom-call | flops 2000000000 | bytes 2000000 | tf_op jit(solution)/shard_map/attend/pallas_call | solution.py:193
  143.5 3.0 %collective-permute-done.26 = bf16[768,256]{1,0:T(8,128)(2,1)S(1)} collective-permute-done((bf16[768,256]{1,0:T(8,128)(2,1)S(1)}, bf16[768,256]{1,0:T(8,128)(2,1)S(1)}, u32[]{:S(2)}, u32[]{:S(2)}) %collective-permute-start.26) | collective-permute-done | bytes 393248 | tf_op jit(solution)/shard_map/ppermute | solution.py:74
  146.6 2.0 %attend.13 = (f32[6,128,256]{2,1,0:T(8,128)S(1)}, f32[6,128,256]{2,1,0:T(8,128)S(1)}) custom-call(s32[6]{0:T(128)S(1)} %stack.27.place, s32[7,384]{1,0:T(8,128)S(1)} %get-tuple-element.43.pairs, s32[1,7]{1,0:T(1,128)S(1)} %get-tuple-element.44.counts, bf16[12,128,128]{2,1,0:T(8,128)(2,1)S(1)} %bitcast.47, bf16[6,128,256]{2,1,0:T(8,128)(2,1)S(1)} %bitcast.61, ...), custom_call_target="tpu_custom_call" | custom-call | flops 2000000000 | bytes 2000000 | tf_op jit(solution)/shard_map/attend/pallas_call | solution.py:193
  148.5 1.9 %collective-permute-start.27 = (f32[6,128,256]{2,1,0:T(8,128)S(1)}, f32[6,128,256]{2,1,0:T(8,128)S(1)}, u32[]{:S(2)}, u32[]{:S(2)}) collective-permute-start(f32[6,128,256]{2,1,0:T(8,128)S(1)} %get-tuple-element.64), channel_id=1, source_target_pairs={{0,1},{1,0},{2,3},{3,2},{4,5},{5,4},{6,7},{7,6},{8,9},{9,8},{10,11... | collective-permute-start | bytes 2359304 | tf_op jit(solution)/shard_map/ppermute | solution.py:64
  150.5 2.3 %collective-permute-done.27 = f32[6,128,256]{2,1,0:T(8,128)S(1)} collective-permute-done((f32[6,128,256]{2,1,0:T(8,128)S(1)}, f32[6,128,256]{2,1,0:T(8,128)S(1)}, u32[]{:S(2)}, u32[]{:S(2)}) %collective-permute-start.27) | collective-permute-done | bytes 786464 | tf_op jit(solution)/shard_map/ppermute | solution.py:64
  152.7 0.1 add.19
  152.8 0.1 fusion
  152.9 10.5 %all_to_all.19 = bf16[16,48,128]{2,1,0:T(8,128)(2,1)S(1)} all-to-all(bf16[16,48,128]{2,1,0:T(8,128)(2,1)S(1)} %bitcast.64), channel_id=1, replica_groups=mesh['seq'=16,'bal'=32] {'seq'}, dimensions={0} | all-to-all | bytes 393216 | tf_op jit(solution)/shard_map/all_to_all | solution.py:358
  163.4 0.7 copy_bitcast_fusion
  (23 shorter events, 0.1 us)
Async XLA Ops:
  0.0 68.9 %copy-start = (s32[1,192,64]{1,2,0:T(8,128)S(1)}, s32[1,192,64]{1,2,0:T(8,128)}, u32[]{:S(2)}) copy-start(s32[1,192,64]{1,2,0:T(8,128)} %param.10) | copy-start | bytes 147460
  0.0 36.4 %copy-start.1 = (bf16[3072,1,3,128]{3,0,2,1:T(8,128)(2,1)S(1)}, bf16[3072,1,3,128]{3,0,2,1:T(8,128)(2,1)}, u32[]{:S(2)}) copy-start(bf16[3072,1,3,128]{3,0,2,1:T(8,128)(2,1)} %param.7) | copy-start | bytes 7077892
  0.0 12.8 %collective-permute-start.3 = (bf16[48,3072]{1,0:T(8,128)(2,1)}, bf16[48,3072]{1,0:T(8,128)(2,1)S(1)}, u32[]{:S(2)}, u32[]{:S(2)}) collective-permute-start(bf16[48,3072]{1,0:T(8,128)(2,1)} %upper.1), channel_id=1, source_target_pairs={{0,96},{32,0},{64,32},{96,64},{128,224},{160,128},{192,160},{224,1... | collective-permute-start | bytes 884744 | tf_op jit(solution)/shard_map/ppermute | solution.py:34
  5.6 9.3 %collective-permute-start.4 = (bf16[48,3072]{1,0:T(8,128)(2,1)}, bf16[48,3072]{1,0:T(8,128)(2,1)S(1)}, u32[]{:S(2)}, u32[]{:S(2)}) collective-permute-start(bf16[48,3072]{1,0:T(8,128)(2,1)} %upper.1), channel_id=1, source_target_pairs={{0,64},{32,96},{64,0},{96,32},{128,192},{160,224},{192,128},{224,1... | collective-permute-start | bytes 884744 | tf_op jit(solution)/shard_map/ppermute | solution.py:34
  7.9 11.6 %collective-permute-start = (bf16[48,3072]{1,0:T(8,128)(2,1)}, bf16[48,3072]{1,0:T(8,128)(2,1)S(1)}, u32[]{:S(2)}, u32[]{:S(2)}) collective-permute-start(bf16[48,3072]{1,0:T(8,128)(2,1)} %upper.1), channel_id=1, source_target_pairs={{0,32},{32,64},{64,96},{96,0},{128,160},{160,192},{192,224},{224,1... | collective-permute-start | bytes 884744 | tf_op jit(solution)/shard_map/ppermute | solution.py:34
  15.0 14.7 %collective-permute-start.5 = (bf16[96,3072]{1,0:T(8,128)(2,1)S(1)}, bf16[96,3072]{1,0:T(8,128)(2,1)}, u32[]{:S(2)}, u32[]{:S(2)}) collective-permute-start(bf16[96,3072]{1,0:T(8,128)(2,1)S(1)} %join.3.refs_1_), channel_id=1, source_target_pairs={{0,384},{32,416},{64,448},{96,480},{128,0},{160,32},{192,64},{224,... | collective-permute-start | bytes 1769480 | tf_op jit(solution)/shard_map/ppermute | solution.py:34
  19.4 1.0 copy-start.2
  21.3 12.4 %collective-permute-start.1 = (bf16[96,3072]{1,0:T(8,128)(2,1)}, bf16[96,3072]{1,0:T(8,128)(2,1)}, u32[]{:S(2)}, u32[]{:S(2)}) collective-permute-start(bf16[96,3072]{1,0:T(8,128)(2,1)} %join.2.refs_0_), channel_id=1, source_target_pairs={{0,128},{32,160},{64,192},{96,224},{128,256},{160,288},{192,320},{... | collective-permute-start | bytes 1769480 | tf_op jit(solution)/shard_map/ppermute | solution.py:34
  23.2 17.0 %collective-permute-start.8 = (bf16[96,3072]{1,0:T(8,128)(2,1)S(1)}, bf16[96,3072]{1,0:T(8,128)(2,1)}, u32[]{:S(2)}, u32[]{:S(2)}) collective-permute-start(bf16[96,3072]{1,0:T(8,128)(2,1)S(1)} %join.3.refs_1_), channel_id=1, source_target_pairs={{0,128},{32,160},{64,192},{96,224},{128,256},{160,288},{192,320},{... | collective-permute-start | bytes 1769480 | tf_op jit(solution)/shard_map/ppermute | solution.py:34
  26.0 14.1 %collective-permute-start.7 = (bf16[96,3072]{1,0:T(8,128)(2,1)}, bf16[96,3072]{1,0:T(8,128)(2,1)}, u32[]{:S(2)}, u32[]{:S(2)}) collective-permute-start(bf16[96,3072]{1,0:T(8,128)(2,1)} %join.2.refs_0_), channel_id=1, source_target_pairs={{0,384},{32,416},{64,448},{96,480},{128,0},{160,32},{192,64},{224,... | collective-permute-start | bytes 1769480 | tf_op jit(solution)/shard_map/ppermute | solution.py:34
  29.7 13.9 %collective-permute-start.6 = (bf16[96,3072]{1,0:T(8,128)(2,1)}, bf16[96,3072]{1,0:T(8,128)(2,1)}, u32[]{:S(2)}, u32[]{:S(2)}) collective-permute-start(bf16[96,3072]{1,0:T(8,128)(2,1)} %collective-permute-done.5.refs_3_), channel_id=1, source_target_pairs={{0,384},{32,416},{64,448},{96,480},{128,0},{160,32},{192,64},{224,... | collective-permute-start | bytes 1769480 | tf_op jit(solution)/shard_map/ppermute | solution.py:34
  33.7 12.6 %collective-permute-start.2 = (bf16[96,3072]{1,0:T(8,128)(2,1)}, bf16[96,3072]{1,0:T(8,128)(2,1)}, u32[]{:S(2)}, u32[]{:S(2)}) collective-permute-start(bf16[96,3072]{1,0:T(8,128)(2,1)} %collective-permute-done.1.refs_2_), channel_id=1, source_target_pairs={{0,128},{32,160},{64,192},{96,224},{128,256},{160,288},{192,320},{... | collective-permute-start | bytes 1769480 | tf_op jit(solution)/shard_map/ppermute | solution.py:34
  46.3 22.4 %copy-start.3 = (s32[1,192]{1,0:T(1,128)S(1)}, s32[1,192]{1,0:T(1,128)}, u32[]{:S(2)}) copy-start(s32[1,192]{1,0:T(1,128)} %param.11) | copy-start | bytes 2308
  49.2 16.9 %collective-permute-start.10 = (bf16[768,256]{1,0:T(8,128)(2,1)}, bf16[768,256]{1,0:T(8,128)(2,1)S(1)}, u32[]{:S(2)}, u32[]{:S(2)}) collective-permute-start(bf16[768,256]{1,0:T(8,128)(2,1)} %get-tuple-element.39), channel_id=1, source_target_pairs={{0,1},{1,0},{2,3},{3,2},{4,5},{5,4},{6,7},{7,6},{8,9},{9,8},{10,11... | collective-permute-start | bytes 1179656 | tf_op jit(solution)/shard_map/ppermute | solution.py:64
  55.6 15.9 %collective-permute-start.9 = (bf16[768,256]{1,0:T(8,128)(2,1)}, bf16[768,256]{1,0:T(8,128)(2,1)S(1)}, u32[]{:S(2)}, u32[]{:S(2)}) collective-permute-start(bf16[768,256]{1,0:T(8,128)(2,1)} %get-tuple-element.39), channel_id=1, source_target_pairs={{0,2},{1,31},{2,4},{3,1},{4,6},{5,3},{6,8},{7,5},{8,10},{9,7},{10,... | collective-permute-start | bytes 1179656 | tf_op jit(solution)/shard_map/ppermute | solution.py:74
  66.1 9.9 %collective-permute-start.11 = (bf16[768,256]{1,0:T(8,128)(2,1)S(1)}, bf16[768,256]{1,0:T(8,128)(2,1)S(1)}, u32[]{:S(2)}, u32[]{:S(2)}) collective-permute-start(bf16[768,256]{1,0:T(8,128)(2,1)S(1)} %collective-permute-done.10), channel_id=1, source_target_pairs={{0,2},{1,31},{2,4},{3,1},{4,6},{5,3},{6,8},{7,5},{8,10},{9,7},{10,... | collective-permute-start | bytes 1179656 | tf_op jit(solution)/shard_map/ppermute | solution.py:74
  71.5 10.6 %collective-permute-start.14 = (bf16[768,256]{1,0:T(8,128)(2,1)S(1)}, bf16[768,256]{1,0:T(8,128)(2,1)S(1)}, u32[]{:S(2)}, u32[]{:S(2)}) collective-permute-start(bf16[768,256]{1,0:T(8,128)(2,1)S(1)} %collective-permute-done.9), channel_id=1, source_target_pairs={{0,2},{1,31},{2,4},{3,1},{4,6},{5,3},{6,8},{7,5},{8,10},{9,7},{10,... | collective-permute-start | bytes 1179656 | tf_op jit(solution)/shard_map/ppermute | solution.py:74
  76.1 9.7 %collective-permute-start.13 = (bf16[768,128]{1,0:T(8,128)(2,1)S(1)}, bf16[768,128]{1,0:T(8,128)(2,1)S(1)}, u32[]{:S(2)}, u32[]{:S(2)}) collective-permute-start(bf16[768,128]{1,0:T(8,128)(2,1)S(1)} %get-tuple-element.47), channel_id=1, source_target_pairs={{0,1},{1,0},{2,3},{3,2},{4,5},{5,4},{6,7},{7,6},{8,9},{9,8},{10,11... | collective-permute-start | bytes 589832 | tf_op jit(solution)/shard_map/ppermute | solution.py:64
  78.5 8.8 %collective-permute-start.12 = (bf16[768,256]{1,0:T(8,128)(2,1)S(1)}, bf16[768,256]{1,0:T(8,128)(2,1)S(1)}, u32[]{:S(2)}, u32[]{:S(2)}) collective-permute-start(bf16[768,256]{1,0:T(8,128)(2,1)S(1)} %collective-permute-done.11), channel_id=1, source_target_pairs={{0,2},{1,31},{2,4},{3,1},{4,6},{5,3},{6,8},{7,5},{8,10},{9,7},{10,... | collective-permute-start | bytes 1179656 | tf_op jit(solution)/shard_map/ppermute | solution.py:74
  82.2 12.9 %collective-permute-start.15 = (bf16[768,256]{1,0:T(8,128)(2,1)S(1)}, bf16[768,256]{1,0:T(8,128)(2,1)S(1)}, u32[]{:S(2)}, u32[]{:S(2)}) collective-permute-start(bf16[768,256]{1,0:T(8,128)(2,1)S(1)} %collective-permute-done.14), channel_id=1, source_target_pairs={{0,2},{1,31},{2,4},{3,1},{4,6},{5,3},{6,8},{7,5},{8,10},{9,7},{10,... | collective-permute-start | bytes 1179656 | tf_op jit(solution)/shard_map/ppermute | solution.py:74
  87.3 11.2 %collective-permute-start.17 = (bf16[768,256]{1,0:T(8,128)(2,1)S(1)}, bf16[768,256]{1,0:T(8,128)(2,1)S(1)}, u32[]{:S(2)}, u32[]{:S(2)}) collective-permute-start(bf16[768,256]{1,0:T(8,128)(2,1)S(1)} %collective-permute-done.12), channel_id=1, source_target_pairs={{0,2},{1,31},{2,4},{3,1},{4,6},{5,3},{6,8},{7,5},{8,10},{9,7},{10,... | collective-permute-start | bytes 1179656 | tf_op jit(solution)/shard_map/ppermute | solution.py:74
  95.1 8.8 %collective-permute-start.16 = (bf16[768,256]{1,0:T(8,128)(2,1)S(1)}, bf16[768,256]{1,0:T(8,128)(2,1)S(1)}, u32[]{:S(2)}, u32[]{:S(2)}) collective-permute-start(bf16[768,256]{1,0:T(8,128)(2,1)S(1)} %collective-permute-done.15), channel_id=1, source_target_pairs={{0,2},{1,31},{2,4},{3,1},{4,6},{5,3},{6,8},{7,5},{8,10},{9,7},{10,... | collective-permute-start | bytes 1179656 | tf_op jit(solution)/shard_map/ppermute | solution.py:74
  98.5 9.7 %collective-permute-start.19 = (bf16[768,256]{1,0:T(8,128)(2,1)S(1)}, bf16[768,256]{1,0:T(8,128)(2,1)S(1)}, u32[]{:S(2)}, u32[]{:S(2)}) collective-permute-start(bf16[768,256]{1,0:T(8,128)(2,1)S(1)} %collective-permute-done.17), channel_id=1, source_target_pairs={{0,2},{1,31},{2,4},{3,1},{4,6},{5,3},{6,8},{7,5},{8,10},{9,7},{10,... | collective-permute-start | bytes 1179656 | tf_op jit(solution)/shard_map/ppermute | solution.py:74
  103.9 10.5 %collective-permute-start.18 = (bf16[768,256]{1,0:T(8,128)(2,1)S(1)}, bf16[768,256]{1,0:T(8,128)(2,1)S(1)}, u32[]{:S(2)}, u32[]{:S(2)}) collective-permute-start(bf16[768,256]{1,0:T(8,128)(2,1)S(1)} %collective-permute-done.16), channel_id=1, source_target_pairs={{0,2},{1,31},{2,4},{3,1},{4,6},{5,3},{6,8},{7,5},{8,10},{9,7},{10,... | collective-permute-start | bytes 1179656 | tf_op jit(solution)/shard_map/ppermute | solution.py:74
  108.2 9.7 %collective-permute-start.21 = (bf16[768,256]{1,0:T(8,128)(2,1)S(1)}, bf16[768,256]{1,0:T(8,128)(2,1)S(1)}, u32[]{:S(2)}, u32[]{:S(2)}) collective-permute-start(bf16[768,256]{1,0:T(8,128)(2,1)S(1)} %collective-permute-done.19), channel_id=1, source_target_pairs={{0,2},{1,31},{2,4},{3,1},{4,6},{5,3},{6,8},{7,5},{8,10},{9,7},{10,... | collective-permute-start | bytes 1179656 | tf_op jit(solution)/shard_map/ppermute | solution.py:74
  114.4 9.7 %collective-permute-start.20 = (bf16[768,256]{1,0:T(8,128)(2,1)S(1)}, bf16[768,256]{1,0:T(8,128)(2,1)S(1)}, u32[]{:S(2)}, u32[]{:S(2)}) collective-permute-start(bf16[768,256]{1,0:T(8,128)(2,1)S(1)} %collective-permute-done.18), channel_id=1, source_target_pairs={{0,2},{1,31},{2,4},{3,1},{4,6},{5,3},{6,8},{7,5},{8,10},{9,7},{10,... | collective-permute-start | bytes 1179656 | tf_op jit(solution)/shard_map/ppermute | solution.py:74
  117.9 9.7 %collective-permute-start.23 = (bf16[768,256]{1,0:T(8,128)(2,1)S(1)}, bf16[768,256]{1,0:T(8,128)(2,1)S(1)}, u32[]{:S(2)}, u32[]{:S(2)}) collective-permute-start(bf16[768,256]{1,0:T(8,128)(2,1)S(1)} %collective-permute-done.21), channel_id=1, source_target_pairs={{0,2},{1,31},{2,4},{3,1},{4,6},{5,3},{6,8},{7,5},{8,10},{9,7},{10,... | collective-permute-start | bytes 1179656 | tf_op jit(solution)/shard_map/ppermute | solution.py:74
  124.1 9.7 %collective-permute-start.22 = (bf16[768,256]{1,0:T(8,128)(2,1)S(1)}, bf16[768,256]{1,0:T(8,128)(2,1)S(1)}, u32[]{:S(2)}, u32[]{:S(2)}) collective-permute-start(bf16[768,256]{1,0:T(8,128)(2,1)S(1)} %collective-permute-done.20), channel_id=1, source_target_pairs={{0,2},{1,31},{2,4},{3,1},{4,6},{5,3},{6,8},{7,5},{8,10},{9,7},{10,... | collective-permute-start | bytes 1179656 | tf_op jit(solution)/shard_map/ppermute | solution.py:74
  127.6 9.7 %collective-permute-start.25 = (bf16[768,256]{1,0:T(8,128)(2,1)S(1)}, bf16[768,256]{1,0:T(8,128)(2,1)S(1)}, u32[]{:S(2)}, u32[]{:S(2)}) collective-permute-start(bf16[768,256]{1,0:T(8,128)(2,1)S(1)} %collective-permute-done.23), channel_id=1, source_target_pairs={{0,2},{1,31},{2,4},{3,1},{4,6},{5,3},{6,8},{7,5},{8,10},{9,7},{10,... | collective-permute-start | bytes 1179656 | tf_op jit(solution)/shard_map/ppermute | solution.py:74
  133.8 9.7 %collective-permute-start.24 = (bf16[768,256]{1,0:T(8,128)(2,1)S(1)}, bf16[768,256]{1,0:T(8,128)(2,1)S(1)}, u32[]{:S(2)}, u32[]{:S(2)}) collective-permute-start(bf16[768,256]{1,0:T(8,128)(2,1)S(1)} %collective-permute-done.22), channel_id=1, source_target_pairs={{1,31},{3,1},{5,3},{7,5},{9,7},{11,9},{13,11},{15,13},{17,15},{19,... | collective-permute-start | bytes 1179656 | tf_op jit(solution)/shard_map/ppermute | solution.py:74
  137.4 9.2 %collective-permute-start.26 = (bf16[768,256]{1,0:T(8,128)(2,1)S(1)}, bf16[768,256]{1,0:T(8,128)(2,1)S(1)}, u32[]{:S(2)}, u32[]{:S(2)}) collective-permute-start(bf16[768,256]{1,0:T(8,128)(2,1)S(1)} %collective-permute-done.25), channel_id=1, source_target_pairs={{1,31},{3,1},{5,3},{7,5},{9,7},{11,9},{13,11},{15,13},{17,15},{19,... | collective-permute-start | bytes 1179656 | tf_op jit(solution)/shard_map/ppermute | solution.py:74
  148.5 4.2 %collective-permute-start.27 = (f32[6,128,256]{2,1,0:T(8,128)S(1)}, f32[6,128,256]{2,1,0:T(8,128)S(1)}, u32[]{:S(2)}, u32[]{:S(2)}) collective-permute-start(f32[6,128,256]{2,1,0:T(8,128)S(1)} %get-tuple-element.64), channel_id=1, source_target_pairs={{0,1},{1,0},{2,3},{3,2},{4,5},{5,4},{6,7},{7,6},{8,9},{9,8},{10,11... | collective-permute-start | bytes 2359304 | tf_op jit(solution)/shard_map/ppermute | solution.py:64

commit v10 on v9

--- a/solution.py
+++ b/solution.py
@@ -290,12 +290,14 @@
     slots = 16 * PIECE // TILE
     before = send(tokens, 1, 1)
     after = send(tokens, 1, -1)
-    across = send(tokens, 1, 2)
     low = join(tokens, before)
+    low, late = lax.optimization_barrier((low, tokens))
+    across = send(late, 1, 2)
     before_low = send(low, 2, 1)
+    after_low = send(low, 2, -1)
+    before_low, after_low = lax.optimization_barrier((before_low, after_low))
     high = join(after, across)
     after_high = send(high, 2, -1)
-    after_low = send(low, 2, -1)
     before_high = send(high, 2, 1)
     across_low = send(before_low, 2, 1)
     across_high = send(after_high, 2, -1)
@@ -340,8 +342,9 @@
             key_tiles, other[0] = lax.optimization_barrier((key_tiles, other[0]))
             pairs, counts = list_pairs(CALLS, key_tiles[0], key_counts, place, slots)
             same[1], pairs, counts = lax.optimization_barrier((same[1], pairs, counts))
-            queries, other[1] = lax.optimization_barrier((queries, other[1]))
+            queries, other[0] = lax.optimization_barrier((queries, other[0]))
             other_queries = swap_cores(queries)
+            same[1], other_queries = lax.optimization_barrier((same[1], other_queries))
         if step == 2:
             low_queries = jnp.where(core == 0, queries, other_queries)
             high_queries = jnp.where(core == 0, other_queries, queries)

time: 165 us -> 169 us (1.024)
  Pallas kernels: 27.9 us -> 25 us
  blocking collectives: 10.5 us -> 13.2 us
  starting transfers between devices: 107 us -> 109 us
    ppermute x16, starting transfers between devices: 67.6 us -> 63.1 us  [pass_on(): return lax.ppermute(block, 'bal', pairs)]
    ppermute x3, starting transfers between devices: 10.7 us -> 14.8 us  [swap_cores(): return lax.ppermute(block, 'bal', [(at, at ^ 1) for at in range(32)])]
    pallas_call x7, Pallas kernels: 15 us -> 12.1 us  [attend(): pl.pallas_call(functools.partial(attend_kernel, scale, first_call, last_c...]
    ppermute x9, starting transfers between devices: 28.5 us -> 31.3 us  [send(): return lax.ppermute(block, MESH_AXES, plane_perm(phase, shift))]
    all_to_all x1, blocking collectives: 10.5 us -> 13.2 us  [on_device(): lax.all_to_all(result.reshape(slots * TILE, HEAD), 'seq', split_axis=0, c...]
  transfers between devices with their start and end apart: 28 -> 28, of which waited for: 9 -> 10; matrix products, arithmetic and copies ran while one was open for 1% -> 0% of each run, Pallas kernels for 14% -> 12%
where the time goes in v10:
time: 169 us; the launch traced here: 168 us
  starting transfers between devices  109 us (64%)
  Pallas kernels  25 us (15%)
  waiting for transfers between devices  16.8 us (10%)
  blocking collectives  13.2 us (8%)
  local copies, waits for them, and re-layouts  2.75 us (2%)
    ppermute x16, starting transfers between devices, pass_on(): return lax.ppermute(block, 'bal', pairs)  63.1 us
    ppermute x9, starting transfers between devices, send(): return lax.ppermute(block, MESH_AXES, plane_perm(phase, shift))  31.3 us
    ppermute x3, starting transfers between devices, swap_cores(): return lax.ppermute(block, 'bal', [(at, at ^ 1) for at in range(32)])  14.8 us
    all_to_all x1, blocking collectives, on_device(): lax.all_to_all(result.reshape(slots * TILE, HEAD), 'seq', split_axis=0, c...  13.2 us
    pallas_call x7, Pallas kernels, attend(): pl.pallas_call(functools.partial(attend_kernel, scale, first_call, last_c...  12.1 us
    pallas_call x3, Pallas kernels, project(): pl.pallas_call(functools.partial(project_kernel, shares), out_shape=(jax....  9.26 us
    ppermute x9, waiting for transfers between devices, send(): return lax.ppermute(block, MESH_AXES, plane_perm(phase, shift))  8.59 us
    ppermute x16, waiting for transfers between devices, pass_on(): return lax.ppermute(block, 'bal', pairs)  6.28 us
  transfers between devices with their start and end apart: 28, of which 10 were waited for; matrix products, arithmetic and copies ran while one was open for 0% of the time, Pallas kernels for 12%

profile of v10, /device:TPU:1, one launch (start us, length us, event | category | flops | bytes accessed | tf_op | source)
XLA Modules:
  0.0 167.6 jit_solution(15277264053953851247)
XLA Ops:
  0.0 4.2 %collective-permute-start = (bf16[48,3072]{1,0:T(8,128)(2,1)}, bf16[48,3072]{1,0:T(8,128)(2,1)S(1)}, u32[]{:S(2)}, u32[]{:S(2)}) collective-permute-start(bf16[48,3072]{1,0:T(8,128)(2,1)} %upper.1), channel_id=1, source_target_pairs={{0,32},{32,64},{64,96},{96,0},{128,160},{160,192},{192,224},{224,1... | collective-permute-start | bytes 884744 | tf_op jit(solution)/shard_map/ppermute | solution.py:34
  4.2 3.4 %collective-permute-start.4 = (bf16[48,3072]{1,0:T(8,128)(2,1)}, bf16[48,3072]{1,0:T(8,128)(2,1)S(1)}, u32[]{:S(2)}, u32[]{:S(2)}) collective-permute-start(bf16[48,3072]{1,0:T(8,128)(2,1)} %upper.1), channel_id=1, source_target_pairs={{0,96},{32,0},{64,32},{96,64},{128,224},{160,128},{192,160},{224,1... | collective-permute-start | bytes 884744 | tf_op jit(solution)/shard_map/ppermute | solution.py:34
  7.5 2.4 %collective-permute-done.lower = bf16[48,3072]{1,0:T(8,128)(2,1)S(1)} collective-permute-done((bf16[48,3072]{1,0:T(8,128)(2,1)}, bf16[48,3072]{1,0:T(8,128)(2,1)S(1)}, u32[]{:S(2)}, u32[]{:S(2)}) %collective-permute-start) | collective-permute-done | bytes 294944 | tf_op jit(solution)/shard_map/ppermute | solution.py:34
  9.9 1.0 copy-done.4
  10.9 0.1 join.2.refs_0_
  11.0 3.8 %collective-permute-start.5 = (bf16[48,3072]{1,0:T(8,128)(2,1)}, bf16[48,3072]{1,0:T(8,128)(2,1)S(1)}, u32[]{:S(2)}, u32[]{:S(2)}) collective-permute-start(bf16[48,3072]{1,0:T(8,128)(2,1)} %upper.1), channel_id=1, source_target_pairs={{0,64},{32,96},{64,0},{96,32},{128,192},{160,224},{192,128},{224,1... | collective-permute-start | bytes 884744 | tf_op jit(solution)/shard_map/ppermute | solution.py:34
  14.9 3.1 %collective-permute-start.1 = (bf16[96,3072]{1,0:T(8,128)(2,1)S(1)}, bf16[96,3072]{1,0:T(8,128)(2,1)}, u32[]{:S(2)}, u32[]{:S(2)}) collective-permute-start(bf16[96,3072]{1,0:T(8,128)(2,1)S(1)} %join.2.refs_0_), channel_id=1, source_target_pairs={{0,128},{32,160},{64,192},{96,224},{128,256},{160,288},{192,320},{... | collective-permute-start | bytes 1769480 | tf_op jit(solution)/shard_map/ppermute | solution.py:34
  18.0 3.4 %collective-permute-start.2 = (bf16[96,3072]{1,0:T(8,128)(2,1)S(1)}, bf16[96,3072]{1,0:T(8,128)(2,1)S(1)}, u32[]{:S(2)}, u32[]{:S(2)}) collective-permute-start(bf16[96,3072]{1,0:T(8,128)(2,1)S(1)} %join.2.refs_0_), channel_id=1, source_target_pairs={{0,384},{32,416},{64,448},{96,480},{128,0},{160,32},{192,64},{224,... | collective-permute-start | bytes 1769480 | tf_op jit(solution)/shard_map/ppermute | solution.py:34
  21.4 0.0 collective-permute-done.4.upper
  21.4 0.8 join.3.refs_1_
  22.3 3.2 %collective-permute-start.6 = (bf16[96,3072]{1,0:T(8,128)(2,1)}, bf16[96,3072]{1,0:T(8,128)(2,1)}, u32[]{:S(2)}, u32[]{:S(2)}) collective-permute-start(bf16[96,3072]{1,0:T(8,128)(2,1)} %join.3.refs_1_), channel_id=1, source_target_pairs={{0,384},{32,416},{64,448},{96,480},{128,0},{160,32},{192,64},{224,... | collective-permute-start | bytes 1769480 | tf_op jit(solution)/shard_map/ppermute | solution.py:34
  25.5 2.1 %collective-permute-start.8 = (bf16[96,3072]{1,0:T(8,128)(2,1)}, bf16[96,3072]{1,0:T(8,128)(2,1)}, u32[]{:S(2)}, u32[]{:S(2)}) collective-permute-start(bf16[96,3072]{1,0:T(8,128)(2,1)} %join.3.refs_1_), channel_id=1, source_target_pairs={{0,128},{32,160},{64,192},{96,224},{128,256},{160,288},{192,320},{... | collective-permute-start | bytes 1769480 | tf_op jit(solution)/shard_map/ppermute | solution.py:34
  27.6 1.6 collective-permute-done.1.refs_2_
  29.1 2.4 %collective-permute-done.2.refs_0_ = bf16[96,3072]{1,0:T(8,128)(2,1)S(1)} collective-permute-done((bf16[96,3072]{1,0:T(8,128)(2,1)S(1)}, bf16[96,3072]{1,0:T(8,128)(2,1)S(1)}, u32[]{:S(2)}, u32[]{:S(2)}) %collective-permute-start.2) | collective-permute-done | bytes 589856 | tf_op jit(solution)/shard_map/ppermute | solution.py:34
  31.5 0.8 copy-done.2
  32.3 3.4 %collective-permute-start.3 = (bf16[96,3072]{1,0:T(8,128)(2,1)}, bf16[96,3072]{1,0:T(8,128)(2,1)}, u32[]{:S(2)}, u32[]{:S(2)}) collective-permute-start(bf16[96,3072]{1,0:T(8,128)(2,1)} %collective-permute-done.1.refs_2_), channel_id=1, source_target_pairs={{0,128},{32,160},{64,192},{96,224},{128,256},{160,288},{192,320},{... | collective-permute-start | bytes 1769480 | tf_op jit(solution)/shard_map/ppermute | solution.py:34
  35.7 1.8 %collective-permute-done.6.refs_3_ = bf16[96,3072]{1,0:T(8,128)(2,1)} collective-permute-done((bf16[96,3072]{1,0:T(8,128)(2,1)}, bf16[96,3072]{1,0:T(8,128)(2,1)}, u32[]{:S(2)}, u32[]{:S(2)}) %collective-permute-start.6) | collective-permute-done | bytes 589856 | tf_op jit(solution)/shard_map/ppermute | solution.py:34
  37.5 4.7 %collective-permute-start.7 = (bf16[96,3072]{1,0:T(8,128)(2,1)}, bf16[96,3072]{1,0:T(8,128)(2,1)}, u32[]{:S(2)}, u32[]{:S(2)}) collective-permute-start(bf16[96,3072]{1,0:T(8,128)(2,1)} %collective-permute-done.6.refs_3_), channel_id=1, source_target_pairs={{0,384},{32,416},{64,448},{96,480},{128,0},{160,32},{192,64},{224,... | collective-permute-start | bytes 1769480 | tf_op jit(solution)/shard_map/ppermute | solution.py:34
  42.3 0.1 stack.27.place
  42.5 3.8 %project.3 = (bf16[768,128]{1,0:T(8,128)(2,1)S(1)}, bf16[768,256]{1,0:T(8,128)(2,1)}) custom-call(s32[6]{0:T(128)S(1)} %stack.27.place, bf16[96,3072]{1,0:T(8,128)(2,1)S(1)} %join.2.refs_0_, bf16[96,3072]{1,0:T(8,128)(2,1)} %join.3.refs_1_, bf16[96,3072]{1,0:T(8,128)(2,1)} %collective-permute-done.1.refs_2_, ...), custom_call_target="tpu_custom_call" | custom-call | tf_op jit(solution)/shard_map/project/pallas_call | solution.py:115
  46.2 0.0 collective-permute-done.8.refs_1_
  46.3 2.7 %project.4 = (bf16[768,128]{1,0:T(8,128)(2,1)S(1)}, bf16[768,256]{1,0:T(8,128)(2,1)}) custom-call(s32[6]{0:T(128)S(1)} %stack.27.place, bf16[96,3072]{1,0:T(8,128)(2,1)S(1)} %copy-done.3, bf16[96,3072]{1,0:T(8,128)(2,1)} %collective-permute-done.8.refs_1_, bf16[3,3072,128]{2,1,0:T(8,128)(2,1)S(1)} %bitcast.39, ...), custom_call_target="tpu_custom_call", output_to_operand_aliasing={{0}: (5, {}), {1}: (6, {})} | custom-call | tf_op jit(solution)/shard_map/project/pallas_call | solution.py:115
  48.9 0.0 collective-permute-done.3.refs_0_
  48.9 0.5 collective-permute-done.7.refs_1_
  49.4 2.8 %project.5 = (bf16[768,128]{1,0:T(8,128)(2,1)S(1)}, bf16[768,256]{1,0:T(8,128)(2,1)}) custom-call(s32[6]{0:T(128)S(1)} %stack.27.place, bf16[96,3072]{1,0:T(8,128)(2,1)} %collective-permute-done.3.refs_0_, bf16[96,3072]{1,0:T(8,128)(2,1)} %collective-permute-done.7.refs_1_, ...), custom_call_target="tpu_custom_call", output_to_operand_aliasing={{0}: (5, {}), {1}: (6, {})} | custom-call | tf_op jit(solution)/shard_map/project/pallas_call | solution.py:115
  52.2 9.2 %collective-permute-start.10 = (bf16[768,256]{1,0:T(8,128)(2,1)}, bf16[768,256]{1,0:T(8,128)(2,1)S(1)}, u32[]{:S(2)}, u32[]{:S(2)}) collective-permute-start(bf16[768,256]{1,0:T(8,128)(2,1)} %get-tuple-element.47), channel_id=1, source_target_pairs={{0,1},{1,0},{2,3},{3,2},{4,5},{5,4},{6,7},{7,6},{8,9},{9,8},{10,11... | collective-permute-start | bytes 1179656 | tf_op jit(solution)/shard_map/ppermute | solution.py:64
  61.5 7.3 %collective-permute-start.9 = (bf16[768,256]{1,0:T(8,128)(2,1)}, bf16[768,256]{1,0:T(8,128)(2,1)S(1)}, u32[]{:S(2)}, u32[]{:S(2)}) collective-permute-start(bf16[768,256]{1,0:T(8,128)(2,1)} %get-tuple-element.47), channel_id=1, source_target_pairs={{0,2},{1,31},{2,4},{3,1},{4,6},{5,3},{6,8},{7,5},{8,10},{9,7},{10,... | collective-permute-start | bytes 1179656 | tf_op jit(solution)/shard_map/ppermute | solution.py:74
  68.8 0.0 collective-permute-done.10
  68.8 2.6 %collective-permute-start.11 = (bf16[768,256]{1,0:T(8,128)(2,1)S(1)}, bf16[768,256]{1,0:T(8,128)(2,1)S(1)}, u32[]{:S(2)}, u32[]{:S(2)}) collective-permute-start(bf16[768,256]{1,0:T(8,128)(2,1)S(1)} %collective-permute-done.10), channel_id=1, source_target_pairs={{0,2},{1,31},{2,4},{3,1},{4,6},{5,3},{6,8},{7,5},{8,10},{9,7},{10,... | collective-permute-start | bytes 1179656 | tf_op jit(solution)/shard_map/ppermute | solution.py:74
  71.4 1.9 %collective-permute-start.13 = (bf16[768,128]{1,0:T(8,128)(2,1)S(1)}, bf16[768,128]{1,0:T(8,128)(2,1)S(1)}, u32[]{:S(2)}, u32[]{:S(2)}) collective-permute-start(bf16[768,128]{1,0:T(8,128)(2,1)S(1)} %get-tuple-element.53), channel_id=1, source_target_pairs={{0,1},{1,0},{2,3},{3,2},{4,5},{5,4},{6,7},{7,6},{8,9},{9,8},{10,11... | collective-permute-start | bytes 589832 | tf_op jit(solution)/shard_map/ppermute | solution.py:64
  73.4 0.1 constant_dynamic-slice_fusion.counts
  73.5 0.1 dynamic-slice_bitcast_fusion.tiles
  73.5 2.6 %lists.1 = (s32[7,384]{1,0:T(8,128)S(1)}, s32[1,7]{1,0:T(1,128)S(1)}) custom-call(s32[6]{0:T(128)S(1)} %stack.27.place, s32[64,12]{1,0:T(8,128)S(1)} %dynamic-slice_bitcast_fusion.tiles, s32[1,12]{1,0:T(1,128)S(1)} %constant_dynamic-slice_fusion.counts), custom_call_target="tpu_custom_call" | custom-call | tf_op jit(solution)/shard_map/lists/pallas_call | solution.py:262
  76.2 2.6 %collective-permute-start.14 = (bf16[768,256]{1,0:T(8,128)(2,1)S(1)}, bf16[768,256]{1,0:T(8,128)(2,1)S(1)}, u32[]{:S(2)}, u32[]{:S(2)}) collective-permute-start(bf16[768,256]{1,0:T(8,128)(2,1)S(1)} %collective-permute-done.9), channel_id=1, source_target_pairs={{0,2},{1,31},{2,4},{3,1},{4,6},{5,3},{6,8},{7,5},{8,10},{9,7},{10,... | collective-permute-start | bytes 1179656 | tf_op jit(solution)/shard_map/ppermute | solution.py:74
  78.8 4.1 %collective-permute-start.12 = (bf16[768,256]{1,0:T(8,128)(2,1)S(1)}, bf16[768,256]{1,0:T(8,128)(2,1)S(1)}, u32[]{:S(2)}, u32[]{:S(2)}) collective-permute-start(bf16[768,256]{1,0:T(8,128)(2,1)S(1)} %collective-permute-done.11), channel_id=1, source_target_pairs={{0,2},{1,31},{2,4},{3,1},{4,6},{5,3},{6,8},{7,5},{8,10},{9,7},{10,... | collective-permute-start | bytes 1179656 | tf_op jit(solution)/shard_map/ppermute | solution.py:74
  83.0 2.0 %collective-permute-done.14 = bf16[768,256]{1,0:T(8,128)(2,1)S(1)} collective-permute-done((bf16[768,256]{1,0:T(8,128)(2,1)S(1)}, bf16[768,256]{1,0:T(8,128)(2,1)S(1)}, u32[]{:S(2)}, u32[]{:S(2)}) %collective-permute-start.14) | collective-permute-done | bytes 393248 | tf_op jit(solution)/shard_map/ppermute | solution.py:74
  85.0 3.5 %collective-permute-start.15 = (bf16[768,256]{1,0:T(8,128)(2,1)S(1)}, bf16[768,256]{1,0:T(8,128)(2,1)S(1)}, u32[]{:S(2)}, u32[]{:S(2)}) collective-permute-start(bf16[768,256]{1,0:T(8,128)(2,1)S(1)} %collective-permute-done.14), channel_id=1, source_target_pairs={{0,2},{1,31},{2,4},{3,1},{4,6},{5,3},{6,8},{7,5},{8,10},{9,7},{10,... | collective-permute-start | bytes 1179656 | tf_op jit(solution)/shard_map/ppermute | solution.py:74
  88.5 0.7 collective-permute-done.12
  89.2 3.5 %collective-permute-start.17 = (bf16[768,256]{1,0:T(8,128)(2,1)S(1)}, bf16[768,256]{1,0:T(8,128)(2,1)S(1)}, u32[]{:S(2)}, u32[]{:S(2)}) collective-permute-start(bf16[768,256]{1,0:T(8,128)(2,1)S(1)} %collective-permute-done.12), channel_id=1, source_target_pairs={{0,2},{1,31},{2,4},{3,1},{4,6},{5,3},{6,8},{7,5},{8,10},{9,7},{10,... | collective-permute-start | bytes 1179656 | tf_op jit(solution)/shard_map/ppermute | solution.py:74
  92.7 2.7 %attend.7.refs_2_ = f32[13,128,256]{2,1,0:T(8,128)S(1)} custom-call(s32[6]{0:T(128)S(1)} %stack.27.place, s32[7,384]{1,0:T(8,128)S(1)} %get-tuple-element.51.pairs, s32[1,7]{1,0:T(1,128)S(1)} %get-tuple-element.52.counts, bf16[12,128,128]{2,1,0:T(8,128)(2,1)S(1)} %bitcast.41, bf16[6,128,256]{2,1,0:T(8,128)(2,1)} %bitcast.12.refs_0_, ...), custom_call_target="tpu_custom_call" | custom-call | flops 5000000000 | bytes 5000000 | tf_op jit(solution)/shard_map/attend/pallas_call | solution.py:193
  95.4 2.9 %collective-permute-start.16 = (bf16[768,256]{1,0:T(8,128)(2,1)S(1)}, bf16[768,256]{1,0:T(8,128)(2,1)S(1)}, u32[]{:S(2)}, u32[]{:S(2)}) collective-permute-start(bf16[768,256]{1,0:T(8,128)(2,1)S(1)} %collective-permute-done.15), channel_id=1, source_target_pairs={{0,2},{1,31},{2,4},{3,1},{4,6},{5,3},{6,8},{7,5},{8,10},{9,7},{10,... | collective-permute-start | bytes 1179656 | tf_op jit(solution)/shard_map/ppermute | solution.py:74
  98.3 4.1 %collective-permute-start.19 = (bf16[768,256]{1,0:T(8,128)(2,1)S(1)}, bf16[768,256]{1,0:T(8,128)(2,1)S(1)}, u32[]{:S(2)}, u32[]{:S(2)}) collective-permute-start(bf16[768,256]{1,0:T(8,128)(2,1)S(1)} %collective-permute-done.17), channel_id=1, source_target_pairs={{0,2},{1,31},{2,4},{3,1},{4,6},{5,3},{6,8},{7,5},{8,10},{9,7},{10,... | collective-permute-start | bytes 1179656 | tf_op jit(solution)/shard_map/ppermute | solution.py:74
  102.5 1.5 attend.8.refs_2_
  104.0 4.1 %collective-permute-start.18 = (bf16[768,256]{1,0:T(8,128)(2,1)S(1)}, bf16[768,256]{1,0:T(8,128)(2,1)S(1)}, u32[]{:S(2)}, u32[]{:S(2)}) collective-permute-start(bf16[768,256]{1,0:T(8,128)(2,1)S(1)} %collective-permute-done.16), channel_id=1, source_target_pairs={{0,2},{1,31},{2,4},{3,1},{4,6},{5,3},{6,8},{7,5},{8,10},{9,7},{10,... | collective-permute-start | bytes 1179656 | tf_op jit(solution)/shard_map/ppermute | solution.py:74
  108.0 0.4 collective-permute-done.19
  108.5 3.8 %collective-permute-start.21 = (bf16[768,256]{1,0:T(8,128)(2,1)S(1)}, bf16[768,256]{1,0:T(8,128)(2,1)S(1)}, u32[]{:S(2)}, u32[]{:S(2)}) collective-permute-start(bf16[768,256]{1,0:T(8,128)(2,1)S(1)} %collective-permute-done.19), channel_id=1, source_target_pairs={{0,2},{1,31},{2,4},{3,1},{4,6},{5,3},{6,8},{7,5},{8,10},{9,7},{10,... | collective-permute-start | bytes 1179656 | tf_op jit(solution)/shard_map/ppermute | solution.py:74
  112.2 1.5 attend.9.refs_2_
  113.8 4.0 %collective-permute-start.20 = (bf16[768,256]{1,0:T(8,128)(2,1)S(1)}, bf16[768,256]{1,0:T(8,128)(2,1)S(1)}, u32[]{:S(2)}, u32[]{:S(2)}) collective-permute-start(bf16[768,256]{1,0:T(8,128)(2,1)S(1)} %collective-permute-done.18), channel_id=1, source_target_pairs={{0,2},{1,31},{2,4},{3,1},{4,6},{5,3},{6,8},{7,5},{8,10},{9,7},{10,... | collective-permute-start | bytes 1179656 | tf_op jit(solution)/shard_map/ppermute | solution.py:74
  117.8 4.2 %collective-permute-start.23 = (bf16[768,256]{1,0:T(8,128)(2,1)S(1)}, bf16[768,256]{1,0:T(8,128)(2,1)S(1)}, u32[]{:S(2)}, u32[]{:S(2)}) collective-permute-start(bf16[768,256]{1,0:T(8,128)(2,1)S(1)} %collective-permute-done.21), channel_id=1, source_target_pairs={{0,2},{1,31},{2,4},{3,1},{4,6},{5,3},{6,8},{7,5},{8,10},{9,7},{10,... | collective-permute-start | bytes 1179656 | tf_op jit(solution)/shard_map/ppermute | solution.py:74
  122.0 1.5 attend.10.refs_2_
  123.5 4.0 %collective-permute-start.22 = (bf16[768,256]{1,0:T(8,128)(2,1)S(1)}, bf16[768,256]{1,0:T(8,128)(2,1)S(1)}, u32[]{:S(2)}, u32[]{:S(2)}) collective-permute-start(bf16[768,256]{1,0:T(8,128)(2,1)S(1)} %collective-permute-done.20), channel_id=1, source_target_pairs={{0,2},{1,31},{2,4},{3,1},{4,6},{5,3},{6,8},{7,5},{8,10},{9,7},{10,... | collective-permute-start | bytes 1179656 | tf_op jit(solution)/shard_map/ppermute | solution.py:74
  127.5 4.2 %collective-permute-start.25 = (bf16[768,256]{1,0:T(8,128)(2,1)S(1)}, bf16[768,256]{1,0:T(8,128)(2,1)S(1)}, u32[]{:S(2)}, u32[]{:S(2)}) collective-permute-start(bf16[768,256]{1,0:T(8,128)(2,1)S(1)} %collective-permute-done.23), channel_id=1, source_target_pairs={{0,2},{1,31},{2,4},{3,1},{4,6},{5,3},{6,8},{7,5},{8,10},{9,7},{10,... | collective-permute-start | bytes 1179656 | tf_op jit(solution)/shard_map/ppermute | solution.py:74
  131.7 1.5 attend.11.refs_2_
  133.2 4.0 %collective-permute-start.24 = (bf16[768,256]{1,0:T(8,128)(2,1)S(1)}, bf16[768,256]{1,0:T(8,128)(2,1)S(1)}, u32[]{:S(2)}, u32[]{:S(2)}) collective-permute-start(bf16[768,256]{1,0:T(8,128)(2,1)S(1)} %collective-permute-done.22), channel_id=1, source_target_pairs={{1,31},{3,1},{5,3},{7,5},{9,7},{11,9},{13,11},{15,13},{17,15},{19,... | collective-permute-start | bytes 1179656 | tf_op jit(solution)/shard_map/ppermute | solution.py:74
  137.2 4.2 %collective-permute-start.26 = (bf16[768,256]{1,0:T(8,128)(2,1)S(1)}, bf16[768,256]{1,0:T(8,128)(2,1)S(1)}, u32[]{:S(2)}, u32[]{:S(2)}) collective-permute-start(bf16[768,256]{1,0:T(8,128)(2,1)S(1)} %collective-permute-done.25), channel_id=1, source_target_pairs={{1,31},{3,1},{5,3},{7,5},{9,7},{11,9},{13,11},{15,13},{17,15},{19,... | collective-permute-start | bytes 1179656 | tf_op jit(solution)/shard_map/ppermute | solution.py:74
  141.4 1.5 attend.12.refs_2_
  142.9 3.2 %collective-permute-done.26 = bf16[768,256]{1,0:T(8,128)(2,1)S(1)} collective-permute-done((bf16[768,256]{1,0:T(8,128)(2,1)S(1)}, bf16[768,256]{1,0:T(8,128)(2,1)S(1)}, u32[]{:S(2)}, u32[]{:S(2)}) %collective-permute-start.26) | collective-permute-done | bytes 393248 | tf_op jit(solution)/shard_map/ppermute | solution.py:74
  146.1 2.0 %attend.13 = (f32[6,128,256]{2,1,0:T(8,128)S(1)}, f32[6,128,256]{2,1,0:T(8,128)S(1)}) custom-call(s32[6]{0:T(128)S(1)} %stack.27.place, s32[7,384]{1,0:T(8,128)S(1)} %get-tuple-element.51.pairs, s32[1,7]{1,0:T(1,128)S(1)} %get-tuple-element.52.counts, bf16[12,128,128]{2,1,0:T(8,128)(2,1)S(1)} %bitcast.47, bf16[6,128,256]{2,1,0:T(8,128)(2,1)S(1)} %bitcast.61, ...), custom_call_target="tpu_custom_call" | custom-call | flops 2000000000 | bytes 2000000 | tf_op jit(solution)/shard_map/attend/pallas_call | solution.py:193
  148.1 3.6 %collective-permute-start.27 = (f32[6,128,256]{2,1,0:T(8,128)S(1)}, f32[6,128,256]{2,1,0:T(8,128)S(1)}, u32[]{:S(2)}, u32[]{:S(2)}) collective-permute-start(f32[6,128,256]{2,1,0:T(8,128)S(1)} %get-tuple-element.72), channel_id=1, source_target_pairs={{0,1},{1,0},{2,3},{3,2},{4,5},{5,4},{6,7},{7,6},{8,9},{9,8},{10,11... | collective-permute-start | bytes 2359304 | tf_op jit(solution)/shard_map/ppermute | solution.py:64
  151.7 1.9 %collective-permute-done.27 = f32[6,128,256]{2,1,0:T(8,128)S(1)} collective-permute-done((f32[6,128,256]{2,1,0:T(8,128)S(1)}, f32[6,128,256]{2,1,0:T(8,128)S(1)}, u32[]{:S(2)}, u32[]{:S(2)}) %collective-permute-start.27) | collective-permute-done | bytes 786464 | tf_op jit(solution)/shard_map/ppermute | solution.py:64
  153.6 0.1 add.19
  153.7 0.1 fusion
  153.8 13.2 %all_to_all.19 = bf16[16,48,128]{2,1,0:T(8,128)(2,1)S(1)} all-to-all(bf16[16,48,128]{2,1,0:T(8,128)(2,1)S(1)} %bitcast.64), channel_id=1, replica_groups=mesh['seq'=16,'bal'=32] {'seq'}, dimensions={0} | all-to-all | bytes 393216 | tf_op jit(solution)/shard_map/all_to_all | solution.py:361
  166.9 0.7 copy_bitcast_fusion
  (31 shorter events, 0.1 us)
Async XLA Ops:
  0.0 73.5 %copy-start = (s32[1,192,64]{1,2,0:T(8,128)S(1)}, s32[1,192,64]{1,2,0:T(8,128)}, u32[]{:S(2)}) copy-start(s32[1,192,64]{1,2,0:T(8,128)} %param.10) | copy-start | bytes 147460
  0.0 42.4 %copy-start.1 = (bf16[3072,1,3,128]{3,0,2,1:T(8,128)(2,1)S(1)}, bf16[3072,1,3,128]{3,0,2,1:T(8,128)(2,1)}, u32[]{:S(2)}) copy-start(bf16[3072,1,3,128]{3,0,2,1:T(8,128)(2,1)} %param.7) | copy-start | bytes 7077892
  0.0 9.9 %collective-permute-start = (bf16[48,3072]{1,0:T(8,128)(2,1)}, bf16[48,3072]{1,0:T(8,128)(2,1)S(1)}, u32[]{:S(2)}, u32[]{:S(2)}) collective-permute-start(bf16[48,3072]{1,0:T(8,128)(2,1)} %upper.1), channel_id=1, source_target_pairs={{0,32},{32,64},{64,96},{96,0},{128,160},{160,192},{192,224},{224,1... | collective-permute-start | bytes 884744 | tf_op jit(solution)/shard_map/ppermute | solution.py:34
  4.2 17.2 %collective-permute-start.4 = (bf16[48,3072]{1,0:T(8,128)(2,1)}, bf16[48,3072]{1,0:T(8,128)(2,1)S(1)}, u32[]{:S(2)}, u32[]{:S(2)}) collective-permute-start(bf16[48,3072]{1,0:T(8,128)(2,1)} %upper.1), channel_id=1, source_target_pairs={{0,96},{32,0},{64,32},{96,64},{128,224},{160,128},{192,160},{224,1... | collective-permute-start | bytes 884744 | tf_op jit(solution)/shard_map/ppermute | solution.py:34
  9.9 1.0 copy-start.4
  10.9 31.5 %copy-start.5 = (f32[1,128]{1,0:T(1,128)S(1)}, f32[1,128]{1,0:T(1,128)}, u32[]{:S(2)}) copy-start(f32[1,128]{1,0:T(1,128)} %param.9) | copy-start | bytes 1540
  10.9 31.5 %copy-start.6 = (f32[1,128]{1,0:T(1,128)S(1)}, f32[1,128]{1,0:T(1,128)}, u32[]{:S(2)}) copy-start(f32[1,128]{1,0:T(1,128)} %param.8) | copy-start | bytes 1540
  11.0 10.4 %collective-permute-start.5 = (bf16[48,3072]{1,0:T(8,128)(2,1)}, bf16[48,3072]{1,0:T(8,128)(2,1)S(1)}, u32[]{:S(2)}, u32[]{:S(2)}) collective-permute-start(bf16[48,3072]{1,0:T(8,128)(2,1)} %upper.1), channel_id=1, source_target_pairs={{0,64},{32,96},{64,0},{96,32},{128,192},{160,224},{192,128},{224,1... | collective-permute-start | bytes 884744 | tf_op jit(solution)/shard_map/ppermute | solution.py:34
  14.9 14.2 %collective-permute-start.1 = (bf16[96,3072]{1,0:T(8,128)(2,1)S(1)}, bf16[96,3072]{1,0:T(8,128)(2,1)}, u32[]{:S(2)}, u32[]{:S(2)}) collective-permute-start(bf16[96,3072]{1,0:T(8,128)(2,1)S(1)} %join.2.refs_0_), channel_id=1, source_target_pairs={{0,128},{32,160},{64,192},{96,224},{128,256},{160,288},{192,320},{... | collective-permute-start | bytes 1769480 | tf_op jit(solution)/shard_map/ppermute | solution.py:34
  18.0 13.5 %collective-permute-start.2 = (bf16[96,3072]{1,0:T(8,128)(2,1)S(1)}, bf16[96,3072]{1,0:T(8,128)(2,1)S(1)}, u32[]{:S(2)}, u32[]{:S(2)}) collective-permute-start(bf16[96,3072]{1,0:T(8,128)(2,1)S(1)} %join.2.refs_0_), channel_id=1, source_target_pairs={{0,384},{32,416},{64,448},{96,480},{128,0},{160,32},{192,64},{224,... | collective-permute-start | bytes 1769480 | tf_op jit(solution)/shard_map/ppermute | solution.py:34
  22.3 15.3 %collective-permute-start.6 = (bf16[96,3072]{1,0:T(8,128)(2,1)}, bf16[96,3072]{1,0:T(8,128)(2,1)}, u32[]{:S(2)}, u32[]{:S(2)}) collective-permute-start(bf16[96,3072]{1,0:T(8,128)(2,1)} %join.3.refs_1_), channel_id=1, source_target_pairs={{0,384},{32,416},{64,448},{96,480},{128,0},{160,32},{192,64},{224,... | collective-permute-start | bytes 1769480 | tf_op jit(solution)/shard_map/ppermute | solution.py:34
  25.5 20.8 %collective-permute-start.8 = (bf16[96,3072]{1,0:T(8,128)(2,1)}, bf16[96,3072]{1,0:T(8,128)(2,1)}, u32[]{:S(2)}, u32[]{:S(2)}) collective-permute-start(bf16[96,3072]{1,0:T(8,128)(2,1)} %join.3.refs_1_), channel_id=1, source_target_pairs={{0,128},{32,160},{64,192},{96,224},{128,256},{160,288},{192,320},{... | collective-permute-start | bytes 1769480 | tf_op jit(solution)/shard_map/ppermute | solution.py:34
  31.5 0.8 copy-start.2
  32.3 16.6 %collective-permute-start.3 = (bf16[96,3072]{1,0:T(8,128)(2,1)}, bf16[96,3072]{1,0:T(8,128)(2,1)}, u32[]{:S(2)}, u32[]{:S(2)}) collective-permute-start(bf16[96,3072]{1,0:T(8,128)(2,1)} %collective-permute-done.1.refs_2_), channel_id=1, source_target_pairs={{0,128},{32,160},{64,192},{96,224},{128,256},{160,288},{192,320},{... | collective-permute-start | bytes 1769480 | tf_op jit(solution)/shard_map/ppermute | solution.py:34
  37.5 11.9 %collective-permute-start.7 = (bf16[96,3072]{1,0:T(8,128)(2,1)}, bf16[96,3072]{1,0:T(8,128)(2,1)}, u32[]{:S(2)}, u32[]{:S(2)}) collective-permute-start(bf16[96,3072]{1,0:T(8,128)(2,1)} %collective-permute-done.6.refs_3_), channel_id=1, source_target_pairs={{0,384},{32,416},{64,448},{96,480},{128,0},{160,32},{192,64},{224,... | collective-permute-start | bytes 1769480 | tf_op jit(solution)/shard_map/ppermute | solution.py:34
  42.4 3.8 %copy-start.3 = (bf16[96,3072]{1,0:T(8,128)(2,1)S(1)}, bf16[96,3072]{1,0:T(8,128)(2,1)}, u32[]{:S(2)}) copy-start(bf16[96,3072]{1,0:T(8,128)(2,1)} %copy-done.2) | copy-start | bytes 1769476
  49.4 24.0 %copy-start.7 = (s32[1,192]{1,0:T(1,128)S(1)}, s32[1,192]{1,0:T(1,128)}, u32[]{:S(2)}) copy-start(s32[1,192]{1,0:T(1,128)} %param.11) | copy-start | bytes 2308
  52.2 16.5 %collective-permute-start.10 = (bf16[768,256]{1,0:T(8,128)(2,1)}, bf16[768,256]{1,0:T(8,128)(2,1)S(1)}, u32[]{:S(2)}, u32[]{:S(2)}) collective-permute-start(bf16[768,256]{1,0:T(8,128)(2,1)} %get-tuple-element.47), channel_id=1, source_target_pairs={{0,1},{1,0},{2,3},{3,2},{4,5},{5,4},{6,7},{7,6},{8,9},{9,8},{10,11... | collective-permute-start | bytes 1179656 | tf_op jit(solution)/shard_map/ppermute | solution.py:64
  61.5 14.6 %collective-permute-start.9 = (bf16[768,256]{1,0:T(8,128)(2,1)}, bf16[768,256]{1,0:T(8,128)(2,1)S(1)}, u32[]{:S(2)}, u32[]{:S(2)}) collective-permute-start(bf16[768,256]{1,0:T(8,128)(2,1)} %get-tuple-element.47), channel_id=1, source_target_pairs={{0,2},{1,31},{2,4},{3,1},{4,6},{5,3},{6,8},{7,5},{8,10},{9,7},{10,... | collective-permute-start | bytes 1179656 | tf_op jit(solution)/shard_map/ppermute | solution.py:74
  68.8 10.0 %collective-permute-start.11 = (bf16[768,256]{1,0:T(8,128)(2,1)S(1)}, bf16[768,256]{1,0:T(8,128)(2,1)S(1)}, u32[]{:S(2)}, u32[]{:S(2)}) collective-permute-start(bf16[768,256]{1,0:T(8,128)(2,1)S(1)} %collective-permute-done.10), channel_id=1, source_target_pairs={{0,2},{1,31},{2,4},{3,1},{4,6},{5,3},{6,8},{7,5},{8,10},{9,7},{10,... | collective-permute-start | bytes 1179656 | tf_op jit(solution)/shard_map/ppermute | solution.py:74
  71.4 4.7 %collective-permute-start.13 = (bf16[768,128]{1,0:T(8,128)(2,1)S(1)}, bf16[768,128]{1,0:T(8,128)(2,1)S(1)}, u32[]{:S(2)}, u32[]{:S(2)}) collective-permute-start(bf16[768,128]{1,0:T(8,128)(2,1)S(1)} %get-tuple-element.53), channel_id=1, source_target_pairs={{0,1},{1,0},{2,3},{3,2},{4,5},{5,4},{6,7},{7,6},{8,9},{9,8},{10,11... | collective-permute-start | bytes 589832 | tf_op jit(solution)/shard_map/ppermute | solution.py:64
  76.2 8.8 %collective-permute-start.14 = (bf16[768,256]{1,0:T(8,128)(2,1)S(1)}, bf16[768,256]{1,0:T(8,128)(2,1)S(1)}, u32[]{:S(2)}, u32[]{:S(2)}) collective-permute-start(bf16[768,256]{1,0:T(8,128)(2,1)S(1)} %collective-permute-done.9), channel_id=1, source_target_pairs={{0,2},{1,31},{2,4},{3,1},{4,6},{5,3},{6,8},{7,5},{8,10},{9,7},{10,... | collective-permute-start | bytes 1179656 | tf_op jit(solution)/shard_map/ppermute | solution.py:74
  78.8 10.4 %collective-permute-start.12 = (bf16[768,256]{1,0:T(8,128)(2,1)S(1)}, bf16[768,256]{1,0:T(8,128)(2,1)S(1)}, u32[]{:S(2)}, u32[]{:S(2)}) collective-permute-start(bf16[768,256]{1,0:T(8,128)(2,1)S(1)} %collective-permute-done.11), channel_id=1, source_target_pairs={{0,2},{1,31},{2,4},{3,1},{4,6},{5,3},{6,8},{7,5},{8,10},{9,7},{10,... | collective-permute-start | bytes 1179656 | tf_op jit(solution)/shard_map/ppermute | solution.py:74
  85.0 10.4 %collective-permute-start.15 = (bf16[768,256]{1,0:T(8,128)(2,1)S(1)}, bf16[768,256]{1,0:T(8,128)(2,1)S(1)}, u32[]{:S(2)}, u32[]{:S(2)}) collective-permute-start(bf16[768,256]{1,0:T(8,128)(2,1)S(1)} %collective-permute-done.14), channel_id=1, source_target_pairs={{0,2},{1,31},{2,4},{3,1},{4,6},{5,3},{6,8},{7,5},{8,10},{9,7},{10,... | collective-permute-start | bytes 1179656 | tf_op jit(solution)/shard_map/ppermute | solution.py:74
  89.2 9.1 %collective-permute-start.17 = (bf16[768,256]{1,0:T(8,128)(2,1)S(1)}, bf16[768,256]{1,0:T(8,128)(2,1)S(1)}, u32[]{:S(2)}, u32[]{:S(2)}) collective-permute-start(bf16[768,256]{1,0:T(8,128)(2,1)S(1)} %collective-permute-done.12), channel_id=1, source_target_pairs={{0,2},{1,31},{2,4},{3,1},{4,6},{5,3},{6,8},{7,5},{8,10},{9,7},{10,... | collective-permute-start | bytes 1179656 | tf_op jit(solution)/shard_map/ppermute | solution.py:74
  95.4 8.5 %collective-permute-start.16 = (bf16[768,256]{1,0:T(8,128)(2,1)S(1)}, bf16[768,256]{1,0:T(8,128)(2,1)S(1)}, u32[]{:S(2)}, u32[]{:S(2)}) collective-permute-start(bf16[768,256]{1,0:T(8,128)(2,1)S(1)} %collective-permute-done.15), channel_id=1, source_target_pairs={{0,2},{1,31},{2,4},{3,1},{4,6},{5,3},{6,8},{7,5},{8,10},{9,7},{10,... | collective-permute-start | bytes 1179656 | tf_op jit(solution)/shard_map/ppermute | solution.py:74
  98.3 10.1 %collective-permute-start.19 = (bf16[768,256]{1,0:T(8,128)(2,1)S(1)}, bf16[768,256]{1,0:T(8,128)(2,1)S(1)}, u32[]{:S(2)}, u32[]{:S(2)}) collective-permute-start(bf16[768,256]{1,0:T(8,128)(2,1)S(1)} %collective-permute-done.17), channel_id=1, source_target_pairs={{0,2},{1,31},{2,4},{3,1},{4,6},{5,3},{6,8},{7,5},{8,10},{9,7},{10,... | collective-permute-start | bytes 1179656 | tf_op jit(solution)/shard_map/ppermute | solution.py:74
  104.0 9.8 %collective-permute-start.18 = (bf16[768,256]{1,0:T(8,128)(2,1)S(1)}, bf16[768,256]{1,0:T(8,128)(2,1)S(1)}, u32[]{:S(2)}, u32[]{:S(2)}) collective-permute-start(bf16[768,256]{1,0:T(8,128)(2,1)S(1)} %collective-permute-done.16), channel_id=1, source_target_pairs={{0,2},{1,31},{2,4},{3,1},{4,6},{5,3},{6,8},{7,5},{8,10},{9,7},{10,... | collective-permute-start | bytes 1179656 | tf_op jit(solution)/shard_map/ppermute | solution.py:74
  108.5 9.3 %collective-permute-start.21 = (bf16[768,256]{1,0:T(8,128)(2,1)S(1)}, bf16[768,256]{1,0:T(8,128)(2,1)S(1)}, u32[]{:S(2)}, u32[]{:S(2)}) collective-permute-start(bf16[768,256]{1,0:T(8,128)(2,1)S(1)} %collective-permute-done.19), channel_id=1, source_target_pairs={{0,2},{1,31},{2,4},{3,1},{4,6},{5,3},{6,8},{7,5},{8,10},{9,7},{10,... | collective-permute-start | bytes 1179656 | tf_op jit(solution)/shard_map/ppermute | solution.py:74
  113.8 9.7 %collective-permute-start.20 = (bf16[768,256]{1,0:T(8,128)(2,1)S(1)}, bf16[768,256]{1,0:T(8,128)(2,1)S(1)}, u32[]{:S(2)}, u32[]{:S(2)}) collective-permute-start(bf16[768,256]{1,0:T(8,128)(2,1)S(1)} %collective-permute-done.18), channel_id=1, source_target_pairs={{0,2},{1,31},{2,4},{3,1},{4,6},{5,3},{6,8},{7,5},{8,10},{9,7},{10,... | collective-permute-start | bytes 1179656 | tf_op jit(solution)/shard_map/ppermute | solution.py:74
  117.8 9.7 %collective-permute-start.23 = (bf16[768,256]{1,0:T(8,128)(2,1)S(1)}, bf16[768,256]{1,0:T(8,128)(2,1)S(1)}, u32[]{:S(2)}, u32[]{:S(2)}) collective-permute-start(bf16[768,256]{1,0:T(8,128)(2,1)S(1)} %collective-permute-done.21), channel_id=1, source_target_pairs={{0,2},{1,31},{2,4},{3,1},{4,6},{5,3},{6,8},{7,5},{8,10},{9,7},{10,... | collective-permute-start | bytes 1179656 | tf_op jit(solution)/shard_map/ppermute | solution.py:74
  123.5 9.7 %collective-permute-start.22 = (bf16[768,256]{1,0:T(8,128)(2,1)S(1)}, bf16[768,256]{1,0:T(8,128)(2,1)S(1)}, u32[]{:S(2)}, u32[]{:S(2)}) collective-permute-start(bf16[768,256]{1,0:T(8,128)(2,1)S(1)} %collective-permute-done.20), channel_id=1, source_target_pairs={{0,2},{1,31},{2,4},{3,1},{4,6},{5,3},{6,8},{7,5},{8,10},{9,7},{10,... | collective-permute-start | bytes 1179656 | tf_op jit(solution)/shard_map/ppermute | solution.py:74
  127.5 9.7 %collective-permute-start.25 = (bf16[768,256]{1,0:T(8,128)(2,1)S(1)}, bf16[768,256]{1,0:T(8,128)(2,1)S(1)}, u32[]{:S(2)}, u32[]{:S(2)}) collective-permute-start(bf16[768,256]{1,0:T(8,128)(2,1)S(1)} %collective-permute-done.23), channel_id=1, source_target_pairs={{0,2},{1,31},{2,4},{3,1},{4,6},{5,3},{6,8},{7,5},{8,10},{9,7},{10,... | collective-permute-start | bytes 1179656 | tf_op jit(solution)/shard_map/ppermute | solution.py:74
  133.2 9.7 %collective-permute-start.24 = (bf16[768,256]{1,0:T(8,128)(2,1)S(1)}, bf16[768,256]{1,0:T(8,128)(2,1)S(1)}, u32[]{:S(2)}, u32[]{:S(2)}) collective-permute-start(bf16[768,256]{1,0:T(8,128)(2,1)S(1)} %collective-permute-done.22), channel_id=1, source_target_pairs={{1,31},{3,1},{5,3},{7,5},{9,7},{11,9},{13,11},{15,13},{17,15},{19,... | collective-permute-start | bytes 1179656 | tf_op jit(solution)/shard_map/ppermute | solution.py:74
  137.2 8.9 %collective-permute-start.26 = (bf16[768,256]{1,0:T(8,128)(2,1)S(1)}, bf16[768,256]{1,0:T(8,128)(2,1)S(1)}, u32[]{:S(2)}, u32[]{:S(2)}) collective-permute-start(bf16[768,256]{1,0:T(8,128)(2,1)S(1)} %collective-permute-done.25), channel_id=1, source_target_pairs={{1,31},{3,1},{5,3},{7,5},{9,7},{11,9},{13,11},{15,13},{17,15},{19,... | collective-permute-start | bytes 1179656 | tf_op jit(solution)/shard_map/ppermute | solution.py:74
  148.1 5.5 %collective-permute-start.27 = (f32[6,128,256]{2,1,0:T(8,128)S(1)}, f32[6,128,256]{2,1,0:T(8,128)S(1)}, u32[]{:S(2)}, u32[]{:S(2)}) collective-permute-start(f32[6,128,256]{2,1,0:T(8,128)S(1)} %get-tuple-element.72), channel_id=1, source_target_pairs={{0,1},{1,0},{2,3},{3,2},{4,5},{5,4},{6,7},{7,6},{8,9},{9,8},{10,11... | collective-permute-start | bytes 2359304 | tf_op jit(solution)/shard_map/ppermute | solution.py:64

commit v11 on v10

--- a/solution.py
+++ b/solution.py
@@ -289,22 +289,21 @@
     ).astype(jnp.int32)
     slots = 16 * PIECE // TILE
     before = send(tokens, 1, 1)
+    across = send(tokens, 1, 2)
     after = send(tokens, 1, -1)
     low = join(tokens, before)
-    low, late = lax.optimization_barrier((low, tokens))
-    across = send(late, 1, 2)
+    gains = jnp.concatenate((q_gain, k_gain), axis=0)
+    weight = jnp.transpose(qkv_weight[:, 0], (1, 0, 2))
+    low, gains, across, after = lax.optimization_barrier((low, gains, across, after))
+    high = join(across, after)
+    after_high = send(high, 2, -1)
     before_low = send(low, 2, 1)
+    before_high = send(high, 2, 1)
     after_low = send(low, 2, -1)
-    before_low, after_low = lax.optimization_barrier((before_low, after_low))
-    high = join(after, across)
-    after_high = send(high, 2, -1)
-    before_high = send(high, 2, 1)
     across_low = send(before_low, 2, 1)
     across_high = send(after_high, 2, -1)
 
-    gains = jnp.concatenate((q_gain, k_gain), axis=0)
-    weight = jnp.transpose(qkv_weight[:, 0], (1, 0, 2))
-    low_pieces, high_pieces = (0, 3), (1, 2)
+    low_pieces, high_pieces = (0, 3), (2, 1)
     begun = project(
         ((0, low_pieces), (0, high_pieces), (3, low_pieces), (1, high_pieces)),
         (low, high, before_low, after_high),

time: 169 us -> 165 us (0.976)
  Pallas kernels: 25 us -> 27.5 us
  starting transfers between devices: 109 us -> 107 us
  waiting for transfers between devices: 16.8 us -> 15 us
    pallas_call x7, Pallas kernels: 12.1 us -> 14.5 us  [attend(): pl.pallas_call(functools.partial(attend_kernel, scale, first_call, last_c...]
    ppermute x3, starting transfers between devices: 14.8 us -> 13 us  [swap_cores(): return lax.ppermute(block, 'bal', [(at, at ^ 1) for at in range(32)])]
  transfers between devices with their start and end apart: 28 -> 28, of which waited for: 10 -> 11; matrix products, arithmetic and copies ran while one was open for 0% -> 1% of each run, Pallas kernels for 12% -> 13%
where the time goes in v11:
time: 165 us; the launch traced here: 164 us
  starting transfers between devices  107 us (65%)
  Pallas kernels  27.5 us (17%)
  waiting for transfers between devices  15 us (9%)
  blocking collectives  11.9 us (7%)
  local copies, waits for them, and re-layouts  1.9 us (1%)
    ppermute x16, starting transfers between devices, pass_on(): return lax.ppermute(block, 'bal', pairs)  63.7 us
    ppermute x9, starting transfers between devices, send(): return lax.ppermute(block, MESH_AXES, plane_perm(phase, shift))  30.1 us
    pallas_call x7, Pallas kernels, attend(): pl.pallas_call(functools.partial(attend_kernel, scale, first_call, last_c...  14.5 us
    ppermute x3, starting transfers between devices, swap_cores(): return lax.ppermute(block, 'bal', [(at, at ^ 1) for at in range(32)])  13 us
    all_to_all x1, blocking collectives, on_device(): lax.all_to_all(result.reshape(slots * TILE, HEAD), 'seq', split_axis=0, c...  11.9 us
    pallas_call x3, Pallas kernels, project(): pl.pallas_call(functools.partial(project_kernel, shares), out_shape=(jax....  9.36 us
    ppermute x9, waiting for transfers between devices, send(): return lax.ppermute(block, MESH_AXES, plane_perm(phase, shift))  7.35 us
    ppermute x16, waiting for transfers between devices, pass_on(): return lax.ppermute(block, 'bal', pairs)  5.71 us
  transfers between devices with their start and end apart: 28, of which 11 were waited for; matrix products, arithmetic and copies ran while one was open for 1% of the time, Pallas kernels for 13%

profile of v11, /device:TPU:1, one launch (start us, length us, event | category | flops | bytes accessed | tf_op | source)
XLA Modules:
  0.0 164.4 jit_solution(4810994866816492860)
XLA Ops:
  0.0 4.2 %collective-permute-start = (bf16[48,3072]{1,0:T(8,128)(2,1)}, bf16[48,3072]{1,0:T(8,128)(2,1)S(1)}, u32[]{:S(2)}, u32[]{:S(2)}) collective-permute-start(bf16[48,3072]{1,0:T(8,128)(2,1)} %upper.1), channel_id=1, source_target_pairs={{0,32},{32,64},{64,96},{96,0},{128,160},{160,192},{192,224},{224,1... | collective-permute-start | bytes 884744 | tf_op jit(solution)/shard_map/ppermute | solution.py:34
  4.2 4.5 %collective-permute-start.1 = (bf16[48,3072]{1,0:T(8,128)(2,1)}, bf16[48,3072]{1,0:T(8,128)(2,1)S(1)}, u32[]{:S(2)}, u32[]{:S(2)}) collective-permute-start(bf16[48,3072]{1,0:T(8,128)(2,1)} %upper.1), channel_id=1, source_target_pairs={{0,64},{32,96},{64,0},{96,32},{128,192},{160,224},{192,128},{224,1... | collective-permute-start | bytes 884744 | tf_op jit(solution)/shard_map/ppermute | solution.py:34
  8.7 3.0 %collective-permute-start.2 = (bf16[48,3072]{1,0:T(8,128)(2,1)}, bf16[48,3072]{1,0:T(8,128)(2,1)S(1)}, u32[]{:S(2)}, u32[]{:S(2)}) collective-permute-start(bf16[48,3072]{1,0:T(8,128)(2,1)} %upper.1), channel_id=1, source_target_pairs={{0,96},{32,0},{64,32},{96,64},{128,224},{160,128},{192,160},{224,1... | collective-permute-start | bytes 884744 | tf_op jit(solution)/shard_map/ppermute | solution.py:34
  11.7 0.7 pad_maximum_fusion.1.refs_5_.refs_3_
  12.4 0.0 collective-permute-done.lower
  12.4 0.0 copy-start.2
  12.4 1.0 copy-done.2
  13.3 0.1 join.2.refs_0_
  13.5 0.8 collective-permute-done.1.upper
  14.2 2.4 %collective-permute-done.2.lower = bf16[48,3072]{1,0:T(8,128)(2,1)S(1)} collective-permute-done((bf16[48,3072]{1,0:T(8,128)(2,1)}, bf16[48,3072]{1,0:T(8,128)(2,1)S(1)}, u32[]{:S(2)}, u32[]{:S(2)}) %collective-permute-start.2) | collective-permute-done | bytes 294944 | tf_op jit(solution)/shard_map/ppermute | solution.py:34
  16.7 0.8 join.3.refs_1_
  17.5 4.4 %collective-permute-start.5 = (bf16[96,3072]{1,0:T(8,128)(2,1)}, bf16[96,3072]{1,0:T(8,128)(2,1)}, u32[]{:S(2)}, u32[]{:S(2)}) collective-permute-start(bf16[96,3072]{1,0:T(8,128)(2,1)} %join.3.refs_1_), channel_id=1, source_target_pairs={{0,384},{32,416},{64,448},{96,480},{128,0},{160,32},{192,64},{224,... | collective-permute-start | bytes 1769480 | tf_op jit(solution)/shard_map/ppermute | solution.py:34
  21.9 1.9 %collective-permute-start.3 = (bf16[96,3072]{1,0:T(8,128)(2,1)S(1)}, bf16[96,3072]{1,0:T(8,128)(2,1)}, u32[]{:S(2)}, u32[]{:S(2)}) collective-permute-start(bf16[96,3072]{1,0:T(8,128)(2,1)S(1)} %join.2.refs_0_), channel_id=1, source_target_pairs={{0,128},{32,160},{64,192},{96,224},{128,256},{160,288},{192,320},{... | collective-permute-start | bytes 1769480 | tf_op jit(solution)/shard_map/ppermute | solution.py:34
  23.9 2.1 %collective-permute-start.8 = (bf16[96,3072]{1,0:T(8,128)(2,1)}, bf16[96,3072]{1,0:T(8,128)(2,1)}, u32[]{:S(2)}, u32[]{:S(2)}) collective-permute-start(bf16[96,3072]{1,0:T(8,128)(2,1)} %join.3.refs_1_), channel_id=1, source_target_pairs={{0,128},{32,160},{64,192},{96,224},{128,256},{160,288},{192,320},{... | collective-permute-start | bytes 1769480 | tf_op jit(solution)/shard_map/ppermute | solution.py:34
  26.0 4.4 %collective-permute-start.7 = (bf16[96,3072]{1,0:T(8,128)(2,1)S(1)}, bf16[96,3072]{1,0:T(8,128)(2,1)}, u32[]{:S(2)}, u32[]{:S(2)}) collective-permute-start(bf16[96,3072]{1,0:T(8,128)(2,1)S(1)} %join.2.refs_0_), channel_id=1, source_target_pairs={{0,384},{32,416},{64,448},{96,480},{128,0},{160,32},{192,64},{224,... | collective-permute-start | bytes 1769480 | tf_op jit(solution)/shard_map/ppermute | solution.py:34
  30.4 0.0 collective-permute-done.5.refs_3_
  30.4 3.7 %collective-permute-start.6 = (bf16[96,3072]{1,0:T(8,128)(2,1)}, bf16[96,3072]{1,0:T(8,128)(2,1)}, u32[]{:S(2)}, u32[]{:S(2)}) collective-permute-start(bf16[96,3072]{1,0:T(8,128)(2,1)} %collective-permute-done.5.refs_3_), channel_id=1, source_target_pairs={{0,384},{32,416},{64,448},{96,480},{128,0},{160,32},{192,64},{224,... | collective-permute-start | bytes 1769480 | tf_op jit(solution)/shard_map/ppermute | solution.py:34
  34.1 0.1 collective-permute-done.3.refs_2_
  34.2 1.9 %collective-permute-start.4 = (bf16[96,3072]{1,0:T(8,128)(2,1)}, bf16[96,3072]{1,0:T(8,128)(2,1)}, u32[]{:S(2)}, u32[]{:S(2)}) collective-permute-start(bf16[96,3072]{1,0:T(8,128)(2,1)} %collective-permute-done.3.refs_2_), channel_id=1, source_target_pairs={{0,128},{32,160},{64,192},{96,224},{128,256},{160,288},{192,320},{... | collective-permute-start | bytes 1769480 | tf_op jit(solution)/shard_map/ppermute | solution.py:34
  36.1 0.1 stack.27.place
  36.2 3.7 %project.3 = (bf16[768,128]{1,0:T(8,128)(2,1)S(1)}, bf16[768,256]{1,0:T(8,128)(2,1)}) custom-call(s32[6]{0:T(128)S(1)} %stack.27.place, bf16[96,3072]{1,0:T(8,128)(2,1)S(1)} %join.2.refs_0_, bf16[96,3072]{1,0:T(8,128)(2,1)} %join.3.refs_1_, bf16[96,3072]{1,0:T(8,128)(2,1)} %collective-permute-done.3.refs_2_, ...), custom_call_target="tpu_custom_call" | custom-call | tf_op jit(solution)/shard_map/project/pallas_call | solution.py:115
  39.9 0.6 collective-permute-done.8.refs_1_
  40.5 2.8 %project.4 = (bf16[768,128]{1,0:T(8,128)(2,1)S(1)}, bf16[768,256]{1,0:T(8,128)(2,1)}) custom-call(s32[6]{0:T(128)S(1)} %stack.27.place, bf16[96,3072]{1,0:T(8,128)(2,1)} %collective-permute-done.7.refs_0_, bf16[96,3072]{1,0:T(8,128)(2,1)} %collective-permute-done.8.refs_1_, ...), custom_call_target="tpu_custom_call", output_to_operand_aliasing={{0}: (5, {}), {1}: (6, {})} | custom-call | tf_op jit(solution)/shard_map/project/pallas_call | solution.py:115
  43.3 0.3 collective-permute-done.6.refs_1_
  43.6 3.2 %collective-permute-done.4.refs_0_ = bf16[96,3072]{1,0:T(8,128)(2,1)} collective-permute-done((bf16[96,3072]{1,0:T(8,128)(2,1)}, bf16[96,3072]{1,0:T(8,128)(2,1)}, u32[]{:S(2)}, u32[]{:S(2)}) %collective-permute-start.4) | collective-permute-done | bytes 589856 | tf_op jit(solution)/shard_map/ppermute | solution.py:34
  46.8 2.8 %project.5 = (bf16[768,128]{1,0:T(8,128)(2,1)S(1)}, bf16[768,256]{1,0:T(8,128)(2,1)}) custom-call(s32[6]{0:T(128)S(1)} %stack.27.place, bf16[96,3072]{1,0:T(8,128)(2,1)} %collective-permute-done.4.refs_0_, bf16[96,3072]{1,0:T(8,128)(2,1)} %collective-permute-done.6.refs_1_, ...), custom_call_target="tpu_custom_call", output_to_operand_aliasing={{0}: (5, {}), {1}: (6, {})} | custom-call | tf_op jit(solution)/shard_map/project/pallas_call | solution.py:115
  49.7 7.6 %collective-permute-start.10 = (bf16[768,256]{1,0:T(8,128)(2,1)}, bf16[768,256]{1,0:T(8,128)(2,1)S(1)}, u32[]{:S(2)}, u32[]{:S(2)}) collective-permute-start(bf16[768,256]{1,0:T(8,128)(2,1)} %get-tuple-element.47), channel_id=1, source_target_pairs={{0,1},{1,0},{2,3},{3,2},{4,5},{5,4},{6,7},{7,6},{8,9},{9,8},{10,11... | collective-permute-start | bytes 1179656 | tf_op jit(solution)/shard_map/ppermute | solution.py:64
  57.3 9.5 %collective-permute-start.9 = (bf16[768,256]{1,0:T(8,128)(2,1)}, bf16[768,256]{1,0:T(8,128)(2,1)S(1)}, u32[]{:S(2)}, u32[]{:S(2)}) collective-permute-start(bf16[768,256]{1,0:T(8,128)(2,1)} %get-tuple-element.47), channel_id=1, source_target_pairs={{0,2},{1,31},{2,4},{3,1},{4,6},{5,3},{6,8},{7,5},{8,10},{9,7},{10,... | collective-permute-start | bytes 1179656 | tf_op jit(solution)/shard_map/ppermute | solution.py:74
  66.8 2.6 %collective-permute-start.11 = (bf16[768,256]{1,0:T(8,128)(2,1)S(1)}, bf16[768,256]{1,0:T(8,128)(2,1)S(1)}, u32[]{:S(2)}, u32[]{:S(2)}) collective-permute-start(bf16[768,256]{1,0:T(8,128)(2,1)S(1)} %collective-permute-done.10), channel_id=1, source_target_pairs={{0,2},{1,31},{2,4},{3,1},{4,6},{5,3},{6,8},{7,5},{8,10},{9,7},{10,... | collective-permute-start | bytes 1179656 | tf_op jit(solution)/shard_map/ppermute | solution.py:74
  69.5 1.9 %collective-permute-start.13 = (bf16[768,128]{1,0:T(8,128)(2,1)S(1)}, bf16[768,128]{1,0:T(8,128)(2,1)S(1)}, u32[]{:S(2)}, u32[]{:S(2)}) collective-permute-start(bf16[768,128]{1,0:T(8,128)(2,1)S(1)} %get-tuple-element.53), channel_id=1, source_target_pairs={{0,1},{1,0},{2,3},{3,2},{4,5},{5,4},{6,7},{7,6},{8,9},{9,8},{10,11... | collective-permute-start | bytes 589832 | tf_op jit(solution)/shard_map/ppermute | solution.py:64
  71.4 0.1 constant_dynamic-slice_fusion.counts
  71.5 0.1 dynamic-slice_bitcast_fusion.tiles
  71.5 2.6 %lists.1 = (s32[7,384]{1,0:T(8,128)S(1)}, s32[1,7]{1,0:T(1,128)S(1)}) custom-call(s32[6]{0:T(128)S(1)} %stack.27.place, s32[64,12]{1,0:T(8,128)S(1)} %dynamic-slice_bitcast_fusion.tiles, s32[1,12]{1,0:T(1,128)S(1)} %constant_dynamic-slice_fusion.counts), custom_call_target="tpu_custom_call" | custom-call | tf_op jit(solution)/shard_map/lists/pallas_call | solution.py:262
  74.2 2.6 %collective-permute-start.14 = (bf16[768,256]{1,0:T(8,128)(2,1)S(1)}, bf16[768,256]{1,0:T(8,128)(2,1)S(1)}, u32[]{:S(2)}, u32[]{:S(2)}) collective-permute-start(bf16[768,256]{1,0:T(8,128)(2,1)S(1)} %collective-permute-done.9), channel_id=1, source_target_pairs={{0,2},{1,31},{2,4},{3,1},{4,6},{5,3},{6,8},{7,5},{8,10},{9,7},{10,... | collective-permute-start | bytes 1179656 | tf_op jit(solution)/shard_map/ppermute | solution.py:74
  76.8 4.1 %collective-permute-start.12 = (bf16[768,256]{1,0:T(8,128)(2,1)S(1)}, bf16[768,256]{1,0:T(8,128)(2,1)S(1)}, u32[]{:S(2)}, u32[]{:S(2)}) collective-permute-start(bf16[768,256]{1,0:T(8,128)(2,1)S(1)} %collective-permute-done.11), channel_id=1, source_target_pairs={{0,2},{1,31},{2,4},{3,1},{4,6},{5,3},{6,8},{7,5},{8,10},{9,7},{10,... | collective-permute-start | bytes 1179656 | tf_op jit(solution)/shard_map/ppermute | solution.py:74
  81.0 2.0 %collective-permute-done.14 = bf16[768,256]{1,0:T(8,128)(2,1)S(1)} collective-permute-done((bf16[768,256]{1,0:T(8,128)(2,1)S(1)}, bf16[768,256]{1,0:T(8,128)(2,1)S(1)}, u32[]{:S(2)}, u32[]{:S(2)}) %collective-permute-start.14) | collective-permute-done | bytes 393248 | tf_op jit(solution)/shard_map/ppermute | solution.py:74
  83.0 3.5 %collective-permute-start.15 = (bf16[768,256]{1,0:T(8,128)(2,1)S(1)}, bf16[768,256]{1,0:T(8,128)(2,1)S(1)}, u32[]{:S(2)}, u32[]{:S(2)}) collective-permute-start(bf16[768,256]{1,0:T(8,128)(2,1)S(1)} %collective-permute-done.14), channel_id=1, source_target_pairs={{0,2},{1,31},{2,4},{3,1},{4,6},{5,3},{6,8},{7,5},{8,10},{9,7},{10,... | collective-permute-start | bytes 1179656 | tf_op jit(solution)/shard_map/ppermute | solution.py:74
  86.5 0.7 collective-permute-done.12
  87.2 3.5 %collective-permute-start.17 = (bf16[768,256]{1,0:T(8,128)(2,1)S(1)}, bf16[768,256]{1,0:T(8,128)(2,1)S(1)}, u32[]{:S(2)}, u32[]{:S(2)}) collective-permute-start(bf16[768,256]{1,0:T(8,128)(2,1)S(1)} %collective-permute-done.12), channel_id=1, source_target_pairs={{0,2},{1,31},{2,4},{3,1},{4,6},{5,3},{6,8},{7,5},{8,10},{9,7},{10,... | collective-permute-start | bytes 1179656 | tf_op jit(solution)/shard_map/ppermute | solution.py:74
  90.7 2.7 %attend.7.refs_2_ = f32[13,128,256]{2,1,0:T(8,128)S(1)} custom-call(s32[6]{0:T(128)S(1)} %stack.27.place, s32[7,384]{1,0:T(8,128)S(1)} %get-tuple-element.51.pairs, s32[1,7]{1,0:T(1,128)S(1)} %get-tuple-element.52.counts, bf16[12,128,128]{2,1,0:T(8,128)(2,1)S(1)} %bitcast.41, bf16[6,128,256]{2,1,0:T(8,128)(2,1)} %bitcast.12.refs_0_, ...), custom_call_target="tpu_custom_call" | custom-call | flops 5000000000 | bytes 5000000 | tf_op jit(solution)/shard_map/attend/pallas_call | solution.py:193
  93.5 2.8 %collective-permute-start.16 = (bf16[768,256]{1,0:T(8,128)(2,1)S(1)}, bf16[768,256]{1,0:T(8,128)(2,1)S(1)}, u32[]{:S(2)}, u32[]{:S(2)}) collective-permute-start(bf16[768,256]{1,0:T(8,128)(2,1)S(1)} %collective-permute-done.15), channel_id=1, source_target_pairs={{0,2},{1,31},{2,4},{3,1},{4,6},{5,3},{6,8},{7,5},{8,10},{9,7},{10,... | collective-permute-start | bytes 1179656 | tf_op jit(solution)/shard_map/ppermute | solution.py:74
  96.3 4.2 %collective-permute-start.19 = (bf16[768,256]{1,0:T(8,128)(2,1)S(1)}, bf16[768,256]{1,0:T(8,128)(2,1)S(1)}, u32[]{:S(2)}, u32[]{:S(2)}) collective-permute-start(bf16[768,256]{1,0:T(8,128)(2,1)S(1)} %collective-permute-done.17), channel_id=1, source_target_pairs={{0,2},{1,31},{2,4},{3,1},{4,6},{5,3},{6,8},{7,5},{8,10},{9,7},{10,... | collective-permute-start | bytes 1179656 | tf_op jit(solution)/shard_map/ppermute | solution.py:74
  100.5 2.0 %attend.8.refs_2_ = f32[13,128,256]{2,1,0:T(8,128)S(1)} custom-call(s32[6]{0:T(128)S(1)} %stack.27.place, s32[7,384]{1,0:T(8,128)S(1)} %get-tuple-element.51.pairs, s32[1,7]{1,0:T(1,128)S(1)} %get-tuple-element.52.counts, bf16[12,128,128]{2,1,0:T(8,128)(2,1)S(1)} %bitcast.42, bf16[6,128,256]{2,1,0:T(8,128)(2,1)S(1)} %bitcast.53, ...), custom_call_target="tpu_custom_call", output_to_operand_aliasing={{}: (6, {})} | custom-call | flops 2000000000 | bytes 2000000 | tf_op jit(solution)/shard_map/attend/pallas_call | solution.py:193
  102.5 3.5 %collective-permute-start.18 = (bf16[768,256]{1,0:T(8,128)(2,1)S(1)}, bf16[768,256]{1,0:T(8,128)(2,1)S(1)}, u32[]{:S(2)}, u32[]{:S(2)}) collective-permute-start(bf16[768,256]{1,0:T(8,128)(2,1)S(1)} %collective-permute-done.16), channel_id=1, source_target_pairs={{0,2},{1,31},{2,4},{3,1},{4,6},{5,3},{6,8},{7,5},{8,10},{9,7},{10,... | collective-permute-start | bytes 1179656 | tf_op jit(solution)/shard_map/ppermute | solution.py:74
  106.0 0.5 collective-permute-done.19
  106.5 3.7 %collective-permute-start.21 = (bf16[768,256]{1,0:T(8,128)(2,1)S(1)}, bf16[768,256]{1,0:T(8,128)(2,1)S(1)}, u32[]{:S(2)}, u32[]{:S(2)}) collective-permute-start(bf16[768,256]{1,0:T(8,128)(2,1)S(1)} %collective-permute-done.19), channel_id=1, source_target_pairs={{0,2},{1,31},{2,4},{3,1},{4,6},{5,3},{6,8},{7,5},{8,10},{9,7},{10,... | collective-permute-start | bytes 1179656 | tf_op jit(solution)/shard_map/ppermute | solution.py:74
  110.2 1.5 attend.9.refs_2_
  111.7 4.0 %collective-permute-start.20 = (bf16[768,256]{1,0:T(8,128)(2,1)S(1)}, bf16[768,256]{1,0:T(8,128)(2,1)S(1)}, u32[]{:S(2)}, u32[]{:S(2)}) collective-permute-start(bf16[768,256]{1,0:T(8,128)(2,1)S(1)} %collective-permute-done.18), channel_id=1, source_target_pairs={{0,2},{1,31},{2,4},{3,1},{4,6},{5,3},{6,8},{7,5},{8,10},{9,7},{10,... | collective-permute-start | bytes 1179656 | tf_op jit(solution)/shard_map/ppermute | solution.py:74
  115.7 4.2 %collective-permute-start.23 = (bf16[768,256]{1,0:T(8,128)(2,1)S(1)}, bf16[768,256]{1,0:T(8,128)(2,1)S(1)}, u32[]{:S(2)}, u32[]{:S(2)}) collective-permute-start(bf16[768,256]{1,0:T(8,128)(2,1)S(1)} %collective-permute-done.21), channel_id=1, source_target_pairs={{0,2},{1,31},{2,4},{3,1},{4,6},{5,3},{6,8},{7,5},{8,10},{9,7},{10,... | collective-permute-start | bytes 1179656 | tf_op jit(solution)/shard_map/ppermute | solution.py:74
  119.9 2.0 %attend.10.refs_2_ = f32[13,128,256]{2,1,0:T(8,128)S(1)} custom-call(s32[6]{0:T(128)S(1)} %stack.27.place, s32[7,384]{1,0:T(8,128)S(1)} %get-tuple-element.51.pairs, s32[1,7]{1,0:T(1,128)S(1)} %get-tuple-element.52.counts, bf16[12,128,128]{2,1,0:T(8,128)(2,1)S(1)} %bitcast.44, bf16[6,128,256]{2,1,0:T(8,128)(2,1)S(1)} %bitcast.56, ...), custom_call_target="tpu_custom_call", output_to_operand_aliasing={{}: (6, {})} | custom-call | flops 2000000000 | bytes 2000000 | tf_op jit(solution)/shard_map/attend/pallas_call | solution.py:193
  121.9 3.5 %collective-permute-start.22 = (bf16[768,256]{1,0:T(8,128)(2,1)S(1)}, bf16[768,256]{1,0:T(8,128)(2,1)S(1)}, u32[]{:S(2)}, u32[]{:S(2)}) collective-permute-start(bf16[768,256]{1,0:T(8,128)(2,1)S(1)} %collective-permute-done.20), channel_id=1, source_target_pairs={{0,2},{1,31},{2,4},{3,1},{4,6},{5,3},{6,8},{7,5},{8,10},{9,7},{10,... | collective-permute-start | bytes 1179656 | tf_op jit(solution)/shard_map/ppermute | solution.py:74
  125.4 4.2 %collective-permute-start.25 = (bf16[768,256]{1,0:T(8,128)(2,1)S(1)}, bf16[768,256]{1,0:T(8,128)(2,1)S(1)}, u32[]{:S(2)}, u32[]{:S(2)}) collective-permute-start(bf16[768,256]{1,0:T(8,128)(2,1)S(1)} %collective-permute-done.23), channel_id=1, source_target_pairs={{0,2},{1,31},{2,4},{3,1},{4,6},{5,3},{6,8},{7,5},{8,10},{9,7},{10,... | collective-permute-start | bytes 1179656 | tf_op jit(solution)/shard_map/ppermute | solution.py:74
  129.6 2.0 %attend.11.refs_2_ = f32[13,128,256]{2,1,0:T(8,128)S(1)} custom-call(s32[6]{0:T(128)S(1)} %stack.27.place, s32[7,384]{1,0:T(8,128)S(1)} %get-tuple-element.51.pairs, s32[1,7]{1,0:T(1,128)S(1)} %get-tuple-element.52.counts, bf16[12,128,128]{2,1,0:T(8,128)(2,1)S(1)} %bitcast.45, bf16[6,128,256]{2,1,0:T(8,128)(2,1)S(1)} %bitcast.58, ...), custom_call_target="tpu_custom_call", output_to_operand_aliasing={{}: (6, {})} | custom-call | flops 2000000000 | bytes 2000000 | tf_op jit(solution)/shard_map/attend/pallas_call | solution.py:193
  131.6 3.5 %collective-permute-start.24 = (bf16[768,256]{1,0:T(8,128)(2,1)S(1)}, bf16[768,256]{1,0:T(8,128)(2,1)S(1)}, u32[]{:S(2)}, u32[]{:S(2)}) collective-permute-start(bf16[768,256]{1,0:T(8,128)(2,1)S(1)} %collective-permute-done.22), channel_id=1, source_target_pairs={{1,31},{3,1},{5,3},{7,5},{9,7},{11,9},{13,11},{15,13},{17,15},{19,... | collective-permute-start | bytes 1179656 | tf_op jit(solution)/shard_map/ppermute | solution.py:74
  135.1 4.2 %collective-permute-start.26 = (bf16[768,256]{1,0:T(8,128)(2,1)S(1)}, bf16[768,256]{1,0:T(8,128)(2,1)S(1)}, u32[]{:S(2)}, u32[]{:S(2)}) collective-permute-start(bf16[768,256]{1,0:T(8,128)(2,1)S(1)} %collective-permute-done.25), channel_id=1, source_target_pairs={{1,31},{3,1},{5,3},{7,5},{9,7},{11,9},{13,11},{15,13},{17,15},{19,... | collective-permute-start | bytes 1179656 | tf_op jit(solution)/shard_map/ppermute | solution.py:74
  139.3 2.5 %attend.12.refs_2_ = f32[13,128,256]{2,1,0:T(8,128)S(1)} custom-call(s32[6]{0:T(128)S(1)} %stack.27.place, s32[7,384]{1,0:T(8,128)S(1)} %get-tuple-element.51.pairs, s32[1,7]{1,0:T(1,128)S(1)} %get-tuple-element.52.counts, bf16[12,128,128]{2,1,0:T(8,128)(2,1)S(1)} %bitcast.46, bf16[6,128,256]{2,1,0:T(8,128)(2,1)S(1)} %bitcast.60, ...), custom_call_target="tpu_custom_call", output_to_operand_aliasing={{}: (6, {})} | custom-call | flops 2000000000 | bytes 2000000 | tf_op jit(solution)/shard_map/attend/pallas_call | solution.py:193
  141.8 2.5 %collective-permute-done.26 = bf16[768,256]{1,0:T(8,128)(2,1)S(1)} collective-permute-done((bf16[768,256]{1,0:T(8,128)(2,1)S(1)}, bf16[768,256]{1,0:T(8,128)(2,1)S(1)}, u32[]{:S(2)}, u32[]{:S(2)}) %collective-permute-start.26) | collective-permute-done | bytes 393248 | tf_op jit(solution)/shard_map/ppermute | solution.py:74
  144.3 2.0 %attend.13 = (f32[6,128,256]{2,1,0:T(8,128)S(1)}, f32[6,128,256]{2,1,0:T(8,128)S(1)}) custom-call(s32[6]{0:T(128)S(1)} %stack.27.place, s32[7,384]{1,0:T(8,128)S(1)} %get-tuple-element.51.pairs, s32[1,7]{1,0:T(1,128)S(1)} %get-tuple-element.52.counts, bf16[12,128,128]{2,1,0:T(8,128)(2,1)S(1)} %bitcast.47, bf16[6,128,256]{2,1,0:T(8,128)(2,1)S(1)} %bitcast.61, ...), custom_call_target="tpu_custom_call" | custom-call | flops 2000000000 | bytes 2000000 | tf_op jit(solution)/shard_map/attend/pallas_call | solution.py:193
  146.3 3.4 %collective-permute-start.27 = (f32[6,128,256]{2,1,0:T(8,128)S(1)}, f32[6,128,256]{2,1,0:T(8,128)S(1)}, u32[]{:S(2)}, u32[]{:S(2)}) collective-permute-start(f32[6,128,256]{2,1,0:T(8,128)S(1)} %get-tuple-element.72), channel_id=1, source_target_pairs={{0,1},{1,0},{2,3},{3,2},{4,5},{5,4},{6,7},{7,6},{8,9},{9,8},{10,11... | collective-permute-start | bytes 2359304 | tf_op jit(solution)/shard_map/ppermute | solution.py:64
  149.7 1.9 %collective-permute-done.27 = f32[6,128,256]{2,1,0:T(8,128)S(1)} collective-permute-done((f32[6,128,256]{2,1,0:T(8,128)S(1)}, f32[6,128,256]{2,1,0:T(8,128)S(1)}, u32[]{:S(2)}, u32[]{:S(2)}) %collective-permute-start.27) | collective-permute-done | bytes 786464 | tf_op jit(solution)/shard_map/ppermute | solution.py:64
  151.6 0.1 add.19
  151.7 0.1 fusion
  151.8 11.9 %all_to_all.19 = bf16[16,48,128]{2,1,0:T(8,128)(2,1)S(1)} all-to-all(bf16[16,48,128]{2,1,0:T(8,128)(2,1)S(1)} %bitcast.64), channel_id=1, replica_groups=mesh['seq'=16,'bal'=32] {'seq'}, dimensions={0} | all-to-all | bytes 393216 | tf_op jit(solution)/shard_map/all_to_all | solution.py:360
  163.7 0.7 copy_bitcast_fusion
  (23 shorter events, 0.1 us)
Async XLA Ops:
  0.0 71.5 %copy-start = (s32[1,192,64]{1,2,0:T(8,128)S(1)}, s32[1,192,64]{1,2,0:T(8,128)}, u32[]{:S(2)}) copy-start(s32[1,192,64]{1,2,0:T(8,128)} %param.10) | copy-start | bytes 147460
  0.0 36.2 %copy-start.1 = (bf16[3072,1,3,128]{3,0,2,1:T(8,128)(2,1)S(1)}, bf16[3072,1,3,128]{3,0,2,1:T(8,128)(2,1)}, u32[]{:S(2)}) copy-start(bf16[3072,1,3,128]{3,0,2,1:T(8,128)(2,1)} %param.7) | copy-start | bytes 7077892
  0.0 12.4 %collective-permute-start = (bf16[48,3072]{1,0:T(8,128)(2,1)}, bf16[48,3072]{1,0:T(8,128)(2,1)S(1)}, u32[]{:S(2)}, u32[]{:S(2)}) collective-permute-start(bf16[48,3072]{1,0:T(8,128)(2,1)} %upper.1), channel_id=1, source_target_pairs={{0,32},{32,64},{64,96},{96,0},{128,160},{160,192},{192,224},{224,1... | collective-permute-start | bytes 884744 | tf_op jit(solution)/shard_map/ppermute | solution.py:34
  4.2 10.1 %collective-permute-start.1 = (bf16[48,3072]{1,0:T(8,128)(2,1)}, bf16[48,3072]{1,0:T(8,128)(2,1)S(1)}, u32[]{:S(2)}, u32[]{:S(2)}) collective-permute-start(bf16[48,3072]{1,0:T(8,128)(2,1)} %upper.1), channel_id=1, source_target_pairs={{0,64},{32,96},{64,0},{96,32},{128,192},{160,224},{192,128},{224,1... | collective-permute-start | bytes 884744 | tf_op jit(solution)/shard_map/ppermute | solution.py:34
  8.7 8.0 %collective-permute-start.2 = (bf16[48,3072]{1,0:T(8,128)(2,1)}, bf16[48,3072]{1,0:T(8,128)(2,1)S(1)}, u32[]{:S(2)}, u32[]{:S(2)}) collective-permute-start(bf16[48,3072]{1,0:T(8,128)(2,1)} %upper.1), channel_id=1, source_target_pairs={{0,96},{32,0},{64,32},{96,64},{128,224},{160,128},{192,160},{224,1... | collective-permute-start | bytes 884744 | tf_op jit(solution)/shard_map/ppermute | solution.py:34
  12.4 1.0 copy-start.2
  17.5 12.8 %collective-permute-start.5 = (bf16[96,3072]{1,0:T(8,128)(2,1)}, bf16[96,3072]{1,0:T(8,128)(2,1)}, u32[]{:S(2)}, u32[]{:S(2)}) collective-permute-start(bf16[96,3072]{1,0:T(8,128)(2,1)} %join.3.refs_1_), channel_id=1, source_target_pairs={{0,384},{32,416},{64,448},{96,480},{128,0},{160,32},{192,64},{224,... | collective-permute-start | bytes 1769480 | tf_op jit(solution)/shard_map/ppermute | solution.py:34
  21.9 12.2 %collective-permute-start.3 = (bf16[96,3072]{1,0:T(8,128)(2,1)S(1)}, bf16[96,3072]{1,0:T(8,128)(2,1)}, u32[]{:S(2)}, u32[]{:S(2)}) collective-permute-start(bf16[96,3072]{1,0:T(8,128)(2,1)S(1)} %join.2.refs_0_), channel_id=1, source_target_pairs={{0,128},{32,160},{64,192},{96,224},{128,256},{160,288},{192,320},{... | collective-permute-start | bytes 1769480 | tf_op jit(solution)/shard_map/ppermute | solution.py:34
  23.9 16.6 %collective-permute-start.8 = (bf16[96,3072]{1,0:T(8,128)(2,1)}, bf16[96,3072]{1,0:T(8,128)(2,1)}, u32[]{:S(2)}, u32[]{:S(2)}) collective-permute-start(bf16[96,3072]{1,0:T(8,128)(2,1)} %join.3.refs_1_), channel_id=1, source_target_pairs={{0,128},{32,160},{64,192},{96,224},{128,256},{160,288},{192,320},{... | collective-permute-start | bytes 1769480 | tf_op jit(solution)/shard_map/ppermute | solution.py:34
  26.0 14.5 %collective-permute-start.7 = (bf16[96,3072]{1,0:T(8,128)(2,1)S(1)}, bf16[96,3072]{1,0:T(8,128)(2,1)}, u32[]{:S(2)}, u32[]{:S(2)}) collective-permute-start(bf16[96,3072]{1,0:T(8,128)(2,1)S(1)} %join.2.refs_0_), channel_id=1, source_target_pairs={{0,384},{32,416},{64,448},{96,480},{128,0},{160,32},{192,64},{224,... | collective-permute-start | bytes 1769480 | tf_op jit(solution)/shard_map/ppermute | solution.py:34
  30.4 13.2 %collective-permute-start.6 = (bf16[96,3072]{1,0:T(8,128)(2,1)}, bf16[96,3072]{1,0:T(8,128)(2,1)}, u32[]{:S(2)}, u32[]{:S(2)}) collective-permute-start(bf16[96,3072]{1,0:T(8,128)(2,1)} %collective-permute-done.5.refs_3_), channel_id=1, source_target_pairs={{0,384},{32,416},{64,448},{96,480},{128,0},{160,32},{192,64},{224,... | collective-permute-start | bytes 1769480 | tf_op jit(solution)/shard_map/ppermute | solution.py:34
  34.2 12.6 %collective-permute-start.4 = (bf16[96,3072]{1,0:T(8,128)(2,1)}, bf16[96,3072]{1,0:T(8,128)(2,1)}, u32[]{:S(2)}, u32[]{:S(2)}) collective-permute-start(bf16[96,3072]{1,0:T(8,128)(2,1)} %collective-permute-done.3.refs_2_), channel_id=1, source_target_pairs={{0,128},{32,160},{64,192},{96,224},{128,256},{160,288},{192,320},{... | collective-permute-start | bytes 1769480 | tf_op jit(solution)/shard_map/ppermute | solution.py:34
  46.8 24.6 %copy-start.3 = (s32[1,192]{1,0:T(1,128)S(1)}, s32[1,192]{1,0:T(1,128)}, u32[]{:S(2)}) copy-start(s32[1,192]{1,0:T(1,128)} %param.11) | copy-start | bytes 2308
  49.7 17.1 %collective-permute-start.10 = (bf16[768,256]{1,0:T(8,128)(2,1)}, bf16[768,256]{1,0:T(8,128)(2,1)S(1)}, u32[]{:S(2)}, u32[]{:S(2)}) collective-permute-start(bf16[768,256]{1,0:T(8,128)(2,1)} %get-tuple-element.47), channel_id=1, source_target_pairs={{0,1},{1,0},{2,3},{3,2},{4,5},{5,4},{6,7},{7,6},{8,9},{9,8},{10,11... | collective-permute-start | bytes 1179656 | tf_op jit(solution)/shard_map/ppermute | solution.py:64
  57.3 16.8 %collective-permute-start.9 = (bf16[768,256]{1,0:T(8,128)(2,1)}, bf16[768,256]{1,0:T(8,128)(2,1)S(1)}, u32[]{:S(2)}, u32[]{:S(2)}) collective-permute-start(bf16[768,256]{1,0:T(8,128)(2,1)} %get-tuple-element.47), channel_id=1, source_target_pairs={{0,2},{1,31},{2,4},{3,1},{4,6},{5,3},{6,8},{7,5},{8,10},{9,7},{10,... | collective-permute-start | bytes 1179656 | tf_op jit(solution)/shard_map/ppermute | solution.py:74
  66.8 10.0 %collective-permute-start.11 = (bf16[768,256]{1,0:T(8,128)(2,1)S(1)}, bf16[768,256]{1,0:T(8,128)(2,1)S(1)}, u32[]{:S(2)}, u32[]{:S(2)}) collective-permute-start(bf16[768,256]{1,0:T(8,128)(2,1)S(1)} %collective-permute-done.10), channel_id=1, source_target_pairs={{0,2},{1,31},{2,4},{3,1},{4,6},{5,3},{6,8},{7,5},{8,10},{9,7},{10,... | collective-permute-start | bytes 1179656 | tf_op jit(solution)/shard_map/ppermute | solution.py:74
  69.5 4.7 %collective-permute-start.13 = (bf16[768,128]{1,0:T(8,128)(2,1)S(1)}, bf16[768,128]{1,0:T(8,128)(2,1)S(1)}, u32[]{:S(2)}, u32[]{:S(2)}) collective-permute-start(bf16[768,128]{1,0:T(8,128)(2,1)S(1)} %get-tuple-element.53), channel_id=1, source_target_pairs={{0,1},{1,0},{2,3},{3,2},{4,5},{5,4},{6,7},{7,6},{8,9},{9,8},{10,11... | collective-permute-start | bytes 589832 | tf_op jit(solution)/shard_map/ppermute | solution.py:64
  74.2 8.8 %collective-permute-start.14 = (bf16[768,256]{1,0:T(8,128)(2,1)S(1)}, bf16[768,256]{1,0:T(8,128)(2,1)S(1)}, u32[]{:S(2)}, u32[]{:S(2)}) collective-permute-start(bf16[768,256]{1,0:T(8,128)(2,1)S(1)} %collective-permute-done.9), channel_id=1, source_target_pairs={{0,2},{1,31},{2,4},{3,1},{4,6},{5,3},{6,8},{7,5},{8,10},{9,7},{10,... | collective-permute-start | bytes 1179656 | tf_op jit(solution)/shard_map/ppermute | solution.py:74
  76.8 10.4 %collective-permute-start.12 = (bf16[768,256]{1,0:T(8,128)(2,1)S(1)}, bf16[768,256]{1,0:T(8,128)(2,1)S(1)}, u32[]{:S(2)}, u32[]{:S(2)}) collective-permute-start(bf16[768,256]{1,0:T(8,128)(2,1)S(1)} %collective-permute-done.11), channel_id=1, source_target_pairs={{0,2},{1,31},{2,4},{3,1},{4,6},{5,3},{6,8},{7,5},{8,10},{9,7},{10,... | collective-permute-start | bytes 1179656 | tf_op jit(solution)/shard_map/ppermute | solution.py:74
  83.0 10.5 %collective-permute-start.15 = (bf16[768,256]{1,0:T(8,128)(2,1)S(1)}, bf16[768,256]{1,0:T(8,128)(2,1)S(1)}, u32[]{:S(2)}, u32[]{:S(2)}) collective-permute-start(bf16[768,256]{1,0:T(8,128)(2,1)S(1)} %collective-permute-done.14), channel_id=1, source_target_pairs={{0,2},{1,31},{2,4},{3,1},{4,6},{5,3},{6,8},{7,5},{8,10},{9,7},{10,... | collective-permute-start | bytes 1179656 | tf_op jit(solution)/shard_map/ppermute | solution.py:74
  87.2 9.1 %collective-permute-start.17 = (bf16[768,256]{1,0:T(8,128)(2,1)S(1)}, bf16[768,256]{1,0:T(8,128)(2,1)S(1)}, u32[]{:S(2)}, u32[]{:S(2)}) collective-permute-start(bf16[768,256]{1,0:T(8,128)(2,1)S(1)} %collective-permute-done.12), channel_id=1, source_target_pairs={{0,2},{1,31},{2,4},{3,1},{4,6},{5,3},{6,8},{7,5},{8,10},{9,7},{10,... | collective-permute-start | bytes 1179656 | tf_op jit(solution)/shard_map/ppermute | solution.py:74
  93.5 9.0 %collective-permute-start.16 = (bf16[768,256]{1,0:T(8,128)(2,1)S(1)}, bf16[768,256]{1,0:T(8,128)(2,1)S(1)}, u32[]{:S(2)}, u32[]{:S(2)}) collective-permute-start(bf16[768,256]{1,0:T(8,128)(2,1)S(1)} %collective-permute-done.15), channel_id=1, source_target_pairs={{0,2},{1,31},{2,4},{3,1},{4,6},{5,3},{6,8},{7,5},{8,10},{9,7},{10,... | collective-permute-start | bytes 1179656 | tf_op jit(solution)/shard_map/ppermute | solution.py:74
  96.3 10.2 %collective-permute-start.19 = (bf16[768,256]{1,0:T(8,128)(2,1)S(1)}, bf16[768,256]{1,0:T(8,128)(2,1)S(1)}, u32[]{:S(2)}, u32[]{:S(2)}) collective-permute-start(bf16[768,256]{1,0:T(8,128)(2,1)S(1)} %collective-permute-done.17), channel_id=1, source_target_pairs={{0,2},{1,31},{2,4},{3,1},{4,6},{5,3},{6,8},{7,5},{8,10},{9,7},{10,... | collective-permute-start | bytes 1179656 | tf_op jit(solution)/shard_map/ppermute | solution.py:74
  102.5 9.2 %collective-permute-start.18 = (bf16[768,256]{1,0:T(8,128)(2,1)S(1)}, bf16[768,256]{1,0:T(8,128)(2,1)S(1)}, u32[]{:S(2)}, u32[]{:S(2)}) collective-permute-start(bf16[768,256]{1,0:T(8,128)(2,1)S(1)} %collective-permute-done.16), channel_id=1, source_target_pairs={{0,2},{1,31},{2,4},{3,1},{4,6},{5,3},{6,8},{7,5},{8,10},{9,7},{10,... | collective-permute-start | bytes 1179656 | tf_op jit(solution)/shard_map/ppermute | solution.py:74
  106.5 9.2 %collective-permute-start.21 = (bf16[768,256]{1,0:T(8,128)(2,1)S(1)}, bf16[768,256]{1,0:T(8,128)(2,1)S(1)}, u32[]{:S(2)}, u32[]{:S(2)}) collective-permute-start(bf16[768,256]{1,0:T(8,128)(2,1)S(1)} %collective-permute-done.19), channel_id=1, source_target_pairs={{0,2},{1,31},{2,4},{3,1},{4,6},{5,3},{6,8},{7,5},{8,10},{9,7},{10,... | collective-permute-start | bytes 1179656 | tf_op jit(solution)/shard_map/ppermute | solution.py:74
  111.7 10.2 %collective-permute-start.20 = (bf16[768,256]{1,0:T(8,128)(2,1)S(1)}, bf16[768,256]{1,0:T(8,128)(2,1)S(1)}, u32[]{:S(2)}, u32[]{:S(2)}) collective-permute-start(bf16[768,256]{1,0:T(8,128)(2,1)S(1)} %collective-permute-done.18), channel_id=1, source_target_pairs={{0,2},{1,31},{2,4},{3,1},{4,6},{5,3},{6,8},{7,5},{8,10},{9,7},{10,... | collective-permute-start | bytes 1179656 | tf_op jit(solution)/shard_map/ppermute | solution.py:74
  115.7 9.7 %collective-permute-start.23 = (bf16[768,256]{1,0:T(8,128)(2,1)S(1)}, bf16[768,256]{1,0:T(8,128)(2,1)S(1)}, u32[]{:S(2)}, u32[]{:S(2)}) collective-permute-start(bf16[768,256]{1,0:T(8,128)(2,1)S(1)} %collective-permute-done.21), channel_id=1, source_target_pairs={{0,2},{1,31},{2,4},{3,1},{4,6},{5,3},{6,8},{7,5},{8,10},{9,7},{10,... | collective-permute-start | bytes 1179656 | tf_op jit(solution)/shard_map/ppermute | solution.py:74
  121.9 9.7 %collective-permute-start.22 = (bf16[768,256]{1,0:T(8,128)(2,1)S(1)}, bf16[768,256]{1,0:T(8,128)(2,1)S(1)}, u32[]{:S(2)}, u32[]{:S(2)}) collective-permute-start(bf16[768,256]{1,0:T(8,128)(2,1)S(1)} %collective-permute-done.20), channel_id=1, source_target_pairs={{0,2},{1,31},{2,4},{3,1},{4,6},{5,3},{6,8},{7,5},{8,10},{9,7},{10,... | collective-permute-start | bytes 1179656 | tf_op jit(solution)/shard_map/ppermute | solution.py:74
  125.4 9.7 %collective-permute-start.25 = (bf16[768,256]{1,0:T(8,128)(2,1)S(1)}, bf16[768,256]{1,0:T(8,128)(2,1)S(1)}, u32[]{:S(2)}, u32[]{:S(2)}) collective-permute-start(bf16[768,256]{1,0:T(8,128)(2,1)S(1)} %collective-permute-done.23), channel_id=1, source_target_pairs={{0,2},{1,31},{2,4},{3,1},{4,6},{5,3},{6,8},{7,5},{8,10},{9,7},{10,... | collective-permute-start | bytes 1179656 | tf_op jit(solution)/shard_map/ppermute | solution.py:74
  131.6 10.2 %collective-permute-start.24 = (bf16[768,256]{1,0:T(8,128)(2,1)S(1)}, bf16[768,256]{1,0:T(8,128)(2,1)S(1)}, u32[]{:S(2)}, u32[]{:S(2)}) collective-permute-start(bf16[768,256]{1,0:T(8,128)(2,1)S(1)} %collective-permute-done.22), channel_id=1, source_target_pairs={{1,31},{3,1},{5,3},{7,5},{9,7},{11,9},{13,11},{15,13},{17,15},{19,... | collective-permute-start | bytes 1179656 | tf_op jit(solution)/shard_map/ppermute | solution.py:74
  135.1 9.2 %collective-permute-start.26 = (bf16[768,256]{1,0:T(8,128)(2,1)S(1)}, bf16[768,256]{1,0:T(8,128)(2,1)S(1)}, u32[]{:S(2)}, u32[]{:S(2)}) collective-permute-start(bf16[768,256]{1,0:T(8,128)(2,1)S(1)} %collective-permute-done.25), channel_id=1, source_target_pairs={{1,31},{3,1},{5,3},{7,5},{9,7},{11,9},{13,11},{15,13},{17,15},{19,... | collective-permute-start | bytes 1179656 | tf_op jit(solution)/shard_map/ppermute | solution.py:74
  146.3 5.3 %collective-permute-start.27 = (f32[6,128,256]{2,1,0:T(8,128)S(1)}, f32[6,128,256]{2,1,0:T(8,128)S(1)}, u32[]{:S(2)}, u32[]{:S(2)}) collective-permute-start(f32[6,128,256]{2,1,0:T(8,128)S(1)} %get-tuple-element.72), channel_id=1, source_target_pairs={{0,1},{1,0},{2,3},{3,2},{4,5},{5,4},{6,7},{7,6},{8,9},{9,8},{10,11... | collective-permute-start | bytes 2359304 | tf_op jit(solution)/shard_map/ppermute | solution.py:64

commit v12 on v11

--- a/solution.py
+++ b/solution.py
@@ -34,30 +34,31 @@
     return lax.ppermute(block, MESH_AXES, plane_perm(phase, shift))
 
 
-def join_kernel(upper, lower, out, done):
-    rows = upper.shape[0]
-    copies = [
-        pltpu.make_async_copy(upper, out.at[pl.ds(0, rows), :], done.at[0]),
-        pltpu.make_async_copy(lower, out.at[pl.ds(rows, rows), :], done.at[1]),
-    ]
+def join_kernel(starts, *refs):
+    parts = refs[: len(starts)]
+    out, done = refs[-2:]
+    copies = []
+    for at, start in enumerate(starts):
+        here = out.at[pl.ds(start, parts[at].shape[0]), :]
+        copies.append(pltpu.make_async_copy(parts[at], here, done.at[at]))
     for copy in copies:
         copy.start()
     for copy in copies:
         copy.wait()
 
 
-def join(upper, lower):
-    rows, width = upper.shape
+def join(rows, starts, parts, begun=()):
     anywhere = pl.BlockSpec(memory_space=pl.ANY)
     return pl.pallas_call(
-        join_kernel,
-        out_shape=jax.ShapeDtypeStruct((2 * rows, width), upper.dtype),
-        in_specs=[anywhere, anywhere],
+        functools.partial(join_kernel, starts),
+        out_shape=jax.ShapeDtypeStruct((rows, parts[0].shape[1]), parts[0].dtype),
+        in_specs=[anywhere] * (len(parts) + len(begun)),
         out_specs=anywhere,
-        scratch_shapes=[pltpu.SemaphoreType.DMA((2,))],
+        scratch_shapes=[pltpu.SemaphoreType.DMA((len(parts),))],
+        input_output_aliases={len(parts): 0} if begun else {},
         compiler_params=pltpu.CompilerParams(vmem_limit_bytes=1024 * 1024),
         name="join",
-    )(upper, lower)
+    )(*parts, *begun)
 
 
 def swap_cores(block):
@@ -289,21 +290,22 @@
     ).astype(jnp.int32)
     slots = 16 * PIECE // TILE
     before = send(tokens, 1, 1)
+    after = send(tokens, 1, -1)
     across = send(tokens, 1, 2)
-    after = send(tokens, 1, -1)
-    low = join(tokens, before)
     gains = jnp.concatenate((q_gain, k_gain), axis=0)
     weight = jnp.transpose(qkv_weight[:, 0], (1, 0, 2))
-    low, gains, across, after = lax.optimization_barrier((low, gains, across, after))
-    high = join(across, after)
+    own = join(2 * PIECE, (0,), (tokens,))
+    after, own, gains = lax.optimization_barrier((after, own, gains))
+    high = join(2 * PIECE, (0, PIECE), (after, across))
     after_high = send(high, 2, -1)
+    low = join(2 * PIECE, (PIECE,), (before,), (own,))
     before_low = send(low, 2, 1)
     before_high = send(high, 2, 1)
     after_low = send(low, 2, -1)
     across_low = send(before_low, 2, 1)
     across_high = send(after_high, 2, -1)
 
-    low_pieces, high_pieces = (0, 3), (2, 1)
+    low_pieces, high_pieces = (0, 3), (1, 2)
     begun = project(
         ((0, low_pieces), (0, high_pieces), (3, low_pieces), (1, high_pieces)),
         (low, high, before_low, after_high),
@@ -338,13 +340,13 @@
         if sums is not None:
             same[-1], sums = lax.optimization_barrier((same[-1], sums))
         if step == 1:
-            key_tiles, other[0] = lax.optimization_barrier((key_tiles, other[0]))
-            pairs, counts = list_pairs(CALLS, key_tiles[0], key_counts, place, slots)
-            same[1], pairs, counts = lax.optimization_barrier((same[1], pairs, counts))
             queries, other[0] = lax.optimization_barrier((queries, other[0]))
             other_queries = swap_cores(queries)
             same[1], other_queries = lax.optimization_barrier((same[1], other_queries))
         if step == 2:
+            key_tiles, other[1] = lax.optimization_barrier((key_tiles, other[1]))
+            pairs, counts = list_pairs(CALLS, key_tiles[0], key_counts, place, slots)
+            same[2], pairs, counts = lax.optimization_barrier((same[2], pairs, counts))
             low_queries = jnp.where(core == 0, queries, other_queries)
             high_queries = jnp.where(core == 0, other_queries, queries)
             chip_queries = tiles(jnp.concatenate((low_queries, high_queries), axis=0))

time: 165 us -> 164 us (level)
  starting transfers between devices: 107 us -> 102 us
  Pallas kernels: 27.5 us -> 30.8 us
  waiting for transfers between devices: 15 us -> 16.9 us
    ppermute x3, starting transfers between devices: 13 us -> 9.55 us  [swap_cores(): return lax.ppermute(block, 'bal', [(at, at ^ 1) for at in range(32)])]
    pallas_call x7, Pallas kernels: 14.5 us -> 17.9 us  [attend(): pl.pallas_call(functools.partial(attend_kernel, scale, first_call, last_c...]
  transfers between devices with their start and end apart: 28 -> 28, of which waited for: 11 -> 10; matrix products, arithmetic and copies ran while one was open for 1% -> 1% of each run, Pallas kernels for 13% -> 16%
where the time goes in v12:
time: 164 us; the launch traced here: 163 us
  starting transfers between devices  102 us (62%)
  Pallas kernels  30.8 us (19%)
  waiting for transfers between devices  16.9 us (10%)
  blocking collectives  10.5 us (6%)
  local copies, waits for them, and re-layouts  1.91 us (1%)
    ppermute x16, starting transfers between devices, pass_on(): return lax.ppermute(block, 'bal', pairs)  62.9 us
    ppermute x9, starting transfers between devices, send(): return lax.ppermute(block, MESH_AXES, plane_perm(phase, shift))  29.3 us
    pallas_call x7, Pallas kernels, attend(): pl.pallas_call(functools.partial(attend_kernel, scale, first_call, last_c...  17.9 us
    all_to_all x1, blocking collectives, on_device(): lax.all_to_all(result.reshape(slots * TILE, HEAD), 'seq', split_axis=0, c...  10.5 us
    ppermute x3, starting transfers between devices, swap_cores(): return lax.ppermute(block, 'bal', [(at, at ^ 1) for at in range(32)])  9.55 us
    pallas_call x3, Pallas kernels, project(): pl.pallas_call(functools.partial(project_kernel, shares), out_shape=(jax....  9.37 us
    ppermute x9, waiting for transfers between devices, send(): return lax.ppermute(block, MESH_AXES, plane_perm(phase, shift))  8.29 us
    ppermute x16, waiting for transfers between devices, pass_on(): return lax.ppermute(block, 'bal', pairs)  5.34 us
  transfers between devices with their start and end apart: 28, of which 10 were waited for; matrix products, arithmetic and copies ran while one was open for 1% of the time, Pallas kernels for 16%

profile of v12, /device:TPU:1, one launch (start us, length us, event | category | flops | bytes accessed | tf_op | source)
XLA Modules:
  0.0 163.3 jit_solution(9786222673886489800)
XLA Ops:
  0.0 5.6 %collective-permute-start.1 = (bf16[48,3072]{1,0:T(8,128)(2,1)}, bf16[48,3072]{1,0:T(8,128)(2,1)S(1)}, u32[]{:S(2)}, u32[]{:S(2)}) collective-permute-start(bf16[48,3072]{1,0:T(8,128)(2,1)} %refs_0_.1), channel_id=1, source_target_pairs={{0,96},{32,0},{64,32},{96,64},{128,224},{160,128},{192,160},{224,1... | collective-permute-start | bytes 884744 | tf_op jit(solution)/shard_map/ppermute | solution.py:34
  5.6 1.9 %collective-permute-start = (bf16[48,3072]{1,0:T(8,128)(2,1)}, bf16[48,3072]{1,0:T(8,128)(2,1)S(1)}, u32[]{:S(2)}, u32[]{:S(2)}) collective-permute-start(bf16[48,3072]{1,0:T(8,128)(2,1)} %refs_0_.1), channel_id=1, source_target_pairs={{0,32},{32,64},{64,96},{96,0},{128,160},{160,192},{192,224},{224,1... | collective-permute-start | bytes 884744 | tf_op jit(solution)/shard_map/ppermute | solution.py:34
  7.5 3.5 %collective-permute-start.4 = (bf16[48,3072]{1,0:T(8,128)(2,1)}, bf16[48,3072]{1,0:T(8,128)(2,1)S(1)}, u32[]{:S(2)}, u32[]{:S(2)}) collective-permute-start(bf16[48,3072]{1,0:T(8,128)(2,1)} %refs_0_.1), channel_id=1, source_target_pairs={{0,64},{32,96},{64,0},{96,32},{128,192},{160,224},{192,128},{224,1... | collective-permute-start | bytes 884744 | tf_op jit(solution)/shard_map/ppermute | solution.py:34
  11.1 1.0 copy-done.2
  12.1 0.1 join.3.refs_1_
  12.1 0.7 pad_maximum_fusion.1.refs_5_.refs_3_
  12.8 0.0 collective-permute-done.1.refs_0_
  12.8 5.1 %collective-permute-done.refs_0_ = bf16[48,3072]{1,0:T(8,128)(2,1)S(1)} collective-permute-done((bf16[48,3072]{1,0:T(8,128)(2,1)}, bf16[48,3072]{1,0:T(8,128)(2,1)S(1)}, u32[]{:S(2)}, u32[]{:S(2)}) %collective-permute-start) | collective-permute-done | bytes 294944 | tf_op jit(solution)/shard_map/ppermute | solution.py:34
  17.9 0.1 join.4.refs_0_
  18.0 2.8 %collective-permute-start.2 = (bf16[96,3072]{1,0:T(8,128)(2,1)S(1)}, bf16[96,3072]{1,0:T(8,128)(2,1)}, u32[]{:S(2)}, u32[]{:S(2)}) collective-permute-start(bf16[96,3072]{1,0:T(8,128)(2,1)S(1)} %join.4.refs_0_), channel_id=1, source_target_pairs={{0,128},{32,160},{64,192},{96,224},{128,256},{160,288},{192,320},{... | collective-permute-start | bytes 1769480 | tf_op jit(solution)/shard_map/ppermute | solution.py:34
  20.9 0.8 join.5.refs_1_
  21.7 3.7 %collective-permute-start.5 = (bf16[96,3072]{1,0:T(8,128)(2,1)}, bf16[96,3072]{1,0:T(8,128)(2,1)}, u32[]{:S(2)}, u32[]{:S(2)}) collective-permute-start(bf16[96,3072]{1,0:T(8,128)(2,1)} %join.5.refs_1_), channel_id=1, source_target_pairs={{0,384},{32,416},{64,448},{96,480},{128,0},{160,32},{192,64},{224,... | collective-permute-start | bytes 1769480 | tf_op jit(solution)/shard_map/ppermute | solution.py:34
  25.4 2.9 %collective-permute-start.7 = (bf16[96,3072]{1,0:T(8,128)(2,1)S(1)}, bf16[96,3072]{1,0:T(8,128)(2,1)}, u32[]{:S(2)}, u32[]{:S(2)}) collective-permute-start(bf16[96,3072]{1,0:T(8,128)(2,1)S(1)} %join.4.refs_0_), channel_id=1, source_target_pairs={{0,384},{32,416},{64,448},{96,480},{128,0},{160,32},{192,64},{224,... | collective-permute-start | bytes 1769480 | tf_op jit(solution)/shard_map/ppermute | solution.py:34
  28.3 2.4 %collective-permute-start.8 = (bf16[96,3072]{1,0:T(8,128)(2,1)}, bf16[96,3072]{1,0:T(8,128)(2,1)}, u32[]{:S(2)}, u32[]{:S(2)}) collective-permute-start(bf16[96,3072]{1,0:T(8,128)(2,1)} %join.5.refs_1_), channel_id=1, source_target_pairs={{0,128},{32,160},{64,192},{96,224},{128,256},{160,288},{192,320},{... | collective-permute-start | bytes 1769480 | tf_op jit(solution)/shard_map/ppermute | solution.py:34
  30.7 1.9 %collective-permute-start.3 = (bf16[96,3072]{1,0:T(8,128)(2,1)}, bf16[96,3072]{1,0:T(8,128)(2,1)}, u32[]{:S(2)}, u32[]{:S(2)}) collective-permute-start(bf16[96,3072]{1,0:T(8,128)(2,1)} %collective-permute-done.2.refs_2_), channel_id=1, source_target_pairs={{0,128},{32,160},{64,192},{96,224},{128,256},{160,288},{192,320},{... | collective-permute-start | bytes 1769480 | tf_op jit(solution)/shard_map/ppermute | solution.py:34
  32.6 0.3 collective-permute-done.5.refs_3_
  33.0 4.6 %collective-permute-start.6 = (bf16[96,3072]{1,0:T(8,128)(2,1)}, bf16[96,3072]{1,0:T(8,128)(2,1)}, u32[]{:S(2)}, u32[]{:S(2)}) collective-permute-start(bf16[96,3072]{1,0:T(8,128)(2,1)} %collective-permute-done.5.refs_3_), channel_id=1, source_target_pairs={{0,384},{32,416},{64,448},{96,480},{128,0},{160,32},{192,64},{224,... | collective-permute-start | bytes 1769480 | tf_op jit(solution)/shard_map/ppermute | solution.py:34
  37.6 0.1 stack.27.place
  37.7 3.7 %project.3 = (bf16[768,128]{1,0:T(8,128)(2,1)S(1)}, bf16[768,256]{1,0:T(8,128)(2,1)}) custom-call(s32[6]{0:T(128)S(1)} %stack.27.place, bf16[96,3072]{1,0:T(8,128)(2,1)S(1)} %join.4.refs_0_, bf16[96,3072]{1,0:T(8,128)(2,1)} %join.5.refs_1_, bf16[96,3072]{1,0:T(8,128)(2,1)} %collective-permute-done.2.refs_2_, ...), custom_call_target="tpu_custom_call" | custom-call | tf_op jit(solution)/shard_map/project/pallas_call | solution.py:116
  41.4 0.0 collective-permute-done.8.refs_1_
  41.4 2.8 %project.4 = (bf16[768,128]{1,0:T(8,128)(2,1)S(1)}, bf16[768,256]{1,0:T(8,128)(2,1)}) custom-call(s32[6]{0:T(128)S(1)} %stack.27.place, bf16[96,3072]{1,0:T(8,128)(2,1)} %collective-permute-done.7.refs_0_, bf16[96,3072]{1,0:T(8,128)(2,1)} %collective-permute-done.8.refs_1_, ...), custom_call_target="tpu_custom_call", output_to_operand_aliasing={{0}: (5, {}), {1}: (6, {})} | custom-call | tf_op jit(solution)/shard_map/project/pallas_call | solution.py:116
  44.2 2.8 %collective-permute-done.3.refs_0_ = bf16[96,3072]{1,0:T(8,128)(2,1)} collective-permute-done((bf16[96,3072]{1,0:T(8,128)(2,1)}, bf16[96,3072]{1,0:T(8,128)(2,1)}, u32[]{:S(2)}, u32[]{:S(2)}) %collective-permute-start.3) | collective-permute-done | bytes 589856 | tf_op jit(solution)/shard_map/ppermute | solution.py:34
  47.1 2.8 %project.5 = (bf16[768,128]{1,0:T(8,128)(2,1)S(1)}, bf16[768,256]{1,0:T(8,128)(2,1)}) custom-call(s32[6]{0:T(128)S(1)} %stack.27.place, bf16[96,3072]{1,0:T(8,128)(2,1)} %collective-permute-done.3.refs_0_, bf16[96,3072]{1,0:T(8,128)(2,1)} %collective-permute-done.6.refs_1_, ...), custom_call_target="tpu_custom_call", output_to_operand_aliasing={{0}: (5, {}), {1}: (6, {})} | custom-call | tf_op jit(solution)/shard_map/project/pallas_call | solution.py:116
  49.9 5.7 %collective-permute-start.10 = (bf16[768,256]{1,0:T(8,128)(2,1)}, bf16[768,256]{1,0:T(8,128)(2,1)S(1)}, u32[]{:S(2)}, u32[]{:S(2)}) collective-permute-start(bf16[768,256]{1,0:T(8,128)(2,1)} %get-tuple-element.47), channel_id=1, source_target_pairs={{0,1},{1,0},{2,3},{3,2},{4,5},{5,4},{6,7},{7,6},{8,9},{9,8},{10,11... | collective-permute-start | bytes 1179656 | tf_op jit(solution)/shard_map/ppermute | solution.py:65
  55.6 11.1 %collective-permute-start.9 = (bf16[768,256]{1,0:T(8,128)(2,1)}, bf16[768,256]{1,0:T(8,128)(2,1)S(1)}, u32[]{:S(2)}, u32[]{:S(2)}) collective-permute-start(bf16[768,256]{1,0:T(8,128)(2,1)} %get-tuple-element.47), channel_id=1, source_target_pairs={{0,2},{1,31},{2,4},{3,1},{4,6},{5,3},{6,8},{7,5},{8,10},{9,7},{10,... | collective-permute-start | bytes 1179656 | tf_op jit(solution)/shard_map/ppermute | solution.py:75
  66.8 2.6 %collective-permute-start.13 = (bf16[768,256]{1,0:T(8,128)(2,1)S(1)}, bf16[768,256]{1,0:T(8,128)(2,1)S(1)}, u32[]{:S(2)}, u32[]{:S(2)}) collective-permute-start(bf16[768,256]{1,0:T(8,128)(2,1)S(1)} %collective-permute-done.10), channel_id=1, source_target_pairs={{0,2},{1,31},{2,4},{3,1},{4,6},{5,3},{6,8},{7,5},{8,10},{9,7},{10,... | collective-permute-start | bytes 1179656 | tf_op jit(solution)/shard_map/ppermute | solution.py:75
  69.4 1.9 %collective-permute-start.11 = (bf16[768,128]{1,0:T(8,128)(2,1)S(1)}, bf16[768,128]{1,0:T(8,128)(2,1)S(1)}, u32[]{:S(2)}, u32[]{:S(2)}) collective-permute-start(bf16[768,128]{1,0:T(8,128)(2,1)S(1)} %get-tuple-element.49), channel_id=1, source_target_pairs={{0,1},{1,0},{2,3},{3,2},{4,5},{5,4},{6,7},{7,6},{8,9},{9,8},{10,11... | collective-permute-start | bytes 589832 | tf_op jit(solution)/shard_map/ppermute | solution.py:65
  71.4 0.1 constant_dynamic-slice_fusion.counts
  71.4 0.3 collective-permute-done.9
  71.8 1.0 collective-permute-done.11
  72.7 3.9 %collective-permute-start.12 = (bf16[768,256]{1,0:T(8,128)(2,1)S(1)}, bf16[768,256]{1,0:T(8,128)(2,1)S(1)}, u32[]{:S(2)}, u32[]{:S(2)}) collective-permute-start(bf16[768,256]{1,0:T(8,128)(2,1)S(1)} %collective-permute-done.9), channel_id=1, source_target_pairs={{0,2},{1,31},{2,4},{3,1},{4,6},{5,3},{6,8},{7,5},{8,10},{9,7},{10,... | collective-permute-start | bytes 1179656 | tf_op jit(solution)/shard_map/ppermute | solution.py:75
  76.7 0.0 collective-permute-done.13
  76.7 4.2 %collective-permute-start.14 = (bf16[768,256]{1,0:T(8,128)(2,1)S(1)}, bf16[768,256]{1,0:T(8,128)(2,1)S(1)}, u32[]{:S(2)}, u32[]{:S(2)}) collective-permute-start(bf16[768,256]{1,0:T(8,128)(2,1)S(1)} %collective-permute-done.13), channel_id=1, source_target_pairs={{0,2},{1,31},{2,4},{3,1},{4,6},{5,3},{6,8},{7,5},{8,10},{9,7},{10,... | collective-permute-start | bytes 1179656 | tf_op jit(solution)/shard_map/ppermute | solution.py:75
  81.0 0.1 dynamic-slice_bitcast_fusion.tiles
  81.1 2.6 %lists.1 = (s32[7,384]{1,0:T(8,128)S(1)}, s32[1,7]{1,0:T(1,128)S(1)}) custom-call(s32[6]{0:T(128)S(1)} %stack.27.place, s32[64,12]{1,0:T(8,128)S(1)} %dynamic-slice_bitcast_fusion.tiles, s32[1,12]{1,0:T(1,128)S(1)} %constant_dynamic-slice_fusion.counts), custom_call_target="tpu_custom_call" | custom-call | tf_op jit(solution)/shard_map/lists/pallas_call | solution.py:263
  83.7 2.7 %collective-permute-start.15 = (bf16[768,256]{1,0:T(8,128)(2,1)S(1)}, bf16[768,256]{1,0:T(8,128)(2,1)S(1)}, u32[]{:S(2)}, u32[]{:S(2)}) collective-permute-start(bf16[768,256]{1,0:T(8,128)(2,1)S(1)} %collective-permute-done.12), channel_id=1, source_target_pairs={{0,2},{1,31},{2,4},{3,1},{4,6},{5,3},{6,8},{7,5},{8,10},{9,7},{10,... | collective-permute-start | bytes 1179656 | tf_op jit(solution)/shard_map/ppermute | solution.py:75
  86.4 4.2 %collective-permute-start.17 = (bf16[768,256]{1,0:T(8,128)(2,1)S(1)}, bf16[768,256]{1,0:T(8,128)(2,1)S(1)}, u32[]{:S(2)}, u32[]{:S(2)}) collective-permute-start(bf16[768,256]{1,0:T(8,128)(2,1)S(1)} %collective-permute-done.14), channel_id=1, source_target_pairs={{0,2},{1,31},{2,4},{3,1},{4,6},{5,3},{6,8},{7,5},{8,10},{9,7},{10,... | collective-permute-start | bytes 1179656 | tf_op jit(solution)/shard_map/ppermute | solution.py:75
  90.6 4.1 %attend.7.refs_2_ = f32[13,128,256]{2,1,0:T(8,128)S(1)} custom-call(s32[6]{0:T(128)S(1)} %stack.27.place, s32[7,384]{1,0:T(8,128)S(1)} %get-tuple-element.54.pairs, s32[1,7]{1,0:T(1,128)S(1)} %get-tuple-element.55.counts, bf16[12,128,128]{2,1,0:T(8,128)(2,1)S(1)} %bitcast.41, bf16[6,128,256]{2,1,0:T(8,128)(2,1)} %bitcast.12.refs_0_, ...), custom_call_target="tpu_custom_call" | custom-call | flops 5000000000 | bytes 5000000 | tf_op jit(solution)/shard_map/attend/pallas_call | solution.py:194
  94.8 2.4 %collective-permute-start.16 = (bf16[768,256]{1,0:T(8,128)(2,1)S(1)}, bf16[768,256]{1,0:T(8,128)(2,1)S(1)}, u32[]{:S(2)}, u32[]{:S(2)}) collective-permute-start(bf16[768,256]{1,0:T(8,128)(2,1)S(1)} %collective-permute-done.15), channel_id=1, source_target_pairs={{0,2},{1,31},{2,4},{3,1},{4,6},{5,3},{6,8},{7,5},{8,10},{9,7},{10,... | collective-permute-start | bytes 1179656 | tf_op jit(solution)/shard_map/ppermute | solution.py:75
  97.2 3.1 %collective-permute-start.19 = (bf16[768,256]{1,0:T(8,128)(2,1)S(1)}, bf16[768,256]{1,0:T(8,128)(2,1)S(1)}, u32[]{:S(2)}, u32[]{:S(2)}) collective-permute-start(bf16[768,256]{1,0:T(8,128)(2,1)S(1)} %collective-permute-done.17), channel_id=1, source_target_pairs={{0,2},{1,31},{2,4},{3,1},{4,6},{5,3},{6,8},{7,5},{8,10},{9,7},{10,... | collective-permute-start | bytes 1179656 | tf_op jit(solution)/shard_map/ppermute | solution.py:75
  100.3 2.4 %attend.8.refs_2_ = f32[13,128,256]{2,1,0:T(8,128)S(1)} custom-call(s32[6]{0:T(128)S(1)} %stack.27.place, s32[7,384]{1,0:T(8,128)S(1)} %get-tuple-element.54.pairs, s32[1,7]{1,0:T(1,128)S(1)} %get-tuple-element.55.counts, bf16[12,128,128]{2,1,0:T(8,128)(2,1)S(1)} %bitcast.42, bf16[6,128,256]{2,1,0:T(8,128)(2,1)S(1)} %bitcast.53, ...), custom_call_target="tpu_custom_call", output_to_operand_aliasing={{}: (6, {})} | custom-call | flops 2000000000 | bytes 2000000 | tf_op jit(solution)/shard_map/attend/pallas_call | solution.py:194
  102.8 0.8 collective-permute-done.16
  103.6 3.3 %collective-permute-start.18 = (bf16[768,256]{1,0:T(8,128)(2,1)S(1)}, bf16[768,256]{1,0:T(8,128)(2,1)S(1)}, u32[]{:S(2)}, u32[]{:S(2)}) collective-permute-start(bf16[768,256]{1,0:T(8,128)(2,1)S(1)} %collective-permute-done.16), channel_id=1, source_target_pairs={{0,2},{1,31},{2,4},{3,1},{4,6},{5,3},{6,8},{7,5},{8,10},{9,7},{10,... | collective-permute-start | bytes 1179656 | tf_op jit(solution)/shard_map/ppermute | solution.py:75
  106.9 0.9 collective-permute-done.19
  107.8 3.3 %collective-permute-start.21 = (bf16[768,256]{1,0:T(8,128)(2,1)S(1)}, bf16[768,256]{1,0:T(8,128)(2,1)S(1)}, u32[]{:S(2)}, u32[]{:S(2)}) collective-permute-start(bf16[768,256]{1,0:T(8,128)(2,1)S(1)} %collective-permute-done.19), channel_id=1, source_target_pairs={{0,2},{1,31},{2,4},{3,1},{4,6},{5,3},{6,8},{7,5},{8,10},{9,7},{10,... | collective-permute-start | bytes 1179656 | tf_op jit(solution)/shard_map/ppermute | solution.py:75
  111.1 2.0 %attend.9.refs_2_ = f32[13,128,256]{2,1,0:T(8,128)S(1)} custom-call(s32[6]{0:T(128)S(1)} %stack.27.place, s32[7,384]{1,0:T(8,128)S(1)} %get-tuple-element.54.pairs, s32[1,7]{1,0:T(1,128)S(1)} %get-tuple-element.55.counts, bf16[12,128,128]{2,1,0:T(8,128)(2,1)S(1)} %bitcast.43, bf16[6,128,256]{2,1,0:T(8,128)(2,1)S(1)} %bitcast.54, ...), custom_call_target="tpu_custom_call", output_to_operand_aliasing={{}: (6, {})} | custom-call | flops 2000000000 | bytes 2000000 | tf_op jit(solution)/shard_map/attend/pallas_call | solution.py:194
  113.1 3.5 %collective-permute-start.20 = (bf16[768,256]{1,0:T(8,128)(2,1)S(1)}, bf16[768,256]{1,0:T(8,128)(2,1)S(1)}, u32[]{:S(2)}, u32[]{:S(2)}) collective-permute-start(bf16[768,256]{1,0:T(8,128)(2,1)S(1)} %collective-permute-done.18), channel_id=1, source_target_pairs={{0,2},{1,31},{2,4},{3,1},{4,6},{5,3},{6,8},{7,5},{8,10},{9,7},{10,... | collective-permute-start | bytes 1179656 | tf_op jit(solution)/shard_map/ppermute | solution.py:75
  116.6 4.2 %collective-permute-start.23 = (bf16[768,256]{1,0:T(8,128)(2,1)S(1)}, bf16[768,256]{1,0:T(8,128)(2,1)S(1)}, u32[]{:S(2)}, u32[]{:S(2)}) collective-permute-start(bf16[768,256]{1,0:T(8,128)(2,1)S(1)} %collective-permute-done.21), channel_id=1, source_target_pairs={{0,2},{1,31},{2,4},{3,1},{4,6},{5,3},{6,8},{7,5},{8,10},{9,7},{10,... | collective-permute-start | bytes 1179656 | tf_op jit(solution)/shard_map/ppermute | solution.py:75
  120.8 2.5 %attend.10.refs_2_ = f32[13,128,256]{2,1,0:T(8,128)S(1)} custom-call(s32[6]{0:T(128)S(1)} %stack.27.place, s32[7,384]{1,0:T(8,128)S(1)} %get-tuple-element.54.pairs, s32[1,7]{1,0:T(1,128)S(1)} %get-tuple-element.55.counts, bf16[12,128,128]{2,1,0:T(8,128)(2,1)S(1)} %bitcast.44, bf16[6,128,256]{2,1,0:T(8,128)(2,1)S(1)} %bitcast.56, ...), custom_call_target="tpu_custom_call", output_to_operand_aliasing={{}: (6, {})} | custom-call | flops 2000000000 | bytes 2000000 | tf_op jit(solution)/shard_map/attend/pallas_call | solution.py:194
  123.3 3.0 %collective-permute-start.22 = (bf16[768,256]{1,0:T(8,128)(2,1)S(1)}, bf16[768,256]{1,0:T(8,128)(2,1)S(1)}, u32[]{:S(2)}, u32[]{:S(2)}) collective-permute-start(bf16[768,256]{1,0:T(8,128)(2,1)S(1)} %collective-permute-done.20), channel_id=1, source_target_pairs={{0,2},{1,31},{2,4},{3,1},{4,6},{5,3},{6,8},{7,5},{8,10},{9,7},{10,... | collective-permute-start | bytes 1179656 | tf_op jit(solution)/shard_map/ppermute | solution.py:75
  126.4 4.2 %collective-permute-start.25 = (bf16[768,256]{1,0:T(8,128)(2,1)S(1)}, bf16[768,256]{1,0:T(8,128)(2,1)S(1)}, u32[]{:S(2)}, u32[]{:S(2)}) collective-permute-start(bf16[768,256]{1,0:T(8,128)(2,1)S(1)} %collective-permute-done.23), channel_id=1, source_target_pairs={{0,2},{1,31},{2,4},{3,1},{4,6},{5,3},{6,8},{7,5},{8,10},{9,7},{10,... | collective-permute-start | bytes 1179656 | tf_op jit(solution)/shard_map/ppermute | solution.py:75
  130.6 2.5 %attend.11.refs_2_ = f32[13,128,256]{2,1,0:T(8,128)S(1)} custom-call(s32[6]{0:T(128)S(1)} %stack.27.place, s32[7,384]{1,0:T(8,128)S(1)} %get-tuple-element.54.pairs, s32[1,7]{1,0:T(1,128)S(1)} %get-tuple-element.55.counts, bf16[12,128,128]{2,1,0:T(8,128)(2,1)S(1)} %bitcast.45, bf16[6,128,256]{2,1,0:T(8,128)(2,1)S(1)} %bitcast.58, ...), custom_call_target="tpu_custom_call", output_to_operand_aliasing={{}: (6, {})} | custom-call | flops 2000000000 | bytes 2000000 | tf_op jit(solution)/shard_map/attend/pallas_call | solution.py:194
  133.0 3.0 %collective-permute-start.24 = (bf16[768,256]{1,0:T(8,128)(2,1)S(1)}, bf16[768,256]{1,0:T(8,128)(2,1)S(1)}, u32[]{:S(2)}, u32[]{:S(2)}) collective-permute-start(bf16[768,256]{1,0:T(8,128)(2,1)S(1)} %collective-permute-done.22), channel_id=1, source_target_pairs={{1,31},{3,1},{5,3},{7,5},{9,7},{11,9},{13,11},{15,13},{17,15},{19,... | collective-permute-start | bytes 1179656 | tf_op jit(solution)/shard_map/ppermute | solution.py:75
  136.1 0.3 collective-permute-done.25
  136.4 3.9 %collective-permute-start.26 = (bf16[768,256]{1,0:T(8,128)(2,1)S(1)}, bf16[768,256]{1,0:T(8,128)(2,1)S(1)}, u32[]{:S(2)}, u32[]{:S(2)}) collective-permute-start(bf16[768,256]{1,0:T(8,128)(2,1)S(1)} %collective-permute-done.25), channel_id=1, source_target_pairs={{1,31},{3,1},{5,3},{7,5},{9,7},{11,9},{13,11},{15,13},{17,15},{19,... | collective-permute-start | bytes 1179656 | tf_op jit(solution)/shard_map/ppermute | solution.py:75
  140.3 2.4 %attend.12.refs_2_ = f32[13,128,256]{2,1,0:T(8,128)S(1)} custom-call(s32[6]{0:T(128)S(1)} %stack.27.place, s32[7,384]{1,0:T(8,128)S(1)} %get-tuple-element.54.pairs, s32[1,7]{1,0:T(1,128)S(1)} %get-tuple-element.55.counts, bf16[12,128,128]{2,1,0:T(8,128)(2,1)S(1)} %bitcast.46, bf16[6,128,256]{2,1,0:T(8,128)(2,1)S(1)} %bitcast.60, ...), custom_call_target="tpu_custom_call", output_to_operand_aliasing={{}: (6, {})} | custom-call | flops 2000000000 | bytes 2000000 | tf_op jit(solution)/shard_map/attend/pallas_call | solution.py:194
  142.8 3.0 %collective-permute-done.26 = bf16[768,256]{1,0:T(8,128)(2,1)S(1)} collective-permute-done((bf16[768,256]{1,0:T(8,128)(2,1)S(1)}, bf16[768,256]{1,0:T(8,128)(2,1)S(1)}, u32[]{:S(2)}, u32[]{:S(2)}) %collective-permute-start.26) | collective-permute-done | bytes 393248 | tf_op jit(solution)/shard_map/ppermute | solution.py:75
  145.8 2.0 %attend.13 = (f32[6,128,256]{2,1,0:T(8,128)S(1)}, f32[6,128,256]{2,1,0:T(8,128)S(1)}) custom-call(s32[6]{0:T(128)S(1)} %stack.27.place, s32[7,384]{1,0:T(8,128)S(1)} %get-tuple-element.54.pairs, s32[1,7]{1,0:T(1,128)S(1)} %get-tuple-element.55.counts, bf16[12,128,128]{2,1,0:T(8,128)(2,1)S(1)} %bitcast.47, bf16[6,128,256]{2,1,0:T(8,128)(2,1)S(1)} %bitcast.61, ...), custom_call_target="tpu_custom_call" | custom-call | flops 2000000000 | bytes 2000000 | tf_op jit(solution)/shard_map/attend/pallas_call | solution.py:194
  147.8 1.9 %collective-permute-start.27 = (f32[6,128,256]{2,1,0:T(8,128)S(1)}, f32[6,128,256]{2,1,0:T(8,128)S(1)}, u32[]{:S(2)}, u32[]{:S(2)}) collective-permute-start(f32[6,128,256]{2,1,0:T(8,128)S(1)} %get-tuple-element.74), channel_id=1, source_target_pairs={{0,1},{1,0},{2,3},{3,2},{4,5},{5,4},{6,7},{7,6},{8,9},{9,8},{10,11... | collective-permute-start | bytes 2359304 | tf_op jit(solution)/shard_map/ppermute | solution.py:65
  149.7 2.3 %collective-permute-done.27 = f32[6,128,256]{2,1,0:T(8,128)S(1)} collective-permute-done((f32[6,128,256]{2,1,0:T(8,128)S(1)}, f32[6,128,256]{2,1,0:T(8,128)S(1)}, u32[]{:S(2)}, u32[]{:S(2)}) %collective-permute-start.27) | collective-permute-done | bytes 786464 | tf_op jit(solution)/shard_map/ppermute | solution.py:65
  151.9 0.1 add.19
  152.0 0.1 fusion
  152.1 10.5 %all_to_all.19 = bf16[16,48,128]{2,1,0:T(8,128)(2,1)S(1)} all-to-all(bf16[16,48,128]{2,1,0:T(8,128)(2,1)S(1)} %bitcast.64), channel_id=1, replica_groups=mesh['seq'=16,'bal'=32] {'seq'}, dimensions={0} | all-to-all | bytes 393216 | tf_op jit(solution)/shard_map/all_to_all | solution.py:362
  162.6 0.7 copy_bitcast_fusion
  (24 shorter events, 0.1 us)
Async XLA Ops:
  0.0 81.0 %copy-start = (s32[1,192,64]{1,2,0:T(8,128)S(1)}, s32[1,192,64]{1,2,0:T(8,128)}, u32[]{:S(2)}) copy-start(s32[1,192,64]{1,2,0:T(8,128)} %param.10) | copy-start | bytes 147460
  0.0 37.7 %copy-start.1 = (bf16[3072,1,3,128]{3,0,2,1:T(8,128)(2,1)S(1)}, bf16[3072,1,3,128]{3,0,2,1:T(8,128)(2,1)}, u32[]{:S(2)}) copy-start(bf16[3072,1,3,128]{3,0,2,1:T(8,128)(2,1)} %param.7) | copy-start | bytes 7077892
  0.0 12.8 %collective-permute-start.1 = (bf16[48,3072]{1,0:T(8,128)(2,1)}, bf16[48,3072]{1,0:T(8,128)(2,1)S(1)}, u32[]{:S(2)}, u32[]{:S(2)}) collective-permute-start(bf16[48,3072]{1,0:T(8,128)(2,1)} %refs_0_.1), channel_id=1, source_target_pairs={{0,96},{32,0},{64,32},{96,64},{128,224},{160,128},{192,160},{224,1... | collective-permute-start | bytes 884744 | tf_op jit(solution)/shard_map/ppermute | solution.py:34
  5.6 12.3 %collective-permute-start = (bf16[48,3072]{1,0:T(8,128)(2,1)}, bf16[48,3072]{1,0:T(8,128)(2,1)S(1)}, u32[]{:S(2)}, u32[]{:S(2)}) collective-permute-start(bf16[48,3072]{1,0:T(8,128)(2,1)} %refs_0_.1), channel_id=1, source_target_pairs={{0,32},{32,64},{64,96},{96,0},{128,160},{160,192},{192,224},{224,1... | collective-permute-start | bytes 884744 | tf_op jit(solution)/shard_map/ppermute | solution.py:34
  7.5 13.3 %collective-permute-start.4 = (bf16[48,3072]{1,0:T(8,128)(2,1)}, bf16[48,3072]{1,0:T(8,128)(2,1)S(1)}, u32[]{:S(2)}, u32[]{:S(2)}) collective-permute-start(bf16[48,3072]{1,0:T(8,128)(2,1)} %refs_0_.1), channel_id=1, source_target_pairs={{0,64},{32,96},{64,0},{96,32},{128,192},{160,224},{192,128},{224,1... | collective-permute-start | bytes 884744 | tf_op jit(solution)/shard_map/ppermute | solution.py:34
  11.1 1.0 copy-start.2
  18.0 12.7 %collective-permute-start.2 = (bf16[96,3072]{1,0:T(8,128)(2,1)S(1)}, bf16[96,3072]{1,0:T(8,128)(2,1)}, u32[]{:S(2)}, u32[]{:S(2)}) collective-permute-start(bf16[96,3072]{1,0:T(8,128)(2,1)S(1)} %join.4.refs_0_), channel_id=1, source_target_pairs={{0,128},{32,160},{64,192},{96,224},{128,256},{160,288},{192,320},{... | collective-permute-start | bytes 1769480 | tf_op jit(solution)/shard_map/ppermute | solution.py:34
  21.7 11.2 %collective-permute-start.5 = (bf16[96,3072]{1,0:T(8,128)(2,1)}, bf16[96,3072]{1,0:T(8,128)(2,1)}, u32[]{:S(2)}, u32[]{:S(2)}) collective-permute-start(bf16[96,3072]{1,0:T(8,128)(2,1)} %join.5.refs_1_), channel_id=1, source_target_pairs={{0,384},{32,416},{64,448},{96,480},{128,0},{160,32},{192,64},{224,... | collective-permute-start | bytes 1769480 | tf_op jit(solution)/shard_map/ppermute | solution.py:34
  25.4 16.0 %collective-permute-start.7 = (bf16[96,3072]{1,0:T(8,128)(2,1)S(1)}, bf16[96,3072]{1,0:T(8,128)(2,1)}, u32[]{:S(2)}, u32[]{:S(2)}) collective-permute-start(bf16[96,3072]{1,0:T(8,128)(2,1)S(1)} %join.4.refs_0_), channel_id=1, source_target_pairs={{0,384},{32,416},{64,448},{96,480},{128,0},{160,32},{192,64},{224,... | collective-permute-start | bytes 1769480 | tf_op jit(solution)/shard_map/ppermute | solution.py:34
  28.3 13.1 %collective-permute-start.8 = (bf16[96,3072]{1,0:T(8,128)(2,1)}, bf16[96,3072]{1,0:T(8,128)(2,1)}, u32[]{:S(2)}, u32[]{:S(2)}) collective-permute-start(bf16[96,3072]{1,0:T(8,128)(2,1)} %join.5.refs_1_), channel_id=1, source_target_pairs={{0,128},{32,160},{64,192},{96,224},{128,256},{160,288},{192,320},{... | collective-permute-start | bytes 1769480 | tf_op jit(solution)/shard_map/ppermute | solution.py:34
  30.7 16.3 %collective-permute-start.3 = (bf16[96,3072]{1,0:T(8,128)(2,1)}, bf16[96,3072]{1,0:T(8,128)(2,1)}, u32[]{:S(2)}, u32[]{:S(2)}) collective-permute-start(bf16[96,3072]{1,0:T(8,128)(2,1)} %collective-permute-done.2.refs_2_), channel_id=1, source_target_pairs={{0,128},{32,160},{64,192},{96,224},{128,256},{160,288},{192,320},{... | collective-permute-start | bytes 1769480 | tf_op jit(solution)/shard_map/ppermute | solution.py:34
  33.0 14.1 %collective-permute-start.6 = (bf16[96,3072]{1,0:T(8,128)(2,1)}, bf16[96,3072]{1,0:T(8,128)(2,1)}, u32[]{:S(2)}, u32[]{:S(2)}) collective-permute-start(bf16[96,3072]{1,0:T(8,128)(2,1)} %collective-permute-done.5.refs_3_), channel_id=1, source_target_pairs={{0,384},{32,416},{64,448},{96,480},{128,0},{160,32},{192,64},{224,... | collective-permute-start | bytes 1769480 | tf_op jit(solution)/shard_map/ppermute | solution.py:34
  47.1 24.3 %copy-start.3 = (s32[1,192]{1,0:T(1,128)S(1)}, s32[1,192]{1,0:T(1,128)}, u32[]{:S(2)}) copy-start(s32[1,192]{1,0:T(1,128)} %param.11) | copy-start | bytes 2308
  49.9 16.8 %collective-permute-start.10 = (bf16[768,256]{1,0:T(8,128)(2,1)}, bf16[768,256]{1,0:T(8,128)(2,1)S(1)}, u32[]{:S(2)}, u32[]{:S(2)}) collective-permute-start(bf16[768,256]{1,0:T(8,128)(2,1)} %get-tuple-element.47), channel_id=1, source_target_pairs={{0,1},{1,0},{2,3},{3,2},{4,5},{5,4},{6,7},{7,6},{8,9},{9,8},{10,11... | collective-permute-start | bytes 1179656 | tf_op jit(solution)/shard_map/ppermute | solution.py:65
  55.6 16.1 %collective-permute-start.9 = (bf16[768,256]{1,0:T(8,128)(2,1)}, bf16[768,256]{1,0:T(8,128)(2,1)S(1)}, u32[]{:S(2)}, u32[]{:S(2)}) collective-permute-start(bf16[768,256]{1,0:T(8,128)(2,1)} %get-tuple-element.47), channel_id=1, source_target_pairs={{0,2},{1,31},{2,4},{3,1},{4,6},{5,3},{6,8},{7,5},{8,10},{9,7},{10,... | collective-permute-start | bytes 1179656 | tf_op jit(solution)/shard_map/ppermute | solution.py:75
  66.8 9.9 %collective-permute-start.13 = (bf16[768,256]{1,0:T(8,128)(2,1)S(1)}, bf16[768,256]{1,0:T(8,128)(2,1)S(1)}, u32[]{:S(2)}, u32[]{:S(2)}) collective-permute-start(bf16[768,256]{1,0:T(8,128)(2,1)S(1)} %collective-permute-done.10), channel_id=1, source_target_pairs={{0,2},{1,31},{2,4},{3,1},{4,6},{5,3},{6,8},{7,5},{8,10},{9,7},{10,... | collective-permute-start | bytes 1179656 | tf_op jit(solution)/shard_map/ppermute | solution.py:75
  69.4 3.3 %collective-permute-start.11 = (bf16[768,128]{1,0:T(8,128)(2,1)S(1)}, bf16[768,128]{1,0:T(8,128)(2,1)S(1)}, u32[]{:S(2)}, u32[]{:S(2)}) collective-permute-start(bf16[768,128]{1,0:T(8,128)(2,1)S(1)} %get-tuple-element.49), channel_id=1, source_target_pairs={{0,1},{1,0},{2,3},{3,2},{4,5},{5,4},{6,7},{7,6},{8,9},{9,8},{10,11... | collective-permute-start | bytes 589832 | tf_op jit(solution)/shard_map/ppermute | solution.py:65
  72.7 10.9 %collective-permute-start.12 = (bf16[768,256]{1,0:T(8,128)(2,1)S(1)}, bf16[768,256]{1,0:T(8,128)(2,1)S(1)}, u32[]{:S(2)}, u32[]{:S(2)}) collective-permute-start(bf16[768,256]{1,0:T(8,128)(2,1)S(1)} %collective-permute-done.9), channel_id=1, source_target_pairs={{0,2},{1,31},{2,4},{3,1},{4,6},{5,3},{6,8},{7,5},{8,10},{9,7},{10,... | collective-permute-start | bytes 1179656 | tf_op jit(solution)/shard_map/ppermute | solution.py:75
  76.7 9.7 %collective-permute-start.14 = (bf16[768,256]{1,0:T(8,128)(2,1)S(1)}, bf16[768,256]{1,0:T(8,128)(2,1)S(1)}, u32[]{:S(2)}, u32[]{:S(2)}) collective-permute-start(bf16[768,256]{1,0:T(8,128)(2,1)S(1)} %collective-permute-done.13), channel_id=1, source_target_pairs={{0,2},{1,31},{2,4},{3,1},{4,6},{5,3},{6,8},{7,5},{8,10},{9,7},{10,... | collective-permute-start | bytes 1179656 | tf_op jit(solution)/shard_map/ppermute | solution.py:75
  83.7 11.1 %collective-permute-start.15 = (bf16[768,256]{1,0:T(8,128)(2,1)S(1)}, bf16[768,256]{1,0:T(8,128)(2,1)S(1)}, u32[]{:S(2)}, u32[]{:S(2)}) collective-permute-start(bf16[768,256]{1,0:T(8,128)(2,1)S(1)} %collective-permute-done.12), channel_id=1, source_target_pairs={{0,2},{1,31},{2,4},{3,1},{4,6},{5,3},{6,8},{7,5},{8,10},{9,7},{10,... | collective-permute-start | bytes 1179656 | tf_op jit(solution)/shard_map/ppermute | solution.py:75
  86.4 10.8 %collective-permute-start.17 = (bf16[768,256]{1,0:T(8,128)(2,1)S(1)}, bf16[768,256]{1,0:T(8,128)(2,1)S(1)}, u32[]{:S(2)}, u32[]{:S(2)}) collective-permute-start(bf16[768,256]{1,0:T(8,128)(2,1)S(1)} %collective-permute-done.14), channel_id=1, source_target_pairs={{0,2},{1,31},{2,4},{3,1},{4,6},{5,3},{6,8},{7,5},{8,10},{9,7},{10,... | collective-permute-start | bytes 1179656 | tf_op jit(solution)/shard_map/ppermute | solution.py:75
  94.8 8.8 %collective-permute-start.16 = (bf16[768,256]{1,0:T(8,128)(2,1)S(1)}, bf16[768,256]{1,0:T(8,128)(2,1)S(1)}, u32[]{:S(2)}, u32[]{:S(2)}) collective-permute-start(bf16[768,256]{1,0:T(8,128)(2,1)S(1)} %collective-permute-done.15), channel_id=1, source_target_pairs={{0,2},{1,31},{2,4},{3,1},{4,6},{5,3},{6,8},{7,5},{8,10},{9,7},{10,... | collective-permute-start | bytes 1179656 | tf_op jit(solution)/shard_map/ppermute | solution.py:75
  97.2 10.6 %collective-permute-start.19 = (bf16[768,256]{1,0:T(8,128)(2,1)S(1)}, bf16[768,256]{1,0:T(8,128)(2,1)S(1)}, u32[]{:S(2)}, u32[]{:S(2)}) collective-permute-start(bf16[768,256]{1,0:T(8,128)(2,1)S(1)} %collective-permute-done.17), channel_id=1, source_target_pairs={{0,2},{1,31},{2,4},{3,1},{4,6},{5,3},{6,8},{7,5},{8,10},{9,7},{10,... | collective-permute-start | bytes 1179656 | tf_op jit(solution)/shard_map/ppermute | solution.py:75
  103.6 9.5 %collective-permute-start.18 = (bf16[768,256]{1,0:T(8,128)(2,1)S(1)}, bf16[768,256]{1,0:T(8,128)(2,1)S(1)}, u32[]{:S(2)}, u32[]{:S(2)}) collective-permute-start(bf16[768,256]{1,0:T(8,128)(2,1)S(1)} %collective-permute-done.16), channel_id=1, source_target_pairs={{0,2},{1,31},{2,4},{3,1},{4,6},{5,3},{6,8},{7,5},{8,10},{9,7},{10,... | collective-permute-start | bytes 1179656 | tf_op jit(solution)/shard_map/ppermute | solution.py:75
  107.8 8.8 %collective-permute-start.21 = (bf16[768,256]{1,0:T(8,128)(2,1)S(1)}, bf16[768,256]{1,0:T(8,128)(2,1)S(1)}, u32[]{:S(2)}, u32[]{:S(2)}) collective-permute-start(bf16[768,256]{1,0:T(8,128)(2,1)S(1)} %collective-permute-done.19), channel_id=1, source_target_pairs={{0,2},{1,31},{2,4},{3,1},{4,6},{5,3},{6,8},{7,5},{8,10},{9,7},{10,... | collective-permute-start | bytes 1179656 | tf_op jit(solution)/shard_map/ppermute | solution.py:75
  113.1 10.2 %collective-permute-start.20 = (bf16[768,256]{1,0:T(8,128)(2,1)S(1)}, bf16[768,256]{1,0:T(8,128)(2,1)S(1)}, u32[]{:S(2)}, u32[]{:S(2)}) collective-permute-start(bf16[768,256]{1,0:T(8,128)(2,1)S(1)} %collective-permute-done.18), channel_id=1, source_target_pairs={{0,2},{1,31},{2,4},{3,1},{4,6},{5,3},{6,8},{7,5},{8,10},{9,7},{10,... | collective-permute-start | bytes 1179656 | tf_op jit(solution)/shard_map/ppermute | solution.py:75
  116.6 9.7 %collective-permute-start.23 = (bf16[768,256]{1,0:T(8,128)(2,1)S(1)}, bf16[768,256]{1,0:T(8,128)(2,1)S(1)}, u32[]{:S(2)}, u32[]{:S(2)}) collective-permute-start(bf16[768,256]{1,0:T(8,128)(2,1)S(1)} %collective-permute-done.21), channel_id=1, source_target_pairs={{0,2},{1,31},{2,4},{3,1},{4,6},{5,3},{6,8},{7,5},{8,10},{9,7},{10,... | collective-permute-start | bytes 1179656 | tf_op jit(solution)/shard_map/ppermute | solution.py:75
  123.3 9.7 %collective-permute-start.22 = (bf16[768,256]{1,0:T(8,128)(2,1)S(1)}, bf16[768,256]{1,0:T(8,128)(2,1)S(1)}, u32[]{:S(2)}, u32[]{:S(2)}) collective-permute-start(bf16[768,256]{1,0:T(8,128)(2,1)S(1)} %collective-permute-done.20), channel_id=1, source_target_pairs={{0,2},{1,31},{2,4},{3,1},{4,6},{5,3},{6,8},{7,5},{8,10},{9,7},{10,... | collective-permute-start | bytes 1179656 | tf_op jit(solution)/shard_map/ppermute | solution.py:75
  126.4 10.0 %collective-permute-start.25 = (bf16[768,256]{1,0:T(8,128)(2,1)S(1)}, bf16[768,256]{1,0:T(8,128)(2,1)S(1)}, u32[]{:S(2)}, u32[]{:S(2)}) collective-permute-start(bf16[768,256]{1,0:T(8,128)(2,1)S(1)} %collective-permute-done.23), channel_id=1, source_target_pairs={{0,2},{1,31},{2,4},{3,1},{4,6},{5,3},{6,8},{7,5},{8,10},{9,7},{10,... | collective-permute-start | bytes 1179656 | tf_op jit(solution)/shard_map/ppermute | solution.py:75
  133.0 9.7 %collective-permute-start.24 = (bf16[768,256]{1,0:T(8,128)(2,1)S(1)}, bf16[768,256]{1,0:T(8,128)(2,1)S(1)}, u32[]{:S(2)}, u32[]{:S(2)}) collective-permute-start(bf16[768,256]{1,0:T(8,128)(2,1)S(1)} %collective-permute-done.22), channel_id=1, source_target_pairs={{1,31},{3,1},{5,3},{7,5},{9,7},{11,9},{13,11},{15,13},{17,15},{19,... | collective-permute-start | bytes 1179656 | tf_op jit(solution)/shard_map/ppermute | solution.py:75
  136.4 9.4 %collective-permute-start.26 = (bf16[768,256]{1,0:T(8,128)(2,1)S(1)}, bf16[768,256]{1,0:T(8,128)(2,1)S(1)}, u32[]{:S(2)}, u32[]{:S(2)}) collective-permute-start(bf16[768,256]{1,0:T(8,128)(2,1)S(1)} %collective-permute-done.25), channel_id=1, source_target_pairs={{1,31},{3,1},{5,3},{7,5},{9,7},{11,9},{13,11},{15,13},{17,15},{19,... | collective-permute-start | bytes 1179656 | tf_op jit(solution)/shard_map/ppermute | solution.py:75
  147.8 4.2 %collective-permute-start.27 = (f32[6,128,256]{2,1,0:T(8,128)S(1)}, f32[6,128,256]{2,1,0:T(8,128)S(1)}, u32[]{:S(2)}, u32[]{:S(2)}) collective-permute-start(f32[6,128,256]{2,1,0:T(8,128)S(1)} %get-tuple-element.74), channel_id=1, source_target_pairs={{0,1},{1,0},{2,3},{3,2},{4,5},{5,4},{6,7},{7,6},{8,9},{9,8},{10,11... | collective-permute-start | bytes 2359304 | tf_op jit(solution)/shard_map/ppermute | solution.py:65

commit v13 on v12

--- a/solution.py
+++ b/solution.py
@@ -135,16 +135,18 @@
 def attend_kernel(scale, first_call, last_call, call, blocks, place, pairs, counts, q, *refs):
     pieces = refs[:blocks]
     kv = refs[-1]
-    slots = pieces[0].shape[0]
     rows = q.shape[0]
+    slots = rows // 2
     if last_call:
         sums_in, kept, given, sums = refs[blocks : blocks + 4]
     elif first_call:
         sums = refs[blocks]
     else:
         sums_in, sums = refs[blocks : blocks + 2]
-    for at in range(blocks):
-        kv[at * slots : (at + 1) * slots] = pieces[at][...]
+    start = 0
+    for piece in pieces:
+        kv[start : start + piece.shape[0]] = piece[...]
+        start += piece.shape[0]
     if first_call:
         sums[...] = jnp.zeros_like(sums)
     else:
@@ -184,10 +186,12 @@
 def attend(call, calls, place, pairs, counts, q, pieces, sums=None):
     scale = HEAD ** (-0.5) * LOG2E
     first_call, last_call = call == 0, call == calls - 1
-    blocks, slots, rows = len(pieces), pieces[0].shape[0], q.shape[0]
+    blocks, rows = len(pieces), q.shape[0]
+    slots = rows // 2
+    held = sum(piece.shape[0] for piece in pieces)
     whole = jax.ShapeDtypeStruct((rows + 1, TILE, 2 * HEAD), jnp.float32)
     half = jax.ShapeDtypeStruct((slots, TILE, 2 * HEAD), jnp.float32)
-    scratch = [pltpu.VMEM((blocks * slots, TILE, 2 * HEAD), jnp.bfloat16)]
+    scratch = [pltpu.VMEM((held, TILE, 2 * HEAD), jnp.bfloat16)]
     if last_call:
         scratch.insert(0, pltpu.VMEM(whole.shape, whole.dtype))
     more = () if first_call else (sums,)
@@ -222,8 +226,14 @@
     entry = lax.broadcasted_iota(jnp.int32, (listed, rows), 0)
     column = lax.broadcasted_iota(jnp.int32, (listed, rows), 1)
     least = jnp.where(same, 0, 1)
-    most = PLANES // 2 - 1 + core
-    inside = (away >= least) & (away <= most) & (entry < counts[...])
+    last, half = PLANES // 2, slots // 2
+    order_in = tile - bal * slots
+    far = away == last
+    low_tile = jnp.where(far, jnp.where(same, 0, half), 0)
+    high_tile = jnp.where(far, jnp.where(same, half + half * core, slots * core), slots)
+    moved = jnp.where(far, jnp.where(same, slots - slots * core, -half), 0)
+    inside = (away >= least) & (away <= last) & (entry < counts[...])
+    inside = inside & (order_in >= low_tile) & (order_in < high_tile)
     down = lax.broadcasted_iota(jnp.int32, (listed, listed), 0)
     along = lax.broadcasted_iota(jnp.int32, (listed, listed), 1)
     before = jnp.where(along < down, 1.0, 0.0)
@@ -243,7 +253,7 @@
         order = jnp.where(held > 0.0, order, -1.0).astype(jnp.int32)
         skip = stop - start - max(start, 1)
         block = jnp.where(same, away - start, away + skip)
-        pair = column * TILE + block * slots + tile - bal * slots - nothing
+        pair = column * TILE + block * slots + order_in + moved - nothing
         room = call_room(start, stop, slots)
         spot = lax.broadcasted_iota(jnp.int32, (listed, room), 1)
         placed = jnp.zeros((1, room), jnp.int32)
@@ -334,9 +344,14 @@
 
     same, other, sums = [keys_values], [swap_cores(keys_values)], None
     for step in range(1, PLANES // 2 + 1):
-        cores = (0, 1) if step < PLANES // 2 else (1,)
-        same.append(pass_on(same[-1], cores))
-        other.append(pass_on(other[-1], cores))
+        if step < PLANES // 2:
+            same.append(pass_on(same[-1], (0, 1)))
+            other.append(pass_on(other[-1], (0, 1)))
+        else:
+            half = keys_values.shape[0] // 2
+            same.append(pass_on(same[-1], (1,)))
+            share = jnp.where(core == 0, same[step - 1][:half], other[step - 1][half:])
+            other.append(pass_on(share, (0, 1)))
         if sums is not None:
             same[-1], sums = lax.optimization_barrier((same[-1], sums))
         if step == 1:

time: 164 us -> 169 us (1.030)
  starting transfers between devices: 102 us -> 108 us
    ppermute x3, starting transfers between devices: 9.55 us -> 17.1 us  [swap_cores(): return lax.ppermute(block, 'bal', [(at, at ^ 1) for at in range(32)])]
  transfers between devices with their start and end apart: 28 -> 28, of which waited for: 10 -> 11; matrix products, arithmetic and copies ran while one was open for 1% -> 1% of each run, Pallas kernels for 16% -> 15%
where the time goes in v13:
time: 169 us; the launch traced here: 168 us
  starting transfers between devices  108 us (64%)
  Pallas kernels  30.3 us (18%)
  waiting for transfers between devices  15.8 us (9%)
  blocking collectives  10.3 us (6%)
  local copies, waits for them, and re-layouts  1.91 us (1%)
    ppermute x16, starting transfers between devices, pass_on(): return lax.ppermute(block, 'bal', pairs)  61.4 us
    ppermute x9, starting transfers between devices, send(): return lax.ppermute(block, MESH_AXES, plane_perm(phase, shift))  29.3 us
    pallas_call x7, Pallas kernels, attend(): pl.pallas_call(functools.partial(attend_kernel, scale, first_call, last_c...  17.4 us
    ppermute x3, starting transfers between devices, swap_cores(): return lax.ppermute(block, 'bal', [(at, at ^ 1) for at in range(32)])  17.1 us
    all_to_all x1, blocking collectives, on_device(): lax.all_to_all(result.reshape(slots * TILE, HEAD), 'seq', split_axis=0, c...  10.3 us
    pallas_call x3, Pallas kernels, project(): pl.pallas_call(functools.partial(project_kernel, shares), out_shape=(jax....  9.37 us
    ppermute x9, waiting for transfers between devices, send(): return lax.ppermute(block, MESH_AXES, plane_perm(phase, shift))  8.29 us
    ppermute x16, waiting for transfers between devices, pass_on(): return lax.ppermute(block, 'bal', pairs)  4.61 us
  transfers between devices with their start and end apart: 28, of which 11 were waited for; matrix products, arithmetic and copies ran while one was open for 1% of the time, Pallas kernels for 15%

profile of v13, /device:TPU:1, one launch (start us, length us, event | category | flops | bytes accessed | tf_op | source)
XLA Modules:
  0.0 167.7 jit_solution(8457101042390050267)
XLA Ops:
  0.0 5.6 %collective-permute-start.1 = (bf16[48,3072]{1,0:T(8,128)(2,1)}, bf16[48,3072]{1,0:T(8,128)(2,1)S(1)}, u32[]{:S(2)}, u32[]{:S(2)}) collective-permute-start(bf16[48,3072]{1,0:T(8,128)(2,1)} %refs_0_.1), channel_id=1, source_target_pairs={{0,96},{32,0},{64,32},{96,64},{128,224},{160,128},{192,160},{224,1... | collective-permute-start | bytes 884744 | tf_op jit(solution)/shard_map/ppermute | solution.py:34
  5.6 1.9 %collective-permute-start = (bf16[48,3072]{1,0:T(8,128)(2,1)}, bf16[48,3072]{1,0:T(8,128)(2,1)S(1)}, u32[]{:S(2)}, u32[]{:S(2)}) collective-permute-start(bf16[48,3072]{1,0:T(8,128)(2,1)} %refs_0_.1), channel_id=1, source_target_pairs={{0,32},{32,64},{64,96},{96,0},{128,160},{160,192},{192,224},{224,1... | collective-permute-start | bytes 884744 | tf_op jit(solution)/shard_map/ppermute | solution.py:34
  7.5 3.5 %collective-permute-start.4 = (bf16[48,3072]{1,0:T(8,128)(2,1)}, bf16[48,3072]{1,0:T(8,128)(2,1)S(1)}, u32[]{:S(2)}, u32[]{:S(2)}) collective-permute-start(bf16[48,3072]{1,0:T(8,128)(2,1)} %refs_0_.1), channel_id=1, source_target_pairs={{0,64},{32,96},{64,0},{96,32},{128,192},{160,224},{192,128},{224,1... | collective-permute-start | bytes 884744 | tf_op jit(solution)/shard_map/ppermute | solution.py:34
  11.1 1.0 copy-done.2
  12.1 0.1 join.3.refs_1_
  12.1 0.7 pad_maximum_fusion.1.refs_5_.refs_3_
  12.8 0.0 collective-permute-done.1.refs_0_
  12.8 5.1 %collective-permute-done.refs_0_ = bf16[48,3072]{1,0:T(8,128)(2,1)S(1)} collective-permute-done((bf16[48,3072]{1,0:T(8,128)(2,1)}, bf16[48,3072]{1,0:T(8,128)(2,1)S(1)}, u32[]{:S(2)}, u32[]{:S(2)}) %collective-permute-start) | collective-permute-done | bytes 294944 | tf_op jit(solution)/shard_map/ppermute | solution.py:34
  17.9 0.1 join.4.refs_0_
  18.0 2.8 %collective-permute-start.2 = (bf16[96,3072]{1,0:T(8,128)(2,1)S(1)}, bf16[96,3072]{1,0:T(8,128)(2,1)}, u32[]{:S(2)}, u32[]{:S(2)}) collective-permute-start(bf16[96,3072]{1,0:T(8,128)(2,1)S(1)} %join.4.refs_0_), channel_id=1, source_target_pairs={{0,128},{32,160},{64,192},{96,224},{128,256},{160,288},{192,320},{... | collective-permute-start | bytes 1769480 | tf_op jit(solution)/shard_map/ppermute | solution.py:34
  20.9 0.8 join.5.refs_1_
  21.7 3.7 %collective-permute-start.5 = (bf16[96,3072]{1,0:T(8,128)(2,1)}, bf16[96,3072]{1,0:T(8,128)(2,1)}, u32[]{:S(2)}, u32[]{:S(2)}) collective-permute-start(bf16[96,3072]{1,0:T(8,128)(2,1)} %join.5.refs_1_), channel_id=1, source_target_pairs={{0,384},{32,416},{64,448},{96,480},{128,0},{160,32},{192,64},{224,... | collective-permute-start | bytes 1769480 | tf_op jit(solution)/shard_map/ppermute | solution.py:34
  25.4 2.9 %collective-permute-start.7 = (bf16[96,3072]{1,0:T(8,128)(2,1)S(1)}, bf16[96,3072]{1,0:T(8,128)(2,1)}, u32[]{:S(2)}, u32[]{:S(2)}) collective-permute-start(bf16[96,3072]{1,0:T(8,128)(2,1)S(1)} %join.4.refs_0_), channel_id=1, source_target_pairs={{0,384},{32,416},{64,448},{96,480},{128,0},{160,32},{192,64},{224,... | collective-permute-start | bytes 1769480 | tf_op jit(solution)/shard_map/ppermute | solution.py:34
  28.3 2.4 %collective-permute-start.8 = (bf16[96,3072]{1,0:T(8,128)(2,1)}, bf16[96,3072]{1,0:T(8,128)(2,1)}, u32[]{:S(2)}, u32[]{:S(2)}) collective-permute-start(bf16[96,3072]{1,0:T(8,128)(2,1)} %join.5.refs_1_), channel_id=1, source_target_pairs={{0,128},{32,160},{64,192},{96,224},{128,256},{160,288},{192,320},{... | collective-permute-start | bytes 1769480 | tf_op jit(solution)/shard_map/ppermute | solution.py:34
  30.7 1.9 %collective-permute-start.3 = (bf16[96,3072]{1,0:T(8,128)(2,1)}, bf16[96,3072]{1,0:T(8,128)(2,1)}, u32[]{:S(2)}, u32[]{:S(2)}) collective-permute-start(bf16[96,3072]{1,0:T(8,128)(2,1)} %collective-permute-done.2.refs_2_), channel_id=1, source_target_pairs={{0,128},{32,160},{64,192},{96,224},{128,256},{160,288},{192,320},{... | collective-permute-start | bytes 1769480 | tf_op jit(solution)/shard_map/ppermute | solution.py:34
  32.6 0.3 collective-permute-done.5.refs_3_
  33.0 4.6 %collective-permute-start.6 = (bf16[96,3072]{1,0:T(8,128)(2,1)}, bf16[96,3072]{1,0:T(8,128)(2,1)}, u32[]{:S(2)}, u32[]{:S(2)}) collective-permute-start(bf16[96,3072]{1,0:T(8,128)(2,1)} %collective-permute-done.5.refs_3_), channel_id=1, source_target_pairs={{0,384},{32,416},{64,448},{96,480},{128,0},{160,32},{192,64},{224,... | collective-permute-start | bytes 1769480 | tf_op jit(solution)/shard_map/ppermute | solution.py:34
  37.6 0.1 stack.27.place
  37.7 3.7 %project.3 = (bf16[768,128]{1,0:T(8,128)(2,1)S(1)}, bf16[768,256]{1,0:T(8,128)(2,1)}) custom-call(s32[6]{0:T(128)S(1)} %stack.27.place, bf16[96,3072]{1,0:T(8,128)(2,1)S(1)} %join.4.refs_0_, bf16[96,3072]{1,0:T(8,128)(2,1)} %join.5.refs_1_, bf16[96,3072]{1,0:T(8,128)(2,1)} %collective-permute-done.2.refs_2_, ...), custom_call_target="tpu_custom_call" | custom-call | tf_op jit(solution)/shard_map/project/pallas_call | solution.py:116
  41.4 2.8 %project.4 = (bf16[768,128]{1,0:T(8,128)(2,1)S(1)}, bf16[768,256]{1,0:T(8,128)(2,1)}) custom-call(s32[6]{0:T(128)S(1)} %stack.27.place, bf16[96,3072]{1,0:T(8,128)(2,1)} %collective-permute-done.7.refs_0_, bf16[96,3072]{1,0:T(8,128)(2,1)} %collective-permute-done.8.refs_1_, ...), custom_call_target="tpu_custom_call", output_to_operand_aliasing={{0}: (5, {}), {1}: (6, {})} | custom-call | tf_op jit(solution)/shard_map/project/pallas_call | solution.py:116
  44.2 2.8 %collective-permute-done.3.refs_0_ = bf16[96,3072]{1,0:T(8,128)(2,1)} collective-permute-done((bf16[96,3072]{1,0:T(8,128)(2,1)}, bf16[96,3072]{1,0:T(8,128)(2,1)}, u32[]{:S(2)}, u32[]{:S(2)}) %collective-permute-start.3) | collective-permute-done | bytes 589856 | tf_op jit(solution)/shard_map/ppermute | solution.py:34
  47.1 2.8 %project.5 = (bf16[768,128]{1,0:T(8,128)(2,1)S(1)}, bf16[768,256]{1,0:T(8,128)(2,1)}) custom-call(s32[6]{0:T(128)S(1)} %stack.27.place, bf16[96,3072]{1,0:T(8,128)(2,1)} %collective-permute-done.3.refs_0_, bf16[96,3072]{1,0:T(8,128)(2,1)} %collective-permute-done.6.refs_1_, ...), custom_call_target="tpu_custom_call", output_to_operand_aliasing={{0}: (5, {}), {1}: (6, {})} | custom-call | tf_op jit(solution)/shard_map/project/pallas_call | solution.py:116
  49.9 5.7 %collective-permute-start.10 = (bf16[768,256]{1,0:T(8,128)(2,1)}, bf16[768,256]{1,0:T(8,128)(2,1)S(1)}, u32[]{:S(2)}, u32[]{:S(2)}) collective-permute-start(bf16[768,256]{1,0:T(8,128)(2,1)} %get-tuple-element.47), channel_id=1, source_target_pairs={{0,1},{1,0},{2,3},{3,2},{4,5},{5,4},{6,7},{7,6},{8,9},{9,8},{10,11... | collective-permute-start | bytes 1179656 | tf_op jit(solution)/shard_map/ppermute | solution.py:65
  55.6 11.1 %collective-permute-start.9 = (bf16[768,256]{1,0:T(8,128)(2,1)}, bf16[768,256]{1,0:T(8,128)(2,1)S(1)}, u32[]{:S(2)}, u32[]{:S(2)}) collective-permute-start(bf16[768,256]{1,0:T(8,128)(2,1)} %get-tuple-element.47), channel_id=1, source_target_pairs={{0,2},{1,31},{2,4},{3,1},{4,6},{5,3},{6,8},{7,5},{8,10},{9,7},{10,... | collective-permute-start | bytes 1179656 | tf_op jit(solution)/shard_map/ppermute | solution.py:75
  66.8 2.6 %collective-permute-start.13 = (bf16[768,256]{1,0:T(8,128)(2,1)S(1)}, bf16[768,256]{1,0:T(8,128)(2,1)S(1)}, u32[]{:S(2)}, u32[]{:S(2)}) collective-permute-start(bf16[768,256]{1,0:T(8,128)(2,1)S(1)} %collective-permute-done.10), channel_id=1, source_target_pairs={{0,2},{1,31},{2,4},{3,1},{4,6},{5,3},{6,8},{7,5},{8,10},{9,7},{10,... | collective-permute-start | bytes 1179656 | tf_op jit(solution)/shard_map/ppermute | solution.py:75
  69.4 1.9 %collective-permute-start.11 = (bf16[768,128]{1,0:T(8,128)(2,1)S(1)}, bf16[768,128]{1,0:T(8,128)(2,1)S(1)}, u32[]{:S(2)}, u32[]{:S(2)}) collective-permute-start(bf16[768,128]{1,0:T(8,128)(2,1)S(1)} %get-tuple-element.49), channel_id=1, source_target_pairs={{0,1},{1,0},{2,3},{3,2},{4,5},{5,4},{6,7},{7,6},{8,9},{9,8},{10,11... | collective-permute-start | bytes 589832 | tf_op jit(solution)/shard_map/ppermute | solution.py:65
  71.4 0.1 constant_dynamic-slice_fusion.counts
  71.4 0.3 collective-permute-done.9
  71.8 1.0 collective-permute-done.11
  72.7 3.9 %collective-permute-start.12 = (bf16[768,256]{1,0:T(8,128)(2,1)S(1)}, bf16[768,256]{1,0:T(8,128)(2,1)S(1)}, u32[]{:S(2)}, u32[]{:S(2)}) collective-permute-start(bf16[768,256]{1,0:T(8,128)(2,1)S(1)} %collective-permute-done.9), channel_id=1, source_target_pairs={{0,2},{1,31},{2,4},{3,1},{4,6},{5,3},{6,8},{7,5},{8,10},{9,7},{10,... | collective-permute-start | bytes 1179656 | tf_op jit(solution)/shard_map/ppermute | solution.py:75
  76.7 4.2 %collective-permute-start.14 = (bf16[768,256]{1,0:T(8,128)(2,1)S(1)}, bf16[768,256]{1,0:T(8,128)(2,1)S(1)}, u32[]{:S(2)}, u32[]{:S(2)}) collective-permute-start(bf16[768,256]{1,0:T(8,128)(2,1)S(1)} %collective-permute-done.13), channel_id=1, source_target_pairs={{0,2},{1,31},{2,4},{3,1},{4,6},{5,3},{6,8},{7,5},{8,10},{9,7},{10,... | collective-permute-start | bytes 1179656 | tf_op jit(solution)/shard_map/ppermute | solution.py:75
  81.0 0.1 dynamic-slice_bitcast_fusion.tiles
  81.1 2.6 %lists.1 = (s32[7,384]{1,0:T(8,128)S(1)}, s32[1,7]{1,0:T(1,128)S(1)}) custom-call(s32[6]{0:T(128)S(1)} %stack.27.place, s32[64,12]{1,0:T(8,128)S(1)} %dynamic-slice_bitcast_fusion.tiles, s32[1,12]{1,0:T(1,128)S(1)} %constant_dynamic-slice_fusion.counts), custom_call_target="tpu_custom_call" | custom-call | tf_op jit(solution)/shard_map/lists/pallas_call | solution.py:273
  83.7 2.7 %collective-permute-start.15 = (bf16[768,256]{1,0:T(8,128)(2,1)S(1)}, bf16[768,256]{1,0:T(8,128)(2,1)S(1)}, u32[]{:S(2)}, u32[]{:S(2)}) collective-permute-start(bf16[768,256]{1,0:T(8,128)(2,1)S(1)} %collective-permute-done.12), channel_id=1, source_target_pairs={{0,2},{1,31},{2,4},{3,1},{4,6},{5,3},{6,8},{7,5},{8,10},{9,7},{10,... | collective-permute-start | bytes 1179656 | tf_op jit(solution)/shard_map/ppermute | solution.py:75
  86.4 4.2 %collective-permute-start.17 = (bf16[768,256]{1,0:T(8,128)(2,1)S(1)}, bf16[768,256]{1,0:T(8,128)(2,1)S(1)}, u32[]{:S(2)}, u32[]{:S(2)}) collective-permute-start(bf16[768,256]{1,0:T(8,128)(2,1)S(1)} %collective-permute-done.14), channel_id=1, source_target_pairs={{0,2},{1,31},{2,4},{3,1},{4,6},{5,3},{6,8},{7,5},{8,10},{9,7},{10,... | collective-permute-start | bytes 1179656 | tf_op jit(solution)/shard_map/ppermute | solution.py:75
  90.6 4.1 %attend.7.refs_2_ = f32[13,128,256]{2,1,0:T(8,128)S(1)} custom-call(s32[6]{0:T(128)S(1)} %stack.27.place, s32[7,384]{1,0:T(8,128)S(1)} %get-tuple-element.54.pairs, s32[1,7]{1,0:T(1,128)S(1)} %get-tuple-element.55.counts, bf16[12,128,128]{2,1,0:T(8,128)(2,1)S(1)} %bitcast.41, bf16[6,128,256]{2,1,0:T(8,128)(2,1)} %bitcast.12.refs_0_, ...), custom_call_target="tpu_custom_call" | custom-call | flops 5000000000 | bytes 5000000 | tf_op jit(solution)/shard_map/attend/pallas_call | solution.py:198
  94.8 1.9 %collective-permute-start.16 = (bf16[768,256]{1,0:T(8,128)(2,1)S(1)}, bf16[768,256]{1,0:T(8,128)(2,1)S(1)}, u32[]{:S(2)}, u32[]{:S(2)}) collective-permute-start(bf16[768,256]{1,0:T(8,128)(2,1)S(1)} %collective-permute-done.15), channel_id=1, source_target_pairs={{0,2},{1,31},{2,4},{3,1},{4,6},{5,3},{6,8},{7,5},{8,10},{9,7},{10,... | collective-permute-start | bytes 1179656 | tf_op jit(solution)/shard_map/ppermute | solution.py:75
  96.7 0.0 collective-permute-done.17
  96.7 3.6 %collective-permute-start.19 = (bf16[768,256]{1,0:T(8,128)(2,1)S(1)}, bf16[768,256]{1,0:T(8,128)(2,1)S(1)}, u32[]{:S(2)}, u32[]{:S(2)}) collective-permute-start(bf16[768,256]{1,0:T(8,128)(2,1)S(1)} %collective-permute-done.17), channel_id=1, source_target_pairs={{0,2},{1,31},{2,4},{3,1},{4,6},{5,3},{6,8},{7,5},{8,10},{9,7},{10,... | collective-permute-start | bytes 1179656 | tf_op jit(solution)/shard_map/ppermute | solution.py:75
  100.3 2.0 %attend.8.refs_2_ = f32[13,128,256]{2,1,0:T(8,128)S(1)} custom-call(s32[6]{0:T(128)S(1)} %stack.27.place, s32[7,384]{1,0:T(8,128)S(1)} %get-tuple-element.54.pairs, s32[1,7]{1,0:T(1,128)S(1)} %get-tuple-element.55.counts, bf16[12,128,128]{2,1,0:T(8,128)(2,1)S(1)} %bitcast.42, bf16[6,128,256]{2,1,0:T(8,128)(2,1)S(1)} %bitcast.55, ...), custom_call_target="tpu_custom_call", output_to_operand_aliasing={{}: (6, {})} | custom-call | flops 2000000000 | bytes 2000000 | tf_op jit(solution)/shard_map/attend/pallas_call | solution.py:198
  102.3 1.3 collective-permute-done.16
  103.6 2.8 %collective-permute-start.18 = (bf16[768,256]{1,0:T(8,128)(2,1)S(1)}, bf16[768,256]{1,0:T(8,128)(2,1)S(1)}, u32[]{:S(2)}, u32[]{:S(2)}) collective-permute-start(bf16[768,256]{1,0:T(8,128)(2,1)S(1)} %collective-permute-done.16), channel_id=1, source_target_pairs={{0,2},{1,31},{2,4},{3,1},{4,6},{5,3},{6,8},{7,5},{8,10},{9,7},{10,... | collective-permute-start | bytes 1179656 | tf_op jit(solution)/shard_map/ppermute | solution.py:75
  106.4 1.4 collective-permute-done.19
  107.8 2.8 %collective-permute-start.21 = (bf16[768,256]{1,0:T(8,128)(2,1)S(1)}, bf16[768,256]{1,0:T(8,128)(2,1)S(1)}, u32[]{:S(2)}, u32[]{:S(2)}) collective-permute-start(bf16[768,256]{1,0:T(8,128)(2,1)S(1)} %collective-permute-done.19), channel_id=1, source_target_pairs={{0,2},{1,31},{2,4},{3,1},{4,6},{5,3},{6,8},{7,5},{8,10},{9,7},{10,... | collective-permute-start | bytes 1179656 | tf_op jit(solution)/shard_map/ppermute | solution.py:75
  110.6 2.0 %attend.9.refs_2_ = f32[13,128,256]{2,1,0:T(8,128)S(1)} custom-call(s32[6]{0:T(128)S(1)} %stack.27.place, s32[7,384]{1,0:T(8,128)S(1)} %get-tuple-element.54.pairs, s32[1,7]{1,0:T(1,128)S(1)} %get-tuple-element.55.counts, bf16[12,128,128]{2,1,0:T(8,128)(2,1)S(1)} %bitcast.43, bf16[6,128,256]{2,1,0:T(8,128)(2,1)S(1)} %bitcast.56, ...), custom_call_target="tpu_custom_call", output_to_operand_aliasing={{}: (6, {})} | custom-call | flops 2000000000 | bytes 2000000 | tf_op jit(solution)/shard_map/attend/pallas_call | solution.py:198
  112.6 3.5 %collective-permute-start.20 = (bf16[768,256]{1,0:T(8,128)(2,1)S(1)}, bf16[768,256]{1,0:T(8,128)(2,1)S(1)}, u32[]{:S(2)}, u32[]{:S(2)}) collective-permute-start(bf16[768,256]{1,0:T(8,128)(2,1)S(1)} %collective-permute-done.18), channel_id=1, source_target_pairs={{0,2},{1,31},{2,4},{3,1},{4,6},{5,3},{6,8},{7,5},{8,10},{9,7},{10,... | collective-permute-start | bytes 1179656 | tf_op jit(solution)/shard_map/ppermute | solution.py:75
  116.1 0.5 collective-permute-done.21
  116.6 3.7 %collective-permute-start.23 = (bf16[768,256]{1,0:T(8,128)(2,1)S(1)}, bf16[768,256]{1,0:T(8,128)(2,1)S(1)}, u32[]{:S(2)}, u32[]{:S(2)}) collective-permute-start(bf16[768,256]{1,0:T(8,128)(2,1)S(1)} %collective-permute-done.21), channel_id=1, source_target_pairs={{0,2},{1,31},{2,4},{3,1},{4,6},{5,3},{6,8},{7,5},{8,10},{9,7},{10,... | collective-permute-start | bytes 1179656 | tf_op jit(solution)/shard_map/ppermute | solution.py:75
  120.4 2.5 %attend.10.refs_2_ = f32[13,128,256]{2,1,0:T(8,128)S(1)} custom-call(s32[6]{0:T(128)S(1)} %stack.27.place, s32[7,384]{1,0:T(8,128)S(1)} %get-tuple-element.54.pairs, s32[1,7]{1,0:T(1,128)S(1)} %get-tuple-element.55.counts, bf16[12,128,128]{2,1,0:T(8,128)(2,1)S(1)} %bitcast.44, bf16[6,128,256]{2,1,0:T(8,128)(2,1)S(1)} %bitcast.58, ...), custom_call_target="tpu_custom_call", output_to_operand_aliasing={{}: (6, {})} | custom-call | flops 2000000000 | bytes 2000000 | tf_op jit(solution)/shard_map/attend/pallas_call | solution.py:198
  122.8 3.0 %collective-permute-start.22 = (bf16[768,256]{1,0:T(8,128)(2,1)S(1)}, bf16[768,256]{1,0:T(8,128)(2,1)S(1)}, u32[]{:S(2)}, u32[]{:S(2)}) collective-permute-start(bf16[768,256]{1,0:T(8,128)(2,1)S(1)} %collective-permute-done.20), channel_id=1, source_target_pairs={{0,2},{1,31},{2,4},{3,1},{4,6},{5,3},{6,8},{7,5},{8,10},{9,7},{10,... | collective-permute-start | bytes 1179656 | tf_op jit(solution)/shard_map/ppermute | solution.py:75
  125.9 4.2 %collective-permute-start.25 = (bf16[768,256]{1,0:T(8,128)(2,1)S(1)}, bf16[768,256]{1,0:T(8,128)(2,1)S(1)}, u32[]{:S(2)}, u32[]{:S(2)}) collective-permute-start(bf16[768,256]{1,0:T(8,128)(2,1)S(1)} %collective-permute-done.23), channel_id=1, source_target_pairs={{0,2},{1,31},{2,4},{3,1},{4,6},{5,3},{6,8},{7,5},{8,10},{9,7},{10,... | collective-permute-start | bytes 1179656 | tf_op jit(solution)/shard_map/ppermute | solution.py:75
  130.1 2.4 %attend.11.refs_2_ = f32[13,128,256]{2,1,0:T(8,128)S(1)} custom-call(s32[6]{0:T(128)S(1)} %stack.27.place, s32[7,384]{1,0:T(8,128)S(1)} %get-tuple-element.54.pairs, s32[1,7]{1,0:T(1,128)S(1)} %get-tuple-element.55.counts, bf16[12,128,128]{2,1,0:T(8,128)(2,1)S(1)} %bitcast.45, bf16[6,128,256]{2,1,0:T(8,128)(2,1)S(1)} %bitcast.60, ...), custom_call_target="tpu_custom_call", output_to_operand_aliasing={{}: (6, {})} | custom-call | flops 2000000000 | bytes 2000000 | tf_op jit(solution)/shard_map/attend/pallas_call | solution.py:198
  132.5 3.0 %collective-permute-start.24 = (bf16[768,256]{1,0:T(8,128)(2,1)S(1)}, bf16[768,256]{1,0:T(8,128)(2,1)S(1)}, u32[]{:S(2)}, u32[]{:S(2)}) collective-permute-start(bf16[768,256]{1,0:T(8,128)(2,1)S(1)} %collective-permute-done.22), channel_id=1, source_target_pairs={{1,31},{3,1},{5,3},{7,5},{9,7},{11,9},{13,11},{15,13},{17,15},{19,... | collective-permute-start | bytes 1179656 | tf_op jit(solution)/shard_map/ppermute | solution.py:75
  135.6 0.3 collective-permute-done.25
  135.9 3.9 %collective-permute-start.26 = (bf16[384,256]{1,0:T(8,128)(2,1)S(1)}, bf16[384,256]{1,0:T(8,128)(2,1)S(1)}, u32[]{:S(2)}, u32[]{:S(2)}) collective-permute-start(bf16[384,256]{1,0:T(8,128)(2,1)S(1)} %slice_select_fusion), channel_id=1, source_target_pairs={{0,2},{1,31},{2,4},{3,1},{4,6},{5,3},{6,8},{7,5},{8,10},{9,7},{10,... | collective-permute-start | bytes 589832 | tf_op jit(solution)/shard_map/ppermute | solution.py:75
  139.8 2.5 %attend.12.refs_2_ = f32[13,128,256]{2,1,0:T(8,128)S(1)} custom-call(s32[6]{0:T(128)S(1)} %stack.27.place, s32[7,384]{1,0:T(8,128)S(1)} %get-tuple-element.54.pairs, s32[1,7]{1,0:T(1,128)S(1)} %get-tuple-element.55.counts, bf16[12,128,128]{2,1,0:T(8,128)(2,1)S(1)} %bitcast.46, bf16[6,128,256]{2,1,0:T(8,128)(2,1)S(1)} %bitcast.48, ...), custom_call_target="tpu_custom_call", output_to_operand_aliasing={{}: (6, {})} | custom-call | flops 2000000000 | bytes 2000000 | tf_op jit(solution)/shard_map/attend/pallas_call | solution.py:198
  142.3 0.9 collective-permute-done.26
  143.2 2.0 %attend.13 = (f32[6,128,256]{2,1,0:T(8,128)S(1)}, f32[6,128,256]{2,1,0:T(8,128)S(1)}) custom-call(s32[6]{0:T(128)S(1)} %stack.27.place, s32[7,384]{1,0:T(8,128)S(1)} %get-tuple-element.54.pairs, s32[1,7]{1,0:T(1,128)S(1)} %get-tuple-element.55.counts, bf16[12,128,128]{2,1,0:T(8,128)(2,1)S(1)} %bitcast.47, bf16[6,128,256]{2,1,0:T(8,128)(2,1)S(1)} %bitcast.62, ...), custom_call_target="tpu_custom_call" | custom-call | flops 2000000000 | bytes 2000000 | tf_op jit(solution)/shard_map/attend/pallas_call | solution.py:198
  145.1 9.5 %collective-permute-start.27 = (f32[6,128,256]{2,1,0:T(8,128)S(1)}, f32[6,128,256]{2,1,0:T(8,128)S(1)}, u32[]{:S(2)}, u32[]{:S(2)}) collective-permute-start(f32[6,128,256]{2,1,0:T(8,128)S(1)} %get-tuple-element.74), channel_id=1, source_target_pairs={{0,1},{1,0},{2,3},{3,2},{4,5},{5,4},{6,7},{7,6},{8,9},{9,8},{10,11... | collective-permute-start | bytes 2359304 | tf_op jit(solution)/shard_map/ppermute | solution.py:65
  154.6 1.9 %collective-permute-done.27 = f32[6,128,256]{2,1,0:T(8,128)S(1)} collective-permute-done((f32[6,128,256]{2,1,0:T(8,128)S(1)}, f32[6,128,256]{2,1,0:T(8,128)S(1)}, u32[]{:S(2)}, u32[]{:S(2)}) %collective-permute-start.27) | collective-permute-done | bytes 786464 | tf_op jit(solution)/shard_map/ppermute | solution.py:65
  156.5 0.1 add.19
  156.6 0.1 fusion
  156.7 10.3 %all_to_all.19 = bf16[16,48,128]{2,1,0:T(8,128)(2,1)S(1)} all-to-all(bf16[16,48,128]{2,1,0:T(8,128)(2,1)S(1)} %bitcast.64), channel_id=1, replica_groups=mesh['seq'=16,'bal'=32] {'seq'}, dimensions={0} | all-to-all | bytes 393216 | tf_op jit(solution)/shard_map/all_to_all | solution.py:377
  167.0 0.7 copy_bitcast_fusion
  (25 shorter events, 0.1 us)
Async XLA Ops:
  0.0 81.0 %copy-start = (s32[1,192,64]{1,2,0:T(8,128)S(1)}, s32[1,192,64]{1,2,0:T(8,128)}, u32[]{:S(2)}) copy-start(s32[1,192,64]{1,2,0:T(8,128)} %param.10) | copy-start | bytes 147460
  0.0 37.7 %copy-start.1 = (bf16[3072,1,3,128]{3,0,2,1:T(8,128)(2,1)S(1)}, bf16[3072,1,3,128]{3,0,2,1:T(8,128)(2,1)}, u32[]{:S(2)}) copy-start(bf16[3072,1,3,128]{3,0,2,1:T(8,128)(2,1)} %param.7) | copy-start | bytes 7077892
  0.0 12.8 %collective-permute-start.1 = (bf16[48,3072]{1,0:T(8,128)(2,1)}, bf16[48,3072]{1,0:T(8,128)(2,1)S(1)}, u32[]{:S(2)}, u32[]{:S(2)}) collective-permute-start(bf16[48,3072]{1,0:T(8,128)(2,1)} %refs_0_.1), channel_id=1, source_target_pairs={{0,96},{32,0},{64,32},{96,64},{128,224},{160,128},{192,160},{224,1... | collective-permute-start | bytes 884744 | tf_op jit(solution)/shard_map/ppermute | solution.py:34
  5.6 12.3 %collective-permute-start = (bf16[48,3072]{1,0:T(8,128)(2,1)}, bf16[48,3072]{1,0:T(8,128)(2,1)S(1)}, u32[]{:S(2)}, u32[]{:S(2)}) collective-permute-start(bf16[48,3072]{1,0:T(8,128)(2,1)} %refs_0_.1), channel_id=1, source_target_pairs={{0,32},{32,64},{64,96},{96,0},{128,160},{160,192},{192,224},{224,1... | collective-permute-start | bytes 884744 | tf_op jit(solution)/shard_map/ppermute | solution.py:34
  7.5 13.3 %collective-permute-start.4 = (bf16[48,3072]{1,0:T(8,128)(2,1)}, bf16[48,3072]{1,0:T(8,128)(2,1)S(1)}, u32[]{:S(2)}, u32[]{:S(2)}) collective-permute-start(bf16[48,3072]{1,0:T(8,128)(2,1)} %refs_0_.1), channel_id=1, source_target_pairs={{0,64},{32,96},{64,0},{96,32},{128,192},{160,224},{192,128},{224,1... | collective-permute-start | bytes 884744 | tf_op jit(solution)/shard_map/ppermute | solution.py:34
  11.1 1.0 copy-start.2
  18.0 12.7 %collective-permute-start.2 = (bf16[96,3072]{1,0:T(8,128)(2,1)S(1)}, bf16[96,3072]{1,0:T(8,128)(2,1)}, u32[]{:S(2)}, u32[]{:S(2)}) collective-permute-start(bf16[96,3072]{1,0:T(8,128)(2,1)S(1)} %join.4.refs_0_), channel_id=1, source_target_pairs={{0,128},{32,160},{64,192},{96,224},{128,256},{160,288},{192,320},{... | collective-permute-start | bytes 1769480 | tf_op jit(solution)/shard_map/ppermute | solution.py:34
  21.7 11.2 %collective-permute-start.5 = (bf16[96,3072]{1,0:T(8,128)(2,1)}, bf16[96,3072]{1,0:T(8,128)(2,1)}, u32[]{:S(2)}, u32[]{:S(2)}) collective-permute-start(bf16[96,3072]{1,0:T(8,128)(2,1)} %join.5.refs_1_), channel_id=1, source_target_pairs={{0,384},{32,416},{64,448},{96,480},{128,0},{160,32},{192,64},{224,... | collective-permute-start | bytes 1769480 | tf_op jit(solution)/shard_map/ppermute | solution.py:34
  25.4 16.0 %collective-permute-start.7 = (bf16[96,3072]{1,0:T(8,128)(2,1)S(1)}, bf16[96,3072]{1,0:T(8,128)(2,1)}, u32[]{:S(2)}, u32[]{:S(2)}) collective-permute-start(bf16[96,3072]{1,0:T(8,128)(2,1)S(1)} %join.4.refs_0_), channel_id=1, source_target_pairs={{0,384},{32,416},{64,448},{96,480},{128,0},{160,32},{192,64},{224,... | collective-permute-start | bytes 1769480 | tf_op jit(solution)/shard_map/ppermute | solution.py:34
  28.3 13.1 %collective-permute-start.8 = (bf16[96,3072]{1,0:T(8,128)(2,1)}, bf16[96,3072]{1,0:T(8,128)(2,1)}, u32[]{:S(2)}, u32[]{:S(2)}) collective-permute-start(bf16[96,3072]{1,0:T(8,128)(2,1)} %join.5.refs_1_), channel_id=1, source_target_pairs={{0,128},{32,160},{64,192},{96,224},{128,256},{160,288},{192,320},{... | collective-permute-start | bytes 1769480 | tf_op jit(solution)/shard_map/ppermute | solution.py:34
  30.7 16.3 %collective-permute-start.3 = (bf16[96,3072]{1,0:T(8,128)(2,1)}, bf16[96,3072]{1,0:T(8,128)(2,1)}, u32[]{:S(2)}, u32[]{:S(2)}) collective-permute-start(bf16[96,3072]{1,0:T(8,128)(2,1)} %collective-permute-done.2.refs_2_), channel_id=1, source_target_pairs={{0,128},{32,160},{64,192},{96,224},{128,256},{160,288},{192,320},{... | collective-permute-start | bytes 1769480 | tf_op jit(solution)/shard_map/ppermute | solution.py:34
  33.0 14.1 %collective-permute-start.6 = (bf16[96,3072]{1,0:T(8,128)(2,1)}, bf16[96,3072]{1,0:T(8,128)(2,1)}, u32[]{:S(2)}, u32[]{:S(2)}) collective-permute-start(bf16[96,3072]{1,0:T(8,128)(2,1)} %collective-permute-done.5.refs_3_), channel_id=1, source_target_pairs={{0,384},{32,416},{64,448},{96,480},{128,0},{160,32},{192,64},{224,... | collective-permute-start | bytes 1769480 | tf_op jit(solution)/shard_map/ppermute | solution.py:34
  47.1 24.3 %copy-start.3 = (s32[1,192]{1,0:T(1,128)S(1)}, s32[1,192]{1,0:T(1,128)}, u32[]{:S(2)}) copy-start(s32[1,192]{1,0:T(1,128)} %param.11) | copy-start | bytes 2308
  49.9 16.8 %collective-permute-start.10 = (bf16[768,256]{1,0:T(8,128)(2,1)}, bf16[768,256]{1,0:T(8,128)(2,1)S(1)}, u32[]{:S(2)}, u32[]{:S(2)}) collective-permute-start(bf16[768,256]{1,0:T(8,128)(2,1)} %get-tuple-element.47), channel_id=1, source_target_pairs={{0,1},{1,0},{2,3},{3,2},{4,5},{5,4},{6,7},{7,6},{8,9},{9,8},{10,11... | collective-permute-start | bytes 1179656 | tf_op jit(solution)/shard_map/ppermute | solution.py:65
  55.6 16.1 %collective-permute-start.9 = (bf16[768,256]{1,0:T(8,128)(2,1)}, bf16[768,256]{1,0:T(8,128)(2,1)S(1)}, u32[]{:S(2)}, u32[]{:S(2)}) collective-permute-start(bf16[768,256]{1,0:T(8,128)(2,1)} %get-tuple-element.47), channel_id=1, source_target_pairs={{0,2},{1,31},{2,4},{3,1},{4,6},{5,3},{6,8},{7,5},{8,10},{9,7},{10,... | collective-permute-start | bytes 1179656 | tf_op jit(solution)/shard_map/ppermute | solution.py:75
  66.8 9.9 %collective-permute-start.13 = (bf16[768,256]{1,0:T(8,128)(2,1)S(1)}, bf16[768,256]{1,0:T(8,128)(2,1)S(1)}, u32[]{:S(2)}, u32[]{:S(2)}) collective-permute-start(bf16[768,256]{1,0:T(8,128)(2,1)S(1)} %collective-permute-done.10), channel_id=1, source_target_pairs={{0,2},{1,31},{2,4},{3,1},{4,6},{5,3},{6,8},{7,5},{8,10},{9,7},{10,... | collective-permute-start | bytes 1179656 | tf_op jit(solution)/shard_map/ppermute | solution.py:75
  69.4 3.3 %collective-permute-start.11 = (bf16[768,128]{1,0:T(8,128)(2,1)S(1)}, bf16[768,128]{1,0:T(8,128)(2,1)S(1)}, u32[]{:S(2)}, u32[]{:S(2)}) collective-permute-start(bf16[768,128]{1,0:T(8,128)(2,1)S(1)} %get-tuple-element.49), channel_id=1, source_target_pairs={{0,1},{1,0},{2,3},{3,2},{4,5},{5,4},{6,7},{7,6},{8,9},{9,8},{10,11... | collective-permute-start | bytes 589832 | tf_op jit(solution)/shard_map/ppermute | solution.py:65
  72.7 10.9 %collective-permute-start.12 = (bf16[768,256]{1,0:T(8,128)(2,1)S(1)}, bf16[768,256]{1,0:T(8,128)(2,1)S(1)}, u32[]{:S(2)}, u32[]{:S(2)}) collective-permute-start(bf16[768,256]{1,0:T(8,128)(2,1)S(1)} %collective-permute-done.9), channel_id=1, source_target_pairs={{0,2},{1,31},{2,4},{3,1},{4,6},{5,3},{6,8},{7,5},{8,10},{9,7},{10,... | collective-permute-start | bytes 1179656 | tf_op jit(solution)/shard_map/ppermute | solution.py:75
  76.7 9.7 %collective-permute-start.14 = (bf16[768,256]{1,0:T(8,128)(2,1)S(1)}, bf16[768,256]{1,0:T(8,128)(2,1)S(1)}, u32[]{:S(2)}, u32[]{:S(2)}) collective-permute-start(bf16[768,256]{1,0:T(8,128)(2,1)S(1)} %collective-permute-done.13), channel_id=1, source_target_pairs={{0,2},{1,31},{2,4},{3,1},{4,6},{5,3},{6,8},{7,5},{8,10},{9,7},{10,... | collective-permute-start | bytes 1179656 | tf_op jit(solution)/shard_map/ppermute | solution.py:75
  83.7 11.1 %collective-permute-start.15 = (bf16[768,256]{1,0:T(8,128)(2,1)S(1)}, bf16[768,256]{1,0:T(8,128)(2,1)S(1)}, u32[]{:S(2)}, u32[]{:S(2)}) collective-permute-start(bf16[768,256]{1,0:T(8,128)(2,1)S(1)} %collective-permute-done.12), channel_id=1, source_target_pairs={{0,2},{1,31},{2,4},{3,1},{4,6},{5,3},{6,8},{7,5},{8,10},{9,7},{10,... | collective-permute-start | bytes 1179656 | tf_op jit(solution)/shard_map/ppermute | solution.py:75
  86.4 10.3 %collective-permute-start.17 = (bf16[768,256]{1,0:T(8,128)(2,1)S(1)}, bf16[768,256]{1,0:T(8,128)(2,1)S(1)}, u32[]{:S(2)}, u32[]{:S(2)}) collective-permute-start(bf16[768,256]{1,0:T(8,128)(2,1)S(1)} %collective-permute-done.14), channel_id=1, source_target_pairs={{0,2},{1,31},{2,4},{3,1},{4,6},{5,3},{6,8},{7,5},{8,10},{9,7},{10,... | collective-permute-start | bytes 1179656 | tf_op jit(solution)/shard_map/ppermute | solution.py:75
  94.8 8.8 %collective-permute-start.16 = (bf16[768,256]{1,0:T(8,128)(2,1)S(1)}, bf16[768,256]{1,0:T(8,128)(2,1)S(1)}, u32[]{:S(2)}, u32[]{:S(2)}) collective-permute-start(bf16[768,256]{1,0:T(8,128)(2,1)S(1)} %collective-permute-done.15), channel_id=1, source_target_pairs={{0,2},{1,31},{2,4},{3,1},{4,6},{5,3},{6,8},{7,5},{8,10},{9,7},{10,... | collective-permute-start | bytes 1179656 | tf_op jit(solution)/shard_map/ppermute | solution.py:75
  96.7 11.1 %collective-permute-start.19 = (bf16[768,256]{1,0:T(8,128)(2,1)S(1)}, bf16[768,256]{1,0:T(8,128)(2,1)S(1)}, u32[]{:S(2)}, u32[]{:S(2)}) collective-permute-start(bf16[768,256]{1,0:T(8,128)(2,1)S(1)} %collective-permute-done.17), channel_id=1, source_target_pairs={{0,2},{1,31},{2,4},{3,1},{4,6},{5,3},{6,8},{7,5},{8,10},{9,7},{10,... | collective-permute-start | bytes 1179656 | tf_op jit(solution)/shard_map/ppermute | solution.py:75
  103.6 9.0 %collective-permute-start.18 = (bf16[768,256]{1,0:T(8,128)(2,1)S(1)}, bf16[768,256]{1,0:T(8,128)(2,1)S(1)}, u32[]{:S(2)}, u32[]{:S(2)}) collective-permute-start(bf16[768,256]{1,0:T(8,128)(2,1)S(1)} %collective-permute-done.16), channel_id=1, source_target_pairs={{0,2},{1,31},{2,4},{3,1},{4,6},{5,3},{6,8},{7,5},{8,10},{9,7},{10,... | collective-permute-start | bytes 1179656 | tf_op jit(solution)/shard_map/ppermute | solution.py:75
  107.8 8.8 %collective-permute-start.21 = (bf16[768,256]{1,0:T(8,128)(2,1)S(1)}, bf16[768,256]{1,0:T(8,128)(2,1)S(1)}, u32[]{:S(2)}, u32[]{:S(2)}) collective-permute-start(bf16[768,256]{1,0:T(8,128)(2,1)S(1)} %collective-permute-done.19), channel_id=1, source_target_pairs={{0,2},{1,31},{2,4},{3,1},{4,6},{5,3},{6,8},{7,5},{8,10},{9,7},{10,... | collective-permute-start | bytes 1179656 | tf_op jit(solution)/shard_map/ppermute | solution.py:75
  112.6 10.2 %collective-permute-start.20 = (bf16[768,256]{1,0:T(8,128)(2,1)S(1)}, bf16[768,256]{1,0:T(8,128)(2,1)S(1)}, u32[]{:S(2)}, u32[]{:S(2)}) collective-permute-start(bf16[768,256]{1,0:T(8,128)(2,1)S(1)} %collective-permute-done.18), channel_id=1, source_target_pairs={{0,2},{1,31},{2,4},{3,1},{4,6},{5,3},{6,8},{7,5},{8,10},{9,7},{10,... | collective-permute-start | bytes 1179656 | tf_op jit(solution)/shard_map/ppermute | solution.py:75
  116.6 9.3 %collective-permute-start.23 = (bf16[768,256]{1,0:T(8,128)(2,1)S(1)}, bf16[768,256]{1,0:T(8,128)(2,1)S(1)}, u32[]{:S(2)}, u32[]{:S(2)}) collective-permute-start(bf16[768,256]{1,0:T(8,128)(2,1)S(1)} %collective-permute-done.21), channel_id=1, source_target_pairs={{0,2},{1,31},{2,4},{3,1},{4,6},{5,3},{6,8},{7,5},{8,10},{9,7},{10,... | collective-permute-start | bytes 1179656 | tf_op jit(solution)/shard_map/ppermute | solution.py:75
  122.8 9.7 %collective-permute-start.22 = (bf16[768,256]{1,0:T(8,128)(2,1)S(1)}, bf16[768,256]{1,0:T(8,128)(2,1)S(1)}, u32[]{:S(2)}, u32[]{:S(2)}) collective-permute-start(bf16[768,256]{1,0:T(8,128)(2,1)S(1)} %collective-permute-done.20), channel_id=1, source_target_pairs={{0,2},{1,31},{2,4},{3,1},{4,6},{5,3},{6,8},{7,5},{8,10},{9,7},{10,... | collective-permute-start | bytes 1179656 | tf_op jit(solution)/shard_map/ppermute | solution.py:75
  125.9 10.0 %collective-permute-start.25 = (bf16[768,256]{1,0:T(8,128)(2,1)S(1)}, bf16[768,256]{1,0:T(8,128)(2,1)S(1)}, u32[]{:S(2)}, u32[]{:S(2)}) collective-permute-start(bf16[768,256]{1,0:T(8,128)(2,1)S(1)} %collective-permute-done.23), channel_id=1, source_target_pairs={{0,2},{1,31},{2,4},{3,1},{4,6},{5,3},{6,8},{7,5},{8,10},{9,7},{10,... | collective-permute-start | bytes 1179656 | tf_op jit(solution)/shard_map/ppermute | solution.py:75
  132.5 9.8 %collective-permute-start.24 = (bf16[768,256]{1,0:T(8,128)(2,1)S(1)}, bf16[768,256]{1,0:T(8,128)(2,1)S(1)}, u32[]{:S(2)}, u32[]{:S(2)}) collective-permute-start(bf16[768,256]{1,0:T(8,128)(2,1)S(1)} %collective-permute-done.22), channel_id=1, source_target_pairs={{1,31},{3,1},{5,3},{7,5},{9,7},{11,9},{13,11},{15,13},{17,15},{19,... | collective-permute-start | bytes 1179656 | tf_op jit(solution)/shard_map/ppermute | solution.py:75
  135.9 7.3 %collective-permute-start.26 = (bf16[384,256]{1,0:T(8,128)(2,1)S(1)}, bf16[384,256]{1,0:T(8,128)(2,1)S(1)}, u32[]{:S(2)}, u32[]{:S(2)}) collective-permute-start(bf16[384,256]{1,0:T(8,128)(2,1)S(1)} %slice_select_fusion), channel_id=1, source_target_pairs={{0,2},{1,31},{2,4},{3,1},{4,6},{5,3},{6,8},{7,5},{8,10},{9,7},{10,... | collective-permute-start | bytes 589832 | tf_op jit(solution)/shard_map/ppermute | solution.py:75
  145.1 11.4 %collective-permute-start.27 = (f32[6,128,256]{2,1,0:T(8,128)S(1)}, f32[6,128,256]{2,1,0:T(8,128)S(1)}, u32[]{:S(2)}, u32[]{:S(2)}) collective-permute-start(f32[6,128,256]{2,1,0:T(8,128)S(1)} %get-tuple-element.74), channel_id=1, source_target_pairs={{0,1},{1,0},{2,3},{3,2},{4,5},{5,4},{6,7},{7,6},{8,9},{9,8},{10,11... | collective-permute-start | bytes 2359304 | tf_op jit(solution)/shard_map/ppermute | solution.py:65

commit v14 on v12

--- a/solution.py
+++ b/solution.py
@@ -11,7 +11,8 @@
 PIECE = 48
 PLANES = 16
 UNROLL = 8
-CALLS = ((0, 3),) + tuple((step, step + 1) for step in range(3, 9))
+CALLS = ((0, 3, None),) + tuple((step, step + 1, None) for step in range(3, 8))
+CALLS += ((8, 9, "other"), (8, 9, "own"))
 LOG2E = 1.4426950408889634
 MESH_AXES = ("seq", "bal")
 VMEM = pl.BlockSpec(memory_space=pltpu.VMEM)
@@ -132,23 +133,21 @@
     )(place, *blocks, weight, gains, *begun)
 
 
-def attend_kernel(scale, first_call, last_call, call, blocks, place, pairs, counts, q, *refs):
+def attend_kernel(scale, call, part, blocks, place, pairs, counts, q, *refs):
     pieces = refs[:blocks]
-    kv = refs[-1]
+    sums, kv = refs[-2:]
     slots = pieces[0].shape[0]
     rows = q.shape[0]
-    if last_call:
-        sums_in, kept, given, sums = refs[blocks : blocks + 4]
-    elif first_call:
-        sums = refs[blocks]
-    else:
-        sums_in, sums = refs[blocks : blocks + 2]
     for at in range(blocks):
         kv[at * slots : (at + 1) * slots] = pieces[at][...]
-    if first_call:
+    if call == 0:
         sums[...] = jnp.zeros_like(sums)
+    elif part is None:
+        sums[...] = refs[blocks][...]
     else:
-        sums[...] = sums_in[...]
+        base = (place[4] if part == "own" else 1 - place[4]) * slots
+        for at in range(slots):
+            sums[at] = refs[blocks][base + at]
     ones = jnp.ones((TILE, HEAD), jnp.bfloat16)
 
     def turn(step, _):
@@ -170,34 +169,33 @@
             values = jnp.concatenate((kv[tile, :, HEAD:], ones), axis=1)
             products.append(jnp.dot(weights, values, preferred_element_type=jnp.float32))
         for (row, _), product in zip(rows_here, products):
+            if part is not None:
+                row = jnp.where(row == rows, slots, row - base)
             sums[row] += product
         return 0
 
     lax.fori_loop(0, (counts[0, call] + UNROLL - 1) // UNROLL, turn, 0)
-    if last_call:
-        core = place[4]
-        for at in range(slots):
-            kept[at] = sums[core * slots + at]
-            given[at] = sums[(1 - core) * slots + at]
-
-
-def attend(call, calls, place, pairs, counts, q, pieces, sums=None):
+    if part is not None:
+        refs[-3][...] = sums[:slots]
+
+
+def attend(call, place, pairs, counts, q, pieces, sums=None):
     scale = HEAD ** (-0.5) * LOG2E
-    first_call, last_call = call == 0, call == calls - 1
+    part = CALLS[call][2]
     blocks, slots, rows = len(pieces), pieces[0].shape[0], q.shape[0]
-    whole = jax.ShapeDtypeStruct((rows + 1, TILE, 2 * HEAD), jnp.float32)
-    half = jax.ShapeDtypeStruct((slots, TILE, 2 * HEAD), jnp.float32)
     scratch = [pltpu.VMEM((blocks * slots, TILE, 2 * HEAD), jnp.bfloat16)]
-    if last_call:
-        scratch.insert(0, pltpu.VMEM(whole.shape, whole.dtype))
-    more = () if first_call else (sums,)
+    rows_out = rows + 1
+    if part is not None:
+        rows_out = slots
+        scratch.insert(0, pltpu.VMEM((slots + 1, TILE, 2 * HEAD), jnp.float32))
+    more = () if call == 0 else (sums,)
     return pl.pallas_call(
-        functools.partial(attend_kernel, scale, first_call, last_call, call, blocks),
-        out_shape=(half, half) if last_call else whole,
+        functools.partial(attend_kernel, scale, call, part, blocks),
+        out_shape=jax.ShapeDtypeStruct((rows_out, TILE, 2 * HEAD), jnp.float32),
         in_specs=[SMEM] * 3 + [VMEM] * (1 + blocks + len(more)),
-        out_specs=(VMEM, VMEM) if last_call else VMEM,
+        out_specs=VMEM,
         scratch_shapes=scratch,
-        input_output_aliases={} if first_call or last_call else {4 + blocks: 0},
+        input_output_aliases={4 + blocks: 0} if call > 0 and part is None else {},
         compiler_params=pltpu.CompilerParams(vmem_limit_bytes=16 * 1024 * 1024),
         cost_estimate=pl.CostEstimate(
             flops=blocks * 10**9, bytes_accessed=blocks * 10**6, transcendentals=0
@@ -232,8 +230,11 @@
     ahead = jnp.where(down < along, 1.0, 0.0)
     nothing = rows * TILE
     totals = []
-    for call, (start, stop) in enumerate(calls):
+    theirs = jnp.where(column >= slots, 1 - core, core)
+    for call, (start, stop, part) in enumerate(calls):
         here = inside & (away >= start) & (away < stop)
+        if part is not None:
+            here = here & (theirs == (0 if part == "own" else 1))
         held = jnp.where(here, 1.0, 0.0)
         total = jnp.sum(held, axis=0, keepdims=True)
         order = jnp.dot(before, held, preferred_element_type=jnp.float32)
@@ -259,7 +260,7 @@
     rows = 2 * slots
     tiles = lax.dynamic_slice_in_dim(key_tiles.T, place[5] * rows, rows, 1)
     counts = lax.dynamic_slice_in_dim(key_counts, place[5] * rows, rows, 1)
-    room = max(call_room(start, stop, slots) for start, stop in calls)
+    room = max(call_room(start, stop, slots) for start, stop, _ in calls)
     return pl.pallas_call(
         functools.partial(list_kernel, slots, calls),
         out_shape=(
@@ -268,7 +269,7 @@
         ),
         in_specs=[SMEM, VMEM, VMEM],
         out_specs=(VMEM, VMEM),
-        compiler_params=pltpu.CompilerParams(vmem_limit_bytes=4 * 1024 * 1024),
+        compiler_params=pltpu.CompilerParams(vmem_limit_bytes=12 * 1024 * 1024),
         name="lists",
     )(place, tiles, counts)
 
@@ -353,11 +354,13 @@
             other[2], chip_queries = lax.optimization_barrier((other[2], chip_queries))
         call = step - CALLS[0][1] + 1
         if call >= 0:
-            start, stop = CALLS[call]
+            start, stop, part = CALLS[call]
             blocks = [tiles(block) for block in same[start:stop] + other[max(start, 1) : stop]]
-            sums = attend(call, len(CALLS), place, pairs, counts, chip_queries, blocks, sums)
-    kept, given = sums
-    sums = kept + swap_cores(given)
+            if part is None:
+                sums = attend(call, place, pairs, counts, chip_queries, blocks, sums)
+    given = swap_cores(attend(call, place, pairs, counts, chip_queries, blocks, sums))
+    kept = attend(call + 1, place, pairs, counts, chip_queries, blocks, sums)
+    sums = kept + given
     result = (sums[:, :, :HEAD] / sums[:, :, HEAD:]).astype(jnp.bfloat16)
     return lax.all_to_all(
         result.reshape(slots * TILE, HEAD), "seq", split_axis=0, concat_axis=1, tiled=True

time: 164 us -> 163 us (level)
  starting transfers between devices: 102 us -> 100 us
    ppermute x16, waiting for transfers between devices: 5.34 us -> 7.39 us  [pass_on(): return lax.ppermute(block, 'bal', pairs)]
    ppermute x16, starting transfers between devices: 62.9 us -> 61.1 us  [pass_on(): return lax.ppermute(block, 'bal', pairs)]
    pallas_call x7 -> x8, Pallas kernels: 17.9 us -> 17.2 us  [attend(): pl.pallas_call(functools.partial(attend_kernel, scale, call, part, blocks...]
  transfers between devices with their start and end apart: 28 -> 28, of which waited for: 10 -> 12; matrix products, arithmetic and copies ran while one was open for 1% -> 1% of each run, Pallas kernels for 16% -> 16%
where the time goes in v14:
time: 163 us; the launch traced here: 162 us
  starting transfers between devices  100 us (61%)
  Pallas kernels  30.3 us (19%)
  waiting for transfers between devices  17.5 us (11%)
  blocking collectives  10.5 us (6%)
  local copies, waits for them, and re-layouts  1.91 us (1%)
    ppermute x16, starting transfers between devices, pass_on(): return lax.ppermute(block, 'bal', pairs)  61.1 us
    ppermute x9, starting transfers between devices, send(): return lax.ppermute(block, MESH_AXES, plane_perm(phase, shift))  29.3 us
    pallas_call x8, Pallas kernels, attend(): pl.pallas_call(functools.partial(attend_kernel, scale, call, part, blocks...  17.2 us
    all_to_all x1, blocking collectives, on_device(): lax.all_to_all(result.reshape(slots * TILE, HEAD), 'seq', split_axis=0, c...  10.5 us
    ppermute x3, starting transfers between devices, swap_cores(): return lax.ppermute(block, 'bal', [(at, at ^ 1) for at in range(32)])  9.55 us
    pallas_call x3, Pallas kernels, project(): pl.pallas_call(functools.partial(project_kernel, shares), out_shape=(jax....  9.37 us
    ppermute x9, waiting for transfers between devices, send(): return lax.ppermute(block, MESH_AXES, plane_perm(phase, shift))  8.27 us
    ppermute x16, waiting for transfers between devices, pass_on(): return lax.ppermute(block, 'bal', pairs)  7.39 us
  transfers between devices with their start and end apart: 28, of which 12 were waited for; matrix products, arithmetic and copies ran while one was open for 1% of the time, Pallas kernels for 16%

profile of v14, /device:TPU:1, one launch (start us, length us, event | category | flops | bytes accessed | tf_op | source)
XLA Modules:
  0.0 161.7 jit_solution(13218192798824752155)
XLA Ops:
  0.0 5.6 %collective-permute-start.1 = (bf16[48,3072]{1,0:T(8,128)(2,1)}, bf16[48,3072]{1,0:T(8,128)(2,1)S(1)}, u32[]{:S(2)}, u32[]{:S(2)}) collective-permute-start(bf16[48,3072]{1,0:T(8,128)(2,1)} %refs_0_.1), channel_id=1, source_target_pairs={{0,96},{32,0},{64,32},{96,64},{128,224},{160,128},{192,160},{224,1... | collective-permute-start | bytes 884744 | tf_op jit(solution)/shard_map/ppermute | solution.py:35
  5.6 1.9 %collective-permute-start = (bf16[48,3072]{1,0:T(8,128)(2,1)}, bf16[48,3072]{1,0:T(8,128)(2,1)S(1)}, u32[]{:S(2)}, u32[]{:S(2)}) collective-permute-start(bf16[48,3072]{1,0:T(8,128)(2,1)} %refs_0_.1), channel_id=1, source_target_pairs={{0,32},{32,64},{64,96},{96,0},{128,160},{160,192},{192,224},{224,1... | collective-permute-start | bytes 884744 | tf_op jit(solution)/shard_map/ppermute | solution.py:35
  7.5 3.5 %collective-permute-start.4 = (bf16[48,3072]{1,0:T(8,128)(2,1)}, bf16[48,3072]{1,0:T(8,128)(2,1)S(1)}, u32[]{:S(2)}, u32[]{:S(2)}) collective-permute-start(bf16[48,3072]{1,0:T(8,128)(2,1)} %refs_0_.1), channel_id=1, source_target_pairs={{0,64},{32,96},{64,0},{96,32},{128,192},{160,224},{192,128},{224,1... | collective-permute-start | bytes 884744 | tf_op jit(solution)/shard_map/ppermute | solution.py:35
  11.1 1.0 copy-done.2
  12.1 0.1 join.3.refs_1_
  12.1 0.7 pad_maximum_fusion.1.refs_5_.refs_3_
  12.8 5.1 %collective-permute-done.refs_0_ = bf16[48,3072]{1,0:T(8,128)(2,1)S(1)} collective-permute-done((bf16[48,3072]{1,0:T(8,128)(2,1)}, bf16[48,3072]{1,0:T(8,128)(2,1)S(1)}, u32[]{:S(2)}, u32[]{:S(2)}) %collective-permute-start) | collective-permute-done | bytes 294944 | tf_op jit(solution)/shard_map/ppermute | solution.py:35
  17.9 0.1 join.4.refs_0_
  18.0 2.8 %collective-permute-start.2 = (bf16[96,3072]{1,0:T(8,128)(2,1)S(1)}, bf16[96,3072]{1,0:T(8,128)(2,1)}, u32[]{:S(2)}, u32[]{:S(2)}) collective-permute-start(bf16[96,3072]{1,0:T(8,128)(2,1)S(1)} %join.4.refs_0_), channel_id=1, source_target_pairs={{0,128},{32,160},{64,192},{96,224},{128,256},{160,288},{192,320},{... | collective-permute-start | bytes 1769480 | tf_op jit(solution)/shard_map/ppermute | solution.py:35
  20.9 0.8 join.5.refs_1_
  21.7 3.7 %collective-permute-start.5 = (bf16[96,3072]{1,0:T(8,128)(2,1)}, bf16[96,3072]{1,0:T(8,128)(2,1)}, u32[]{:S(2)}, u32[]{:S(2)}) collective-permute-start(bf16[96,3072]{1,0:T(8,128)(2,1)} %join.5.refs_1_), channel_id=1, source_target_pairs={{0,384},{32,416},{64,448},{96,480},{128,0},{160,32},{192,64},{224,... | collective-permute-start | bytes 1769480 | tf_op jit(solution)/shard_map/ppermute | solution.py:35
  25.4 2.9 %collective-permute-start.7 = (bf16[96,3072]{1,0:T(8,128)(2,1)S(1)}, bf16[96,3072]{1,0:T(8,128)(2,1)}, u32[]{:S(2)}, u32[]{:S(2)}) collective-permute-start(bf16[96,3072]{1,0:T(8,128)(2,1)S(1)} %join.4.refs_0_), channel_id=1, source_target_pairs={{0,384},{32,416},{64,448},{96,480},{128,0},{160,32},{192,64},{224,... | collective-permute-start | bytes 1769480 | tf_op jit(solution)/shard_map/ppermute | solution.py:35
  28.3 2.4 %collective-permute-start.8 = (bf16[96,3072]{1,0:T(8,128)(2,1)}, bf16[96,3072]{1,0:T(8,128)(2,1)}, u32[]{:S(2)}, u32[]{:S(2)}) collective-permute-start(bf16[96,3072]{1,0:T(8,128)(2,1)} %join.5.refs_1_), channel_id=1, source_target_pairs={{0,128},{32,160},{64,192},{96,224},{128,256},{160,288},{192,320},{... | collective-permute-start | bytes 1769480 | tf_op jit(solution)/shard_map/ppermute | solution.py:35
  30.7 1.9 %collective-permute-start.3 = (bf16[96,3072]{1,0:T(8,128)(2,1)}, bf16[96,3072]{1,0:T(8,128)(2,1)}, u32[]{:S(2)}, u32[]{:S(2)}) collective-permute-start(bf16[96,3072]{1,0:T(8,128)(2,1)} %collective-permute-done.2.refs_2_), channel_id=1, source_target_pairs={{0,128},{32,160},{64,192},{96,224},{128,256},{160,288},{192,320},{... | collective-permute-start | bytes 1769480 | tf_op jit(solution)/shard_map/ppermute | solution.py:35
  32.6 0.3 collective-permute-done.5.refs_3_
  32.9 4.6 %collective-permute-start.6 = (bf16[96,3072]{1,0:T(8,128)(2,1)}, bf16[96,3072]{1,0:T(8,128)(2,1)}, u32[]{:S(2)}, u32[]{:S(2)}) collective-permute-start(bf16[96,3072]{1,0:T(8,128)(2,1)} %collective-permute-done.5.refs_3_), channel_id=1, source_target_pairs={{0,384},{32,416},{64,448},{96,480},{128,0},{160,32},{192,64},{224,... | collective-permute-start | bytes 1769480 | tf_op jit(solution)/shard_map/ppermute | solution.py:35
  37.6 0.1 stack.27.place
  37.7 3.7 %project.3 = (bf16[768,128]{1,0:T(8,128)(2,1)S(1)}, bf16[768,256]{1,0:T(8,128)(2,1)}) custom-call(s32[6]{0:T(128)S(1)} %stack.27.place, bf16[96,3072]{1,0:T(8,128)(2,1)S(1)} %join.4.refs_0_, bf16[96,3072]{1,0:T(8,128)(2,1)} %join.5.refs_1_, bf16[96,3072]{1,0:T(8,128)(2,1)} %collective-permute-done.2.refs_2_, ...), custom_call_target="tpu_custom_call" | custom-call | tf_op jit(solution)/shard_map/project/pallas_call | solution.py:117
  41.4 2.8 %project.4 = (bf16[768,128]{1,0:T(8,128)(2,1)S(1)}, bf16[768,256]{1,0:T(8,128)(2,1)}) custom-call(s32[6]{0:T(128)S(1)} %stack.27.place, bf16[96,3072]{1,0:T(8,128)(2,1)} %collective-permute-done.7.refs_0_, bf16[96,3072]{1,0:T(8,128)(2,1)} %collective-permute-done.8.refs_1_, ...), custom_call_target="tpu_custom_call", output_to_operand_aliasing={{0}: (5, {}), {1}: (6, {})} | custom-call | tf_op jit(solution)/shard_map/project/pallas_call | solution.py:117
  44.2 2.8 %collective-permute-done.3.refs_0_ = bf16[96,3072]{1,0:T(8,128)(2,1)} collective-permute-done((bf16[96,3072]{1,0:T(8,128)(2,1)}, bf16[96,3072]{1,0:T(8,128)(2,1)}, u32[]{:S(2)}, u32[]{:S(2)}) %collective-permute-start.3) | collective-permute-done | bytes 589856 | tf_op jit(solution)/shard_map/ppermute | solution.py:35
  47.1 2.8 %project.5 = (bf16[768,128]{1,0:T(8,128)(2,1)S(1)}, bf16[768,256]{1,0:T(8,128)(2,1)}) custom-call(s32[6]{0:T(128)S(1)} %stack.27.place, bf16[96,3072]{1,0:T(8,128)(2,1)} %collective-permute-done.3.refs_0_, bf16[96,3072]{1,0:T(8,128)(2,1)} %collective-permute-done.6.refs_1_, ...), custom_call_target="tpu_custom_call", output_to_operand_aliasing={{0}: (5, {}), {1}: (6, {})} | custom-call | tf_op jit(solution)/shard_map/project/pallas_call | solution.py:117
  49.9 5.7 %collective-permute-start.10 = (bf16[768,256]{1,0:T(8,128)(2,1)}, bf16[768,256]{1,0:T(8,128)(2,1)S(1)}, u32[]{:S(2)}, u32[]{:S(2)}) collective-permute-start(bf16[768,256]{1,0:T(8,128)(2,1)} %get-tuple-element.45), channel_id=1, source_target_pairs={{0,1},{1,0},{2,3},{3,2},{4,5},{5,4},{6,7},{7,6},{8,9},{9,8},{10,11... | collective-permute-start | bytes 1179656 | tf_op jit(solution)/shard_map/ppermute | solution.py:66
  55.6 11.1 %collective-permute-start.9 = (bf16[768,256]{1,0:T(8,128)(2,1)}, bf16[768,256]{1,0:T(8,128)(2,1)S(1)}, u32[]{:S(2)}, u32[]{:S(2)}) collective-permute-start(bf16[768,256]{1,0:T(8,128)(2,1)} %get-tuple-element.45), channel_id=1, source_target_pairs={{0,2},{1,31},{2,4},{3,1},{4,6},{5,3},{6,8},{7,5},{8,10},{9,7},{10,... | collective-permute-start | bytes 1179656 | tf_op jit(solution)/shard_map/ppermute | solution.py:76
  66.8 2.6 %collective-permute-start.13 = (bf16[768,256]{1,0:T(8,128)(2,1)S(1)}, bf16[768,256]{1,0:T(8,128)(2,1)S(1)}, u32[]{:S(2)}, u32[]{:S(2)}) collective-permute-start(bf16[768,256]{1,0:T(8,128)(2,1)S(1)} %collective-permute-done.10), channel_id=1, source_target_pairs={{0,2},{1,31},{2,4},{3,1},{4,6},{5,3},{6,8},{7,5},{8,10},{9,7},{10,... | collective-permute-start | bytes 1179656 | tf_op jit(solution)/shard_map/ppermute | solution.py:76
  69.4 1.9 %collective-permute-start.11 = (bf16[768,128]{1,0:T(8,128)(2,1)S(1)}, bf16[768,128]{1,0:T(8,128)(2,1)S(1)}, u32[]{:S(2)}, u32[]{:S(2)}) collective-permute-start(bf16[768,128]{1,0:T(8,128)(2,1)S(1)} %get-tuple-element.47), channel_id=1, source_target_pairs={{0,1},{1,0},{2,3},{3,2},{4,5},{5,4},{6,7},{7,6},{8,9},{9,8},{10,11... | collective-permute-start | bytes 589832 | tf_op jit(solution)/shard_map/ppermute | solution.py:66
  71.3 0.1 constant_dynamic-slice_fusion.counts
  71.4 0.3 collective-permute-done.9
  71.8 1.0 collective-permute-done.11
  72.7 3.9 %collective-permute-start.12 = (bf16[768,256]{1,0:T(8,128)(2,1)S(1)}, bf16[768,256]{1,0:T(8,128)(2,1)S(1)}, u32[]{:S(2)}, u32[]{:S(2)}) collective-permute-start(bf16[768,256]{1,0:T(8,128)(2,1)S(1)} %collective-permute-done.9), channel_id=1, source_target_pairs={{0,2},{1,31},{2,4},{3,1},{4,6},{5,3},{6,8},{7,5},{8,10},{9,7},{10,... | collective-permute-start | bytes 1179656 | tf_op jit(solution)/shard_map/ppermute | solution.py:76
  76.7 4.2 %collective-permute-start.14 = (bf16[768,256]{1,0:T(8,128)(2,1)S(1)}, bf16[768,256]{1,0:T(8,128)(2,1)S(1)}, u32[]{:S(2)}, u32[]{:S(2)}) collective-permute-start(bf16[768,256]{1,0:T(8,128)(2,1)S(1)} %collective-permute-done.13), channel_id=1, source_target_pairs={{0,2},{1,31},{2,4},{3,1},{4,6},{5,3},{6,8},{7,5},{8,10},{9,7},{10,... | collective-permute-start | bytes 1179656 | tf_op jit(solution)/shard_map/ppermute | solution.py:76
  81.0 0.1 dynamic-slice_bitcast_fusion.tiles
  81.1 2.8 %lists.1 = (s32[8,384]{1,0:T(8,128)S(1)}, s32[1,8]{1,0:T(1,128)S(1)}) custom-call(s32[6]{0:T(128)S(1)} %stack.27.place, s32[64,12]{1,0:T(8,128)S(1)} %dynamic-slice_bitcast_fusion.tiles, s32[1,12]{1,0:T(1,128)S(1)} %constant_dynamic-slice_fusion.counts), custom_call_target="tpu_custom_call" | custom-call | tf_op jit(solution)/shard_map/lists/pallas_call | solution.py:264
  83.8 2.6 %collective-permute-start.15 = (bf16[768,256]{1,0:T(8,128)(2,1)S(1)}, bf16[768,256]{1,0:T(8,128)(2,1)S(1)}, u32[]{:S(2)}, u32[]{:S(2)}) collective-permute-start(bf16[768,256]{1,0:T(8,128)(2,1)S(1)} %collective-permute-done.12), channel_id=1, source_target_pairs={{0,2},{1,31},{2,4},{3,1},{4,6},{5,3},{6,8},{7,5},{8,10},{9,7},{10,... | collective-permute-start | bytes 1179656 | tf_op jit(solution)/shard_map/ppermute | solution.py:76
  86.4 4.2 %collective-permute-start.17 = (bf16[768,256]{1,0:T(8,128)(2,1)S(1)}, bf16[768,256]{1,0:T(8,128)(2,1)S(1)}, u32[]{:S(2)}, u32[]{:S(2)}) collective-permute-start(bf16[768,256]{1,0:T(8,128)(2,1)S(1)} %collective-permute-done.14), channel_id=1, source_target_pairs={{0,2},{1,31},{2,4},{3,1},{4,6},{5,3},{6,8},{7,5},{8,10},{9,7},{10,... | collective-permute-start | bytes 1179656 | tf_op jit(solution)/shard_map/ppermute | solution.py:76
  90.6 3.6 %attend.8.refs_2_ = f32[13,128,256]{2,1,0:T(8,128)S(1)} custom-call(s32[6]{0:T(128)S(1)} %stack.27.place, s32[8,384]{1,0:T(8,128)S(1)} %get-tuple-element.52.pairs, s32[1,8]{1,0:T(1,128)S(1)} %get-tuple-element.53.counts, bf16[12,128,128]{2,1,0:T(8,128)(2,1)S(1)} %bitcast.41, bf16[6,128,256]{2,1,0:T(8,128)(2,1)} %bitcast.12.refs_0_, ...), custom_call_target="tpu_custom_call" | custom-call | flops 5000000000 | bytes 5000000 | tf_op jit(solution)/shard_map/attend/pallas_call | solution.py:192
  94.3 1.9 %collective-permute-start.16 = (bf16[768,256]{1,0:T(8,128)(2,1)S(1)}, bf16[768,256]{1,0:T(8,128)(2,1)S(1)}, u32[]{:S(2)}, u32[]{:S(2)}) collective-permute-start(bf16[768,256]{1,0:T(8,128)(2,1)S(1)} %collective-permute-done.15), channel_id=1, source_target_pairs={{0,2},{1,31},{2,4},{3,1},{4,6},{5,3},{6,8},{7,5},{8,10},{9,7},{10,... | collective-permute-start | bytes 1179656 | tf_op jit(solution)/shard_map/ppermute | solution.py:76
  96.2 0.6 collective-permute-done.17
  96.8 3.5 %collective-permute-start.19 = (bf16[768,256]{1,0:T(8,128)(2,1)S(1)}, bf16[768,256]{1,0:T(8,128)(2,1)S(1)}, u32[]{:S(2)}, u32[]{:S(2)}) collective-permute-start(bf16[768,256]{1,0:T(8,128)(2,1)S(1)} %collective-permute-done.17), channel_id=1, source_target_pairs={{0,2},{1,31},{2,4},{3,1},{4,6},{5,3},{6,8},{7,5},{8,10},{9,7},{10,... | collective-permute-start | bytes 1179656 | tf_op jit(solution)/shard_map/ppermute | solution.py:76
  100.3 2.0 %attend.9.refs_2_ = f32[13,128,256]{2,1,0:T(8,128)S(1)} custom-call(s32[6]{0:T(128)S(1)} %stack.27.place, s32[8,384]{1,0:T(8,128)S(1)} %get-tuple-element.52.pairs, s32[1,8]{1,0:T(1,128)S(1)} %get-tuple-element.53.counts, bf16[12,128,128]{2,1,0:T(8,128)(2,1)S(1)} %bitcast.42, bf16[6,128,256]{2,1,0:T(8,128)(2,1)S(1)} %bitcast.54, ...), custom_call_target="tpu_custom_call", output_to_operand_aliasing={{}: (6, {})} | custom-call | flops 2000000000 | bytes 2000000 | tf_op jit(solution)/shard_map/attend/pallas_call | solution.py:192
  102.3 0.8 collective-permute-done.16
  103.1 2.8 %collective-permute-start.18 = (bf16[768,256]{1,0:T(8,128)(2,1)S(1)}, bf16[768,256]{1,0:T(8,128)(2,1)S(1)}, u32[]{:S(2)}, u32[]{:S(2)}) collective-permute-start(bf16[768,256]{1,0:T(8,128)(2,1)S(1)} %collective-permute-done.16), channel_id=1, source_target_pairs={{0,2},{1,31},{2,4},{3,1},{4,6},{5,3},{6,8},{7,5},{8,10},{9,7},{10,... | collective-permute-start | bytes 1179656 | tf_op jit(solution)/shard_map/ppermute | solution.py:76
  105.9 1.4 collective-permute-done.19
  107.3 2.8 %collective-permute-start.21 = (bf16[768,256]{1,0:T(8,128)(2,1)S(1)}, bf16[768,256]{1,0:T(8,128)(2,1)S(1)}, u32[]{:S(2)}, u32[]{:S(2)}) collective-permute-start(bf16[768,256]{1,0:T(8,128)(2,1)S(1)} %collective-permute-done.19), channel_id=1, source_target_pairs={{0,2},{1,31},{2,4},{3,1},{4,6},{5,3},{6,8},{7,5},{8,10},{9,7},{10,... | collective-permute-start | bytes 1179656 | tf_op jit(solution)/shard_map/ppermute | solution.py:76
  110.1 2.5 %attend.10.refs_2_ = f32[13,128,256]{2,1,0:T(8,128)S(1)} custom-call(s32[6]{0:T(128)S(1)} %stack.27.place, s32[8,384]{1,0:T(8,128)S(1)} %get-tuple-element.52.pairs, s32[1,8]{1,0:T(1,128)S(1)} %get-tuple-element.53.counts, bf16[12,128,128]{2,1,0:T(8,128)(2,1)S(1)} %bitcast.43, bf16[6,128,256]{2,1,0:T(8,128)(2,1)S(1)} %bitcast.55, ...), custom_call_target="tpu_custom_call", output_to_operand_aliasing={{}: (6, {})} | custom-call | flops 2000000000 | bytes 2000000 | tf_op jit(solution)/shard_map/attend/pallas_call | solution.py:192
  112.6 3.0 %collective-permute-start.20 = (bf16[768,256]{1,0:T(8,128)(2,1)S(1)}, bf16[768,256]{1,0:T(8,128)(2,1)S(1)}, u32[]{:S(2)}, u32[]{:S(2)}) collective-permute-start(bf16[768,256]{1,0:T(8,128)(2,1)S(1)} %collective-permute-done.18), channel_id=1, source_target_pairs={{0,2},{1,31},{2,4},{3,1},{4,6},{5,3},{6,8},{7,5},{8,10},{9,7},{10,... | collective-permute-start | bytes 1179656 | tf_op jit(solution)/shard_map/ppermute | solution.py:76
  115.6 0.5 collective-permute-done.21
  116.1 3.7 %collective-permute-start.23 = (bf16[768,256]{1,0:T(8,128)(2,1)S(1)}, bf16[768,256]{1,0:T(8,128)(2,1)S(1)}, u32[]{:S(2)}, u32[]{:S(2)}) collective-permute-start(bf16[768,256]{1,0:T(8,128)(2,1)S(1)} %collective-permute-done.21), channel_id=1, source_target_pairs={{0,2},{1,31},{2,4},{3,1},{4,6},{5,3},{6,8},{7,5},{8,10},{9,7},{10,... | collective-permute-start | bytes 1179656 | tf_op jit(solution)/shard_map/ppermute | solution.py:76
  119.9 2.0 %attend.11.refs_2_ = f32[13,128,256]{2,1,0:T(8,128)S(1)} custom-call(s32[6]{0:T(128)S(1)} %stack.27.place, s32[8,384]{1,0:T(8,128)S(1)} %get-tuple-element.52.pairs, s32[1,8]{1,0:T(1,128)S(1)} %get-tuple-element.53.counts, bf16[12,128,128]{2,1,0:T(8,128)(2,1)S(1)} %bitcast.44, bf16[6,128,256]{2,1,0:T(8,128)(2,1)S(1)} %bitcast.57, ...), custom_call_target="tpu_custom_call", output_to_operand_aliasing={{}: (6, {})} | custom-call | flops 2000000000 | bytes 2000000 | tf_op jit(solution)/shard_map/attend/pallas_call | solution.py:192
  121.8 3.5 %collective-permute-start.22 = (bf16[768,256]{1,0:T(8,128)(2,1)S(1)}, bf16[768,256]{1,0:T(8,128)(2,1)S(1)}, u32[]{:S(2)}, u32[]{:S(2)}) collective-permute-start(bf16[768,256]{1,0:T(8,128)(2,1)S(1)} %collective-permute-done.20), channel_id=1, source_target_pairs={{0,2},{1,31},{2,4},{3,1},{4,6},{5,3},{6,8},{7,5},{8,10},{9,7},{10,... | collective-permute-start | bytes 1179656 | tf_op jit(solution)/shard_map/ppermute | solution.py:76
  125.4 0.3 collective-permute-done.23
  125.6 3.9 %collective-permute-start.25 = (bf16[768,256]{1,0:T(8,128)(2,1)S(1)}, bf16[768,256]{1,0:T(8,128)(2,1)S(1)}, u32[]{:S(2)}, u32[]{:S(2)}) collective-permute-start(bf16[768,256]{1,0:T(8,128)(2,1)S(1)} %collective-permute-done.23), channel_id=1, source_target_pairs={{0,2},{1,31},{2,4},{3,1},{4,6},{5,3},{6,8},{7,5},{8,10},{9,7},{10,... | collective-permute-start | bytes 1179656 | tf_op jit(solution)/shard_map/ppermute | solution.py:76
  129.6 2.5 %attend.12.refs_2_ = f32[13,128,256]{2,1,0:T(8,128)S(1)} custom-call(s32[6]{0:T(128)S(1)} %stack.27.place, s32[8,384]{1,0:T(8,128)S(1)} %get-tuple-element.52.pairs, s32[1,8]{1,0:T(1,128)S(1)} %get-tuple-element.53.counts, bf16[12,128,128]{2,1,0:T(8,128)(2,1)S(1)} %bitcast.45, bf16[6,128,256]{2,1,0:T(8,128)(2,1)S(1)} %bitcast.59, ...), custom_call_target="tpu_custom_call", output_to_operand_aliasing={{}: (6, {})} | custom-call | flops 2000000000 | bytes 2000000 | tf_op jit(solution)/shard_map/attend/pallas_call | solution.py:192
  132.0 3.0 %collective-permute-start.24 = (bf16[768,256]{1,0:T(8,128)(2,1)S(1)}, bf16[768,256]{1,0:T(8,128)(2,1)S(1)}, u32[]{:S(2)}, u32[]{:S(2)}) collective-permute-start(bf16[768,256]{1,0:T(8,128)(2,1)S(1)} %collective-permute-done.22), channel_id=1, source_target_pairs={{1,31},{3,1},{5,3},{7,5},{9,7},{11,9},{13,11},{15,13},{17,15},{19,... | collective-permute-start | bytes 1179656 | tf_op jit(solution)/shard_map/ppermute | solution.py:76
  135.1 4.2 %collective-permute-start.26 = (bf16[768,256]{1,0:T(8,128)(2,1)S(1)}, bf16[768,256]{1,0:T(8,128)(2,1)S(1)}, u32[]{:S(2)}, u32[]{:S(2)}) collective-permute-start(bf16[768,256]{1,0:T(8,128)(2,1)S(1)} %collective-permute-done.25), channel_id=1, source_target_pairs={{1,31},{3,1},{5,3},{7,5},{9,7},{11,9},{13,11},{15,13},{17,15},{19,... | collective-permute-start | bytes 1179656 | tf_op jit(solution)/shard_map/ppermute | solution.py:76
  139.3 2.0 %attend.13.refs_2_ = f32[13,128,256]{2,1,0:T(8,128)S(1)} custom-call(s32[6]{0:T(128)S(1)} %stack.27.place, s32[8,384]{1,0:T(8,128)S(1)} %get-tuple-element.52.pairs, s32[1,8]{1,0:T(1,128)S(1)} %get-tuple-element.53.counts, bf16[12,128,128]{2,1,0:T(8,128)(2,1)S(1)} %bitcast.46, bf16[6,128,256]{2,1,0:T(8,128)(2,1)S(1)} %bitcast.61, ...), custom_call_target="tpu_custom_call", output_to_operand_aliasing={{}: (6, {})} | custom-call | flops 2000000000 | bytes 2000000 | tf_op jit(solution)/shard_map/attend/pallas_call | solution.py:192
  141.3 3.5 %collective-permute-done.26 = bf16[768,256]{1,0:T(8,128)(2,1)S(1)} collective-permute-done((bf16[768,256]{1,0:T(8,128)(2,1)S(1)}, bf16[768,256]{1,0:T(8,128)(2,1)S(1)}, u32[]{:S(2)}, u32[]{:S(2)}) %collective-permute-start.26) | collective-permute-done | bytes 393248 | tf_op jit(solution)/shard_map/ppermute | solution.py:76
  144.8 1.4 attend.15
  146.2 1.9 %collective-permute-start.27 = (f32[6,128,256]{2,1,0:T(8,128)S(1)}, f32[6,128,256]{2,1,0:T(8,128)S(1)}, u32[]{:S(2)}, u32[]{:S(2)}) collective-permute-start(f32[6,128,256]{2,1,0:T(8,128)S(1)} %attend.15), channel_id=1, source_target_pairs={{0,1},{1,0},{2,3},{3,2},{4,5},{5,4},{6,7},{7,6},{8,9},{9,8},{10,11... | collective-permute-start | bytes 2359304 | tf_op jit(solution)/shard_map/ppermute | solution.py:66
  148.1 1.4 attend.14
  149.5 0.9 collective-permute-done.27
  150.3 0.1 add.19
  150.5 0.1 fusion
  150.5 10.5 %all_to_all.19 = bf16[16,48,128]{2,1,0:T(8,128)(2,1)S(1)} all-to-all(bf16[16,48,128]{2,1,0:T(8,128)(2,1)S(1)} %bitcast.67), channel_id=1, replica_groups=mesh['seq'=16,'bal'=32] {'seq'}, dimensions={0} | all-to-all | bytes 393216 | tf_op jit(solution)/shard_map/all_to_all | solution.py:365
  161.1 0.7 copy_bitcast_fusion
  (25 shorter events, 0.1 us)
Async XLA Ops:
  0.0 81.0 %copy-start = (s32[1,192,64]{1,2,0:T(8,128)S(1)}, s32[1,192,64]{1,2,0:T(8,128)}, u32[]{:S(2)}) copy-start(s32[1,192,64]{1,2,0:T(8,128)} %param.10) | copy-start | bytes 147460
  0.0 37.7 %copy-start.1 = (bf16[3072,1,3,128]{3,0,2,1:T(8,128)(2,1)S(1)}, bf16[3072,1,3,128]{3,0,2,1:T(8,128)(2,1)}, u32[]{:S(2)}) copy-start(bf16[3072,1,3,128]{3,0,2,1:T(8,128)(2,1)} %param.7) | copy-start | bytes 7077892
  0.0 12.8 %collective-permute-start.1 = (bf16[48,3072]{1,0:T(8,128)(2,1)}, bf16[48,3072]{1,0:T(8,128)(2,1)S(1)}, u32[]{:S(2)}, u32[]{:S(2)}) collective-permute-start(bf16[48,3072]{1,0:T(8,128)(2,1)} %refs_0_.1), channel_id=1, source_target_pairs={{0,96},{32,0},{64,32},{96,64},{128,224},{160,128},{192,160},{224,1... | collective-permute-start | bytes 884744 | tf_op jit(solution)/shard_map/ppermute | solution.py:35
  5.6 12.3 %collective-permute-start = (bf16[48,3072]{1,0:T(8,128)(2,1)}, bf16[48,3072]{1,0:T(8,128)(2,1)S(1)}, u32[]{:S(2)}, u32[]{:S(2)}) collective-permute-start(bf16[48,3072]{1,0:T(8,128)(2,1)} %refs_0_.1), channel_id=1, source_target_pairs={{0,32},{32,64},{64,96},{96,0},{128,160},{160,192},{192,224},{224,1... | collective-permute-start | bytes 884744 | tf_op jit(solution)/shard_map/ppermute | solution.py:35
  7.5 13.3 %collective-permute-start.4 = (bf16[48,3072]{1,0:T(8,128)(2,1)}, bf16[48,3072]{1,0:T(8,128)(2,1)S(1)}, u32[]{:S(2)}, u32[]{:S(2)}) collective-permute-start(bf16[48,3072]{1,0:T(8,128)(2,1)} %refs_0_.1), channel_id=1, source_target_pairs={{0,64},{32,96},{64,0},{96,32},{128,192},{160,224},{192,128},{224,1... | collective-permute-start | bytes 884744 | tf_op jit(solution)/shard_map/ppermute | solution.py:35
  11.1 1.0 copy-start.2
  18.0 12.7 %collective-permute-start.2 = (bf16[96,3072]{1,0:T(8,128)(2,1)S(1)}, bf16[96,3072]{1,0:T(8,128)(2,1)}, u32[]{:S(2)}, u32[]{:S(2)}) collective-permute-start(bf16[96,3072]{1,0:T(8,128)(2,1)S(1)} %join.4.refs_0_), channel_id=1, source_target_pairs={{0,128},{32,160},{64,192},{96,224},{128,256},{160,288},{192,320},{... | collective-permute-start | bytes 1769480 | tf_op jit(solution)/shard_map/ppermute | solution.py:35
  21.7 11.2 %collective-permute-start.5 = (bf16[96,3072]{1,0:T(8,128)(2,1)}, bf16[96,3072]{1,0:T(8,128)(2,1)}, u32[]{:S(2)}, u32[]{:S(2)}) collective-permute-start(bf16[96,3072]{1,0:T(8,128)(2,1)} %join.5.refs_1_), channel_id=1, source_target_pairs={{0,384},{32,416},{64,448},{96,480},{128,0},{160,32},{192,64},{224,... | collective-permute-start | bytes 1769480 | tf_op jit(solution)/shard_map/ppermute | solution.py:35
  25.4 16.0 %collective-permute-start.7 = (bf16[96,3072]{1,0:T(8,128)(2,1)S(1)}, bf16[96,3072]{1,0:T(8,128)(2,1)}, u32[]{:S(2)}, u32[]{:S(2)}) collective-permute-start(bf16[96,3072]{1,0:T(8,128)(2,1)S(1)} %join.4.refs_0_), channel_id=1, source_target_pairs={{0,384},{32,416},{64,448},{96,480},{128,0},{160,32},{192,64},{224,... | collective-permute-start | bytes 1769480 | tf_op jit(solution)/shard_map/ppermute | solution.py:35
  28.3 13.1 %collective-permute-start.8 = (bf16[96,3072]{1,0:T(8,128)(2,1)}, bf16[96,3072]{1,0:T(8,128)(2,1)}, u32[]{:S(2)}, u32[]{:S(2)}) collective-permute-start(bf16[96,3072]{1,0:T(8,128)(2,1)} %join.5.refs_1_), channel_id=1, source_target_pairs={{0,128},{32,160},{64,192},{96,224},{128,256},{160,288},{192,320},{... | collective-permute-start | bytes 1769480 | tf_op jit(solution)/shard_map/ppermute | solution.py:35
  30.7 16.3 %collective-permute-start.3 = (bf16[96,3072]{1,0:T(8,128)(2,1)}, bf16[96,3072]{1,0:T(8,128)(2,1)}, u32[]{:S(2)}, u32[]{:S(2)}) collective-permute-start(bf16[96,3072]{1,0:T(8,128)(2,1)} %collective-permute-done.2.refs_2_), channel_id=1, source_target_pairs={{0,128},{32,160},{64,192},{96,224},{128,256},{160,288},{192,320},{... | collective-permute-start | bytes 1769480 | tf_op jit(solution)/shard_map/ppermute | solution.py:35
  32.9 14.1 %collective-permute-start.6 = (bf16[96,3072]{1,0:T(8,128)(2,1)}, bf16[96,3072]{1,0:T(8,128)(2,1)}, u32[]{:S(2)}, u32[]{:S(2)}) collective-permute-start(bf16[96,3072]{1,0:T(8,128)(2,1)} %collective-permute-done.5.refs_3_), channel_id=1, source_target_pairs={{0,384},{32,416},{64,448},{96,480},{128,0},{160,32},{192,64},{224,... | collective-permute-start | bytes 1769480 | tf_op jit(solution)/shard_map/ppermute | solution.py:35
  47.1 24.3 %copy-start.3 = (s32[1,192]{1,0:T(1,128)S(1)}, s32[1,192]{1,0:T(1,128)}, u32[]{:S(2)}) copy-start(s32[1,192]{1,0:T(1,128)} %param.11) | copy-start | bytes 2308
  49.9 16.8 %collective-permute-start.10 = (bf16[768,256]{1,0:T(8,128)(2,1)}, bf16[768,256]{1,0:T(8,128)(2,1)S(1)}, u32[]{:S(2)}, u32[]{:S(2)}) collective-permute-start(bf16[768,256]{1,0:T(8,128)(2,1)} %get-tuple-element.45), channel_id=1, source_target_pairs={{0,1},{1,0},{2,3},{3,2},{4,5},{5,4},{6,7},{7,6},{8,9},{9,8},{10,11... | collective-permute-start | bytes 1179656 | tf_op jit(solution)/shard_map/ppermute | solution.py:66
  55.6 16.1 %collective-permute-start.9 = (bf16[768,256]{1,0:T(8,128)(2,1)}, bf16[768,256]{1,0:T(8,128)(2,1)S(1)}, u32[]{:S(2)}, u32[]{:S(2)}) collective-permute-start(bf16[768,256]{1,0:T(8,128)(2,1)} %get-tuple-element.45), channel_id=1, source_target_pairs={{0,2},{1,31},{2,4},{3,1},{4,6},{5,3},{6,8},{7,5},{8,10},{9,7},{10,... | collective-permute-start | bytes 1179656 | tf_op jit(solution)/shard_map/ppermute | solution.py:76
  66.8 9.9 %collective-permute-start.13 = (bf16[768,256]{1,0:T(8,128)(2,1)S(1)}, bf16[768,256]{1,0:T(8,128)(2,1)S(1)}, u32[]{:S(2)}, u32[]{:S(2)}) collective-permute-start(bf16[768,256]{1,0:T(8,128)(2,1)S(1)} %collective-permute-done.10), channel_id=1, source_target_pairs={{0,2},{1,31},{2,4},{3,1},{4,6},{5,3},{6,8},{7,5},{8,10},{9,7},{10,... | collective-permute-start | bytes 1179656 | tf_op jit(solution)/shard_map/ppermute | solution.py:76
  69.4 3.3 %collective-permute-start.11 = (bf16[768,128]{1,0:T(8,128)(2,1)S(1)}, bf16[768,128]{1,0:T(8,128)(2,1)S(1)}, u32[]{:S(2)}, u32[]{:S(2)}) collective-permute-start(bf16[768,128]{1,0:T(8,128)(2,1)S(1)} %get-tuple-element.47), channel_id=1, source_target_pairs={{0,1},{1,0},{2,3},{3,2},{4,5},{5,4},{6,7},{7,6},{8,9},{9,8},{10,11... | collective-permute-start | bytes 589832 | tf_op jit(solution)/shard_map/ppermute | solution.py:66
  72.7 11.1 %collective-permute-start.12 = (bf16[768,256]{1,0:T(8,128)(2,1)S(1)}, bf16[768,256]{1,0:T(8,128)(2,1)S(1)}, u32[]{:S(2)}, u32[]{:S(2)}) collective-permute-start(bf16[768,256]{1,0:T(8,128)(2,1)S(1)} %collective-permute-done.9), channel_id=1, source_target_pairs={{0,2},{1,31},{2,4},{3,1},{4,6},{5,3},{6,8},{7,5},{8,10},{9,7},{10,... | collective-permute-start | bytes 1179656 | tf_op jit(solution)/shard_map/ppermute | solution.py:76
  76.7 9.7 %collective-permute-start.14 = (bf16[768,256]{1,0:T(8,128)(2,1)S(1)}, bf16[768,256]{1,0:T(8,128)(2,1)S(1)}, u32[]{:S(2)}, u32[]{:S(2)}) collective-permute-start(bf16[768,256]{1,0:T(8,128)(2,1)S(1)} %collective-permute-done.13), channel_id=1, source_target_pairs={{0,2},{1,31},{2,4},{3,1},{4,6},{5,3},{6,8},{7,5},{8,10},{9,7},{10,... | collective-permute-start | bytes 1179656 | tf_op jit(solution)/shard_map/ppermute | solution.py:76
  83.8 10.5 %collective-permute-start.15 = (bf16[768,256]{1,0:T(8,128)(2,1)S(1)}, bf16[768,256]{1,0:T(8,128)(2,1)S(1)}, u32[]{:S(2)}, u32[]{:S(2)}) collective-permute-start(bf16[768,256]{1,0:T(8,128)(2,1)S(1)} %collective-permute-done.12), channel_id=1, source_target_pairs={{0,2},{1,31},{2,4},{3,1},{4,6},{5,3},{6,8},{7,5},{8,10},{9,7},{10,... | collective-permute-start | bytes 1179656 | tf_op jit(solution)/shard_map/ppermute | solution.py:76
  86.4 10.4 %collective-permute-start.17 = (bf16[768,256]{1,0:T(8,128)(2,1)S(1)}, bf16[768,256]{1,0:T(8,128)(2,1)S(1)}, u32[]{:S(2)}, u32[]{:S(2)}) collective-permute-start(bf16[768,256]{1,0:T(8,128)(2,1)S(1)} %collective-permute-done.14), channel_id=1, source_target_pairs={{0,2},{1,31},{2,4},{3,1},{4,6},{5,3},{6,8},{7,5},{8,10},{9,7},{10,... | collective-permute-start | bytes 1179656 | tf_op jit(solution)/shard_map/ppermute | solution.py:76
  94.3 8.8 %collective-permute-start.16 = (bf16[768,256]{1,0:T(8,128)(2,1)S(1)}, bf16[768,256]{1,0:T(8,128)(2,1)S(1)}, u32[]{:S(2)}, u32[]{:S(2)}) collective-permute-start(bf16[768,256]{1,0:T(8,128)(2,1)S(1)} %collective-permute-done.15), channel_id=1, source_target_pairs={{0,2},{1,31},{2,4},{3,1},{4,6},{5,3},{6,8},{7,5},{8,10},{9,7},{10,... | collective-permute-start | bytes 1179656 | tf_op jit(solution)/shard_map/ppermute | solution.py:76
  96.8 10.5 %collective-permute-start.19 = (bf16[768,256]{1,0:T(8,128)(2,1)S(1)}, bf16[768,256]{1,0:T(8,128)(2,1)S(1)}, u32[]{:S(2)}, u32[]{:S(2)}) collective-permute-start(bf16[768,256]{1,0:T(8,128)(2,1)S(1)} %collective-permute-done.17), channel_id=1, source_target_pairs={{0,2},{1,31},{2,4},{3,1},{4,6},{5,3},{6,8},{7,5},{8,10},{9,7},{10,... | collective-permute-start | bytes 1179656 | tf_op jit(solution)/shard_map/ppermute | solution.py:76
  103.1 9.5 %collective-permute-start.18 = (bf16[768,256]{1,0:T(8,128)(2,1)S(1)}, bf16[768,256]{1,0:T(8,128)(2,1)S(1)}, u32[]{:S(2)}, u32[]{:S(2)}) collective-permute-start(bf16[768,256]{1,0:T(8,128)(2,1)S(1)} %collective-permute-done.16), channel_id=1, source_target_pairs={{0,2},{1,31},{2,4},{3,1},{4,6},{5,3},{6,8},{7,5},{8,10},{9,7},{10,... | collective-permute-start | bytes 1179656 | tf_op jit(solution)/shard_map/ppermute | solution.py:76
  107.3 8.8 %collective-permute-start.21 = (bf16[768,256]{1,0:T(8,128)(2,1)S(1)}, bf16[768,256]{1,0:T(8,128)(2,1)S(1)}, u32[]{:S(2)}, u32[]{:S(2)}) collective-permute-start(bf16[768,256]{1,0:T(8,128)(2,1)S(1)} %collective-permute-done.19), channel_id=1, source_target_pairs={{0,2},{1,31},{2,4},{3,1},{4,6},{5,3},{6,8},{7,5},{8,10},{9,7},{10,... | collective-permute-start | bytes 1179656 | tf_op jit(solution)/shard_map/ppermute | solution.py:76
  112.6 9.2 %collective-permute-start.20 = (bf16[768,256]{1,0:T(8,128)(2,1)S(1)}, bf16[768,256]{1,0:T(8,128)(2,1)S(1)}, u32[]{:S(2)}, u32[]{:S(2)}) collective-permute-start(bf16[768,256]{1,0:T(8,128)(2,1)S(1)} %collective-permute-done.18), channel_id=1, source_target_pairs={{0,2},{1,31},{2,4},{3,1},{4,6},{5,3},{6,8},{7,5},{8,10},{9,7},{10,... | collective-permute-start | bytes 1179656 | tf_op jit(solution)/shard_map/ppermute | solution.py:76
  116.1 9.5 %collective-permute-start.23 = (bf16[768,256]{1,0:T(8,128)(2,1)S(1)}, bf16[768,256]{1,0:T(8,128)(2,1)S(1)}, u32[]{:S(2)}, u32[]{:S(2)}) collective-permute-start(bf16[768,256]{1,0:T(8,128)(2,1)S(1)} %collective-permute-done.21), channel_id=1, source_target_pairs={{0,2},{1,31},{2,4},{3,1},{4,6},{5,3},{6,8},{7,5},{8,10},{9,7},{10,... | collective-permute-start | bytes 1179656 | tf_op jit(solution)/shard_map/ppermute | solution.py:76
  121.8 10.2 %collective-permute-start.22 = (bf16[768,256]{1,0:T(8,128)(2,1)S(1)}, bf16[768,256]{1,0:T(8,128)(2,1)S(1)}, u32[]{:S(2)}, u32[]{:S(2)}) collective-permute-start(bf16[768,256]{1,0:T(8,128)(2,1)S(1)} %collective-permute-done.20), channel_id=1, source_target_pairs={{0,2},{1,31},{2,4},{3,1},{4,6},{5,3},{6,8},{7,5},{8,10},{9,7},{10,... | collective-permute-start | bytes 1179656 | tf_op jit(solution)/shard_map/ppermute | solution.py:76
  125.6 9.5 %collective-permute-start.25 = (bf16[768,256]{1,0:T(8,128)(2,1)S(1)}, bf16[768,256]{1,0:T(8,128)(2,1)S(1)}, u32[]{:S(2)}, u32[]{:S(2)}) collective-permute-start(bf16[768,256]{1,0:T(8,128)(2,1)S(1)} %collective-permute-done.23), channel_id=1, source_target_pairs={{0,2},{1,31},{2,4},{3,1},{4,6},{5,3},{6,8},{7,5},{8,10},{9,7},{10,... | collective-permute-start | bytes 1179656 | tf_op jit(solution)/shard_map/ppermute | solution.py:76
  132.0 9.2 %collective-permute-start.24 = (bf16[768,256]{1,0:T(8,128)(2,1)S(1)}, bf16[768,256]{1,0:T(8,128)(2,1)S(1)}, u32[]{:S(2)}, u32[]{:S(2)}) collective-permute-start(bf16[768,256]{1,0:T(8,128)(2,1)S(1)} %collective-permute-done.22), channel_id=1, source_target_pairs={{1,31},{3,1},{5,3},{7,5},{9,7},{11,9},{13,11},{15,13},{17,15},{19,... | collective-permute-start | bytes 1179656 | tf_op jit(solution)/shard_map/ppermute | solution.py:76
  135.1 9.7 %collective-permute-start.26 = (bf16[768,256]{1,0:T(8,128)(2,1)S(1)}, bf16[768,256]{1,0:T(8,128)(2,1)S(1)}, u32[]{:S(2)}, u32[]{:S(2)}) collective-permute-start(bf16[768,256]{1,0:T(8,128)(2,1)S(1)} %collective-permute-done.25), channel_id=1, source_target_pairs={{1,31},{3,1},{5,3},{7,5},{9,7},{11,9},{13,11},{15,13},{17,15},{19,... | collective-permute-start | bytes 1179656 | tf_op jit(solution)/shard_map/ppermute | solution.py:76
  146.2 4.2 %collective-permute-start.27 = (f32[6,128,256]{2,1,0:T(8,128)S(1)}, f32[6,128,256]{2,1,0:T(8,128)S(1)}, u32[]{:S(2)}, u32[]{:S(2)}) collective-permute-start(f32[6,128,256]{2,1,0:T(8,128)S(1)} %attend.15), channel_id=1, source_target_pairs={{0,1},{1,0},{2,3},{3,2},{4,5},{5,4},{6,7},{7,6},{8,9},{9,8},{10,11... | collective-permute-start | bytes 2359304 | tf_op jit(solution)/shard_map/ppermute | solution.py:66

commit v15 on v14

--- a/solution.py
+++ b/solution.py
@@ -11,8 +11,8 @@
 PIECE = 48
 PLANES = 16
 UNROLL = 8
-CALLS = ((0, 3, None),) + tuple((step, step + 1, None) for step in range(3, 8))
-CALLS += ((8, 9, "other"), (8, 9, "own"))
+CALLS = ((0, 3, None, None),) + tuple((step, step + 1, None, None) for step in range(3, 8))
+CALLS += ((8, 9, None, "same"), (8, 9, "other", "other"), (8, 9, "own", "other"))
 LOG2E = 1.4426950408889634
 MESH_AXES = ("seq", "bal")
 VMEM = pl.BlockSpec(memory_space=pltpu.VMEM)
@@ -231,10 +231,13 @@
     nothing = rows * TILE
     totals = []
     theirs = jnp.where(column >= slots, 1 - core, core)
-    for call, (start, stop, part) in enumerate(calls):
+    crossed = jnp.where(same, 0, 1)
+    for call, (start, stop, part, kind) in enumerate(calls):
         here = inside & (away >= start) & (away < stop)
         if part is not None:
             here = here & (theirs == (0 if part == "own" else 1))
+        if kind is not None:
+            here = here & (crossed == (0 if kind == "same" else 1))
         held = jnp.where(here, 1.0, 0.0)
         total = jnp.sum(held, axis=0, keepdims=True)
         order = jnp.dot(before, held, preferred_element_type=jnp.float32)
@@ -242,7 +245,7 @@
             jnp.broadcast_to(total, (8, rows)), ahead, preferred_element_type=jnp.float32
         )[:1]
         order = jnp.where(held > 0.0, order, -1.0).astype(jnp.int32)
-        skip = stop - start - max(start, 1)
+        skip = stop - start - max(start, 1) if kind is None else -start
         block = jnp.where(same, away - start, away + skip)
         pair = column * TILE + block * slots + tile - bal * slots - nothing
         room = call_room(start, stop, slots)
@@ -260,7 +263,7 @@
     rows = 2 * slots
     tiles = lax.dynamic_slice_in_dim(key_tiles.T, place[5] * rows, rows, 1)
     counts = lax.dynamic_slice_in_dim(key_counts, place[5] * rows, rows, 1)
-    room = max(call_room(start, stop, slots) for start, stop, _ in calls)
+    room = max(call_room(start, stop, slots) for start, stop, _, _ in calls)
     return pl.pallas_call(
         functools.partial(list_kernel, slots, calls),
         out_shape=(
@@ -269,7 +272,7 @@
         ),
         in_specs=[SMEM, VMEM, VMEM],
         out_specs=(VMEM, VMEM),
-        compiler_params=pltpu.CompilerParams(vmem_limit_bytes=12 * 1024 * 1024),
+        compiler_params=pltpu.CompilerParams(vmem_limit_bytes=16 * 1024 * 1024),
         name="lists",
     )(place, tiles, counts)
 
@@ -352,14 +355,19 @@
             high_queries = jnp.where(core == 0, other_queries, queries)
             chip_queries = tiles(jnp.concatenate((low_queries, high_queries), axis=0))
             other[2], chip_queries = lax.optimization_barrier((other[2], chip_queries))
-        call = step - CALLS[0][1] + 1
-        if call >= 0:
-            start, stop, part = CALLS[call]
-            blocks = [tiles(block) for block in same[start:stop] + other[max(start, 1) : stop]]
+        for call, (start, stop, part, kind) in enumerate(CALLS):
+            if stop != step + 1:
+                continue
+            blocks = [] if kind == "other" else same[start:stop]
+            blocks = blocks + ([] if kind == "same" else other[max(start, 1) : stop])
+            blocks = [tiles(block) for block in blocks]
+            done = attend(call, place, pairs, counts, chip_queries, blocks, sums)
             if part is None:
-                sums = attend(call, place, pairs, counts, chip_queries, blocks, sums)
-    given = swap_cores(attend(call, place, pairs, counts, chip_queries, blocks, sums))
-    kept = attend(call + 1, place, pairs, counts, chip_queries, blocks, sums)
+                sums = done
+            elif part == "other":
+                given = swap_cores(done)
+            else:
+                kept = done
     sums = kept + given
     result = (sums[:, :, :HEAD] / sums[:, :, HEAD:]).astype(jnp.bfloat16)
     return lax.all_to_all(

time: 163 us -> 163 us (level)
  Pallas kernels: 30.3 us -> 34.1 us
  waiting for transfers between devices: 17.5 us -> 14.7 us
    pallas_call x8 -> x9, Pallas kernels: 17.2 us -> 20.9 us  [attend(): pl.pallas_call(functools.partial(attend_kernel, scale, call, part, blocks...]
    ppermute x16, waiting for transfers between devices: 7.39 us -> 5.15 us  [pass_on(): return lax.ppermute(block, 'bal', pairs)]
    ppermute x3, starting transfers between devices: 9.55 us -> 11.3 us  [swap_cores(): return lax.ppermute(block, 'bal', [(at, at ^ 1) for at in range(32)])]
  transfers between devices with their start and end apart: 28 -> 28, of which waited for: 12 -> 13; matrix products, arithmetic and copies ran while one was open for 1% -> 1% of each run, Pallas kernels for 16% -> 18%
where the time goes in v15:
time: 163 us; the launch traced here: 162 us
  starting transfers between devices  100 us (61%)
  Pallas kernels  34.1 us (21%)
  waiting for transfers between devices  14.7 us (9%)
  blocking collectives  9.92 us (6%)
  local copies, waits for them, and re-layouts  1.91 us (1%)
    ppermute x16, starting transfers between devices, pass_on(): return lax.ppermute(block, 'bal', pairs)  59.7 us
    ppermute x9, starting transfers between devices, send(): return lax.ppermute(block, MESH_AXES, plane_perm(phase, shift))  29.3 us
    pallas_call x9, Pallas kernels, attend(): pl.pallas_call(functools.partial(attend_kernel, scale, call, part, blocks...  20.9 us
    ppermute x3, starting transfers between devices, swap_cores(): return lax.ppermute(block, 'bal', [(at, at ^ 1) for at in range(32)])  11.3 us
    all_to_all x1, blocking collectives, on_device(): lax.all_to_all(result.reshape(slots * TILE, HEAD), 'seq', split_axis=0, c...  9.92 us
    pallas_call x3, Pallas kernels, project(): pl.pallas_call(functools.partial(project_kernel, shares), out_shape=(jax....  9.37 us
    ppermute x9, waiting for transfers between devices, send(): return lax.ppermute(block, MESH_AXES, plane_perm(phase, shift))  8.27 us
    ppermute x16, waiting for transfers between devices, pass_on(): return lax.ppermute(block, 'bal', pairs)  5.15 us
  transfers between devices with their start and end apart: 28, of which 13 were waited for; matrix products, arithmetic and copies ran while one was open for 1% of the time, Pallas kernels for 18%

profile of v15, /device:TPU:1, one launch (start us, length us, event | category | flops | bytes accessed | tf_op | source)
XLA Modules:
  0.0 162.4 jit_solution(1689292746396131660)
XLA Ops:
  0.0 5.6 %collective-permute-start.1 = (bf16[48,3072]{1,0:T(8,128)(2,1)}, bf16[48,3072]{1,0:T(8,128)(2,1)S(1)}, u32[]{:S(2)}, u32[]{:S(2)}) collective-permute-start(bf16[48,3072]{1,0:T(8,128)(2,1)} %refs_0_.1), channel_id=1, source_target_pairs={{0,96},{32,0},{64,32},{96,64},{128,224},{160,128},{192,160},{224,1... | collective-permute-start | bytes 884744 | tf_op jit(solution)/shard_map/ppermute | solution.py:35
  5.6 1.9 %collective-permute-start = (bf16[48,3072]{1,0:T(8,128)(2,1)}, bf16[48,3072]{1,0:T(8,128)(2,1)S(1)}, u32[]{:S(2)}, u32[]{:S(2)}) collective-permute-start(bf16[48,3072]{1,0:T(8,128)(2,1)} %refs_0_.1), channel_id=1, source_target_pairs={{0,32},{32,64},{64,96},{96,0},{128,160},{160,192},{192,224},{224,1... | collective-permute-start | bytes 884744 | tf_op jit(solution)/shard_map/ppermute | solution.py:35
  7.5 3.5 %collective-permute-start.4 = (bf16[48,3072]{1,0:T(8,128)(2,1)}, bf16[48,3072]{1,0:T(8,128)(2,1)S(1)}, u32[]{:S(2)}, u32[]{:S(2)}) collective-permute-start(bf16[48,3072]{1,0:T(8,128)(2,1)} %refs_0_.1), channel_id=1, source_target_pairs={{0,64},{32,96},{64,0},{96,32},{128,192},{160,224},{192,128},{224,1... | collective-permute-start | bytes 884744 | tf_op jit(solution)/shard_map/ppermute | solution.py:35
  11.1 1.0 copy-done.2
  12.1 0.7 pad_maximum_fusion.1.refs_5_.refs_3_
  12.8 5.1 %collective-permute-done.refs_0_ = bf16[48,3072]{1,0:T(8,128)(2,1)S(1)} collective-permute-done((bf16[48,3072]{1,0:T(8,128)(2,1)}, bf16[48,3072]{1,0:T(8,128)(2,1)S(1)}, u32[]{:S(2)}, u32[]{:S(2)}) %collective-permute-start) | collective-permute-done | bytes 294944 | tf_op jit(solution)/shard_map/ppermute | solution.py:35
  17.9 0.1 join.4.refs_0_
  18.0 2.8 %collective-permute-start.2 = (bf16[96,3072]{1,0:T(8,128)(2,1)S(1)}, bf16[96,3072]{1,0:T(8,128)(2,1)}, u32[]{:S(2)}, u32[]{:S(2)}) collective-permute-start(bf16[96,3072]{1,0:T(8,128)(2,1)S(1)} %join.4.refs_0_), channel_id=1, source_target_pairs={{0,128},{32,160},{64,192},{96,224},{128,256},{160,288},{192,320},{... | collective-permute-start | bytes 1769480 | tf_op jit(solution)/shard_map/ppermute | solution.py:35
  20.9 0.8 join.5.refs_1_
  21.7 3.7 %collective-permute-start.5 = (bf16[96,3072]{1,0:T(8,128)(2,1)}, bf16[96,3072]{1,0:T(8,128)(2,1)}, u32[]{:S(2)}, u32[]{:S(2)}) collective-permute-start(bf16[96,3072]{1,0:T(8,128)(2,1)} %join.5.refs_1_), channel_id=1, source_target_pairs={{0,384},{32,416},{64,448},{96,480},{128,0},{160,32},{192,64},{224,... | collective-permute-start | bytes 1769480 | tf_op jit(solution)/shard_map/ppermute | solution.py:35
  25.4 2.9 %collective-permute-start.7 = (bf16[96,3072]{1,0:T(8,128)(2,1)S(1)}, bf16[96,3072]{1,0:T(8,128)(2,1)}, u32[]{:S(2)}, u32[]{:S(2)}) collective-permute-start(bf16[96,3072]{1,0:T(8,128)(2,1)S(1)} %join.4.refs_0_), channel_id=1, source_target_pairs={{0,384},{32,416},{64,448},{96,480},{128,0},{160,32},{192,64},{224,... | collective-permute-start | bytes 1769480 | tf_op jit(solution)/shard_map/ppermute | solution.py:35
  28.3 2.4 %collective-permute-start.8 = (bf16[96,3072]{1,0:T(8,128)(2,1)}, bf16[96,3072]{1,0:T(8,128)(2,1)}, u32[]{:S(2)}, u32[]{:S(2)}) collective-permute-start(bf16[96,3072]{1,0:T(8,128)(2,1)} %join.5.refs_1_), channel_id=1, source_target_pairs={{0,128},{32,160},{64,192},{96,224},{128,256},{160,288},{192,320},{... | collective-permute-start | bytes 1769480 | tf_op jit(solution)/shard_map/ppermute | solution.py:35
  30.7 1.9 %collective-permute-start.3 = (bf16[96,3072]{1,0:T(8,128)(2,1)}, bf16[96,3072]{1,0:T(8,128)(2,1)}, u32[]{:S(2)}, u32[]{:S(2)}) collective-permute-start(bf16[96,3072]{1,0:T(8,128)(2,1)} %collective-permute-done.2.refs_2_), channel_id=1, source_target_pairs={{0,128},{32,160},{64,192},{96,224},{128,256},{160,288},{192,320},{... | collective-permute-start | bytes 1769480 | tf_op jit(solution)/shard_map/ppermute | solution.py:35
  32.6 0.3 collective-permute-done.5.refs_3_
  32.9 4.6 %collective-permute-start.6 = (bf16[96,3072]{1,0:T(8,128)(2,1)}, bf16[96,3072]{1,0:T(8,128)(2,1)}, u32[]{:S(2)}, u32[]{:S(2)}) collective-permute-start(bf16[96,3072]{1,0:T(8,128)(2,1)} %collective-permute-done.5.refs_3_), channel_id=1, source_target_pairs={{0,384},{32,416},{64,448},{96,480},{128,0},{160,32},{192,64},{224,... | collective-permute-start | bytes 1769480 | tf_op jit(solution)/shard_map/ppermute | solution.py:35
  37.6 0.1 stack.27.place
  37.7 3.7 %project.3 = (bf16[768,128]{1,0:T(8,128)(2,1)S(1)}, bf16[768,256]{1,0:T(8,128)(2,1)}) custom-call(s32[6]{0:T(128)S(1)} %stack.27.place, bf16[96,3072]{1,0:T(8,128)(2,1)S(1)} %join.4.refs_0_, bf16[96,3072]{1,0:T(8,128)(2,1)} %join.5.refs_1_, bf16[96,3072]{1,0:T(8,128)(2,1)} %collective-permute-done.2.refs_2_, ...), custom_call_target="tpu_custom_call" | custom-call | tf_op jit(solution)/shard_map/project/pallas_call | solution.py:117
  41.4 2.8 %project.4 = (bf16[768,128]{1,0:T(8,128)(2,1)S(1)}, bf16[768,256]{1,0:T(8,128)(2,1)}) custom-call(s32[6]{0:T(128)S(1)} %stack.27.place, bf16[96,3072]{1,0:T(8,128)(2,1)} %collective-permute-done.7.refs_0_, bf16[96,3072]{1,0:T(8,128)(2,1)} %collective-permute-done.8.refs_1_, ...), custom_call_target="tpu_custom_call", output_to_operand_aliasing={{0}: (5, {}), {1}: (6, {})} | custom-call | tf_op jit(solution)/shard_map/project/pallas_call | solution.py:117
  44.2 2.8 %collective-permute-done.3.refs_0_ = bf16[96,3072]{1,0:T(8,128)(2,1)} collective-permute-done((bf16[96,3072]{1,0:T(8,128)(2,1)}, bf16[96,3072]{1,0:T(8,128)(2,1)}, u32[]{:S(2)}, u32[]{:S(2)}) %collective-permute-start.3) | collective-permute-done | bytes 589856 | tf_op jit(solution)/shard_map/ppermute | solution.py:35
  47.1 2.8 %project.5 = (bf16[768,128]{1,0:T(8,128)(2,1)S(1)}, bf16[768,256]{1,0:T(8,128)(2,1)}) custom-call(s32[6]{0:T(128)S(1)} %stack.27.place, bf16[96,3072]{1,0:T(8,128)(2,1)} %collective-permute-done.3.refs_0_, bf16[96,3072]{1,0:T(8,128)(2,1)} %collective-permute-done.6.refs_1_, ...), custom_call_target="tpu_custom_call", output_to_operand_aliasing={{0}: (5, {}), {1}: (6, {})} | custom-call | tf_op jit(solution)/shard_map/project/pallas_call | solution.py:117
  49.9 5.7 %collective-permute-start.10 = (bf16[768,256]{1,0:T(8,128)(2,1)}, bf16[768,256]{1,0:T(8,128)(2,1)S(1)}, u32[]{:S(2)}, u32[]{:S(2)}) collective-permute-start(bf16[768,256]{1,0:T(8,128)(2,1)} %get-tuple-element.45), channel_id=1, source_target_pairs={{0,1},{1,0},{2,3},{3,2},{4,5},{5,4},{6,7},{7,6},{8,9},{9,8},{10,11... | collective-permute-start | bytes 1179656 | tf_op jit(solution)/shard_map/ppermute | solution.py:66
  55.6 11.1 %collective-permute-start.9 = (bf16[768,256]{1,0:T(8,128)(2,1)}, bf16[768,256]{1,0:T(8,128)(2,1)S(1)}, u32[]{:S(2)}, u32[]{:S(2)}) collective-permute-start(bf16[768,256]{1,0:T(8,128)(2,1)} %get-tuple-element.45), channel_id=1, source_target_pairs={{0,2},{1,31},{2,4},{3,1},{4,6},{5,3},{6,8},{7,5},{8,10},{9,7},{10,... | collective-permute-start | bytes 1179656 | tf_op jit(solution)/shard_map/ppermute | solution.py:76
  66.8 2.6 %collective-permute-start.13 = (bf16[768,256]{1,0:T(8,128)(2,1)S(1)}, bf16[768,256]{1,0:T(8,128)(2,1)S(1)}, u32[]{:S(2)}, u32[]{:S(2)}) collective-permute-start(bf16[768,256]{1,0:T(8,128)(2,1)S(1)} %collective-permute-done.10), channel_id=1, source_target_pairs={{0,2},{1,31},{2,4},{3,1},{4,6},{5,3},{6,8},{7,5},{8,10},{9,7},{10,... | collective-permute-start | bytes 1179656 | tf_op jit(solution)/shard_map/ppermute | solution.py:76
  69.4 1.9 %collective-permute-start.11 = (bf16[768,128]{1,0:T(8,128)(2,1)S(1)}, bf16[768,128]{1,0:T(8,128)(2,1)S(1)}, u32[]{:S(2)}, u32[]{:S(2)}) collective-permute-start(bf16[768,128]{1,0:T(8,128)(2,1)S(1)} %get-tuple-element.47), channel_id=1, source_target_pairs={{0,1},{1,0},{2,3},{3,2},{4,5},{5,4},{6,7},{7,6},{8,9},{9,8},{10,11... | collective-permute-start | bytes 589832 | tf_op jit(solution)/shard_map/ppermute | solution.py:66
  71.3 0.1 constant_dynamic-slice_fusion.counts
  71.4 0.3 collective-permute-done.9
  71.8 1.0 collective-permute-done.11
  72.7 3.9 %collective-permute-start.12 = (bf16[768,256]{1,0:T(8,128)(2,1)S(1)}, bf16[768,256]{1,0:T(8,128)(2,1)S(1)}, u32[]{:S(2)}, u32[]{:S(2)}) collective-permute-start(bf16[768,256]{1,0:T(8,128)(2,1)S(1)} %collective-permute-done.9), channel_id=1, source_target_pairs={{0,2},{1,31},{2,4},{3,1},{4,6},{5,3},{6,8},{7,5},{8,10},{9,7},{10,... | collective-permute-start | bytes 1179656 | tf_op jit(solution)/shard_map/ppermute | solution.py:76
  76.7 4.2 %collective-permute-start.14 = (bf16[768,256]{1,0:T(8,128)(2,1)S(1)}, bf16[768,256]{1,0:T(8,128)(2,1)S(1)}, u32[]{:S(2)}, u32[]{:S(2)}) collective-permute-start(bf16[768,256]{1,0:T(8,128)(2,1)S(1)} %collective-permute-done.13), channel_id=1, source_target_pairs={{0,2},{1,31},{2,4},{3,1},{4,6},{5,3},{6,8},{7,5},{8,10},{9,7},{10,... | collective-permute-start | bytes 1179656 | tf_op jit(solution)/shard_map/ppermute | solution.py:76
  81.0 0.1 dynamic-slice_bitcast_fusion.tiles
  81.1 2.9 %lists.1 = (s32[9,384]{1,0:T(8,128)S(1)}, s32[1,9]{1,0:T(1,128)S(1)}) custom-call(s32[6]{0:T(128)S(1)} %stack.27.place, s32[64,12]{1,0:T(8,128)S(1)} %dynamic-slice_bitcast_fusion.tiles, s32[1,12]{1,0:T(1,128)S(1)} %constant_dynamic-slice_fusion.counts), custom_call_target="tpu_custom_call" | custom-call | tf_op jit(solution)/shard_map/lists/pallas_call | solution.py:267
  83.9 2.5 %collective-permute-start.21 = (bf16[768,256]{1,0:T(8,128)(2,1)S(1)}, bf16[768,256]{1,0:T(8,128)(2,1)S(1)}, u32[]{:S(2)}, u32[]{:S(2)}) collective-permute-start(bf16[768,256]{1,0:T(8,128)(2,1)S(1)} %collective-permute-done.12), channel_id=1, source_target_pairs={{0,2},{1,31},{2,4},{3,1},{4,6},{5,3},{6,8},{7,5},{8,10},{9,7},{10,... | collective-permute-start | bytes 1179656 | tf_op jit(solution)/shard_map/ppermute | solution.py:76
  86.4 4.2 %collective-permute-start.15 = (bf16[768,256]{1,0:T(8,128)(2,1)S(1)}, bf16[768,256]{1,0:T(8,128)(2,1)S(1)}, u32[]{:S(2)}, u32[]{:S(2)}) collective-permute-start(bf16[768,256]{1,0:T(8,128)(2,1)S(1)} %collective-permute-done.14), channel_id=1, source_target_pairs={{0,2},{1,31},{2,4},{3,1},{4,6},{5,3},{6,8},{7,5},{8,10},{9,7},{10,... | collective-permute-start | bytes 1179656 | tf_op jit(solution)/shard_map/ppermute | solution.py:76
  90.6 3.6 %attend.9.refs_2_ = f32[13,128,256]{2,1,0:T(8,128)S(1)} custom-call(s32[6]{0:T(128)S(1)} %stack.27.place, s32[9,384]{1,0:T(8,128)S(1)} %get-tuple-element.52.pairs, s32[1,9]{1,0:T(1,128)S(1)} %get-tuple-element.53.counts, bf16[12,128,128]{2,1,0:T(8,128)(2,1)S(1)} %bitcast.41, bf16[6,128,256]{2,1,0:T(8,128)(2,1)} %bitcast.13.refs_0_, ...), custom_call_target="tpu_custom_call" | custom-call | flops 5000000000 | bytes 5000000 | tf_op jit(solution)/shard_map/attend/pallas_call | solution.py:192
  94.3 1.9 %collective-permute-start.22 = (bf16[768,256]{1,0:T(8,128)(2,1)S(1)}, bf16[768,256]{1,0:T(8,128)(2,1)S(1)}, u32[]{:S(2)}, u32[]{:S(2)}) collective-permute-start(bf16[768,256]{1,0:T(8,128)(2,1)S(1)} %collective-permute-done.21), channel_id=1, source_target_pairs={{0,2},{1,31},{2,4},{3,1},{4,6},{5,3},{6,8},{7,5},{8,10},{9,7},{10,... | collective-permute-start | bytes 1179656 | tf_op jit(solution)/shard_map/ppermute | solution.py:76
  96.2 0.8 collective-permute-done.15
  97.0 3.4 %collective-permute-start.16 = (bf16[768,256]{1,0:T(8,128)(2,1)S(1)}, bf16[768,256]{1,0:T(8,128)(2,1)S(1)}, u32[]{:S(2)}, u32[]{:S(2)}) collective-permute-start(bf16[768,256]{1,0:T(8,128)(2,1)S(1)} %collective-permute-done.15), channel_id=1, source_target_pairs={{0,2},{1,31},{2,4},{3,1},{4,6},{5,3},{6,8},{7,5},{8,10},{9,7},{10,... | collective-permute-start | bytes 1179656 | tf_op jit(solution)/shard_map/ppermute | solution.py:76
  100.3 2.6 %attend.10.refs_2_ = f32[13,128,256]{2,1,0:T(8,128)S(1)} custom-call(s32[6]{0:T(128)S(1)} %stack.27.place, s32[9,384]{1,0:T(8,128)S(1)} %get-tuple-element.52.pairs, s32[1,9]{1,0:T(1,128)S(1)} %get-tuple-element.53.counts, bf16[12,128,128]{2,1,0:T(8,128)(2,1)S(1)} %bitcast.42, bf16[6,128,256]{2,1,0:T(8,128)(2,1)S(1)} %bitcast.56, ...), custom_call_target="tpu_custom_call", output_to_operand_aliasing={{}: (6, {})} | custom-call | flops 2000000000 | bytes 2000000 | tf_op jit(solution)/shard_map/attend/pallas_call | solution.py:192
  103.0 0.1 collective-permute-done.22
  103.1 2.8 %collective-permute-start.23 = (bf16[768,256]{1,0:T(8,128)(2,1)S(1)}, bf16[768,256]{1,0:T(8,128)(2,1)S(1)}, u32[]{:S(2)}, u32[]{:S(2)}) collective-permute-start(bf16[768,256]{1,0:T(8,128)(2,1)S(1)} %collective-permute-done.22), channel_id=1, source_target_pairs={{0,2},{1,31},{2,4},{3,1},{4,6},{5,3},{6,8},{7,5},{8,10},{9,7},{10,... | collective-permute-start | bytes 1179656 | tf_op jit(solution)/shard_map/ppermute | solution.py:76
  105.9 1.4 collective-permute-done.16
  107.3 2.8 %collective-permute-start.17 = (bf16[768,256]{1,0:T(8,128)(2,1)S(1)}, bf16[768,256]{1,0:T(8,128)(2,1)S(1)}, u32[]{:S(2)}, u32[]{:S(2)}) collective-permute-start(bf16[768,256]{1,0:T(8,128)(2,1)S(1)} %collective-permute-done.16), channel_id=1, source_target_pairs={{0,2},{1,31},{2,4},{3,1},{4,6},{5,3},{6,8},{7,5},{8,10},{9,7},{10,... | collective-permute-start | bytes 1179656 | tf_op jit(solution)/shard_map/ppermute | solution.py:76
  110.1 2.6 %attend.11.refs_2_ = f32[13,128,256]{2,1,0:T(8,128)S(1)} custom-call(s32[6]{0:T(128)S(1)} %stack.27.place, s32[9,384]{1,0:T(8,128)S(1)} %get-tuple-element.52.pairs, s32[1,9]{1,0:T(1,128)S(1)} %get-tuple-element.53.counts, bf16[12,128,128]{2,1,0:T(8,128)(2,1)S(1)} %bitcast.43, bf16[6,128,256]{2,1,0:T(8,128)(2,1)S(1)} %bitcast.57, ...), custom_call_target="tpu_custom_call", output_to_operand_aliasing={{}: (6, {})} | custom-call | flops 2000000000 | bytes 2000000 | tf_op jit(solution)/shard_map/attend/pallas_call | solution.py:192
  112.8 2.8 %collective-permute-start.24 = (bf16[768,256]{1,0:T(8,128)(2,1)S(1)}, bf16[768,256]{1,0:T(8,128)(2,1)S(1)}, u32[]{:S(2)}, u32[]{:S(2)}) collective-permute-start(bf16[768,256]{1,0:T(8,128)(2,1)S(1)} %collective-permute-done.23), channel_id=1, source_target_pairs={{0,2},{1,31},{2,4},{3,1},{4,6},{5,3},{6,8},{7,5},{8,10},{9,7},{10,... | collective-permute-start | bytes 1179656 | tf_op jit(solution)/shard_map/ppermute | solution.py:76
  115.6 0.5 collective-permute-done.17
  116.1 3.7 %collective-permute-start.18 = (bf16[768,256]{1,0:T(8,128)(2,1)S(1)}, bf16[768,256]{1,0:T(8,128)(2,1)S(1)}, u32[]{:S(2)}, u32[]{:S(2)}) collective-permute-start(bf16[768,256]{1,0:T(8,128)(2,1)S(1)} %collective-permute-done.17), channel_id=1, source_target_pairs={{0,2},{1,31},{2,4},{3,1},{4,6},{5,3},{6,8},{7,5},{8,10},{9,7},{10,... | collective-permute-start | bytes 1179656 | tf_op jit(solution)/shard_map/ppermute | solution.py:76
  119.8 2.6 %attend.12.refs_2_ = f32[13,128,256]{2,1,0:T(8,128)S(1)} custom-call(s32[6]{0:T(128)S(1)} %stack.27.place, s32[9,384]{1,0:T(8,128)S(1)} %get-tuple-element.52.pairs, s32[1,9]{1,0:T(1,128)S(1)} %get-tuple-element.53.counts, bf16[12,128,128]{2,1,0:T(8,128)(2,1)S(1)} %bitcast.44, bf16[6,128,256]{2,1,0:T(8,128)(2,1)S(1)} %bitcast.59, ...), custom_call_target="tpu_custom_call", output_to_operand_aliasing={{}: (6, {})} | custom-call | flops 2000000000 | bytes 2000000 | tf_op jit(solution)/shard_map/attend/pallas_call | solution.py:192
  122.5 2.8 %collective-permute-start.25 = (bf16[768,256]{1,0:T(8,128)(2,1)S(1)}, bf16[768,256]{1,0:T(8,128)(2,1)S(1)}, u32[]{:S(2)}, u32[]{:S(2)}) collective-permute-start(bf16[768,256]{1,0:T(8,128)(2,1)S(1)} %collective-permute-done.24), channel_id=1, source_target_pairs={{0,2},{1,31},{2,4},{3,1},{4,6},{5,3},{6,8},{7,5},{8,10},{9,7},{10,... | collective-permute-start | bytes 1179656 | tf_op jit(solution)/shard_map/ppermute | solution.py:76
  125.3 0.5 collective-permute-done.18
  125.8 3.7 %collective-permute-start.19 = (bf16[768,256]{1,0:T(8,128)(2,1)S(1)}, bf16[768,256]{1,0:T(8,128)(2,1)S(1)}, u32[]{:S(2)}, u32[]{:S(2)}) collective-permute-start(bf16[768,256]{1,0:T(8,128)(2,1)S(1)} %collective-permute-done.18), channel_id=1, source_target_pairs={{0,2},{1,31},{2,4},{3,1},{4,6},{5,3},{6,8},{7,5},{8,10},{9,7},{10,... | collective-permute-start | bytes 1179656 | tf_op jit(solution)/shard_map/ppermute | solution.py:76
  129.6 2.2 %attend.13.refs_2_ = f32[13,128,256]{2,1,0:T(8,128)S(1)} custom-call(s32[6]{0:T(128)S(1)} %stack.27.place, s32[9,384]{1,0:T(8,128)S(1)} %get-tuple-element.52.pairs, s32[1,9]{1,0:T(1,128)S(1)} %get-tuple-element.53.counts, bf16[12,128,128]{2,1,0:T(8,128)(2,1)S(1)} %bitcast.45, bf16[6,128,256]{2,1,0:T(8,128)(2,1)S(1)} %bitcast.61, ...), custom_call_target="tpu_custom_call", output_to_operand_aliasing={{}: (6, {})} | custom-call | flops 2000000000 | bytes 2000000 | tf_op jit(solution)/shard_map/attend/pallas_call | solution.py:192
  131.7 3.3 %collective-permute-start.26 = (bf16[768,256]{1,0:T(8,128)(2,1)S(1)}, bf16[768,256]{1,0:T(8,128)(2,1)S(1)}, u32[]{:S(2)}, u32[]{:S(2)}) collective-permute-start(bf16[768,256]{1,0:T(8,128)(2,1)S(1)} %collective-permute-done.25), channel_id=1, source_target_pairs={{1,31},{3,1},{5,3},{7,5},{9,7},{11,9},{13,11},{15,13},{17,15},{19,... | collective-permute-start | bytes 1179656 | tf_op jit(solution)/shard_map/ppermute | solution.py:76
  135.1 0.5 collective-permute-done.19
  135.5 3.7 %collective-permute-start.20 = (bf16[768,256]{1,0:T(8,128)(2,1)S(1)}, bf16[768,256]{1,0:T(8,128)(2,1)S(1)}, u32[]{:S(2)}, u32[]{:S(2)}) collective-permute-start(bf16[768,256]{1,0:T(8,128)(2,1)S(1)} %collective-permute-done.19), channel_id=1, source_target_pairs={{1,31},{3,1},{5,3},{7,5},{9,7},{11,9},{13,11},{15,13},{17,15},{19,... | collective-permute-start | bytes 1179656 | tf_op jit(solution)/shard_map/ppermute | solution.py:76
  139.3 2.4 %attend.14.refs_1_ = f32[13,128,256]{2,1,0:T(8,128)S(1)} custom-call(s32[6]{0:T(128)S(1)} %stack.27.place, s32[9,384]{1,0:T(8,128)S(1)} %get-tuple-element.52.pairs, s32[1,9]{1,0:T(1,128)S(1)} %get-tuple-element.53.counts, bf16[12,128,128]{2,1,0:T(8,128)(2,1)S(1)} %bitcast.46, bf16[6,128,256]{2,1,0:T(8,128)(2,1)S(1)} %bitcast.63, ...), custom_call_target="tpu_custom_call", output_to_operand_aliasing={{}: (6, {})} | custom-call | flops 2000000000 | bytes 2000000 | tf_op jit(solution)/shard_map/attend/pallas_call | solution.py:192
  141.7 1.7 %attend.15.refs_1_ = f32[13,128,256]{2,1,0:T(8,128)S(1)} custom-call(s32[6]{0:T(128)S(1)} %stack.27.place, s32[9,384]{1,0:T(8,128)S(1)} %get-tuple-element.52.pairs, s32[1,9]{1,0:T(1,128)S(1)} %get-tuple-element.53.counts, bf16[12,128,128]{2,1,0:T(8,128)(2,1)S(1)} %bitcast.47, bf16[6,128,256]{2,1,0:T(8,128)(2,1)S(1)} %bitcast.50, ...), custom_call_target="tpu_custom_call", output_to_operand_aliasing={{}: (5, {})} | custom-call | flops 1000000000 | bytes 1000000 | tf_op jit(solution)/shard_map/attend/pallas_call | solution.py:192
  143.3 1.1 collective-permute-done.20
  144.5 1.5 attend.17
  146.0 3.6 %collective-permute-start.27 = (f32[6,128,256]{2,1,0:T(8,128)S(1)}, f32[6,128,256]{2,1,0:T(8,128)S(1)}, u32[]{:S(2)}, u32[]{:S(2)}) collective-permute-start(f32[6,128,256]{2,1,0:T(8,128)S(1)} %attend.17), channel_id=1, source_target_pairs={{0,1},{1,0},{2,3},{3,2},{4,5},{5,4},{6,7},{7,6},{8,9},{9,8},{10,11... | collective-permute-start | bytes 2359304 | tf_op jit(solution)/shard_map/ppermute | solution.py:66
  149.7 1.6 attend.16
  151.2 0.3 collective-permute-done.27
  151.6 0.1 add.19
  151.7 9.9 %all_to_all.19 = bf16[16,48,128]{2,1,0:T(8,128)(2,1)S(1)} all-to-all(bf16[16,48,128]{2,1,0:T(8,128)(2,1)S(1)} %bitcast.67), channel_id=1, replica_groups=mesh['seq'=16,'bal'=32] {'seq'}, dimensions={0} | all-to-all | bytes 393216 | tf_op jit(solution)/shard_map/all_to_all | solution.py:373
  161.7 0.7 copy_bitcast_fusion
  (26 shorter events, 0.2 us)
Async XLA Ops:
  0.0 81.0 %copy-start = (s32[1,192,64]{1,2,0:T(8,128)S(1)}, s32[1,192,64]{1,2,0:T(8,128)}, u32[]{:S(2)}) copy-start(s32[1,192,64]{1,2,0:T(8,128)} %param.10) | copy-start | bytes 147460
  0.0 37.7 %copy-start.1 = (bf16[3072,1,3,128]{3,0,2,1:T(8,128)(2,1)S(1)}, bf16[3072,1,3,128]{3,0,2,1:T(8,128)(2,1)}, u32[]{:S(2)}) copy-start(bf16[3072,1,3,128]{3,0,2,1:T(8,128)(2,1)} %param.7) | copy-start | bytes 7077892
  0.0 12.8 %collective-permute-start.1 = (bf16[48,3072]{1,0:T(8,128)(2,1)}, bf16[48,3072]{1,0:T(8,128)(2,1)S(1)}, u32[]{:S(2)}, u32[]{:S(2)}) collective-permute-start(bf16[48,3072]{1,0:T(8,128)(2,1)} %refs_0_.1), channel_id=1, source_target_pairs={{0,96},{32,0},{64,32},{96,64},{128,224},{160,128},{192,160},{224,1... | collective-permute-start | bytes 884744 | tf_op jit(solution)/shard_map/ppermute | solution.py:35
  5.6 12.3 %collective-permute-start = (bf16[48,3072]{1,0:T(8,128)(2,1)}, bf16[48,3072]{1,0:T(8,128)(2,1)S(1)}, u32[]{:S(2)}, u32[]{:S(2)}) collective-permute-start(bf16[48,3072]{1,0:T(8,128)(2,1)} %refs_0_.1), channel_id=1, source_target_pairs={{0,32},{32,64},{64,96},{96,0},{128,160},{160,192},{192,224},{224,1... | collective-permute-start | bytes 884744 | tf_op jit(solution)/shard_map/ppermute | solution.py:35
  7.5 13.3 %collective-permute-start.4 = (bf16[48,3072]{1,0:T(8,128)(2,1)}, bf16[48,3072]{1,0:T(8,128)(2,1)S(1)}, u32[]{:S(2)}, u32[]{:S(2)}) collective-permute-start(bf16[48,3072]{1,0:T(8,128)(2,1)} %refs_0_.1), channel_id=1, source_target_pairs={{0,64},{32,96},{64,0},{96,32},{128,192},{160,224},{192,128},{224,1... | collective-permute-start | bytes 884744 | tf_op jit(solution)/shard_map/ppermute | solution.py:35
  11.1 1.0 copy-start.2
  18.0 12.7 %collective-permute-start.2 = (bf16[96,3072]{1,0:T(8,128)(2,1)S(1)}, bf16[96,3072]{1,0:T(8,128)(2,1)}, u32[]{:S(2)}, u32[]{:S(2)}) collective-permute-start(bf16[96,3072]{1,0:T(8,128)(2,1)S(1)} %join.4.refs_0_), channel_id=1, source_target_pairs={{0,128},{32,160},{64,192},{96,224},{128,256},{160,288},{192,320},{... | collective-permute-start | bytes 1769480 | tf_op jit(solution)/shard_map/ppermute | solution.py:35
  21.7 11.2 %collective-permute-start.5 = (bf16[96,3072]{1,0:T(8,128)(2,1)}, bf16[96,3072]{1,0:T(8,128)(2,1)}, u32[]{:S(2)}, u32[]{:S(2)}) collective-permute-start(bf16[96,3072]{1,0:T(8,128)(2,1)} %join.5.refs_1_), channel_id=1, source_target_pairs={{0,384},{32,416},{64,448},{96,480},{128,0},{160,32},{192,64},{224,... | collective-permute-start | bytes 1769480 | tf_op jit(solution)/shard_map/ppermute | solution.py:35
  25.4 16.0 %collective-permute-start.7 = (bf16[96,3072]{1,0:T(8,128)(2,1)S(1)}, bf16[96,3072]{1,0:T(8,128)(2,1)}, u32[]{:S(2)}, u32[]{:S(2)}) collective-permute-start(bf16[96,3072]{1,0:T(8,128)(2,1)S(1)} %join.4.refs_0_), channel_id=1, source_target_pairs={{0,384},{32,416},{64,448},{96,480},{128,0},{160,32},{192,64},{224,... | collective-permute-start | bytes 1769480 | tf_op jit(solution)/shard_map/ppermute | solution.py:35
  28.3 13.1 %collective-permute-start.8 = (bf16[96,3072]{1,0:T(8,128)(2,1)}, bf16[96,3072]{1,0:T(8,128)(2,1)}, u32[]{:S(2)}, u32[]{:S(2)}) collective-permute-start(bf16[96,3072]{1,0:T(8,128)(2,1)} %join.5.refs_1_), channel_id=1, source_target_pairs={{0,128},{32,160},{64,192},{96,224},{128,256},{160,288},{192,320},{... | collective-permute-start | bytes 1769480 | tf_op jit(solution)/shard_map/ppermute | solution.py:35
  30.7 16.3 %collective-permute-start.3 = (bf16[96,3072]{1,0:T(8,128)(2,1)}, bf16[96,3072]{1,0:T(8,128)(2,1)}, u32[]{:S(2)}, u32[]{:S(2)}) collective-permute-start(bf16[96,3072]{1,0:T(8,128)(2,1)} %collective-permute-done.2.refs_2_), channel_id=1, source_target_pairs={{0,128},{32,160},{64,192},{96,224},{128,256},{160,288},{192,320},{... | collective-permute-start | bytes 1769480 | tf_op jit(solution)/shard_map/ppermute | solution.py:35
  32.9 14.1 %collective-permute-start.6 = (bf16[96,3072]{1,0:T(8,128)(2,1)}, bf16[96,3072]{1,0:T(8,128)(2,1)}, u32[]{:S(2)}, u32[]{:S(2)}) collective-permute-start(bf16[96,3072]{1,0:T(8,128)(2,1)} %collective-permute-done.5.refs_3_), channel_id=1, source_target_pairs={{0,384},{32,416},{64,448},{96,480},{128,0},{160,32},{192,64},{224,... | collective-permute-start | bytes 1769480 | tf_op jit(solution)/shard_map/ppermute | solution.py:35
  47.1 24.3 %copy-start.3 = (s32[1,192]{1,0:T(1,128)S(1)}, s32[1,192]{1,0:T(1,128)}, u32[]{:S(2)}) copy-start(s32[1,192]{1,0:T(1,128)} %param.11) | copy-start | bytes 2308
  49.9 16.8 %collective-permute-start.10 = (bf16[768,256]{1,0:T(8,128)(2,1)}, bf16[768,256]{1,0:T(8,128)(2,1)S(1)}, u32[]{:S(2)}, u32[]{:S(2)}) collective-permute-start(bf16[768,256]{1,0:T(8,128)(2,1)} %get-tuple-element.45), channel_id=1, source_target_pairs={{0,1},{1,0},{2,3},{3,2},{4,5},{5,4},{6,7},{7,6},{8,9},{9,8},{10,11... | collective-permute-start | bytes 1179656 | tf_op jit(solution)/shard_map/ppermute | solution.py:66
  55.6 16.1 %collective-permute-start.9 = (bf16[768,256]{1,0:T(8,128)(2,1)}, bf16[768,256]{1,0:T(8,128)(2,1)S(1)}, u32[]{:S(2)}, u32[]{:S(2)}) collective-permute-start(bf16[768,256]{1,0:T(8,128)(2,1)} %get-tuple-element.45), channel_id=1, source_target_pairs={{0,2},{1,31},{2,4},{3,1},{4,6},{5,3},{6,8},{7,5},{8,10},{9,7},{10,... | collective-permute-start | bytes 1179656 | tf_op jit(solution)/shard_map/ppermute | solution.py:76
  66.8 9.9 %collective-permute-start.13 = (bf16[768,256]{1,0:T(8,128)(2,1)S(1)}, bf16[768,256]{1,0:T(8,128)(2,1)S(1)}, u32[]{:S(2)}, u32[]{:S(2)}) collective-permute-start(bf16[768,256]{1,0:T(8,128)(2,1)S(1)} %collective-permute-done.10), channel_id=1, source_target_pairs={{0,2},{1,31},{2,4},{3,1},{4,6},{5,3},{6,8},{7,5},{8,10},{9,7},{10,... | collective-permute-start | bytes 1179656 | tf_op jit(solution)/shard_map/ppermute | solution.py:76
  69.4 3.3 %collective-permute-start.11 = (bf16[768,128]{1,0:T(8,128)(2,1)S(1)}, bf16[768,128]{1,0:T(8,128)(2,1)S(1)}, u32[]{:S(2)}, u32[]{:S(2)}) collective-permute-start(bf16[768,128]{1,0:T(8,128)(2,1)S(1)} %get-tuple-element.47), channel_id=1, source_target_pairs={{0,1},{1,0},{2,3},{3,2},{4,5},{5,4},{6,7},{7,6},{8,9},{9,8},{10,11... | collective-permute-start | bytes 589832 | tf_op jit(solution)/shard_map/ppermute | solution.py:66
  72.7 11.2 %collective-permute-start.12 = (bf16[768,256]{1,0:T(8,128)(2,1)S(1)}, bf16[768,256]{1,0:T(8,128)(2,1)S(1)}, u32[]{:S(2)}, u32[]{:S(2)}) collective-permute-start(bf16[768,256]{1,0:T(8,128)(2,1)S(1)} %collective-permute-done.9), channel_id=1, source_target_pairs={{0,2},{1,31},{2,4},{3,1},{4,6},{5,3},{6,8},{7,5},{8,10},{9,7},{10,... | collective-permute-start | bytes 1179656 | tf_op jit(solution)/shard_map/ppermute | solution.py:76
  76.7 9.7 %collective-permute-start.14 = (bf16[768,256]{1,0:T(8,128)(2,1)S(1)}, bf16[768,256]{1,0:T(8,128)(2,1)S(1)}, u32[]{:S(2)}, u32[]{:S(2)}) collective-permute-start(bf16[768,256]{1,0:T(8,128)(2,1)S(1)} %collective-permute-done.13), channel_id=1, source_target_pairs={{0,2},{1,31},{2,4},{3,1},{4,6},{5,3},{6,8},{7,5},{8,10},{9,7},{10,... | collective-permute-start | bytes 1179656 | tf_op jit(solution)/shard_map/ppermute | solution.py:76
  83.9 10.3 %collective-permute-start.21 = (bf16[768,256]{1,0:T(8,128)(2,1)S(1)}, bf16[768,256]{1,0:T(8,128)(2,1)S(1)}, u32[]{:S(2)}, u32[]{:S(2)}) collective-permute-start(bf16[768,256]{1,0:T(8,128)(2,1)S(1)} %collective-permute-done.12), channel_id=1, source_target_pairs={{0,2},{1,31},{2,4},{3,1},{4,6},{5,3},{6,8},{7,5},{8,10},{9,7},{10,... | collective-permute-start | bytes 1179656 | tf_op jit(solution)/shard_map/ppermute | solution.py:76
  86.4 10.6 %collective-permute-start.15 = (bf16[768,256]{1,0:T(8,128)(2,1)S(1)}, bf16[768,256]{1,0:T(8,128)(2,1)S(1)}, u32[]{:S(2)}, u32[]{:S(2)}) collective-permute-start(bf16[768,256]{1,0:T(8,128)(2,1)S(1)} %collective-permute-done.14), channel_id=1, source_target_pairs={{0,2},{1,31},{2,4},{3,1},{4,6},{5,3},{6,8},{7,5},{8,10},{9,7},{10,... | collective-permute-start | bytes 1179656 | tf_op jit(solution)/shard_map/ppermute | solution.py:76
  94.3 8.8 %collective-permute-start.22 = (bf16[768,256]{1,0:T(8,128)(2,1)S(1)}, bf16[768,256]{1,0:T(8,128)(2,1)S(1)}, u32[]{:S(2)}, u32[]{:S(2)}) collective-permute-start(bf16[768,256]{1,0:T(8,128)(2,1)S(1)} %collective-permute-done.21), channel_id=1, source_target_pairs={{0,2},{1,31},{2,4},{3,1},{4,6},{5,3},{6,8},{7,5},{8,10},{9,7},{10,... | collective-permute-start | bytes 1179656 | tf_op jit(solution)/shard_map/ppermute | solution.py:76
  97.0 10.3 %collective-permute-start.16 = (bf16[768,256]{1,0:T(8,128)(2,1)S(1)}, bf16[768,256]{1,0:T(8,128)(2,1)S(1)}, u32[]{:S(2)}, u32[]{:S(2)}) collective-permute-start(bf16[768,256]{1,0:T(8,128)(2,1)S(1)} %collective-permute-done.15), channel_id=1, source_target_pairs={{0,2},{1,31},{2,4},{3,1},{4,6},{5,3},{6,8},{7,5},{8,10},{9,7},{10,... | collective-permute-start | bytes 1179656 | tf_op jit(solution)/shard_map/ppermute | solution.py:76
  103.1 9.7 %collective-permute-start.23 = (bf16[768,256]{1,0:T(8,128)(2,1)S(1)}, bf16[768,256]{1,0:T(8,128)(2,1)S(1)}, u32[]{:S(2)}, u32[]{:S(2)}) collective-permute-start(bf16[768,256]{1,0:T(8,128)(2,1)S(1)} %collective-permute-done.22), channel_id=1, source_target_pairs={{0,2},{1,31},{2,4},{3,1},{4,6},{5,3},{6,8},{7,5},{8,10},{9,7},{10,... | collective-permute-start | bytes 1179656 | tf_op jit(solution)/shard_map/ppermute | solution.py:76
  107.3 8.8 %collective-permute-start.17 = (bf16[768,256]{1,0:T(8,128)(2,1)S(1)}, bf16[768,256]{1,0:T(8,128)(2,1)S(1)}, u32[]{:S(2)}, u32[]{:S(2)}) collective-permute-start(bf16[768,256]{1,0:T(8,128)(2,1)S(1)} %collective-permute-done.16), channel_id=1, source_target_pairs={{0,2},{1,31},{2,4},{3,1},{4,6},{5,3},{6,8},{7,5},{8,10},{9,7},{10,... | collective-permute-start | bytes 1179656 | tf_op jit(solution)/shard_map/ppermute | solution.py:76
  112.8 9.7 %collective-permute-start.24 = (bf16[768,256]{1,0:T(8,128)(2,1)S(1)}, bf16[768,256]{1,0:T(8,128)(2,1)S(1)}, u32[]{:S(2)}, u32[]{:S(2)}) collective-permute-start(bf16[768,256]{1,0:T(8,128)(2,1)S(1)} %collective-permute-done.23), channel_id=1, source_target_pairs={{0,2},{1,31},{2,4},{3,1},{4,6},{5,3},{6,8},{7,5},{8,10},{9,7},{10,... | collective-permute-start | bytes 1179656 | tf_op jit(solution)/shard_map/ppermute | solution.py:76
  116.1 9.7 %collective-permute-start.18 = (bf16[768,256]{1,0:T(8,128)(2,1)S(1)}, bf16[768,256]{1,0:T(8,128)(2,1)S(1)}, u32[]{:S(2)}, u32[]{:S(2)}) collective-permute-start(bf16[768,256]{1,0:T(8,128)(2,1)S(1)} %collective-permute-done.17), channel_id=1, source_target_pairs={{0,2},{1,31},{2,4},{3,1},{4,6},{5,3},{6,8},{7,5},{8,10},{9,7},{10,... | collective-permute-start | bytes 1179656 | tf_op jit(solution)/shard_map/ppermute | solution.py:76
  122.5 9.2 %collective-permute-start.25 = (bf16[768,256]{1,0:T(8,128)(2,1)S(1)}, bf16[768,256]{1,0:T(8,128)(2,1)S(1)}, u32[]{:S(2)}, u32[]{:S(2)}) collective-permute-start(bf16[768,256]{1,0:T(8,128)(2,1)S(1)} %collective-permute-done.24), channel_id=1, source_target_pairs={{0,2},{1,31},{2,4},{3,1},{4,6},{5,3},{6,8},{7,5},{8,10},{9,7},{10,... | collective-permute-start | bytes 1179656 | tf_op jit(solution)/shard_map/ppermute | solution.py:76
  125.8 9.7 %collective-permute-start.19 = (bf16[768,256]{1,0:T(8,128)(2,1)S(1)}, bf16[768,256]{1,0:T(8,128)(2,1)S(1)}, u32[]{:S(2)}, u32[]{:S(2)}) collective-permute-start(bf16[768,256]{1,0:T(8,128)(2,1)S(1)} %collective-permute-done.18), channel_id=1, source_target_pairs={{0,2},{1,31},{2,4},{3,1},{4,6},{5,3},{6,8},{7,5},{8,10},{9,7},{10,... | collective-permute-start | bytes 1179656 | tf_op jit(solution)/shard_map/ppermute | solution.py:76
  131.7 9.9 %collective-permute-start.26 = (bf16[768,256]{1,0:T(8,128)(2,1)S(1)}, bf16[768,256]{1,0:T(8,128)(2,1)S(1)}, u32[]{:S(2)}, u32[]{:S(2)}) collective-permute-start(bf16[768,256]{1,0:T(8,128)(2,1)S(1)} %collective-permute-done.25), channel_id=1, source_target_pairs={{1,31},{3,1},{5,3},{7,5},{9,7},{11,9},{13,11},{15,13},{17,15},{19,... | collective-permute-start | bytes 1179656 | tf_op jit(solution)/shard_map/ppermute | solution.py:76
  135.5 8.9 %collective-permute-start.20 = (bf16[768,256]{1,0:T(8,128)(2,1)S(1)}, bf16[768,256]{1,0:T(8,128)(2,1)S(1)}, u32[]{:S(2)}, u32[]{:S(2)}) collective-permute-start(bf16[768,256]{1,0:T(8,128)(2,1)S(1)} %collective-permute-done.19), channel_id=1, source_target_pairs={{1,31},{3,1},{5,3},{7,5},{9,7},{11,9},{13,11},{15,13},{17,15},{19,... | collective-permute-start | bytes 1179656 | tf_op jit(solution)/shard_map/ppermute | solution.py:76
  146.0 5.5 %collective-permute-start.27 = (f32[6,128,256]{2,1,0:T(8,128)S(1)}, f32[6,128,256]{2,1,0:T(8,128)S(1)}, u32[]{:S(2)}, u32[]{:S(2)}) collective-permute-start(f32[6,128,256]{2,1,0:T(8,128)S(1)} %attend.17), channel_id=1, source_target_pairs={{0,1},{1,0},{2,3},{3,2},{4,5},{5,4},{6,7},{7,6},{8,9},{9,8},{10,11... | collective-permute-start | bytes 2359304 | tf_op jit(solution)/shard_map/ppermute | solution.py:66

commit v16 on v14

--- a/solution.py
+++ b/solution.py
@@ -176,7 +176,7 @@
 
     lax.fori_loop(0, (counts[0, call] + UNROLL - 1) // UNROLL, turn, 0)
     if part is not None:
-        refs[-3][...] = sums[:slots]
+        refs[-3][...] = sums[:slots].astype(refs[-3].dtype)
 
 
 def attend(call, place, pairs, counts, q, pieces, sums=None):
@@ -191,7 +191,9 @@
     more = () if call == 0 else (sums,)
     return pl.pallas_call(
         functools.partial(attend_kernel, scale, call, part, blocks),
-        out_shape=jax.ShapeDtypeStruct((rows_out, TILE, 2 * HEAD), jnp.float32),
+        out_shape=jax.ShapeDtypeStruct(
+            (rows_out, TILE, 2 * HEAD), jnp.bfloat16 if part == "other" else jnp.float32
+        ),
         in_specs=[SMEM] * 3 + [VMEM] * (1 + blocks + len(more)),
         out_specs=VMEM,
         scratch_shapes=scratch,
@@ -360,7 +362,7 @@
                 sums = attend(call, place, pairs, counts, chip_queries, blocks, sums)
     given = swap_cores(attend(call, place, pairs, counts, chip_queries, blocks, sums))
     kept = attend(call + 1, place, pairs, counts, chip_queries, blocks, sums)
-    sums = kept + given
+    sums = kept + given.astype(jnp.float32)
     result = (sums[:, :, :HEAD] / sums[:, :, HEAD:]).astype(jnp.bfloat16)
     return lax.all_to_all(
         result.reshape(slots * TILE, HEAD), "seq", split_axis=0, concat_axis=1, tiled=True

time: 163 us -> 164 us (level)
  starting transfers between devices: 100 us -> 104 us
  waiting for transfers between devices: 17.5 us -> 14.3 us
  blocking collectives: 10.5 us -> 12.8 us
    ppermute x16, starting transfers between devices: 61.1 us -> 64 us  [pass_on(): return lax.ppermute(block, 'bal', pairs)]
    ppermute x16, waiting for transfers between devices: 7.39 us -> 5.06 us  [pass_on(): return lax.ppermute(block, 'bal', pairs)]
    all_to_all x1, blocking collectives: 10.5 us -> 12.8 us  [on_device(): lax.all_to_all(result.reshape(slots * TILE, HEAD), 'seq', split_axis=0, c...]
  transfers between devices with their start and end apart: 28 -> 28, of which waited for: 12 -> 9; matrix products, arithmetic and copies ran while one was open for 1% -> 1% of each run, Pallas kernels for 16% -> 15%
where the time goes in v16:
time: 164 us; the launch traced here: 163 us
  starting transfers between devices  104 us (63%)
  Pallas kernels  28.9 us (18%)
  waiting for transfers between devices  14.3 us (9%)
  blocking collectives  12.8 us (8%)
  local copies, waits for them, and re-layouts  1.91 us (1%)
    ppermute x16, starting transfers between devices, pass_on(): return lax.ppermute(block, 'bal', pairs)  64 us
    ppermute x9, starting transfers between devices, send(): return lax.ppermute(block, MESH_AXES, plane_perm(phase, shift))  29.3 us
    pallas_call x8, Pallas kernels, attend(): pl.pallas_call(functools.partial(attend_kernel, scale, call, part, blocks...  15.8 us
    all_to_all x1, blocking collectives, on_device(): lax.all_to_all(result.reshape(slots * TILE, HEAD), 'seq', split_axis=0, c...  12.8 us
    ppermute x3, starting transfers between devices, swap_cores(): return lax.ppermute(block, 'bal', [(at, at ^ 1) for at in range(32)])  10.3 us
    pallas_call x3, Pallas kernels, project(): pl.pallas_call(functools.partial(project_kernel, shares), out_shape=(jax....  9.37 us
    ppermute x9, waiting for transfers between devices, send(): return lax.ppermute(block, MESH_AXES, plane_perm(phase, shift))  8.27 us
    ppermute x16, waiting for transfers between devices, pass_on(): return lax.ppermute(block, 'bal', pairs)  5.06 us
  transfers between devices with their start and end apart: 28, of which 9 were waited for; matrix products, arithmetic and copies ran while one was open for 1% of the time, Pallas kernels for 15%

profile of v16, /device:TPU:1, one launch (start us, length us, event | category | flops | bytes accessed | tf_op | source)
XLA Modules:
  0.0 163.0 jit_solution(10125889849595642456)
XLA Ops:
  0.0 5.6 %collective-permute-start.1 = (bf16[48,3072]{1,0:T(8,128)(2,1)}, bf16[48,3072]{1,0:T(8,128)(2,1)S(1)}, u32[]{:S(2)}, u32[]{:S(2)}) collective-permute-start(bf16[48,3072]{1,0:T(8,128)(2,1)} %refs_0_.1), channel_id=1, source_target_pairs={{0,96},{32,0},{64,32},{96,64},{128,224},{160,128},{192,160},{224,1... | collective-permute-start | bytes 884744 | tf_op jit(solution)/shard_map/ppermute | solution.py:35
  5.6 1.9 %collective-permute-start = (bf16[48,3072]{1,0:T(8,128)(2,1)}, bf16[48,3072]{1,0:T(8,128)(2,1)S(1)}, u32[]{:S(2)}, u32[]{:S(2)}) collective-permute-start(bf16[48,3072]{1,0:T(8,128)(2,1)} %refs_0_.1), channel_id=1, source_target_pairs={{0,32},{32,64},{64,96},{96,0},{128,160},{160,192},{192,224},{224,1... | collective-permute-start | bytes 884744 | tf_op jit(solution)/shard_map/ppermute | solution.py:35
  7.5 3.5 %collective-permute-start.4 = (bf16[48,3072]{1,0:T(8,128)(2,1)}, bf16[48,3072]{1,0:T(8,128)(2,1)S(1)}, u32[]{:S(2)}, u32[]{:S(2)}) collective-permute-start(bf16[48,3072]{1,0:T(8,128)(2,1)} %refs_0_.1), channel_id=1, source_target_pairs={{0,64},{32,96},{64,0},{96,32},{128,192},{160,224},{192,128},{224,1... | collective-permute-start | bytes 884744 | tf_op jit(solution)/shard_map/ppermute | solution.py:35
  11.1 1.0 copy-done.2
  12.1 0.1 join.3.refs_1_
  12.1 0.7 pad_maximum_fusion.1.refs_5_.refs_3_
  12.8 0.0 collective-permute-done.1.refs_0_
  12.8 5.1 %collective-permute-done.refs_0_ = bf16[48,3072]{1,0:T(8,128)(2,1)S(1)} collective-permute-done((bf16[48,3072]{1,0:T(8,128)(2,1)}, bf16[48,3072]{1,0:T(8,128)(2,1)S(1)}, u32[]{:S(2)}, u32[]{:S(2)}) %collective-permute-start) | collective-permute-done | bytes 294944 | tf_op jit(solution)/shard_map/ppermute | solution.py:35
  17.9 0.1 join.4.refs_0_
  18.0 2.8 %collective-permute-start.2 = (bf16[96,3072]{1,0:T(8,128)(2,1)S(1)}, bf16[96,3072]{1,0:T(8,128)(2,1)}, u32[]{:S(2)}, u32[]{:S(2)}) collective-permute-start(bf16[96,3072]{1,0:T(8,128)(2,1)S(1)} %join.4.refs_0_), channel_id=1, source_target_pairs={{0,128},{32,160},{64,192},{96,224},{128,256},{160,288},{192,320},{... | collective-permute-start | bytes 1769480 | tf_op jit(solution)/shard_map/ppermute | solution.py:35
  20.9 0.8 join.5.refs_1_
  21.7 3.7 %collective-permute-start.5 = (bf16[96,3072]{1,0:T(8,128)(2,1)}, bf16[96,3072]{1,0:T(8,128)(2,1)}, u32[]{:S(2)}, u32[]{:S(2)}) collective-permute-start(bf16[96,3072]{1,0:T(8,128)(2,1)} %join.5.refs_1_), channel_id=1, source_target_pairs={{0,384},{32,416},{64,448},{96,480},{128,0},{160,32},{192,64},{224,... | collective-permute-start | bytes 1769480 | tf_op jit(solution)/shard_map/ppermute | solution.py:35
  25.4 2.9 %collective-permute-start.7 = (bf16[96,3072]{1,0:T(8,128)(2,1)S(1)}, bf16[96,3072]{1,0:T(8,128)(2,1)}, u32[]{:S(2)}, u32[]{:S(2)}) collective-permute-start(bf16[96,3072]{1,0:T(8,128)(2,1)S(1)} %join.4.refs_0_), channel_id=1, source_target_pairs={{0,384},{32,416},{64,448},{96,480},{128,0},{160,32},{192,64},{224,... | collective-permute-start | bytes 1769480 | tf_op jit(solution)/shard_map/ppermute | solution.py:35
  28.3 2.4 %collective-permute-start.8 = (bf16[96,3072]{1,0:T(8,128)(2,1)}, bf16[96,3072]{1,0:T(8,128)(2,1)}, u32[]{:S(2)}, u32[]{:S(2)}) collective-permute-start(bf16[96,3072]{1,0:T(8,128)(2,1)} %join.5.refs_1_), channel_id=1, source_target_pairs={{0,128},{32,160},{64,192},{96,224},{128,256},{160,288},{192,320},{... | collective-permute-start | bytes 1769480 | tf_op jit(solution)/shard_map/ppermute | solution.py:35
  30.7 0.0 collective-permute-done.2.refs_2_
  30.7 1.9 %collective-permute-start.3 = (bf16[96,3072]{1,0:T(8,128)(2,1)}, bf16[96,3072]{1,0:T(8,128)(2,1)}, u32[]{:S(2)}, u32[]{:S(2)}) collective-permute-start(bf16[96,3072]{1,0:T(8,128)(2,1)} %collective-permute-done.2.refs_2_), channel_id=1, source_target_pairs={{0,128},{32,160},{64,192},{96,224},{128,256},{160,288},{192,320},{... | collective-permute-start | bytes 1769480 | tf_op jit(solution)/shard_map/ppermute | solution.py:35
  32.6 0.3 collective-permute-done.5.refs_3_
  32.9 4.6 %collective-permute-start.6 = (bf16[96,3072]{1,0:T(8,128)(2,1)}, bf16[96,3072]{1,0:T(8,128)(2,1)}, u32[]{:S(2)}, u32[]{:S(2)}) collective-permute-start(bf16[96,3072]{1,0:T(8,128)(2,1)} %collective-permute-done.5.refs_3_), channel_id=1, source_target_pairs={{0,384},{32,416},{64,448},{96,480},{128,0},{160,32},{192,64},{224,... | collective-permute-start | bytes 1769480 | tf_op jit(solution)/shard_map/ppermute | solution.py:35
  37.6 0.1 stack.27.place
  37.7 3.7 %project.3 = (bf16[768,128]{1,0:T(8,128)(2,1)S(1)}, bf16[768,256]{1,0:T(8,128)(2,1)}) custom-call(s32[6]{0:T(128)S(1)} %stack.27.place, bf16[96,3072]{1,0:T(8,128)(2,1)S(1)} %join.4.refs_0_, bf16[96,3072]{1,0:T(8,128)(2,1)} %join.5.refs_1_, bf16[96,3072]{1,0:T(8,128)(2,1)} %collective-permute-done.2.refs_2_, ...), custom_call_target="tpu_custom_call" | custom-call | tf_op jit(solution)/shard_map/project/pallas_call | solution.py:117
  41.4 0.0 collective-permute-done.8.refs_1_
  41.4 2.8 %project.4 = (bf16[768,128]{1,0:T(8,128)(2,1)S(1)}, bf16[768,256]{1,0:T(8,128)(2,1)}) custom-call(s32[6]{0:T(128)S(1)} %stack.27.place, bf16[96,3072]{1,0:T(8,128)(2,1)} %collective-permute-done.7.refs_0_, bf16[96,3072]{1,0:T(8,128)(2,1)} %collective-permute-done.8.refs_1_, ...), custom_call_target="tpu_custom_call", output_to_operand_aliasing={{0}: (5, {}), {1}: (6, {})} | custom-call | tf_op jit(solution)/shard_map/project/pallas_call | solution.py:117
  44.2 2.8 %collective-permute-done.3.refs_0_ = bf16[96,3072]{1,0:T(8,128)(2,1)} collective-permute-done((bf16[96,3072]{1,0:T(8,128)(2,1)}, bf16[96,3072]{1,0:T(8,128)(2,1)}, u32[]{:S(2)}, u32[]{:S(2)}) %collective-permute-start.3) | collective-permute-done | bytes 589856 | tf_op jit(solution)/shard_map/ppermute | solution.py:35
  47.1 2.8 %project.5 = (bf16[768,128]{1,0:T(8,128)(2,1)S(1)}, bf16[768,256]{1,0:T(8,128)(2,1)}) custom-call(s32[6]{0:T(128)S(1)} %stack.27.place, bf16[96,3072]{1,0:T(8,128)(2,1)} %collective-permute-done.3.refs_0_, bf16[96,3072]{1,0:T(8,128)(2,1)} %collective-permute-done.6.refs_1_, ...), custom_call_target="tpu_custom_call", output_to_operand_aliasing={{0}: (5, {}), {1}: (6, {})} | custom-call | tf_op jit(solution)/shard_map/project/pallas_call | solution.py:117
  49.9 5.7 %collective-permute-start.10 = (bf16[768,256]{1,0:T(8,128)(2,1)}, bf16[768,256]{1,0:T(8,128)(2,1)S(1)}, u32[]{:S(2)}, u32[]{:S(2)}) collective-permute-start(bf16[768,256]{1,0:T(8,128)(2,1)} %get-tuple-element.45), channel_id=1, source_target_pairs={{0,1},{1,0},{2,3},{3,2},{4,5},{5,4},{6,7},{7,6},{8,9},{9,8},{10,11... | collective-permute-start | bytes 1179656 | tf_op jit(solution)/shard_map/ppermute | solution.py:66
  55.6 11.1 %collective-permute-start.9 = (bf16[768,256]{1,0:T(8,128)(2,1)}, bf16[768,256]{1,0:T(8,128)(2,1)S(1)}, u32[]{:S(2)}, u32[]{:S(2)}) collective-permute-start(bf16[768,256]{1,0:T(8,128)(2,1)} %get-tuple-element.45), channel_id=1, source_target_pairs={{0,2},{1,31},{2,4},{3,1},{4,6},{5,3},{6,8},{7,5},{8,10},{9,7},{10,... | collective-permute-start | bytes 1179656 | tf_op jit(solution)/shard_map/ppermute | solution.py:76
  66.8 2.6 %collective-permute-start.13 = (bf16[768,256]{1,0:T(8,128)(2,1)S(1)}, bf16[768,256]{1,0:T(8,128)(2,1)S(1)}, u32[]{:S(2)}, u32[]{:S(2)}) collective-permute-start(bf16[768,256]{1,0:T(8,128)(2,1)S(1)} %collective-permute-done.10), channel_id=1, source_target_pairs={{0,2},{1,31},{2,4},{3,1},{4,6},{5,3},{6,8},{7,5},{8,10},{9,7},{10,... | collective-permute-start | bytes 1179656 | tf_op jit(solution)/shard_map/ppermute | solution.py:76
  69.4 1.9 %collective-permute-start.11 = (bf16[768,128]{1,0:T(8,128)(2,1)S(1)}, bf16[768,128]{1,0:T(8,128)(2,1)S(1)}, u32[]{:S(2)}, u32[]{:S(2)}) collective-permute-start(bf16[768,128]{1,0:T(8,128)(2,1)S(1)} %get-tuple-element.47), channel_id=1, source_target_pairs={{0,1},{1,0},{2,3},{3,2},{4,5},{5,4},{6,7},{7,6},{8,9},{9,8},{10,11... | collective-permute-start | bytes 589832 | tf_op jit(solution)/shard_map/ppermute | solution.py:66
  71.3 0.1 constant_dynamic-slice_fusion.counts
  71.4 0.3 collective-permute-done.9
  71.8 1.0 collective-permute-done.11
  72.7 3.9 %collective-permute-start.12 = (bf16[768,256]{1,0:T(8,128)(2,1)S(1)}, bf16[768,256]{1,0:T(8,128)(2,1)S(1)}, u32[]{:S(2)}, u32[]{:S(2)}) collective-permute-start(bf16[768,256]{1,0:T(8,128)(2,1)S(1)} %collective-permute-done.9), channel_id=1, source_target_pairs={{0,2},{1,31},{2,4},{3,1},{4,6},{5,3},{6,8},{7,5},{8,10},{9,7},{10,... | collective-permute-start | bytes 1179656 | tf_op jit(solution)/shard_map/ppermute | solution.py:76
  76.7 4.2 %collective-permute-start.14 = (bf16[768,256]{1,0:T(8,128)(2,1)S(1)}, bf16[768,256]{1,0:T(8,128)(2,1)S(1)}, u32[]{:S(2)}, u32[]{:S(2)}) collective-permute-start(bf16[768,256]{1,0:T(8,128)(2,1)S(1)} %collective-permute-done.13), channel_id=1, source_target_pairs={{0,2},{1,31},{2,4},{3,1},{4,6},{5,3},{6,8},{7,5},{8,10},{9,7},{10,... | collective-permute-start | bytes 1179656 | tf_op jit(solution)/shard_map/ppermute | solution.py:76
  81.0 0.1 dynamic-slice_bitcast_fusion.tiles
  81.1 2.8 %lists.1 = (s32[8,384]{1,0:T(8,128)S(1)}, s32[1,8]{1,0:T(1,128)S(1)}) custom-call(s32[6]{0:T(128)S(1)} %stack.27.place, s32[64,12]{1,0:T(8,128)S(1)} %dynamic-slice_bitcast_fusion.tiles, s32[1,12]{1,0:T(1,128)S(1)} %constant_dynamic-slice_fusion.counts), custom_call_target="tpu_custom_call" | custom-call | tf_op jit(solution)/shard_map/lists/pallas_call | solution.py:266
  83.8 2.6 %collective-permute-start.15 = (bf16[768,256]{1,0:T(8,128)(2,1)S(1)}, bf16[768,256]{1,0:T(8,128)(2,1)S(1)}, u32[]{:S(2)}, u32[]{:S(2)}) collective-permute-start(bf16[768,256]{1,0:T(8,128)(2,1)S(1)} %collective-permute-done.12), channel_id=1, source_target_pairs={{0,2},{1,31},{2,4},{3,1},{4,6},{5,3},{6,8},{7,5},{8,10},{9,7},{10,... | collective-permute-start | bytes 1179656 | tf_op jit(solution)/shard_map/ppermute | solution.py:76
  86.4 4.2 %collective-permute-start.17 = (bf16[768,256]{1,0:T(8,128)(2,1)S(1)}, bf16[768,256]{1,0:T(8,128)(2,1)S(1)}, u32[]{:S(2)}, u32[]{:S(2)}) collective-permute-start(bf16[768,256]{1,0:T(8,128)(2,1)S(1)} %collective-permute-done.14), channel_id=1, source_target_pairs={{0,2},{1,31},{2,4},{3,1},{4,6},{5,3},{6,8},{7,5},{8,10},{9,7},{10,... | collective-permute-start | bytes 1179656 | tf_op jit(solution)/shard_map/ppermute | solution.py:76
  90.6 3.2 %attend.8.refs_2_ = f32[13,128,256]{2,1,0:T(8,128)S(1)} custom-call(s32[6]{0:T(128)S(1)} %stack.27.place, s32[8,384]{1,0:T(8,128)S(1)} %get-tuple-element.52.pairs, s32[1,8]{1,0:T(1,128)S(1)} %get-tuple-element.53.counts, bf16[12,128,128]{2,1,0:T(8,128)(2,1)S(1)} %bitcast.41, bf16[6,128,256]{2,1,0:T(8,128)(2,1)} %bitcast.12.refs_0_, ...), custom_call_target="tpu_custom_call" | custom-call | flops 5000000000 | bytes 5000000 | tf_op jit(solution)/shard_map/attend/pallas_call | solution.py:192
  93.8 2.3 %collective-permute-start.16 = (bf16[768,256]{1,0:T(8,128)(2,1)S(1)}, bf16[768,256]{1,0:T(8,128)(2,1)S(1)}, u32[]{:S(2)}, u32[]{:S(2)}) collective-permute-start(bf16[768,256]{1,0:T(8,128)(2,1)S(1)} %collective-permute-done.15), channel_id=1, source_target_pairs={{0,2},{1,31},{2,4},{3,1},{4,6},{5,3},{6,8},{7,5},{8,10},{9,7},{10,... | collective-permute-start | bytes 1179656 | tf_op jit(solution)/shard_map/ppermute | solution.py:76
  96.1 0.7 collective-permute-done.17
  96.8 3.5 %collective-permute-start.19 = (bf16[768,256]{1,0:T(8,128)(2,1)S(1)}, bf16[768,256]{1,0:T(8,128)(2,1)S(1)}, u32[]{:S(2)}, u32[]{:S(2)}) collective-permute-start(bf16[768,256]{1,0:T(8,128)(2,1)S(1)} %collective-permute-done.17), channel_id=1, source_target_pairs={{0,2},{1,31},{2,4},{3,1},{4,6},{5,3},{6,8},{7,5},{8,10},{9,7},{10,... | collective-permute-start | bytes 1179656 | tf_op jit(solution)/shard_map/ppermute | solution.py:76
  100.3 2.4 %attend.9.refs_2_ = f32[13,128,256]{2,1,0:T(8,128)S(1)} custom-call(s32[6]{0:T(128)S(1)} %stack.27.place, s32[8,384]{1,0:T(8,128)S(1)} %get-tuple-element.52.pairs, s32[1,8]{1,0:T(1,128)S(1)} %get-tuple-element.53.counts, bf16[12,128,128]{2,1,0:T(8,128)(2,1)S(1)} %bitcast.42, bf16[6,128,256]{2,1,0:T(8,128)(2,1)S(1)} %bitcast.54, ...), custom_call_target="tpu_custom_call", output_to_operand_aliasing={{}: (6, {})} | custom-call | flops 2000000000 | bytes 2000000 | tf_op jit(solution)/shard_map/attend/pallas_call | solution.py:192
  102.8 3.0 %collective-permute-start.18 = (bf16[768,256]{1,0:T(8,128)(2,1)S(1)}, bf16[768,256]{1,0:T(8,128)(2,1)S(1)}, u32[]{:S(2)}, u32[]{:S(2)}) collective-permute-start(bf16[768,256]{1,0:T(8,128)(2,1)S(1)} %collective-permute-done.16), channel_id=1, source_target_pairs={{0,2},{1,31},{2,4},{3,1},{4,6},{5,3},{6,8},{7,5},{8,10},{9,7},{10,... | collective-permute-start | bytes 1179656 | tf_op jit(solution)/shard_map/ppermute | solution.py:76
  105.8 1.0 collective-permute-done.19
  106.8 3.2 %collective-permute-start.21 = (bf16[768,256]{1,0:T(8,128)(2,1)S(1)}, bf16[768,256]{1,0:T(8,128)(2,1)S(1)}, u32[]{:S(2)}, u32[]{:S(2)}) collective-permute-start(bf16[768,256]{1,0:T(8,128)(2,1)S(1)} %collective-permute-done.19), channel_id=1, source_target_pairs={{0,2},{1,31},{2,4},{3,1},{4,6},{5,3},{6,8},{7,5},{8,10},{9,7},{10,... | collective-permute-start | bytes 1179656 | tf_op jit(solution)/shard_map/ppermute | solution.py:76
  110.0 2.0 %attend.10.refs_2_ = f32[13,128,256]{2,1,0:T(8,128)S(1)} custom-call(s32[6]{0:T(128)S(1)} %stack.27.place, s32[8,384]{1,0:T(8,128)S(1)} %get-tuple-element.52.pairs, s32[1,8]{1,0:T(1,128)S(1)} %get-tuple-element.53.counts, bf16[12,128,128]{2,1,0:T(8,128)(2,1)S(1)} %bitcast.43, bf16[6,128,256]{2,1,0:T(8,128)(2,1)S(1)} %bitcast.55, ...), custom_call_target="tpu_custom_call", output_to_operand_aliasing={{}: (6, {})} | custom-call | flops 2000000000 | bytes 2000000 | tf_op jit(solution)/shard_map/attend/pallas_call | solution.py:192
  112.0 3.5 %collective-permute-start.20 = (bf16[768,256]{1,0:T(8,128)(2,1)S(1)}, bf16[768,256]{1,0:T(8,128)(2,1)S(1)}, u32[]{:S(2)}, u32[]{:S(2)}) collective-permute-start(bf16[768,256]{1,0:T(8,128)(2,1)S(1)} %collective-permute-done.18), channel_id=1, source_target_pairs={{0,2},{1,31},{2,4},{3,1},{4,6},{5,3},{6,8},{7,5},{8,10},{9,7},{10,... | collective-permute-start | bytes 1179656 | tf_op jit(solution)/shard_map/ppermute | solution.py:76
  115.6 0.3 collective-permute-done.21
  115.8 3.9 %collective-permute-start.23 = (bf16[768,256]{1,0:T(8,128)(2,1)S(1)}, bf16[768,256]{1,0:T(8,128)(2,1)S(1)}, u32[]{:S(2)}, u32[]{:S(2)}) collective-permute-start(bf16[768,256]{1,0:T(8,128)(2,1)S(1)} %collective-permute-done.21), channel_id=1, source_target_pairs={{0,2},{1,31},{2,4},{3,1},{4,6},{5,3},{6,8},{7,5},{8,10},{9,7},{10,... | collective-permute-start | bytes 1179656 | tf_op jit(solution)/shard_map/ppermute | solution.py:76
  119.8 2.0 %attend.11.refs_2_ = f32[13,128,256]{2,1,0:T(8,128)S(1)} custom-call(s32[6]{0:T(128)S(1)} %stack.27.place, s32[8,384]{1,0:T(8,128)S(1)} %get-tuple-element.52.pairs, s32[1,8]{1,0:T(1,128)S(1)} %get-tuple-element.53.counts, bf16[12,128,128]{2,1,0:T(8,128)(2,1)S(1)} %bitcast.44, bf16[6,128,256]{2,1,0:T(8,128)(2,1)S(1)} %bitcast.57, ...), custom_call_target="tpu_custom_call", output_to_operand_aliasing={{}: (6, {})} | custom-call | flops 2000000000 | bytes 2000000 | tf_op jit(solution)/shard_map/attend/pallas_call | solution.py:192
  121.8 3.5 %collective-permute-start.22 = (bf16[768,256]{1,0:T(8,128)(2,1)S(1)}, bf16[768,256]{1,0:T(8,128)(2,1)S(1)}, u32[]{:S(2)}, u32[]{:S(2)}) collective-permute-start(bf16[768,256]{1,0:T(8,128)(2,1)S(1)} %collective-permute-done.20), channel_id=1, source_target_pairs={{0,2},{1,31},{2,4},{3,1},{4,6},{5,3},{6,8},{7,5},{8,10},{9,7},{10,... | collective-permute-start | bytes 1179656 | tf_op jit(solution)/shard_map/ppermute | solution.py:76
  125.3 4.2 %collective-permute-start.25 = (bf16[768,256]{1,0:T(8,128)(2,1)S(1)}, bf16[768,256]{1,0:T(8,128)(2,1)S(1)}, u32[]{:S(2)}, u32[]{:S(2)}) collective-permute-start(bf16[768,256]{1,0:T(8,128)(2,1)S(1)} %collective-permute-done.23), channel_id=1, source_target_pairs={{0,2},{1,31},{2,4},{3,1},{4,6},{5,3},{6,8},{7,5},{8,10},{9,7},{10,... | collective-permute-start | bytes 1179656 | tf_op jit(solution)/shard_map/ppermute | solution.py:76
  129.5 1.5 attend.12.refs_2_
  131.0 4.0 %collective-permute-start.24 = (bf16[768,256]{1,0:T(8,128)(2,1)S(1)}, bf16[768,256]{1,0:T(8,128)(2,1)S(1)}, u32[]{:S(2)}, u32[]{:S(2)}) collective-permute-start(bf16[768,256]{1,0:T(8,128)(2,1)S(1)} %collective-permute-done.22), channel_id=1, source_target_pairs={{1,31},{3,1},{5,3},{7,5},{9,7},{11,9},{13,11},{15,13},{17,15},{19,... | collective-permute-start | bytes 1179656 | tf_op jit(solution)/shard_map/ppermute | solution.py:76
  135.0 4.2 %collective-permute-start.26 = (bf16[768,256]{1,0:T(8,128)(2,1)S(1)}, bf16[768,256]{1,0:T(8,128)(2,1)S(1)}, u32[]{:S(2)}, u32[]{:S(2)}) collective-permute-start(bf16[768,256]{1,0:T(8,128)(2,1)S(1)} %collective-permute-done.25), channel_id=1, source_target_pairs={{1,31},{3,1},{5,3},{7,5},{9,7},{11,9},{13,11},{15,13},{17,15},{19,... | collective-permute-start | bytes 1179656 | tf_op jit(solution)/shard_map/ppermute | solution.py:76
  139.2 2.0 %attend.13.refs_2_ = f32[13,128,256]{2,1,0:T(8,128)S(1)} custom-call(s32[6]{0:T(128)S(1)} %stack.27.place, s32[8,384]{1,0:T(8,128)S(1)} %get-tuple-element.52.pairs, s32[1,8]{1,0:T(1,128)S(1)} %get-tuple-element.53.counts, bf16[12,128,128]{2,1,0:T(8,128)(2,1)S(1)} %bitcast.46, bf16[6,128,256]{2,1,0:T(8,128)(2,1)S(1)} %bitcast.61, ...), custom_call_target="tpu_custom_call", output_to_operand_aliasing={{}: (6, {})} | custom-call | flops 2000000000 | bytes 2000000 | tf_op jit(solution)/shard_map/attend/pallas_call | solution.py:192
  141.2 2.7 %collective-permute-done.26 = bf16[768,256]{1,0:T(8,128)(2,1)S(1)} collective-permute-done((bf16[768,256]{1,0:T(8,128)(2,1)S(1)}, bf16[768,256]{1,0:T(8,128)(2,1)S(1)}, u32[]{:S(2)}, u32[]{:S(2)}) %collective-permute-start.26) | collective-permute-done | bytes 393248 | tf_op jit(solution)/shard_map/ppermute | solution.py:76
  143.9 1.4 attend.15
  145.3 2.6 %collective-permute-start.27 = (bf16[6,128,256]{2,1,0:T(8,128)(2,1)S(1)}, bf16[6,128,256]{2,1,0:T(8,128)(2,1)S(1)}, u32[]{:S(2)}, u32[]{:S(2)}) collective-permute-start(bf16[6,128,256]{2,1,0:T(8,128)(2,1)S(1)} %attend.15), channel_id=1, source_target_pairs={{0,1},{1,0},{2,3},{3,2},{4,5},{5,4},{6,7},{7,6},{8,9},{9,8},{10,11... | collective-permute-start | bytes 1179656 | tf_op jit(solution)/shard_map/ppermute | solution.py:66
  147.9 1.4 attend.14
  149.3 0.1 convert_add_fusion
  149.4 0.1 fusion
  149.5 12.8 %all_to_all.19 = bf16[16,48,128]{2,1,0:T(8,128)(2,1)S(1)} all-to-all(bf16[16,48,128]{2,1,0:T(8,128)(2,1)S(1)} %bitcast.67), channel_id=1, replica_groups=mesh['seq'=16,'bal'=32] {'seq'}, dimensions={0} | all-to-all | bytes 393216 | tf_op jit(solution)/shard_map/all_to_all | solution.py:367
  162.3 0.7 copy_bitcast_fusion
  (25 shorter events, 0.1 us)
Async XLA Ops:
  0.0 81.0 %copy-start = (s32[1,192,64]{1,2,0:T(8,128)S(1)}, s32[1,192,64]{1,2,0:T(8,128)}, u32[]{:S(2)}) copy-start(s32[1,192,64]{1,2,0:T(8,128)} %param.10) | copy-start | bytes 147460
  0.0 37.7 %copy-start.1 = (bf16[3072,1,3,128]{3,0,2,1:T(8,128)(2,1)S(1)}, bf16[3072,1,3,128]{3,0,2,1:T(8,128)(2,1)}, u32[]{:S(2)}) copy-start(bf16[3072,1,3,128]{3,0,2,1:T(8,128)(2,1)} %param.7) | copy-start | bytes 7077892
  0.0 12.8 %collective-permute-start.1 = (bf16[48,3072]{1,0:T(8,128)(2,1)}, bf16[48,3072]{1,0:T(8,128)(2,1)S(1)}, u32[]{:S(2)}, u32[]{:S(2)}) collective-permute-start(bf16[48,3072]{1,0:T(8,128)(2,1)} %refs_0_.1), channel_id=1, source_target_pairs={{0,96},{32,0},{64,32},{96,64},{128,224},{160,128},{192,160},{224,1... | collective-permute-start | bytes 884744 | tf_op jit(solution)/shard_map/ppermute | solution.py:35
  5.6 12.3 %collective-permute-start = (bf16[48,3072]{1,0:T(8,128)(2,1)}, bf16[48,3072]{1,0:T(8,128)(2,1)S(1)}, u32[]{:S(2)}, u32[]{:S(2)}) collective-permute-start(bf16[48,3072]{1,0:T(8,128)(2,1)} %refs_0_.1), channel_id=1, source_target_pairs={{0,32},{32,64},{64,96},{96,0},{128,160},{160,192},{192,224},{224,1... | collective-permute-start | bytes 884744 | tf_op jit(solution)/shard_map/ppermute | solution.py:35
  7.5 13.3 %collective-permute-start.4 = (bf16[48,3072]{1,0:T(8,128)(2,1)}, bf16[48,3072]{1,0:T(8,128)(2,1)S(1)}, u32[]{:S(2)}, u32[]{:S(2)}) collective-permute-start(bf16[48,3072]{1,0:T(8,128)(2,1)} %refs_0_.1), channel_id=1, source_target_pairs={{0,64},{32,96},{64,0},{96,32},{128,192},{160,224},{192,128},{224,1... | collective-permute-start | bytes 884744 | tf_op jit(solution)/shard_map/ppermute | solution.py:35
  11.1 1.0 copy-start.2
  18.0 12.7 %collective-permute-start.2 = (bf16[96,3072]{1,0:T(8,128)(2,1)S(1)}, bf16[96,3072]{1,0:T(8,128)(2,1)}, u32[]{:S(2)}, u32[]{:S(2)}) collective-permute-start(bf16[96,3072]{1,0:T(8,128)(2,1)S(1)} %join.4.refs_0_), channel_id=1, source_target_pairs={{0,128},{32,160},{64,192},{96,224},{128,256},{160,288},{192,320},{... | collective-permute-start | bytes 1769480 | tf_op jit(solution)/shard_map/ppermute | solution.py:35
  21.7 11.2 %collective-permute-start.5 = (bf16[96,3072]{1,0:T(8,128)(2,1)}, bf16[96,3072]{1,0:T(8,128)(2,1)}, u32[]{:S(2)}, u32[]{:S(2)}) collective-permute-start(bf16[96,3072]{1,0:T(8,128)(2,1)} %join.5.refs_1_), channel_id=1, source_target_pairs={{0,384},{32,416},{64,448},{96,480},{128,0},{160,32},{192,64},{224,... | collective-permute-start | bytes 1769480 | tf_op jit(solution)/shard_map/ppermute | solution.py:35
  25.4 16.0 %collective-permute-start.7 = (bf16[96,3072]{1,0:T(8,128)(2,1)S(1)}, bf16[96,3072]{1,0:T(8,128)(2,1)}, u32[]{:S(2)}, u32[]{:S(2)}) collective-permute-start(bf16[96,3072]{1,0:T(8,128)(2,1)S(1)} %join.4.refs_0_), channel_id=1, source_target_pairs={{0,384},{32,416},{64,448},{96,480},{128,0},{160,32},{192,64},{224,... | collective-permute-start | bytes 1769480 | tf_op jit(solution)/shard_map/ppermute | solution.py:35
  28.3 13.1 %collective-permute-start.8 = (bf16[96,3072]{1,0:T(8,128)(2,1)}, bf16[96,3072]{1,0:T(8,128)(2,1)}, u32[]{:S(2)}, u32[]{:S(2)}) collective-permute-start(bf16[96,3072]{1,0:T(8,128)(2,1)} %join.5.refs_1_), channel_id=1, source_target_pairs={{0,128},{32,160},{64,192},{96,224},{128,256},{160,288},{192,320},{... | collective-permute-start | bytes 1769480 | tf_op jit(solution)/shard_map/ppermute | solution.py:35
  30.7 16.3 %collective-permute-start.3 = (bf16[96,3072]{1,0:T(8,128)(2,1)}, bf16[96,3072]{1,0:T(8,128)(2,1)}, u32[]{:S(2)}, u32[]{:S(2)}) collective-permute-start(bf16[96,3072]{1,0:T(8,128)(2,1)} %collective-permute-done.2.refs_2_), channel_id=1, source_target_pairs={{0,128},{32,160},{64,192},{96,224},{128,256},{160,288},{192,320},{... | collective-permute-start | bytes 1769480 | tf_op jit(solution)/shard_map/ppermute | solution.py:35
  32.9 14.1 %collective-permute-start.6 = (bf16[96,3072]{1,0:T(8,128)(2,1)}, bf16[96,3072]{1,0:T(8,128)(2,1)}, u32[]{:S(2)}, u32[]{:S(2)}) collective-permute-start(bf16[96,3072]{1,0:T(8,128)(2,1)} %collective-permute-done.5.refs_3_), channel_id=1, source_target_pairs={{0,384},{32,416},{64,448},{96,480},{128,0},{160,32},{192,64},{224,... | collective-permute-start | bytes 1769480 | tf_op jit(solution)/shard_map/ppermute | solution.py:35
  47.1 24.3 %copy-start.3 = (s32[1,192]{1,0:T(1,128)S(1)}, s32[1,192]{1,0:T(1,128)}, u32[]{:S(2)}) copy-start(s32[1,192]{1,0:T(1,128)} %param.11) | copy-start | bytes 2308
  49.9 16.8 %collective-permute-start.10 = (bf16[768,256]{1,0:T(8,128)(2,1)}, bf16[768,256]{1,0:T(8,128)(2,1)S(1)}, u32[]{:S(2)}, u32[]{:S(2)}) collective-permute-start(bf16[768,256]{1,0:T(8,128)(2,1)} %get-tuple-element.45), channel_id=1, source_target_pairs={{0,1},{1,0},{2,3},{3,2},{4,5},{5,4},{6,7},{7,6},{8,9},{9,8},{10,11... | collective-permute-start | bytes 1179656 | tf_op jit(solution)/shard_map/ppermute | solution.py:66
  55.6 16.1 %collective-permute-start.9 = (bf16[768,256]{1,0:T(8,128)(2,1)}, bf16[768,256]{1,0:T(8,128)(2,1)S(1)}, u32[]{:S(2)}, u32[]{:S(2)}) collective-permute-start(bf16[768,256]{1,0:T(8,128)(2,1)} %get-tuple-element.45), channel_id=1, source_target_pairs={{0,2},{1,31},{2,4},{3,1},{4,6},{5,3},{6,8},{7,5},{8,10},{9,7},{10,... | collective-permute-start | bytes 1179656 | tf_op jit(solution)/shard_map/ppermute | solution.py:76
  66.8 9.9 %collective-permute-start.13 = (bf16[768,256]{1,0:T(8,128)(2,1)S(1)}, bf16[768,256]{1,0:T(8,128)(2,1)S(1)}, u32[]{:S(2)}, u32[]{:S(2)}) collective-permute-start(bf16[768,256]{1,0:T(8,128)(2,1)S(1)} %collective-permute-done.10), channel_id=1, source_target_pairs={{0,2},{1,31},{2,4},{3,1},{4,6},{5,3},{6,8},{7,5},{8,10},{9,7},{10,... | collective-permute-start | bytes 1179656 | tf_op jit(solution)/shard_map/ppermute | solution.py:76
  69.4 3.3 %collective-permute-start.11 = (bf16[768,128]{1,0:T(8,128)(2,1)S(1)}, bf16[768,128]{1,0:T(8,128)(2,1)S(1)}, u32[]{:S(2)}, u32[]{:S(2)}) collective-permute-start(bf16[768,128]{1,0:T(8,128)(2,1)S(1)} %get-tuple-element.47), channel_id=1, source_target_pairs={{0,1},{1,0},{2,3},{3,2},{4,5},{5,4},{6,7},{7,6},{8,9},{9,8},{10,11... | collective-permute-start | bytes 589832 | tf_op jit(solution)/shard_map/ppermute | solution.py:66
  72.7 11.1 %collective-permute-start.12 = (bf16[768,256]{1,0:T(8,128)(2,1)S(1)}, bf16[768,256]{1,0:T(8,128)(2,1)S(1)}, u32[]{:S(2)}, u32[]{:S(2)}) collective-permute-start(bf16[768,256]{1,0:T(8,128)(2,1)S(1)} %collective-permute-done.9), channel_id=1, source_target_pairs={{0,2},{1,31},{2,4},{3,1},{4,6},{5,3},{6,8},{7,5},{8,10},{9,7},{10,... | collective-permute-start | bytes 1179656 | tf_op jit(solution)/shard_map/ppermute | solution.py:76
  76.7 9.7 %collective-permute-start.14 = (bf16[768,256]{1,0:T(8,128)(2,1)S(1)}, bf16[768,256]{1,0:T(8,128)(2,1)S(1)}, u32[]{:S(2)}, u32[]{:S(2)}) collective-permute-start(bf16[768,256]{1,0:T(8,128)(2,1)S(1)} %collective-permute-done.13), channel_id=1, source_target_pairs={{0,2},{1,31},{2,4},{3,1},{4,6},{5,3},{6,8},{7,5},{8,10},{9,7},{10,... | collective-permute-start | bytes 1179656 | tf_op jit(solution)/shard_map/ppermute | solution.py:76
  83.8 10.0 %collective-permute-start.15 = (bf16[768,256]{1,0:T(8,128)(2,1)S(1)}, bf16[768,256]{1,0:T(8,128)(2,1)S(1)}, u32[]{:S(2)}, u32[]{:S(2)}) collective-permute-start(bf16[768,256]{1,0:T(8,128)(2,1)S(1)} %collective-permute-done.12), channel_id=1, source_target_pairs={{0,2},{1,31},{2,4},{3,1},{4,6},{5,3},{6,8},{7,5},{8,10},{9,7},{10,... | collective-permute-start | bytes 1179656 | tf_op jit(solution)/shard_map/ppermute | solution.py:76
  86.4 10.4 %collective-permute-start.17 = (bf16[768,256]{1,0:T(8,128)(2,1)S(1)}, bf16[768,256]{1,0:T(8,128)(2,1)S(1)}, u32[]{:S(2)}, u32[]{:S(2)}) collective-permute-start(bf16[768,256]{1,0:T(8,128)(2,1)S(1)} %collective-permute-done.14), channel_id=1, source_target_pairs={{0,2},{1,31},{2,4},{3,1},{4,6},{5,3},{6,8},{7,5},{8,10},{9,7},{10,... | collective-permute-start | bytes 1179656 | tf_op jit(solution)/shard_map/ppermute | solution.py:76
  93.8 9.0 %collective-permute-start.16 = (bf16[768,256]{1,0:T(8,128)(2,1)S(1)}, bf16[768,256]{1,0:T(8,128)(2,1)S(1)}, u32[]{:S(2)}, u32[]{:S(2)}) collective-permute-start(bf16[768,256]{1,0:T(8,128)(2,1)S(1)} %collective-permute-done.15), channel_id=1, source_target_pairs={{0,2},{1,31},{2,4},{3,1},{4,6},{5,3},{6,8},{7,5},{8,10},{9,7},{10,... | collective-permute-start | bytes 1179656 | tf_op jit(solution)/shard_map/ppermute | solution.py:76
  96.8 10.0 %collective-permute-start.19 = (bf16[768,256]{1,0:T(8,128)(2,1)S(1)}, bf16[768,256]{1,0:T(8,128)(2,1)S(1)}, u32[]{:S(2)}, u32[]{:S(2)}) collective-permute-start(bf16[768,256]{1,0:T(8,128)(2,1)S(1)} %collective-permute-done.17), channel_id=1, source_target_pairs={{0,2},{1,31},{2,4},{3,1},{4,6},{5,3},{6,8},{7,5},{8,10},{9,7},{10,... | collective-permute-start | bytes 1179656 | tf_op jit(solution)/shard_map/ppermute | solution.py:76
  102.8 9.2 %collective-permute-start.18 = (bf16[768,256]{1,0:T(8,128)(2,1)S(1)}, bf16[768,256]{1,0:T(8,128)(2,1)S(1)}, u32[]{:S(2)}, u32[]{:S(2)}) collective-permute-start(bf16[768,256]{1,0:T(8,128)(2,1)S(1)} %collective-permute-done.16), channel_id=1, source_target_pairs={{0,2},{1,31},{2,4},{3,1},{4,6},{5,3},{6,8},{7,5},{8,10},{9,7},{10,... | collective-permute-start | bytes 1179656 | tf_op jit(solution)/shard_map/ppermute | solution.py:76
  106.8 9.0 %collective-permute-start.21 = (bf16[768,256]{1,0:T(8,128)(2,1)S(1)}, bf16[768,256]{1,0:T(8,128)(2,1)S(1)}, u32[]{:S(2)}, u32[]{:S(2)}) collective-permute-start(bf16[768,256]{1,0:T(8,128)(2,1)S(1)} %collective-permute-done.19), channel_id=1, source_target_pairs={{0,2},{1,31},{2,4},{3,1},{4,6},{5,3},{6,8},{7,5},{8,10},{9,7},{10,... | collective-permute-start | bytes 1179656 | tf_op jit(solution)/shard_map/ppermute | solution.py:76
  112.0 9.7 %collective-permute-start.20 = (bf16[768,256]{1,0:T(8,128)(2,1)S(1)}, bf16[768,256]{1,0:T(8,128)(2,1)S(1)}, u32[]{:S(2)}, u32[]{:S(2)}) collective-permute-start(bf16[768,256]{1,0:T(8,128)(2,1)S(1)} %collective-permute-done.18), channel_id=1, source_target_pairs={{0,2},{1,31},{2,4},{3,1},{4,6},{5,3},{6,8},{7,5},{8,10},{9,7},{10,... | collective-permute-start | bytes 1179656 | tf_op jit(solution)/shard_map/ppermute | solution.py:76
  115.8 9.5 %collective-permute-start.23 = (bf16[768,256]{1,0:T(8,128)(2,1)S(1)}, bf16[768,256]{1,0:T(8,128)(2,1)S(1)}, u32[]{:S(2)}, u32[]{:S(2)}) collective-permute-start(bf16[768,256]{1,0:T(8,128)(2,1)S(1)} %collective-permute-done.21), channel_id=1, source_target_pairs={{0,2},{1,31},{2,4},{3,1},{4,6},{5,3},{6,8},{7,5},{8,10},{9,7},{10,... | collective-permute-start | bytes 1179656 | tf_op jit(solution)/shard_map/ppermute | solution.py:76
  121.8 9.2 %collective-permute-start.22 = (bf16[768,256]{1,0:T(8,128)(2,1)S(1)}, bf16[768,256]{1,0:T(8,128)(2,1)S(1)}, u32[]{:S(2)}, u32[]{:S(2)}) collective-permute-start(bf16[768,256]{1,0:T(8,128)(2,1)S(1)} %collective-permute-done.20), channel_id=1, source_target_pairs={{0,2},{1,31},{2,4},{3,1},{4,6},{5,3},{6,8},{7,5},{8,10},{9,7},{10,... | collective-permute-start | bytes 1179656 | tf_op jit(solution)/shard_map/ppermute | solution.py:76
  125.3 9.7 %collective-permute-start.25 = (bf16[768,256]{1,0:T(8,128)(2,1)S(1)}, bf16[768,256]{1,0:T(8,128)(2,1)S(1)}, u32[]{:S(2)}, u32[]{:S(2)}) collective-permute-start(bf16[768,256]{1,0:T(8,128)(2,1)S(1)} %collective-permute-done.23), channel_id=1, source_target_pairs={{0,2},{1,31},{2,4},{3,1},{4,6},{5,3},{6,8},{7,5},{8,10},{9,7},{10,... | collective-permute-start | bytes 1179656 | tf_op jit(solution)/shard_map/ppermute | solution.py:76
  131.0 10.2 %collective-permute-start.24 = (bf16[768,256]{1,0:T(8,128)(2,1)S(1)}, bf16[768,256]{1,0:T(8,128)(2,1)S(1)}, u32[]{:S(2)}, u32[]{:S(2)}) collective-permute-start(bf16[768,256]{1,0:T(8,128)(2,1)S(1)} %collective-permute-done.22), channel_id=1, source_target_pairs={{1,31},{3,1},{5,3},{7,5},{9,7},{11,9},{13,11},{15,13},{17,15},{19,... | collective-permute-start | bytes 1179656 | tf_op jit(solution)/shard_map/ppermute | solution.py:76
  135.0 8.9 %collective-permute-start.26 = (bf16[768,256]{1,0:T(8,128)(2,1)S(1)}, bf16[768,256]{1,0:T(8,128)(2,1)S(1)}, u32[]{:S(2)}, u32[]{:S(2)}) collective-permute-start(bf16[768,256]{1,0:T(8,128)(2,1)S(1)} %collective-permute-done.25), channel_id=1, source_target_pairs={{1,31},{3,1},{5,3},{7,5},{9,7},{11,9},{13,11},{15,13},{17,15},{19,... | collective-permute-start | bytes 1179656 | tf_op jit(solution)/shard_map/ppermute | solution.py:76
  145.3 4.0 %collective-permute-start.27 = (bf16[6,128,256]{2,1,0:T(8,128)(2,1)S(1)}, bf16[6,128,256]{2,1,0:T(8,128)(2,1)S(1)}, u32[]{:S(2)}, u32[]{:S(2)}) collective-permute-start(bf16[6,128,256]{2,1,0:T(8,128)(2,1)S(1)} %attend.15), channel_id=1, source_target_pairs={{0,1},{1,0},{2,3},{3,2},{4,5},{5,4},{6,7},{7,6},{8,9},{9,8},{10,11... | collective-permute-start | bytes 1179656 | tf_op jit(solution)/shard_map/ppermute | solution.py:66

commit v17 on v14

--- a/solution.py
+++ b/solution.py
@@ -343,7 +343,7 @@
         if step == 1:
             queries, other[0] = lax.optimization_barrier((queries, other[0]))
             other_queries = swap_cores(queries)
-            same[1], other_queries = lax.optimization_barrier((same[1], other_queries))
+            other[1], other_queries = lax.optimization_barrier((other[1], other_queries))
         if step == 2:
             key_tiles, other[1] = lax.optimization_barrier((key_tiles, other[1]))
             pairs, counts = list_pairs(CALLS, key_tiles[0], key_counts, place, slots)

time: 163 us -> 164 us (level)
  starting transfers between devices: 100 us -> 108 us
  Pallas kernels: 30.3 us -> 24 us
    ppermute x16, starting transfers between devices: 61.1 us -> 67.4 us  [pass_on(): return lax.ppermute(block, 'bal', pairs)]
    pallas_call x8, Pallas kernels: 17.2 us -> 12.2 us  [attend(): pl.pallas_call(functools.partial(attend_kernel, scale, call, part, blocks...]
  transfers between devices with their start and end apart: 28 -> 28, of which waited for: 12 -> 9; matrix products, arithmetic and copies ran while one was open for 1% -> 1% of each run, Pallas kernels for 16% -> 12%
where the time goes in v17:
time: 164 us; the launch traced here: 163 us
  starting transfers between devices  108 us (66%)
  Pallas kernels  24 us (15%)
  waiting for transfers between devices  16.7 us (10%)
  blocking collectives  10.3 us (6%)
  local copies, waits for them, and re-layouts  2.67 us (2%)
    ppermute x16, starting transfers between devices, pass_on(): return lax.ppermute(block, 'bal', pairs)  67.4 us
    ppermute x9, starting transfers between devices, send(): return lax.ppermute(block, MESH_AXES, plane_perm(phase, shift))  29.3 us
    pallas_call x8, Pallas kernels, attend(): pl.pallas_call(functools.partial(attend_kernel, scale, call, part, blocks...  12.2 us
    ppermute x3, starting transfers between devices, swap_cores(): return lax.ppermute(block, 'bal', [(at, at ^ 1) for at in range(32)])  11.1 us
    all_to_all x1, blocking collectives, on_device(): lax.all_to_all(result.reshape(slots * TILE, HEAD), 'seq', split_axis=0, c...  10.3 us
    ppermute x9, waiting for transfers between devices, send(): return lax.ppermute(block, MESH_AXES, plane_perm(phase, shift))  9.11 us
    pallas_call x3, Pallas kernels, project(): pl.pallas_call(functools.partial(project_kernel, shares), out_shape=(jax....  8.07 us
    ppermute x16, waiting for transfers between devices, pass_on(): return lax.ppermute(block, 'bal', pairs)  5.79 us
  transfers between devices with their start and end apart: 28, of which 9 were waited for; matrix products, arithmetic and copies ran while one was open for 1% of the time, Pallas kernels for 12%

profile of v17, /device:TPU:1, one launch (start us, length us, event | category | flops | bytes accessed | tf_op | source)
XLA Modules:
  0.0 163.0 jit_solution(1187848047814070169)
XLA Ops:
  0.0 5.6 %collective-permute-start.1 = (bf16[48,3072]{1,0:T(8,128)(2,1)}, bf16[48,3072]{1,0:T(8,128)(2,1)S(1)}, u32[]{:S(2)}, u32[]{:S(2)}) collective-permute-start(bf16[48,3072]{1,0:T(8,128)(2,1)} %refs_0_.1), channel_id=1, source_target_pairs={{0,96},{32,0},{64,32},{96,64},{128,224},{160,128},{192,160},{224,1... | collective-permute-start | bytes 884744 | tf_op jit(solution)/shard_map/ppermute | solution.py:35
  5.6 1.9 %collective-permute-start = (bf16[48,3072]{1,0:T(8,128)(2,1)}, bf16[48,3072]{1,0:T(8,128)(2,1)S(1)}, u32[]{:S(2)}, u32[]{:S(2)}) collective-permute-start(bf16[48,3072]{1,0:T(8,128)(2,1)} %refs_0_.1), channel_id=1, source_target_pairs={{0,32},{32,64},{64,96},{96,0},{128,160},{160,192},{192,224},{224,1... | collective-permute-start | bytes 884744 | tf_op jit(solution)/shard_map/ppermute | solution.py:35
  7.5 3.5 %collective-permute-start.4 = (bf16[48,3072]{1,0:T(8,128)(2,1)}, bf16[48,3072]{1,0:T(8,128)(2,1)S(1)}, u32[]{:S(2)}, u32[]{:S(2)}) collective-permute-start(bf16[48,3072]{1,0:T(8,128)(2,1)} %refs_0_.1), channel_id=1, source_target_pairs={{0,64},{32,96},{64,0},{96,32},{128,192},{160,224},{192,128},{224,1... | collective-permute-start | bytes 884744 | tf_op jit(solution)/shard_map/ppermute | solution.py:35
  11.1 1.0 copy-done.4
  12.1 0.1 join.3.refs_1_
  12.1 0.7 pad_maximum_fusion.1.refs_5_.refs_3_
  12.8 0.0 collective-permute-done.1.refs_0_
  12.8 5.1 %collective-permute-done.refs_0_ = bf16[48,3072]{1,0:T(8,128)(2,1)S(1)} collective-permute-done((bf16[48,3072]{1,0:T(8,128)(2,1)}, bf16[48,3072]{1,0:T(8,128)(2,1)S(1)}, u32[]{:S(2)}, u32[]{:S(2)}) %collective-permute-start) | collective-permute-done | bytes 294944 | tf_op jit(solution)/shard_map/ppermute | solution.py:35
  17.9 0.1 join.4.refs_0_
  18.0 2.8 %collective-permute-start.2 = (bf16[96,3072]{1,0:T(8,128)(2,1)S(1)}, bf16[96,3072]{1,0:T(8,128)(2,1)}, u32[]{:S(2)}, u32[]{:S(2)}) collective-permute-start(bf16[96,3072]{1,0:T(8,128)(2,1)S(1)} %join.4.refs_0_), channel_id=1, source_target_pairs={{0,128},{32,160},{64,192},{96,224},{128,256},{160,288},{192,320},{... | collective-permute-start | bytes 1769480 | tf_op jit(solution)/shard_map/ppermute | solution.py:35
  20.9 0.8 join.5.refs_1_
  21.7 3.7 %collective-permute-start.5 = (bf16[96,3072]{1,0:T(8,128)(2,1)}, bf16[96,3072]{1,0:T(8,128)(2,1)}, u32[]{:S(2)}, u32[]{:S(2)}) collective-permute-start(bf16[96,3072]{1,0:T(8,128)(2,1)} %join.5.refs_1_), channel_id=1, source_target_pairs={{0,384},{32,416},{64,448},{96,480},{128,0},{160,32},{192,64},{224,... | collective-permute-start | bytes 1769480 | tf_op jit(solution)/shard_map/ppermute | solution.py:35
  25.4 2.9 %collective-permute-start.7 = (bf16[96,3072]{1,0:T(8,128)(2,1)S(1)}, bf16[96,3072]{1,0:T(8,128)(2,1)}, u32[]{:S(2)}, u32[]{:S(2)}) collective-permute-start(bf16[96,3072]{1,0:T(8,128)(2,1)S(1)} %join.4.refs_0_), channel_id=1, source_target_pairs={{0,384},{32,416},{64,448},{96,480},{128,0},{160,32},{192,64},{224,... | collective-permute-start | bytes 1769480 | tf_op jit(solution)/shard_map/ppermute | solution.py:35
  28.3 2.4 %collective-permute-start.8 = (bf16[96,3072]{1,0:T(8,128)(2,1)}, bf16[96,3072]{1,0:T(8,128)(2,1)}, u32[]{:S(2)}, u32[]{:S(2)}) collective-permute-start(bf16[96,3072]{1,0:T(8,128)(2,1)} %join.5.refs_1_), channel_id=1, source_target_pairs={{0,128},{32,160},{64,192},{96,224},{128,256},{160,288},{192,320},{... | collective-permute-start | bytes 1769480 | tf_op jit(solution)/shard_map/ppermute | solution.py:35
  30.7 0.0 collective-permute-done.2.refs_2_
  30.7 1.9 %collective-permute-start.3 = (bf16[96,3072]{1,0:T(8,128)(2,1)}, bf16[96,3072]{1,0:T(8,128)(2,1)}, u32[]{:S(2)}, u32[]{:S(2)}) collective-permute-start(bf16[96,3072]{1,0:T(8,128)(2,1)} %collective-permute-done.2.refs_2_), channel_id=1, source_target_pairs={{0,128},{32,160},{64,192},{96,224},{128,256},{160,288},{192,320},{... | collective-permute-start | bytes 1769480 | tf_op jit(solution)/shard_map/ppermute | solution.py:35
  32.6 0.3 collective-permute-done.5.refs_3_
  32.9 4.6 %collective-permute-start.6 = (bf16[96,3072]{1,0:T(8,128)(2,1)}, bf16[96,3072]{1,0:T(8,128)(2,1)}, u32[]{:S(2)}, u32[]{:S(2)}) collective-permute-start(bf16[96,3072]{1,0:T(8,128)(2,1)} %collective-permute-done.5.refs_3_), channel_id=1, source_target_pairs={{0,384},{32,416},{64,448},{96,480},{128,0},{160,32},{192,64},{224,... | collective-permute-start | bytes 1769480 | tf_op jit(solution)/shard_map/ppermute | solution.py:35
  37.6 0.1 stack.27.place
  37.7 3.3 %project.3 = (bf16[768,128]{1,0:T(8,128)(2,1)S(1)}, bf16[768,256]{1,0:T(8,128)(2,1)S(1)}) custom-call(s32[6]{0:T(128)S(1)} %stack.27.place, bf16[96,3072]{1,0:T(8,128)(2,1)S(1)} %join.4.refs_0_, bf16[96,3072]{1,0:T(8,128)(2,1)} %join.5.refs_1_, bf16[96,3072]{1,0:T(8,128)(2,1)} %collective-permute-done.2.refs_2_, ...), custom_call_target="tpu_custom_call" | custom-call | tf_op jit(solution)/shard_map/project/pallas_call | solution.py:117
  41.0 2.4 %project.4 = (bf16[768,128]{1,0:T(8,128)(2,1)S(1)}, bf16[768,256]{1,0:T(8,128)(2,1)S(1)}) custom-call(s32[6]{0:T(128)S(1)} %stack.27.place, bf16[96,3072]{1,0:T(8,128)(2,1)} %collective-permute-done.7.refs_0_, bf16[96,3072]{1,0:T(8,128)(2,1)} %collective-permute-done.8.refs_1_, ...), custom_call_target="tpu_custom_call", output_to_operand_aliasing={{0}: (5, {}), {1}: (6, {})} | custom-call | tf_op jit(solution)/shard_map/project/pallas_call | solution.py:117
  43.4 3.6 %collective-permute-done.3.refs_0_ = bf16[96,3072]{1,0:T(8,128)(2,1)} collective-permute-done((bf16[96,3072]{1,0:T(8,128)(2,1)}, bf16[96,3072]{1,0:T(8,128)(2,1)}, u32[]{:S(2)}, u32[]{:S(2)}) %collective-permute-start.3) | collective-permute-done | bytes 589856 | tf_op jit(solution)/shard_map/ppermute | solution.py:35
  47.1 2.4 %project.5 = (bf16[768,128]{1,0:T(8,128)(2,1)S(1)}, bf16[768,256]{1,0:T(8,128)(2,1)S(1)}) custom-call(s32[6]{0:T(128)S(1)} %stack.27.place, bf16[96,3072]{1,0:T(8,128)(2,1)} %collective-permute-done.3.refs_0_, bf16[96,3072]{1,0:T(8,128)(2,1)} %collective-permute-done.6.refs_1_, ...), custom_call_target="tpu_custom_call", output_to_operand_aliasing={{0}: (5, {}), {1}: (6, {})} | custom-call | tf_op jit(solution)/shard_map/project/pallas_call | solution.py:117
  49.4 5.7 %collective-permute-start.11 = (bf16[768,256]{1,0:T(8,128)(2,1)S(1)}, bf16[768,256]{1,0:T(8,128)(2,1)S(1)}, u32[]{:S(2)}, u32[]{:S(2)}) collective-permute-start(bf16[768,256]{1,0:T(8,128)(2,1)S(1)} %get-tuple-element.45), channel_id=1, source_target_pairs={{0,1},{1,0},{2,3},{3,2},{4,5},{5,4},{6,7},{7,6},{8,9},{9,8},{10,11... | collective-permute-start | bytes 1179656 | tf_op jit(solution)/shard_map/ppermute | solution.py:66
  55.1 11.1 %collective-permute-start.9 = (bf16[768,256]{1,0:T(8,128)(2,1)S(1)}, bf16[768,256]{1,0:T(8,128)(2,1)S(1)}, u32[]{:S(2)}, u32[]{:S(2)}) collective-permute-start(bf16[768,256]{1,0:T(8,128)(2,1)S(1)} %get-tuple-element.45), channel_id=1, source_target_pairs={{0,2},{1,31},{2,4},{3,1},{4,6},{5,3},{6,8},{7,5},{8,10},{9,7},{10,... | collective-permute-start | bytes 1179656 | tf_op jit(solution)/shard_map/ppermute | solution.py:76
  66.3 0.8 copy-done.2
  67.0 2.8 %collective-permute-start.12 = (bf16[768,256]{1,0:T(8,128)(2,1)S(1)}, bf16[768,256]{1,0:T(8,128)(2,1)S(1)}, u32[]{:S(2)}, u32[]{:S(2)}) collective-permute-start(bf16[768,256]{1,0:T(8,128)(2,1)S(1)} %collective-permute-done.11), channel_id=1, source_target_pairs={{0,2},{1,31},{2,4},{3,1},{4,6},{5,3},{6,8},{7,5},{8,10},{9,7},{10,... | collective-permute-start | bytes 1179656 | tf_op jit(solution)/shard_map/ppermute | solution.py:76
  69.8 1.2 collective-permute-done.9
  71.0 5.0 %collective-permute-start.10 = (bf16[768,256]{1,0:T(8,128)(2,1)S(1)}, bf16[768,256]{1,0:T(8,128)(2,1)S(1)}, u32[]{:S(2)}, u32[]{:S(2)}) collective-permute-start(bf16[768,256]{1,0:T(8,128)(2,1)S(1)} %collective-permute-done.9), channel_id=1, source_target_pairs={{0,2},{1,31},{2,4},{3,1},{4,6},{5,3},{6,8},{7,5},{8,10},{9,7},{10,... | collective-permute-start | bytes 1179656 | tf_op jit(solution)/shard_map/ppermute | solution.py:76
  76.0 1.9 %collective-permute-start.13 = (bf16[768,128]{1,0:T(8,128)(2,1)S(1)}, bf16[768,128]{1,0:T(8,128)(2,1)S(1)}, u32[]{:S(2)}, u32[]{:S(2)}) collective-permute-start(bf16[768,128]{1,0:T(8,128)(2,1)S(1)} %get-tuple-element.47), channel_id=1, source_target_pairs={{0,1},{1,0},{2,3},{3,2},{4,5},{5,4},{6,7},{7,6},{8,9},{9,8},{10,11... | collective-permute-start | bytes 589832 | tf_op jit(solution)/shard_map/ppermute | solution.py:66
  77.9 0.1 constant_dynamic-slice_fusion.counts
  78.0 1.3 collective-permute-done.13
  79.3 2.7 %collective-permute-start.14 = (bf16[768,256]{1,0:T(8,128)(2,1)S(1)}, bf16[768,256]{1,0:T(8,128)(2,1)S(1)}, u32[]{:S(2)}, u32[]{:S(2)}) collective-permute-start(bf16[768,256]{1,0:T(8,128)(2,1)S(1)} %collective-permute-done.12), channel_id=1, source_target_pairs={{0,2},{1,31},{2,4},{3,1},{4,6},{5,3},{6,8},{7,5},{8,10},{9,7},{10,... | collective-permute-start | bytes 1179656 | tf_op jit(solution)/shard_map/ppermute | solution.py:76
  82.0 0.1 dynamic-slice_bitcast_fusion.tiles
  82.1 2.8 %lists.1 = (s32[8,384]{1,0:T(8,128)S(1)}, s32[1,8]{1,0:T(1,128)S(1)}) custom-call(s32[6]{0:T(128)S(1)} %stack.27.place, s32[64,12]{1,0:T(8,128)S(1)} %dynamic-slice_bitcast_fusion.tiles, s32[1,12]{1,0:T(1,128)S(1)} %constant_dynamic-slice_fusion.counts), custom_call_target="tpu_custom_call" | custom-call | tf_op jit(solution)/shard_map/lists/pallas_call | solution.py:264
  84.9 2.4 %collective-permute-start.15 = (bf16[768,256]{1,0:T(8,128)(2,1)S(1)}, bf16[768,256]{1,0:T(8,128)(2,1)S(1)}, u32[]{:S(2)}, u32[]{:S(2)}) collective-permute-start(bf16[768,256]{1,0:T(8,128)(2,1)S(1)} %collective-permute-done.10), channel_id=1, source_target_pairs={{0,2},{1,31},{2,4},{3,1},{4,6},{5,3},{6,8},{7,5},{8,10},{9,7},{10,... | collective-permute-start | bytes 1179656 | tf_op jit(solution)/shard_map/ppermute | solution.py:76
  87.4 0.7 collective-permute-done.14
  88.1 3.6 %collective-permute-start.17 = (bf16[768,256]{1,0:T(8,128)(2,1)S(1)}, bf16[768,256]{1,0:T(8,128)(2,1)S(1)}, u32[]{:S(2)}, u32[]{:S(2)}) collective-permute-start(bf16[768,256]{1,0:T(8,128)(2,1)S(1)} %collective-permute-done.14), channel_id=1, source_target_pairs={{0,2},{1,31},{2,4},{3,1},{4,6},{5,3},{6,8},{7,5},{8,10},{9,7},{10,... | collective-permute-start | bytes 1179656 | tf_op jit(solution)/shard_map/ppermute | solution.py:76
  91.8 1.9 %attend.8.refs_2_ = f32[13,128,256]{2,1,0:T(8,128)S(1)} custom-call(s32[6]{0:T(128)S(1)} %stack.27.place, s32[8,384]{1,0:T(8,128)S(1)} %get-tuple-element.52.pairs, s32[1,8]{1,0:T(1,128)S(1)} %get-tuple-element.53.counts, bf16[12,128,128]{2,1,0:T(8,128)(2,1)S(1)} %bitcast.42, bf16[6,128,256]{2,1,0:T(8,128)(2,1)S(1)} %bitcast.41, ...), custom_call_target="tpu_custom_call" | custom-call | flops 5000000000 | bytes 5000000 | tf_op jit(solution)/shard_map/attend/pallas_call | solution.py:192
  93.7 3.3 %collective-permute-start.16 = (bf16[768,256]{1,0:T(8,128)(2,1)S(1)}, bf16[768,256]{1,0:T(8,128)(2,1)S(1)}, u32[]{:S(2)}, u32[]{:S(2)}) collective-permute-start(bf16[768,256]{1,0:T(8,128)(2,1)S(1)} %collective-permute-done.15), channel_id=1, source_target_pairs={{0,2},{1,31},{2,4},{3,1},{4,6},{5,3},{6,8},{7,5},{8,10},{9,7},{10,... | collective-permute-start | bytes 1179656 | tf_op jit(solution)/shard_map/ppermute | solution.py:76
  97.1 0.9 collective-permute-done.17
  97.9 3.5 %collective-permute-start.19 = (bf16[768,256]{1,0:T(8,128)(2,1)S(1)}, bf16[768,256]{1,0:T(8,128)(2,1)S(1)}, u32[]{:S(2)}, u32[]{:S(2)}) collective-permute-start(bf16[768,256]{1,0:T(8,128)(2,1)S(1)} %collective-permute-done.17), channel_id=1, source_target_pairs={{0,2},{1,31},{2,4},{3,1},{4,6},{5,3},{6,8},{7,5},{8,10},{9,7},{10,... | collective-permute-start | bytes 1179656 | tf_op jit(solution)/shard_map/ppermute | solution.py:76
  101.5 1.5 attend.9.refs_2_
  103.0 3.8 %collective-permute-start.18 = (bf16[768,256]{1,0:T(8,128)(2,1)S(1)}, bf16[768,256]{1,0:T(8,128)(2,1)S(1)}, u32[]{:S(2)}, u32[]{:S(2)}) collective-permute-start(bf16[768,256]{1,0:T(8,128)(2,1)S(1)} %collective-permute-done.16), channel_id=1, source_target_pairs={{0,2},{1,31},{2,4},{3,1},{4,6},{5,3},{6,8},{7,5},{8,10},{9,7},{10,... | collective-permute-start | bytes 1179656 | tf_op jit(solution)/shard_map/ppermute | solution.py:76
  106.8 4.4 %collective-permute-start.21 = (bf16[768,256]{1,0:T(8,128)(2,1)S(1)}, bf16[768,256]{1,0:T(8,128)(2,1)S(1)}, u32[]{:S(2)}, u32[]{:S(2)}) collective-permute-start(bf16[768,256]{1,0:T(8,128)(2,1)S(1)} %collective-permute-done.19), channel_id=1, source_target_pairs={{0,2},{1,31},{2,4},{3,1},{4,6},{5,3},{6,8},{7,5},{8,10},{9,7},{10,... | collective-permute-start | bytes 1179656 | tf_op jit(solution)/shard_map/ppermute | solution.py:76
  111.2 1.5 attend.10.refs_2_
  112.7 3.8 %collective-permute-start.20 = (bf16[768,256]{1,0:T(8,128)(2,1)S(1)}, bf16[768,256]{1,0:T(8,128)(2,1)S(1)}, u32[]{:S(2)}, u32[]{:S(2)}) collective-permute-start(bf16[768,256]{1,0:T(8,128)(2,1)S(1)} %collective-permute-done.18), channel_id=1, source_target_pairs={{0,2},{1,31},{2,4},{3,1},{4,6},{5,3},{6,8},{7,5},{8,10},{9,7},{10,... | collective-permute-start | bytes 1179656 | tf_op jit(solution)/shard_map/ppermute | solution.py:76
  116.5 4.4 %collective-permute-start.23 = (bf16[768,256]{1,0:T(8,128)(2,1)S(1)}, bf16[768,256]{1,0:T(8,128)(2,1)S(1)}, u32[]{:S(2)}, u32[]{:S(2)}) collective-permute-start(bf16[768,256]{1,0:T(8,128)(2,1)S(1)} %collective-permute-done.21), channel_id=1, source_target_pairs={{0,2},{1,31},{2,4},{3,1},{4,6},{5,3},{6,8},{7,5},{8,10},{9,7},{10,... | collective-permute-start | bytes 1179656 | tf_op jit(solution)/shard_map/ppermute | solution.py:76
  120.9 1.5 attend.11.refs_2_
  122.4 3.8 %collective-permute-start.22 = (bf16[768,256]{1,0:T(8,128)(2,1)S(1)}, bf16[768,256]{1,0:T(8,128)(2,1)S(1)}, u32[]{:S(2)}, u32[]{:S(2)}) collective-permute-start(bf16[768,256]{1,0:T(8,128)(2,1)S(1)} %collective-permute-done.20), channel_id=1, source_target_pairs={{0,2},{1,31},{2,4},{3,1},{4,6},{5,3},{6,8},{7,5},{8,10},{9,7},{10,... | collective-permute-start | bytes 1179656 | tf_op jit(solution)/shard_map/ppermute | solution.py:76
  126.2 4.4 %collective-permute-start.25 = (bf16[768,256]{1,0:T(8,128)(2,1)S(1)}, bf16[768,256]{1,0:T(8,128)(2,1)S(1)}, u32[]{:S(2)}, u32[]{:S(2)}) collective-permute-start(bf16[768,256]{1,0:T(8,128)(2,1)S(1)} %collective-permute-done.23), channel_id=1, source_target_pairs={{0,2},{1,31},{2,4},{3,1},{4,6},{5,3},{6,8},{7,5},{8,10},{9,7},{10,... | collective-permute-start | bytes 1179656 | tf_op jit(solution)/shard_map/ppermute | solution.py:76
  130.6 1.5 attend.12.refs_2_
  132.2 3.8 %collective-permute-start.24 = (bf16[768,256]{1,0:T(8,128)(2,1)S(1)}, bf16[768,256]{1,0:T(8,128)(2,1)S(1)}, u32[]{:S(2)}, u32[]{:S(2)}) collective-permute-start(bf16[768,256]{1,0:T(8,128)(2,1)S(1)} %collective-permute-done.22), channel_id=1, source_target_pairs={{1,31},{3,1},{5,3},{7,5},{9,7},{11,9},{13,11},{15,13},{17,15},{19,... | collective-permute-start | bytes 1179656 | tf_op jit(solution)/shard_map/ppermute | solution.py:76
  135.9 4.6 %collective-permute-start.26 = (bf16[768,256]{1,0:T(8,128)(2,1)S(1)}, bf16[768,256]{1,0:T(8,128)(2,1)S(1)}, u32[]{:S(2)}, u32[]{:S(2)}) collective-permute-start(bf16[768,256]{1,0:T(8,128)(2,1)S(1)} %collective-permute-done.25), channel_id=1, source_target_pairs={{1,31},{3,1},{5,3},{7,5},{9,7},{11,9},{13,11},{15,13},{17,15},{19,... | collective-permute-start | bytes 1179656 | tf_op jit(solution)/shard_map/ppermute | solution.py:76
  140.5 1.5 attend.13.refs_2_
  142.1 3.0 %collective-permute-done.26 = bf16[768,256]{1,0:T(8,128)(2,1)S(1)} collective-permute-done((bf16[768,256]{1,0:T(8,128)(2,1)S(1)}, bf16[768,256]{1,0:T(8,128)(2,1)S(1)}, u32[]{:S(2)}, u32[]{:S(2)}) %collective-permute-start.26) | collective-permute-done | bytes 393248 | tf_op jit(solution)/shard_map/ppermute | solution.py:76
  145.1 1.4 attend.15
  146.4 3.5 %collective-permute-start.27 = (f32[6,128,256]{2,1,0:T(8,128)S(1)}, f32[6,128,256]{2,1,0:T(8,128)S(1)}, u32[]{:S(2)}, u32[]{:S(2)}) collective-permute-start(f32[6,128,256]{2,1,0:T(8,128)S(1)} %attend.15), channel_id=1, source_target_pairs={{0,1},{1,0},{2,3},{3,2},{4,5},{5,4},{6,7},{7,6},{8,9},{9,8},{10,11... | collective-permute-start | bytes 2359304 | tf_op jit(solution)/shard_map/ppermute | solution.py:66
  149.9 1.4 attend.14
  151.3 0.5 collective-permute-done.27
  151.8 0.1 add.19
  151.9 0.1 fusion
  152.0 10.3 %all_to_all.19 = bf16[16,48,128]{2,1,0:T(8,128)(2,1)S(1)} all-to-all(bf16[16,48,128]{2,1,0:T(8,128)(2,1)S(1)} %bitcast.68), channel_id=1, replica_groups=mesh['seq'=16,'bal'=32] {'seq'}, dimensions={0} | all-to-all | bytes 393216 | tf_op jit(solution)/shard_map/all_to_all | solution.py:365
  162.3 0.7 copy_bitcast_fusion
  (29 shorter events, 0.1 us)
Async XLA Ops:
  0.0 82.0 %copy-start = (s32[1,192,64]{1,2,0:T(8,128)S(1)}, s32[1,192,64]{1,2,0:T(8,128)}, u32[]{:S(2)}) copy-start(s32[1,192,64]{1,2,0:T(8,128)} %param.10) | copy-start | bytes 147460
  0.0 37.7 %copy-start.1 = (bf16[3072,1,3,128]{3,0,2,1:T(8,128)(2,1)S(1)}, bf16[3072,1,3,128]{3,0,2,1:T(8,128)(2,1)}, u32[]{:S(2)}) copy-start(bf16[3072,1,3,128]{3,0,2,1:T(8,128)(2,1)} %param.7) | copy-start | bytes 7077892
  0.0 12.8 %collective-permute-start.1 = (bf16[48,3072]{1,0:T(8,128)(2,1)}, bf16[48,3072]{1,0:T(8,128)(2,1)S(1)}, u32[]{:S(2)}, u32[]{:S(2)}) collective-permute-start(bf16[48,3072]{1,0:T(8,128)(2,1)} %refs_0_.1), channel_id=1, source_target_pairs={{0,96},{32,0},{64,32},{96,64},{128,224},{160,128},{192,160},{224,1... | collective-permute-start | bytes 884744 | tf_op jit(solution)/shard_map/ppermute | solution.py:35
  5.6 12.3 %collective-permute-start = (bf16[48,3072]{1,0:T(8,128)(2,1)}, bf16[48,3072]{1,0:T(8,128)(2,1)S(1)}, u32[]{:S(2)}, u32[]{:S(2)}) collective-permute-start(bf16[48,3072]{1,0:T(8,128)(2,1)} %refs_0_.1), channel_id=1, source_target_pairs={{0,32},{32,64},{64,96},{96,0},{128,160},{160,192},{192,224},{224,1... | collective-permute-start | bytes 884744 | tf_op jit(solution)/shard_map/ppermute | solution.py:35
  7.5 13.3 %collective-permute-start.4 = (bf16[48,3072]{1,0:T(8,128)(2,1)}, bf16[48,3072]{1,0:T(8,128)(2,1)S(1)}, u32[]{:S(2)}, u32[]{:S(2)}) collective-permute-start(bf16[48,3072]{1,0:T(8,128)(2,1)} %refs_0_.1), channel_id=1, source_target_pairs={{0,64},{32,96},{64,0},{96,32},{128,192},{160,224},{192,128},{224,1... | collective-permute-start | bytes 884744 | tf_op jit(solution)/shard_map/ppermute | solution.py:35
  11.1 1.0 copy-start.4
  18.0 12.7 %collective-permute-start.2 = (bf16[96,3072]{1,0:T(8,128)(2,1)S(1)}, bf16[96,3072]{1,0:T(8,128)(2,1)}, u32[]{:S(2)}, u32[]{:S(2)}) collective-permute-start(bf16[96,3072]{1,0:T(8,128)(2,1)S(1)} %join.4.refs_0_), channel_id=1, source_target_pairs={{0,128},{32,160},{64,192},{96,224},{128,256},{160,288},{192,320},{... | collective-permute-start | bytes 1769480 | tf_op jit(solution)/shard_map/ppermute | solution.py:35
  21.7 11.2 %collective-permute-start.5 = (bf16[96,3072]{1,0:T(8,128)(2,1)}, bf16[96,3072]{1,0:T(8,128)(2,1)}, u32[]{:S(2)}, u32[]{:S(2)}) collective-permute-start(bf16[96,3072]{1,0:T(8,128)(2,1)} %join.5.refs_1_), channel_id=1, source_target_pairs={{0,384},{32,416},{64,448},{96,480},{128,0},{160,32},{192,64},{224,... | collective-permute-start | bytes 1769480 | tf_op jit(solution)/shard_map/ppermute | solution.py:35
  25.4 15.6 %collective-permute-start.7 = (bf16[96,3072]{1,0:T(8,128)(2,1)S(1)}, bf16[96,3072]{1,0:T(8,128)(2,1)}, u32[]{:S(2)}, u32[]{:S(2)}) collective-permute-start(bf16[96,3072]{1,0:T(8,128)(2,1)S(1)} %join.4.refs_0_), channel_id=1, source_target_pairs={{0,384},{32,416},{64,448},{96,480},{128,0},{160,32},{192,64},{224,... | collective-permute-start | bytes 1769480 | tf_op jit(solution)/shard_map/ppermute | solution.py:35
  28.3 12.8 %collective-permute-start.8 = (bf16[96,3072]{1,0:T(8,128)(2,1)}, bf16[96,3072]{1,0:T(8,128)(2,1)}, u32[]{:S(2)}, u32[]{:S(2)}) collective-permute-start(bf16[96,3072]{1,0:T(8,128)(2,1)} %join.5.refs_1_), channel_id=1, source_target_pairs={{0,128},{32,160},{64,192},{96,224},{128,256},{160,288},{192,320},{... | collective-permute-start | bytes 1769480 | tf_op jit(solution)/shard_map/ppermute | solution.py:35
  30.7 16.3 %collective-permute-start.3 = (bf16[96,3072]{1,0:T(8,128)(2,1)}, bf16[96,3072]{1,0:T(8,128)(2,1)}, u32[]{:S(2)}, u32[]{:S(2)}) collective-permute-start(bf16[96,3072]{1,0:T(8,128)(2,1)} %collective-permute-done.2.refs_2_), channel_id=1, source_target_pairs={{0,128},{32,160},{64,192},{96,224},{128,256},{160,288},{192,320},{... | collective-permute-start | bytes 1769480 | tf_op jit(solution)/shard_map/ppermute | solution.py:35
  32.9 14.1 %collective-permute-start.6 = (bf16[96,3072]{1,0:T(8,128)(2,1)}, bf16[96,3072]{1,0:T(8,128)(2,1)}, u32[]{:S(2)}, u32[]{:S(2)}) collective-permute-start(bf16[96,3072]{1,0:T(8,128)(2,1)} %collective-permute-done.5.refs_3_), channel_id=1, source_target_pairs={{0,384},{32,416},{64,448},{96,480},{128,0},{160,32},{192,64},{224,... | collective-permute-start | bytes 1769480 | tf_op jit(solution)/shard_map/ppermute | solution.py:35
  47.1 30.9 %copy-start.5 = (s32[1,192]{1,0:T(1,128)S(1)}, s32[1,192]{1,0:T(1,128)}, u32[]{:S(2)}) copy-start(s32[1,192]{1,0:T(1,128)} %param.11) | copy-start | bytes 2308
  49.4 17.6 %collective-permute-start.11 = (bf16[768,256]{1,0:T(8,128)(2,1)S(1)}, bf16[768,256]{1,0:T(8,128)(2,1)S(1)}, u32[]{:S(2)}, u32[]{:S(2)}) collective-permute-start(bf16[768,256]{1,0:T(8,128)(2,1)S(1)} %get-tuple-element.45), channel_id=1, source_target_pairs={{0,1},{1,0},{2,3},{3,2},{4,5},{5,4},{6,7},{7,6},{8,9},{9,8},{10,11... | collective-permute-start | bytes 1179656 | tf_op jit(solution)/shard_map/ppermute | solution.py:66
  55.1 15.8 %collective-permute-start.9 = (bf16[768,256]{1,0:T(8,128)(2,1)S(1)}, bf16[768,256]{1,0:T(8,128)(2,1)S(1)}, u32[]{:S(2)}, u32[]{:S(2)}) collective-permute-start(bf16[768,256]{1,0:T(8,128)(2,1)S(1)} %get-tuple-element.45), channel_id=1, source_target_pairs={{0,2},{1,31},{2,4},{3,1},{4,6},{5,3},{6,8},{7,5},{8,10},{9,7},{10,... | collective-permute-start | bytes 1179656 | tf_op jit(solution)/shard_map/ppermute | solution.py:76
  66.3 0.8 copy-start.2
  67.0 24.7 %copy-start.3 = (bf16[768,256]{1,0:T(8,128)(2,1)S(1)}, bf16[768,256]{1,0:T(8,128)(2,1)}, u32[]{:S(2)}) copy-start(bf16[768,256]{1,0:T(8,128)(2,1)} %copy-done.2) | copy-start | bytes 1179652
  67.0 12.3 %collective-permute-start.12 = (bf16[768,256]{1,0:T(8,128)(2,1)S(1)}, bf16[768,256]{1,0:T(8,128)(2,1)S(1)}, u32[]{:S(2)}, u32[]{:S(2)}) collective-permute-start(bf16[768,256]{1,0:T(8,128)(2,1)S(1)} %collective-permute-done.11), channel_id=1, source_target_pairs={{0,2},{1,31},{2,4},{3,1},{4,6},{5,3},{6,8},{7,5},{8,10},{9,7},{10,... | collective-permute-start | bytes 1179656 | tf_op jit(solution)/shard_map/ppermute | solution.py:76
  71.0 13.9 %collective-permute-start.10 = (bf16[768,256]{1,0:T(8,128)(2,1)S(1)}, bf16[768,256]{1,0:T(8,128)(2,1)S(1)}, u32[]{:S(2)}, u32[]{:S(2)}) collective-permute-start(bf16[768,256]{1,0:T(8,128)(2,1)S(1)} %collective-permute-done.9), channel_id=1, source_target_pairs={{0,2},{1,31},{2,4},{3,1},{4,6},{5,3},{6,8},{7,5},{8,10},{9,7},{10,... | collective-permute-start | bytes 1179656 | tf_op jit(solution)/shard_map/ppermute | solution.py:76
  76.0 3.3 %collective-permute-start.13 = (bf16[768,128]{1,0:T(8,128)(2,1)S(1)}, bf16[768,128]{1,0:T(8,128)(2,1)S(1)}, u32[]{:S(2)}, u32[]{:S(2)}) collective-permute-start(bf16[768,128]{1,0:T(8,128)(2,1)S(1)} %get-tuple-element.47), channel_id=1, source_target_pairs={{0,1},{1,0},{2,3},{3,2},{4,5},{5,4},{6,7},{7,6},{8,9},{9,8},{10,11... | collective-permute-start | bytes 589832 | tf_op jit(solution)/shard_map/ppermute | solution.py:66
  79.3 8.8 %collective-permute-start.14 = (bf16[768,256]{1,0:T(8,128)(2,1)S(1)}, bf16[768,256]{1,0:T(8,128)(2,1)S(1)}, u32[]{:S(2)}, u32[]{:S(2)}) collective-permute-start(bf16[768,256]{1,0:T(8,128)(2,1)S(1)} %collective-permute-done.12), channel_id=1, source_target_pairs={{0,2},{1,31},{2,4},{3,1},{4,6},{5,3},{6,8},{7,5},{8,10},{9,7},{10,... | collective-permute-start | bytes 1179656 | tf_op jit(solution)/shard_map/ppermute | solution.py:76
  84.9 8.8 %collective-permute-start.15 = (bf16[768,256]{1,0:T(8,128)(2,1)S(1)}, bf16[768,256]{1,0:T(8,128)(2,1)S(1)}, u32[]{:S(2)}, u32[]{:S(2)}) collective-permute-start(bf16[768,256]{1,0:T(8,128)(2,1)S(1)} %collective-permute-done.10), channel_id=1, source_target_pairs={{0,2},{1,31},{2,4},{3,1},{4,6},{5,3},{6,8},{7,5},{8,10},{9,7},{10,... | collective-permute-start | bytes 1179656 | tf_op jit(solution)/shard_map/ppermute | solution.py:76
  88.1 9.8 %collective-permute-start.17 = (bf16[768,256]{1,0:T(8,128)(2,1)S(1)}, bf16[768,256]{1,0:T(8,128)(2,1)S(1)}, u32[]{:S(2)}, u32[]{:S(2)}) collective-permute-start(bf16[768,256]{1,0:T(8,128)(2,1)S(1)} %collective-permute-done.14), channel_id=1, source_target_pairs={{0,2},{1,31},{2,4},{3,1},{4,6},{5,3},{6,8},{7,5},{8,10},{9,7},{10,... | collective-permute-start | bytes 1179656 | tf_op jit(solution)/shard_map/ppermute | solution.py:76
  93.7 9.3 %collective-permute-start.16 = (bf16[768,256]{1,0:T(8,128)(2,1)S(1)}, bf16[768,256]{1,0:T(8,128)(2,1)S(1)}, u32[]{:S(2)}, u32[]{:S(2)}) collective-permute-start(bf16[768,256]{1,0:T(8,128)(2,1)S(1)} %collective-permute-done.15), channel_id=1, source_target_pairs={{0,2},{1,31},{2,4},{3,1},{4,6},{5,3},{6,8},{7,5},{8,10},{9,7},{10,... | collective-permute-start | bytes 1179656 | tf_op jit(solution)/shard_map/ppermute | solution.py:76
  97.9 8.9 %collective-permute-start.19 = (bf16[768,256]{1,0:T(8,128)(2,1)S(1)}, bf16[768,256]{1,0:T(8,128)(2,1)S(1)}, u32[]{:S(2)}, u32[]{:S(2)}) collective-permute-start(bf16[768,256]{1,0:T(8,128)(2,1)S(1)} %collective-permute-done.17), channel_id=1, source_target_pairs={{0,2},{1,31},{2,4},{3,1},{4,6},{5,3},{6,8},{7,5},{8,10},{9,7},{10,... | collective-permute-start | bytes 1179656 | tf_op jit(solution)/shard_map/ppermute | solution.py:76
  103.0 9.7 %collective-permute-start.18 = (bf16[768,256]{1,0:T(8,128)(2,1)S(1)}, bf16[768,256]{1,0:T(8,128)(2,1)S(1)}, u32[]{:S(2)}, u32[]{:S(2)}) collective-permute-start(bf16[768,256]{1,0:T(8,128)(2,1)S(1)} %collective-permute-done.16), channel_id=1, source_target_pairs={{0,2},{1,31},{2,4},{3,1},{4,6},{5,3},{6,8},{7,5},{8,10},{9,7},{10,... | collective-permute-start | bytes 1179656 | tf_op jit(solution)/shard_map/ppermute | solution.py:76
  106.8 9.7 %collective-permute-start.21 = (bf16[768,256]{1,0:T(8,128)(2,1)S(1)}, bf16[768,256]{1,0:T(8,128)(2,1)S(1)}, u32[]{:S(2)}, u32[]{:S(2)}) collective-permute-start(bf16[768,256]{1,0:T(8,128)(2,1)S(1)} %collective-permute-done.19), channel_id=1, source_target_pairs={{0,2},{1,31},{2,4},{3,1},{4,6},{5,3},{6,8},{7,5},{8,10},{9,7},{10,... | collective-permute-start | bytes 1179656 | tf_op jit(solution)/shard_map/ppermute | solution.py:76
  112.7 9.7 %collective-permute-start.20 = (bf16[768,256]{1,0:T(8,128)(2,1)S(1)}, bf16[768,256]{1,0:T(8,128)(2,1)S(1)}, u32[]{:S(2)}, u32[]{:S(2)}) collective-permute-start(bf16[768,256]{1,0:T(8,128)(2,1)S(1)} %collective-permute-done.18), channel_id=1, source_target_pairs={{0,2},{1,31},{2,4},{3,1},{4,6},{5,3},{6,8},{7,5},{8,10},{9,7},{10,... | collective-permute-start | bytes 1179656 | tf_op jit(solution)/shard_map/ppermute | solution.py:76
  116.5 9.7 %collective-permute-start.23 = (bf16[768,256]{1,0:T(8,128)(2,1)S(1)}, bf16[768,256]{1,0:T(8,128)(2,1)S(1)}, u32[]{:S(2)}, u32[]{:S(2)}) collective-permute-start(bf16[768,256]{1,0:T(8,128)(2,1)S(1)} %collective-permute-done.21), channel_id=1, source_target_pairs={{0,2},{1,31},{2,4},{3,1},{4,6},{5,3},{6,8},{7,5},{8,10},{9,7},{10,... | collective-permute-start | bytes 1179656 | tf_op jit(solution)/shard_map/ppermute | solution.py:76
  122.4 9.7 %collective-permute-start.22 = (bf16[768,256]{1,0:T(8,128)(2,1)S(1)}, bf16[768,256]{1,0:T(8,128)(2,1)S(1)}, u32[]{:S(2)}, u32[]{:S(2)}) collective-permute-start(bf16[768,256]{1,0:T(8,128)(2,1)S(1)} %collective-permute-done.20), channel_id=1, source_target_pairs={{0,2},{1,31},{2,4},{3,1},{4,6},{5,3},{6,8},{7,5},{8,10},{9,7},{10,... | collective-permute-start | bytes 1179656 | tf_op jit(solution)/shard_map/ppermute | solution.py:76
  126.2 9.7 %collective-permute-start.25 = (bf16[768,256]{1,0:T(8,128)(2,1)S(1)}, bf16[768,256]{1,0:T(8,128)(2,1)S(1)}, u32[]{:S(2)}, u32[]{:S(2)}) collective-permute-start(bf16[768,256]{1,0:T(8,128)(2,1)S(1)} %collective-permute-done.23), channel_id=1, source_target_pairs={{0,2},{1,31},{2,4},{3,1},{4,6},{5,3},{6,8},{7,5},{8,10},{9,7},{10,... | collective-permute-start | bytes 1179656 | tf_op jit(solution)/shard_map/ppermute | solution.py:76
  132.2 9.9 %collective-permute-start.24 = (bf16[768,256]{1,0:T(8,128)(2,1)S(1)}, bf16[768,256]{1,0:T(8,128)(2,1)S(1)}, u32[]{:S(2)}, u32[]{:S(2)}) collective-permute-start(bf16[768,256]{1,0:T(8,128)(2,1)S(1)} %collective-permute-done.22), channel_id=1, source_target_pairs={{1,31},{3,1},{5,3},{7,5},{9,7},{11,9},{13,11},{15,13},{17,15},{19,... | collective-permute-start | bytes 1179656 | tf_op jit(solution)/shard_map/ppermute | solution.py:76
  135.9 9.1 %collective-permute-start.26 = (bf16[768,256]{1,0:T(8,128)(2,1)S(1)}, bf16[768,256]{1,0:T(8,128)(2,1)S(1)}, u32[]{:S(2)}, u32[]{:S(2)}) collective-permute-start(bf16[768,256]{1,0:T(8,128)(2,1)S(1)} %collective-permute-done.25), channel_id=1, source_target_pairs={{1,31},{3,1},{5,3},{7,5},{9,7},{11,9},{13,11},{15,13},{17,15},{19,... | collective-permute-start | bytes 1179656 | tf_op jit(solution)/shard_map/ppermute | solution.py:76
  146.4 5.4 %collective-permute-start.27 = (f32[6,128,256]{2,1,0:T(8,128)S(1)}, f32[6,128,256]{2,1,0:T(8,128)S(1)}, u32[]{:S(2)}, u32[]{:S(2)}) collective-permute-start(f32[6,128,256]{2,1,0:T(8,128)S(1)} %attend.15), channel_id=1, source_target_pairs={{0,1},{1,0},{2,3},{3,2},{4,5},{5,4},{6,7},{7,6},{8,9},{9,8},{10,11... | collective-permute-start | bytes 2359304 | tf_op jit(solution)/shard_map/ppermute | solution.py:66
